TPU v7x, 32 devices: a whole 2x2x4 slice. The times are simulated.
32 devices in a mesh: tile: 4 (over z), chan: 8 (over y, x, core).
Axes of the slice: x: 2, y: 2, z: 4, core: 2. Of those that a mesh axis runs over, the one named last changes fastest.
Arguments:
- fields: float32 [32, 128, 411], P('chan', 'tile'), may hold values from -12 to 12
- diffusivity: float32 [32, 128], P('chan', 'tile'), may hold values from 0.02 to 0.24
- owners: int32 [256, 1], replicated, may hold values from 0 to 3; in each aligned block of 64 rows (0 to 63, 64 to 127, ...) at most 32 rows name the same one
- observed: bfloat16 [512, 6144], P('tile', 'chan'), may hold values from -6 to 6
- usable: int32 [512], P('tile'), may hold values 0 or 1
- w_hidden: bfloat16 [411, 2048], P(None, 'chan'), may hold values from -0.3125 to 0.3125
- b_hidden: float32 [2048], P('chan'), may hold values from -3 to 3
- w_radiance: bfloat16 [2048, 6144], P(None, 'chan'), may hold values from -0.125 to 0.125
- b_radiance: float32 [6144], P('chan'), may hold values from -3 to 3
- inv_cov: bfloat16 [6144, 6144], P('tile', 'chan'), may hold values from -6 to 22
Outputs:
- gradient: float32 [32, 128, 411], P('chan', 'tile')
Inputs may be any that keep to these rules, and one draw needn't show every extreme that they name: `owners`: in each tile's block of 64 consecutive entries no owner appears more than 32 times, and in some blocks one appears exactly 32 times.
All inputs are finite; a program needn't handle non-finite values. No bound on the sum of `usable` on one device may be relied on, other than what follows from the above.
Results may differ from a plain program's by a relative error of at most 0.0045.
Values may be sent and summed in bfloat16 or wider, within the bound.
No kernel may reach another device: no remote copies, remote signals or barrier semaphores. Data moves between devices by JAX's collectives and lax.ppermute only.
A program may use at most 64 MiB of HBM per device.

v0:
```python
import jax
import jax.numpy as jnp
from jax import lax
from jax.sharding import PartitionSpec as P


def padded_2(value, sides, width, wrap):
    for axis, dim in sides:
        devices, length = (lax.axis_size(axis), value.shape[dim])
        up = [(i, (i + 1) % devices) for i in range(devices if wrap else devices - 1)]
        down = [(j, i) for i, j in up]
        last = lax.slice_in_dim(value, length - width, length, axis=dim)
        first = lax.slice_in_dim(value, 0, width, axis=dim)
        before = lax.ppermute(last, axis, up)
        after = lax.ppermute(first, axis, down)
        value = jnp.concatenate([before, value, after], axis=dim)
    return value


def add_rims(values):
    rowwise = padded_2(values, (("chan", 0),), 1, False)
    return padded_2(rowwise, (("tile", 1),), 1, True)


def body(
    fields,
    diffusivity,
    owners,
    observed,
    usable,
    w_hidden,
    b_hidden,
    w_radiance,
    b_radiance,
    inv_cov,
):
    tile_count = lax.axis_size("tile")
    chan_count = lax.axis_size("chan")
    tile_index = lax.axis_index("tile")
    chan_index = lax.axis_index("chan")
    slot_count = observed.shape[0]
    capacity = slot_count // tile_count
    cells_across, cells_along, features = fields.shape
    own_cols = cells_across // 4 * (cells_along // 4)
    tile_cols = chan_count * own_cols
    hidden_dev = w_hidden.shape[1]
    owner_table = owners[:, 0].reshape(tile_count, tile_cols)
    owner_hits = (
        owner_table[:, :, None] == jnp.arange(tile_count, dtype=jnp.int32)[None, None, :]
    ).astype(jnp.int32)
    before = jnp.sum((jnp.cumsum(owner_hits, axis=1) - owner_hits) * owner_hits, axis=2)
    tallies = jnp.sum(owner_hits, axis=1)
    slot_of = lax.dynamic_index_in_dim(
        owner_table * capacity + before, tile_index, 0, keepdims=False
    )
    arriving = lax.dynamic_index_in_dim(tallies, tile_index, 1, keepdims=False)
    occupied = (jnp.arange(capacity, dtype=jnp.int32)[None, :] < arriving[:, None]).reshape(
        slot_count
    )
    grouped = fields.reshape(cells_across // 4, 4, cells_along // 4, 4, features)
    columns = (
        (jnp.sum(grouped, axis=(1, 3)) * 0.0625).reshape(own_cols, features).astype(jnp.bfloat16)
    )
    placer = (slot_of[None, :] == jnp.arange(slot_count, dtype=jnp.int32)[:, None]).astype(
        jnp.bfloat16
    )
    picks = placer
    outgoing = jnp.dot(
        picks,
        lax.all_gather(columns, "chan", axis=0, tiled=True),
        preferred_element_type=jnp.float32,
    )
    incoming = lax.all_to_all(
        outgoing.astype(jnp.bfloat16), "tile", split_axis=0, concat_axis=0, tiled=True
    )
    preact = lax.dot_general(
        w_hidden, incoming, (((0,), (1,)), ((), ())), preferred_element_type=jnp.float32
    )
    preact = preact + b_hidden[:, None]
    squash = jax.nn.sigmoid(preact)
    active = (preact * squash).astype(jnp.bfloat16)
    weights = w_radiance
    radiance = lax.dot_general(
        lax.all_gather(active, "chan", axis=0, tiled=True),
        weights,
        (((0,), (0,)), ((), ())),
        preferred_element_type=jnp.float32,
    )
    radiance = radiance + b_radiance[None, :]
    in_use = usable.astype(jnp.float32) * occupied.astype(jnp.float32)
    departure = ((radiance - observed.astype(jnp.float32)) * in_use[:, None]).astype(jnp.bfloat16)
    all_depart = lax.all_gather(departure, "chan", axis=1, tiled=True)
    picks = all_depart
    cotangent = jnp.dot(
        picks,
        lax.all_gather(inv_cov, "tile", axis=0, tiled=True),
        preferred_element_type=jnp.float32,
    )
    cotangent = cotangent.astype(jnp.bfloat16)
    weights = w_radiance
    full_sum = lax.psum(
        lax.dot_general(
            weights, cotangent, (((1,), (1,)), ((), ())), preferred_element_type=jnp.float32
        ),
        "chan",
    )
    grad_hidden = lax.dynamic_slice_in_dim(full_sum, chan_index * hidden_dev, hidden_dev, 0)
    slope_term = squash * (1.0 + preact * (1.0 - squash))
    grad_pre = (grad_hidden * slope_term).astype(jnp.bfloat16)
    part_grad = lax.dot_general(
        grad_pre, w_hidden, (((0,), (1,)), ((), ())), preferred_element_type=jnp.float32
    )
    returned = lax.all_to_all(part_grad, "tile", split_axis=0, concat_axis=0, tiled=True)
    column_grad = lax.psum_scatter(
        jnp.take(returned, slot_of, axis=0), "chan", scatter_dimension=0, tiled=True
    )
    spread = jnp.repeat(
        column_grad.reshape(cells_across // 4, cells_along // 4, features), 4, axis=0
    )
    adjoint = jnp.repeat(spread, 4, axis=1) * 0.0625
    kappa_root = jnp.sqrt(diffusivity)
    root_rim = add_rims(kappa_root)
    coef_north = (kappa_root * root_rim[2:, 1:-1])[:, :, None]
    coef_south = (kappa_root * root_rim[:-2, 1:-1])[:, :, None]
    coef_east = (kappa_root * root_rim[1:-1, 2:])[:, :, None]
    coef_west = (kappa_root * root_rim[1:-1, :-2])[:, :, None]
    for sweep_index in range(2):
        padded = add_rims(adjoint)
        adjoint = (
            adjoint
            + coef_north * (padded[2:, 1:-1] - adjoint)
            + coef_south * (padded[:-2, 1:-1] - adjoint)
            + coef_east * (padded[1:-1, 2:] - adjoint)
            + coef_west * (padded[1:-1, :-2] - adjoint)
        )
    return adjoint


def solution(mesh):
    placed = (
        P("chan", "tile", None),
        P("chan", "tile"),
        P(),
        P("tile", "chan"),
        P("tile"),
        P(None, "chan"),
        P("chan"),
        P(None, "chan"),
        P("chan"),
        P("tile", "chan"),
    )
    return jax.shard_map(
        body, mesh=mesh, in_specs=placed, out_specs=P("chan", "tile", None), check_vma=False
    )
```

profile of v0, /device:TPU:0, one launch (start us, length us, event | category | flops | bytes accessed | tf_op | source)
XLA Modules:
  0.0 381.8 jit_solution(2550175356596755827)
XLA Ops:
  6.5 1.1 reduce_sum.35
  7.8 10.7 %all_gather.12 = bf16[64,411]{1,0:T(8,128)(2,1)S(1)} all-gather(bf16[8,411]{1,0:T(8,128)(2,1)S(1)} %multiply_convert_fusion.3), channel_id=1, replica_groups=mesh['tile'=4,'chan'=8] {'chan'}, dimensions={0}, use_global_device_ids=true | all-gather | bytes 59184 | tf_op jit(solution)/shard_map/all_gather | solution.py:70
  18.4 0.5 broadcast.86
  19.0 1.3 reduce.8
  20.3 0.1 reshape_squeeze.3
  20.4 0.1 fusion.28
  20.5 0.1 reduce_window_sum.11
  20.6 0.2 fusion.29
  20.9 0.5 compare_and_fusion
  21.4 0.2 convolution_convert_fusion.1
  21.6 0.8 copy.21
  22.4 4.9 %all-to-all-start = ((bf16[4,32,411]{2,1,0:T(8,128)(2,1)}), bf16[4,32,411]{2,1,0:T(8,128)(2,1)S(1)}, u32[]{:S(2)}, u32[]{:S(2)}) async-start(bf16[4,32,411]{2,1,0:T(8,128)(2,1)} %bitcast.1), calls=%async_computation | async-start | bytes 262144 | tf_op jit(solution)/shard_map/all_to_all | solution.py:73
  27.3 0.2 dynamic-slice_reduce_fusion
  27.4 0.1 iota_compare_fusion.3
  27.5 0.1 lt.56
  27.6 0.7 convert_select_fusion
  28.3 5.4 %all-to-all-done = bf16[4,32,411]{2,1,0:T(8,128)(2,1)S(1)} async-done(((bf16[4,32,411]{2,1,0:T(8,128)(2,1)}), bf16[4,32,411]{2,1,0:T(8,128)(2,1)S(1)}, u32[]{:S(2)}, u32[]{:S(2)}) %all-to-all-start) | async-done | bytes 105248 | tf_op jit(solution)/shard_map/all_to_all | solution.py:73
  33.7 1.8 multiply_convert_fusion.1
  35.4 10.9 %all_gather.13 = bf16[2048,128]{0,1:T(8,128)(2,1)S(1)} all-gather(bf16[256,128]{0,1:T(8,128)(2,1)S(1)} %get-tuple-element.27), channel_id=1, replica_groups=mesh['tile'=4,'chan'=8] {'chan'}, dimensions={0}, use_global_device_ids=true | all-gather | bytes 589824 | tf_op jit(solution)/shard_map/all_gather | solution.py:84
  46.3 2.2 fusion.2
  48.5 0.0 all-gather.3.cloned.1.call-update
  48.5 0.0 all-gather.5.cloned.1.call-start
  48.6 0.7 all-gather.5.cloned.1.call-update
  49.3 0.0 copy-start.1
  49.3 0.0 copy-start.5
  49.3 0.0 all-reduce.2.cloned.1.call-start
  49.4 23.3 %all-gather.3.cloned.1.call-done = bf16[128,6144]{1,0:T(8,128)(2,1)} async-done(((bf16[128,768]{1,0:T(8,128)(2,1)}), bf16[128,6144]{1,0:T(8,128)(2,1)}) %all-gather.3.cloned.1.call-update) | async-done | bytes 1572880 | tf_op jit(solution)/shard_map/all_gather | solution.py:92
  72.7 168.4 %all-gather.5.cloned.1.call-done = bf16[6144,768]{1,0:T(8,128)(2,1)} async-done(((bf16[1536,768]{1,0:T(8,128)(2,1)}), bf16[6144,768]{1,0:T(8,128)(2,1)}) %all-gather.5.cloned.1.call-update) | async-done | bytes 9437200 | tf_op jit(solution)/shard_map/all_gather | solution.py:96
  241.1 8.1 %convolution_bitcast_fusion = f32[2048,128]{0,1:T(8,128)} fusion(bf16[2048,768]{1,0:T(8,128)(2,1)S(1)} %copy-done, bf16[128,6144]{1,0:T(8,128)(2,1)} %all-gather.3.cloned.1.call-done, bf16[6144,768]{1,0:T(8,128)(2,1)} %all-gather.5.cloned.1.call-done), kind=kOutput, calls=%fused_computation.1 | convolution fusion | flops 1610711040 | bytes 15204352 | tf_op jit(solution)/shard_map/dot_general | solution.py:102
  249.2 0.0 all-reduce.2.cloned.1.call-update
  249.2 1.3 collective-permute-start
  250.5 3.0 collective-permute-start.2
  253.6 50.6 %all-reduce.2.cloned.1.call-done = f32[2048,128]{0,1:T(8,128)} async-done(((f32[2048,128]{0,1:T(8,128)}), f32[2048,128]{0,1:T(8,128)}) %all-reduce.2.cloned.1.call-update) | async-done | bytes 1048592 | tf_op jit(solution)/shard_map/psum | solution.py:101
  304.1 1.9 fusion.30
  306.0 4.5 %all-to-all-start.1 = ((f32[4,32,411]{2,1,0:T(8,128)}), f32[4,32,411]{2,1,0:T(8,128)S(1)}, u32[]{:S(2)}, u32[]{:S(2)}) async-start(f32[4,32,411]{2,1,0:T(8,128)} %bitcast.26), calls=%async_computation.1 | async-start | bytes 524288 | tf_op jit(solution)/shard_map/all_to_all | solution.py:113
  310.5 0.0 collective-permute-done.2
  310.6 8.1 %all-to-all-done.1 = f32[4,32,411]{2,1,0:T(8,128)S(1)} async-done(((f32[4,32,411]{2,1,0:T(8,128)}), f32[4,32,411]{2,1,0:T(8,128)S(1)}, u32[]{:S(2)}, u32[]{:S(2)}) %all-to-all-start.1) | async-done | bytes 210464 | tf_op jit(solution)/shard_map/all_to_all | solution.py:113
  318.6 0.7 gather_fusion
  319.3 1.3 broadcast_select_fusion
  320.6 0.0 reduce-scatter.2.cloned.1.call-update
  320.6 0.1 fusion.39
  320.7 1.3 collective-permute-start.4
  322.0 0.8 collective-permute-start.6
  322.7 0.7 pad_maximum_fusion.22
  323.4 28.2 %reduce-scatter.2.cloned.1.call-done = f32[8,411]{1,0:T(8,128)} async-done(((f32[64,411]{1,0:T(8,128)}), f32[8,411]{1,0:T(8,128)}) %reduce-scatter.2.cloned.1.call-update) | async-done | bytes 13168 | tf_op jit(solution)/shard_map/reduce_scatter | solution.py:114
  351.6 0.7 broadcast_multiply_fusion
  352.4 1.3 collective-permute-start.1
  353.7 3.0 collective-permute-start.3
  356.7 0.0 collective-permute-done.6
  356.8 0.8 pad_maximum_fusion.25
  357.6 0.0 collective-permute-done.3
  357.7 1.5 collective-permute-start.7
  359.2 2.3 collective-permute-start.5
  361.6 0.1 slice_multiply_fusion.3
  361.6 1.6 collective-permute-done.7
  363.3 0.0 collective-permute-done.5
  363.3 0.2 fusion.18
  363.5 1.3 collective-permute-start.8
  364.8 3.0 collective-permute-start.9
  367.9 0.9 collective-permute-done.9
  368.8 1.2 collective-permute-start.11
  370.0 2.7 collective-permute-start.10
  372.7 1.6 collective-permute-done.11
  374.3 0.9 fusion.6
  (33 shorter events, 0.3 us)
Async XLA Ops:
  6.5 39.8 %copy-start = (bf16[2048,768]{1,0:T(8,128)(2,1)S(1)}, bf16[2048,768]{1,0:T(8,128)(2,1)}, u32[]{:S(2)}) copy-start(bf16[2048,768]{1,0:T(8,128)(2,1)} %param.17) | copy-start | bytes 9437188
  6.5 39.8 %copy-start.4 = (f32[768]{0:T(1024)S(1)}, f32[768]{0:T(1024)}, u32[]{:S(2)}) copy-start(f32[768]{0:T(1024)} %param.18) | copy-start | bytes 9220
  22.4 11.3 %all-to-all-start = ((bf16[4,32,411]{2,1,0:T(8,128)(2,1)}), bf16[4,32,411]{2,1,0:T(8,128)(2,1)S(1)}, u32[]{:S(2)}, u32[]{:S(2)}) async-start(bf16[4,32,411]{2,1,0:T(8,128)(2,1)} %bitcast.1), calls=%async_computation | async-start | bytes 262144 | tf_op jit(solution)/shard_map/all_to_all | solution.py:73
  27.3 45.4 %all-gather.3.cloned.1.call-start = ((), (), s32[]{:S(2)}) async-start(), calls=%async_computation.3 | async-start | bytes 1769472 | tf_op jit(solution)/shard_map/all_gather | solution.py:92
  48.5 192.5 %all-gather.5.cloned.1.call-start = ((), (), s32[]{:S(2)}) async-start(), calls=%async_computation.4 | async-start | bytes 11796480 | tf_op jit(solution)/shard_map/all_gather | solution.py:96
  49.3 199.9 %copy-start.1 = (f32[4,32]{1,0:T(4,128)S(1)}, f32[4,32]{1,0:T(4,128)}, u32[]{:S(2)}) copy-start(f32[4,32]{1,0:T(4,128)} %param.11) | copy-start | bytes 1540
  49.3 254.8 %copy-start.5 = (bf16[411,256]{1,0:T(8,128)(2,1)S(1)}, bf16[411,256]{1,0:T(8,128)(2,1)}, u32[]{:S(2)}) copy-start(bf16[411,256]{1,0:T(8,128)(2,1)} %param.15) | copy-start | bytes 631300
  49.3 254.8 %all-reduce.2.cloned.1.call-start = ((), (), s32[]{:S(2)}) async-start(), calls=%async_computation.5 | async-start | bytes 2097152 | tf_op jit(solution)/shard_map/psum | solution.py:101
  249.2 61.3 %collective-permute-start = (f32[1,32]{1,0:T(1,128)S(1)}, f32[1,32]{1,0:T(1,128)S(1)}, u32[]{:S(2)}, u32[]{:S(2)}) collective-permute-start(f32[1,32]{1,0:T(1,128)S(1)} %get-tuple-element.26), channel_id=1, source_target_pairs={{1,0},{2,1},{3,2},{4,3},{5,4},{6,5},{7,6},{9,8},{10,9},{11,10},{12... | collective-permute-start | bytes 392 | tf_op jit(solution)/shard_map/ppermute | solution.py:15
  250.5 60.0 %collective-permute-start.2 = (f32[1,32]{1,0:T(1,128)S(1)}, f32[1,32]{1,0:T(1,128)S(1)}, u32[]{:S(2)}, u32[]{:S(2)}) collective-permute-start(f32[1,32]{1,0:T(1,128)S(1)} %get-tuple-element.25), channel_id=1, source_target_pairs={{0,1},{1,2},{2,3},{3,4},{4,5},{5,6},{6,7},{8,9},{9,10},{10,11},{11... | collective-permute-start | bytes 392 | tf_op jit(solution)/shard_map/ppermute | solution.py:14
  306.0 12.6 %all-to-all-start.1 = ((f32[4,32,411]{2,1,0:T(8,128)}), f32[4,32,411]{2,1,0:T(8,128)S(1)}, u32[]{:S(2)}, u32[]{:S(2)}) async-start(f32[4,32,411]{2,1,0:T(8,128)} %bitcast.26), calls=%async_computation.1 | async-start | bytes 524288 | tf_op jit(solution)/shard_map/all_to_all | solution.py:113
  310.5 41.1 %reduce-scatter.2.cloned.1.call-start = ((), (), s32[]{:S(2)}) async-start(), calls=%async_computation.6 | async-start | bytes 147456 | tf_op jit(solution)/shard_map/reduce_scatter | solution.py:114
  310.5 8.1 %copy-start.2 = (f32[1,32]{1,0:T(1,128)}, f32[1,32]{1,0:T(1,128)S(1)}, u32[]{:S(2)}) copy-start(f32[1,32]{1,0:T(1,128)S(1)} %collective-permute-done) | copy-start | bytes 388
  310.5 8.1 %copy-start.3 = (f32[1,32]{1,0:T(1,128)}, f32[1,32]{1,0:T(1,128)S(1)}, u32[]{:S(2)}) copy-start(f32[1,32]{1,0:T(1,128)S(1)} %collective-permute-done.2) | copy-start | bytes 388
  320.7 36.0 %collective-permute-start.4 = (f32[6,1]{1,0:T(8,128)S(1)}, f32[6,1]{1,0:T(8,128)S(1)}, u32[]{:S(2)}, u32[]{:S(2)}) collective-permute-start(f32[6,1]{1,0:T(8,128)S(1)} %get-tuple-element.15), channel_id=1, source_target_pairs={{8,0},{16,8},{24,16},{0,24},{9,1},{17,9},{25,17},{1,25},{10,2},{18... | collective-permute-start | bytes 80 | tf_op jit(solution)/shard_map/ppermute | solution.py:15
  322.0 34.8 %collective-permute-start.6 = (f32[6,1]{1,0:T(8,128)S(1)}, f32[6,1]{1,0:T(8,128)S(1)}, u32[]{:S(2)}, u32[]{:S(2)}) collective-permute-start(f32[6,1]{1,0:T(8,128)S(1)} %get-tuple-element.16), channel_id=1, source_target_pairs={{0,8},{8,16},{16,24},{24,0},{1,9},{9,17},{17,25},{25,1},{2,10},{10... | collective-permute-start | bytes 80 | tf_op jit(solution)/shard_map/ppermute | solution.py:14
  352.4 5.2 %collective-permute-start.1 = (f32[1,32,411]{2,1,0:T(8,128)S(1)}, f32[1,32,411]{2,1,0:T(8,128)S(1)}, u32[]{:S(2)}, u32[]{:S(2)}) collective-permute-start(f32[1,32,411]{2,1,0:T(8,128)S(1)} %mul.147), channel_id=1, source_target_pairs={{1,0},{2,1},{3,2},{4,3},{5,4},{6,5},{7,6},{9,8},{10,9},{11,10},{12... | collective-permute-start | bytes 157832 | tf_op jit(solution)/shard_map/ppermute | solution.py:15
  353.7 3.9 %collective-permute-start.3 = (f32[1,32,411]{2,1,0:T(8,128)S(1)}, f32[1,32,411]{2,1,0:T(8,128)S(1)}, u32[]{:S(2)}, u32[]{:S(2)}) collective-permute-start(f32[1,32,411]{2,1,0:T(8,128)S(1)} %mul.147), channel_id=1, source_target_pairs={{0,1},{1,2},{2,3},{3,4},{4,5},{5,6},{6,7},{8,9},{9,10},{10,11},{11... | collective-permute-start | bytes 157832 | tf_op jit(solution)/shard_map/ppermute | solution.py:14
  357.7 5.6 %collective-permute-start.7 = (f32[6,1,411]{2,1,0:T(1,128)S(1)}, f32[6,1,411]{2,1,0:T(1,128)S(1)}, u32[]{:S(2)}, u32[]{:S(2)}) collective-permute-start(f32[6,1,411]{2,1,0:T(1,128)S(1)} %get-tuple-element.12), channel_id=1, source_target_pairs={{0,8},{8,16},{16,24},{24,0},{1,9},{9,17},{17,25},{25,1},{2,10},{10... | collective-permute-start | bytes 29600 | tf_op jit(solution)/shard_map/ppermute | solution.py:14
  359.2 4.0 %collective-permute-start.5 = (f32[6,1,411]{2,1,0:T(1,128)S(1)}, f32[6,1,411]{2,1,0:T(1,128)S(1)}, u32[]{:S(2)}, u32[]{:S(2)}) collective-permute-start(f32[6,1,411]{2,1,0:T(1,128)S(1)} %get-tuple-element.11), channel_id=1, source_target_pairs={{8,0},{16,8},{24,16},{0,24},{9,1},{17,9},{25,17},{1,25},{10,2},{18... | collective-permute-start | bytes 29600 | tf_op jit(solution)/shard_map/ppermute | solution.py:15
  363.5 4.3 %collective-permute-start.8 = (f32[1,32,411]{2,1,0:T(8,128)S(1)}, f32[1,32,411]{2,1,0:T(8,128)S(1)}, u32[]{:S(2)}, u32[]{:S(2)}) collective-permute-start(f32[1,32,411]{2,1,0:T(8,128)S(1)} %get-tuple-element.14), channel_id=1, source_target_pairs={{1,0},{2,1},{3,2},{4,3},{5,4},{6,5},{7,6},{9,8},{10,9},{11,10},{12... | collective-permute-start | bytes 157832 | tf_op jit(solution)/shard_map/ppermute | solution.py:15
  364.8 3.9 %collective-permute-start.9 = (f32[1,32,411]{2,1,0:T(8,128)S(1)}, f32[1,32,411]{2,1,0:T(8,128)S(1)}, u32[]{:S(2)}, u32[]{:S(2)}) collective-permute-start(f32[1,32,411]{2,1,0:T(8,128)S(1)} %get-tuple-element.13), channel_id=1, source_target_pairs={{0,1},{1,2},{2,3},{3,4},{4,5},{5,6},{6,7},{8,9},{9,10},{10,11},{11... | collective-permute-start | bytes 157832 | tf_op jit(solution)/shard_map/ppermute | solution.py:14
  368.8 5.5 %collective-permute-start.11 = (f32[6,1,411]{2,1,0:T(1,128)S(1)}, f32[6,1,411]{2,1,0:T(1,128)S(1)}, u32[]{:S(2)}, u32[]{:S(2)}) collective-permute-start(f32[6,1,411]{2,1,0:T(1,128)S(1)} %get-tuple-element.10), channel_id=1, source_target_pairs={{0,8},{8,16},{16,24},{24,0},{1,9},{9,17},{17,25},{25,1},{2,10},{10... | collective-permute-start | bytes 29600 | tf_op jit(solution)/shard_map/ppermute | solution.py:14
  370.0 4.3 %collective-permute-start.10 = (f32[6,1,411]{2,1,0:T(1,128)S(1)}, f32[6,1,411]{2,1,0:T(1,128)S(1)}, u32[]{:S(2)}, u32[]{:S(2)}) collective-permute-start(f32[6,1,411]{2,1,0:T(1,128)S(1)} %get-tuple-element.9), channel_id=1, source_target_pairs={{8,0},{16,8},{24,16},{0,24},{9,1},{17,9},{25,17},{1,25},{10,2},{18... | collective-permute-start | bytes 29600 | tf_op jit(solution)/shard_map/ppermute | solution.py:15
Sparse Core Ops, SparseCore 0:
  48.7 23.9 all-gather.2
  74.3 166.7 all-gather.4
  249.3 54.7 all-reduce.1
  320.8 30.8 reduce-scatter.1
where the time goes:
time: 388 us; the launch traced here: 382 us
  waiting for transfers between devices  289 us (74%)
  starting transfers between devices  32.2 us (8%)
  blocking collectives  21.6 us (6%)
  matrix products  14.2 us (4%)
  between operations  13.4 us (3%)
  other arithmetic  9.02 us (2%)
    all_gather x1, waiting for transfers between devices, body(): lax.all_gather(inv_cov, 'tile', axis=0, tiled=True)  168 us
    psum x1, waiting for transfers between devices, body(): lax.psum(lax.dot_general(weights, cotangent, (((1,), (1,)), ((), ())), pr...  50.6 us
    reduce_scatter x1, waiting for transfers between devices, body(): lax.psum_scatter(jnp.take(returned, slot_of, axis=0), 'chan', scatter_dim...  28.2 us
    all_gather x1, waiting for transfers between devices, body(): all_depart = lax.all_gather(departure, 'chan', axis=1, tiled=True)  23.3 us
    ppermute x6, starting transfers between devices, padded_2(): before = lax.ppermute(last, axis, up)  12.6 us
    all_gather x1, blocking collectives, body(): lax.all_gather(active, 'chan', axis=0, tiled=True)  10.9 us
    all_gather x1, blocking collectives, body(): lax.all_gather(columns, 'chan', axis=0, tiled=True)  10.7 us
    ppermute x6, starting transfers between devices, padded_2(): after = lax.ppermute(first, axis, down)  10.2 us
  transfers between devices with their start and end apart: 18, of which 9 were waited for; matrix products, arithmetic and copies ran while one was open for 1% of the time, Pallas kernels for 0%

commit v1 on v0

--- a/solution.py
+++ b/solution.py
@@ -1,7 +1,15 @@
+import functools
+
 import jax
 import jax.numpy as jnp
+import numpy as np
 from jax import lax
+from jax.experimental import pallas as pl
+from jax.experimental.pallas import tpu as pltpu
 from jax.sharding import PartitionSpec as P
+
+VMEM_BYTES = 40 * 1024 * 1024
+NT_DIMS = (((1,), (1,)), ((), ()))
 
 
 def padded_2(value, sides, width, wrap):
@@ -22,7 +30,7 @@
     return padded_2(rowwise, (("tile", 1),), 1, True)
 
 
-def body(
+def body_by_owner(
     fields,
     diffusivity,
     owners,
@@ -64,9 +72,8 @@
     placer = (slot_of[None, :] == jnp.arange(slot_count, dtype=jnp.int32)[:, None]).astype(
         jnp.bfloat16
     )
-    picks = placer
     outgoing = jnp.dot(
-        picks,
+        placer,
         lax.all_gather(columns, "chan", axis=0, tiled=True),
         preferred_element_type=jnp.float32,
     )
@@ -79,29 +86,23 @@
     preact = preact + b_hidden[:, None]
     squash = jax.nn.sigmoid(preact)
     active = (preact * squash).astype(jnp.bfloat16)
-    weights = w_radiance
     radiance = lax.dot_general(
         lax.all_gather(active, "chan", axis=0, tiled=True),
-        weights,
+        w_radiance,
         (((0,), (0,)), ((), ())),
         preferred_element_type=jnp.float32,
     )
     radiance = radiance + b_radiance[None, :]
     in_use = usable.astype(jnp.float32) * occupied.astype(jnp.float32)
     departure = ((radiance - observed.astype(jnp.float32)) * in_use[:, None]).astype(jnp.bfloat16)
-    all_depart = lax.all_gather(departure, "chan", axis=1, tiled=True)
-    picks = all_depart
     cotangent = jnp.dot(
-        picks,
+        lax.all_gather(departure, "chan", axis=1, tiled=True),
         lax.all_gather(inv_cov, "tile", axis=0, tiled=True),
         preferred_element_type=jnp.float32,
     )
     cotangent = cotangent.astype(jnp.bfloat16)
-    weights = w_radiance
     full_sum = lax.psum(
-        lax.dot_general(
-            weights, cotangent, (((1,), (1,)), ((), ())), preferred_element_type=jnp.float32
-        ),
+        lax.dot_general(w_radiance, cotangent, NT_DIMS, preferred_element_type=jnp.float32),
         "chan",
     )
     grad_hidden = lax.dynamic_slice_in_dim(full_sum, chan_index * hidden_dev, hidden_dev, 0)
@@ -136,7 +137,355 @@
     return adjoint
 
 
+def up_to(value, multiple):
+    return -(-value // multiple) * multiple
+
+
+def in_three(value):
+    high = lax.reduce_precision(value, 8, 7)
+    middle = lax.reduce_precision(value - high, 8, 7)
+    low = lax.reduce_precision(value - high - middle, 8, 7)
+    return [part.astype(jnp.bfloat16) for part in (high, middle, low)]
+
+
+def as_rows(flat, width):
+    length = up_to(flat.shape[0], width)
+    return jnp.pad(flat, (0, length - flat.shape[0])).reshape(-1, width)
+
+
+def flip(value, mask):
+    count = lax.axis_size("chan")
+    return lax.ppermute(value, "chan", [(i, i ^ mask) for i in range(count)])
+
+
+def dot(left, right):
+    return jnp.dot(left, right, preferred_element_type=jnp.float32)
+
+
+def call(kernel, out_shape, args, scalars, scratch=(), flops=0):
+    bytes_accessed = sum(a.size * a.dtype.itemsize for a in args)
+    return pl.pallas_call(
+        kernel,
+        out_shape=out_shape,
+        in_specs=[pl.BlockSpec(memory_space=pltpu.SMEM)] * scalars
+        + [pl.BlockSpec(memory_space=pltpu.VMEM)] * (len(args) - scalars),
+        out_specs=jax.tree.map(lambda _: pl.BlockSpec(memory_space=pltpu.VMEM), out_shape),
+        scratch_shapes=list(scratch),
+        compiler_params=pltpu.CompilerParams(vmem_limit_bytes=VMEM_BYTES),
+        cost_estimate=pl.CostEstimate(
+            flops=flops, bytes_accessed=bytes_accessed, transcendentals=0
+        ),
+    )(*args)
+
+
+def forward_kernel(
+    tiles, group, block, own_cols, order_ref, gathered_ref, spot_ref, place_ref, usable_ref, bias_ref,
+    w_radiance_ref, *rest,
+):
+    observed_refs = rest[:tiles]
+    near_refs = rest[tiles:-4]
+    far_ref, departure_ref, slope_ref, active_ref = rest[-4:]
+    rows = spot_ref.shape[0]
+    chips = len(near_refs)
+    hidden = near_refs[0].shape[1]
+    slots = observed_refs[0].shape[0]
+    row = lax.broadcasted_iota(jnp.int32, (rows, gathered_ref.shape[0]), 0)
+    source = lax.broadcasted_iota(jnp.int32, (rows, gathered_ref.shape[0]), 1)
+    pick = (source == row // own_cols * block + row % own_cols).astype(jnp.bfloat16)
+    columns = dot(pick, gathered_ref[...]).astype(jnp.bfloat16)
+    for chip in range(chips):
+        for member in range(group):
+            k = chip * group + member
+            weights = near_refs[chip][...] if member == 0 else far_ref[member - 1, chip]
+            preact = dot(columns, weights)
+            squash = jax.nn.sigmoid(preact)
+            slope_ref[k] = squash * (1.0 + preact * (1.0 - squash))
+            at = pl.multiple_of(order_ref[k] * hidden, hidden)
+            active_ref[:, pl.ds(at, hidden)] = (preact * squash).astype(jnp.bfloat16)
+    slot = lax.broadcasted_iota(jnp.int32, (rows, slots), 1)
+    in_use = jnp.zeros((rows, 1), jnp.float32)
+    seen = jnp.zeros(departure_ref.shape, jnp.float32)
+    for k in range(tiles):
+        hit = spot_ref[...] == slot + k * slots
+        in_use = in_use + jnp.sum(
+            jnp.where(hit, usable_ref[k : k + 1, :], 0.0), axis=1, keepdims=True
+        )
+        hit = place_ref[...] == slot + k * slots
+        seen = seen + dot(hit.astype(jnp.bfloat16), observed_refs[k][...])
+    radiance = dot(active_ref[...], w_radiance_ref[...]) + bias_ref[...]
+    departure_ref[...] = ((radiance - seen) * in_use).astype(jnp.bfloat16)
+
+
+def backward_kernel(
+    tiles, group, own_cols, steps, order_ref, at_ref, inv_cov_ref, w_radiance_ref, slope_ref, *rest
+):
+    chan_width = w_radiance_ref.shape[1]
+    own_refs, other_ref = rest[: steps], rest[steps]
+    near_refs = rest[steps + 1 : -3]
+    far_ref, out_ref, pre_ref = rest[-3:]
+    chips = len(near_refs)
+    hidden = near_refs[0].shape[1]
+    own = jnp.concatenate([r[...] for r in own_refs], axis=0)
+    rows = own.shape[0]
+    at = pl.multiple_of(at_ref[0] * chan_width, chan_width)
+    cotangent = dot(own, inv_cov_ref[pl.ds(at, chan_width), :])
+    for member in range(1, group):
+        at = pl.multiple_of(at_ref[member] * chan_width, chan_width)
+        cotangent = cotangent + dot(other_ref[member - 1], inv_cov_ref[pl.ds(at, chan_width), :])
+    cotangent = cotangent.astype(jnp.bfloat16)
+    total = jnp.zeros((rows, near_refs[0].shape[0]), jnp.float32)
+    for chip in range(chips):
+        for member in range(group):
+            k = chip * group + member
+            at = pl.multiple_of(order_ref[k] * hidden, hidden)
+            grad_hidden = lax.dot_general(
+                cotangent,
+                w_radiance_ref[pl.ds(at, hidden), :],
+                NT_DIMS,
+                preferred_element_type=jnp.float32,
+            )
+            grad_pre = (grad_hidden * slope_ref[k]).astype(jnp.bfloat16)
+            weights = near_refs[chip][...] if member == 0 else far_ref[member - 1, chip]
+            total = total + lax.dot_general(
+                grad_pre, weights, NT_DIMS, preferred_element_type=jnp.float32
+            )
+    wide = out_ref.shape[0] // tiles
+    per_row = wide // (rows // tiles // own_cols)
+    target = lax.broadcasted_iota(jnp.int32, (out_ref.shape[0], rows), 0)
+    source = lax.broadcasted_iota(jnp.int32, (out_ref.shape[0], rows), 1)
+    tile, inner = target // wide, target % wide
+    row, along = inner // per_row, inner % per_row - 1 + own_cols
+    tile = (tile + along // own_cols - 1 + tiles) % tiles
+    wanted = tile * (rows // tiles) + row * own_cols + along % own_cols
+    pick = (source == wanted).astype(jnp.bfloat16)
+    out_ref[...] = dot(pick, total.astype(jnp.bfloat16)).astype(jnp.bfloat16)
+
+
+def middle_kernel(chans, per_row, in_ref, out_ref):
+    total = in_ref[0].astype(jnp.float32)
+    for k in range(1, in_ref.shape[0]):
+        total = total + in_ref[k].astype(jnp.float32)
+    shape = (out_ref.shape[0], total.shape[0])
+    block = out_ref.shape[0] // chans
+    target = lax.broadcasted_iota(jnp.int32, shape, 0)
+    source = lax.broadcasted_iota(jnp.int32, shape, 1)
+    chan, inner = target // block, target % block
+    wanted = (chan + inner // per_row - 1) * per_row + inner % per_row
+    pick = (source == wanted) & (inner < 3 * per_row)
+    out_ref[...] = dot(pick.astype(jnp.bfloat16), total.astype(jnp.bfloat16)).astype(jnp.bfloat16)
+
+
+def diffuse_kernel(per_row, edge, in_ref, root_ref, out_ref):
+    total = in_ref[0].astype(jnp.float32)
+    for k in range(1, in_ref.shape[0]):
+        total = total + in_ref[k].astype(jnp.float32)
+    cells_across, cells_along, features = out_ref.shape
+    length = cells_along + 2 * edge
+    total = total * 0.0625
+    shape = (length, total.shape[0])
+    cell = lax.broadcasted_iota(jnp.int32, shape, 0)
+    source = lax.broadcasted_iota(jnp.int32, shape, 1)
+    column = (cell - edge + 4) // 4
+    spread = []
+    for k in range(3):
+        pick = (source == column + k * per_row) & (column >= 0) & (column < per_row)
+        spread.append(
+            jnp.dot(
+                pick.astype(jnp.float32),
+                total,
+                precision=lax.Precision.HIGHEST,
+                preferred_element_type=jnp.float32,
+            )
+        )
+    root = root_ref[...]
+    state = [spread[(row + 2) // 4] for row in range(cells_across + 4)]
+    east_of = functools.partial(pltpu.roll, shift=length - 1, axis=0)
+    west_of = functools.partial(pltpu.roll, shift=1, axis=0)
+    root_east, root_west = east_of(root), west_of(root)
+    north = root[:, :-1] * root[:, 1:]
+    east, west = root * root_east, root * root_west
+    for sweep in range(2):
+        fresh = list(state)
+        for row in range(1 + sweep, cells_across + 3 - sweep):
+            here = state[row]
+            fresh[row] = (
+                here
+                + north[:, row : row + 1] * (state[row + 1] - here)
+                + north[:, row - 1 : row] * (state[row - 1] - here)
+                + east[:, row : row + 1] * (east_of(here) - here)
+                + west[:, row : row + 1] * (west_of(here) - here)
+            )
+        state = fresh
+    for row in range(cells_across):
+        out_ref[row] = state[row + 2][edge : edge + cells_along, :features]
+
+
+def body_by_column(
+    fields,
+    diffusivity,
+    owners,
+    observed,
+    usable,
+    w_hidden,
+    b_hidden,
+    w_radiance,
+    b_radiance,
+    inv_cov,
+):
+    tiles = lax.axis_size("tile")
+    chans = lax.axis_size("chan")
+    t = lax.axis_index("tile")
+    c = lax.axis_index("chan")
+    slots = observed.shape[0]
+    capacity = slots // tiles
+    cells_across, cells_along, features = fields.shape
+    own_cols = cells_across // 4 * (cells_along // 4)
+    hidden = w_hidden.shape[1]
+    rows = owners.shape[0]
+    tile_cols = rows // tiles
+    group = chans // tiles
+    chips = chans // group
+    steps = chips.bit_length() - 1
+    width = up_to(features + 3, 16)
+    both = ("tile", "chan")
+
+    w_own = jnp.concatenate(
+        [w_hidden]
+        + [part[None, :] for part in in_three(b_hidden)]
+        + [jnp.zeros((width - features - 3, hidden), jnp.bfloat16)],
+        axis=0,
+    )
+    near = [w_own] + [flip(w_own, k * group) for k in range(1, chips)]
+
+    seen = [observed]
+    for k in range(1, tiles):
+        pairs = [
+            ((j // group + k) % tiles * chans + j, j // group * chans + j) for j in range(chans)
+        ]
+        seen.append(lax.ppermute(observed, both, pairs))
+
+    grouped = fields.reshape(cells_across // 4, 4, cells_along // 4, 4, features)
+    averaged = (jnp.sum(grouped, axis=(1, 3)) * 0.0625).reshape(own_cols, features)
+    columns = jnp.concatenate(
+        [
+            averaged.astype(jnp.bfloat16),
+            jnp.ones((own_cols, 3), jnp.bfloat16),
+            jnp.zeros((own_cols, width - features - 3), jnp.bfloat16),
+        ],
+        axis=1,
+    )
+    cells = as_rows(jnp.concatenate(in_three(diffusivity.reshape(-1))), width)
+    flags = as_rows(usable.astype(jnp.bfloat16), width)
+    block = up_to(own_cols + cells.shape[0] + flags.shape[0], 16)
+    packed = jnp.concatenate([columns, cells, flags], axis=0)
+    packed = jnp.pad(packed, ((0, block - packed.shape[0]), (0, 0)))
+    gathered = lax.all_gather(packed, both, axis=0, tiled=True)
+
+    stack = jnp.stack(near)
+    far = jnp.stack([flip(stack, k) for k in range(1, group)])
+
+    owner = owners[:, 0]
+    number = jnp.arange(rows, dtype=jnp.int32)
+    same = (
+        (owner[:, None] == owner[None, :])
+        & (number[:, None] // tile_cols == number[None, :] // tile_cols)
+        & (number[None, :] < number[:, None])
+    )
+    rank = jnp.sum(same.astype(jnp.int32), axis=1, keepdims=True)
+    within = number[:, None] // tile_cols * capacity + rank
+    spot = owners * slots + within
+    place = (owners + tiles - t) % tiles * slots + within
+    order = jnp.bitwise_xor(jnp.arange(chans, dtype=jnp.int32), c)
+
+    by_device = gathered.reshape(tiles, chans, block, width)
+    low = own_cols + cells.shape[0]
+    usable_all = by_device[:, 0, low : low + flags.shape[0]].reshape(tiles, -1)[:, :slots]
+    usable_all = usable_all.astype(jnp.float32)
+
+    departure, slope = call(
+        functools.partial(forward_kernel, tiles, group, block, own_cols),
+        (
+            jax.ShapeDtypeStruct((rows, observed.shape[1]), jnp.bfloat16),
+            jax.ShapeDtypeStruct((chans, rows, hidden), jnp.float32),
+        ),
+        [order, gathered, spot, place, usable_all, b_radiance[None, :], w_radiance]
+        + seen
+        + near
+        + [far],
+        1,
+        scratch=[pltpu.VMEM((rows, hidden * chans), jnp.bfloat16)],
+        flops=2 * rows * hidden * chans * (width + observed.shape[1]),
+    )
+
+    parts = jnp.split(departure, steps, axis=0)
+    source = lax.div(c, jnp.int32(group)) ^ t
+    for step in range(steps):
+        moved = []
+        for j in range(steps):
+            reached = sum(1 << (j + k) % steps for k in range(step))
+            bit = 1 << (j + step) % steps
+            pairs = [
+                (a * chans + b, a * chans + (b ^ bit * group))
+                for a in range(tiles)
+                for b in range(chans)
+                if (b // group ^ a) & ~reached == 0
+            ]
+            arrived = lax.ppermute(parts[j], both, pairs)
+            is_new = (source & ~jnp.int32(reached)) == bit
+            moved.append(jnp.where(is_new, arrived, parts[j]))
+        parts = moved
+    joined = jnp.concatenate(parts, axis=0)
+    others = jnp.stack([flip(joined, k) for k in range(1, group)])
+    at = jnp.bitwise_xor(jnp.arange(group, dtype=jnp.int32), c % group)
+
+    per_row = own_cols + 2
+    partial = call(
+        functools.partial(backward_kernel, tiles, group, own_cols, steps),
+        jax.ShapeDtypeStruct((tiles * chans * per_row, width), jnp.bfloat16),
+        [order, at, inv_cov, w_radiance, slope] + parts + [others] + near + [far],
+        2,
+        scratch=[pltpu.VMEM((16, 128), jnp.bfloat16)],
+        flops=2 * rows * (hidden * chans * (width + observed.shape[1]) + inv_cov.size),
+    )
+    partial = lax.all_to_all(
+        partial.reshape(tiles, chans * per_row, width), "tile", 0, 0, tiled=True
+    )
+    room = up_to(3 * per_row, 16)
+    partial = call(
+        functools.partial(middle_kernel, chans, per_row),
+        jax.ShapeDtypeStruct((chans * room, width), jnp.bfloat16),
+        [partial],
+        0,
+        flops=2 * chans * room * chans * per_row * width,
+    )
+    partial = lax.all_to_all(partial.reshape(chans, room, width), "chan", 0, 0, tiled=True)
+
+    edge = 8
+    cell_rows = by_device[:, :, own_cols:low].reshape(tiles, chans, -1)
+    cell_rows = cell_rows[:, :, : 3 * cells_across * cells_along].astype(jnp.float32)
+    kappa = jnp.sum(cell_rows.reshape(tiles, chans, 3, cells_across, cells_along), axis=2)
+    kappa = kappa.transpose(0, 3, 1, 2).reshape(tiles * cells_along, chans * cells_across)
+    kappa = jnp.concatenate([kappa[-edge:], kappa, kappa[:edge]], axis=0)
+    kappa = jnp.pad(kappa, ((0, 0), (2, 2)))
+    root = jnp.sqrt(
+        lax.dynamic_slice(
+            kappa,
+            (t * cells_along, c * cells_across),
+            (cells_along + 2 * edge, cells_across + 4),
+        )
+    )
+    return call(
+        functools.partial(diffuse_kernel, per_row, edge),
+        jax.ShapeDtypeStruct(fields.shape, jnp.float32),
+        [partial, root],
+        0,
+        flops=100 * fields.size,
+    )
+
+
 def solution(mesh):
+    tiles, chans = mesh.shape["tile"], mesh.shape["chan"]
+    by_column = chans % tiles == 0 and chans & (chans - 1) == 0 and chans // tiles > 1
     placed = (
         P("chan", "tile", None),
         P("chan", "tile"),
@@ -150,5 +499,9 @@
         P("tile", "chan"),
     )
     return jax.shard_map(
-        body, mesh=mesh, in_specs=placed, out_specs=P("chan", "tile", None), check_vma=False
-    )
+        body_by_column if by_column else body_by_owner,
+        mesh=mesh,
+        in_specs=placed,
+        out_specs=P("chan", "tile", None),
+        check_vma=False,
+    )

time: 388 us -> 156 us (0.40); the launches traced: 382 us -> 154 us
  waiting for transfers between devices: 289 us -> 24.4 us
  local copies, waits for them, and re-layouts: 2.52 us -> 27.5 us
  blocking collectives: 21.6 us -> 43.6 us
  matrix products: 14.2 us -> 0 us
  between operations: 13.4 us -> 0.24 us
  Pallas kernels: 0 us -> 12.3 us
  other arithmetic: 9.02 us -> 20.6 us
  starting transfers between devices: 32.2 us -> 25.8 us
    all_gather x2 -> x0, waiting for transfers between devices: 192 us -> none  [the longest x1 168 us: body(): lax.all_gather(inv_cov, 'tile', axis=0, tiled=True)]
    psum x1 -> x0, waiting for transfers between devices: 50.6 us -> none  [body(): lax.psum(lax.dot_general(weights, cotangent, (((1,), (1,)), ((), ())), pr...]
    reduce_scatter x1 -> x0, waiting for transfers between devices: 28.2 us -> none  [body(): lax.psum_scatter(jnp.take(returned, slot_of, axis=0), 'chan', scatter_dim...]
    all_gather x2 -> x1, blocking collectives: 21.6 us -> 43.6 us  [body_by_column(): gathered = lax.all_gather(packed, both, axis=0, tiled=True)]
    dot_general x5 -> x0, matrix products: 14.2 us -> none  [the longest x1 8.09 us: body(): lax.dot_general(weights, cotangent, (((1,), (1,)), ((), ())), preferred_e...]
    pallas_call x0 -> x4, Pallas kernels: none -> 12.3 us  [call(): pl.pallas_call(kernel, out_shape=out_shape, in_specs=[pl.BlockSpec(memory...]
    unnamed x13 -> x30, local copies, waits for them, and re-layouts: 0.54 us -> 11.3 us
    ppermute x12, waiting for transfers between devices: 4.14 us -> 8.23 us  [the longest x4 7.75 us: body_by_column(): arrived = lax.ppermute(parts[j], both, pairs)]
  transfers between devices with their start and end apart: 18 -> 14, of which waited for: 9 -> 7; matrix products, arithmetic and copies ran while one was open for 1% -> 19% of each run, Pallas kernels for 0% -> 0%
where the time goes in v1:
time: 156 us; the launch traced here: 154 us
  blocking collectives  43.6 us (28%)
  local copies, waits for them, and re-layouts  27.5 us (18%)
  starting transfers between devices  25.8 us (17%)
  waiting for transfers between devices  24.4 us (16%)
  other arithmetic  20.6 us (13%)
  Pallas kernels  12.3 us (8%)
    all_gather x1, blocking collectives, body_by_column(): gathered = lax.all_gather(packed, both, axis=0, tiled=True)  43.6 us
    pallas_call x4, Pallas kernels, call(): pl.pallas_call(kernel, out_shape=out_shape, in_specs=[pl.BlockSpec(memory...  12.3 us
    unnamed x30, local copies, waits for them, and re-layouts  11.3 us
    ppermute x4, starting transfers between devices, body_by_column(): arrived = lax.ppermute(parts[j], both, pairs)  10.5 us
    all_to_all x1, waiting for transfers between devices, body_by_column(): lax.all_to_all(partial.reshape(tiles, chans * per_row, width), 'tile', 0,...  9.64 us
    ppermute x4, waiting for transfers between devices, body_by_column(): arrived = lax.ppermute(parts[j], both, pairs)  7.75 us
    all_to_all x1, waiting for transfers between devices, body_by_column(): lax.all_to_all(partial.reshape(chans, room, width), 'chan', 0, 0, tiled=T...  6.58 us
    ppermute x5, starting transfers between devices, flip(): return lax.ppermute(value, 'chan', [(i, i ^ mask) for i in range(count)])  4.55 us
  transfers between devices with their start and end apart: 14, of which 7 were waited for; matrix products, arithmetic and copies ran while one was open for 19% of the time, Pallas kernels for 0%

profile of v1, /device:TPU:0, one launch (start us, length us, event | category | flops | bytes accessed | tf_op | source)
XLA Modules:
  0.0 154.4 jit_solution(12104813663560538814)
XLA Ops:
  0.0 0.8 fusion.24
  1.4 0.6 broadcast_in_dim.23
  2.0 0.6 broadcast_in_dim.24
  2.6 0.6 broadcast_in_dim.25
  3.2 1.7 %concatenate.21.rest_4_.rest_3_ = bf16[416,256]{1,0:T(8,128)(2,1)S(1)} concatenate(bf16[411,256]{1,0:T(8,128)(2,1)} %param.15, bf16[1,256]{1,0:T(2,128)(2,1)} %broadcast_in_dim.22, bf16[1,256]{1,0:T(2,128)(2,1)} %broadcast_in_dim.23, bf16[1,256]{1,0:T(2,128)(2,1)} %broadcast_in_dim.24, bf16[2,256]{1,0:T(2,128)(2,1)} %broadcast_in_dim.25), dimensions={0} | concatenate | bytes 425984 | tf_op jit(solution)/shard_map/concatenate | solution.py:352
  4.8 3.0 %collective-permute-start.3 = (bf16[416,256]{1,0:T(8,128)(2,1)S(1)}, bf16[416,256]{1,0:T(8,128)(2,1)}, u32[]{:S(2)}, u32[]{:S(2)}) collective-permute-start(bf16[416,256]{1,0:T(8,128)(2,1)S(1)} %concatenate.21.rest_4_.rest_3_), channel_id=1, source_target_pairs={{0,2},{1,3},{2,0},{3,1},{4,6},{5,7},{6,4},{7,5},{8,10},{9,11},{10,... | collective-permute-start | bytes 638984 | tf_op jit(solution)/shard_map/ppermute | solution.py:158
  7.8 1.5 collective-permute-start.4
  9.4 1.3 collective-permute-start
  10.7 1.3 collective-permute-start.1
  12.6 1.2 broadcast_multiply_fusion
  13.8 1.3 broadcast_compare_fusion
  15.1 1.5 copy.93
  16.5 1.4 copy.96
  17.9 1.5 %convert_reduce_fusion = s32[256]{0:T(256)} fusion(s32[256]{0:T(256)} %and_select_fusion, s32[256]{0:T(256)} %bitcast.26), kind=kLoop, calls=%fused_computation.2 | loop fusion | flops 458496 | bytes 3072 | tf_op jit(solution)/shard_map/reduce_sum | solution.py:394
  19.5 1.5 copy.89
  21.0 1.4 copy.90
  22.4 1.3 reshape.147
  23.7 0.7 reduce-precision_convert_fusion.3
  25.0 1.6 %reduce_sum.36 = f32[32,411]{1,0:T(8,128)} reduce(f32[4,32,411]{2,1,0:T(8,128)} %param.10, f32[]{:T(128)} %constant.79.clone.1), dimensions={0}, to_apply=%region_0.0 | reduce | flops 39456 | bytes 263044 | tf_op jit(solution)/shard_map/reduce_sum | solution.py:368
  26.6 1.5 reduce_sum.37
  28.1 1.5 reduce_sum.38
  29.5 0.7 convert_element_type.43
  30.2 0.7 multiply_convert_fusion
  30.9 1.3 collective-permute-start.2
  32.3 2.2 %pad_maximum_fusion = bf16[4,416,256]{2,1,0:T(8,128)(2,1)} fusion(bf16[1,416,256]{2,1,0:T(8,128)(2,1)} %bitcast.7, bf16[1,416,256]{2,1,0:T(8,128)(2,1)} %bitcast.6, bf16[1,416,256]{2,1,0:T(8,128)(2,1)} %bitcast.5, bf16[1,416,256]{2,1,0:T(8,128)(2,1)S(1)} %bitcast.20), kind=kLoop, calls=%fused_computation | loop fusion | flops 1277952 | bytes 1703936 | tf_op jit(solution)/shard_map/stack | solution.py:384
  34.4 0.7 fusion.19
  35.2 43.6 %all_gather.3.gathered_ref = bf16[512,416]{1,0:T(8,128)(2,1)S(1)} all-gather(bf16[16,416]{1,0:T(8,128)(2,1)S(1)} %fusion.19), channel_id=1, replica_groups=mesh['tile'=4,'chan'=8] {'tile','chan'}, dimensions={0}, use_global_device_ids=true | all-gather | bytes 439296 | tf_op jit(solution)/shard_map/all_gather | solution.py:382
  78.8 0.8 copy-done.1
  79.6 0.6 copy.114
  80.2 0.7 broadcast_in_dim.10.bias_ref
  80.9 1.1 fusion.5
  82.1 0.7 slice_convert_fusion.1.usable_ref
  82.8 1.0 copy-done.2
  83.8 4.2 %shard_map.100 = (bf16[256,768]{1,0:T(8,128)(2,1)S(1)}, f32[8,256,256]{2,1,0:T(8,128)S(1)}) custom-call(s32[8]{0:T(128)S(1)} %iota_xor_fusion.1.order_ref, bf16[512,416]{1,0:T(8,128)(2,1)S(1)} %copy-done.2, s32[256,1]{1,0:T(8,128)S(1)} %get-tuple-element.16.spot_ref, s32[256,1]{1,0:T(8,128)S(1)} %get-tuple-element.15.place_ref, ...), custom_call_target="tpu_custom_call" | custom-call | flops 1241513984 | bytes 6069280 | tf_op jit(solution)/shard_map/pallas_call | solution.py:167
  88.1 1.3 copy-done.4
  89.4 0.7 copy-done.8
  90.2 0.7 fusion.29
  90.9 2.0 %collective-permute-start.7 = (bf16[128,768]{1,0:T(8,128)(2,1)}, bf16[128,768]{1,0:T(8,128)(2,1)}, u32[]{:S(2)}, u32[]{:S(2)}) collective-permute-start(bf16[128,768]{1,0:T(8,128)(2,1)} %get-tuple-element.14), channel_id=1, source_target_pairs={{0,2},{1,3},{10,8},{11,9},{20,22},{21,23},{30,28},{31,29}} | collective-permute-start | bytes 589832 | tf_op jit(solution)/shard_map/ppermute | solution.py:433
  92.8 2.0 %collective-permute-start.9 = (bf16[128,768]{1,0:T(8,128)(2,1)S(1)}, bf16[128,768]{1,0:T(8,128)(2,1)}, u32[]{:S(2)}, u32[]{:S(2)}) collective-permute-start(bf16[128,768]{1,0:T(8,128)(2,1)S(1)} %get-tuple-element.13), channel_id=1, source_target_pairs={{0,4},{1,5},{10,14},{11,15},{20,16},{21,17},{30,26},{31,27}} | collective-permute-start | bytes 589832 | tf_op jit(solution)/shard_map/ppermute | solution.py:433
  94.8 2.6 %collective-permute-done.7 = bf16[128,768]{1,0:T(8,128)(2,1)} collective-permute-done((bf16[128,768]{1,0:T(8,128)(2,1)}, bf16[128,768]{1,0:T(8,128)(2,1)}, u32[]{:S(2)}, u32[]{:S(2)}) %collective-permute-start.7) | collective-permute-done | bytes 196640 | tf_op jit(solution)/shard_map/ppermute | solution.py:433
  97.4 1.7 %collective-permute-done.9 = bf16[128,768]{1,0:T(8,128)(2,1)} collective-permute-done((bf16[128,768]{1,0:T(8,128)(2,1)S(1)}, bf16[128,768]{1,0:T(8,128)(2,1)}, u32[]{:S(2)}, u32[]{:S(2)}) %collective-permute-start.9) | collective-permute-done | bytes 196640 | tf_op jit(solution)/shard_map/ppermute | solution.py:433
  99.0 1.7 %broadcast_select_fusion = (bf16[128,768]{1,0:T(8,128)(2,1)S(1)}, bf16[128,768]{1,0:T(8,128)(2,1)}) fusion(bf16[128,768]{1,0:T(8,128)(2,1)} %collective-permute-done.9, pred[]{:T(512)S(6)} %eq.54, bf16[256,768]{1,0:T(8,128)(2,1)} %copy-done.8, bf16[128,768]{1,0:T(8,128)(2,1)} %collective-permute-done.7, pred[]{:T(512)S(6)} %eq.52), kind=kLoop, calls=%fused_computation.12 | loop fusion | flops 196608 | bytes 1179650 | tf_op jit(solution)/shard_map/jit(_where)/select_n | solution.py:435
  100.8 3.5 %collective-permute-start.10 = (bf16[128,768]{1,0:T(8,128)(2,1)S(1)}, bf16[128,768]{1,0:T(8,128)(2,1)}, u32[]{:S(2)}, u32[]{:S(2)}) collective-permute-start(bf16[128,768]{1,0:T(8,128)(2,1)S(1)} %get-tuple-element.11), channel_id=1, source_target_pairs={{0,2},{1,3},{4,6},{5,7},{10,8},{11,9},{14,12},{15,13},{16,18},{17,... | collective-permute-start | bytes 589832 | tf_op jit(solution)/shard_map/ppermute | solution.py:433
  104.3 3.0 %collective-permute-start.8 = (bf16[128,768]{1,0:T(8,128)(2,1)}, bf16[128,768]{1,0:T(8,128)(2,1)S(1)}, u32[]{:S(2)}, u32[]{:S(2)}) collective-permute-start(bf16[128,768]{1,0:T(8,128)(2,1)} %get-tuple-element.12), channel_id=1, source_target_pairs={{0,4},{1,5},{2,6},{3,7},{8,12},{9,13},{10,14},{11,15},{20,16},{21,... | collective-permute-start | bytes 589832 | tf_op jit(solution)/shard_map/ppermute | solution.py:433
  107.8 1.0 broadcast_select_fusion.1.rest_1_
  108.7 3.1 %collective-permute-done.8 = bf16[128,768]{1,0:T(8,128)(2,1)S(1)} collective-permute-done((bf16[128,768]{1,0:T(8,128)(2,1)}, bf16[128,768]{1,0:T(8,128)(2,1)S(1)}, u32[]{:S(2)}, u32[]{:S(2)}) %collective-permute-start.8) | collective-permute-done | bytes 196640 | tf_op jit(solution)/shard_map/ppermute | solution.py:433
  111.8 0.9 broadcast_select_fusion.3.rest_0_
  112.8 0.8 pad_maximum_fusion.1
  113.6 0.7 copy-done.6
  114.2 1.0 slice.26
  115.2 0.6 copy.113
  116.3 1.7 %copy-done.3 = bf16[1536,768]{1,0:T(8,128)(2,1)S(1)} copy-done((bf16[1536,768]{1,0:T(8,128)(2,1)S(1)}, bf16[1536,768]{1,0:T(8,128)(2,1)}, u32[]{:S(2)}) %copy-start.3) | copy-done | bytes 2359320
  118.0 1.6 %copy-done.5 = f32[8,256,256]{2,1,0:T(8,128)S(1)} copy-done((f32[8,256,256]{2,1,0:T(8,128)S(1)}, f32[8,256,256]{2,1,0:T(8,128)}, u32[]{:S(2)}) %copy-start.5) | copy-done | bytes 2097176
  119.6 0.9 copy-done.7
  120.5 0.6 copy-done.12
  121.1 5.7 %shard_map.101 = bf16[320,416]{1,0:T(8,128)(2,1)S(1)} custom-call(s32[8]{0:T(128)S(1)} %copy-done.12, s32[2]{0:T(128)S(1)} %iota_xor_fusion.at_ref, bf16[1536,768]{1,0:T(8,128)(2,1)S(1)} %copy-done.3, bf16[2048,768]{1,0:T(8,128)(2,1)S(1)} %copy-done, f32[8,256,256]{2,1,0:T(8,128)S(1)} %copy-done.5, bf16[128,768]{1,0:T(8,128)(2,1)S(1)} %copy-done.7, ...), custom_call_target="tpu_custom_call" | custom-call | flops 1845493760 | bytes 10092584 | tf_op jit(solution)/shard_map/pallas_call | solution.py:167
  126.8 0.7 copy-done.9
  127.5 3.5 %all-to-all-start = ((bf16[4,80,416]{2,1,0:T(8,128)(2,1)}), bf16[4,80,416]{2,1,0:T(8,128)(2,1)S(1)}, u32[]{:S(2)}, u32[]{:S(2)}) async-start(bf16[4,80,416]{2,1,0:T(8,128)(2,1)} %bitcast.23), calls=%async_computation | async-start | bytes 655360 | tf_op jit(solution)/shard_map/all_to_all | solution.py:450
  131.0 0.7 slice_convert_fusion
  132.2 9.6 %all-to-all-done.in_ref = bf16[4,80,416]{2,1,0:T(8,128)(2,1)S(1)} async-done(((bf16[4,80,416]{2,1,0:T(8,128)(2,1)}), bf16[4,80,416]{2,1,0:T(8,128)(2,1)S(1)}, u32[]{:S(2)}, u32[]{:S(2)}) %all-to-all-start) | async-done | bytes 266272 | tf_op jit(solution)/shard_map/all_to_all | solution.py:450
  141.8 1.0 shard_map.102
  142.8 3.4 %all-to-all-start.1 = ((bf16[8,32,416]{2,1,0:T(8,128)(2,1)}), bf16[8,32,416]{2,1,0:T(8,128)(2,1)S(1)}, u32[]{:S(2)}, u32[]{:S(2)}) async-start(bf16[8,32,416]{2,1,0:T(8,128)(2,1)} %bitcast.11), calls=%async_computation.1 | async-start | bytes 524288 | tf_op jit(solution)/shard_map/all_to_all | solution.py:461
  146.5 6.6 %all-to-all-done.1.in_ref = bf16[8,32,416]{2,1,0:T(8,128)(2,1)S(1)} async-done(((bf16[8,32,416]{2,1,0:T(8,128)(2,1)}), bf16[8,32,416]{2,1,0:T(8,128)(2,1)S(1)}, u32[]{:S(2)}, u32[]{:S(2)}) %all-to-all-start.1) | async-done | bytes 213024 | tf_op jit(solution)/shard_map/all_to_all | solution.py:461
  153.1 1.4 shard_map.103
  (49 shorter events, 3.4 us)
Async XLA Ops:
  0.0 82.7 %copy-start.10 = (bf16[128,768]{1,0:T(8,128)(2,1)S(1)}, bf16[128,768]{1,0:T(8,128)(2,1)}, u32[]{:S(2)}) copy-start(bf16[128,768]{1,0:T(8,128)(2,1)} %rest_0_.1) | copy-start | bytes 589828
  0.0 82.8 %copy-start = (bf16[2048,768]{1,0:T(8,128)(2,1)S(1)}, bf16[2048,768]{1,0:T(8,128)(2,1)}, u32[]{:S(2)}) copy-start(bf16[2048,768]{1,0:T(8,128)(2,1)} %w_radiance_ref.3) | copy-start | bytes 9437188
  4.8 26.1 %collective-permute-start.3 = (bf16[416,256]{1,0:T(8,128)(2,1)S(1)}, bf16[416,256]{1,0:T(8,128)(2,1)}, u32[]{:S(2)}, u32[]{:S(2)}) collective-permute-start(bf16[416,256]{1,0:T(8,128)(2,1)S(1)} %concatenate.21.rest_4_.rest_3_), channel_id=1, source_target_pairs={{0,2},{1,3},{2,0},{3,1},{4,6},{5,7},{6,4},{7,5},{8,10},{9,11},{10,... | collective-permute-start | bytes 638984 | tf_op jit(solution)/shard_map/ppermute | solution.py:158
  7.8 24.4 %collective-permute-start.4 = (bf16[416,256]{1,0:T(8,128)(2,1)S(1)}, bf16[416,256]{1,0:T(8,128)(2,1)}, u32[]{:S(2)}, u32[]{:S(2)}) collective-permute-start(bf16[416,256]{1,0:T(8,128)(2,1)S(1)} %concatenate.21.rest_4_.rest_3_), channel_id=1, source_target_pairs={{0,4},{1,5},{2,6},{3,7},{4,0},{5,1},{6,2},{7,3},{8,12},{9,13},{10,... | collective-permute-start | bytes 638984 | tf_op jit(solution)/shard_map/ppermute | solution.py:158
  9.4 22.9 %collective-permute-start.5 = (bf16[416,256]{1,0:T(8,128)(2,1)S(1)}, bf16[416,256]{1,0:T(8,128)(2,1)}, u32[]{:S(2)}, u32[]{:S(2)}) collective-permute-start(bf16[416,256]{1,0:T(8,128)(2,1)S(1)} %concatenate.21.rest_4_.rest_3_), channel_id=1, source_target_pairs={{0,6},{1,7},{2,4},{3,5},{4,2},{5,3},{6,0},{7,1},{8,14},{9,15},{10,... | collective-permute-start | bytes 638984 | tf_op jit(solution)/shard_map/ppermute | solution.py:158
  9.4 73.3 %collective-permute-start = (bf16[128,768]{1,0:T(8,128)(2,1)}, bf16[128,768]{1,0:T(8,128)(2,1)}, u32[]{:S(2)}, u32[]{:S(2)}) collective-permute-start(bf16[128,768]{1,0:T(8,128)(2,1)} %rest_0_.1), channel_id=1, source_target_pairs={{8,0},{9,1},{18,10},{19,11},{28,20},{29,21},{6,30},{7,31}} | collective-permute-start | bytes 589832 | tf_op jit(solution)/shard_map/ppermute | solution.py:365
  10.7 72.1 %collective-permute-start.1 = (bf16[128,768]{1,0:T(8,128)(2,1)}, bf16[128,768]{1,0:T(8,128)(2,1)}, u32[]{:S(2)}, u32[]{:S(2)}) collective-permute-start(bf16[128,768]{1,0:T(8,128)(2,1)} %rest_0_.1), channel_id=1, source_target_pairs={{16,0},{17,1},{26,10},{27,11},{4,20},{5,21},{14,30},{15,31}} | collective-permute-start | bytes 589832 | tf_op jit(solution)/shard_map/ppermute | solution.py:365
  30.9 51.8 %collective-permute-start.2 = (bf16[128,768]{1,0:T(8,128)(2,1)}, bf16[128,768]{1,0:T(8,128)(2,1)}, u32[]{:S(2)}, u32[]{:S(2)}) collective-permute-start(bf16[128,768]{1,0:T(8,128)(2,1)} %rest_0_.1), channel_id=1, source_target_pairs={{24,0},{25,1},{2,10},{3,11},{12,20},{13,21},{22,30},{23,31}} | collective-permute-start | bytes 589832 | tf_op jit(solution)/shard_map/ppermute | solution.py:365
  34.4 48.3 %collective-permute-start.6 = (bf16[4,416,256]{2,1,0:T(8,128)(2,1)}, bf16[4,416,256]{2,1,0:T(8,128)(2,1)}, u32[]{:S(2)}, u32[]{:S(2)}) collective-permute-start(bf16[4,416,256]{2,1,0:T(8,128)(2,1)} %pad_maximum_fusion), channel_id=1, source_target_pairs={{0,1},{1,0},{2,3},{3,2},{4,5},{5,4},{6,7},{7,6},{8,9},{9,8},{10,11... | collective-permute-start | bytes 2555912 | tf_op jit(solution)/shard_map/ppermute | solution.py:158
  78.8 0.8 copy-start.1
  80.9 7.1 %copy-start.11 = (s32[8]{0:T(128)}, s32[8]{0:T(128)S(1)}, u32[]{:S(2)}) copy-start(s32[8]{0:T(128)S(1)} %iota_xor_fusion.1.order_ref) | copy-start | bytes 100
  82.8 1.0 copy-start.2
  88.1 1.3 copy-start.4
  89.4 0.8 copy-start.8
  90.9 6.5 %collective-permute-start.7 = (bf16[128,768]{1,0:T(8,128)(2,1)}, bf16[128,768]{1,0:T(8,128)(2,1)}, u32[]{:S(2)}, u32[]{:S(2)}) collective-permute-start(bf16[128,768]{1,0:T(8,128)(2,1)} %get-tuple-element.14), channel_id=1, source_target_pairs={{0,2},{1,3},{10,8},{11,9},{20,22},{21,23},{30,28},{31,29}} | collective-permute-start | bytes 589832 | tf_op jit(solution)/shard_map/ppermute | solution.py:433
  92.8 6.2 %collective-permute-start.9 = (bf16[128,768]{1,0:T(8,128)(2,1)S(1)}, bf16[128,768]{1,0:T(8,128)(2,1)}, u32[]{:S(2)}, u32[]{:S(2)}) collective-permute-start(bf16[128,768]{1,0:T(8,128)(2,1)S(1)} %get-tuple-element.13), channel_id=1, source_target_pairs={{0,4},{1,5},{10,14},{11,15},{20,16},{21,17},{30,26},{31,27}} | collective-permute-start | bytes 589832 | tf_op jit(solution)/shard_map/ppermute | solution.py:433
  100.8 6.6 %copy-start.13 = (bf16[128,768]{1,0:T(8,128)(2,1)}, bf16[128,768]{1,0:T(8,128)(2,1)S(1)}, u32[]{:S(2)}) copy-start(bf16[128,768]{1,0:T(8,128)(2,1)S(1)} %get-tuple-element.11) | copy-start | bytes 589828
  100.8 7.0 %collective-permute-start.10 = (bf16[128,768]{1,0:T(8,128)(2,1)S(1)}, bf16[128,768]{1,0:T(8,128)(2,1)}, u32[]{:S(2)}, u32[]{:S(2)}) collective-permute-start(bf16[128,768]{1,0:T(8,128)(2,1)S(1)} %get-tuple-element.11), channel_id=1, source_target_pairs={{0,2},{1,3},{4,6},{5,7},{10,8},{11,9},{14,12},{15,13},{16,18},{17,... | collective-permute-start | bytes 589832 | tf_op jit(solution)/shard_map/ppermute | solution.py:433
  104.3 7.5 %collective-permute-start.8 = (bf16[128,768]{1,0:T(8,128)(2,1)}, bf16[128,768]{1,0:T(8,128)(2,1)S(1)}, u32[]{:S(2)}, u32[]{:S(2)}) collective-permute-start(bf16[128,768]{1,0:T(8,128)(2,1)} %get-tuple-element.12), channel_id=1, source_target_pairs={{0,4},{1,5},{2,6},{3,7},{8,12},{9,13},{10,14},{11,15},{20,16},{21,... | collective-permute-start | bytes 589832 | tf_op jit(solution)/shard_map/ppermute | solution.py:433
  113.6 0.7 copy-start.6
  114.2 2.1 %collective-permute-start.11 = (bf16[256,768]{1,0:T(8,128)(2,1)}, bf16[256,768]{1,0:T(8,128)(2,1)}, u32[]{:S(2)}, u32[]{:S(2)}) collective-permute-start(bf16[256,768]{1,0:T(8,128)(2,1)} %pad_maximum_fusion.1), channel_id=1, source_target_pairs={{0,1},{1,0},{2,3},{3,2},{4,5},{5,4},{6,7},{7,6},{8,9},{9,8},{10,11... | collective-permute-start | bytes 1179656 | tf_op jit(solution)/shard_map/ppermute | solution.py:158
  116.3 1.7 %copy-start.3 = (bf16[1536,768]{1,0:T(8,128)(2,1)S(1)}, bf16[1536,768]{1,0:T(8,128)(2,1)}, u32[]{:S(2)}) copy-start(bf16[1536,768]{1,0:T(8,128)(2,1)} %inv_cov_ref.1) | copy-start | bytes 7077892
  118.0 1.6 %copy-start.5 = (f32[8,256,256]{2,1,0:T(8,128)S(1)}, f32[8,256,256]{2,1,0:T(8,128)}, u32[]{:S(2)}) copy-start(f32[8,256,256]{2,1,0:T(8,128)} %copy-done.4) | copy-start | bytes 6291460
  119.6 0.9 copy-start.7
  120.5 0.6 copy-start.12
  126.8 0.7 copy-start.9
  127.5 14.3 %all-to-all-start = ((bf16[4,80,416]{2,1,0:T(8,128)(2,1)}), bf16[4,80,416]{2,1,0:T(8,128)(2,1)S(1)}, u32[]{:S(2)}, u32[]{:S(2)}) async-start(bf16[4,80,416]{2,1,0:T(8,128)(2,1)} %bitcast.23), calls=%async_computation | async-start | bytes 655360 | tf_op jit(solution)/shard_map/all_to_all | solution.py:450
  142.8 10.3 %all-to-all-start.1 = ((bf16[8,32,416]{2,1,0:T(8,128)(2,1)}), bf16[8,32,416]{2,1,0:T(8,128)(2,1)S(1)}, u32[]{:S(2)}, u32[]{:S(2)}) async-start(bf16[8,32,416]{2,1,0:T(8,128)(2,1)} %bitcast.11), calls=%async_computation.1 | async-start | bytes 524288 | tf_op jit(solution)/shard_map/all_to_all | solution.py:461

commit v2 on v0

--- a/solution.py
+++ b/solution.py
@@ -1,7 +1,14 @@
+import functools
+
 import jax
 import jax.numpy as jnp
 from jax import lax
+from jax.experimental import pallas as pl
+from jax.experimental.pallas import tpu as pltpu
 from jax.sharding import PartitionSpec as P
+
+VMEM_BYTES = 24 * 1024 * 1024
+NT_DIMS = (((1,), (1,)), ((), ()))
 
 
 def padded_2(value, sides, width, wrap):
@@ -22,7 +29,7 @@
     return padded_2(rowwise, (("tile", 1),), 1, True)
 
 
-def body(
+def body_by_owner(
     fields,
     diffusivity,
     owners,
@@ -64,9 +71,8 @@
     placer = (slot_of[None, :] == jnp.arange(slot_count, dtype=jnp.int32)[:, None]).astype(
         jnp.bfloat16
     )
-    picks = placer
     outgoing = jnp.dot(
-        picks,
+        placer,
         lax.all_gather(columns, "chan", axis=0, tiled=True),
         preferred_element_type=jnp.float32,
     )
@@ -79,29 +85,23 @@
     preact = preact + b_hidden[:, None]
     squash = jax.nn.sigmoid(preact)
     active = (preact * squash).astype(jnp.bfloat16)
-    weights = w_radiance
     radiance = lax.dot_general(
         lax.all_gather(active, "chan", axis=0, tiled=True),
-        weights,
+        w_radiance,
         (((0,), (0,)), ((), ())),
         preferred_element_type=jnp.float32,
     )
     radiance = radiance + b_radiance[None, :]
     in_use = usable.astype(jnp.float32) * occupied.astype(jnp.float32)
     departure = ((radiance - observed.astype(jnp.float32)) * in_use[:, None]).astype(jnp.bfloat16)
-    all_depart = lax.all_gather(departure, "chan", axis=1, tiled=True)
-    picks = all_depart
     cotangent = jnp.dot(
-        picks,
+        lax.all_gather(departure, "chan", axis=1, tiled=True),
         lax.all_gather(inv_cov, "tile", axis=0, tiled=True),
         preferred_element_type=jnp.float32,
     )
     cotangent = cotangent.astype(jnp.bfloat16)
-    weights = w_radiance
     full_sum = lax.psum(
-        lax.dot_general(
-            weights, cotangent, (((1,), (1,)), ((), ())), preferred_element_type=jnp.float32
-        ),
+        lax.dot_general(w_radiance, cotangent, NT_DIMS, preferred_element_type=jnp.float32),
         "chan",
     )
     grad_hidden = lax.dynamic_slice_in_dim(full_sum, chan_index * hidden_dev, hidden_dev, 0)
@@ -136,7 +136,535 @@
     return adjoint
 
 
+def up_to(value, multiple):
+    return -(-value // multiple) * multiple
+
+
+def dot(left, right):
+    return jnp.dot(left, right, preferred_element_type=jnp.float32)
+
+
+def dot_nt(left, right):
+    return lax.dot_general(left, right, NT_DIMS, preferred_element_type=jnp.float32)
+
+
+def split_three(value):
+    high = value.astype(jnp.bfloat16).astype(jnp.float32)
+    middle = (value - high).astype(jnp.bfloat16).astype(jnp.float32)
+    return high, middle, value - high - middle
+
+
+def call(kernel, out_shape, args, in_hbm=(), out_hbm=False, scratch=(), flops=0):
+    far, near = pl.BlockSpec(memory_space=pl.ANY), pl.BlockSpec(memory_space=pltpu.VMEM)
+    bytes_accessed = sum(a.size * a.dtype.itemsize for a in args)
+    return pl.pallas_call(
+        kernel,
+        out_shape=out_shape,
+        in_specs=[far if k in in_hbm else near for k in range(len(args))],
+        out_specs=jax.tree.map(lambda _: far if out_hbm else near, out_shape),
+        scratch_shapes=list(scratch),
+        compiler_params=pltpu.CompilerParams(vmem_limit_bytes=VMEM_BYTES),
+        cost_estimate=pl.CostEstimate(
+            flops=flops, bytes_accessed=bytes_accessed, transcendentals=0
+        ),
+    )(*args)
+
+
+class Plan:
+    def __init__(self, tiles, chans, fields, owners, observed, w_hidden):
+        self.tiles, self.chans = tiles, chans
+        self.across, self.along, self.features = fields
+        self.own_cols = self.across // 4 * (self.along // 4)
+        self.rows = owners[0]
+        self.tile_cols = self.rows // tiles
+        self.slots = observed[0]
+        self.shard = observed[1]
+        self.capacity = self.slots // tiles
+        self.hidden = w_hidden[1]
+        self.group = chans // tiles
+        self.chips = chans // self.group
+        self.steps = self.chips.bit_length() - 1
+        self.lane = up_to(self.along, 128)
+        self.flag_at = up_to(self.hidden, 128)
+        self.width = max(
+            up_to(self.features, 128),
+            2 * self.flag_at,
+            self.flag_at + up_to(self.slots, 128),
+            3 * self.lane,
+        )
+        self.block = up_to(self.own_cols + 2 + self.across, 16)
+        self.per_row = self.own_cols + 2
+        self.room = up_to(3 * self.per_row, 16)
+        self.patch = 3 * tiles * self.own_cols
+
+
+def prepare_kernel(p, fields_ref, diffusivity_ref, usable_ref, bias_ref, out_ref, flat, packed, sem):
+    flat[...] = jnp.zeros(flat.shape, jnp.float32)
+    shape = (p.own_cols, p.along)
+    row = lax.broadcasted_iota(jnp.int32, shape, 0)
+    member = row == lax.broadcasted_iota(jnp.int32, shape, 1) // 4
+    total = jnp.dot(
+        member.astype(jnp.float32),
+        fields_ref[0] + fields_ref[1] + fields_ref[2] + fields_ref[3],
+        precision=lax.Precision.HIGHEST,
+        preferred_element_type=jnp.float32,
+    )
+    flat[: p.own_cols, : p.features] = total * 0.0625
+    at = p.own_cols
+    high, middle, low = split_three(bias_ref[...].reshape(1, p.hidden))
+    flat[at : at + 1, : p.hidden] = high
+    flat[at : at + 1, p.flag_at : p.flag_at + p.hidden] = middle
+    flat[at + 1 : at + 2, : p.hidden] = low
+    flags = usable_ref[...].reshape(1, p.slots).astype(jnp.float32)
+    flat[at + 1 : at + 2, p.flag_at : p.flag_at + p.slots] = flags
+    for k, part in enumerate(split_three(diffusivity_ref[...])):
+        flat[at + 2 : at + 2 + p.across, k * p.lane : k * p.lane + p.along] = part
+    packed[...] = flat[...].astype(jnp.bfloat16)
+    copy = pltpu.make_async_copy(packed, out_ref, sem)
+    copy.start()
+    copy.wait()
+
+
+def place_kernel(p, owners_ref, out_ref):
+    owner = owners_ref[...]
+    shape = (p.rows, p.rows)
+    row = lax.broadcasted_iota(jnp.int32, shape, 0)
+    other = lax.broadcasted_iota(jnp.int32, shape, 1)
+    across = jnp.sum(jnp.where(row == other, owner, 0), axis=0, keepdims=True)
+    same = (owner == across) & (row // p.tile_cols == other // p.tile_cols) & (other < row)
+    rank = jnp.sum(jnp.where(same, 1, 0), axis=1, keepdims=True)
+    number = lax.broadcasted_iota(jnp.int32, owner.shape, 0)
+    near = (owner + p.tiles - lax.axis_index("tile")) % p.tiles
+    out_ref[...] = near * p.slots + number // p.tile_cols * p.capacity + rank
+
+
+def join_kernel(*refs):
+    count = (len(refs) - 2) // 1
+    ins, out_ref, sems = refs[:count], refs[count], refs[count + 1]
+    size = ins[0].shape[0]
+    copies = [
+        pltpu.make_async_copy(ref, out_ref.at[pl.ds(k * size, size)], sems.at[k])
+        for k, ref in enumerate(ins)
+    ]
+    for copy in copies:
+        copy.start()
+    for copy in copies:
+        copy.wait()
+
+
+def forward_kernel(p, *refs):
+    refs = list(refs)
+    take = lambda n: [refs.pop(0) for _ in range(n)]
+    place_ref, bias_ref, w_radiance_ref = take(3)
+    gathered_refs, seen_refs, weight_refs = take(p.chans), take(p.tiles), take(p.chans)
+    *part_refs, slope_out, kappa_out = take(p.steps + 2)
+    stack, seen, weights, slope, active, departure, kappa, sems = take(8)
+    t, c = lax.axis_index("tile"), lax.axis_index("chan")
+    count = iter(range(3 * p.chans + p.tiles + p.steps + 1))
+
+    def begin(source, target):
+        copy = pltpu.make_async_copy(source, target, sems.at[next(count)])
+        copy.start()
+        return copy
+
+    wide = p.tiles * p.block
+    packs = [
+        begin(ref, stack.at[pl.ds(k * wide, wide)]) for k, ref in enumerate(gathered_refs)
+    ]
+    loads = [begin(ref, weights.at[k]) for k, ref in enumerate(weight_refs)]
+    views = [begin(ref, seen.at[k]) for k, ref in enumerate(seen_refs)]
+    for copy in packs:
+        copy.wait()
+    shape = (p.rows, p.chans * wide)
+    row = lax.broadcasted_iota(jnp.int32, shape, 0)
+    source = lax.broadcasted_iota(jnp.int32, shape, 1)
+    tile = (row // p.tile_cols + p.tiles - t) % p.tiles
+    chan = (row % p.tile_cols // p.own_cols) ^ c
+    pick = source == chan * wide + tile * p.block + row % p.own_cols
+    everything = stack[...]
+    columns = dot(pick.astype(jnp.bfloat16), everything).astype(jnp.bfloat16)[:, : p.features]
+    out = []
+    for k in range(p.chans):
+        loads[k].wait()
+        low = stack[k * wide + p.own_cols : k * wide + p.own_cols + 2, :].astype(jnp.float32)
+        bias = (
+            low[:1, : p.hidden]
+            + low[:1, p.flag_at : p.flag_at + p.hidden]
+            + low[1:, : p.hidden]
+        )
+        preact = dot(columns, weights[k]) + bias
+        squash = jax.nn.sigmoid(preact)
+        slope[k] = squash * (1.0 + preact * (1.0 - squash))
+        out.append(begin(slope.at[k], slope_out.at[k]))
+        at = pl.multiple_of((c ^ k) * p.hidden, p.hidden)
+        active[:, pl.ds(at, p.hidden)] = (preact * squash).astype(jnp.bfloat16)
+    for copy in views:
+        copy.wait()
+    part = p.rows // p.steps
+    slot = lax.broadcasted_iota(jnp.int32, (part, p.slots), 1)
+    for j, part_ref in enumerate(part_refs):
+        at = slice(j * part, (j + 1) * part)
+        in_use = jnp.zeros((part, 1), jnp.float32)
+        observed = jnp.zeros((part, p.shard), jnp.float32)
+        for k in range(p.tiles):
+            hit = place_ref[at, :] == slot + k * p.slots
+            low = k * p.block + p.own_cols + 1
+            flags = stack[low : low + 1, p.flag_at : p.flag_at + p.slots].astype(jnp.float32)
+            in_use = in_use + jnp.sum(jnp.where(hit, flags, 0.0), axis=1, keepdims=True)
+            observed = observed + dot(hit.astype(jnp.bfloat16), seen[k])
+        radiance = dot(active[at, :], w_radiance_ref[...]) + bias_ref[...].reshape(1, p.shard)
+        departure[at, :] = ((radiance - observed) * in_use).astype(jnp.bfloat16)
+        out.append(begin(departure.at[pl.ds(j * part, part)], part_ref))
+    reach = p.across + 4
+    shape = (3 * reach, p.chans * wide)
+    row = lax.broadcasted_iota(jnp.int32, shape, 0)
+    source = lax.broadcasted_iota(jnp.int32, shape, 1)
+    tile = (row // reach - 1 + p.tiles) % p.tiles
+    cell = c * p.across - 2 + row % reach
+    inside = (cell >= 0) & (cell < p.chans * p.across)
+    cell = jnp.where(inside, cell, 0)
+    wanted = (cell // p.across ^ c) * wide + tile * p.block + p.own_cols + 2 + cell % p.across
+    pick = (source == wanted) & inside
+    parts = dot(pick.astype(jnp.bfloat16), everything)
+    kappa[...] = sum(parts[:, k * p.lane : (k + 1) * p.lane] for k in range(3))
+    out.append(begin(kappa, kappa_out))
+    for copy in out:
+        copy.wait()
+
+
+def choose_kernel(p, choices, *refs):
+    refs, out_ref, sems = refs[:-2], refs[-2], refs[-1]
+    size = refs[0].shape[0]
+    role = (lax.axis_index("chan") // p.group) ^ lax.axis_index("tile")
+    for place in range(p.chips):
+
+        @pl.when(role == place)
+        def _():
+            copies = [
+                pltpu.make_async_copy(
+                    refs[choices[place, j]], out_ref.at[pl.ds(j * size, size)], sems.at[j]
+                )
+                for j in range(p.steps)
+            ]
+            for copy in copies:
+                copy.start()
+            for copy in copies:
+                copy.wait()
+
+
+def backward_kernel(p, *refs):
+    refs = list(refs)
+    take = lambda n: [refs.pop(0) for _ in range(n)]
+    (w_radiance_ref,) = take(1)
+    inv_cov_ref, slope_ref = take(2)
+    depart_refs, weight_refs, out_refs = take(p.group), take(p.chans), take(p.group)
+    inv_cov, slope, depart, weights, result, sems = take(6)
+    t, c = lax.axis_index("tile"), lax.axis_index("chan")
+    count = iter(range(2 * p.group + 2 * p.chans + p.group))
+
+    def begin(source, target):
+        copy = pltpu.make_async_copy(source, target, sems.at[next(count)])
+        copy.start()
+        return copy
+
+    loads = []
+    for k, ref in enumerate(depart_refs):
+        at = pl.multiple_of((c % p.group ^ k) * p.shard, p.shard)
+        loads.append(
+            (
+                begin(ref, depart.at[k]),
+                begin(inv_cov_ref.at[pl.ds(at, p.shard)], inv_cov.at[k]),
+            )
+        )
+    slopes = [begin(slope_ref.at[k], slope.at[k]) for k in range(p.chans)]
+    firsts = [begin(ref, weights.at[k]) for k, ref in enumerate(weight_refs)]
+    cotangent = None
+    for k, copies in enumerate(loads):
+        for copy in copies:
+            copy.wait()
+        term = dot(depart[k], inv_cov[k])
+        cotangent = term if cotangent is None else cotangent + term
+    cotangent = cotangent.astype(jnp.bfloat16)
+    total = jnp.zeros((p.rows, p.features), jnp.float32)
+    for k in range(p.chans):
+        at = pl.multiple_of((c ^ k) * p.hidden, p.hidden)
+        grad_hidden = dot_nt(cotangent, w_radiance_ref[pl.ds(at, p.hidden), :])
+        slopes[k].wait()
+        firsts[k].wait()
+        grad_pre = (grad_hidden * slope[k]).astype(jnp.bfloat16)
+        total = total + dot_nt(grad_pre, weights[k])
+    total = total.astype(jnp.bfloat16)
+    shape = (p.chips * p.patch, p.rows)
+    target = lax.broadcasted_iota(jnp.int32, shape, 0)
+    source = lax.broadcasted_iota(jnp.int32, shape, 1)
+    chip, inner = target // p.patch, target % p.patch
+    beside, inner = inner // (p.patch // 3) - 1, inner % (p.patch // 3)
+    tile, along = inner // p.own_cols, inner % p.own_cols
+    copies = []
+    for k in range(p.group):
+        row = ((chip ^ (c // p.group)) * p.group + (c % p.group ^ k)) + beside
+        wanted = tile * p.tile_cols + row * p.own_cols + along
+        pick = (source == wanted) & (row >= 0) & (row < p.chans)
+        result[k] = dot(pick.astype(jnp.bfloat16), total).astype(jnp.bfloat16)
+        copies.append(begin(result.at[k], out_refs[k]))
+    for copy in copies:
+        copy.wait()
+
+
+def add(refs, at=slice(None)):
+    total = refs[0][at, :].astype(jnp.float32)
+    for ref in refs[1:]:
+        total = total + ref[at, :].astype(jnp.float32)
+    return total
+
+
+def add_group_kernel(p, *refs):
+    ins, outs = refs[: p.group], refs[p.group :]
+    for k, out_ref in enumerate(outs):
+        out_ref[...] = add(ins, slice(k * p.patch, (k + 1) * p.patch)).astype(jnp.bfloat16)
+
+
+def add_chips_kernel(p, *refs):
+    ins, outs = refs[: p.chips], refs[p.chips :]
+    total = add(ins).astype(jnp.bfloat16)
+    shape = (p.room, p.patch)
+    target = lax.broadcasted_iota(jnp.int32, shape, 0)
+    source = lax.broadcasted_iota(jnp.int32, shape, 1)
+    row, along = target // p.per_row, target % p.per_row - 1
+    for k, out_ref in enumerate(outs):
+        tile = (lax.axis_index("tile") + k) % p.tiles
+        cell = (tile * p.own_cols + along + p.tiles * p.own_cols) % (p.tiles * p.own_cols)
+        pick = (source == row * (p.tiles * p.own_cols) + cell) & (row < 3)
+        out_ref[...] = dot(pick.astype(jnp.bfloat16), total).astype(jnp.bfloat16)
+
+
+def diffuse_kernel(p, edge, *refs):
+    ins, root_ref, out_ref = refs[: p.tiles], refs[-2], refs[-1]
+    total = add(ins) * 0.0625
+    length = p.along + 2 * edge
+    shape = (length, p.room)
+    cell = lax.broadcasted_iota(jnp.int32, shape, 0)
+    source = lax.broadcasted_iota(jnp.int32, shape, 1)
+    column = (cell - edge + 4) // 4
+    spread = []
+    for k in range(3):
+        pick = (source == column + k * p.per_row) & (column >= 0) & (column < p.per_row)
+        spread.append(
+            jnp.dot(
+                pick.astype(jnp.float32),
+                total,
+                precision=lax.Precision.HIGHEST,
+                preferred_element_type=jnp.float32,
+            )
+        )
+    root = root_ref[...]
+    state = [spread[(row + 2) // 4] for row in range(p.across + 4)]
+    east_of = functools.partial(pltpu.roll, shift=length - 1, axis=0)
+    west_of = functools.partial(pltpu.roll, shift=1, axis=0)
+    north = root[:, :-1] * root[:, 1:]
+    east, west = root * east_of(root), root * west_of(root)
+    for sweep in range(2):
+        fresh = list(state)
+        for row in range(1 + sweep, p.across + 3 - sweep):
+            here = state[row]
+            fresh[row] = (
+                here
+                + north[:, row : row + 1] * (state[row + 1] - here)
+                + north[:, row - 1 : row] * (state[row - 1] - here)
+                + east[:, row : row + 1] * (east_of(here) - here)
+                + west[:, row : row + 1] * (west_of(here) - here)
+            )
+        state = fresh
+    for row in range(p.across):
+        out_ref[row] = state[row + 2][edge : edge + p.along, : p.features]
+
+
+def body_by_column(
+    fields,
+    diffusivity,
+    owners,
+    observed,
+    usable,
+    w_hidden,
+    b_hidden,
+    w_radiance,
+    b_radiance,
+    inv_cov,
+):
+    p = Plan(
+        lax.axis_size("tile"),
+        lax.axis_size("chan"),
+        fields.shape,
+        owners.shape,
+        observed.shape,
+        w_hidden.shape,
+    )
+    half, single = jnp.bfloat16, jnp.float32
+    shape = jax.ShapeDtypeStruct
+    both = ("tile", "chan")
+    everyone = [(a, b) for a in range(p.tiles) for b in range(p.chans)]
+
+    def flip(value, mask):
+        return lax.ppermute(value, "chan", [(b, b ^ mask) for b in range(p.chans)])
+
+    def shift(value, by):
+        return lax.ppermute(value, "tile", [(a, (a + by) % p.tiles) for a in range(p.tiles)])
+
+    def send(value, wanted):
+        pairs = dict(wanted)
+        pairs.update({target: source for source, target in wanted.items()})
+        for a, b in everyone:
+            if (a, b) not in pairs:
+                pairs[a, b] = (a, b ^ 1)
+        number = lambda place: place[0] * p.chans + place[1]
+        return lax.ppermute(
+            value, both, sorted((number(a), number(b)) for a, b in pairs.items())
+        )
+
+    weights = [None] * p.chans
+    weights[0] = w_hidden
+    for chip in range(1, p.chips):
+        weights[chip * p.group] = flip(w_hidden, chip * p.group)
+
+    seen = [observed] + [
+        send(
+            observed,
+            {((b // p.group + k) % p.tiles, b): (b // p.group, b) for b in range(p.chans)},
+        )
+        for k in range(1, p.tiles)
+    ]
+
+    packed = call(
+        functools.partial(prepare_kernel, p),
+        shape((p.block, p.width), half),
+        [fields, diffusivity, usable, b_hidden],
+        out_hbm=True,
+        scratch=[
+            pltpu.VMEM((p.block, p.width), single),
+            pltpu.VMEM((p.block, p.width), half),
+            pltpu.SemaphoreType.DMA,
+        ],
+    )
+    strips = [packed] + [shift(packed, p.tiles - k) for k in range(1, p.tiles)]
+    joined = call(
+        join_kernel,
+        shape((p.tiles * p.block, p.width), half),
+        strips,
+        in_hbm=range(p.tiles),
+        out_hbm=True,
+        scratch=[pltpu.SemaphoreType.DMA((p.tiles,))],
+    )
+    gathered = [joined] + [None] * (p.chans - 1)
+    for chip in range(1, p.chips):
+        gathered[chip * p.group] = flip(joined, chip * p.group)
+    for held in (weights, gathered):
+        for k in range(p.chans):
+            if k % p.group:
+                held[k] = flip(held[k - k % p.group], k % p.group)
+    place = call(functools.partial(place_kernel, p), shape((p.rows, 1), jnp.int32), [owners])
+
+    reach = p.across + 4
+    *parts, slope, kappa = call(
+        functools.partial(forward_kernel, p),
+        [shape((p.rows // p.steps, p.shard), half)] * p.steps
+        + [shape((p.chans, p.rows, p.hidden), single), shape((3 * reach, p.lane), single)],
+        [place, b_radiance, w_radiance] + gathered + seen + weights,
+        in_hbm=range(3, 3 + 2 * p.chans + p.tiles),
+        out_hbm=True,
+        scratch=[
+            pltpu.VMEM((p.chans * p.tiles * p.block, p.width), half),
+            pltpu.VMEM((p.tiles, p.slots, p.shard), half),
+            pltpu.VMEM((p.chans, p.features, p.hidden), half),
+            pltpu.VMEM((p.chans, p.rows, p.hidden), single),
+            pltpu.VMEM((p.rows, p.hidden * p.chans), half),
+            pltpu.VMEM((p.rows, p.shard), half),
+            pltpu.VMEM((3 * reach, p.lane), single),
+            pltpu.SemaphoreType.DMA((3 * p.chans + p.tiles + p.steps + 1,)),
+        ],
+        flops=2 * p.rows * p.hidden * p.chans * (p.features + p.shard),
+    )
+
+    pool, held, choices = list(parts), {}, {}
+    for j in range(p.steps):
+        held[0, j] = choices[0, j] = j
+    for step in range(p.steps):
+        for since in range(-1, step):
+            for j in range(p.steps):
+                order = [1 << (j + k) % p.steps for k in range(p.steps)]
+                roles = [0] if since < 0 else [
+                    order[since] + rest
+                    for rest in range(p.chips)
+                    if rest & ~sum(order[:since]) == 0
+                ]
+                wanted = {
+                    (a, b): (a, b ^ order[step] * p.group)
+                    for a, b in everyone
+                    if (b // p.group ^ a) in roles
+                }
+                source = pool[choices[roles[0], j]]
+                for role in roles:
+                    choices[role + order[step], j] = len(pool)
+                pool.append(send(source, wanted))
+    chosen = call(
+        functools.partial(choose_kernel, p, choices),
+        shape((p.rows, p.shard), half),
+        pool,
+        in_hbm=range(len(pool)),
+        out_hbm=True,
+        scratch=[pltpu.SemaphoreType.DMA((p.steps,))],
+    )
+    depart = [chosen] + [flip(chosen, k) for k in range(1, p.group)]
+
+    count = p.group + p.chans
+    partial = call(
+        functools.partial(backward_kernel, p),
+        [shape((p.chips * p.patch, p.features), half)] * p.group,
+        [w_radiance, inv_cov, slope] + depart + weights,
+        in_hbm=range(1, 3 + count),
+        out_hbm=True,
+        scratch=[
+            pltpu.VMEM((p.group, p.shard, p.shard), half),
+            pltpu.VMEM((p.chans, p.rows, p.hidden), single),
+            pltpu.VMEM((p.group, p.rows, p.shard), half),
+            pltpu.VMEM((p.chans, p.features, p.hidden), half),
+            pltpu.VMEM((p.group, p.chips * p.patch, p.features), half),
+            pltpu.SemaphoreType.DMA((2 * p.group + 2 * p.chans + p.group,)),
+        ],
+        flops=2 * p.rows * (p.hidden * p.chans * (p.features + p.shard) + inv_cov.size),
+    )
+    partial = [partial[0]] + [flip(partial[k], k) for k in range(1, p.group)]
+    partial = call(
+        functools.partial(add_group_kernel, p),
+        [shape((p.patch, p.features), half)] * p.chips,
+        partial,
+    )
+    partial = [partial[0]] + [flip(partial[k], k * p.group) for k in range(1, p.chips)]
+    partial = call(
+        functools.partial(add_chips_kernel, p),
+        [shape((p.room, p.features), half)] * p.tiles,
+        partial,
+    )
+    partial = [partial[0]] + [shift(partial[k], k) for k in range(1, p.tiles)]
+
+    edge = 8
+    kappa = kappa.reshape(3, reach, p.lane)
+    root = jnp.sqrt(
+        jnp.concatenate(
+            [kappa[0, :, p.along - edge : p.along], kappa[1, :, : p.along], kappa[2, :, :edge]],
+            axis=1,
+        ).T
+    )
+    return call(
+        functools.partial(diffuse_kernel, p, edge),
+        shape(fields.shape, single),
+        partial + [root],
+        flops=100 * fields.size,
+    )
+
+
 def solution(mesh):
+    tiles, chans = mesh.shape["tile"], mesh.shape["chan"]
+    by_column = chans % tiles == 0 and chans & (chans - 1) == 0 and chans // tiles > 1
     placed = (
         P("chan", "tile", None),
         P("chan", "tile"),
@@ -150,5 +678,9 @@
         P("tile", "chan"),
     )
     return jax.shard_map(
-        body, mesh=mesh, in_specs=placed, out_specs=P("chan", "tile", None), check_vma=False
-    )
+        body_by_column if by_column else body_by_owner,
+        mesh=mesh,
+        in_specs=placed,
+        out_specs=P("chan", "tile", None),
+        check_vma=False,
+    )

time: 388 us -> 103 us (0.27); the launches traced: 382 us -> 103 us
  waiting for transfers between devices: 289 us -> 45.1 us
  Pallas kernels: 0 us -> 22.1 us
  blocking collectives: 21.6 us -> 0 us
  matrix products: 14.2 us -> 0 us
  between operations: 13.4 us -> 0.19 us
  other arithmetic: 9.02 us -> 0.08 us
  local copies, waits for them, and re-layouts: 2.52 us -> 8.37 us
  starting transfers between devices: 32.2 us -> 27.4 us
    all_gather x2 -> x0, waiting for transfers between devices: 192 us -> none  [the longest x1 168 us: body(): lax.all_gather(inv_cov, 'tile', axis=0, tiled=True)]
    psum x1 -> x0, waiting for transfers between devices: 50.6 us -> none  [body(): lax.psum(lax.dot_general(weights, cotangent, (((1,), (1,)), ((), ())), pr...]
    ppermute x12 -> x34, waiting for transfers between devices: 4.14 us -> 45.1 us  [the longest x9 24.9 us: send(): lax.ppermute(value, both, sorted(((number(a), number(b)) for a, b in pair...]
    reduce_scatter x1 -> x0, waiting for transfers between devices: 28.2 us -> none  [body(): lax.psum_scatter(jnp.take(returned, slot_of, axis=0), 'chan', scatter_dim...]
    pallas_call x0 -> x9, Pallas kernels: none -> 22.1 us  [call(): pl.pallas_call(kernel, out_shape=out_shape, in_specs=[far if k in in_hbm...]
    all_gather x2 -> x0, blocking collectives: 21.6 us -> none  [the longest x1 10.9 us: body(): lax.all_gather(active, 'chan', axis=0, tiled=True)]
    dot_general x5 -> x0, matrix products: 14.2 us -> none  [the longest x1 8.09 us: body(): lax.dot_general(weights, cotangent, (((1,), (1,)), ((), ())), preferred_e...]
    all_to_all x2 -> x0, waiting for transfers between devices: 13.5 us -> none  [the longest x1 8.08 us: body(): lax.all_to_all(part_grad, 'tile', split_axis=0, concat_axis=0, tiled=True)]
  transfers between devices with their start and end apart: 18 -> 34, of which waited for: 9 -> 18; matrix products, arithmetic and copies ran while one was open for 1% -> 1% of each run, Pallas kernels for 0% -> 0%
where the time goes in v2:
time: 103 us
  waiting for transfers between devices  45.1 us (44%)
  starting transfers between devices  27.4 us (27%)
  Pallas kernels  22.1 us (21%)
  local copies, waits for them, and re-layouts  8.37 us (8%)
    ppermute x9, waiting for transfers between devices, send(): lax.ppermute(value, both, sorted(((number(a), number(b)) for a, b in pair...  24.9 us
    pallas_call x9, Pallas kernels, call(): pl.pallas_call(kernel, out_shape=out_shape, in_specs=[far if k in in_hbm...  22.1 us
    ppermute x19, waiting for transfers between devices, flip(): return lax.ppermute(value, 'chan', [(b, b ^ mask) for b in range(p.chans)])  13.5 us
    ppermute x19, starting transfers between devices, flip(): return lax.ppermute(value, 'chan', [(b, b ^ mask) for b in range(p.chans)])  13.2 us
    ppermute x6, starting transfers between devices, shift(): lax.ppermute(value, 'tile', [(a, (a + by) % p.tiles) for a in range(p.til...  9.98 us
    unnamed x23, local copies, waits for them, and re-layouts  8.21 us
    ppermute x6, waiting for transfers between devices, shift(): lax.ppermute(value, 'tile', [(a, (a + by) % p.tiles) for a in range(p.til...  6.81 us
    ppermute x9, starting transfers between devices, send(): lax.ppermute(value, both, sorted(((number(a), number(b)) for a, b in pair...  4.22 us
  transfers between devices with their start and end apart: 34, of which 18 were waited for; matrix products, arithmetic and copies ran while one was open for 1% of the time, Pallas kernels for 0%

profile of v2, /device:TPU:0, one launch (start us, length us, event | category | flops | bytes accessed | tf_op | source)
XLA Modules:
  0.0 103.2 jit_solution(1270615423662128451)
XLA Ops:
  0.0 0.9 copy-done.5
  1.0 0.7 copy-done.8
  1.6 0.7 copy-done.9
  2.3 0.7 copy-done.10
  3.0 0.2 shard_map.101.refs_0_
  3.2 5.1 %collective-permute-start = (bf16[16,512]{1,0:T(8,128)(2,1)S(1)}, bf16[16,512]{1,0:T(8,128)(2,1)S(1)}, u32[]{:S(2)}, u32[]{:S(2)}) collective-permute-start(bf16[16,512]{1,0:T(8,128)(2,1)S(1)} %shard_map.101.refs_0_), channel_id=1, source_target_pairs={{0,24},{8,0},{16,8},{24,16},{1,25},{9,1},{17,9},{25,17},{2,26},{10... | collective-permute-start | bytes 49160 | tf_op jit(solution)/shard_map/ppermute | solution.py:511
  8.3 1.0 collective-permute-start.2
  9.3 0.4 collective-permute-done.refs_1_
  9.7 3.2 %collective-permute-done.1.refs_2_ = bf16[16,512]{1,0:T(8,128)(2,1)S(1)} collective-permute-done((bf16[16,512]{1,0:T(8,128)(2,1)S(1)}, bf16[16,512]{1,0:T(8,128)(2,1)S(1)}, u32[]{:S(2)}, u32[]{:S(2)}) %collective-permute-start.1) | collective-permute-done | bytes 16416 | tf_op jit(solution)/shard_map/ppermute | solution.py:511
  12.9 0.9 collective-permute-done.2.refs_3_
  13.8 0.1 shard_map.102.refs_3_
  13.9 1.6 %collective-permute-start.4 = (bf16[64,512]{1,0:T(8,128)(2,1)S(1)}, bf16[64,512]{1,0:T(8,128)(2,1)S(1)}, u32[]{:S(2)}, u32[]{:S(2)}) collective-permute-start(bf16[64,512]{1,0:T(8,128)(2,1)S(1)} %shard_map.102.refs_3_), channel_id=1, source_target_pairs={{0,2},{1,3},{2,0},{3,1},{4,6},{5,7},{6,4},{7,5},{8,10},{9,11},{10,... | collective-permute-start | bytes 196616 | tf_op jit(solution)/shard_map/ppermute | solution.py:508
  15.5 1.5 %collective-permute-start.6 = (bf16[64,512]{1,0:T(8,128)(2,1)S(1)}, bf16[64,512]{1,0:T(8,128)(2,1)S(1)}, u32[]{:S(2)}, u32[]{:S(2)}) collective-permute-start(bf16[64,512]{1,0:T(8,128)(2,1)S(1)} %shard_map.102.refs_3_), channel_id=1, source_target_pairs={{0,4},{1,5},{2,6},{3,7},{4,0},{5,1},{6,2},{7,3},{8,12},{9,13},{10,... | collective-permute-start | bytes 196616 | tf_op jit(solution)/shard_map/ppermute | solution.py:508
  17.0 0.5 collective-permute-start.8
  17.5 1.3 %collective-permute-done.4.refs_5_ = bf16[64,512]{1,0:T(8,128)(2,1)S(1)} collective-permute-done((bf16[64,512]{1,0:T(8,128)(2,1)S(1)}, bf16[64,512]{1,0:T(8,128)(2,1)S(1)}, u32[]{:S(2)}, u32[]{:S(2)}) %collective-permute-start.4) | collective-permute-done | bytes 65568 | tf_op jit(solution)/shard_map/ppermute | solution.py:508
  18.8 1.2 %collective-permute-done.6.refs_7_ = bf16[64,512]{1,0:T(8,128)(2,1)S(1)} collective-permute-done((bf16[64,512]{1,0:T(8,128)(2,1)S(1)}, bf16[64,512]{1,0:T(8,128)(2,1)S(1)}, u32[]{:S(2)}, u32[]{:S(2)}) %collective-permute-start.6) | collective-permute-done | bytes 65568 | tf_op jit(solution)/shard_map/ppermute | solution.py:508
  20.0 2.1 %collective-permute-done.8.refs_9_ = bf16[64,512]{1,0:T(8,128)(2,1)S(1)} collective-permute-done((bf16[64,512]{1,0:T(8,128)(2,1)S(1)}, bf16[64,512]{1,0:T(8,128)(2,1)S(1)}, u32[]{:S(2)}, u32[]{:S(2)}) %collective-permute-start.8) | collective-permute-done | bytes 65568 | tf_op jit(solution)/shard_map/ppermute | solution.py:508
  22.2 0.5 collective-permute-start.14
  22.7 0.5 collective-permute-start.16
  23.2 2.4 %collective-permute-start.18 = (bf16[411,256]{1,0:T(8,128)(2,1)}, bf16[411,256]{1,0:T(8,128)(2,1)S(1)}, u32[]{:S(2)}, u32[]{:S(2)}) collective-permute-start(bf16[411,256]{1,0:T(8,128)(2,1)} %refs_5_.1), channel_id=1, source_target_pairs={{0,6},{1,7},{2,4},{3,5},{4,2},{5,3},{6,0},{7,1},{8,14},{9,15},{10,... | collective-permute-start | bytes 631304 | tf_op jit(solution)/shard_map/ppermute | solution.py:508
  25.7 1.2 %collective-permute-start.11 = (bf16[128,768]{1,0:T(8,128)(2,1)}, bf16[128,768]{1,0:T(8,128)(2,1)S(1)}, u32[]{:S(2)}, u32[]{:S(2)}) collective-permute-start(bf16[128,768]{1,0:T(8,128)(2,1)} %refs_11_.1), channel_id=1, source_target_pairs={{0,16},{1,17},{2,3},{3,2},{4,20},{5,21},{6,7},{7,6},{8,9},{9,8},{1... | collective-permute-start | bytes 589832 | tf_op jit(solution)/shard_map/ppermute | solution.py:520
  26.9 9.7 %collective-permute-done.10.refs_12_ = bf16[128,768]{1,0:T(8,128)(2,1)S(1)} collective-permute-done((bf16[128,768]{1,0:T(8,128)(2,1)}, bf16[128,768]{1,0:T(8,128)(2,1)S(1)}, u32[]{:S(2)}, u32[]{:S(2)}) %collective-permute-start.10) | collective-permute-done | bytes 196640 | tf_op jit(solution)/shard_map/ppermute | solution.py:520
  36.6 0.5 collective-permute-start.15
  37.1 0.1 collective-permute-start.17
  37.2 0.4 collective-permute-start.19
  37.6 0.8 copy.22.owners_ref
  38.4 0.0 copy-start.4
  38.4 0.3 shard_map.100.refs_0_
  38.7 7.8 %collective-permute-done.12.refs_14_ = bf16[128,768]{1,0:T(8,128)(2,1)S(1)} collective-permute-done((bf16[128,768]{1,0:T(8,128)(2,1)}, bf16[128,768]{1,0:T(8,128)(2,1)S(1)}, u32[]{:S(2)}, u32[]{:S(2)}) %collective-permute-start.12) | collective-permute-done | bytes 196640 | tf_op jit(solution)/shard_map/ppermute | solution.py:520
  46.5 1.9 %copy-done = bf16[2048,768]{1,0:T(8,128)(2,1)S(1)} copy-done((bf16[2048,768]{1,0:T(8,128)(2,1)S(1)}, bf16[2048,768]{1,0:T(8,128)(2,1)}, u32[]{:S(2)}) %copy-start) | copy-done | bytes 3145752
  48.4 0.9 copy-done.3
  49.3 0.9 copy-done.6
  50.3 0.7 copy-done.7
  51.0 10.0 %shard_map.103 = (bf16[128,768]{1,0:T(8,128)(2,1)S(1)}, bf16[128,768]{1,0:T(8,128)(2,1)S(1)}, f32[8,256,256]{2,1,0:T(8,128)S(1)}, f32[24,128]{1,0:T(8,128)S(1)}) custom-call(s32[256,1]{1,0:T(8,128)S(1)} %shard_map.100.refs_0_, f32[768]{0:T(1024)S(1)} %copy-done.7, bf16[2048,768]{1,0:T(8,128)(2,1)S(1)} %copy-done, bf16[64,512]{1,0:T(8,128)(2,1)S(1)} %shard_map.102.refs_3_, ...), custom_call_target="tpu_custom_call" | custom-call | flops 1236271104 | bytes 6144000 | tf_op jit(solution)/shard_map/pallas_call | solution.py:160
  61.0 0.1 collective-permute-start.20
  61.1 0.1 collective-permute-start.21
  61.1 2.0 %collective-permute-start.22 = (bf16[128,768]{1,0:T(8,128)(2,1)S(1)}, bf16[128,768]{1,0:T(8,128)(2,1)S(1)}, u32[]{:S(2)}, u32[]{:S(2)}) collective-permute-start(bf16[128,768]{1,0:T(8,128)(2,1)S(1)} %get-tuple-element.20.refs_0_), channel_id=1, source_target_pairs={{0,4},{1,5},{2,3},{3,2},{4,0},{5,1},{6,7},{7,6},{8,9},{9,8},{10,14... | collective-permute-start | bytes 589832 | tf_op jit(solution)/shard_map/ppermute | solution.py:520
  63.2 0.4 collective-permute-start.23
  63.6 5.3 %collective-permute-done.20.refs_2_ = bf16[128,768]{1,0:T(8,128)(2,1)S(1)} collective-permute-done((bf16[128,768]{1,0:T(8,128)(2,1)S(1)}, bf16[128,768]{1,0:T(8,128)(2,1)S(1)}, u32[]{:S(2)}, u32[]{:S(2)}) %collective-permute-start.20) | collective-permute-done | bytes 196640 | tf_op jit(solution)/shard_map/ppermute | solution.py:520
  68.9 0.1 collective-permute-done.21.refs_3_
  69.0 0.4 collective-permute-start.25
  69.4 2.0 %collective-permute-done.22.refs_4_ = bf16[128,768]{1,0:T(8,128)(2,1)S(1)} collective-permute-done((bf16[128,768]{1,0:T(8,128)(2,1)S(1)}, bf16[128,768]{1,0:T(8,128)(2,1)S(1)}, u32[]{:S(2)}, u32[]{:S(2)}) %collective-permute-start.22) | collective-permute-done | bytes 196640 | tf_op jit(solution)/shard_map/ppermute | solution.py:520
  71.4 0.6 shard_map.104.refs_3_
  72.0 0.1 collective-permute-start.26
  72.0 1.7 %collective-permute-done.26.refs_4_ = bf16[256,768]{1,0:T(8,128)(2,1)S(1)} collective-permute-done((bf16[256,768]{1,0:T(8,128)(2,1)S(1)}, bf16[256,768]{1,0:T(8,128)(2,1)S(1)}, u32[]{:S(2)}, u32[]{:S(2)}) %collective-permute-start.26) | collective-permute-done | bytes 393248 | tf_op jit(solution)/shard_map/ppermute | solution.py:508
  73.8 9.2 %shard_map.105 = (bf16[384,411]{1,0:T(8,128)(2,1)S(1)}, bf16[384,411]{1,0:T(8,128)(2,1)S(1)}) custom-call(bf16[2048,768]{1,0:T(8,128)(2,1)S(1)} %copy-done.1, bf16[1536,768]{1,0:T(8,128)(2,1)S(1)} %copy-done.2, f32[8,256,256]{2,1,0:T(8,128)S(1)} %get-tuple-element.19.refs_2_, bf16[256,768]{1,0:T(8,128)(2,1)S(1)} %shard_map.104.refs_3_, ...), custom_call_target="tpu_custom_call" | custom-call | flops 1840250880 | bytes 10072064 | tf_op jit(solution)/shard_map/pallas_call | solution.py:160
  83.0 0.2 collective-permute-start.27
  83.2 0.1 slice_bitcast_fusion.2
  83.3 1.5 %collective-permute-done.27.refs_1_ = bf16[384,411]{1,0:T(8,128)(2,1)S(1)} collective-permute-done((bf16[384,411]{1,0:T(8,128)(2,1)S(1)}, bf16[384,411]{1,0:T(8,128)(2,1)S(1)}, u32[]{:S(2)}, u32[]{:S(2)}) %collective-permute-start.27) | collective-permute-done | bytes 315680 | tf_op jit(solution)/shard_map/ppermute | solution.py:508
  84.8 0.1 shard_map.106
  84.9 2.8 %collective-permute-start.28 = (bf16[96,411]{1,0:T(8,128)(2,1)S(1)}, bf16[96,411]{1,0:T(8,128)(2,1)S(1)}, u32[]{:S(2)}, u32[]{:S(2)}) collective-permute-start(bf16[96,411]{1,0:T(8,128)(2,1)S(1)} %get-tuple-element.25), channel_id=1, source_target_pairs={{0,2},{1,3},{2,0},{3,1},{4,6},{5,7},{6,4},{7,5},{8,10},{9,11},{10,... | collective-permute-start | bytes 236744 | tf_op jit(solution)/shard_map/ppermute | solution.py:508
  87.7 2.0 %collective-permute-start.29 = (bf16[96,411]{1,0:T(8,128)(2,1)S(1)}, bf16[96,411]{1,0:T(8,128)(2,1)S(1)}, u32[]{:S(2)}, u32[]{:S(2)}) collective-permute-start(bf16[96,411]{1,0:T(8,128)(2,1)S(1)} %get-tuple-element.26), channel_id=1, source_target_pairs={{0,4},{1,5},{2,6},{3,7},{4,0},{5,1},{6,2},{7,3},{8,12},{9,13},{10,... | collective-permute-start | bytes 236744 | tf_op jit(solution)/shard_map/ppermute | solution.py:508
  89.7 1.1 %collective-permute-done.28.refs_1_ = bf16[96,411]{1,0:T(8,128)(2,1)S(1)} collective-permute-done((bf16[96,411]{1,0:T(8,128)(2,1)S(1)}, bf16[96,411]{1,0:T(8,128)(2,1)S(1)}, u32[]{:S(2)}, u32[]{:S(2)}) %collective-permute-start.28) | collective-permute-done | bytes 78944 | tf_op jit(solution)/shard_map/ppermute | solution.py:508
  90.8 3.1 %collective-permute-done.29.refs_2_ = bf16[96,411]{1,0:T(8,128)(2,1)S(1)} collective-permute-done((bf16[96,411]{1,0:T(8,128)(2,1)S(1)}, bf16[96,411]{1,0:T(8,128)(2,1)S(1)}, u32[]{:S(2)}, u32[]{:S(2)}) %collective-permute-start.29) | collective-permute-done | bytes 78944 | tf_op jit(solution)/shard_map/ppermute | solution.py:508
  93.9 1.3 %collective-permute-done.30.refs_3_ = bf16[96,411]{1,0:T(8,128)(2,1)S(1)} collective-permute-done((bf16[96,411]{1,0:T(8,128)(2,1)S(1)}, bf16[96,411]{1,0:T(8,128)(2,1)S(1)}, u32[]{:S(2)}, u32[]{:S(2)}) %collective-permute-start.30) | collective-permute-done | bytes 78944 | tf_op jit(solution)/shard_map/ppermute | solution.py:508
  95.2 0.2 shard_map.107
  95.5 0.1 collective-permute-start.31
  95.5 0.1 collective-permute-start.32
  95.6 3.7 %collective-permute-start.33 = (bf16[32,411]{1,0:T(8,128)(2,1)S(1)}, bf16[32,411]{1,0:T(8,128)(2,1)S(1)}, u32[]{:S(2)}, u32[]{:S(2)}) collective-permute-start(bf16[32,411]{1,0:T(8,128)(2,1)S(1)} %get-tuple-element.31), channel_id=1, source_target_pairs={{0,24},{8,0},{16,8},{24,16},{1,25},{9,1},{17,9},{25,17},{2,26},{10... | collective-permute-start | bytes 78920 | tf_op jit(solution)/shard_map/ppermute | solution.py:511
  99.4 0.1 maximum_sqrt_fusion
  99.4 0.1 copy.23
  99.5 1.7 %collective-permute-done.31.refs_1_ = bf16[32,411]{1,0:T(8,128)(2,1)S(1)} collective-permute-done((bf16[32,411]{1,0:T(8,128)(2,1)S(1)}, bf16[32,411]{1,0:T(8,128)(2,1)S(1)}, u32[]{:S(2)}, u32[]{:S(2)}) %collective-permute-start.31) | collective-permute-done | bytes 26336 | tf_op jit(solution)/shard_map/ppermute | solution.py:511
  101.2 0.6 collective-permute-done.33.refs_3_
  101.8 1.4 %shard_map.108 = f32[4,32,411]{2,1,0:T(8,128)} custom-call(bf16[32,411]{1,0:T(8,128)(2,1)S(1)} %get-tuple-element.28.refs_0_, bf16[32,411]{1,0:T(8,128)(2,1)S(1)} %collective-permute-done.31.refs_1_, bf16[32,411]{1,0:T(8,128)(2,1)S(1)} %collective-permute-done.32.refs_2_, bf16[32,411]{1,0:T(8,128)(2,1)S(1)} %collective-permute-done.33.refs_3_, ...), custom_call_target="tpu_custom_call" | custom-call | flops 5260800 | bytes 106752 | tf_op jit(solution)/shard_map/pallas_call | solution.py:160
  (40 shorter events, 0.1 us)
Async XLA Ops:
  0.0 0.9 copy-start.5
  1.0 0.7 copy-start.8
  1.6 0.7 copy-start.9
  2.3 0.7 copy-start.10
  3.2 6.5 %collective-permute-start = (bf16[16,512]{1,0:T(8,128)(2,1)S(1)}, bf16[16,512]{1,0:T(8,128)(2,1)S(1)}, u32[]{:S(2)}, u32[]{:S(2)}) collective-permute-start(bf16[16,512]{1,0:T(8,128)(2,1)S(1)} %shard_map.101.refs_0_), channel_id=1, source_target_pairs={{0,24},{8,0},{16,8},{24,16},{1,25},{9,1},{17,9},{25,17},{2,26},{10... | collective-permute-start | bytes 49160 | tf_op jit(solution)/shard_map/ppermute | solution.py:511
  8.3 4.6 %collective-permute-start.1 = (bf16[16,512]{1,0:T(8,128)(2,1)S(1)}, bf16[16,512]{1,0:T(8,128)(2,1)S(1)}, u32[]{:S(2)}, u32[]{:S(2)}) collective-permute-start(bf16[16,512]{1,0:T(8,128)(2,1)S(1)} %shard_map.101.refs_0_), channel_id=1, source_target_pairs={{0,16},{8,24},{16,0},{24,8},{1,17},{9,25},{17,1},{25,9},{2,18},{10... | collective-permute-start | bytes 49160 | tf_op jit(solution)/shard_map/ppermute | solution.py:511
  8.3 5.5 %collective-permute-start.2 = (bf16[16,512]{1,0:T(8,128)(2,1)S(1)}, bf16[16,512]{1,0:T(8,128)(2,1)S(1)}, u32[]{:S(2)}, u32[]{:S(2)}) collective-permute-start(bf16[16,512]{1,0:T(8,128)(2,1)S(1)} %shard_map.101.refs_0_), channel_id=1, source_target_pairs={{0,8},{8,16},{16,24},{24,0},{1,9},{9,17},{17,25},{25,1},{2,10},{10... | collective-permute-start | bytes 49160 | tf_op jit(solution)/shard_map/ppermute | solution.py:511
  13.9 4.9 %collective-permute-start.4 = (bf16[64,512]{1,0:T(8,128)(2,1)S(1)}, bf16[64,512]{1,0:T(8,128)(2,1)S(1)}, u32[]{:S(2)}, u32[]{:S(2)}) collective-permute-start(bf16[64,512]{1,0:T(8,128)(2,1)S(1)} %shard_map.102.refs_3_), channel_id=1, source_target_pairs={{0,2},{1,3},{2,0},{3,1},{4,6},{5,7},{6,4},{7,5},{8,10},{9,11},{10,... | collective-permute-start | bytes 196616 | tf_op jit(solution)/shard_map/ppermute | solution.py:508
  15.5 4.5 %collective-permute-start.6 = (bf16[64,512]{1,0:T(8,128)(2,1)S(1)}, bf16[64,512]{1,0:T(8,128)(2,1)S(1)}, u32[]{:S(2)}, u32[]{:S(2)}) collective-permute-start(bf16[64,512]{1,0:T(8,128)(2,1)S(1)} %shard_map.102.refs_3_), channel_id=1, source_target_pairs={{0,4},{1,5},{2,6},{3,7},{4,0},{5,1},{6,2},{7,3},{8,12},{9,13},{10,... | collective-permute-start | bytes 196616 | tf_op jit(solution)/shard_map/ppermute | solution.py:508
  17.0 5.2 %collective-permute-start.8 = (bf16[64,512]{1,0:T(8,128)(2,1)S(1)}, bf16[64,512]{1,0:T(8,128)(2,1)S(1)}, u32[]{:S(2)}, u32[]{:S(2)}) collective-permute-start(bf16[64,512]{1,0:T(8,128)(2,1)S(1)} %shard_map.102.refs_3_), channel_id=1, source_target_pairs={{0,6},{1,7},{2,4},{3,5},{4,2},{5,3},{6,0},{7,1},{8,14},{9,15},{10,... | collective-permute-start | bytes 196616 | tf_op jit(solution)/shard_map/ppermute | solution.py:508
  17.5 5.2 %collective-permute-start.3 = (bf16[64,512]{1,0:T(8,128)(2,1)S(1)}, bf16[64,512]{1,0:T(8,128)(2,1)S(1)}, u32[]{:S(2)}, u32[]{:S(2)}) collective-permute-start(bf16[64,512]{1,0:T(8,128)(2,1)S(1)} %shard_map.102.refs_3_), channel_id=1, source_target_pairs={{0,1},{1,0},{2,3},{3,2},{4,5},{5,4},{6,7},{7,6},{8,9},{9,8},{10,11... | collective-permute-start | bytes 196616 | tf_op jit(solution)/shard_map/ppermute | solution.py:508
  18.8 4.4 %collective-permute-start.5 = (bf16[64,512]{1,0:T(8,128)(2,1)S(1)}, bf16[64,512]{1,0:T(8,128)(2,1)S(1)}, u32[]{:S(2)}, u32[]{:S(2)}) collective-permute-start(bf16[64,512]{1,0:T(8,128)(2,1)S(1)} %collective-permute-done.4.refs_5_), channel_id=1, source_target_pairs={{0,1},{1,0},{2,3},{3,2},{4,5},{5,4},{6,7},{7,6},{8,9},{9,8},{10,11... | collective-permute-start | bytes 196616 | tf_op jit(solution)/shard_map/ppermute | solution.py:508
  20.0 5.7 %collective-permute-start.7 = (bf16[64,512]{1,0:T(8,128)(2,1)S(1)}, bf16[64,512]{1,0:T(8,128)(2,1)S(1)}, u32[]{:S(2)}, u32[]{:S(2)}) collective-permute-start(bf16[64,512]{1,0:T(8,128)(2,1)S(1)} %collective-permute-done.6.refs_7_), channel_id=1, source_target_pairs={{0,1},{1,0},{2,3},{3,2},{4,5},{5,4},{6,7},{7,6},{8,9},{9,8},{10,11... | collective-permute-start | bytes 196616 | tf_op jit(solution)/shard_map/ppermute | solution.py:508
  22.2 3.5 %collective-permute-start.9 = (bf16[64,512]{1,0:T(8,128)(2,1)S(1)}, bf16[64,512]{1,0:T(8,128)(2,1)S(1)}, u32[]{:S(2)}, u32[]{:S(2)}) collective-permute-start(bf16[64,512]{1,0:T(8,128)(2,1)S(1)} %collective-permute-done.8.refs_9_), channel_id=1, source_target_pairs={{0,1},{1,0},{2,3},{3,2},{4,5},{5,4},{6,7},{7,6},{8,9},{9,8},{10,11... | collective-permute-start | bytes 196616 | tf_op jit(solution)/shard_map/ppermute | solution.py:508
  22.2 14.4 %collective-permute-start.14 = (bf16[411,256]{1,0:T(8,128)(2,1)}, bf16[411,256]{1,0:T(8,128)(2,1)S(1)}, u32[]{:S(2)}, u32[]{:S(2)}) collective-permute-start(bf16[411,256]{1,0:T(8,128)(2,1)} %refs_5_.1), channel_id=1, source_target_pairs={{0,2},{1,3},{2,0},{3,1},{4,6},{5,7},{6,4},{7,5},{8,10},{9,11},{10,... | collective-permute-start | bytes 631304 | tf_op jit(solution)/shard_map/ppermute | solution.py:508
  22.7 14.4 %collective-permute-start.16 = (bf16[411,256]{1,0:T(8,128)(2,1)}, bf16[411,256]{1,0:T(8,128)(2,1)S(1)}, u32[]{:S(2)}, u32[]{:S(2)}) collective-permute-start(bf16[411,256]{1,0:T(8,128)(2,1)} %refs_5_.1), channel_id=1, source_target_pairs={{0,4},{1,5},{2,6},{3,7},{4,0},{5,1},{6,2},{7,3},{8,12},{9,13},{10,... | collective-permute-start | bytes 631304 | tf_op jit(solution)/shard_map/ppermute | solution.py:508
  23.2 13.9 %collective-permute-start.18 = (bf16[411,256]{1,0:T(8,128)(2,1)}, bf16[411,256]{1,0:T(8,128)(2,1)S(1)}, u32[]{:S(2)}, u32[]{:S(2)}) collective-permute-start(bf16[411,256]{1,0:T(8,128)(2,1)} %refs_5_.1), channel_id=1, source_target_pairs={{0,6},{1,7},{2,4},{3,5},{4,2},{5,3},{6,0},{7,1},{8,14},{9,15},{10,... | collective-permute-start | bytes 631304 | tf_op jit(solution)/shard_map/ppermute | solution.py:508
  25.7 10.9 %collective-permute-start.10 = (bf16[128,768]{1,0:T(8,128)(2,1)}, bf16[128,768]{1,0:T(8,128)(2,1)S(1)}, u32[]{:S(2)}, u32[]{:S(2)}) collective-permute-start(bf16[128,768]{1,0:T(8,128)(2,1)} %refs_11_.1), channel_id=1, source_target_pairs={{0,8},{1,9},{2,3},{3,2},{4,5},{5,4},{6,30},{7,31},{8,0},{9,1},{10,... | collective-permute-start | bytes 589832 | tf_op jit(solution)/shard_map/ppermute | solution.py:520
  25.7 11.9 %collective-permute-start.11 = (bf16[128,768]{1,0:T(8,128)(2,1)}, bf16[128,768]{1,0:T(8,128)(2,1)S(1)}, u32[]{:S(2)}, u32[]{:S(2)}) collective-permute-start(bf16[128,768]{1,0:T(8,128)(2,1)} %refs_11_.1), channel_id=1, source_target_pairs={{0,16},{1,17},{2,3},{3,2},{4,20},{5,21},{6,7},{7,6},{8,9},{9,8},{1... | collective-permute-start | bytes 589832 | tf_op jit(solution)/shard_map/ppermute | solution.py:520
  36.6 9.9 %collective-permute-start.13 = (bf16[411,256]{1,0:T(8,128)(2,1)}, bf16[411,256]{1,0:T(8,128)(2,1)S(1)}, u32[]{:S(2)}, u32[]{:S(2)}) collective-permute-start(bf16[411,256]{1,0:T(8,128)(2,1)} %refs_5_.1), channel_id=1, source_target_pairs={{0,1},{1,0},{2,3},{3,2},{4,5},{5,4},{6,7},{7,6},{8,9},{9,8},{10,11... | collective-permute-start | bytes 631304 | tf_op jit(solution)/shard_map/ppermute | solution.py:508
  36.6 9.9 %collective-permute-start.15 = (bf16[411,256]{1,0:T(8,128)(2,1)S(1)}, bf16[411,256]{1,0:T(8,128)(2,1)S(1)}, u32[]{:S(2)}, u32[]{:S(2)}) collective-permute-start(bf16[411,256]{1,0:T(8,128)(2,1)S(1)} %collective-permute-done.14.refs_17_.refs_7_), channel_id=1, source_target_pairs={{0,1},{1,0},{2,3},{3,2},{4,5},{5,4},{6,7},{7,6},{8,9},{9,8},{10,11... | collective-permute-start | bytes 631304 | tf_op jit(solution)/shard_map/ppermute | solution.py:508
  37.1 9.4 %collective-permute-start.17 = (bf16[411,256]{1,0:T(8,128)(2,1)S(1)}, bf16[411,256]{1,0:T(8,128)(2,1)S(1)}, u32[]{:S(2)}, u32[]{:S(2)}) collective-permute-start(bf16[411,256]{1,0:T(8,128)(2,1)S(1)} %collective-permute-done.16.refs_19_.refs_9_), channel_id=1, source_target_pairs={{0,1},{1,0},{2,3},{3,2},{4,5},{5,4},{6,7},{7,6},{8,9},{9,8},{10,11... | collective-permute-start | bytes 631304 | tf_op jit(solution)/shard_map/ppermute | solution.py:508
  37.2 9.3 %collective-permute-start.19 = (bf16[411,256]{1,0:T(8,128)(2,1)S(1)}, bf16[411,256]{1,0:T(8,128)(2,1)S(1)}, u32[]{:S(2)}, u32[]{:S(2)}) collective-permute-start(bf16[411,256]{1,0:T(8,128)(2,1)S(1)} %collective-permute-done.18.refs_21_.refs_11_), channel_id=1, source_target_pairs={{0,1},{1,0},{2,3},{3,2},{4,5},{5,4},{6,7},{7,6},{8,9},{9,8},{10,11... | collective-permute-start | bytes 631304 | tf_op jit(solution)/shard_map/ppermute | solution.py:508
  37.6 8.9 %collective-permute-start.12 = (bf16[128,768]{1,0:T(8,128)(2,1)}, bf16[128,768]{1,0:T(8,128)(2,1)S(1)}, u32[]{:S(2)}, u32[]{:S(2)}) collective-permute-start(bf16[128,768]{1,0:T(8,128)(2,1)} %refs_11_.1), channel_id=1, source_target_pairs={{0,24},{1,25},{2,10},{3,11},{4,5},{5,4},{6,7},{7,6},{8,9},{9,8},{1... | collective-permute-start | bytes 589832 | tf_op jit(solution)/shard_map/ppermute | solution.py:520
  38.4 35.3 %copy-start.4 = (bf16[411,256]{1,0:T(8,128)(2,1)S(1)}, bf16[411,256]{1,0:T(8,128)(2,1)}, u32[]{:S(2)}) copy-start(bf16[411,256]{1,0:T(8,128)(2,1)} %refs_5_.1) | copy-start | bytes 631300
  46.5 1.9 %copy-start = (bf16[2048,768]{1,0:T(8,128)(2,1)S(1)}, bf16[2048,768]{1,0:T(8,128)(2,1)}, u32[]{:S(2)}) copy-start(bf16[2048,768]{1,0:T(8,128)(2,1)} %refs_0_.1) | copy-start | bytes 9437188
  48.4 0.9 copy-start.3
  49.3 0.9 copy-start.6
  50.3 0.7 copy-start.7
  51.0 22.8 %copy-start.1 = (bf16[2048,768]{1,0:T(8,128)(2,1)S(1)}, bf16[2048,768]{1,0:T(8,128)(2,1)}, u32[]{:S(2)}) copy-start(bf16[2048,768]{1,0:T(8,128)(2,1)} %refs_0_.1) | copy-start | bytes 9437188
  51.0 22.8 %copy-start.2 = (bf16[1536,768]{1,0:T(8,128)(2,1)S(1)}, bf16[1536,768]{1,0:T(8,128)(2,1)}, u32[]{:S(2)}) copy-start(bf16[1536,768]{1,0:T(8,128)(2,1)} %refs_1_.3) | copy-start | bytes 7077892
  61.0 7.9 %collective-permute-start.20 = (bf16[128,768]{1,0:T(8,128)(2,1)S(1)}, bf16[128,768]{1,0:T(8,128)(2,1)S(1)}, u32[]{:S(2)}, u32[]{:S(2)}) collective-permute-start(bf16[128,768]{1,0:T(8,128)(2,1)S(1)} %get-tuple-element.20.refs_0_), channel_id=1, source_target_pairs={{0,2},{1,3},{2,0},{3,1},{4,5},{5,4},{6,7},{7,6},{8,10},{9,11},{10,... | collective-permute-start | bytes 589832 | tf_op jit(solution)/shard_map/ppermute | solution.py:520
  61.1 7.9 %collective-permute-start.21 = (bf16[128,768]{1,0:T(8,128)(2,1)S(1)}, bf16[128,768]{1,0:T(8,128)(2,1)S(1)}, u32[]{:S(2)}, u32[]{:S(2)}) collective-permute-start(bf16[128,768]{1,0:T(8,128)(2,1)S(1)} %get-tuple-element.21.refs_1_), channel_id=1, source_target_pairs={{0,4},{1,5},{2,3},{3,2},{4,0},{5,1},{6,7},{7,6},{8,9},{9,8},{10,14... | collective-permute-start | bytes 589832 | tf_op jit(solution)/shard_map/ppermute | solution.py:520
  61.1 10.2 %collective-permute-start.22 = (bf16[128,768]{1,0:T(8,128)(2,1)S(1)}, bf16[128,768]{1,0:T(8,128)(2,1)S(1)}, u32[]{:S(2)}, u32[]{:S(2)}) collective-permute-start(bf16[128,768]{1,0:T(8,128)(2,1)S(1)} %get-tuple-element.20.refs_0_), channel_id=1, source_target_pairs={{0,4},{1,5},{2,3},{3,2},{4,0},{5,1},{6,7},{7,6},{8,9},{9,8},{10,14... | collective-permute-start | bytes 589832 | tf_op jit(solution)/shard_map/ppermute | solution.py:520
  63.2 8.2 %collective-permute-start.23 = (bf16[128,768]{1,0:T(8,128)(2,1)S(1)}, bf16[128,768]{1,0:T(8,128)(2,1)S(1)}, u32[]{:S(2)}, u32[]{:S(2)}) collective-permute-start(bf16[128,768]{1,0:T(8,128)(2,1)S(1)} %get-tuple-element.21.refs_1_), channel_id=1, source_target_pairs={{0,2},{1,3},{2,0},{3,1},{4,5},{5,4},{6,7},{7,6},{8,10},{9,11},{10,... | collective-permute-start | bytes 589832 | tf_op jit(solution)/shard_map/ppermute | solution.py:520
  68.9 2.5 %collective-permute-start.24 = (bf16[128,768]{1,0:T(8,128)(2,1)S(1)}, bf16[128,768]{1,0:T(8,128)(2,1)S(1)}, u32[]{:S(2)}, u32[]{:S(2)}) collective-permute-start(bf16[128,768]{1,0:T(8,128)(2,1)S(1)} %collective-permute-done.20.refs_2_), channel_id=1, source_target_pairs={{0,1},{1,0},{2,6},{3,7},{4,5},{5,4},{6,2},{7,3},{8,12},{9,13},{10,... | collective-permute-start | bytes 589832 | tf_op jit(solution)/shard_map/ppermute | solution.py:520
  69.0 2.4 %collective-permute-start.25 = (bf16[128,768]{1,0:T(8,128)(2,1)S(1)}, bf16[128,768]{1,0:T(8,128)(2,1)S(1)}, u32[]{:S(2)}, u32[]{:S(2)}) collective-permute-start(bf16[128,768]{1,0:T(8,128)(2,1)S(1)} %collective-permute-done.21.refs_3_), channel_id=1, source_target_pairs={{0,1},{1,0},{2,3},{3,2},{4,6},{5,7},{6,4},{7,5},{8,9},{9,8},{10,11... | collective-permute-start | bytes 589832 | tf_op jit(solution)/shard_map/ppermute | solution.py:520
  72.0 1.8 %collective-permute-start.26 = (bf16[256,768]{1,0:T(8,128)(2,1)S(1)}, bf16[256,768]{1,0:T(8,128)(2,1)S(1)}, u32[]{:S(2)}, u32[]{:S(2)}) collective-permute-start(bf16[256,768]{1,0:T(8,128)(2,1)S(1)} %shard_map.104.refs_3_), channel_id=1, source_target_pairs={{0,1},{1,0},{2,3},{3,2},{4,5},{5,4},{6,7},{7,6},{8,9},{9,8},{10,11... | collective-permute-start | bytes 1179656 | tf_op jit(solution)/shard_map/ppermute | solution.py:508
  83.0 1.8 %collective-permute-start.27 = (bf16[384,411]{1,0:T(8,128)(2,1)S(1)}, bf16[384,411]{1,0:T(8,128)(2,1)S(1)}, u32[]{:S(2)}, u32[]{:S(2)}) collective-permute-start(bf16[384,411]{1,0:T(8,128)(2,1)S(1)} %get-tuple-element.23), channel_id=1, source_target_pairs={{0,1},{1,0},{2,3},{3,2},{4,5},{5,4},{6,7},{7,6},{8,9},{9,8},{10,11... | collective-permute-start | bytes 946952 | tf_op jit(solution)/shard_map/ppermute | solution.py:508
  84.9 5.9 %collective-permute-start.28 = (bf16[96,411]{1,0:T(8,128)(2,1)S(1)}, bf16[96,411]{1,0:T(8,128)(2,1)S(1)}, u32[]{:S(2)}, u32[]{:S(2)}) collective-permute-start(bf16[96,411]{1,0:T(8,128)(2,1)S(1)} %get-tuple-element.25), channel_id=1, source_target_pairs={{0,2},{1,3},{2,0},{3,1},{4,6},{5,7},{6,4},{7,5},{8,10},{9,11},{10,... | collective-permute-start | bytes 236744 | tf_op jit(solution)/shard_map/ppermute | solution.py:508
  87.7 6.2 %collective-permute-start.29 = (bf16[96,411]{1,0:T(8,128)(2,1)S(1)}, bf16[96,411]{1,0:T(8,128)(2,1)S(1)}, u32[]{:S(2)}, u32[]{:S(2)}) collective-permute-start(bf16[96,411]{1,0:T(8,128)(2,1)S(1)} %get-tuple-element.26), channel_id=1, source_target_pairs={{0,4},{1,5},{2,6},{3,7},{4,0},{5,1},{6,2},{7,3},{8,12},{9,13},{10,... | collective-permute-start | bytes 236744 | tf_op jit(solution)/shard_map/ppermute | solution.py:508
  89.7 5.5 %collective-permute-start.30 = (bf16[96,411]{1,0:T(8,128)(2,1)S(1)}, bf16[96,411]{1,0:T(8,128)(2,1)S(1)}, u32[]{:S(2)}, u32[]{:S(2)}) collective-permute-start(bf16[96,411]{1,0:T(8,128)(2,1)S(1)} %get-tuple-element.27), channel_id=1, source_target_pairs={{0,6},{1,7},{2,4},{3,5},{4,2},{5,3},{6,0},{7,1},{8,14},{9,15},{10,... | collective-permute-start | bytes 236744 | tf_op jit(solution)/shard_map/ppermute | solution.py:508
  95.5 5.8 %collective-permute-start.31 = (bf16[32,411]{1,0:T(8,128)(2,1)S(1)}, bf16[32,411]{1,0:T(8,128)(2,1)S(1)}, u32[]{:S(2)}, u32[]{:S(2)}) collective-permute-start(bf16[32,411]{1,0:T(8,128)(2,1)S(1)} %get-tuple-element.29), channel_id=1, source_target_pairs={{0,8},{8,16},{16,24},{24,0},{1,9},{9,17},{17,25},{25,1},{2,10},{10... | collective-permute-start | bytes 78920 | tf_op jit(solution)/shard_map/ppermute | solution.py:511
  95.5 5.7 %collective-permute-start.32 = (bf16[32,411]{1,0:T(8,128)(2,1)S(1)}, bf16[32,411]{1,0:T(8,128)(2,1)S(1)}, u32[]{:S(2)}, u32[]{:S(2)}) collective-permute-start(bf16[32,411]{1,0:T(8,128)(2,1)S(1)} %get-tuple-element.30), channel_id=1, source_target_pairs={{0,16},{8,24},{16,0},{24,8},{1,17},{9,25},{17,1},{25,9},{2,18},{10... | collective-permute-start | bytes 78920 | tf_op jit(solution)/shard_map/ppermute | solution.py:511
  95.6 6.2 %collective-permute-start.33 = (bf16[32,411]{1,0:T(8,128)(2,1)S(1)}, bf16[32,411]{1,0:T(8,128)(2,1)S(1)}, u32[]{:S(2)}, u32[]{:S(2)}) collective-permute-start(bf16[32,411]{1,0:T(8,128)(2,1)S(1)} %get-tuple-element.31), channel_id=1, source_target_pairs={{0,24},{8,0},{16,8},{24,16},{1,25},{9,1},{17,9},{25,17},{2,26},{10... | collective-permute-start | bytes 78920 | tf_op jit(solution)/shard_map/ppermute | solution.py:511

commit v3 on v2

--- a/solution.py
+++ b/solution.py
@@ -8,6 +8,8 @@
 from jax.sharding import PartitionSpec as P
 
 VMEM_BYTES = 24 * 1024 * 1024
+WHOLE_VMEM_BYTES = 63 * 1024 * 1024
+SLACK_FLOPS = 5 * 10**9
 NT_DIMS = (((1,), (1,)), ((), ()))
 
 
@@ -154,7 +156,9 @@
     return high, middle, value - high - middle
 
 
-def call(kernel, out_shape, args, in_hbm=(), out_hbm=False, scratch=(), flops=0):
+def call(
+    kernel, out_shape, args, in_hbm=(), out_hbm=False, scratch=(), flops=0, vmem=VMEM_BYTES
+):
     far, near = pl.BlockSpec(memory_space=pl.ANY), pl.BlockSpec(memory_space=pltpu.VMEM)
     bytes_accessed = sum(a.size * a.dtype.itemsize for a in args)
     return pl.pallas_call(
@@ -163,7 +167,7 @@
         in_specs=[far if k in in_hbm else near for k in range(len(args))],
         out_specs=jax.tree.map(lambda _: far if out_hbm else near, out_shape),
         scratch_shapes=list(scratch),
-        compiler_params=pltpu.CompilerParams(vmem_limit_bytes=VMEM_BYTES),
+        compiler_params=pltpu.CompilerParams(vmem_limit_bytes=vmem),
         cost_estimate=pl.CostEstimate(
             flops=flops, bytes_accessed=bytes_accessed, transcendentals=0
         ),
@@ -196,10 +200,32 @@
         self.per_row = self.own_cols + 2
         self.room = up_to(3 * self.per_row, 16)
         self.patch = 3 * tiles * self.own_cols
-
-
-def prepare_kernel(p, fields_ref, diffusivity_ref, usable_ref, bias_ref, out_ref, flat, packed, sem):
+        self.deep = up_to(self.features, 16)
+        self.strips = self.chips * tiles * self.block
+
+    def order(self, mask):
+        return mask % self.group * self.chips + mask // self.group
+
+    def layer(self, refs, k):
+        at = k % self.chips * self.deep
+        return refs[k // self.chips][at : at + self.features, :]
+
+    def mask(self, k):
+        return k % self.chips * self.group + k // self.chips
+
+
+def prepare_kernel(p, *refs):
+    ins, out_ref = refs[:4], refs[4]
+    fields_ref, diffusivity_ref, usable_ref, bias_ref, flat, packed, sems = refs[5:]
+    copies = [
+        pltpu.make_async_copy(source, target, sems.at[k])
+        for k, (source, target) in enumerate(zip(ins, refs[5:9]))
+    ]
+    for copy in copies:
+        copy.start()
     flat[...] = jnp.zeros(flat.shape, jnp.float32)
+    for copy in copies:
+        copy.wait()
     shape = (p.own_cols, p.along)
     row = lax.broadcasted_iota(jnp.int32, shape, 0)
     member = row == lax.broadcasted_iota(jnp.int32, shape, 1) // 4
@@ -220,30 +246,60 @@
     for k, part in enumerate(split_three(diffusivity_ref[...])):
         flat[at + 2 : at + 2 + p.across, k * p.lane : k * p.lane + p.along] = part
     packed[...] = flat[...].astype(jnp.bfloat16)
-    copy = pltpu.make_async_copy(packed, out_ref, sem)
+    copy = pltpu.make_async_copy(packed, out_ref, sems.at[4])
     copy.start()
     copy.wait()
 
 
-def place_kernel(p, owners_ref, out_ref):
+def place_kernel(p, owners_ref, place_ref, source_ref, cell_ref, *target_refs):
+    t, c = lax.axis_index("tile"), lax.axis_index("chan")
     owner = owners_ref[...]
     shape = (p.rows, p.rows)
     row = lax.broadcasted_iota(jnp.int32, shape, 0)
     other = lax.broadcasted_iota(jnp.int32, shape, 1)
     across = jnp.sum(jnp.where(row == other, owner, 0), axis=0, keepdims=True)
-    same = (owner == across) & (row // p.tile_cols == other // p.tile_cols) & (other < row)
+    first = lax.broadcasted_iota(jnp.int32, owner.shape, 0)
+    begin = first // p.tile_cols * p.tile_cols
+    same = (owner == across) & (other >= begin) & (other < row)
     rank = jnp.sum(jnp.where(same, 1, 0), axis=1, keepdims=True)
-    number = lax.broadcasted_iota(jnp.int32, owner.shape, 0)
-    near = (owner + p.tiles - lax.axis_index("tile")) % p.tiles
-    out_ref[...] = near * p.slots + number // p.tile_cols * p.capacity + rank
-
-
-def join_kernel(*refs):
-    count = (len(refs) - 2) // 1
-    ins, out_ref, sems = refs[:count], refs[count], refs[count + 1]
-    size = ins[0].shape[0]
+    tile = first // p.tile_cols
+    place_ref[...] = (owner ^ t) * p.slots + tile * p.capacity + rank
+
+    def strip(tile, chan):
+        other = chan ^ c
+        return p.order(other) * p.tiles + (tile ^ t)
+
+    source_ref[...] = (
+        strip(tile, first % p.tile_cols // p.own_cols) * p.block + first % p.own_cols
+    )
+
+    row = lax.broadcasted_iota(jnp.int32, cell_ref.shape, 0)
+    reach = p.across + 4
+    tile = (t + row // reach - 1 + p.tiles) % p.tiles
+    cell = c * p.across - 2 + row % reach
+    inside = (cell >= 0) & (cell < p.chans * p.across)
+    cell = jnp.where(inside, cell, 0)
+    wanted = strip(tile, cell // p.across) * p.block + p.own_cols + 2 + cell % p.across
+    cell_ref[...] = jnp.where(inside, wanted, -1)
+
+    target = lax.broadcasted_iota(jnp.int32, target_refs[0].shape, 0)
+    chip, inner = target // p.patch, target % p.patch
+    beside, inner = inner // (p.patch // 3) - 1, inner % (p.patch // 3)
+    tile, along = inner // p.own_cols, inner % p.own_cols
+    for k, target_ref in enumerate(target_refs):
+        row = ((chip ^ (c // p.group)) * p.group + (c % p.group ^ k)) + beside
+        wanted = tile * p.tile_cols + row * p.own_cols + along
+        target_ref[...] = jnp.where((row >= 0) & (row < p.chans), wanted, -1)
+
+
+def join_kernel(count, *refs):
+    ins, out_ref, sems = refs[:count], refs[-2], refs[-1]
+    size = out_ref.shape[0] // count
     copies = [
-        pltpu.make_async_copy(ref, out_ref.at[pl.ds(k * size, size)], sems.at[k])
+        pltpu.make_async_copy(
+            ref, out_ref.at[k] if ref.ndim < out_ref.ndim else out_ref.at[pl.ds(k * size, size)],
+            sems.at[k],
+        )
         for k, ref in enumerate(ins)
     ]
     for copy in copies:
@@ -252,84 +308,69 @@
         copy.wait()
 
 
+def stack_kernel(p, *refs):
+    for k, ref in enumerate(refs[: p.chips]):
+        refs[-1][k * p.deep : k * p.deep + p.features, :] = ref[...]
+        refs[-1][k * p.deep + p.features : (k + 1) * p.deep, :] = jnp.zeros(
+            (p.deep - p.features, p.hidden), jnp.bfloat16
+        )
+
+
+def one_hot(wanted, first, count):
+    source = lax.broadcasted_iota(jnp.int32, (wanted.shape[0], count), 1)
+    return (source + first == wanted).astype(jnp.bfloat16)
+
+
 def forward_kernel(p, *refs):
     refs = list(refs)
     take = lambda n: [refs.pop(0) for _ in range(n)]
-    place_ref, bias_ref, w_radiance_ref = take(3)
-    gathered_refs, seen_refs, weight_refs = take(p.chans), take(p.tiles), take(p.chans)
-    *part_refs, slope_out, kappa_out = take(p.steps + 2)
-    stack, seen, weights, slope, active, departure, kappa, sems = take(8)
-    t, c = lax.axis_index("tile"), lax.axis_index("chan")
-    count = iter(range(3 * p.chans + p.tiles + p.steps + 1))
-
-    def begin(source, target):
-        copy = pltpu.make_async_copy(source, target, sems.at[next(count)])
-        copy.start()
-        return copy
-
-    wide = p.tiles * p.block
-    packs = [
-        begin(ref, stack.at[pl.ds(k * wide, wide)]) for k, ref in enumerate(gathered_refs)
-    ]
-    loads = [begin(ref, weights.at[k]) for k, ref in enumerate(weight_refs)]
-    views = [begin(ref, seen.at[k]) for k, ref in enumerate(seen_refs)]
-    for copy in packs:
-        copy.wait()
-    shape = (p.rows, p.chans * wide)
-    row = lax.broadcasted_iota(jnp.int32, shape, 0)
-    source = lax.broadcasted_iota(jnp.int32, shape, 1)
-    tile = (row // p.tile_cols + p.tiles - t) % p.tiles
-    chan = (row % p.tile_cols // p.own_cols) ^ c
-    pick = source == chan * wide + tile * p.block + row % p.own_cols
-    everything = stack[...]
-    columns = dot(pick.astype(jnp.bfloat16), everything).astype(jnp.bfloat16)[:, : p.features]
-    out = []
+    place_ref, source_ref, cell_ref, bias_ref, w_radiance_ref = take(5)
+    strip_refs, weight_refs, seen_refs = take(p.group), take(p.group), take(2)
+    part_refs = take(p.steps)
+    slope_ref, kappa_ref, active = refs
+    c = lax.axis_index("chan")
+    gathered = [ref[...] for ref in strip_refs]
+    columns = sum(
+        dot(one_hot(source_ref[...], k * p.strips, p.strips), strips)
+        for k, strips in enumerate(gathered)
+    )
+    columns = columns.astype(jnp.bfloat16)[:, : p.features]
     for k in range(p.chans):
-        loads[k].wait()
-        low = stack[k * wide + p.own_cols : k * wide + p.own_cols + 2, :].astype(jnp.float32)
+        member, chip = k // p.chips, k % p.chips
+        at = chip * p.tiles * p.block + p.own_cols
+        low = strip_refs[member][at : at + 2, :].astype(jnp.float32)
         bias = (
             low[:1, : p.hidden]
             + low[:1, p.flag_at : p.flag_at + p.hidden]
             + low[1:, : p.hidden]
         )
-        preact = dot(columns, weights[k]) + bias
+        preact = dot(columns, p.layer(weight_refs, k)) + bias
         squash = jax.nn.sigmoid(preact)
-        slope[k] = squash * (1.0 + preact * (1.0 - squash))
-        out.append(begin(slope.at[k], slope_out.at[k]))
-        at = pl.multiple_of((c ^ k) * p.hidden, p.hidden)
+        slope_ref[k] = squash * (1.0 + preact * (1.0 - squash))
+        at = pl.multiple_of((c ^ p.mask(k)) * p.hidden, p.hidden)
         active[:, pl.ds(at, p.hidden)] = (preact * squash).astype(jnp.bfloat16)
-    for copy in views:
-        copy.wait()
     part = p.rows // p.steps
-    slot = lax.broadcasted_iota(jnp.int32, (part, p.slots), 1)
+    count = seen_refs[0].shape[0]
     for j, part_ref in enumerate(part_refs):
         at = slice(j * part, (j + 1) * part)
         in_use = jnp.zeros((part, 1), jnp.float32)
-        observed = jnp.zeros((part, p.shard), jnp.float32)
         for k in range(p.tiles):
-            hit = place_ref[at, :] == slot + k * p.slots
+            slot = lax.broadcasted_iota(jnp.int32, (part, p.slots), 1) + k * p.slots
             low = k * p.block + p.own_cols + 1
-            flags = stack[low : low + 1, p.flag_at : p.flag_at + p.slots].astype(jnp.float32)
-            in_use = in_use + jnp.sum(jnp.where(hit, flags, 0.0), axis=1, keepdims=True)
-            observed = observed + dot(hit.astype(jnp.bfloat16), seen[k])
+            flags = strip_refs[0][low : low + 1, p.flag_at : p.flag_at + p.slots]
+            flags = jnp.where(place_ref[at, :] == slot, flags.astype(jnp.float32), 0.0)
+            in_use = in_use + jnp.sum(flags, axis=1, keepdims=True)
+        observed = sum(
+            dot(one_hot(place_ref[at, :], k * count, count), ref[...])
+            for k, ref in enumerate(seen_refs)
+        )
         radiance = dot(active[at, :], w_radiance_ref[...]) + bias_ref[...].reshape(1, p.shard)
-        departure[at, :] = ((radiance - observed) * in_use).astype(jnp.bfloat16)
-        out.append(begin(departure.at[pl.ds(j * part, part)], part_ref))
-    reach = p.across + 4
-    shape = (3 * reach, p.chans * wide)
-    row = lax.broadcasted_iota(jnp.int32, shape, 0)
-    source = lax.broadcasted_iota(jnp.int32, shape, 1)
-    tile = (row // reach - 1 + p.tiles) % p.tiles
-    cell = c * p.across - 2 + row % reach
-    inside = (cell >= 0) & (cell < p.chans * p.across)
-    cell = jnp.where(inside, cell, 0)
-    wanted = (cell // p.across ^ c) * wide + tile * p.block + p.own_cols + 2 + cell % p.across
-    pick = (source == wanted) & inside
-    parts = dot(pick.astype(jnp.bfloat16), everything)
-    kappa[...] = sum(parts[:, k * p.lane : (k + 1) * p.lane] for k in range(3))
-    out.append(begin(kappa, kappa_out))
-    for copy in out:
-        copy.wait()
+        part_ref[...] = ((radiance - observed) * in_use).astype(jnp.bfloat16)
+    parts = sum(
+        dot(one_hot(cell_ref[...], k * p.strips, p.strips), strips)
+        for k, strips in enumerate(gathered)
+    )
+    kappa_ref[...] = sum(parts[:, k * p.lane : (k + 1) * p.lane] for k in range(3))
 
 
 def choose_kernel(p, choices, *refs):
@@ -355,60 +396,25 @@
 def backward_kernel(p, *refs):
     refs = list(refs)
     take = lambda n: [refs.pop(0) for _ in range(n)]
-    (w_radiance_ref,) = take(1)
-    inv_cov_ref, slope_ref = take(2)
-    depart_refs, weight_refs, out_refs = take(p.group), take(p.chans), take(p.group)
-    inv_cov, slope, depart, weights, result, sems = take(6)
-    t, c = lax.axis_index("tile"), lax.axis_index("chan")
-    count = iter(range(2 * p.group + 2 * p.chans + p.group))
-
-    def begin(source, target):
-        copy = pltpu.make_async_copy(source, target, sems.at[next(count)])
-        copy.start()
-        return copy
-
-    loads = []
+    w_radiance_ref, inv_cov_ref, slope_ref = take(3)
+    depart_refs, weight_refs, target_refs = take(p.group), take(p.group), take(p.group)
+    out_refs = refs
+    c = lax.axis_index("chan")
+    cotangent = None
     for k, ref in enumerate(depart_refs):
         at = pl.multiple_of((c % p.group ^ k) * p.shard, p.shard)
-        loads.append(
-            (
-                begin(ref, depart.at[k]),
-                begin(inv_cov_ref.at[pl.ds(at, p.shard)], inv_cov.at[k]),
-            )
-        )
-    slopes = [begin(slope_ref.at[k], slope.at[k]) for k in range(p.chans)]
-    firsts = [begin(ref, weights.at[k]) for k, ref in enumerate(weight_refs)]
-    cotangent = None
-    for k, copies in enumerate(loads):
-        for copy in copies:
-            copy.wait()
-        term = dot(depart[k], inv_cov[k])
+        term = dot(ref[...], inv_cov_ref[pl.ds(at, p.shard), :])
         cotangent = term if cotangent is None else cotangent + term
     cotangent = cotangent.astype(jnp.bfloat16)
     total = jnp.zeros((p.rows, p.features), jnp.float32)
     for k in range(p.chans):
-        at = pl.multiple_of((c ^ k) * p.hidden, p.hidden)
+        at = pl.multiple_of((c ^ p.mask(k)) * p.hidden, p.hidden)
         grad_hidden = dot_nt(cotangent, w_radiance_ref[pl.ds(at, p.hidden), :])
-        slopes[k].wait()
-        firsts[k].wait()
-        grad_pre = (grad_hidden * slope[k]).astype(jnp.bfloat16)
-        total = total + dot_nt(grad_pre, weights[k])
+        grad_pre = (grad_hidden * slope_ref[k]).astype(jnp.bfloat16)
+        total = total + dot_nt(grad_pre, p.layer(weight_refs, k))
     total = total.astype(jnp.bfloat16)
-    shape = (p.chips * p.patch, p.rows)
-    target = lax.broadcasted_iota(jnp.int32, shape, 0)
-    source = lax.broadcasted_iota(jnp.int32, shape, 1)
-    chip, inner = target // p.patch, target % p.patch
-    beside, inner = inner // (p.patch // 3) - 1, inner % (p.patch // 3)
-    tile, along = inner // p.own_cols, inner % p.own_cols
-    copies = []
-    for k in range(p.group):
-        row = ((chip ^ (c // p.group)) * p.group + (c % p.group ^ k)) + beside
-        wanted = tile * p.tile_cols + row * p.own_cols + along
-        pick = (source == wanted) & (row >= 0) & (row < p.chans)
-        result[k] = dot(pick.astype(jnp.bfloat16), total).astype(jnp.bfloat16)
-        copies.append(begin(result.at[k], out_refs[k]))
-    for copy in copies:
-        copy.wait()
+    for target_ref, out_ref in zip(target_refs, out_refs):
+        out_ref[...] = dot(one_hot(target_ref[...], 0, p.rows), total).astype(jnp.bfloat16)
 
 
 def add(refs, at=slice(None)):
@@ -521,66 +527,85 @@
             value, both, sorted((number(a), number(b)) for a, b in pairs.items())
         )
 
-    weights = [None] * p.chans
-    weights[0] = w_hidden
-    for chip in range(1, p.chips):
-        weights[chip * p.group] = flip(w_hidden, chip * p.group)
-
-    seen = [observed] + [
-        send(
-            observed,
-            {((b // p.group + k) % p.tiles, b): (b // p.group, b) for b in range(p.chans)},
-        )
-        for k in range(1, p.tiles)
-    ]
-
-    packed = call(
+    def join(values, kernel_shape, after=()):
+        return call(
+            functools.partial(join_kernel, len(values)),
+            shape(kernel_shape, half),
+            [*values, *after],
+            in_hbm=range(len(values) + len(after)),
+            out_hbm=True,
+            scratch=[pltpu.SemaphoreType.DMA((len(values),))],
+            flops=0,
+        )
+
+    def grow(value, over, after=()):
+        return join([value, over(value)], (2 * value.shape[0],) + value.shape[1:], after)
+
+    def trade(value, mask):
+        return lax.ppermute(value, "tile", [(a, a ^ mask) for a in range(p.tiles)])
+
+    strips = call(
         functools.partial(prepare_kernel, p),
         shape((p.block, p.width), half),
         [fields, diffusivity, usable, b_hidden],
+        in_hbm=range(4),
         out_hbm=True,
         scratch=[
+            pltpu.VMEM(fields.shape, single),
+            pltpu.VMEM(diffusivity.shape, single),
+            pltpu.VMEM(usable.shape, jnp.int32),
+            pltpu.VMEM(b_hidden.shape, single),
             pltpu.VMEM((p.block, p.width), single),
             pltpu.VMEM((p.block, p.width), half),
-            pltpu.SemaphoreType.DMA,
+            pltpu.SemaphoreType.DMA((5,)),
         ],
-    )
-    strips = [packed] + [shift(packed, p.tiles - k) for k in range(1, p.tiles)]
-    joined = call(
-        join_kernel,
-        shape((p.tiles * p.block, p.width), half),
-        strips,
-        in_hbm=range(p.tiles),
-        out_hbm=True,
-        scratch=[pltpu.SemaphoreType.DMA((p.tiles,))],
-    )
-    gathered = [joined] + [None] * (p.chans - 1)
-    for chip in range(1, p.chips):
-        gathered[chip * p.group] = flip(joined, chip * p.group)
-    for held in (weights, gathered):
-        for k in range(p.chans):
-            if k % p.group:
-                held[k] = flip(held[k - k % p.group], k % p.group)
-    place = call(functools.partial(place_kernel, p), shape((p.rows, 1), jnp.int32), [owners])
+        vmem=WHOLE_VMEM_BYTES,
+    )
+    seen, stages = observed, []
+    bit = 1
+    while bit < p.tiles:
+        if 2 * bit < p.tiles:
+            seen = grow(seen, lambda value: trade(value, bit))
+        strips = grow(strips, lambda value: trade(value, bit), [seen] if 2 * bit == p.tiles else ())
+        stages.append(strips)
+        bit *= 2
+    bit = p.group
+    while bit < p.chans:
+        strips = grow(strips, lambda value: flip(value, bit))
+        stages.append(strips)
+        bit *= 2
+    strips = [strips] + [flip(strips, k) for k in range(1, p.group)]
+
+    near = [w_hidden] + [flip(w_hidden, chip * p.group) for chip in range(1, p.chips)]
+    near = call(
+        functools.partial(stack_kernel, p),
+        shape((p.chips * p.deep, p.hidden), half),
+        near + [stages[-2]],
+        in_hbm=[len(near)],
+    )
+    weights = [near] + [flip(near, k) for k in range(1, p.group)]
+
+    far_half = p.tiles // 2
+    seen = [
+        seen,
+        send(seen, {(b // p.group ^ far_half, b): (b // p.group, b) for b in range(p.chans)}),
+    ]
 
     reach = p.across + 4
+    place, source, cell, *targets = call(
+        functools.partial(place_kernel, p),
+        [shape((p.rows, 1), jnp.int32)] * 2
+        + [shape((3 * reach, 1), jnp.int32)]
+        + [shape((p.chips * p.patch, 1), jnp.int32)] * p.group,
+        [owners],
+        flops=SLACK_FLOPS,
+    )
     *parts, slope, kappa = call(
         functools.partial(forward_kernel, p),
         [shape((p.rows // p.steps, p.shard), half)] * p.steps
         + [shape((p.chans, p.rows, p.hidden), single), shape((3 * reach, p.lane), single)],
-        [place, b_radiance, w_radiance] + gathered + seen + weights,
-        in_hbm=range(3, 3 + 2 * p.chans + p.tiles),
-        out_hbm=True,
-        scratch=[
-            pltpu.VMEM((p.chans * p.tiles * p.block, p.width), half),
-            pltpu.VMEM((p.tiles, p.slots, p.shard), half),
-            pltpu.VMEM((p.chans, p.features, p.hidden), half),
-            pltpu.VMEM((p.chans, p.rows, p.hidden), single),
-            pltpu.VMEM((p.rows, p.hidden * p.chans), half),
-            pltpu.VMEM((p.rows, p.shard), half),
-            pltpu.VMEM((3 * reach, p.lane), single),
-            pltpu.SemaphoreType.DMA((3 * p.chans + p.tiles + p.steps + 1,)),
-        ],
+        [place, source, cell, b_radiance, w_radiance] + strips + weights + seen,
+        scratch=[pltpu.VMEM((p.rows, p.hidden * p.chans), half)],
         flops=2 * p.rows * p.hidden * p.chans * (p.features + p.shard),
     )
 
@@ -615,21 +640,10 @@
     )
     depart = [chosen] + [flip(chosen, k) for k in range(1, p.group)]
 
-    count = p.group + p.chans
     partial = call(
         functools.partial(backward_kernel, p),
         [shape((p.chips * p.patch, p.features), half)] * p.group,
-        [w_radiance, inv_cov, slope] + depart + weights,
-        in_hbm=range(1, 3 + count),
-        out_hbm=True,
-        scratch=[
-            pltpu.VMEM((p.group, p.shard, p.shard), half),
-            pltpu.VMEM((p.chans, p.rows, p.hidden), single),
-            pltpu.VMEM((p.group, p.rows, p.shard), half),
-            pltpu.VMEM((p.chans, p.features, p.hidden), half),
-            pltpu.VMEM((p.group, p.chips * p.patch, p.features), half),
-            pltpu.SemaphoreType.DMA((2 * p.group + 2 * p.chans + p.group,)),
-        ],
+        [w_radiance, inv_cov, slope] + depart + weights + targets,
         flops=2 * p.rows * (p.hidden * p.chans * (p.features + p.shard) + inv_cov.size),
     )
     partial = [partial[0]] + [flip(partial[k], k) for k in range(1, p.group)]
@@ -664,7 +678,7 @@
 
 def solution(mesh):
     tiles, chans = mesh.shape["tile"], mesh.shape["chan"]
-    by_column = chans % tiles == 0 and chans & (chans - 1) == 0 and chans // tiles > 1
+    by_column = tiles > 1 and chans % tiles == 0 and chans & (chans - 1) == 0 and chans > tiles
     placed = (
         P("chan", "tile", None),
         P("chan", "tile"),

time: 103 us -> 79 us (0.77)
  waiting for transfers between devices: 45.1 us -> 34 us
  Pallas kernels: 22.1 us -> 12.4 us
  local copies, waits for them, and re-layouts: 8.37 us -> 2.88 us
  starting transfers between devices: 27.4 us -> 29.2 us
    ppermute x9 -> x7, waiting for transfers between devices: 24.9 us -> 14.3 us  [send(): lax.ppermute(value, both, sorted(((number(a), number(b)) for a, b in pair...]
    pallas_call x9 -> x14, Pallas kernels: 22.1 us -> 12.4 us  [call(): pl.pallas_call(kernel, out_shape=out_shape, in_specs=[far if k in in_hbm...]
    ppermute x0 -> x3, starting transfers between devices: none -> 5.82 us  [trade(): return lax.ppermute(value, 'tile', [(a, a ^ mask) for a in range(p.tiles)])]
    unnamed x23 -> x15, local copies, waits for them, and re-layouts: 8.21 us -> 2.73 us
    ppermute x6 -> x3, starting transfers between devices: 9.98 us -> 5.29 us  [shift(): lax.ppermute(value, 'tile', [(a, (a + by) % p.tiles) for a in range(p.til...]
    ppermute x0 -> x3, waiting for transfers between devices: none -> 4.67 us  [trade(): return lax.ppermute(value, 'tile', [(a, a ^ mask) for a in range(p.tiles)])]
    ppermute x6 -> x3, waiting for transfers between devices: 6.81 us -> 2.41 us  [shift(): lax.ppermute(value, 'tile', [(a, (a + by) % p.tiles) for a in range(p.til...]
    ppermute x9 -> x7, starting transfers between devices: 4.22 us -> 5.45 us  [send(): lax.ppermute(value, both, sorted(((number(a), number(b)) for a, b in pair...]
  transfers between devices with their start and end apart: 34 -> 25, of which waited for: 18 -> 16; matrix products, arithmetic and copies ran while one was open for 1% -> 0% of each run, Pallas kernels for 0% -> 5%
where the time goes in v3:
time: 79 us; the launch traced here: 78.8 us
  waiting for transfers between devices  34 us (43%)
  starting transfers between devices  29.2 us (37%)
  Pallas kernels  12.4 us (16%)
  local copies, waits for them, and re-layouts  2.88 us (4%)
    ppermute x7, waiting for transfers between devices, send(): lax.ppermute(value, both, sorted(((number(a), number(b)) for a, b in pair...  14.3 us
    ppermute x12, waiting for transfers between devices, flip(): return lax.ppermute(value, 'chan', [(b, b ^ mask) for b in range(p.chans)])  12.6 us
    ppermute x12, starting transfers between devices, flip(): return lax.ppermute(value, 'chan', [(b, b ^ mask) for b in range(p.chans)])  12.6 us
    pallas_call x14, Pallas kernels, call(): pl.pallas_call(kernel, out_shape=out_shape, in_specs=[far if k in in_hbm...  12.4 us
    ppermute x3, starting transfers between devices, trade(): return lax.ppermute(value, 'tile', [(a, a ^ mask) for a in range(p.tiles)])  5.82 us
    ppermute x7, starting transfers between devices, send(): lax.ppermute(value, both, sorted(((number(a), number(b)) for a, b in pair...  5.45 us
    ppermute x3, starting transfers between devices, shift(): lax.ppermute(value, 'tile', [(a, (a + by) % p.tiles) for a in range(p.til...  5.29 us
    ppermute x3, waiting for transfers between devices, trade(): return lax.ppermute(value, 'tile', [(a, a ^ mask) for a in range(p.tiles)])  4.67 us
  transfers between devices with their start and end apart: 25, of which 16 were waited for; matrix products, arithmetic and copies ran while one was open for 0% of the time, Pallas kernels for 5%

profile of v3, /device:TPU:0, one launch (start us, length us, event | category | flops | bytes accessed | tf_op | source)
XLA Modules:
  0.0 78.8 jit_solution(4198567979834543031)
XLA Ops:
  0.0 3.0 %collective-permute-start.2 = (bf16[128,768]{1,0:T(8,128)(2,1)}, bf16[128,768]{1,0:T(8,128)(2,1)S(1)}, u32[]{:S(2)}, u32[]{:S(2)}) collective-permute-start(bf16[128,768]{1,0:T(8,128)(2,1)} %refs_0_.5), channel_id=1, source_target_pairs={{0,8},{8,0},{16,24},{24,16},{1,9},{9,1},{17,25},{25,17},{2,10},{10... | collective-permute-start | bytes 589832 | tf_op jit(solution)/shard_map/ppermute | solution.py:545
  3.0 1.5 %collective-permute-start.7 = (bf16[411,256]{1,0:T(8,128)(2,1)}, bf16[411,256]{1,0:T(8,128)(2,1)S(1)}, u32[]{:S(2)}, u32[]{:S(2)}) collective-permute-start(bf16[411,256]{1,0:T(8,128)(2,1)} %refs_0_.6), channel_id=1, source_target_pairs={{0,4},{1,5},{2,6},{3,7},{4,0},{5,1},{6,2},{7,3},{8,12},{9,13},{10,... | collective-permute-start | bytes 631304 | tf_op jit(solution)/shard_map/ppermute | solution.py:514
  4.5 1.5 %collective-permute-start.6 = (bf16[411,256]{1,0:T(8,128)(2,1)}, bf16[411,256]{1,0:T(8,128)(2,1)S(1)}, u32[]{:S(2)}, u32[]{:S(2)}) collective-permute-start(bf16[411,256]{1,0:T(8,128)(2,1)} %refs_0_.6), channel_id=1, source_target_pairs={{0,2},{1,3},{2,0},{3,1},{4,6},{5,7},{6,4},{7,5},{8,10},{9,11},{10,... | collective-permute-start | bytes 631304 | tf_op jit(solution)/shard_map/ppermute | solution.py:514
  6.0 0.5 collective-permute-start.8
  6.5 1.8 %shard_map.101.refs_0_ = bf16[16,512]{1,0:T(8,128)(2,1)} custom-call(f32[4,32,411]{2,1,0:T(8,128)} %refs_0_.4, f32[4,32]{1,0:T(4,128)} %refs_1_.2, s32[128]{0:T(128)} %refs_2_.1, f32[256]{0:T(256)} %refs_3_.2), custom_call_target="tpu_custom_call" | custom-call | bytes 212480 | tf_op jit(solution)/shard_map/pallas_call | solution.py:164
  8.3 0.1 collective-permute-start
  8.4 3.9 %collective-permute-done.refs_1_ = bf16[16,512]{1,0:T(8,128)(2,1)S(1)} collective-permute-done((bf16[16,512]{1,0:T(8,128)(2,1)}, bf16[16,512]{1,0:T(8,128)(2,1)S(1)}, u32[]{:S(2)}, u32[]{:S(2)}) %collective-permute-start) | collective-permute-done | bytes 16416 | tf_op jit(solution)/shard_map/ppermute | solution.py:545
  12.3 0.7 copy-done.4
  13.1 2.7 %collective-permute-start.1 = (bf16[32,512]{1,0:T(8,128)(2,1)S(1)}, bf16[32,512]{1,0:T(8,128)(2,1)S(1)}, u32[]{:S(2)}, u32[]{:S(2)}) collective-permute-start(bf16[32,512]{1,0:T(8,128)(2,1)S(1)} %shard_map.102.refs_0_), channel_id=1, source_target_pairs={{0,16},{8,24},{16,0},{24,8},{1,17},{9,25},{17,1},{25,9},{2,18},{10... | collective-permute-start | bytes 98312 | tf_op jit(solution)/shard_map/ppermute | solution.py:545
  15.7 0.9 %copy-done.3 = bf16[128,768]{1,0:T(8,128)(2,1)S(1)} copy-done((bf16[128,768]{1,0:T(8,128)(2,1)S(1)}, bf16[128,768]{1,0:T(8,128)(2,1)}, u32[]{:S(2)}) %copy-start.3) | copy-done | bytes 196632
  16.7 0.5 shard_map.103.refs_2_.refs_9_
  17.2 0.8 collective-permute-done.1.refs_1_
  18.0 0.1 shard_map.104.refs_0_
  18.0 1.8 %collective-permute-start.3 = (bf16[64,512]{1,0:T(8,128)(2,1)S(1)}, bf16[64,512]{1,0:T(8,128)(2,1)S(1)}, u32[]{:S(2)}, u32[]{:S(2)}) collective-permute-start(bf16[64,512]{1,0:T(8,128)(2,1)S(1)} %shard_map.104.refs_0_), channel_id=1, source_target_pairs={{0,2},{1,3},{2,0},{3,1},{4,6},{5,7},{6,4},{7,5},{8,10},{9,11},{10,... | collective-permute-start | bytes 196616 | tf_op jit(solution)/shard_map/ppermute | solution.py:514
  19.8 2.5 %collective-permute-done.3.refs_1_ = bf16[64,512]{1,0:T(8,128)(2,1)S(1)} collective-permute-done((bf16[64,512]{1,0:T(8,128)(2,1)S(1)}, bf16[64,512]{1,0:T(8,128)(2,1)S(1)}, u32[]{:S(2)}, u32[]{:S(2)}) %collective-permute-start.3) | collective-permute-done | bytes 65568 | tf_op jit(solution)/shard_map/ppermute | solution.py:514
  22.4 0.2 shard_map.105.refs_0_.refs_4_
  22.6 0.0 copy-start.2
  22.6 0.9 %copy-done.2 = bf16[411,256]{1,0:T(8,128)(2,1)S(1)} copy-done((bf16[411,256]{1,0:T(8,128)(2,1)S(1)}, bf16[411,256]{1,0:T(8,128)(2,1)}, u32[]{:S(2)}) %copy-start.2) | copy-done | bytes 210456
  23.5 0.1 shard_map.107.refs_7_.refs_5_
  23.6 0.1 collective-permute-start.9
  23.7 1.8 %collective-permute-start.4 = (bf16[128,512]{1,0:T(8,128)(2,1)S(1)}, bf16[128,512]{1,0:T(8,128)(2,1)S(1)}, u32[]{:S(2)}, u32[]{:S(2)}) collective-permute-start(bf16[128,512]{1,0:T(8,128)(2,1)S(1)} %shard_map.105.refs_0_.refs_4_), channel_id=1, source_target_pairs={{0,4},{1,5},{2,6},{3,7},{4,0},{5,1},{6,2},{7,3},{8,12},{9,13},{10,... | collective-permute-start | bytes 393224 | tf_op jit(solution)/shard_map/ppermute | solution.py:514
  25.5 0.1 copy.22.owners_ref
  25.6 2.4 %collective-permute-start.10 = (bf16[256,768]{1,0:T(8,128)(2,1)S(1)}, bf16[256,768]{1,0:T(8,128)(2,1)S(1)}, u32[]{:S(2)}, u32[]{:S(2)}) collective-permute-start(bf16[256,768]{1,0:T(8,128)(2,1)S(1)} %shard_map.103.refs_2_.refs_9_), channel_id=1, source_target_pairs={{0,16},{1,17},{2,3},{3,2},{4,20},{5,21},{6,7},{7,6},{8,9},{9,8},{1... | collective-permute-start | bytes 1179656 | tf_op jit(solution)/shard_map/ppermute | solution.py:526
  28.0 1.5 %collective-permute-done.4.refs_1_ = bf16[128,512]{1,0:T(8,128)(2,1)S(1)} collective-permute-done((bf16[128,512]{1,0:T(8,128)(2,1)S(1)}, bf16[128,512]{1,0:T(8,128)(2,1)S(1)}, u32[]{:S(2)}, u32[]{:S(2)}) %collective-permute-start.4) | collective-permute-done | bytes 131104 | tf_op jit(solution)/shard_map/ppermute | solution.py:514
  29.6 0.3 shard_map.106.refs_5_
  29.9 0.0 copy-start
  29.9 0.0 copy-start.5
  29.9 0.1 collective-permute-start.5
  30.0 0.9 %shard_map.100 = (s32[256,1]{1,0:T(8,128)S(1)}, s32[256,1]{1,0:T(8,128)S(1)}, s32[24,1]{1,0:T(8,128)S(1)}, s32[384,1]{1,0:T(8,128)S(1)}, s32[384,1]{1,0:T(8,128)S(1)}) custom-call(s32[256,1]{1,0:T(8,128)S(1)} %copy.22.owners_ref), custom_call_target="tpu_custom_call" | custom-call | flops 5000000000 | bytes 1024 | tf_op jit(solution)/shard_map/pallas_call | solution.py:164
  30.9 6.9 %collective-permute-done.10.refs_10_ = bf16[256,768]{1,0:T(8,128)(2,1)S(1)} collective-permute-done((bf16[256,768]{1,0:T(8,128)(2,1)S(1)}, bf16[256,768]{1,0:T(8,128)(2,1)S(1)}, u32[]{:S(2)}, u32[]{:S(2)}) %collective-permute-start.10) | collective-permute-done | bytes 393248 | tf_op jit(solution)/shard_map/ppermute | solution.py:526
  37.8 0.0 copy-start.1
  37.8 2.4 %shard_map.108 = (bf16[128,768]{1,0:T(8,128)(2,1)S(1)}, bf16[128,768]{1,0:T(8,128)(2,1)S(1)}, f32[8,256,256]{2,1,0:T(8,128)S(1)}, f32[24,128]{1,0:T(8,128)S(1)}) custom-call(s32[256,1]{1,0:T(8,128)S(1)} %get-tuple-element.24.refs_0_, s32[256,1]{1,0:T(8,128)S(1)} %get-tuple-element.25.refs_1_, s32[24,1]{1,0:T(8,128)S(1)} %get-tuple-element.26.refs_2_, ...), custom_call_target="tpu_custom_call" | custom-call | flops 1236271104 | bytes 6165600 | tf_op jit(solution)/shard_map/pallas_call | solution.py:164
  40.2 0.1 collective-permute-start.11
  40.2 0.3 collective-permute-start.12
  40.6 1.7 %collective-permute-start.13 = (bf16[128,768]{1,0:T(8,128)(2,1)S(1)}, bf16[128,768]{1,0:T(8,128)(2,1)S(1)}, u32[]{:S(2)}, u32[]{:S(2)}) collective-permute-start(bf16[128,768]{1,0:T(8,128)(2,1)S(1)} %get-tuple-element.28.refs_0_), channel_id=1, source_target_pairs={{0,4},{1,5},{2,3},{3,2},{4,0},{5,1},{6,7},{7,6},{8,9},{9,8},{10,14... | collective-permute-start | bytes 589832 | tf_op jit(solution)/shard_map/ppermute | solution.py:526
  42.3 0.4 collective-permute-start.14
  42.8 5.3 %collective-permute-done.11.refs_2_ = bf16[128,768]{1,0:T(8,128)(2,1)S(1)} collective-permute-done((bf16[128,768]{1,0:T(8,128)(2,1)S(1)}, bf16[128,768]{1,0:T(8,128)(2,1)S(1)}, u32[]{:S(2)}, u32[]{:S(2)}) %collective-permute-start.11) | collective-permute-done | bytes 196640 | tf_op jit(solution)/shard_map/ppermute | solution.py:526
  48.1 0.1 collective-permute-done.12.refs_3_
  48.1 0.4 collective-permute-start.16
  48.6 2.1 %collective-permute-done.13.refs_4_ = bf16[128,768]{1,0:T(8,128)(2,1)S(1)} collective-permute-done((bf16[128,768]{1,0:T(8,128)(2,1)S(1)}, bf16[128,768]{1,0:T(8,128)(2,1)S(1)}, u32[]{:S(2)}, u32[]{:S(2)}) %collective-permute-start.13) | collective-permute-done | bytes 196640 | tf_op jit(solution)/shard_map/ppermute | solution.py:526
  50.7 0.6 shard_map.109.refs_3_
  51.2 0.1 collective-permute-start.17
  51.3 1.7 %collective-permute-done.17.refs_4_ = bf16[256,768]{1,0:T(8,128)(2,1)S(1)} collective-permute-done((bf16[256,768]{1,0:T(8,128)(2,1)S(1)}, bf16[256,768]{1,0:T(8,128)(2,1)S(1)}, u32[]{:S(2)}, u32[]{:S(2)}) %collective-permute-start.17) | collective-permute-done | bytes 393248 | tf_op jit(solution)/shard_map/ppermute | solution.py:514
  53.0 3.9 %shard_map.110 = (bf16[384,411]{1,0:T(8,128)(2,1)S(1)}, bf16[384,411]{1,0:T(8,128)(2,1)S(1)}) custom-call(bf16[2048,768]{1,0:T(8,128)(2,1)S(1)} %copy-done, bf16[1536,768]{1,0:T(8,128)(2,1)S(1)} %copy-done.1, f32[8,256,256]{2,1,0:T(8,128)S(1)} %get-tuple-element.27.refs_2_, bf16[256,768]{1,0:T(8,128)(2,1)S(1)} %shard_map.109.refs_3_, ...), custom_call_target="tpu_custom_call" | custom-call | flops 1840250880 | bytes 10095616 | tf_op jit(solution)/shard_map/pallas_call | solution.py:164
  57.0 0.2 collective-permute-start.18
  57.2 0.1 slice_bitcast_fusion.2
  57.3 1.5 %collective-permute-done.18.refs_1_ = bf16[384,411]{1,0:T(8,128)(2,1)S(1)} collective-permute-done((bf16[384,411]{1,0:T(8,128)(2,1)S(1)}, bf16[384,411]{1,0:T(8,128)(2,1)S(1)}, u32[]{:S(2)}, u32[]{:S(2)}) %collective-permute-start.18) | collective-permute-done | bytes 315680 | tf_op jit(solution)/shard_map/ppermute | solution.py:514
  58.8 0.1 shard_map.111
  58.9 2.9 %collective-permute-start.19 = (bf16[96,411]{1,0:T(8,128)(2,1)S(1)}, bf16[96,411]{1,0:T(8,128)(2,1)S(1)}, u32[]{:S(2)}, u32[]{:S(2)}) collective-permute-start(bf16[96,411]{1,0:T(8,128)(2,1)S(1)} %get-tuple-element.35), channel_id=1, source_target_pairs={{0,2},{1,3},{2,0},{3,1},{4,6},{5,7},{6,4},{7,5},{8,10},{9,11},{10,... | collective-permute-start | bytes 236744 | tf_op jit(solution)/shard_map/ppermute | solution.py:514
  61.8 2.0 %collective-permute-start.20 = (bf16[96,411]{1,0:T(8,128)(2,1)S(1)}, bf16[96,411]{1,0:T(8,128)(2,1)S(1)}, u32[]{:S(2)}, u32[]{:S(2)}) collective-permute-start(bf16[96,411]{1,0:T(8,128)(2,1)S(1)} %get-tuple-element.36), channel_id=1, source_target_pairs={{0,4},{1,5},{2,6},{3,7},{4,0},{5,1},{6,2},{7,3},{8,12},{9,13},{10,... | collective-permute-start | bytes 236744 | tf_op jit(solution)/shard_map/ppermute | solution.py:514
  63.8 0.2 collective-permute-start.21
  64.0 0.9 %collective-permute-done.19.refs_1_ = bf16[96,411]{1,0:T(8,128)(2,1)S(1)} collective-permute-done((bf16[96,411]{1,0:T(8,128)(2,1)S(1)}, bf16[96,411]{1,0:T(8,128)(2,1)S(1)}, u32[]{:S(2)}, u32[]{:S(2)}) %collective-permute-start.19) | collective-permute-done | bytes 78944 | tf_op jit(solution)/shard_map/ppermute | solution.py:514
  64.9 3.1 %collective-permute-done.20.refs_2_ = bf16[96,411]{1,0:T(8,128)(2,1)S(1)} collective-permute-done((bf16[96,411]{1,0:T(8,128)(2,1)S(1)}, bf16[96,411]{1,0:T(8,128)(2,1)S(1)}, u32[]{:S(2)}, u32[]{:S(2)}) %collective-permute-start.20) | collective-permute-done | bytes 78944 | tf_op jit(solution)/shard_map/ppermute | solution.py:514
  68.0 1.3 %collective-permute-done.21.refs_3_ = bf16[96,411]{1,0:T(8,128)(2,1)S(1)} collective-permute-done((bf16[96,411]{1,0:T(8,128)(2,1)S(1)}, bf16[96,411]{1,0:T(8,128)(2,1)S(1)}, u32[]{:S(2)}, u32[]{:S(2)}) %collective-permute-start.21) | collective-permute-done | bytes 78944 | tf_op jit(solution)/shard_map/ppermute | solution.py:514
  69.3 0.2 shard_map.112
  69.5 0.7 collective-permute-start.22
  70.3 3.2 %collective-permute-start.23 = (bf16[32,411]{1,0:T(8,128)(2,1)S(1)}, bf16[32,411]{1,0:T(8,128)(2,1)S(1)}, u32[]{:S(2)}, u32[]{:S(2)}) collective-permute-start(bf16[32,411]{1,0:T(8,128)(2,1)S(1)} %get-tuple-element.40), channel_id=1, source_target_pairs={{0,16},{8,24},{16,0},{24,8},{1,17},{9,25},{17,1},{25,9},{2,18},{10... | collective-permute-start | bytes 78920 | tf_op jit(solution)/shard_map/ppermute | solution.py:517
  73.5 1.3 %collective-permute-start.24 = (bf16[32,411]{1,0:T(8,128)(2,1)S(1)}, bf16[32,411]{1,0:T(8,128)(2,1)S(1)}, u32[]{:S(2)}, u32[]{:S(2)}) collective-permute-start(bf16[32,411]{1,0:T(8,128)(2,1)S(1)} %get-tuple-element.41), channel_id=1, source_target_pairs={{0,24},{8,0},{16,8},{24,16},{1,25},{9,1},{17,9},{25,17},{2,26},{10... | collective-permute-start | bytes 78920 | tf_op jit(solution)/shard_map/ppermute | solution.py:517
  74.8 0.1 maximum_sqrt_fusion
  74.9 0.1 copy.23
  75.0 0.4 collective-permute-done.22.refs_1_
  75.3 0.3 collective-permute-done.23.refs_2_
  75.7 1.7 %collective-permute-done.24.refs_3_ = bf16[32,411]{1,0:T(8,128)(2,1)S(1)} collective-permute-done((bf16[32,411]{1,0:T(8,128)(2,1)S(1)}, bf16[32,411]{1,0:T(8,128)(2,1)S(1)}, u32[]{:S(2)}, u32[]{:S(2)}) %collective-permute-start.24) | collective-permute-done | bytes 26336 | tf_op jit(solution)/shard_map/ppermute | solution.py:517
  77.4 1.4 %shard_map.113 = f32[4,32,411]{2,1,0:T(8,128)} custom-call(bf16[32,411]{1,0:T(8,128)(2,1)S(1)} %get-tuple-element.38.refs_0_, bf16[32,411]{1,0:T(8,128)(2,1)S(1)} %collective-permute-done.22.refs_1_, bf16[32,411]{1,0:T(8,128)(2,1)S(1)} %collective-permute-done.23.refs_2_, bf16[32,411]{1,0:T(8,128)(2,1)S(1)} %collective-permute-done.24.refs_3_, ...), custom_call_target="tpu_custom_call" | custom-call | flops 5260800 | bytes 106752 | tf_op jit(solution)/shard_map/pallas_call | solution.py:164
  (19 shorter events, 0.1 us)
Async XLA Ops:
  0.0 25.5 %copy-start.6 = (s32[256,1]{0,1:T(1,128)S(1)}, s32[256,1]{0,1:T(1,128)}, u32[]{:S(2)}) copy-start(s32[256,1]{0,1:T(1,128)} %param.12) | copy-start | bytes 3076
  0.0 15.7 %collective-permute-start.2 = (bf16[128,768]{1,0:T(8,128)(2,1)}, bf16[128,768]{1,0:T(8,128)(2,1)S(1)}, u32[]{:S(2)}, u32[]{:S(2)}) collective-permute-start(bf16[128,768]{1,0:T(8,128)(2,1)} %refs_0_.5), channel_id=1, source_target_pairs={{0,8},{8,0},{16,24},{24,16},{1,9},{9,1},{17,25},{25,17},{2,10},{10... | collective-permute-start | bytes 589832 | tf_op jit(solution)/shard_map/ppermute | solution.py:545
  3.0 19.5 %collective-permute-start.7 = (bf16[411,256]{1,0:T(8,128)(2,1)}, bf16[411,256]{1,0:T(8,128)(2,1)S(1)}, u32[]{:S(2)}, u32[]{:S(2)}) collective-permute-start(bf16[411,256]{1,0:T(8,128)(2,1)} %refs_0_.6), channel_id=1, source_target_pairs={{0,4},{1,5},{2,6},{3,7},{4,0},{5,1},{6,2},{7,3},{8,12},{9,13},{10,... | collective-permute-start | bytes 631304 | tf_op jit(solution)/shard_map/ppermute | solution.py:514
  4.5 18.0 %collective-permute-start.6 = (bf16[411,256]{1,0:T(8,128)(2,1)}, bf16[411,256]{1,0:T(8,128)(2,1)S(1)}, u32[]{:S(2)}, u32[]{:S(2)}) collective-permute-start(bf16[411,256]{1,0:T(8,128)(2,1)} %refs_0_.6), channel_id=1, source_target_pairs={{0,2},{1,3},{2,0},{3,1},{4,6},{5,7},{6,4},{7,5},{8,10},{9,11},{10,... | collective-permute-start | bytes 631304 | tf_op jit(solution)/shard_map/ppermute | solution.py:514
  6.0 16.5 %collective-permute-start.8 = (bf16[411,256]{1,0:T(8,128)(2,1)}, bf16[411,256]{1,0:T(8,128)(2,1)S(1)}, u32[]{:S(2)}, u32[]{:S(2)}) collective-permute-start(bf16[411,256]{1,0:T(8,128)(2,1)} %refs_0_.6), channel_id=1, source_target_pairs={{0,6},{1,7},{2,4},{3,5},{4,2},{5,3},{6,0},{7,1},{8,14},{9,15},{10,... | collective-permute-start | bytes 631304 | tf_op jit(solution)/shard_map/ppermute | solution.py:514
  8.3 4.0 %collective-permute-start = (bf16[16,512]{1,0:T(8,128)(2,1)}, bf16[16,512]{1,0:T(8,128)(2,1)S(1)}, u32[]{:S(2)}, u32[]{:S(2)}) collective-permute-start(bf16[16,512]{1,0:T(8,128)(2,1)} %shard_map.101.refs_0_), channel_id=1, source_target_pairs={{0,8},{8,0},{16,24},{24,16},{1,9},{9,1},{17,25},{25,17},{2,10},{10... | collective-permute-start | bytes 49160 | tf_op jit(solution)/shard_map/ppermute | solution.py:545
  12.3 0.7 copy-start.4
  13.1 4.9 %collective-permute-start.1 = (bf16[32,512]{1,0:T(8,128)(2,1)S(1)}, bf16[32,512]{1,0:T(8,128)(2,1)S(1)}, u32[]{:S(2)}, u32[]{:S(2)}) collective-permute-start(bf16[32,512]{1,0:T(8,128)(2,1)S(1)} %shard_map.102.refs_0_), channel_id=1, source_target_pairs={{0,16},{8,24},{16,0},{24,8},{1,17},{9,25},{17,1},{25,9},{2,18},{10... | collective-permute-start | bytes 98312 | tf_op jit(solution)/shard_map/ppermute | solution.py:545
  15.7 0.9 %copy-start.3 = (bf16[128,768]{1,0:T(8,128)(2,1)S(1)}, bf16[128,768]{1,0:T(8,128)(2,1)}, u32[]{:S(2)}) copy-start(bf16[128,768]{1,0:T(8,128)(2,1)} %refs_0_.5) | copy-start | bytes 589828
  18.0 4.3 %collective-permute-start.3 = (bf16[64,512]{1,0:T(8,128)(2,1)S(1)}, bf16[64,512]{1,0:T(8,128)(2,1)S(1)}, u32[]{:S(2)}, u32[]{:S(2)}) collective-permute-start(bf16[64,512]{1,0:T(8,128)(2,1)S(1)} %shard_map.104.refs_0_), channel_id=1, source_target_pairs={{0,2},{1,3},{2,0},{3,1},{4,6},{5,7},{6,4},{7,5},{8,10},{9,11},{10,... | collective-permute-start | bytes 196616 | tf_op jit(solution)/shard_map/ppermute | solution.py:514
  22.6 0.9 %copy-start.2 = (bf16[411,256]{1,0:T(8,128)(2,1)S(1)}, bf16[411,256]{1,0:T(8,128)(2,1)}, u32[]{:S(2)}) copy-start(bf16[411,256]{1,0:T(8,128)(2,1)} %refs_0_.6) | copy-start | bytes 631300
  23.6 14.2 %collective-permute-start.9 = (bf16[1664,256]{1,0:T(8,128)(2,1)S(1)}, bf16[1664,256]{1,0:T(8,128)(2,1)S(1)}, u32[]{:S(2)}, u32[]{:S(2)}) collective-permute-start(bf16[1664,256]{1,0:T(8,128)(2,1)S(1)} %shard_map.107.refs_7_.refs_5_), channel_id=1, source_target_pairs={{0,1},{1,0},{2,3},{3,2},{4,5},{5,4},{6,7},{7,6},{8,9},{9,8},{10,11... | collective-permute-start | bytes 2555912 | tf_op jit(solution)/shard_map/ppermute | solution.py:514
  23.7 5.9 %collective-permute-start.4 = (bf16[128,512]{1,0:T(8,128)(2,1)S(1)}, bf16[128,512]{1,0:T(8,128)(2,1)S(1)}, u32[]{:S(2)}, u32[]{:S(2)}) collective-permute-start(bf16[128,512]{1,0:T(8,128)(2,1)S(1)} %shard_map.105.refs_0_.refs_4_), channel_id=1, source_target_pairs={{0,4},{1,5},{2,6},{3,7},{4,0},{5,1},{6,2},{7,3},{8,12},{9,13},{10,... | collective-permute-start | bytes 393224 | tf_op jit(solution)/shard_map/ppermute | solution.py:514
  25.6 12.1 %collective-permute-start.10 = (bf16[256,768]{1,0:T(8,128)(2,1)S(1)}, bf16[256,768]{1,0:T(8,128)(2,1)S(1)}, u32[]{:S(2)}, u32[]{:S(2)}) collective-permute-start(bf16[256,768]{1,0:T(8,128)(2,1)S(1)} %shard_map.103.refs_2_.refs_9_), channel_id=1, source_target_pairs={{0,16},{1,17},{2,3},{3,2},{4,20},{5,21},{6,7},{7,6},{8,9},{9,8},{1... | collective-permute-start | bytes 1179656 | tf_op jit(solution)/shard_map/ppermute | solution.py:526
  29.9 7.9 %copy-start = (bf16[2048,768]{1,0:T(8,128)(2,1)S(1)}, bf16[2048,768]{1,0:T(8,128)(2,1)}, u32[]{:S(2)}) copy-start(bf16[2048,768]{1,0:T(8,128)(2,1)} %refs_0_.7) | copy-start | bytes 9437188
  29.9 7.9 %copy-start.5 = (f32[768]{0:T(1024)S(1)}, f32[768]{0:T(1024)}, u32[]{:S(2)}) copy-start(f32[768]{0:T(1024)} %refs_3_.3) | copy-start | bytes 9220
  29.9 7.8 %collective-permute-start.5 = (bf16[256,512]{1,0:T(8,128)(2,1)S(1)}, bf16[256,512]{1,0:T(8,128)(2,1)S(1)}, u32[]{:S(2)}, u32[]{:S(2)}) collective-permute-start(bf16[256,512]{1,0:T(8,128)(2,1)S(1)} %shard_map.106.refs_5_), channel_id=1, source_target_pairs={{0,1},{1,0},{2,3},{3,2},{4,5},{5,4},{6,7},{7,6},{8,9},{9,8},{10,11... | collective-permute-start | bytes 786440 | tf_op jit(solution)/shard_map/ppermute | solution.py:514
  37.8 15.2 %copy-start.1 = (bf16[1536,768]{1,0:T(8,128)(2,1)S(1)}, bf16[1536,768]{1,0:T(8,128)(2,1)}, u32[]{:S(2)}) copy-start(bf16[1536,768]{1,0:T(8,128)(2,1)} %refs_1_.3) | copy-start | bytes 7077892
  40.2 7.9 %collective-permute-start.11 = (bf16[128,768]{1,0:T(8,128)(2,1)S(1)}, bf16[128,768]{1,0:T(8,128)(2,1)S(1)}, u32[]{:S(2)}, u32[]{:S(2)}) collective-permute-start(bf16[128,768]{1,0:T(8,128)(2,1)S(1)} %get-tuple-element.28.refs_0_), channel_id=1, source_target_pairs={{0,2},{1,3},{2,0},{3,1},{4,5},{5,4},{6,7},{7,6},{8,10},{9,11},{10,... | collective-permute-start | bytes 589832 | tf_op jit(solution)/shard_map/ppermute | solution.py:526
  40.2 7.9 %collective-permute-start.12 = (bf16[128,768]{1,0:T(8,128)(2,1)S(1)}, bf16[128,768]{1,0:T(8,128)(2,1)S(1)}, u32[]{:S(2)}, u32[]{:S(2)}) collective-permute-start(bf16[128,768]{1,0:T(8,128)(2,1)S(1)} %get-tuple-element.29.refs_1_), channel_id=1, source_target_pairs={{0,4},{1,5},{2,3},{3,2},{4,0},{5,1},{6,7},{7,6},{8,9},{9,8},{10,14... | collective-permute-start | bytes 589832 | tf_op jit(solution)/shard_map/ppermute | solution.py:526
  40.6 10.1 %collective-permute-start.13 = (bf16[128,768]{1,0:T(8,128)(2,1)S(1)}, bf16[128,768]{1,0:T(8,128)(2,1)S(1)}, u32[]{:S(2)}, u32[]{:S(2)}) collective-permute-start(bf16[128,768]{1,0:T(8,128)(2,1)S(1)} %get-tuple-element.28.refs_0_), channel_id=1, source_target_pairs={{0,4},{1,5},{2,3},{3,2},{4,0},{5,1},{6,7},{7,6},{8,9},{9,8},{10,14... | collective-permute-start | bytes 589832 | tf_op jit(solution)/shard_map/ppermute | solution.py:526
  42.3 8.3 %collective-permute-start.14 = (bf16[128,768]{1,0:T(8,128)(2,1)S(1)}, bf16[128,768]{1,0:T(8,128)(2,1)S(1)}, u32[]{:S(2)}, u32[]{:S(2)}) collective-permute-start(bf16[128,768]{1,0:T(8,128)(2,1)S(1)} %get-tuple-element.29.refs_1_), channel_id=1, source_target_pairs={{0,2},{1,3},{2,0},{3,1},{4,5},{5,4},{6,7},{7,6},{8,10},{9,11},{10,... | collective-permute-start | bytes 589832 | tf_op jit(solution)/shard_map/ppermute | solution.py:526
  48.1 2.6 %collective-permute-start.15 = (bf16[128,768]{1,0:T(8,128)(2,1)S(1)}, bf16[128,768]{1,0:T(8,128)(2,1)S(1)}, u32[]{:S(2)}, u32[]{:S(2)}) collective-permute-start(bf16[128,768]{1,0:T(8,128)(2,1)S(1)} %collective-permute-done.11.refs_2_), channel_id=1, source_target_pairs={{0,1},{1,0},{2,6},{3,7},{4,5},{5,4},{6,2},{7,3},{8,12},{9,13},{10,... | collective-permute-start | bytes 589832 | tf_op jit(solution)/shard_map/ppermute | solution.py:526
  48.1 2.5 %collective-permute-start.16 = (bf16[128,768]{1,0:T(8,128)(2,1)S(1)}, bf16[128,768]{1,0:T(8,128)(2,1)S(1)}, u32[]{:S(2)}, u32[]{:S(2)}) collective-permute-start(bf16[128,768]{1,0:T(8,128)(2,1)S(1)} %collective-permute-done.12.refs_3_), channel_id=1, source_target_pairs={{0,1},{1,0},{2,3},{3,2},{4,6},{5,7},{6,4},{7,5},{8,9},{9,8},{10,11... | collective-permute-start | bytes 589832 | tf_op jit(solution)/shard_map/ppermute | solution.py:526
  51.2 1.8 %collective-permute-start.17 = (bf16[256,768]{1,0:T(8,128)(2,1)S(1)}, bf16[256,768]{1,0:T(8,128)(2,1)S(1)}, u32[]{:S(2)}, u32[]{:S(2)}) collective-permute-start(bf16[256,768]{1,0:T(8,128)(2,1)S(1)} %shard_map.109.refs_3_), channel_id=1, source_target_pairs={{0,1},{1,0},{2,3},{3,2},{4,5},{5,4},{6,7},{7,6},{8,9},{9,8},{10,11... | collective-permute-start | bytes 1179656 | tf_op jit(solution)/shard_map/ppermute | solution.py:514
  57.0 1.8 %collective-permute-start.18 = (bf16[384,411]{1,0:T(8,128)(2,1)S(1)}, bf16[384,411]{1,0:T(8,128)(2,1)S(1)}, u32[]{:S(2)}, u32[]{:S(2)}) collective-permute-start(bf16[384,411]{1,0:T(8,128)(2,1)S(1)} %get-tuple-element.33), channel_id=1, source_target_pairs={{0,1},{1,0},{2,3},{3,2},{4,5},{5,4},{6,7},{7,6},{8,9},{9,8},{10,11... | collective-permute-start | bytes 946952 | tf_op jit(solution)/shard_map/ppermute | solution.py:514
  58.9 6.0 %collective-permute-start.19 = (bf16[96,411]{1,0:T(8,128)(2,1)S(1)}, bf16[96,411]{1,0:T(8,128)(2,1)S(1)}, u32[]{:S(2)}, u32[]{:S(2)}) collective-permute-start(bf16[96,411]{1,0:T(8,128)(2,1)S(1)} %get-tuple-element.35), channel_id=1, source_target_pairs={{0,2},{1,3},{2,0},{3,1},{4,6},{5,7},{6,4},{7,5},{8,10},{9,11},{10,... | collective-permute-start | bytes 236744 | tf_op jit(solution)/shard_map/ppermute | solution.py:514
  61.8 6.2 %collective-permute-start.20 = (bf16[96,411]{1,0:T(8,128)(2,1)S(1)}, bf16[96,411]{1,0:T(8,128)(2,1)S(1)}, u32[]{:S(2)}, u32[]{:S(2)}) collective-permute-start(bf16[96,411]{1,0:T(8,128)(2,1)S(1)} %get-tuple-element.36), channel_id=1, source_target_pairs={{0,4},{1,5},{2,6},{3,7},{4,0},{5,1},{6,2},{7,3},{8,12},{9,13},{10,... | collective-permute-start | bytes 236744 | tf_op jit(solution)/shard_map/ppermute | solution.py:514
  63.8 5.5 %collective-permute-start.21 = (bf16[96,411]{1,0:T(8,128)(2,1)S(1)}, bf16[96,411]{1,0:T(8,128)(2,1)S(1)}, u32[]{:S(2)}, u32[]{:S(2)}) collective-permute-start(bf16[96,411]{1,0:T(8,128)(2,1)S(1)} %get-tuple-element.37), channel_id=1, source_target_pairs={{0,6},{1,7},{2,4},{3,5},{4,2},{5,3},{6,0},{7,1},{8,14},{9,15},{10,... | collective-permute-start | bytes 236744 | tf_op jit(solution)/shard_map/ppermute | solution.py:514
  69.5 5.8 %collective-permute-start.22 = (bf16[32,411]{1,0:T(8,128)(2,1)S(1)}, bf16[32,411]{1,0:T(8,128)(2,1)S(1)}, u32[]{:S(2)}, u32[]{:S(2)}) collective-permute-start(bf16[32,411]{1,0:T(8,128)(2,1)S(1)} %get-tuple-element.39), channel_id=1, source_target_pairs={{0,8},{8,16},{16,24},{24,0},{1,9},{9,17},{17,25},{25,1},{2,10},{10... | collective-permute-start | bytes 78920 | tf_op jit(solution)/shard_map/ppermute | solution.py:517
  70.3 5.4 %collective-permute-start.23 = (bf16[32,411]{1,0:T(8,128)(2,1)S(1)}, bf16[32,411]{1,0:T(8,128)(2,1)S(1)}, u32[]{:S(2)}, u32[]{:S(2)}) collective-permute-start(bf16[32,411]{1,0:T(8,128)(2,1)S(1)} %get-tuple-element.40), channel_id=1, source_target_pairs={{0,16},{8,24},{16,0},{24,8},{1,17},{9,25},{17,1},{25,9},{2,18},{10... | collective-permute-start | bytes 78920 | tf_op jit(solution)/shard_map/ppermute | solution.py:517
  73.5 3.9 %collective-permute-start.24 = (bf16[32,411]{1,0:T(8,128)(2,1)S(1)}, bf16[32,411]{1,0:T(8,128)(2,1)S(1)}, u32[]{:S(2)}, u32[]{:S(2)}) collective-permute-start(bf16[32,411]{1,0:T(8,128)(2,1)S(1)} %get-tuple-element.41), channel_id=1, source_target_pairs={{0,24},{8,0},{16,8},{24,16},{1,25},{9,1},{17,9},{25,17},{2,26},{10... | collective-permute-start | bytes 78920 | tf_op jit(solution)/shard_map/ppermute | solution.py:517

commit v4 on v3

--- a/solution.py
+++ b/solution.py
@@ -9,7 +9,7 @@
 
 VMEM_BYTES = 24 * 1024 * 1024
 WHOLE_VMEM_BYTES = 63 * 1024 * 1024
-SLACK_FLOPS = 5 * 10**9
+SLACK_FLOPS = 10**9
 NT_DIMS = (((1,), (1,)), ((), ()))
 
 
@@ -207,8 +207,9 @@
         return mask % self.group * self.chips + mask // self.group
 
     def layer(self, refs, k):
-        at = k % self.chips * self.deep
-        return refs[k // self.chips][at : at + self.features, :]
+        each = self.chans // len(refs)
+        at = k % each * self.deep
+        return refs[k // each][at : at + self.features, :]
 
     def mask(self, k):
         return k % self.chips * self.group + k // self.chips
@@ -308,12 +309,15 @@
         copy.wait()
 
 
-def stack_kernel(p, *refs):
-    for k, ref in enumerate(refs[: p.chips]):
-        refs[-1][k * p.deep : k * p.deep + p.features, :] = ref[...]
-        refs[-1][k * p.deep + p.features : (k + 1) * p.deep, :] = jnp.zeros(
-            (p.deep - p.features, p.hidden), jnp.bfloat16
-        )
+def stack_kernel(p, count, *refs):
+    out_ref, first = refs[-1], 0
+    for ref in refs[:count]:
+        rows = ref.shape[0]
+        out_ref[first : first + rows, :] = ref[...]
+        first += up_to(rows, 16)
+        fill = up_to(rows, 16) - rows
+        if fill:
+            out_ref[first - fill : first, :] = jnp.zeros((fill, p.hidden), jnp.bfloat16)
 
 
 def one_hot(wanted, first, count):
@@ -325,7 +329,7 @@
     refs = list(refs)
     take = lambda n: [refs.pop(0) for _ in range(n)]
     place_ref, source_ref, cell_ref, bias_ref, w_radiance_ref = take(5)
-    strip_refs, weight_refs, seen_refs = take(p.group), take(p.group), take(2)
+    strip_refs, weight_refs, seen_refs = take(p.group), take(2 * p.group), take(2)
     part_refs = take(p.steps)
     slope_ref, kappa_ref, active = refs
     c = lax.axis_index("chan")
@@ -397,7 +401,7 @@
     refs = list(refs)
     take = lambda n: [refs.pop(0) for _ in range(n)]
     w_radiance_ref, inv_cov_ref, slope_ref = take(3)
-    depart_refs, weight_refs, target_refs = take(p.group), take(p.group), take(p.group)
+    depart_refs, weight_refs, target_refs = take(p.group), take(2 * p.group), take(p.group)
     out_refs = refs
     c = lax.axis_index("chan")
     cotangent = None
@@ -538,9 +542,6 @@
             flops=0,
         )
 
-    def grow(value, over, after=()):
-        return join([value, over(value)], (2 * value.shape[0],) + value.shape[1:], after)
-
     def trade(value, mask):
         return lax.ppermute(value, "tile", [(a, a ^ mask) for a in range(p.tiles)])
 
@@ -561,35 +562,35 @@
         ],
         vmem=WHOLE_VMEM_BYTES,
     )
-    seen, stages = observed, []
-    bit = 1
-    while bit < p.tiles:
-        if 2 * bit < p.tiles:
-            seen = grow(seen, lambda value: trade(value, bit))
-        strips = grow(strips, lambda value: trade(value, bit), [seen] if 2 * bit == p.tiles else ())
-        stages.append(strips)
+    strips, w_hidden, observed = lax.optimization_barrier((strips, w_hidden, observed))
+
+    seen, bit = observed, 1
+    while 2 * bit < p.tiles:
+        seen = join([seen, trade(seen, bit)], (2 * seen.shape[0], p.shard))
         bit *= 2
-    bit = p.group
-    while bit < p.chans:
-        strips = grow(strips, lambda value: flip(value, bit))
-        stages.append(strips)
-        bit *= 2
-    strips = [strips] + [flip(strips, k) for k in range(1, p.group)]
-
-    near = [w_hidden] + [flip(w_hidden, chip * p.group) for chip in range(1, p.chips)]
-    near = call(
-        functools.partial(stack_kernel, p),
-        shape((p.chips * p.deep, p.hidden), half),
-        near + [stages[-2]],
-        in_hbm=[len(near)],
-    )
-    weights = [near] + [flip(near, k) for k in range(1, p.group)]
-
-    far_half = p.tiles // 2
     seen = [
         seen,
-        send(seen, {(b // p.group ^ far_half, b): (b // p.group, b) for b in range(p.chans)}),
+        send(seen, {(b // p.group ^ bit, b): (b // p.group, b) for b in range(p.chans)}),
     ]
+
+    strips = [strips] + [trade(strips, k) for k in range(1, p.tiles)]
+    strips = join(strips, (p.tiles * p.block, p.width), [seen[0]])
+
+    near, count, bit = w_hidden, 1, p.group
+    while 2 * bit < p.chans:
+        near = call(
+            functools.partial(stack_kernel, p, 2),
+            shape((2 * count * p.deep, p.hidden), half),
+            [near, flip(near, bit), strips],
+            in_hbm=[2],
+        )
+        count, bit = 2 * count, 2 * bit
+    near = [near, flip(near, bit)]
+    strips = [strips] + [flip(strips, k * p.group) for k in range(1, p.chips)]
+    strips = join(strips, (p.strips, p.width))
+    strips, seen, *near = lax.optimization_barrier((strips, seen, *near))
+    strips = [strips] + [flip(strips, k) for k in range(1, p.group)]
+    weights = near + [flip(value, k) for k in range(1, p.group) for value in near]
 
     reach = p.across + 4
     place, source, cell, *targets = call(

time: 79 us -> 79.8 us (1.010)
  waiting for transfers between devices: 34 us -> 27.8 us
  Pallas kernels: 12.4 us -> 16.4 us
  local copies, waits for them, and re-layouts: 2.88 us -> 5.24 us
    ppermute x7, waiting for transfers between devices: 14.3 us -> 9.22 us  [send(): lax.ppermute(value, both, sorted(((number(a), number(b)) for a, b in pair...]
    pallas_call x14 -> x12, Pallas kernels: 12.4 us -> 16.4 us  [call(): pl.pallas_call(kernel, out_shape=out_shape, in_specs=[far if k in in_hbm...]
    ppermute x3 -> x4, waiting for transfers between devices: 4.67 us -> 1.91 us  [trade(): return lax.ppermute(value, 'tile', [(a, a ^ mask) for a in range(p.tiles)])]
    unnamed x15 -> x21, local copies, waits for them, and re-layouts: 2.73 us -> 5.09 us
    ppermute x12 -> x13, waiting for transfers between devices: 12.6 us -> 14 us  [flip(): return lax.ppermute(value, 'chan', [(b, b ^ mask) for b in range(p.chans)])]
    ppermute x12 -> x13, starting transfers between devices: 12.6 us -> 13.9 us  [flip(): return lax.ppermute(value, 'chan', [(b, b ^ mask) for b in range(p.chans)])]
    ppermute x7, starting transfers between devices: 5.45 us -> 4.48 us  [send(): lax.ppermute(value, both, sorted(((number(a), number(b)) for a, b in pair...]
    ppermute x3 -> x4, starting transfers between devices: 5.82 us -> 5.96 us  [trade(): return lax.ppermute(value, 'tile', [(a, a ^ mask) for a in range(p.tiles)])]
  transfers between devices with their start and end apart: 25 -> 27, of which waited for: 16 -> 15; matrix products, arithmetic and copies ran while one was open for 0% -> 1% of each run, Pallas kernels for 5% -> 3%
where the time goes in v4:
time: 79.8 us; the launch traced here: 79.4 us
  starting transfers between devices  29.8 us (37%)
  waiting for transfers between devices  27.8 us (35%)
  Pallas kernels  16.4 us (21%)
  local copies, waits for them, and re-layouts  5.24 us (7%)
    pallas_call x12, Pallas kernels, call(): pl.pallas_call(kernel, out_shape=out_shape, in_specs=[far if k in in_hbm...  16.4 us
    ppermute x13, waiting for transfers between devices, flip(): return lax.ppermute(value, 'chan', [(b, b ^ mask) for b in range(p.chans)])  14 us
    ppermute x13, starting transfers between devices, flip(): return lax.ppermute(value, 'chan', [(b, b ^ mask) for b in range(p.chans)])  13.9 us
    ppermute x7, waiting for transfers between devices, send(): lax.ppermute(value, both, sorted(((number(a), number(b)) for a, b in pair...  9.22 us
    ppermute x4, starting transfers between devices, trade(): return lax.ppermute(value, 'tile', [(a, a ^ mask) for a in range(p.tiles)])  5.96 us
    ppermute x3, starting transfers between devices, shift(): lax.ppermute(value, 'tile', [(a, (a + by) % p.tiles) for a in range(p.til...  5.4 us
    unnamed x21, local copies, waits for them, and re-layouts  5.09 us
    ppermute x7, starting transfers between devices, send(): lax.ppermute(value, both, sorted(((number(a), number(b)) for a, b in pair...  4.48 us
  transfers between devices with their start and end apart: 27, of which 15 were waited for; matrix products, arithmetic and copies ran while one was open for 1% of the time, Pallas kernels for 3%

profile of v4, /device:TPU:0, one launch (start us, length us, event | category | flops | bytes accessed | tf_op | source)
XLA Modules:
  0.0 79.4 jit_solution(13552924474783292220)
XLA Ops:
  0.0 1.8 %shard_map.101.refs_0_ = bf16[16,512]{1,0:T(8,128)(2,1)} custom-call(f32[4,32,411]{2,1,0:T(8,128)} %refs_0_.2, f32[4,32]{1,0:T(4,128)} %refs_1_.2, s32[128]{0:T(128)} %refs_2_.1, f32[256]{0:T(256)} %refs_3_.2), custom_call_target="tpu_custom_call" | custom-call | bytes 212480 | tf_op jit(solution)/shard_map/pallas_call | solution.py:164
  1.8 3.0 %collective-permute-start.8 = (bf16[411,256]{1,0:T(8,128)(2,1)}, bf16[411,256]{1,0:T(8,128)(2,1)S(1)}, u32[]{:S(2)}, u32[]{:S(2)}) collective-permute-start(bf16[411,256]{1,0:T(8,128)(2,1)} %refs_0_.4), channel_id=1, source_target_pairs={{0,2},{1,3},{2,0},{3,1},{4,6},{5,7},{6,4},{7,5},{8,10},{9,11},{10,... | collective-permute-start | bytes 631304 | tf_op jit(solution)/shard_map/ppermute | solution.py:518
  4.8 1.6 %collective-permute-start.3 = (bf16[128,768]{1,0:T(8,128)(2,1)}, bf16[128,768]{1,0:T(8,128)(2,1)S(1)}, u32[]{:S(2)}, u32[]{:S(2)}) collective-permute-start(bf16[128,768]{1,0:T(8,128)(2,1)} %refs_0_.3), channel_id=1, source_target_pairs={{0,8},{8,0},{16,24},{24,16},{1,9},{9,1},{17,25},{25,17},{2,10},{10... | collective-permute-start | bytes 589832 | tf_op jit(solution)/shard_map/ppermute | solution.py:546
  6.4 2.5 %collective-permute-start.2 = (bf16[16,512]{1,0:T(8,128)(2,1)}, bf16[16,512]{1,0:T(8,128)(2,1)S(1)}, u32[]{:S(2)}, u32[]{:S(2)}) collective-permute-start(bf16[16,512]{1,0:T(8,128)(2,1)} %shard_map.101.refs_0_), channel_id=1, source_target_pairs={{0,24},{8,16},{16,8},{24,0},{1,25},{9,17},{17,9},{25,1},{2,26},{10... | collective-permute-start | bytes 49160 | tf_op jit(solution)/shard_map/ppermute | solution.py:546
  8.9 0.1 collective-permute-start.1
  9.0 1.8 %collective-permute-start = (bf16[16,512]{1,0:T(8,128)(2,1)}, bf16[16,512]{1,0:T(8,128)(2,1)S(1)}, u32[]{:S(2)}, u32[]{:S(2)}) collective-permute-start(bf16[16,512]{1,0:T(8,128)(2,1)} %shard_map.101.refs_0_), channel_id=1, source_target_pairs={{0,8},{8,0},{16,24},{24,16},{1,9},{9,1},{17,25},{25,17},{2,10},{10... | collective-permute-start | bytes 49160 | tf_op jit(solution)/shard_map/ppermute | solution.py:546
  10.8 0.8 collective-permute-done.3.refs_1_
  11.6 0.9 %copy-done.5 = bf16[128,768]{1,0:T(8,128)(2,1)S(1)} copy-done((bf16[128,768]{1,0:T(8,128)(2,1)S(1)}, bf16[128,768]{1,0:T(8,128)(2,1)}, u32[]{:S(2)}) %copy-start.5) | copy-done | bytes 196632
  12.5 0.5 shard_map.102.refs_4_.refs_11_
  13.0 1.1 %collective-permute-done.2.refs_3_ = bf16[16,512]{1,0:T(8,128)(2,1)S(1)} collective-permute-done((bf16[16,512]{1,0:T(8,128)(2,1)}, bf16[16,512]{1,0:T(8,128)(2,1)S(1)}, u32[]{:S(2)}, u32[]{:S(2)}) %collective-permute-start.2) | collective-permute-done | bytes 16416 | tf_op jit(solution)/shard_map/ppermute | solution.py:546
  14.1 0.7 copy-done.7
  14.8 0.1 shard_map.103.refs_0_.refs_2_
  14.9 0.0 collective-permute-done.8.refs_1_
  14.9 0.0 copy-start.4
  15.0 0.9 %copy-done.4 = bf16[411,256]{1,0:T(8,128)(2,1)S(1)} copy-done((bf16[411,256]{1,0:T(8,128)(2,1)S(1)}, bf16[411,256]{1,0:T(8,128)(2,1)}, u32[]{:S(2)}) %copy-start.4) | copy-done | bytes 210456
  15.9 0.8 %shard_map.105.refs_7_.refs_5_ = bf16[832,256]{1,0:T(8,128)(2,1)} custom-call(bf16[411,256]{1,0:T(8,128)(2,1)S(1)} %copy-done.4, bf16[411,256]{1,0:T(8,128)(2,1)S(1)} %collective-permute-done.8.refs_1_, bf16[64,512]{1,0:T(8,128)(2,1)S(1)} %shard_map.103.refs_0_.refs_2_), custom_call_target="tpu_custom_call" | custom-call | bytes 486400 | tf_op jit(solution)/shard_map/pallas_call | solution.py:164
  16.7 1.5 %collective-permute-start.9 = (bf16[832,256]{1,0:T(8,128)(2,1)}, bf16[832,256]{1,0:T(8,128)(2,1)}, u32[]{:S(2)}, u32[]{:S(2)}) collective-permute-start(bf16[832,256]{1,0:T(8,128)(2,1)} %shard_map.105.refs_7_.refs_5_), channel_id=1, source_target_pairs={{0,4},{1,5},{2,6},{3,7},{4,0},{5,1},{6,2},{7,3},{8,12},{9,13},{10,... | collective-permute-start | bytes 1277960 | tf_op jit(solution)/shard_map/ppermute | solution.py:518
  18.2 1.8 %collective-permute-start.7 = (bf16[256,768]{1,0:T(8,128)(2,1)S(1)}, bf16[256,768]{1,0:T(8,128)(2,1)S(1)}, u32[]{:S(2)}, u32[]{:S(2)}) collective-permute-start(bf16[256,768]{1,0:T(8,128)(2,1)S(1)} %shard_map.102.refs_4_.refs_11_), channel_id=1, source_target_pairs={{0,16},{1,17},{2,3},{3,2},{4,20},{5,21},{6,7},{7,6},{8,9},{9,8},{1... | collective-permute-start | bytes 1179656 | tf_op jit(solution)/shard_map/ppermute | solution.py:530
  20.0 0.0 collective-permute-start.6
  20.1 0.5 collective-permute-start.5
  20.6 3.0 %collective-permute-start.4 = (bf16[64,512]{1,0:T(8,128)(2,1)S(1)}, bf16[64,512]{1,0:T(8,128)(2,1)S(1)}, u32[]{:S(2)}, u32[]{:S(2)}) collective-permute-start(bf16[64,512]{1,0:T(8,128)(2,1)S(1)} %shard_map.103.refs_0_.refs_2_), channel_id=1, source_target_pairs={{0,2},{1,3},{2,0},{3,1},{4,6},{5,7},{6,4},{7,5},{8,10},{9,11},{10,... | collective-permute-start | bytes 196616 | tf_op jit(solution)/shard_map/ppermute | solution.py:518
  23.5 1.8 %collective-permute-done.6.refs_3_ = bf16[64,512]{1,0:T(8,128)(2,1)S(1)} collective-permute-done((bf16[64,512]{1,0:T(8,128)(2,1)S(1)}, bf16[64,512]{1,0:T(8,128)(2,1)S(1)}, u32[]{:S(2)}, u32[]{:S(2)}) %collective-permute-start.6) | collective-permute-done | bytes 65568 | tf_op jit(solution)/shard_map/ppermute | solution.py:518
  25.3 4.1 %collective-permute-done.5.refs_2_ = bf16[64,512]{1,0:T(8,128)(2,1)S(1)} collective-permute-done((bf16[64,512]{1,0:T(8,128)(2,1)S(1)}, bf16[64,512]{1,0:T(8,128)(2,1)S(1)}, u32[]{:S(2)}, u32[]{:S(2)}) %collective-permute-start.5) | collective-permute-done | bytes 65568 | tf_op jit(solution)/shard_map/ppermute | solution.py:518
  29.4 0.0 collective-permute-done.4.refs_1_
  29.4 0.7 shard_map.104.refs_5_
  30.2 0.7 copy-done.2
  30.9 0.0 collective-permute-done.9.refs_8_.refs_6_
  30.9 0.5 collective-permute-start.12
  31.4 0.0 collective-permute-start.10
  31.4 0.8 %copy.22.owners_ref = s32[256,1]{1,0:T(8,128)} copy(s32[256,1]{0,1:T(1,128)S(1)} %copy-done.9) | data formatting | bytes 2048 | tf_op args[2]
  32.3 0.9 %copy-done.6 = s32[256,1]{1,0:T(8,128)S(1)} copy-done((s32[256,1]{1,0:T(8,128)S(1)}, s32[256,1]{1,0:T(8,128)}, u32[]{:S(2)}) %copy-start.6) | copy-done | bytes 1048
  33.2 0.9 %shard_map.100 = (s32[256,1]{1,0:T(8,128)S(1)}, s32[256,1]{1,0:T(8,128)S(1)}, s32[24,1]{1,0:T(8,128)S(1)}, s32[384,1]{1,0:T(8,128)S(1)}, s32[384,1]{1,0:T(8,128)S(1)}) custom-call(s32[256,1]{1,0:T(8,128)S(1)} %copy-done.6), custom_call_target="tpu_custom_call" | custom-call | flops 1000000000 | bytes 1024 | tf_op jit(solution)/shard_map/pallas_call | solution.py:164
  34.1 0.1 copy-done.3
  34.2 4.1 %shard_map.106 = (bf16[128,768]{1,0:T(8,128)(2,1)S(1)}, bf16[128,768]{1,0:T(8,128)(2,1)S(1)}, f32[8,256,256]{2,1,0:T(8,128)S(1)}, f32[24,128]{1,0:T(8,128)S(1)}) custom-call(s32[256,1]{1,0:T(8,128)S(1)} %get-tuple-element.32.refs_0_, s32[256,1]{1,0:T(8,128)S(1)} %get-tuple-element.33.refs_1_, s32[24,1]{1,0:T(8,128)S(1)} %get-tuple-element.34.refs_2_, ...), custom_call_target="tpu_custom_call" | custom-call | flops 1236271104 | bytes 6165600 | tf_op jit(solution)/shard_map/pallas_call | solution.py:164
  38.2 0.6 collective-permute-start.13
  38.8 1.5 %collective-permute-start.14 = (bf16[128,768]{1,0:T(8,128)(2,1)S(1)}, bf16[128,768]{1,0:T(8,128)(2,1)S(1)}, u32[]{:S(2)}, u32[]{:S(2)}) collective-permute-start(bf16[128,768]{1,0:T(8,128)(2,1)S(1)} %get-tuple-element.45.refs_1_), channel_id=1, source_target_pairs={{0,4},{1,5},{2,3},{3,2},{4,0},{5,1},{6,7},{7,6},{8,9},{9,8},{10,14... | collective-permute-start | bytes 589832 | tf_op jit(solution)/shard_map/ppermute | solution.py:530
  40.3 0.5 collective-permute-start.15
  40.9 5.1 %collective-permute-done.13.refs_2_ = bf16[128,768]{1,0:T(8,128)(2,1)S(1)} collective-permute-done((bf16[128,768]{1,0:T(8,128)(2,1)S(1)}, bf16[128,768]{1,0:T(8,128)(2,1)S(1)}, u32[]{:S(2)}, u32[]{:S(2)}) %collective-permute-start.13) | collective-permute-done | bytes 196640 | tf_op jit(solution)/shard_map/ppermute | solution.py:530
  46.0 0.6 collective-permute-done.14.refs_3_
  46.6 3.5 %collective-permute-done.15.refs_4_ = bf16[128,768]{1,0:T(8,128)(2,1)S(1)} collective-permute-done((bf16[128,768]{1,0:T(8,128)(2,1)S(1)}, bf16[128,768]{1,0:T(8,128)(2,1)S(1)}, u32[]{:S(2)}, u32[]{:S(2)}) %collective-permute-start.15) | collective-permute-done | bytes 196640 | tf_op jit(solution)/shard_map/ppermute | solution.py:530
  50.1 0.6 shard_map.107.refs_3_
  50.7 0.1 collective-permute-start.19
  50.7 1.7 %collective-permute-done.19.refs_4_ = bf16[256,768]{1,0:T(8,128)(2,1)S(1)} collective-permute-done((bf16[256,768]{1,0:T(8,128)(2,1)S(1)}, bf16[256,768]{1,0:T(8,128)(2,1)S(1)}, u32[]{:S(2)}, u32[]{:S(2)}) %collective-permute-start.19) | collective-permute-done | bytes 393248 | tf_op jit(solution)/shard_map/ppermute | solution.py:518
  52.4 5.3 %shard_map.108 = (bf16[384,411]{1,0:T(8,128)(2,1)S(1)}, bf16[384,411]{1,0:T(8,128)(2,1)S(1)}) custom-call(bf16[2048,768]{1,0:T(8,128)(2,1)S(1)} %copy-done, bf16[1536,768]{1,0:T(8,128)(2,1)S(1)} %copy-done.1, f32[8,256,256]{2,1,0:T(8,128)S(1)} %get-tuple-element.43.refs_2_, bf16[256,768]{1,0:T(8,128)(2,1)S(1)} %shard_map.107.refs_3_, ...), custom_call_target="tpu_custom_call" | custom-call | flops 1840250880 | bytes 10095616 | tf_op jit(solution)/shard_map/pallas_call | solution.py:164
  57.8 0.2 collective-permute-start.20
  58.0 0.1 slice_bitcast_fusion.2
  58.1 1.5 %collective-permute-done.20.refs_1_ = bf16[384,411]{1,0:T(8,128)(2,1)S(1)} collective-permute-done((bf16[384,411]{1,0:T(8,128)(2,1)S(1)}, bf16[384,411]{1,0:T(8,128)(2,1)S(1)}, u32[]{:S(2)}, u32[]{:S(2)}) %collective-permute-start.20) | collective-permute-done | bytes 315680 | tf_op jit(solution)/shard_map/ppermute | solution.py:518
  59.6 0.1 shard_map.109
  59.7 2.6 %collective-permute-start.21 = (bf16[96,411]{1,0:T(8,128)(2,1)S(1)}, bf16[96,411]{1,0:T(8,128)(2,1)S(1)}, u32[]{:S(2)}, u32[]{:S(2)}) collective-permute-start(bf16[96,411]{1,0:T(8,128)(2,1)S(1)} %get-tuple-element.51), channel_id=1, source_target_pairs={{0,2},{1,3},{2,0},{3,1},{4,6},{5,7},{6,4},{7,5},{8,10},{9,11},{10,... | collective-permute-start | bytes 236744 | tf_op jit(solution)/shard_map/ppermute | solution.py:518
  62.3 1.7 %collective-permute-start.22 = (bf16[96,411]{1,0:T(8,128)(2,1)S(1)}, bf16[96,411]{1,0:T(8,128)(2,1)S(1)}, u32[]{:S(2)}, u32[]{:S(2)}) collective-permute-start(bf16[96,411]{1,0:T(8,128)(2,1)S(1)} %get-tuple-element.52), channel_id=1, source_target_pairs={{0,4},{1,5},{2,6},{3,7},{4,0},{5,1},{6,2},{7,3},{8,12},{9,13},{10,... | collective-permute-start | bytes 236744 | tf_op jit(solution)/shard_map/ppermute | solution.py:518
  64.0 0.8 collective-permute-start.23
  64.8 0.6 collective-permute-done.21.refs_1_
  65.4 2.8 %collective-permute-done.22.refs_2_ = bf16[96,411]{1,0:T(8,128)(2,1)S(1)} collective-permute-done((bf16[96,411]{1,0:T(8,128)(2,1)S(1)}, bf16[96,411]{1,0:T(8,128)(2,1)S(1)}, u32[]{:S(2)}, u32[]{:S(2)}) %collective-permute-start.22) | collective-permute-done | bytes 78944 | tf_op jit(solution)/shard_map/ppermute | solution.py:518
  68.2 1.5 %collective-permute-done.23.refs_3_ = bf16[96,411]{1,0:T(8,128)(2,1)S(1)} collective-permute-done((bf16[96,411]{1,0:T(8,128)(2,1)S(1)}, bf16[96,411]{1,0:T(8,128)(2,1)S(1)}, u32[]{:S(2)}, u32[]{:S(2)}) %collective-permute-start.23) | collective-permute-done | bytes 78944 | tf_op jit(solution)/shard_map/ppermute | solution.py:518
  69.7 0.2 shard_map.110
  69.9 1.1 %collective-permute-start.24 = (bf16[32,411]{1,0:T(8,128)(2,1)S(1)}, bf16[32,411]{1,0:T(8,128)(2,1)S(1)}, u32[]{:S(2)}, u32[]{:S(2)}) collective-permute-start(bf16[32,411]{1,0:T(8,128)(2,1)S(1)} %get-tuple-element.55), channel_id=1, source_target_pairs={{0,8},{8,16},{16,24},{24,0},{1,9},{9,17},{17,25},{25,1},{2,10},{10... | collective-permute-start | bytes 78920 | tf_op jit(solution)/shard_map/ppermute | solution.py:521
  71.1 3.1 %collective-permute-start.25 = (bf16[32,411]{1,0:T(8,128)(2,1)S(1)}, bf16[32,411]{1,0:T(8,128)(2,1)S(1)}, u32[]{:S(2)}, u32[]{:S(2)}) collective-permute-start(bf16[32,411]{1,0:T(8,128)(2,1)S(1)} %get-tuple-element.56), channel_id=1, source_target_pairs={{0,16},{8,24},{16,0},{24,8},{1,17},{9,25},{17,1},{25,9},{2,18},{10... | collective-permute-start | bytes 78920 | tf_op jit(solution)/shard_map/ppermute | solution.py:521
  74.2 1.2 %collective-permute-start.26 = (bf16[32,411]{1,0:T(8,128)(2,1)S(1)}, bf16[32,411]{1,0:T(8,128)(2,1)S(1)}, u32[]{:S(2)}, u32[]{:S(2)}) collective-permute-start(bf16[32,411]{1,0:T(8,128)(2,1)S(1)} %get-tuple-element.57), channel_id=1, source_target_pairs={{0,24},{8,0},{16,8},{24,16},{1,25},{9,1},{17,9},{25,17},{2,26},{10... | collective-permute-start | bytes 78920 | tf_op jit(solution)/shard_map/ppermute | solution.py:521
  75.3 0.1 maximum_sqrt_fusion
  75.4 0.1 copy.23
  75.5 0.3 collective-permute-done.24.refs_1_
  75.8 0.4 collective-permute-done.25.refs_2_
  76.2 1.9 %collective-permute-done.26.refs_3_ = bf16[32,411]{1,0:T(8,128)(2,1)S(1)} collective-permute-done((bf16[32,411]{1,0:T(8,128)(2,1)S(1)}, bf16[32,411]{1,0:T(8,128)(2,1)S(1)}, u32[]{:S(2)}, u32[]{:S(2)}) %collective-permute-start.26) | collective-permute-done | bytes 26336 | tf_op jit(solution)/shard_map/ppermute | solution.py:521
  78.1 1.4 %shard_map.111 = f32[4,32,411]{2,1,0:T(8,128)} custom-call(bf16[32,411]{1,0:T(8,128)(2,1)S(1)} %get-tuple-element.54.refs_0_, bf16[32,411]{1,0:T(8,128)(2,1)S(1)} %collective-permute-done.24.refs_1_, bf16[32,411]{1,0:T(8,128)(2,1)S(1)} %collective-permute-done.25.refs_2_, bf16[32,411]{1,0:T(8,128)(2,1)S(1)} %collective-permute-done.26.refs_3_, ...), custom_call_target="tpu_custom_call" | custom-call | flops 5260800 | bytes 106752 | tf_op jit(solution)/shard_map/pallas_call | solution.py:164
  (27 shorter events, 0.1 us)
Async XLA Ops:
  0.0 31.4 %copy-start.9 = (s32[256,1]{0,1:T(1,128)S(1)}, s32[256,1]{0,1:T(1,128)}, u32[]{:S(2)}) copy-start(s32[256,1]{0,1:T(1,128)} %param.12) | copy-start | bytes 3076
  1.8 13.1 %collective-permute-start.8 = (bf16[411,256]{1,0:T(8,128)(2,1)}, bf16[411,256]{1,0:T(8,128)(2,1)S(1)}, u32[]{:S(2)}, u32[]{:S(2)}) collective-permute-start(bf16[411,256]{1,0:T(8,128)(2,1)} %refs_0_.4), channel_id=1, source_target_pairs={{0,2},{1,3},{2,0},{3,1},{4,6},{5,7},{6,4},{7,5},{8,10},{9,11},{10,... | collective-permute-start | bytes 631304 | tf_op jit(solution)/shard_map/ppermute | solution.py:518
  4.8 6.7 %collective-permute-start.3 = (bf16[128,768]{1,0:T(8,128)(2,1)}, bf16[128,768]{1,0:T(8,128)(2,1)S(1)}, u32[]{:S(2)}, u32[]{:S(2)}) collective-permute-start(bf16[128,768]{1,0:T(8,128)(2,1)} %refs_0_.3), channel_id=1, source_target_pairs={{0,8},{8,0},{16,24},{24,16},{1,9},{9,1},{17,25},{25,17},{2,10},{10... | collective-permute-start | bytes 589832 | tf_op jit(solution)/shard_map/ppermute | solution.py:546
  6.4 7.7 %collective-permute-start.2 = (bf16[16,512]{1,0:T(8,128)(2,1)}, bf16[16,512]{1,0:T(8,128)(2,1)S(1)}, u32[]{:S(2)}, u32[]{:S(2)}) collective-permute-start(bf16[16,512]{1,0:T(8,128)(2,1)} %shard_map.101.refs_0_), channel_id=1, source_target_pairs={{0,24},{8,16},{16,8},{24,0},{1,25},{9,17},{17,9},{25,1},{2,26},{10... | collective-permute-start | bytes 49160 | tf_op jit(solution)/shard_map/ppermute | solution.py:546
  8.9 5.3 %collective-permute-start.1 = (bf16[16,512]{1,0:T(8,128)(2,1)}, bf16[16,512]{1,0:T(8,128)(2,1)S(1)}, u32[]{:S(2)}, u32[]{:S(2)}) collective-permute-start(bf16[16,512]{1,0:T(8,128)(2,1)} %shard_map.101.refs_0_), channel_id=1, source_target_pairs={{0,16},{8,24},{16,0},{24,8},{1,17},{9,25},{17,1},{25,9},{2,18},{10... | collective-permute-start | bytes 49160 | tf_op jit(solution)/shard_map/ppermute | solution.py:546
  9.0 5.1 %collective-permute-start = (bf16[16,512]{1,0:T(8,128)(2,1)}, bf16[16,512]{1,0:T(8,128)(2,1)S(1)}, u32[]{:S(2)}, u32[]{:S(2)}) collective-permute-start(bf16[16,512]{1,0:T(8,128)(2,1)} %shard_map.101.refs_0_), channel_id=1, source_target_pairs={{0,8},{8,0},{16,24},{24,16},{1,9},{9,1},{17,25},{25,17},{2,10},{10... | collective-permute-start | bytes 49160 | tf_op jit(solution)/shard_map/ppermute | solution.py:546
  11.6 0.9 %copy-start.5 = (bf16[128,768]{1,0:T(8,128)(2,1)S(1)}, bf16[128,768]{1,0:T(8,128)(2,1)}, u32[]{:S(2)}) copy-start(bf16[128,768]{1,0:T(8,128)(2,1)} %refs_0_.3) | copy-start | bytes 589828
  14.1 0.7 copy-start.7
  14.9 0.9 %copy-start.4 = (bf16[411,256]{1,0:T(8,128)(2,1)S(1)}, bf16[411,256]{1,0:T(8,128)(2,1)}, u32[]{:S(2)}) copy-start(bf16[411,256]{1,0:T(8,128)(2,1)} %refs_0_.4) | copy-start | bytes 631300
  15.9 18.2 %copy-start.8 = (f32[768]{0:T(1024)S(1)}, f32[768]{0:T(1024)}, u32[]{:S(2)}) copy-start(f32[768]{0:T(1024)} %refs_3_.3) | copy-start | bytes 9220
  16.7 17.4 %copy-start = (bf16[2048,768]{1,0:T(8,128)(2,1)S(1)}, bf16[2048,768]{1,0:T(8,128)(2,1)}, u32[]{:S(2)}) copy-start(bf16[2048,768]{1,0:T(8,128)(2,1)} %refs_0_.5) | copy-start | bytes 9437188
  16.7 14.2 %collective-permute-start.9 = (bf16[832,256]{1,0:T(8,128)(2,1)}, bf16[832,256]{1,0:T(8,128)(2,1)}, u32[]{:S(2)}, u32[]{:S(2)}) collective-permute-start(bf16[832,256]{1,0:T(8,128)(2,1)} %shard_map.105.refs_7_.refs_5_), channel_id=1, source_target_pairs={{0,4},{1,5},{2,6},{3,7},{4,0},{5,1},{6,2},{7,3},{8,12},{9,13},{10,... | collective-permute-start | bytes 1277960 | tf_op jit(solution)/shard_map/ppermute | solution.py:518
  18.2 12.0 %collective-permute-start.7 = (bf16[256,768]{1,0:T(8,128)(2,1)S(1)}, bf16[256,768]{1,0:T(8,128)(2,1)S(1)}, u32[]{:S(2)}, u32[]{:S(2)}) collective-permute-start(bf16[256,768]{1,0:T(8,128)(2,1)S(1)} %shard_map.102.refs_4_.refs_11_), channel_id=1, source_target_pairs={{0,16},{1,17},{2,3},{3,2},{4,20},{5,21},{6,7},{7,6},{8,9},{9,8},{1... | collective-permute-start | bytes 1179656 | tf_op jit(solution)/shard_map/ppermute | solution.py:530
  20.0 5.3 %collective-permute-start.6 = (bf16[64,512]{1,0:T(8,128)(2,1)S(1)}, bf16[64,512]{1,0:T(8,128)(2,1)S(1)}, u32[]{:S(2)}, u32[]{:S(2)}) collective-permute-start(bf16[64,512]{1,0:T(8,128)(2,1)S(1)} %shard_map.103.refs_0_.refs_2_), channel_id=1, source_target_pairs={{0,6},{1,7},{2,4},{3,5},{4,2},{5,3},{6,0},{7,1},{8,14},{9,15},{10,... | collective-permute-start | bytes 196616 | tf_op jit(solution)/shard_map/ppermute | solution.py:518
  20.1 9.4 %collective-permute-start.5 = (bf16[64,512]{1,0:T(8,128)(2,1)S(1)}, bf16[64,512]{1,0:T(8,128)(2,1)S(1)}, u32[]{:S(2)}, u32[]{:S(2)}) collective-permute-start(bf16[64,512]{1,0:T(8,128)(2,1)S(1)} %shard_map.103.refs_0_.refs_2_), channel_id=1, source_target_pairs={{0,4},{1,5},{2,6},{3,7},{4,0},{5,1},{6,2},{7,3},{8,12},{9,13},{10,... | collective-permute-start | bytes 196616 | tf_op jit(solution)/shard_map/ppermute | solution.py:518
  20.6 8.9 %collective-permute-start.4 = (bf16[64,512]{1,0:T(8,128)(2,1)S(1)}, bf16[64,512]{1,0:T(8,128)(2,1)S(1)}, u32[]{:S(2)}, u32[]{:S(2)}) collective-permute-start(bf16[64,512]{1,0:T(8,128)(2,1)S(1)} %shard_map.103.refs_0_.refs_2_), channel_id=1, source_target_pairs={{0,2},{1,3},{2,0},{3,1},{4,6},{5,7},{6,4},{7,5},{8,10},{9,11},{10,... | collective-permute-start | bytes 196616 | tf_op jit(solution)/shard_map/ppermute | solution.py:518
  30.2 0.7 copy-start.2
  30.9 3.1 %collective-permute-start.11 = (bf16[832,256]{1,0:T(8,128)(2,1)}, bf16[832,256]{1,0:T(8,128)(2,1)}, u32[]{:S(2)}, u32[]{:S(2)}) collective-permute-start(bf16[832,256]{1,0:T(8,128)(2,1)} %shard_map.105.refs_7_.refs_5_), channel_id=1, source_target_pairs={{0,1},{1,0},{2,3},{3,2},{4,5},{5,4},{6,7},{7,6},{8,9},{9,8},{10,11... | collective-permute-start | bytes 1277960 | tf_op jit(solution)/shard_map/ppermute | solution.py:518
  30.9 3.1 %collective-permute-start.12 = (bf16[832,256]{1,0:T(8,128)(2,1)}, bf16[832,256]{1,0:T(8,128)(2,1)}, u32[]{:S(2)}, u32[]{:S(2)}) collective-permute-start(bf16[832,256]{1,0:T(8,128)(2,1)} %collective-permute-done.9.refs_8_.refs_6_), channel_id=1, source_target_pairs={{0,1},{1,0},{2,3},{3,2},{4,5},{5,4},{6,7},{7,6},{8,9},{9,8},{10,11... | collective-permute-start | bytes 1277960 | tf_op jit(solution)/shard_map/ppermute | solution.py:518
  31.4 2.6 %collective-permute-start.10 = (bf16[256,512]{1,0:T(8,128)(2,1)}, bf16[256,512]{1,0:T(8,128)(2,1)}, u32[]{:S(2)}, u32[]{:S(2)}) collective-permute-start(bf16[256,512]{1,0:T(8,128)(2,1)} %shard_map.104.refs_5_), channel_id=1, source_target_pairs={{0,1},{1,0},{2,3},{3,2},{4,5},{5,4},{6,7},{7,6},{8,9},{9,8},{10,11... | collective-permute-start | bytes 786440 | tf_op jit(solution)/shard_map/ppermute | solution.py:518
  32.3 0.9 %copy-start.6 = (s32[256,1]{1,0:T(8,128)S(1)}, s32[256,1]{1,0:T(8,128)}, u32[]{:S(2)}) copy-start(s32[256,1]{1,0:T(8,128)} %copy.22.owners_ref) | copy-start | bytes 3076
  33.2 1.0 %copy-start.3 = (bf16[256,768]{1,0:T(8,128)(2,1)S(1)}, bf16[256,768]{1,0:T(8,128)(2,1)}, u32[]{:S(2)}) copy-start(bf16[256,768]{1,0:T(8,128)(2,1)} %copy-done.2) | copy-start | bytes 1179652
  34.2 18.3 %copy-start.1 = (bf16[1536,768]{1,0:T(8,128)(2,1)S(1)}, bf16[1536,768]{1,0:T(8,128)(2,1)}, u32[]{:S(2)}) copy-start(bf16[1536,768]{1,0:T(8,128)(2,1)} %refs_1_.3) | copy-start | bytes 7077892
  38.2 7.8 %collective-permute-start.13 = (bf16[128,768]{1,0:T(8,128)(2,1)S(1)}, bf16[128,768]{1,0:T(8,128)(2,1)S(1)}, u32[]{:S(2)}, u32[]{:S(2)}) collective-permute-start(bf16[128,768]{1,0:T(8,128)(2,1)S(1)} %get-tuple-element.44.refs_0_), channel_id=1, source_target_pairs={{0,2},{1,3},{2,0},{3,1},{4,5},{5,4},{6,7},{7,6},{8,10},{9,11},{10,... | collective-permute-start | bytes 589832 | tf_op jit(solution)/shard_map/ppermute | solution.py:530
  38.8 7.7 %collective-permute-start.14 = (bf16[128,768]{1,0:T(8,128)(2,1)S(1)}, bf16[128,768]{1,0:T(8,128)(2,1)S(1)}, u32[]{:S(2)}, u32[]{:S(2)}) collective-permute-start(bf16[128,768]{1,0:T(8,128)(2,1)S(1)} %get-tuple-element.45.refs_1_), channel_id=1, source_target_pairs={{0,4},{1,5},{2,3},{3,2},{4,0},{5,1},{6,7},{7,6},{8,9},{9,8},{10,14... | collective-permute-start | bytes 589832 | tf_op jit(solution)/shard_map/ppermute | solution.py:530
  40.3 9.8 %collective-permute-start.15 = (bf16[128,768]{1,0:T(8,128)(2,1)S(1)}, bf16[128,768]{1,0:T(8,128)(2,1)S(1)}, u32[]{:S(2)}, u32[]{:S(2)}) collective-permute-start(bf16[128,768]{1,0:T(8,128)(2,1)S(1)} %get-tuple-element.44.refs_0_), channel_id=1, source_target_pairs={{0,4},{1,5},{2,3},{3,2},{4,0},{5,1},{6,7},{7,6},{8,9},{9,8},{10,14... | collective-permute-start | bytes 589832 | tf_op jit(solution)/shard_map/ppermute | solution.py:530
  40.8 9.2 %collective-permute-start.16 = (bf16[128,768]{1,0:T(8,128)(2,1)S(1)}, bf16[128,768]{1,0:T(8,128)(2,1)S(1)}, u32[]{:S(2)}, u32[]{:S(2)}) collective-permute-start(bf16[128,768]{1,0:T(8,128)(2,1)S(1)} %get-tuple-element.45.refs_1_), channel_id=1, source_target_pairs={{0,2},{1,3},{2,0},{3,1},{4,5},{5,4},{6,7},{7,6},{8,10},{9,11},{10,... | collective-permute-start | bytes 589832 | tf_op jit(solution)/shard_map/ppermute | solution.py:530
  46.0 4.1 %collective-permute-start.17 = (bf16[128,768]{1,0:T(8,128)(2,1)S(1)}, bf16[128,768]{1,0:T(8,128)(2,1)S(1)}, u32[]{:S(2)}, u32[]{:S(2)}) collective-permute-start(bf16[128,768]{1,0:T(8,128)(2,1)S(1)} %collective-permute-done.13.refs_2_), channel_id=1, source_target_pairs={{0,1},{1,0},{2,6},{3,7},{4,5},{5,4},{6,2},{7,3},{8,12},{9,13},{10,... | collective-permute-start | bytes 589832 | tf_op jit(solution)/shard_map/ppermute | solution.py:530
  46.6 3.5 %collective-permute-start.18 = (bf16[128,768]{1,0:T(8,128)(2,1)S(1)}, bf16[128,768]{1,0:T(8,128)(2,1)S(1)}, u32[]{:S(2)}, u32[]{:S(2)}) collective-permute-start(bf16[128,768]{1,0:T(8,128)(2,1)S(1)} %collective-permute-done.14.refs_3_), channel_id=1, source_target_pairs={{0,1},{1,0},{2,3},{3,2},{4,6},{5,7},{6,4},{7,5},{8,9},{9,8},{10,11... | collective-permute-start | bytes 589832 | tf_op jit(solution)/shard_map/ppermute | solution.py:530
  50.7 1.8 %collective-permute-start.19 = (bf16[256,768]{1,0:T(8,128)(2,1)S(1)}, bf16[256,768]{1,0:T(8,128)(2,1)S(1)}, u32[]{:S(2)}, u32[]{:S(2)}) collective-permute-start(bf16[256,768]{1,0:T(8,128)(2,1)S(1)} %shard_map.107.refs_3_), channel_id=1, source_target_pairs={{0,1},{1,0},{2,3},{3,2},{4,5},{5,4},{6,7},{7,6},{8,9},{9,8},{10,11... | collective-permute-start | bytes 1179656 | tf_op jit(solution)/shard_map/ppermute | solution.py:518
  57.8 1.8 %collective-permute-start.20 = (bf16[384,411]{1,0:T(8,128)(2,1)S(1)}, bf16[384,411]{1,0:T(8,128)(2,1)S(1)}, u32[]{:S(2)}, u32[]{:S(2)}) collective-permute-start(bf16[384,411]{1,0:T(8,128)(2,1)S(1)} %get-tuple-element.49), channel_id=1, source_target_pairs={{0,1},{1,0},{2,3},{3,2},{4,5},{5,4},{6,7},{7,6},{8,9},{9,8},{10,11... | collective-permute-start | bytes 946952 | tf_op jit(solution)/shard_map/ppermute | solution.py:518
  59.7 5.7 %collective-permute-start.21 = (bf16[96,411]{1,0:T(8,128)(2,1)S(1)}, bf16[96,411]{1,0:T(8,128)(2,1)S(1)}, u32[]{:S(2)}, u32[]{:S(2)}) collective-permute-start(bf16[96,411]{1,0:T(8,128)(2,1)S(1)} %get-tuple-element.51), channel_id=1, source_target_pairs={{0,2},{1,3},{2,0},{3,1},{4,6},{5,7},{6,4},{7,5},{8,10},{9,11},{10,... | collective-permute-start | bytes 236744 | tf_op jit(solution)/shard_map/ppermute | solution.py:518
  62.3 5.9 %collective-permute-start.22 = (bf16[96,411]{1,0:T(8,128)(2,1)S(1)}, bf16[96,411]{1,0:T(8,128)(2,1)S(1)}, u32[]{:S(2)}, u32[]{:S(2)}) collective-permute-start(bf16[96,411]{1,0:T(8,128)(2,1)S(1)} %get-tuple-element.52), channel_id=1, source_target_pairs={{0,4},{1,5},{2,6},{3,7},{4,0},{5,1},{6,2},{7,3},{8,12},{9,13},{10,... | collective-permute-start | bytes 236744 | tf_op jit(solution)/shard_map/ppermute | solution.py:518
  64.0 5.7 %collective-permute-start.23 = (bf16[96,411]{1,0:T(8,128)(2,1)S(1)}, bf16[96,411]{1,0:T(8,128)(2,1)S(1)}, u32[]{:S(2)}, u32[]{:S(2)}) collective-permute-start(bf16[96,411]{1,0:T(8,128)(2,1)S(1)} %get-tuple-element.53), channel_id=1, source_target_pairs={{0,6},{1,7},{2,4},{3,5},{4,2},{5,3},{6,0},{7,1},{8,14},{9,15},{10,... | collective-permute-start | bytes 236744 | tf_op jit(solution)/shard_map/ppermute | solution.py:518
  69.9 5.9 %collective-permute-start.24 = (bf16[32,411]{1,0:T(8,128)(2,1)S(1)}, bf16[32,411]{1,0:T(8,128)(2,1)S(1)}, u32[]{:S(2)}, u32[]{:S(2)}) collective-permute-start(bf16[32,411]{1,0:T(8,128)(2,1)S(1)} %get-tuple-element.55), channel_id=1, source_target_pairs={{0,8},{8,16},{16,24},{24,0},{1,9},{9,17},{17,25},{25,1},{2,10},{10... | collective-permute-start | bytes 78920 | tf_op jit(solution)/shard_map/ppermute | solution.py:521
  71.1 5.1 %collective-permute-start.25 = (bf16[32,411]{1,0:T(8,128)(2,1)S(1)}, bf16[32,411]{1,0:T(8,128)(2,1)S(1)}, u32[]{:S(2)}, u32[]{:S(2)}) collective-permute-start(bf16[32,411]{1,0:T(8,128)(2,1)S(1)} %get-tuple-element.56), channel_id=1, source_target_pairs={{0,16},{8,24},{16,0},{24,8},{1,17},{9,25},{17,1},{25,9},{2,18},{10... | collective-permute-start | bytes 78920 | tf_op jit(solution)/shard_map/ppermute | solution.py:521
  74.2 3.9 %collective-permute-start.26 = (bf16[32,411]{1,0:T(8,128)(2,1)S(1)}, bf16[32,411]{1,0:T(8,128)(2,1)S(1)}, u32[]{:S(2)}, u32[]{:S(2)}) collective-permute-start(bf16[32,411]{1,0:T(8,128)(2,1)S(1)} %get-tuple-element.57), channel_id=1, source_target_pairs={{0,24},{8,0},{16,8},{24,16},{1,25},{9,1},{17,9},{25,17},{2,26},{10... | collective-permute-start | bytes 78920 | tf_op jit(solution)/shard_map/ppermute | solution.py:521

commit v5 on v3

--- a/solution.py
+++ b/solution.py
@@ -9,7 +9,7 @@
 
 VMEM_BYTES = 24 * 1024 * 1024
 WHOLE_VMEM_BYTES = 63 * 1024 * 1024
-SLACK_FLOPS = 5 * 10**9
+SLACK_FLOPS = 10**9
 NT_DIMS = (((1,), (1,)), ((), ()))
 
 
@@ -569,18 +569,16 @@
         strips = grow(strips, lambda value: trade(value, bit), [seen] if 2 * bit == p.tiles else ())
         stages.append(strips)
         bit *= 2
-    bit = p.group
-    while bit < p.chans:
-        strips = grow(strips, lambda value: flip(value, bit))
-        stages.append(strips)
-        bit *= 2
+    strips = join(
+        [strips] + [flip(strips, k * p.group) for k in range(1, p.chips)], (p.strips, p.width)
+    )
     strips = [strips] + [flip(strips, k) for k in range(1, p.group)]
 
     near = [w_hidden] + [flip(w_hidden, chip * p.group) for chip in range(1, p.chips)]
     near = call(
         functools.partial(stack_kernel, p),
         shape((p.chips * p.deep, p.hidden), half),
-        near + [stages[-2]],
+        near + [stages[-1]],
         in_hbm=[len(near)],
     )
     weights = [near] + [flip(near, k) for k in range(1, p.group)]

time: 79 us -> 78.4 us (level)
  waiting for transfers between devices: 34 us -> 26.7 us
  Pallas kernels: 12.4 us -> 17.7 us
  local copies, waits for them, and re-layouts: 2.88 us -> 6.05 us
  starting transfers between devices: 29.2 us -> 27.3 us
    pallas_call x14 -> x13, Pallas kernels: 12.4 us -> 17.7 us  [call(): pl.pallas_call(kernel, out_shape=out_shape, in_specs=[far if k in in_hbm...]
    ppermute x7, waiting for transfers between devices: 14.3 us -> 9.71 us  [send(): lax.ppermute(value, both, sorted(((number(a), number(b)) for a, b in pair...]
    unnamed x15 -> x21, local copies, waits for them, and re-layouts: 2.73 us -> 5.89 us
    ppermute x12 -> x13, waiting for transfers between devices: 12.6 us -> 11.2 us  [flip(): return lax.ppermute(value, 'chan', [(b, b ^ mask) for b in range(p.chans)])]
    ppermute x3, starting transfers between devices: 5.82 us -> 4.75 us  [trade(): return lax.ppermute(value, 'tile', [(a, a ^ mask) for a in range(p.tiles)])]
    ppermute x7, starting transfers between devices: 5.45 us -> 4.51 us  [send(): lax.ppermute(value, both, sorted(((number(a), number(b)) for a, b in pair...]
    ppermute x12 -> x13, starting transfers between devices: 12.6 us -> 13.5 us  [flip(): return lax.ppermute(value, 'chan', [(b, b ^ mask) for b in range(p.chans)])]
  transfers between devices with their start and end apart: 25 -> 26, of which waited for: 16 -> 15; matrix products, arithmetic and copies ran while one was open for 0% -> 1% of each run, Pallas kernels for 5% -> 5%
where the time goes in v5:
time: 78.4 us; the launch traced here: 78.1 us
  starting transfers between devices  27.3 us (35%)
  waiting for transfers between devices  26.7 us (34%)
  Pallas kernels  17.7 us (23%)
  local copies, waits for them, and re-layouts  6.05 us (8%)
    pallas_call x13, Pallas kernels, call(): pl.pallas_call(kernel, out_shape=out_shape, in_specs=[far if k in in_hbm...  17.7 us
    ppermute x13, starting transfers between devices, flip(): return lax.ppermute(value, 'chan', [(b, b ^ mask) for b in range(p.chans)])  13.5 us
    ppermute x13, waiting for transfers between devices, flip(): return lax.ppermute(value, 'chan', [(b, b ^ mask) for b in range(p.chans)])  11.2 us
    ppermute x7, waiting for transfers between devices, send(): lax.ppermute(value, both, sorted(((number(a), number(b)) for a, b in pair...  9.71 us
    unnamed x21, local copies, waits for them, and re-layouts  5.89 us
    ppermute x3, starting transfers between devices, trade(): return lax.ppermute(value, 'tile', [(a, a ^ mask) for a in range(p.tiles)])  4.75 us
    ppermute x3, starting transfers between devices, shift(): lax.ppermute(value, 'tile', [(a, (a + by) % p.tiles) for a in range(p.til...  4.59 us
    ppermute x7, starting transfers between devices, send(): lax.ppermute(value, both, sorted(((number(a), number(b)) for a, b in pair...  4.51 us
  transfers between devices with their start and end apart: 26, of which 15 were waited for; matrix products, arithmetic and copies ran while one was open for 1% of the time, Pallas kernels for 5%

profile of v5, /device:TPU:0, one launch (start us, length us, event | category | flops | bytes accessed | tf_op | source)
XLA Modules:
  0.0 78.1 jit_solution(16283084676292364878)
XLA Ops:
  0.0 3.0 %collective-permute-start.8 = (bf16[411,256]{1,0:T(8,128)(2,1)}, bf16[411,256]{1,0:T(8,128)(2,1)S(1)}, u32[]{:S(2)}, u32[]{:S(2)}) collective-permute-start(bf16[411,256]{1,0:T(8,128)(2,1)} %refs_0_.6), channel_id=1, source_target_pairs={{0,4},{1,5},{2,6},{3,7},{4,0},{5,1},{6,2},{7,3},{8,12},{9,13},{10,... | collective-permute-start | bytes 631304 | tf_op jit(solution)/shard_map/ppermute | solution.py:514
  3.0 1.5 %collective-permute-start.7 = (bf16[411,256]{1,0:T(8,128)(2,1)}, bf16[411,256]{1,0:T(8,128)(2,1)S(1)}, u32[]{:S(2)}, u32[]{:S(2)}) collective-permute-start(bf16[411,256]{1,0:T(8,128)(2,1)} %refs_0_.6), channel_id=1, source_target_pairs={{0,2},{1,3},{2,0},{3,1},{4,6},{5,7},{6,4},{7,5},{8,10},{9,11},{10,... | collective-permute-start | bytes 631304 | tf_op jit(solution)/shard_map/ppermute | solution.py:514
  4.5 0.0 collective-permute-start.9
  4.5 2.0 %collective-permute-start.2 = (bf16[128,768]{1,0:T(8,128)(2,1)}, bf16[128,768]{1,0:T(8,128)(2,1)S(1)}, u32[]{:S(2)}, u32[]{:S(2)}) collective-permute-start(bf16[128,768]{1,0:T(8,128)(2,1)} %refs_0_.5), channel_id=1, source_target_pairs={{0,8},{8,0},{16,24},{24,16},{1,9},{9,1},{17,25},{25,17},{2,10},{10... | collective-permute-start | bytes 589832 | tf_op jit(solution)/shard_map/ppermute | solution.py:545
  6.5 1.8 %shard_map.101.refs_0_ = bf16[16,512]{1,0:T(8,128)(2,1)} custom-call(f32[4,32,411]{2,1,0:T(8,128)} %refs_0_.4, f32[4,32]{1,0:T(4,128)} %refs_1_.2, s32[128]{0:T(128)} %refs_2_.1, f32[256]{0:T(256)} %refs_3_.2), custom_call_target="tpu_custom_call" | custom-call | bytes 212480 | tf_op jit(solution)/shard_map/pallas_call | solution.py:164
  8.3 0.1 collective-permute-start
  8.4 3.9 %collective-permute-done.refs_1_ = bf16[16,512]{1,0:T(8,128)(2,1)S(1)} collective-permute-done((bf16[16,512]{1,0:T(8,128)(2,1)}, bf16[16,512]{1,0:T(8,128)(2,1)S(1)}, u32[]{:S(2)}, u32[]{:S(2)}) %collective-permute-start) | collective-permute-done | bytes 16416 | tf_op jit(solution)/shard_map/ppermute | solution.py:545
  12.3 0.7 copy-done.7
  13.1 2.7 %collective-permute-start.1 = (bf16[32,512]{1,0:T(8,128)(2,1)S(1)}, bf16[32,512]{1,0:T(8,128)(2,1)S(1)}, u32[]{:S(2)}, u32[]{:S(2)}) collective-permute-start(bf16[32,512]{1,0:T(8,128)(2,1)S(1)} %shard_map.102.refs_0_), channel_id=1, source_target_pairs={{0,16},{8,24},{16,0},{24,8},{1,17},{9,25},{17,1},{25,9},{2,18},{10... | collective-permute-start | bytes 98312 | tf_op jit(solution)/shard_map/ppermute | solution.py:545
  15.7 0.0 collective-permute-done.2.refs_1_
  15.7 0.7 copy-done.4
  16.4 0.9 %copy-done.3 = bf16[128,768]{1,0:T(8,128)(2,1)S(1)} copy-done((bf16[128,768]{1,0:T(8,128)(2,1)S(1)}, bf16[128,768]{1,0:T(8,128)(2,1)}, u32[]{:S(2)}) %copy-start.3) | copy-done | bytes 196632
  17.3 0.9 %copy-done.5 = bf16[128,768]{1,0:T(8,128)(2,1)S(1)} copy-done((bf16[128,768]{1,0:T(8,128)(2,1)S(1)}, bf16[128,768]{1,0:T(8,128)(2,1)}, u32[]{:S(2)}) %copy-start.5) | copy-done | bytes 196632
  18.3 0.5 shard_map.103.refs_2_.refs_9_
  18.8 0.1 shard_map.104.refs_0_.refs_4_
  18.9 0.0 copy-start.2
  18.9 0.9 %copy-done.2 = bf16[411,256]{1,0:T(8,128)(2,1)S(1)} copy-done((bf16[411,256]{1,0:T(8,128)(2,1)S(1)}, bf16[411,256]{1,0:T(8,128)(2,1)}, u32[]{:S(2)}) %copy-start.2) | copy-done | bytes 210456
  19.9 1.9 %shard_map.106.refs_7_.refs_5_ = bf16[1664,256]{1,0:T(8,128)(2,1)} custom-call(bf16[411,256]{1,0:T(8,128)(2,1)S(1)} %copy-done.2, bf16[411,256]{1,0:T(8,128)(2,1)S(1)} %collective-permute-done.7.refs_1_, bf16[411,256]{1,0:T(8,128)(2,1)S(1)} %collective-permute-done.8.refs_2_, bf16[411,256]{1,0:T(8,128)(2,1)} %collective-permute-done.9.refs_3_, ...), custom_call_target="tpu_custom_call" | custom-call | bytes 907264 | tf_op jit(solution)/shard_map/pallas_call | solution.py:164
  21.8 1.7 %collective-permute-start.11 = (bf16[256,768]{1,0:T(8,128)(2,1)S(1)}, bf16[256,768]{1,0:T(8,128)(2,1)}, u32[]{:S(2)}, u32[]{:S(2)}) collective-permute-start(bf16[256,768]{1,0:T(8,128)(2,1)S(1)} %shard_map.103.refs_2_.refs_9_), channel_id=1, source_target_pairs={{0,16},{1,17},{2,3},{3,2},{4,20},{5,21},{6,7},{7,6},{8,9},{9,8},{1... | collective-permute-start | bytes 1179656 | tf_op jit(solution)/shard_map/ppermute | solution.py:526
  23.5 1.2 %collective-permute-start.5 = (bf16[64,512]{1,0:T(8,128)(2,1)S(1)}, bf16[64,512]{1,0:T(8,128)(2,1)S(1)}, u32[]{:S(2)}, u32[]{:S(2)}) collective-permute-start(bf16[64,512]{1,0:T(8,128)(2,1)S(1)} %shard_map.104.refs_0_.refs_4_), channel_id=1, source_target_pairs={{0,6},{1,7},{2,4},{3,5},{4,2},{5,3},{6,0},{7,1},{8,14},{9,15},{10,... | collective-permute-start | bytes 196616 | tf_op jit(solution)/shard_map/ppermute | solution.py:514
  24.8 0.5 collective-permute-start.4
  25.3 1.8 %collective-permute-start.3 = (bf16[64,512]{1,0:T(8,128)(2,1)S(1)}, bf16[64,512]{1,0:T(8,128)(2,1)S(1)}, u32[]{:S(2)}, u32[]{:S(2)}) collective-permute-start(bf16[64,512]{1,0:T(8,128)(2,1)S(1)} %shard_map.104.refs_0_.refs_4_), channel_id=1, source_target_pairs={{0,2},{1,3},{2,0},{3,1},{4,6},{5,7},{6,4},{7,5},{8,10},{9,11},{10,... | collective-permute-start | bytes 196616 | tf_op jit(solution)/shard_map/ppermute | solution.py:514
  27.0 2.0 %collective-permute-done.5.refs_3_ = bf16[64,512]{1,0:T(8,128)(2,1)S(1)} collective-permute-done((bf16[64,512]{1,0:T(8,128)(2,1)S(1)}, bf16[64,512]{1,0:T(8,128)(2,1)S(1)}, u32[]{:S(2)}, u32[]{:S(2)}) %collective-permute-start.5) | collective-permute-done | bytes 65568 | tf_op jit(solution)/shard_map/ppermute | solution.py:514
  29.0 0.9 %collective-permute-done.4.refs_2_ = bf16[64,512]{1,0:T(8,128)(2,1)S(1)} collective-permute-done((bf16[64,512]{1,0:T(8,128)(2,1)S(1)}, bf16[64,512]{1,0:T(8,128)(2,1)S(1)}, u32[]{:S(2)}, u32[]{:S(2)}) %collective-permute-start.4) | collective-permute-done | bytes 65568 | tf_op jit(solution)/shard_map/ppermute | solution.py:514
  29.9 0.2 collective-permute-done.3.refs_1_
  30.1 0.7 shard_map.105.refs_5_
  30.9 0.1 collective-permute-start.6
  30.9 0.8 %copy.22.owners_ref = s32[256,1]{1,0:T(8,128)} copy(s32[256,1]{0,1:T(1,128)S(1)} %copy-done.9) | data formatting | bytes 2048 | tf_op args[2]
  31.7 0.9 %copy-done.6 = s32[256,1]{1,0:T(8,128)S(1)} copy-done((s32[256,1]{1,0:T(8,128)S(1)}, s32[256,1]{1,0:T(8,128)}, u32[]{:S(2)}) %copy-start.6) | copy-done | bytes 1048
  32.6 0.9 %shard_map.100 = (s32[256,1]{1,0:T(8,128)S(1)}, s32[256,1]{1,0:T(8,128)S(1)}, s32[24,1]{1,0:T(8,128)S(1)}, s32[384,1]{1,0:T(8,128)S(1)}, s32[384,1]{1,0:T(8,128)S(1)}) custom-call(s32[256,1]{1,0:T(8,128)S(1)} %copy-done.6), custom_call_target="tpu_custom_call" | custom-call | flops 1000000000 | bytes 1024 | tf_op jit(solution)/shard_map/pallas_call | solution.py:164
  33.5 0.8 collective-permute-done.11.refs_10_
  34.3 0.0 copy-start.1
  34.4 4.2 %shard_map.107 = (bf16[128,768]{1,0:T(8,128)(2,1)S(1)}, bf16[128,768]{1,0:T(8,128)(2,1)S(1)}, f32[8,256,256]{2,1,0:T(8,128)S(1)}, f32[24,128]{1,0:T(8,128)S(1)}) custom-call(s32[256,1]{1,0:T(8,128)S(1)} %get-tuple-element.24.refs_0_, s32[256,1]{1,0:T(8,128)S(1)} %get-tuple-element.25.refs_1_, s32[24,1]{1,0:T(8,128)S(1)} %get-tuple-element.26.refs_2_, ...), custom_call_target="tpu_custom_call" | custom-call | flops 1236271104 | bytes 6165600 | tf_op jit(solution)/shard_map/pallas_call | solution.py:164
  38.5 0.5 collective-permute-start.12
  39.0 1.2 %collective-permute-start.13 = (bf16[128,768]{1,0:T(8,128)(2,1)S(1)}, bf16[128,768]{1,0:T(8,128)(2,1)S(1)}, u32[]{:S(2)}, u32[]{:S(2)}) collective-permute-start(bf16[128,768]{1,0:T(8,128)(2,1)S(1)} %get-tuple-element.29.refs_1_), channel_id=1, source_target_pairs={{0,4},{1,5},{2,3},{3,2},{4,0},{5,1},{6,7},{7,6},{8,9},{9,8},{10,14... | collective-permute-start | bytes 589832 | tf_op jit(solution)/shard_map/ppermute | solution.py:526
  40.2 0.8 %collective-permute-start.14 = (bf16[128,768]{1,0:T(8,128)(2,1)S(1)}, bf16[128,768]{1,0:T(8,128)(2,1)S(1)}, u32[]{:S(2)}, u32[]{:S(2)}) collective-permute-start(bf16[128,768]{1,0:T(8,128)(2,1)S(1)} %get-tuple-element.28.refs_0_), channel_id=1, source_target_pairs={{0,4},{1,5},{2,3},{3,2},{4,0},{5,1},{6,7},{7,6},{8,9},{9,8},{10,14... | collective-permute-start | bytes 589832 | tf_op jit(solution)/shard_map/ppermute | solution.py:526
  41.0 0.1 collective-permute-start.15
  41.1 5.3 %collective-permute-done.12.refs_2_ = bf16[128,768]{1,0:T(8,128)(2,1)S(1)} collective-permute-done((bf16[128,768]{1,0:T(8,128)(2,1)S(1)}, bf16[128,768]{1,0:T(8,128)(2,1)S(1)}, u32[]{:S(2)}, u32[]{:S(2)}) %collective-permute-start.12) | collective-permute-done | bytes 196640 | tf_op jit(solution)/shard_map/ppermute | solution.py:526
  46.4 0.3 collective-permute-done.13.refs_3_
  46.8 0.2 collective-permute-start.17
  46.9 3.3 %collective-permute-done.14.refs_4_ = bf16[128,768]{1,0:T(8,128)(2,1)S(1)} collective-permute-done((bf16[128,768]{1,0:T(8,128)(2,1)S(1)}, bf16[128,768]{1,0:T(8,128)(2,1)S(1)}, u32[]{:S(2)}, u32[]{:S(2)}) %collective-permute-start.14) | collective-permute-done | bytes 196640 | tf_op jit(solution)/shard_map/ppermute | solution.py:526
  50.3 0.6 shard_map.108.refs_3_
  50.8 0.1 collective-permute-start.18
  50.9 1.7 %collective-permute-done.18.refs_4_ = bf16[256,768]{1,0:T(8,128)(2,1)S(1)} collective-permute-done((bf16[256,768]{1,0:T(8,128)(2,1)S(1)}, bf16[256,768]{1,0:T(8,128)(2,1)S(1)}, u32[]{:S(2)}, u32[]{:S(2)}) %collective-permute-start.18) | collective-permute-done | bytes 393248 | tf_op jit(solution)/shard_map/ppermute | solution.py:514
  52.6 5.3 %shard_map.109 = (bf16[384,411]{1,0:T(8,128)(2,1)S(1)}, bf16[384,411]{1,0:T(8,128)(2,1)S(1)}) custom-call(bf16[2048,768]{1,0:T(8,128)(2,1)S(1)} %copy-done, bf16[1536,768]{1,0:T(8,128)(2,1)S(1)} %copy-done.1, f32[8,256,256]{2,1,0:T(8,128)S(1)} %get-tuple-element.27.refs_2_, bf16[256,768]{1,0:T(8,128)(2,1)S(1)} %shard_map.108.refs_3_, ...), custom_call_target="tpu_custom_call" | custom-call | flops 1840250880 | bytes 10095616 | tf_op jit(solution)/shard_map/pallas_call | solution.py:164
  58.0 0.2 collective-permute-start.19
  58.2 0.1 slice_bitcast_fusion.2
  58.3 1.5 %collective-permute-done.19.refs_1_ = bf16[384,411]{1,0:T(8,128)(2,1)S(1)} collective-permute-done((bf16[384,411]{1,0:T(8,128)(2,1)S(1)}, bf16[384,411]{1,0:T(8,128)(2,1)S(1)}, u32[]{:S(2)}, u32[]{:S(2)}) %collective-permute-start.19) | collective-permute-done | bytes 315680 | tf_op jit(solution)/shard_map/ppermute | solution.py:514
  59.8 0.1 shard_map.110
  59.9 2.6 %collective-permute-start.20 = (bf16[96,411]{1,0:T(8,128)(2,1)S(1)}, bf16[96,411]{1,0:T(8,128)(2,1)S(1)}, u32[]{:S(2)}, u32[]{:S(2)}) collective-permute-start(bf16[96,411]{1,0:T(8,128)(2,1)S(1)} %get-tuple-element.35), channel_id=1, source_target_pairs={{0,2},{1,3},{2,0},{3,1},{4,6},{5,7},{6,4},{7,5},{8,10},{9,11},{10,... | collective-permute-start | bytes 236744 | tf_op jit(solution)/shard_map/ppermute | solution.py:514
  62.5 1.7 %collective-permute-start.21 = (bf16[96,411]{1,0:T(8,128)(2,1)S(1)}, bf16[96,411]{1,0:T(8,128)(2,1)S(1)}, u32[]{:S(2)}, u32[]{:S(2)}) collective-permute-start(bf16[96,411]{1,0:T(8,128)(2,1)S(1)} %get-tuple-element.36), channel_id=1, source_target_pairs={{0,4},{1,5},{2,6},{3,7},{4,0},{5,1},{6,2},{7,3},{8,12},{9,13},{10,... | collective-permute-start | bytes 236744 | tf_op jit(solution)/shard_map/ppermute | solution.py:514
  64.2 0.8 %collective-permute-start.22 = (bf16[96,411]{1,0:T(8,128)(2,1)S(1)}, bf16[96,411]{1,0:T(8,128)(2,1)S(1)}, u32[]{:S(2)}, u32[]{:S(2)}) collective-permute-start(bf16[96,411]{1,0:T(8,128)(2,1)S(1)} %get-tuple-element.37), channel_id=1, source_target_pairs={{0,6},{1,7},{2,4},{3,5},{4,2},{5,3},{6,0},{7,1},{8,14},{9,15},{10,... | collective-permute-start | bytes 236744 | tf_op jit(solution)/shard_map/ppermute | solution.py:514
  65.0 0.6 collective-permute-done.20.refs_1_
  65.6 2.8 %collective-permute-done.21.refs_2_ = bf16[96,411]{1,0:T(8,128)(2,1)S(1)} collective-permute-done((bf16[96,411]{1,0:T(8,128)(2,1)S(1)}, bf16[96,411]{1,0:T(8,128)(2,1)S(1)}, u32[]{:S(2)}, u32[]{:S(2)}) %collective-permute-start.21) | collective-permute-done | bytes 78944 | tf_op jit(solution)/shard_map/ppermute | solution.py:514
  68.4 1.5 %collective-permute-done.22.refs_3_ = bf16[96,411]{1,0:T(8,128)(2,1)S(1)} collective-permute-done((bf16[96,411]{1,0:T(8,128)(2,1)S(1)}, bf16[96,411]{1,0:T(8,128)(2,1)S(1)}, u32[]{:S(2)}, u32[]{:S(2)}) %collective-permute-start.22) | collective-permute-done | bytes 78944 | tf_op jit(solution)/shard_map/ppermute | solution.py:514
  69.9 0.2 shard_map.111
  70.2 1.2 %collective-permute-start.23 = (bf16[32,411]{1,0:T(8,128)(2,1)S(1)}, bf16[32,411]{1,0:T(8,128)(2,1)S(1)}, u32[]{:S(2)}, u32[]{:S(2)}) collective-permute-start(bf16[32,411]{1,0:T(8,128)(2,1)S(1)} %get-tuple-element.39), channel_id=1, source_target_pairs={{0,8},{8,16},{16,24},{24,0},{1,9},{9,17},{17,25},{25,1},{2,10},{10... | collective-permute-start | bytes 78920 | tf_op jit(solution)/shard_map/ppermute | solution.py:517
  71.4 1.4 %collective-permute-start.24 = (bf16[32,411]{1,0:T(8,128)(2,1)S(1)}, bf16[32,411]{1,0:T(8,128)(2,1)S(1)}, u32[]{:S(2)}, u32[]{:S(2)}) collective-permute-start(bf16[32,411]{1,0:T(8,128)(2,1)S(1)} %get-tuple-element.40), channel_id=1, source_target_pairs={{0,16},{8,24},{16,0},{24,8},{1,17},{9,25},{17,1},{25,9},{2,18},{10... | collective-permute-start | bytes 78920 | tf_op jit(solution)/shard_map/ppermute | solution.py:517
  72.8 2.0 %collective-permute-start.25 = (bf16[32,411]{1,0:T(8,128)(2,1)S(1)}, bf16[32,411]{1,0:T(8,128)(2,1)S(1)}, u32[]{:S(2)}, u32[]{:S(2)}) collective-permute-start(bf16[32,411]{1,0:T(8,128)(2,1)S(1)} %get-tuple-element.41), channel_id=1, source_target_pairs={{0,24},{8,0},{16,8},{24,16},{1,25},{9,1},{17,9},{25,17},{2,26},{10... | collective-permute-start | bytes 78920 | tf_op jit(solution)/shard_map/ppermute | solution.py:517
  74.7 0.1 maximum_sqrt_fusion
  74.8 0.1 copy.23
  74.9 1.1 %collective-permute-done.23.refs_1_ = bf16[32,411]{1,0:T(8,128)(2,1)S(1)} collective-permute-done((bf16[32,411]{1,0:T(8,128)(2,1)S(1)}, bf16[32,411]{1,0:T(8,128)(2,1)S(1)}, u32[]{:S(2)}, u32[]{:S(2)}) %collective-permute-start.23) | collective-permute-done | bytes 26336 | tf_op jit(solution)/shard_map/ppermute | solution.py:517
  76.0 0.7 collective-permute-done.24.refs_2_
  76.7 1.4 %shard_map.112 = f32[4,32,411]{2,1,0:T(8,128)} custom-call(bf16[32,411]{1,0:T(8,128)(2,1)S(1)} %get-tuple-element.38.refs_0_, bf16[32,411]{1,0:T(8,128)(2,1)S(1)} %collective-permute-done.23.refs_1_, bf16[32,411]{1,0:T(8,128)(2,1)S(1)} %collective-permute-done.24.refs_2_, bf16[32,411]{1,0:T(8,128)(2,1)S(1)} %collective-permute-done.25.refs_3_, ...), custom_call_target="tpu_custom_call" | custom-call | flops 5260800 | bytes 106752 | tf_op jit(solution)/shard_map/pallas_call | solution.py:164
  (26 shorter events, 0.1 us)
Async XLA Ops:
  0.0 30.9 %copy-start.9 = (s32[256,1]{0,1:T(1,128)S(1)}, s32[256,1]{0,1:T(1,128)}, u32[]{:S(2)}) copy-start(s32[256,1]{0,1:T(1,128)} %param.12) | copy-start | bytes 3076
  0.0 18.9 %collective-permute-start.8 = (bf16[411,256]{1,0:T(8,128)(2,1)}, bf16[411,256]{1,0:T(8,128)(2,1)S(1)}, u32[]{:S(2)}, u32[]{:S(2)}) collective-permute-start(bf16[411,256]{1,0:T(8,128)(2,1)} %refs_0_.6), channel_id=1, source_target_pairs={{0,4},{1,5},{2,6},{3,7},{4,0},{5,1},{6,2},{7,3},{8,12},{9,13},{10,... | collective-permute-start | bytes 631304 | tf_op jit(solution)/shard_map/ppermute | solution.py:514
  3.0 15.9 %collective-permute-start.7 = (bf16[411,256]{1,0:T(8,128)(2,1)}, bf16[411,256]{1,0:T(8,128)(2,1)S(1)}, u32[]{:S(2)}, u32[]{:S(2)}) collective-permute-start(bf16[411,256]{1,0:T(8,128)(2,1)} %refs_0_.6), channel_id=1, source_target_pairs={{0,2},{1,3},{2,0},{3,1},{4,6},{5,7},{6,4},{7,5},{8,10},{9,11},{10,... | collective-permute-start | bytes 631304 | tf_op jit(solution)/shard_map/ppermute | solution.py:514
  4.5 14.5 %collective-permute-start.9 = (bf16[411,256]{1,0:T(8,128)(2,1)}, bf16[411,256]{1,0:T(8,128)(2,1)}, u32[]{:S(2)}, u32[]{:S(2)}) collective-permute-start(bf16[411,256]{1,0:T(8,128)(2,1)} %refs_0_.6), channel_id=1, source_target_pairs={{0,6},{1,7},{2,4},{3,5},{4,2},{5,3},{6,0},{7,1},{8,14},{9,15},{10,... | collective-permute-start | bytes 631304 | tf_op jit(solution)/shard_map/ppermute | solution.py:514
  4.5 11.2 %collective-permute-start.2 = (bf16[128,768]{1,0:T(8,128)(2,1)}, bf16[128,768]{1,0:T(8,128)(2,1)S(1)}, u32[]{:S(2)}, u32[]{:S(2)}) collective-permute-start(bf16[128,768]{1,0:T(8,128)(2,1)} %refs_0_.5), channel_id=1, source_target_pairs={{0,8},{8,0},{16,24},{24,16},{1,9},{9,1},{17,25},{25,17},{2,10},{10... | collective-permute-start | bytes 589832 | tf_op jit(solution)/shard_map/ppermute | solution.py:545
  8.3 4.0 %collective-permute-start = (bf16[16,512]{1,0:T(8,128)(2,1)}, bf16[16,512]{1,0:T(8,128)(2,1)S(1)}, u32[]{:S(2)}, u32[]{:S(2)}) collective-permute-start(bf16[16,512]{1,0:T(8,128)(2,1)} %shard_map.101.refs_0_), channel_id=1, source_target_pairs={{0,8},{8,0},{16,24},{24,16},{1,9},{9,1},{17,25},{25,17},{2,10},{10... | collective-permute-start | bytes 49160 | tf_op jit(solution)/shard_map/ppermute | solution.py:545
  12.3 0.7 copy-start.7
  13.1 5.7 %collective-permute-start.1 = (bf16[32,512]{1,0:T(8,128)(2,1)S(1)}, bf16[32,512]{1,0:T(8,128)(2,1)S(1)}, u32[]{:S(2)}, u32[]{:S(2)}) collective-permute-start(bf16[32,512]{1,0:T(8,128)(2,1)S(1)} %shard_map.102.refs_0_), channel_id=1, source_target_pairs={{0,16},{8,24},{16,0},{24,8},{1,17},{9,25},{17,1},{25,9},{2,18},{10... | collective-permute-start | bytes 98312 | tf_op jit(solution)/shard_map/ppermute | solution.py:545
  15.7 0.7 copy-start.4
  16.4 0.9 %copy-start.3 = (bf16[128,768]{1,0:T(8,128)(2,1)S(1)}, bf16[128,768]{1,0:T(8,128)(2,1)}, u32[]{:S(2)}) copy-start(bf16[128,768]{1,0:T(8,128)(2,1)} %refs_0_.5) | copy-start | bytes 589828
  17.3 0.9 %copy-start.5 = (bf16[128,768]{1,0:T(8,128)(2,1)S(1)}, bf16[128,768]{1,0:T(8,128)(2,1)}, u32[]{:S(2)}) copy-start(bf16[128,768]{1,0:T(8,128)(2,1)} %copy-done.4) | copy-start | bytes 589828
  18.9 0.9 %copy-start.2 = (bf16[411,256]{1,0:T(8,128)(2,1)S(1)}, bf16[411,256]{1,0:T(8,128)(2,1)}, u32[]{:S(2)}) copy-start(bf16[411,256]{1,0:T(8,128)(2,1)} %refs_0_.6) | copy-start | bytes 631300
  19.9 14.5 %copy-start.8 = (f32[768]{0:T(1024)S(1)}, f32[768]{0:T(1024)}, u32[]{:S(2)}) copy-start(f32[768]{0:T(1024)} %refs_3_.3) | copy-start | bytes 9220
  21.8 12.5 %copy-start = (bf16[2048,768]{1,0:T(8,128)(2,1)S(1)}, bf16[2048,768]{1,0:T(8,128)(2,1)}, u32[]{:S(2)}) copy-start(bf16[2048,768]{1,0:T(8,128)(2,1)} %refs_0_.7) | copy-start | bytes 9437188
  21.8 12.5 %collective-permute-start.10 = (bf16[1664,256]{1,0:T(8,128)(2,1)}, bf16[1664,256]{1,0:T(8,128)(2,1)}, u32[]{:S(2)}, u32[]{:S(2)}) collective-permute-start(bf16[1664,256]{1,0:T(8,128)(2,1)} %shard_map.106.refs_7_.refs_5_), channel_id=1, source_target_pairs={{0,1},{1,0},{2,3},{3,2},{4,5},{5,4},{6,7},{7,6},{8,9},{9,8},{10,11... | collective-permute-start | bytes 2555912 | tf_op jit(solution)/shard_map/ppermute | solution.py:514
  21.8 12.5 %collective-permute-start.11 = (bf16[256,768]{1,0:T(8,128)(2,1)S(1)}, bf16[256,768]{1,0:T(8,128)(2,1)}, u32[]{:S(2)}, u32[]{:S(2)}) collective-permute-start(bf16[256,768]{1,0:T(8,128)(2,1)S(1)} %shard_map.103.refs_2_.refs_9_), channel_id=1, source_target_pairs={{0,16},{1,17},{2,3},{3,2},{4,20},{5,21},{6,7},{7,6},{8,9},{9,8},{1... | collective-permute-start | bytes 1179656 | tf_op jit(solution)/shard_map/ppermute | solution.py:526
  23.5 5.4 %collective-permute-start.5 = (bf16[64,512]{1,0:T(8,128)(2,1)S(1)}, bf16[64,512]{1,0:T(8,128)(2,1)S(1)}, u32[]{:S(2)}, u32[]{:S(2)}) collective-permute-start(bf16[64,512]{1,0:T(8,128)(2,1)S(1)} %shard_map.104.refs_0_.refs_4_), channel_id=1, source_target_pairs={{0,6},{1,7},{2,4},{3,5},{4,2},{5,3},{6,0},{7,1},{8,14},{9,15},{10,... | collective-permute-start | bytes 196616 | tf_op jit(solution)/shard_map/ppermute | solution.py:514
  24.8 5.1 %collective-permute-start.4 = (bf16[64,512]{1,0:T(8,128)(2,1)S(1)}, bf16[64,512]{1,0:T(8,128)(2,1)S(1)}, u32[]{:S(2)}, u32[]{:S(2)}) collective-permute-start(bf16[64,512]{1,0:T(8,128)(2,1)S(1)} %shard_map.104.refs_0_.refs_4_), channel_id=1, source_target_pairs={{0,4},{1,5},{2,6},{3,7},{4,0},{5,1},{6,2},{7,3},{8,12},{9,13},{10,... | collective-permute-start | bytes 196616 | tf_op jit(solution)/shard_map/ppermute | solution.py:514
  25.3 4.9 %collective-permute-start.3 = (bf16[64,512]{1,0:T(8,128)(2,1)S(1)}, bf16[64,512]{1,0:T(8,128)(2,1)S(1)}, u32[]{:S(2)}, u32[]{:S(2)}) collective-permute-start(bf16[64,512]{1,0:T(8,128)(2,1)S(1)} %shard_map.104.refs_0_.refs_4_), channel_id=1, source_target_pairs={{0,2},{1,3},{2,0},{3,1},{4,6},{5,7},{6,4},{7,5},{8,10},{9,11},{10,... | collective-permute-start | bytes 196616 | tf_op jit(solution)/shard_map/ppermute | solution.py:514
  30.9 2.7 %collective-permute-start.6 = (bf16[256,512]{1,0:T(8,128)(2,1)}, bf16[256,512]{1,0:T(8,128)(2,1)}, u32[]{:S(2)}, u32[]{:S(2)}) collective-permute-start(bf16[256,512]{1,0:T(8,128)(2,1)} %shard_map.105.refs_5_), channel_id=1, source_target_pairs={{0,1},{1,0},{2,3},{3,2},{4,5},{5,4},{6,7},{7,6},{8,9},{9,8},{10,11... | collective-permute-start | bytes 786440 | tf_op jit(solution)/shard_map/ppermute | solution.py:514
  31.7 0.9 %copy-start.6 = (s32[256,1]{1,0:T(8,128)S(1)}, s32[256,1]{1,0:T(8,128)}, u32[]{:S(2)}) copy-start(s32[256,1]{1,0:T(8,128)} %copy.22.owners_ref) | copy-start | bytes 3076
  34.3 18.3 %copy-start.1 = (bf16[1536,768]{1,0:T(8,128)(2,1)S(1)}, bf16[1536,768]{1,0:T(8,128)(2,1)}, u32[]{:S(2)}) copy-start(bf16[1536,768]{1,0:T(8,128)(2,1)} %refs_1_.3) | copy-start | bytes 7077892
  38.5 7.9 %collective-permute-start.12 = (bf16[128,768]{1,0:T(8,128)(2,1)S(1)}, bf16[128,768]{1,0:T(8,128)(2,1)S(1)}, u32[]{:S(2)}, u32[]{:S(2)}) collective-permute-start(bf16[128,768]{1,0:T(8,128)(2,1)S(1)} %get-tuple-element.28.refs_0_), channel_id=1, source_target_pairs={{0,2},{1,3},{2,0},{3,1},{4,5},{5,4},{6,7},{7,6},{8,10},{9,11},{10,... | collective-permute-start | bytes 589832 | tf_op jit(solution)/shard_map/ppermute | solution.py:526
  39.0 7.7 %collective-permute-start.13 = (bf16[128,768]{1,0:T(8,128)(2,1)S(1)}, bf16[128,768]{1,0:T(8,128)(2,1)S(1)}, u32[]{:S(2)}, u32[]{:S(2)}) collective-permute-start(bf16[128,768]{1,0:T(8,128)(2,1)S(1)} %get-tuple-element.29.refs_1_), channel_id=1, source_target_pairs={{0,4},{1,5},{2,3},{3,2},{4,0},{5,1},{6,7},{7,6},{8,9},{9,8},{10,14... | collective-permute-start | bytes 589832 | tf_op jit(solution)/shard_map/ppermute | solution.py:526
  40.2 10.0 %collective-permute-start.14 = (bf16[128,768]{1,0:T(8,128)(2,1)S(1)}, bf16[128,768]{1,0:T(8,128)(2,1)S(1)}, u32[]{:S(2)}, u32[]{:S(2)}) collective-permute-start(bf16[128,768]{1,0:T(8,128)(2,1)S(1)} %get-tuple-element.28.refs_0_), channel_id=1, source_target_pairs={{0,4},{1,5},{2,3},{3,2},{4,0},{5,1},{6,7},{7,6},{8,9},{9,8},{10,14... | collective-permute-start | bytes 589832 | tf_op jit(solution)/shard_map/ppermute | solution.py:526
  41.0 9.2 %collective-permute-start.15 = (bf16[128,768]{1,0:T(8,128)(2,1)S(1)}, bf16[128,768]{1,0:T(8,128)(2,1)S(1)}, u32[]{:S(2)}, u32[]{:S(2)}) collective-permute-start(bf16[128,768]{1,0:T(8,128)(2,1)S(1)} %get-tuple-element.29.refs_1_), channel_id=1, source_target_pairs={{0,2},{1,3},{2,0},{3,1},{4,5},{5,4},{6,7},{7,6},{8,10},{9,11},{10,... | collective-permute-start | bytes 589832 | tf_op jit(solution)/shard_map/ppermute | solution.py:526
  46.4 3.8 %collective-permute-start.16 = (bf16[128,768]{1,0:T(8,128)(2,1)S(1)}, bf16[128,768]{1,0:T(8,128)(2,1)S(1)}, u32[]{:S(2)}, u32[]{:S(2)}) collective-permute-start(bf16[128,768]{1,0:T(8,128)(2,1)S(1)} %collective-permute-done.12.refs_2_), channel_id=1, source_target_pairs={{0,1},{1,0},{2,6},{3,7},{4,5},{5,4},{6,2},{7,3},{8,12},{9,13},{10,... | collective-permute-start | bytes 589832 | tf_op jit(solution)/shard_map/ppermute | solution.py:526
  46.8 3.5 %collective-permute-start.17 = (bf16[128,768]{1,0:T(8,128)(2,1)S(1)}, bf16[128,768]{1,0:T(8,128)(2,1)S(1)}, u32[]{:S(2)}, u32[]{:S(2)}) collective-permute-start(bf16[128,768]{1,0:T(8,128)(2,1)S(1)} %collective-permute-done.13.refs_3_), channel_id=1, source_target_pairs={{0,1},{1,0},{2,3},{3,2},{4,6},{5,7},{6,4},{7,5},{8,9},{9,8},{10,11... | collective-permute-start | bytes 589832 | tf_op jit(solution)/shard_map/ppermute | solution.py:526
  50.8 1.8 %collective-permute-start.18 = (bf16[256,768]{1,0:T(8,128)(2,1)S(1)}, bf16[256,768]{1,0:T(8,128)(2,1)S(1)}, u32[]{:S(2)}, u32[]{:S(2)}) collective-permute-start(bf16[256,768]{1,0:T(8,128)(2,1)S(1)} %shard_map.108.refs_3_), channel_id=1, source_target_pairs={{0,1},{1,0},{2,3},{3,2},{4,5},{5,4},{6,7},{7,6},{8,9},{9,8},{10,11... | collective-permute-start | bytes 1179656 | tf_op jit(solution)/shard_map/ppermute | solution.py:514
  58.0 1.8 %collective-permute-start.19 = (bf16[384,411]{1,0:T(8,128)(2,1)S(1)}, bf16[384,411]{1,0:T(8,128)(2,1)S(1)}, u32[]{:S(2)}, u32[]{:S(2)}) collective-permute-start(bf16[384,411]{1,0:T(8,128)(2,1)S(1)} %get-tuple-element.33), channel_id=1, source_target_pairs={{0,1},{1,0},{2,3},{3,2},{4,5},{5,4},{6,7},{7,6},{8,9},{9,8},{10,11... | collective-permute-start | bytes 946952 | tf_op jit(solution)/shard_map/ppermute | solution.py:514
  59.9 5.7 %collective-permute-start.20 = (bf16[96,411]{1,0:T(8,128)(2,1)S(1)}, bf16[96,411]{1,0:T(8,128)(2,1)S(1)}, u32[]{:S(2)}, u32[]{:S(2)}) collective-permute-start(bf16[96,411]{1,0:T(8,128)(2,1)S(1)} %get-tuple-element.35), channel_id=1, source_target_pairs={{0,2},{1,3},{2,0},{3,1},{4,6},{5,7},{6,4},{7,5},{8,10},{9,11},{10,... | collective-permute-start | bytes 236744 | tf_op jit(solution)/shard_map/ppermute | solution.py:514
  62.5 5.9 %collective-permute-start.21 = (bf16[96,411]{1,0:T(8,128)(2,1)S(1)}, bf16[96,411]{1,0:T(8,128)(2,1)S(1)}, u32[]{:S(2)}, u32[]{:S(2)}) collective-permute-start(bf16[96,411]{1,0:T(8,128)(2,1)S(1)} %get-tuple-element.36), channel_id=1, source_target_pairs={{0,4},{1,5},{2,6},{3,7},{4,0},{5,1},{6,2},{7,3},{8,12},{9,13},{10,... | collective-permute-start | bytes 236744 | tf_op jit(solution)/shard_map/ppermute | solution.py:514
  64.2 5.7 %collective-permute-start.22 = (bf16[96,411]{1,0:T(8,128)(2,1)S(1)}, bf16[96,411]{1,0:T(8,128)(2,1)S(1)}, u32[]{:S(2)}, u32[]{:S(2)}) collective-permute-start(bf16[96,411]{1,0:T(8,128)(2,1)S(1)} %get-tuple-element.37), channel_id=1, source_target_pairs={{0,6},{1,7},{2,4},{3,5},{4,2},{5,3},{6,0},{7,1},{8,14},{9,15},{10,... | collective-permute-start | bytes 236744 | tf_op jit(solution)/shard_map/ppermute | solution.py:514
  70.2 5.8 %collective-permute-start.23 = (bf16[32,411]{1,0:T(8,128)(2,1)S(1)}, bf16[32,411]{1,0:T(8,128)(2,1)S(1)}, u32[]{:S(2)}, u32[]{:S(2)}) collective-permute-start(bf16[32,411]{1,0:T(8,128)(2,1)S(1)} %get-tuple-element.39), channel_id=1, source_target_pairs={{0,8},{8,16},{16,24},{24,0},{1,9},{9,17},{17,25},{25,1},{2,10},{10... | collective-permute-start | bytes 78920 | tf_op jit(solution)/shard_map/ppermute | solution.py:517
  71.4 5.3 %collective-permute-start.24 = (bf16[32,411]{1,0:T(8,128)(2,1)S(1)}, bf16[32,411]{1,0:T(8,128)(2,1)S(1)}, u32[]{:S(2)}, u32[]{:S(2)}) collective-permute-start(bf16[32,411]{1,0:T(8,128)(2,1)S(1)} %get-tuple-element.40), channel_id=1, source_target_pairs={{0,16},{8,24},{16,0},{24,8},{1,17},{9,25},{17,1},{25,9},{2,18},{10... | collective-permute-start | bytes 78920 | tf_op jit(solution)/shard_map/ppermute | solution.py:517
  72.8 4.0 %collective-permute-start.25 = (bf16[32,411]{1,0:T(8,128)(2,1)S(1)}, bf16[32,411]{1,0:T(8,128)(2,1)S(1)}, u32[]{:S(2)}, u32[]{:S(2)}) collective-permute-start(bf16[32,411]{1,0:T(8,128)(2,1)S(1)} %get-tuple-element.41), channel_id=1, source_target_pairs={{0,24},{8,0},{16,8},{24,16},{1,25},{9,1},{17,9},{25,17},{2,26},{10... | collective-permute-start | bytes 78920 | tf_op jit(solution)/shard_map/ppermute | solution.py:517

commit v6 on v5

--- a/solution.py
+++ b/solution.py
@@ -9,7 +9,7 @@
 
 VMEM_BYTES = 24 * 1024 * 1024
 WHOLE_VMEM_BYTES = 63 * 1024 * 1024
-SLACK_FLOPS = 10**9
+SLACK_FLOPS = 2 * 10**9
 NT_DIMS = (((1,), (1,)), ((), ()))
 
 
@@ -253,11 +253,11 @@
 
 def place_kernel(p, owners_ref, place_ref, source_ref, cell_ref, *target_refs):
     t, c = lax.axis_index("tile"), lax.axis_index("chan")
-    owner = owners_ref[...]
+    across = owners_ref[...]
     shape = (p.rows, p.rows)
     row = lax.broadcasted_iota(jnp.int32, shape, 0)
     other = lax.broadcasted_iota(jnp.int32, shape, 1)
-    across = jnp.sum(jnp.where(row == other, owner, 0), axis=0, keepdims=True)
+    owner = jnp.sum(jnp.where(row == other, across, 0), axis=1, keepdims=True)
     first = lax.broadcasted_iota(jnp.int32, owner.shape, 0)
     begin = first // p.tile_cols * p.tile_cols
     same = (owner == across) & (other >= begin) & (other < row)
@@ -595,7 +595,7 @@
         [shape((p.rows, 1), jnp.int32)] * 2
         + [shape((3 * reach, 1), jnp.int32)]
         + [shape((p.chips * p.patch, 1), jnp.int32)] * p.group,
-        [owners],
+        [owners.reshape(1, p.rows)],
         flops=SLACK_FLOPS,
     )
     *parts, slope, kappa = call(

time: 78.4 us -> 73.2 us (0.934)
  Pallas kernels: 17.7 us -> 12.3 us
  local copies, waits for them, and re-layouts: 6.05 us -> 2.75 us
  starting transfers between devices: 27.3 us -> 29.2 us
  waiting for transfers between devices: 26.7 us -> 28.4 us
    pallas_call x13, Pallas kernels: 17.7 us -> 12.3 us  [call(): pl.pallas_call(kernel, out_shape=out_shape, in_specs=[far if k in in_hbm...]
    unnamed x21 -> x14, local copies, waits for them, and re-layouts: 5.89 us -> 2.6 us
    ppermute x3, waiting for transfers between devices: 3.94 us -> 5.08 us  [trade(): return lax.ppermute(value, 'tile', [(a, a ^ mask) for a in range(p.tiles)])]
    ppermute x7, starting transfers between devices: 4.51 us -> 5.41 us  [send(): lax.ppermute(value, both, sorted(((number(a), number(b)) for a, b in pair...]
  transfers between devices with their start and end apart: 26 -> 26, of which waited for: 15 -> 16; matrix products, arithmetic and copies ran while one was open for 1% -> 0% of each run, Pallas kernels for 5% -> 5%
where the time goes in v6:
time: 73.2 us; the launch traced here: 72.9 us
  starting transfers between devices  29.2 us (40%)
  waiting for transfers between devices  28.4 us (39%)
  Pallas kernels  12.3 us (17%)
  local copies, waits for them, and re-layouts  2.75 us (4%)
    ppermute x13, starting transfers between devices, flip(): return lax.ppermute(value, 'chan', [(b, b ^ mask) for b in range(p.chans)])  13.9 us
    pallas_call x13, Pallas kernels, call(): pl.pallas_call(kernel, out_shape=out_shape, in_specs=[far if k in in_hbm...  12.3 us
    ppermute x13, waiting for transfers between devices, flip(): return lax.ppermute(value, 'chan', [(b, b ^ mask) for b in range(p.chans)])  11.7 us
    ppermute x7, waiting for transfers between devices, send(): lax.ppermute(value, both, sorted(((number(a), number(b)) for a, b in pair...  9.91 us
    ppermute x7, starting transfers between devices, send(): lax.ppermute(value, both, sorted(((number(a), number(b)) for a, b in pair...  5.41 us
    ppermute x3, starting transfers between devices, shift(): lax.ppermute(value, 'tile', [(a, (a + by) % p.tiles) for a in range(p.til...  5.15 us
    ppermute x3, waiting for transfers between devices, trade(): return lax.ppermute(value, 'tile', [(a, a ^ mask) for a in range(p.tiles)])  5.08 us
    ppermute x3, starting transfers between devices, trade(): return lax.ppermute(value, 'tile', [(a, a ^ mask) for a in range(p.tiles)])  4.75 us
  transfers between devices with their start and end apart: 26, of which 16 were waited for; matrix products, arithmetic and copies ran while one was open for 0% of the time, Pallas kernels for 5%

profile of v6, /device:TPU:0, one launch (start us, length us, event | category | flops | bytes accessed | tf_op | source)
XLA Modules:
  0.0 72.9 jit_solution(10659754615994121141)
XLA Ops:
  0.0 3.0 %collective-permute-start.8 = (bf16[411,256]{1,0:T(8,128)(2,1)}, bf16[411,256]{1,0:T(8,128)(2,1)S(1)}, u32[]{:S(2)}, u32[]{:S(2)}) collective-permute-start(bf16[411,256]{1,0:T(8,128)(2,1)} %refs_0_.6), channel_id=1, source_target_pairs={{0,4},{1,5},{2,6},{3,7},{4,0},{5,1},{6,2},{7,3},{8,12},{9,13},{10,... | collective-permute-start | bytes 631304 | tf_op jit(solution)/shard_map/ppermute | solution.py:514
  3.0 1.5 %collective-permute-start.7 = (bf16[411,256]{1,0:T(8,128)(2,1)}, bf16[411,256]{1,0:T(8,128)(2,1)S(1)}, u32[]{:S(2)}, u32[]{:S(2)}) collective-permute-start(bf16[411,256]{1,0:T(8,128)(2,1)} %refs_0_.6), channel_id=1, source_target_pairs={{0,2},{1,3},{2,0},{3,1},{4,6},{5,7},{6,4},{7,5},{8,10},{9,11},{10,... | collective-permute-start | bytes 631304 | tf_op jit(solution)/shard_map/ppermute | solution.py:514
  4.5 0.0 collective-permute-start.9
  4.5 2.0 %collective-permute-start.2 = (bf16[128,768]{1,0:T(8,128)(2,1)}, bf16[128,768]{1,0:T(8,128)(2,1)S(1)}, u32[]{:S(2)}, u32[]{:S(2)}) collective-permute-start(bf16[128,768]{1,0:T(8,128)(2,1)} %refs_0_.5), channel_id=1, source_target_pairs={{0,8},{8,0},{16,24},{24,16},{1,9},{9,1},{17,25},{25,17},{2,10},{10... | collective-permute-start | bytes 589832 | tf_op jit(solution)/shard_map/ppermute | solution.py:545
  6.5 1.8 %shard_map.101.refs_0_ = bf16[16,512]{1,0:T(8,128)(2,1)} custom-call(f32[4,32,411]{2,1,0:T(8,128)} %refs_0_.4, f32[4,32]{1,0:T(4,128)} %refs_1_.2, s32[128]{0:T(128)} %refs_2_.1, f32[256]{0:T(256)} %refs_3_.2), custom_call_target="tpu_custom_call" | custom-call | bytes 212480 | tf_op jit(solution)/shard_map/pallas_call | solution.py:164
  8.3 0.1 collective-permute-start
  8.4 3.9 %collective-permute-done.refs_1_ = bf16[16,512]{1,0:T(8,128)(2,1)S(1)} collective-permute-done((bf16[16,512]{1,0:T(8,128)(2,1)}, bf16[16,512]{1,0:T(8,128)(2,1)S(1)}, u32[]{:S(2)}, u32[]{:S(2)}) %collective-permute-start) | collective-permute-done | bytes 16416 | tf_op jit(solution)/shard_map/ppermute | solution.py:545
  12.3 0.7 copy-done.4
  13.1 2.7 %collective-permute-start.1 = (bf16[32,512]{1,0:T(8,128)(2,1)S(1)}, bf16[32,512]{1,0:T(8,128)(2,1)S(1)}, u32[]{:S(2)}, u32[]{:S(2)}) collective-permute-start(bf16[32,512]{1,0:T(8,128)(2,1)S(1)} %shard_map.102.refs_0_), channel_id=1, source_target_pairs={{0,16},{8,24},{16,0},{24,8},{1,17},{9,25},{17,1},{25,9},{2,18},{10... | collective-permute-start | bytes 98312 | tf_op jit(solution)/shard_map/ppermute | solution.py:545
  15.7 0.9 %copy-done.3 = bf16[128,768]{1,0:T(8,128)(2,1)S(1)} copy-done((bf16[128,768]{1,0:T(8,128)(2,1)S(1)}, bf16[128,768]{1,0:T(8,128)(2,1)}, u32[]{:S(2)}) %copy-start.3) | copy-done | bytes 196632
  16.7 0.5 shard_map.103.refs_2_.refs_9_
  17.2 1.1 %collective-permute-done.1.refs_1_ = bf16[32,512]{1,0:T(8,128)(2,1)S(1)} collective-permute-done((bf16[32,512]{1,0:T(8,128)(2,1)S(1)}, bf16[32,512]{1,0:T(8,128)(2,1)S(1)}, u32[]{:S(2)}, u32[]{:S(2)}) %collective-permute-start.1) | collective-permute-done | bytes 32800 | tf_op jit(solution)/shard_map/ppermute | solution.py:545
  18.3 0.1 shard_map.104.refs_0_.refs_4_
  18.4 0.0 copy-start.2
  18.4 0.9 %copy-done.2 = bf16[411,256]{1,0:T(8,128)(2,1)S(1)} copy-done((bf16[411,256]{1,0:T(8,128)(2,1)S(1)}, bf16[411,256]{1,0:T(8,128)(2,1)}, u32[]{:S(2)}) %copy-start.2) | copy-done | bytes 210456
  19.4 0.1 shard_map.106.refs_7_.refs_5_
  19.4 0.1 collective-permute-start.10
  19.5 2.3 %collective-permute-start.11 = (bf16[256,768]{1,0:T(8,128)(2,1)S(1)}, bf16[256,768]{1,0:T(8,128)(2,1)S(1)}, u32[]{:S(2)}, u32[]{:S(2)}) collective-permute-start(bf16[256,768]{1,0:T(8,128)(2,1)S(1)} %shard_map.103.refs_2_.refs_9_), channel_id=1, source_target_pairs={{0,16},{1,17},{2,3},{3,2},{4,20},{5,21},{6,7},{7,6},{8,9},{9,8},{1... | collective-permute-start | bytes 1179656 | tf_op jit(solution)/shard_map/ppermute | solution.py:526
  21.8 0.6 collective-permute-start.5
  22.4 0.9 %collective-permute-start.4 = (bf16[64,512]{1,0:T(8,128)(2,1)S(1)}, bf16[64,512]{1,0:T(8,128)(2,1)S(1)}, u32[]{:S(2)}, u32[]{:S(2)}) collective-permute-start(bf16[64,512]{1,0:T(8,128)(2,1)S(1)} %shard_map.104.refs_0_.refs_4_), channel_id=1, source_target_pairs={{0,4},{1,5},{2,6},{3,7},{4,0},{5,1},{6,2},{7,3},{8,12},{9,13},{10,... | collective-permute-start | bytes 196616 | tf_op jit(solution)/shard_map/ppermute | solution.py:514
  23.3 2.0 %collective-permute-start.3 = (bf16[64,512]{1,0:T(8,128)(2,1)S(1)}, bf16[64,512]{1,0:T(8,128)(2,1)S(1)}, u32[]{:S(2)}, u32[]{:S(2)}) collective-permute-start(bf16[64,512]{1,0:T(8,128)(2,1)S(1)} %shard_map.104.refs_0_.refs_4_), channel_id=1, source_target_pairs={{0,2},{1,3},{2,0},{3,1},{4,6},{5,7},{6,4},{7,5},{8,10},{9,11},{10,... | collective-permute-start | bytes 196616 | tf_op jit(solution)/shard_map/ppermute | solution.py:514
  25.3 2.0 %collective-permute-done.5.refs_3_ = bf16[64,512]{1,0:T(8,128)(2,1)S(1)} collective-permute-done((bf16[64,512]{1,0:T(8,128)(2,1)S(1)}, bf16[64,512]{1,0:T(8,128)(2,1)S(1)}, u32[]{:S(2)}, u32[]{:S(2)}) %collective-permute-start.5) | collective-permute-done | bytes 65568 | tf_op jit(solution)/shard_map/ppermute | solution.py:514
  27.3 0.3 collective-permute-done.4.refs_2_
  27.6 0.7 collective-permute-done.3.refs_1_
  28.3 0.3 shard_map.105.refs_5_
  28.7 0.1 collective-permute-start.6
  28.8 0.0 copy-start
  28.8 0.0 copy-start.5
  28.8 0.9 %shard_map.100 = (s32[256,1]{1,0:T(8,128)S(1)}, s32[256,1]{1,0:T(8,128)S(1)}, s32[24,1]{1,0:T(8,128)S(1)}, s32[384,1]{1,0:T(8,128)S(1)}, s32[384,1]{1,0:T(8,128)S(1)}) custom-call(s32[1,256]{1,0:T(1,128)S(1)} %bitcast.12), custom_call_target="tpu_custom_call" | custom-call | flops 2000000000 | bytes 1024 | tf_op jit(solution)/shard_map/pallas_call | solution.py:164
  29.8 0.5 collective-permute-done.6.refs_6_
  30.3 1.6 %collective-permute-done.11.refs_10_ = bf16[256,768]{1,0:T(8,128)(2,1)S(1)} collective-permute-done((bf16[256,768]{1,0:T(8,128)(2,1)S(1)}, bf16[256,768]{1,0:T(8,128)(2,1)S(1)}, u32[]{:S(2)}, u32[]{:S(2)}) %collective-permute-start.11) | collective-permute-done | bytes 393248 | tf_op jit(solution)/shard_map/ppermute | solution.py:526
  31.9 0.0 copy-start.1
  32.0 2.4 %shard_map.107 = (bf16[128,768]{1,0:T(8,128)(2,1)S(1)}, bf16[128,768]{1,0:T(8,128)(2,1)S(1)}, f32[8,256,256]{2,1,0:T(8,128)S(1)}, f32[24,128]{1,0:T(8,128)S(1)}) custom-call(s32[256,1]{1,0:T(8,128)S(1)} %get-tuple-element.24.refs_0_, s32[256,1]{1,0:T(8,128)S(1)} %get-tuple-element.25.refs_1_, s32[24,1]{1,0:T(8,128)S(1)} %get-tuple-element.26.refs_2_, ...), custom_call_target="tpu_custom_call" | custom-call | flops 1236271104 | bytes 6165600 | tf_op jit(solution)/shard_map/pallas_call | solution.py:164
  34.3 0.1 collective-permute-start.12
  34.4 1.6 %collective-permute-start.13 = (bf16[128,768]{1,0:T(8,128)(2,1)S(1)}, bf16[128,768]{1,0:T(8,128)(2,1)S(1)}, u32[]{:S(2)}, u32[]{:S(2)}) collective-permute-start(bf16[128,768]{1,0:T(8,128)(2,1)S(1)} %get-tuple-element.29.refs_1_), channel_id=1, source_target_pairs={{0,4},{1,5},{2,3},{3,2},{4,0},{5,1},{6,7},{7,6},{8,9},{9,8},{10,14... | collective-permute-start | bytes 589832 | tf_op jit(solution)/shard_map/ppermute | solution.py:526
  36.0 0.5 collective-permute-start.14
  36.5 0.4 collective-permute-start.15
  36.9 5.3 %collective-permute-done.12.refs_2_ = bf16[128,768]{1,0:T(8,128)(2,1)S(1)} collective-permute-done((bf16[128,768]{1,0:T(8,128)(2,1)S(1)}, bf16[128,768]{1,0:T(8,128)(2,1)S(1)}, u32[]{:S(2)}, u32[]{:S(2)}) %collective-permute-start.12) | collective-permute-done | bytes 196640 | tf_op jit(solution)/shard_map/ppermute | solution.py:526
  42.2 0.5 collective-permute-start.17
  42.7 3.0 %collective-permute-done.14.refs_4_ = bf16[128,768]{1,0:T(8,128)(2,1)S(1)} collective-permute-done((bf16[128,768]{1,0:T(8,128)(2,1)S(1)}, bf16[128,768]{1,0:T(8,128)(2,1)S(1)}, u32[]{:S(2)}, u32[]{:S(2)}) %collective-permute-start.14) | collective-permute-done | bytes 196640 | tf_op jit(solution)/shard_map/ppermute | solution.py:526
  45.7 0.6 shard_map.108.refs_3_
  46.3 0.1 collective-permute-start.18
  46.4 1.7 %collective-permute-done.18.refs_4_ = bf16[256,768]{1,0:T(8,128)(2,1)S(1)} collective-permute-done((bf16[256,768]{1,0:T(8,128)(2,1)S(1)}, bf16[256,768]{1,0:T(8,128)(2,1)S(1)}, u32[]{:S(2)}, u32[]{:S(2)}) %collective-permute-start.18) | collective-permute-done | bytes 393248 | tf_op jit(solution)/shard_map/ppermute | solution.py:514
  48.1 3.9 %shard_map.109 = (bf16[384,411]{1,0:T(8,128)(2,1)S(1)}, bf16[384,411]{1,0:T(8,128)(2,1)S(1)}) custom-call(bf16[2048,768]{1,0:T(8,128)(2,1)S(1)} %copy-done, bf16[1536,768]{1,0:T(8,128)(2,1)S(1)} %copy-done.1, f32[8,256,256]{2,1,0:T(8,128)S(1)} %get-tuple-element.27.refs_2_, bf16[256,768]{1,0:T(8,128)(2,1)S(1)} %shard_map.108.refs_3_, ...), custom_call_target="tpu_custom_call" | custom-call | flops 1840250880 | bytes 10095616 | tf_op jit(solution)/shard_map/pallas_call | solution.py:164
  52.0 0.2 collective-permute-start.19
  52.2 0.1 slice_bitcast_fusion.2
  52.3 1.5 %collective-permute-done.19.refs_1_ = bf16[384,411]{1,0:T(8,128)(2,1)S(1)} collective-permute-done((bf16[384,411]{1,0:T(8,128)(2,1)S(1)}, bf16[384,411]{1,0:T(8,128)(2,1)S(1)}, u32[]{:S(2)}, u32[]{:S(2)}) %collective-permute-start.19) | collective-permute-done | bytes 315680 | tf_op jit(solution)/shard_map/ppermute | solution.py:514
  53.8 0.1 shard_map.110
  53.9 2.4 %collective-permute-start.20 = (bf16[96,411]{1,0:T(8,128)(2,1)S(1)}, bf16[96,411]{1,0:T(8,128)(2,1)S(1)}, u32[]{:S(2)}, u32[]{:S(2)}) collective-permute-start(bf16[96,411]{1,0:T(8,128)(2,1)S(1)} %get-tuple-element.35), channel_id=1, source_target_pairs={{0,2},{1,3},{2,0},{3,1},{4,6},{5,7},{6,4},{7,5},{8,10},{9,11},{10,... | collective-permute-start | bytes 236744 | tf_op jit(solution)/shard_map/ppermute | solution.py:514
  56.3 1.9 %collective-permute-start.21 = (bf16[96,411]{1,0:T(8,128)(2,1)S(1)}, bf16[96,411]{1,0:T(8,128)(2,1)S(1)}, u32[]{:S(2)}, u32[]{:S(2)}) collective-permute-start(bf16[96,411]{1,0:T(8,128)(2,1)S(1)} %get-tuple-element.36), channel_id=1, source_target_pairs={{0,4},{1,5},{2,6},{3,7},{4,0},{5,1},{6,2},{7,3},{8,12},{9,13},{10,... | collective-permute-start | bytes 236744 | tf_op jit(solution)/shard_map/ppermute | solution.py:514
  58.2 1.2 %collective-permute-start.22 = (bf16[96,411]{1,0:T(8,128)(2,1)S(1)}, bf16[96,411]{1,0:T(8,128)(2,1)S(1)}, u32[]{:S(2)}, u32[]{:S(2)}) collective-permute-start(bf16[96,411]{1,0:T(8,128)(2,1)S(1)} %get-tuple-element.37), channel_id=1, source_target_pairs={{0,6},{1,7},{2,4},{3,5},{4,2},{5,3},{6,0},{7,1},{8,14},{9,15},{10,... | collective-permute-start | bytes 236744 | tf_op jit(solution)/shard_map/ppermute | solution.py:514
  59.4 0.0 collective-permute-done.20.refs_1_
  59.4 3.1 %collective-permute-done.21.refs_2_ = bf16[96,411]{1,0:T(8,128)(2,1)S(1)} collective-permute-done((bf16[96,411]{1,0:T(8,128)(2,1)S(1)}, bf16[96,411]{1,0:T(8,128)(2,1)S(1)}, u32[]{:S(2)}, u32[]{:S(2)}) %collective-permute-start.21) | collective-permute-done | bytes 78944 | tf_op jit(solution)/shard_map/ppermute | solution.py:514
  62.4 1.8 %collective-permute-done.22.refs_3_ = bf16[96,411]{1,0:T(8,128)(2,1)S(1)} collective-permute-done((bf16[96,411]{1,0:T(8,128)(2,1)S(1)}, bf16[96,411]{1,0:T(8,128)(2,1)S(1)}, u32[]{:S(2)}, u32[]{:S(2)}) %collective-permute-start.22) | collective-permute-done | bytes 78944 | tf_op jit(solution)/shard_map/ppermute | solution.py:514
  64.3 0.2 shard_map.111
  64.5 0.9 %collective-permute-start.23 = (bf16[32,411]{1,0:T(8,128)(2,1)S(1)}, bf16[32,411]{1,0:T(8,128)(2,1)S(1)}, u32[]{:S(2)}, u32[]{:S(2)}) collective-permute-start(bf16[32,411]{1,0:T(8,128)(2,1)S(1)} %get-tuple-element.39), channel_id=1, source_target_pairs={{0,8},{8,16},{16,24},{24,0},{1,9},{9,17},{17,25},{25,1},{2,10},{10... | collective-permute-start | bytes 78920 | tf_op jit(solution)/shard_map/ppermute | solution.py:517
  65.5 2.2 %collective-permute-start.24 = (bf16[32,411]{1,0:T(8,128)(2,1)S(1)}, bf16[32,411]{1,0:T(8,128)(2,1)S(1)}, u32[]{:S(2)}, u32[]{:S(2)}) collective-permute-start(bf16[32,411]{1,0:T(8,128)(2,1)S(1)} %get-tuple-element.40), channel_id=1, source_target_pairs={{0,16},{8,24},{16,0},{24,8},{1,17},{9,25},{17,1},{25,9},{2,18},{10... | collective-permute-start | bytes 78920 | tf_op jit(solution)/shard_map/ppermute | solution.py:517
  67.6 2.0 %collective-permute-start.25 = (bf16[32,411]{1,0:T(8,128)(2,1)S(1)}, bf16[32,411]{1,0:T(8,128)(2,1)S(1)}, u32[]{:S(2)}, u32[]{:S(2)}) collective-permute-start(bf16[32,411]{1,0:T(8,128)(2,1)S(1)} %get-tuple-element.41), channel_id=1, source_target_pairs={{0,24},{8,0},{16,8},{24,16},{1,25},{9,1},{17,9},{25,17},{2,26},{10... | collective-permute-start | bytes 78920 | tf_op jit(solution)/shard_map/ppermute | solution.py:517
  69.7 0.1 maximum_sqrt_fusion
  69.8 0.1 copy.19
  69.8 0.5 collective-permute-done.23.refs_1_
  70.4 0.4 collective-permute-done.24.refs_2_
  70.8 0.8 %collective-permute-done.25.refs_3_ = bf16[32,411]{1,0:T(8,128)(2,1)S(1)} collective-permute-done((bf16[32,411]{1,0:T(8,128)(2,1)S(1)}, bf16[32,411]{1,0:T(8,128)(2,1)S(1)}, u32[]{:S(2)}, u32[]{:S(2)}) %collective-permute-start.25) | collective-permute-done | bytes 26336 | tf_op jit(solution)/shard_map/ppermute | solution.py:517
  71.6 1.4 %shard_map.112 = f32[4,32,411]{2,1,0:T(8,128)} custom-call(bf16[32,411]{1,0:T(8,128)(2,1)S(1)} %get-tuple-element.38.refs_0_, bf16[32,411]{1,0:T(8,128)(2,1)S(1)} %collective-permute-done.23.refs_1_, bf16[32,411]{1,0:T(8,128)(2,1)S(1)} %collective-permute-done.24.refs_2_, bf16[32,411]{1,0:T(8,128)(2,1)S(1)} %collective-permute-done.25.refs_3_, ...), custom_call_target="tpu_custom_call" | custom-call | flops 5260800 | bytes 106752 | tf_op jit(solution)/shard_map/pallas_call | solution.py:164
  (19 shorter events, 0.1 us)
Async XLA Ops:
  0.0 28.8 %copy-start.6 = (s32[256,1]{0,1:T(1,128)S(1)}, s32[256,1]{0,1:T(1,128)}, u32[]{:S(2)}) copy-start(s32[256,1]{0,1:T(1,128)} %param.12) | copy-start | bytes 3076
  0.0 18.4 %collective-permute-start.8 = (bf16[411,256]{1,0:T(8,128)(2,1)}, bf16[411,256]{1,0:T(8,128)(2,1)S(1)}, u32[]{:S(2)}, u32[]{:S(2)}) collective-permute-start(bf16[411,256]{1,0:T(8,128)(2,1)} %refs_0_.6), channel_id=1, source_target_pairs={{0,4},{1,5},{2,6},{3,7},{4,0},{5,1},{6,2},{7,3},{8,12},{9,13},{10,... | collective-permute-start | bytes 631304 | tf_op jit(solution)/shard_map/ppermute | solution.py:514
  3.0 15.4 %collective-permute-start.7 = (bf16[411,256]{1,0:T(8,128)(2,1)}, bf16[411,256]{1,0:T(8,128)(2,1)S(1)}, u32[]{:S(2)}, u32[]{:S(2)}) collective-permute-start(bf16[411,256]{1,0:T(8,128)(2,1)} %refs_0_.6), channel_id=1, source_target_pairs={{0,2},{1,3},{2,0},{3,1},{4,6},{5,7},{6,4},{7,5},{8,10},{9,11},{10,... | collective-permute-start | bytes 631304 | tf_op jit(solution)/shard_map/ppermute | solution.py:514
  4.5 14.0 %collective-permute-start.9 = (bf16[411,256]{1,0:T(8,128)(2,1)}, bf16[411,256]{1,0:T(8,128)(2,1)S(1)}, u32[]{:S(2)}, u32[]{:S(2)}) collective-permute-start(bf16[411,256]{1,0:T(8,128)(2,1)} %refs_0_.6), channel_id=1, source_target_pairs={{0,6},{1,7},{2,4},{3,5},{4,2},{5,3},{6,0},{7,1},{8,14},{9,15},{10,... | collective-permute-start | bytes 631304 | tf_op jit(solution)/shard_map/ppermute | solution.py:514
  4.5 11.2 %collective-permute-start.2 = (bf16[128,768]{1,0:T(8,128)(2,1)}, bf16[128,768]{1,0:T(8,128)(2,1)S(1)}, u32[]{:S(2)}, u32[]{:S(2)}) collective-permute-start(bf16[128,768]{1,0:T(8,128)(2,1)} %refs_0_.5), channel_id=1, source_target_pairs={{0,8},{8,0},{16,24},{24,16},{1,9},{9,1},{17,25},{25,17},{2,10},{10... | collective-permute-start | bytes 589832 | tf_op jit(solution)/shard_map/ppermute | solution.py:545
  8.3 4.0 %collective-permute-start = (bf16[16,512]{1,0:T(8,128)(2,1)}, bf16[16,512]{1,0:T(8,128)(2,1)S(1)}, u32[]{:S(2)}, u32[]{:S(2)}) collective-permute-start(bf16[16,512]{1,0:T(8,128)(2,1)} %shard_map.101.refs_0_), channel_id=1, source_target_pairs={{0,8},{8,0},{16,24},{24,16},{1,9},{9,1},{17,25},{25,17},{2,10},{10... | collective-permute-start | bytes 49160 | tf_op jit(solution)/shard_map/ppermute | solution.py:545
  12.3 0.7 copy-start.4
  13.1 5.2 %collective-permute-start.1 = (bf16[32,512]{1,0:T(8,128)(2,1)S(1)}, bf16[32,512]{1,0:T(8,128)(2,1)S(1)}, u32[]{:S(2)}, u32[]{:S(2)}) collective-permute-start(bf16[32,512]{1,0:T(8,128)(2,1)S(1)} %shard_map.102.refs_0_), channel_id=1, source_target_pairs={{0,16},{8,24},{16,0},{24,8},{1,17},{9,25},{17,1},{25,9},{2,18},{10... | collective-permute-start | bytes 98312 | tf_op jit(solution)/shard_map/ppermute | solution.py:545
  15.7 0.9 %copy-start.3 = (bf16[128,768]{1,0:T(8,128)(2,1)S(1)}, bf16[128,768]{1,0:T(8,128)(2,1)}, u32[]{:S(2)}) copy-start(bf16[128,768]{1,0:T(8,128)(2,1)} %refs_0_.5) | copy-start | bytes 589828
  18.4 0.9 %copy-start.2 = (bf16[411,256]{1,0:T(8,128)(2,1)S(1)}, bf16[411,256]{1,0:T(8,128)(2,1)}, u32[]{:S(2)}) copy-start(bf16[411,256]{1,0:T(8,128)(2,1)} %refs_0_.6) | copy-start | bytes 631300
  19.4 12.5 %collective-permute-start.10 = (bf16[1664,256]{1,0:T(8,128)(2,1)S(1)}, bf16[1664,256]{1,0:T(8,128)(2,1)S(1)}, u32[]{:S(2)}, u32[]{:S(2)}) collective-permute-start(bf16[1664,256]{1,0:T(8,128)(2,1)S(1)} %shard_map.106.refs_7_.refs_5_), channel_id=1, source_target_pairs={{0,1},{1,0},{2,3},{3,2},{4,5},{5,4},{6,7},{7,6},{8,9},{9,8},{10,11... | collective-permute-start | bytes 2555912 | tf_op jit(solution)/shard_map/ppermute | solution.py:514
  19.5 12.4 %collective-permute-start.11 = (bf16[256,768]{1,0:T(8,128)(2,1)S(1)}, bf16[256,768]{1,0:T(8,128)(2,1)S(1)}, u32[]{:S(2)}, u32[]{:S(2)}) collective-permute-start(bf16[256,768]{1,0:T(8,128)(2,1)S(1)} %shard_map.103.refs_2_.refs_9_), channel_id=1, source_target_pairs={{0,16},{1,17},{2,3},{3,2},{4,20},{5,21},{6,7},{7,6},{8,9},{9,8},{1... | collective-permute-start | bytes 1179656 | tf_op jit(solution)/shard_map/ppermute | solution.py:526
  21.8 5.5 %collective-permute-start.5 = (bf16[64,512]{1,0:T(8,128)(2,1)S(1)}, bf16[64,512]{1,0:T(8,128)(2,1)S(1)}, u32[]{:S(2)}, u32[]{:S(2)}) collective-permute-start(bf16[64,512]{1,0:T(8,128)(2,1)S(1)} %shard_map.104.refs_0_.refs_4_), channel_id=1, source_target_pairs={{0,6},{1,7},{2,4},{3,5},{4,2},{5,3},{6,0},{7,1},{8,14},{9,15},{10,... | collective-permute-start | bytes 196616 | tf_op jit(solution)/shard_map/ppermute | solution.py:514
  22.4 5.2 %collective-permute-start.4 = (bf16[64,512]{1,0:T(8,128)(2,1)S(1)}, bf16[64,512]{1,0:T(8,128)(2,1)S(1)}, u32[]{:S(2)}, u32[]{:S(2)}) collective-permute-start(bf16[64,512]{1,0:T(8,128)(2,1)S(1)} %shard_map.104.refs_0_.refs_4_), channel_id=1, source_target_pairs={{0,4},{1,5},{2,6},{3,7},{4,0},{5,1},{6,2},{7,3},{8,12},{9,13},{10,... | collective-permute-start | bytes 196616 | tf_op jit(solution)/shard_map/ppermute | solution.py:514
  23.3 5.0 %collective-permute-start.3 = (bf16[64,512]{1,0:T(8,128)(2,1)S(1)}, bf16[64,512]{1,0:T(8,128)(2,1)S(1)}, u32[]{:S(2)}, u32[]{:S(2)}) collective-permute-start(bf16[64,512]{1,0:T(8,128)(2,1)S(1)} %shard_map.104.refs_0_.refs_4_), channel_id=1, source_target_pairs={{0,2},{1,3},{2,0},{3,1},{4,6},{5,7},{6,4},{7,5},{8,10},{9,11},{10,... | collective-permute-start | bytes 196616 | tf_op jit(solution)/shard_map/ppermute | solution.py:514
  28.7 1.6 %collective-permute-start.6 = (bf16[256,512]{1,0:T(8,128)(2,1)S(1)}, bf16[256,512]{1,0:T(8,128)(2,1)S(1)}, u32[]{:S(2)}, u32[]{:S(2)}) collective-permute-start(bf16[256,512]{1,0:T(8,128)(2,1)S(1)} %shard_map.105.refs_5_), channel_id=1, source_target_pairs={{0,1},{1,0},{2,3},{3,2},{4,5},{5,4},{6,7},{7,6},{8,9},{9,8},{10,11... | collective-permute-start | bytes 786440 | tf_op jit(solution)/shard_map/ppermute | solution.py:514
  28.8 3.2 %copy-start = (bf16[2048,768]{1,0:T(8,128)(2,1)S(1)}, bf16[2048,768]{1,0:T(8,128)(2,1)}, u32[]{:S(2)}) copy-start(bf16[2048,768]{1,0:T(8,128)(2,1)} %refs_0_.7) | copy-start | bytes 9437188
  28.8 3.2 %copy-start.5 = (f32[768]{0:T(1024)S(1)}, f32[768]{0:T(1024)}, u32[]{:S(2)}) copy-start(f32[768]{0:T(1024)} %refs_3_.3) | copy-start | bytes 9220
  31.9 16.1 %copy-start.1 = (bf16[1536,768]{1,0:T(8,128)(2,1)S(1)}, bf16[1536,768]{1,0:T(8,128)(2,1)}, u32[]{:S(2)}) copy-start(bf16[1536,768]{1,0:T(8,128)(2,1)} %refs_1_.3) | copy-start | bytes 7077892
  34.3 7.9 %collective-permute-start.12 = (bf16[128,768]{1,0:T(8,128)(2,1)S(1)}, bf16[128,768]{1,0:T(8,128)(2,1)S(1)}, u32[]{:S(2)}, u32[]{:S(2)}) collective-permute-start(bf16[128,768]{1,0:T(8,128)(2,1)S(1)} %get-tuple-element.28.refs_0_), channel_id=1, source_target_pairs={{0,2},{1,3},{2,0},{3,1},{4,5},{5,4},{6,7},{7,6},{8,10},{9,11},{10,... | collective-permute-start | bytes 589832 | tf_op jit(solution)/shard_map/ppermute | solution.py:526
  34.4 7.8 %collective-permute-start.13 = (bf16[128,768]{1,0:T(8,128)(2,1)S(1)}, bf16[128,768]{1,0:T(8,128)(2,1)S(1)}, u32[]{:S(2)}, u32[]{:S(2)}) collective-permute-start(bf16[128,768]{1,0:T(8,128)(2,1)S(1)} %get-tuple-element.29.refs_1_), channel_id=1, source_target_pairs={{0,4},{1,5},{2,3},{3,2},{4,0},{5,1},{6,7},{7,6},{8,9},{9,8},{10,14... | collective-permute-start | bytes 589832 | tf_op jit(solution)/shard_map/ppermute | solution.py:526
  36.0 9.7 %collective-permute-start.14 = (bf16[128,768]{1,0:T(8,128)(2,1)S(1)}, bf16[128,768]{1,0:T(8,128)(2,1)S(1)}, u32[]{:S(2)}, u32[]{:S(2)}) collective-permute-start(bf16[128,768]{1,0:T(8,128)(2,1)S(1)} %get-tuple-element.28.refs_0_), channel_id=1, source_target_pairs={{0,4},{1,5},{2,3},{3,2},{4,0},{5,1},{6,7},{7,6},{8,9},{9,8},{10,14... | collective-permute-start | bytes 589832 | tf_op jit(solution)/shard_map/ppermute | solution.py:526
  36.5 9.2 %collective-permute-start.15 = (bf16[128,768]{1,0:T(8,128)(2,1)S(1)}, bf16[128,768]{1,0:T(8,128)(2,1)S(1)}, u32[]{:S(2)}, u32[]{:S(2)}) collective-permute-start(bf16[128,768]{1,0:T(8,128)(2,1)S(1)} %get-tuple-element.29.refs_1_), channel_id=1, source_target_pairs={{0,2},{1,3},{2,0},{3,1},{4,5},{5,4},{6,7},{7,6},{8,10},{9,11},{10,... | collective-permute-start | bytes 589832 | tf_op jit(solution)/shard_map/ppermute | solution.py:526
  42.2 3.5 %collective-permute-start.16 = (bf16[128,768]{1,0:T(8,128)(2,1)S(1)}, bf16[128,768]{1,0:T(8,128)(2,1)S(1)}, u32[]{:S(2)}, u32[]{:S(2)}) collective-permute-start(bf16[128,768]{1,0:T(8,128)(2,1)S(1)} %collective-permute-done.12.refs_2_), channel_id=1, source_target_pairs={{0,1},{1,0},{2,6},{3,7},{4,5},{5,4},{6,2},{7,3},{8,12},{9,13},{10,... | collective-permute-start | bytes 589832 | tf_op jit(solution)/shard_map/ppermute | solution.py:526
  42.2 3.5 %collective-permute-start.17 = (bf16[128,768]{1,0:T(8,128)(2,1)S(1)}, bf16[128,768]{1,0:T(8,128)(2,1)S(1)}, u32[]{:S(2)}, u32[]{:S(2)}) collective-permute-start(bf16[128,768]{1,0:T(8,128)(2,1)S(1)} %collective-permute-done.13.refs_3_), channel_id=1, source_target_pairs={{0,1},{1,0},{2,3},{3,2},{4,6},{5,7},{6,4},{7,5},{8,9},{9,8},{10,11... | collective-permute-start | bytes 589832 | tf_op jit(solution)/shard_map/ppermute | solution.py:526
  46.3 1.8 %collective-permute-start.18 = (bf16[256,768]{1,0:T(8,128)(2,1)S(1)}, bf16[256,768]{1,0:T(8,128)(2,1)S(1)}, u32[]{:S(2)}, u32[]{:S(2)}) collective-permute-start(bf16[256,768]{1,0:T(8,128)(2,1)S(1)} %shard_map.108.refs_3_), channel_id=1, source_target_pairs={{0,1},{1,0},{2,3},{3,2},{4,5},{5,4},{6,7},{7,6},{8,9},{9,8},{10,11... | collective-permute-start | bytes 1179656 | tf_op jit(solution)/shard_map/ppermute | solution.py:514
  52.0 1.8 %collective-permute-start.19 = (bf16[384,411]{1,0:T(8,128)(2,1)S(1)}, bf16[384,411]{1,0:T(8,128)(2,1)S(1)}, u32[]{:S(2)}, u32[]{:S(2)}) collective-permute-start(bf16[384,411]{1,0:T(8,128)(2,1)S(1)} %get-tuple-element.33), channel_id=1, source_target_pairs={{0,1},{1,0},{2,3},{3,2},{4,5},{5,4},{6,7},{7,6},{8,9},{9,8},{10,11... | collective-permute-start | bytes 946952 | tf_op jit(solution)/shard_map/ppermute | solution.py:514
  53.9 5.5 %collective-permute-start.20 = (bf16[96,411]{1,0:T(8,128)(2,1)S(1)}, bf16[96,411]{1,0:T(8,128)(2,1)S(1)}, u32[]{:S(2)}, u32[]{:S(2)}) collective-permute-start(bf16[96,411]{1,0:T(8,128)(2,1)S(1)} %get-tuple-element.35), channel_id=1, source_target_pairs={{0,2},{1,3},{2,0},{3,1},{4,6},{5,7},{6,4},{7,5},{8,10},{9,11},{10,... | collective-permute-start | bytes 236744 | tf_op jit(solution)/shard_map/ppermute | solution.py:514
  56.3 6.2 %collective-permute-start.21 = (bf16[96,411]{1,0:T(8,128)(2,1)S(1)}, bf16[96,411]{1,0:T(8,128)(2,1)S(1)}, u32[]{:S(2)}, u32[]{:S(2)}) collective-permute-start(bf16[96,411]{1,0:T(8,128)(2,1)S(1)} %get-tuple-element.36), channel_id=1, source_target_pairs={{0,4},{1,5},{2,6},{3,7},{4,0},{5,1},{6,2},{7,3},{8,12},{9,13},{10,... | collective-permute-start | bytes 236744 | tf_op jit(solution)/shard_map/ppermute | solution.py:514
  58.2 6.1 %collective-permute-start.22 = (bf16[96,411]{1,0:T(8,128)(2,1)S(1)}, bf16[96,411]{1,0:T(8,128)(2,1)S(1)}, u32[]{:S(2)}, u32[]{:S(2)}) collective-permute-start(bf16[96,411]{1,0:T(8,128)(2,1)S(1)} %get-tuple-element.37), channel_id=1, source_target_pairs={{0,6},{1,7},{2,4},{3,5},{4,2},{5,3},{6,0},{7,1},{8,14},{9,15},{10,... | collective-permute-start | bytes 236744 | tf_op jit(solution)/shard_map/ppermute | solution.py:514
  64.5 5.9 %collective-permute-start.23 = (bf16[32,411]{1,0:T(8,128)(2,1)S(1)}, bf16[32,411]{1,0:T(8,128)(2,1)S(1)}, u32[]{:S(2)}, u32[]{:S(2)}) collective-permute-start(bf16[32,411]{1,0:T(8,128)(2,1)S(1)} %get-tuple-element.39), channel_id=1, source_target_pairs={{0,8},{8,16},{16,24},{24,0},{1,9},{9,17},{17,25},{25,1},{2,10},{10... | collective-permute-start | bytes 78920 | tf_op jit(solution)/shard_map/ppermute | solution.py:517
  65.5 5.3 %collective-permute-start.24 = (bf16[32,411]{1,0:T(8,128)(2,1)S(1)}, bf16[32,411]{1,0:T(8,128)(2,1)S(1)}, u32[]{:S(2)}, u32[]{:S(2)}) collective-permute-start(bf16[32,411]{1,0:T(8,128)(2,1)S(1)} %get-tuple-element.40), channel_id=1, source_target_pairs={{0,16},{8,24},{16,0},{24,8},{1,17},{9,25},{17,1},{25,9},{2,18},{10... | collective-permute-start | bytes 78920 | tf_op jit(solution)/shard_map/ppermute | solution.py:517
  67.6 3.9 %collective-permute-start.25 = (bf16[32,411]{1,0:T(8,128)(2,1)S(1)}, bf16[32,411]{1,0:T(8,128)(2,1)S(1)}, u32[]{:S(2)}, u32[]{:S(2)}) collective-permute-start(bf16[32,411]{1,0:T(8,128)(2,1)S(1)} %get-tuple-element.41), channel_id=1, source_target_pairs={{0,24},{8,0},{16,8},{24,16},{1,25},{9,1},{17,9},{25,17},{2,26},{10... | collective-permute-start | bytes 78920 | tf_op jit(solution)/shard_map/ppermute | solution.py:517

commit v7 on v6

--- a/solution.py
+++ b/solution.py
@@ -198,8 +198,8 @@
         )
         self.block = up_to(self.own_cols + 2 + self.across, 16)
         self.per_row = self.own_cols + 2
-        self.room = up_to(3 * self.per_row, 16)
-        self.patch = 3 * tiles * self.own_cols
+        self.rows_each = chans // self.group
+        self.around = (self.group + 2) * self.per_row
         self.deep = up_to(self.features, 16)
         self.strips = self.chips * tiles * self.block
 
@@ -282,14 +282,11 @@
     wanted = strip(tile, cell // p.across) * p.block + p.own_cols + 2 + cell % p.across
     cell_ref[...] = jnp.where(inside, wanted, -1)
 
+    each = p.rows_each * p.own_cols
     target = lax.broadcasted_iota(jnp.int32, target_refs[0].shape, 0)
-    chip, inner = target // p.patch, target % p.patch
-    beside, inner = inner // (p.patch // 3) - 1, inner % (p.patch // 3)
-    tile, along = inner // p.own_cols, inner % p.own_cols
     for k, target_ref in enumerate(target_refs):
-        row = ((chip ^ (c // p.group)) * p.group + (c % p.group ^ k)) + beside
-        wanted = tile * p.tile_cols + row * p.own_cols + along
-        target_ref[...] = jnp.where((row >= 0) & (row < p.chans), wanted, -1)
+        first = (c % p.group ^ k) * each
+        target_ref[...] = target // each * p.tile_cols + first + target % each
 
 
 def join_kernel(count, *refs):
@@ -327,7 +324,7 @@
     place_ref, source_ref, cell_ref, bias_ref, w_radiance_ref = take(5)
     strip_refs, weight_refs, seen_refs = take(p.group), take(p.group), take(2)
     part_refs = take(p.steps)
-    slope_ref, kappa_ref, active = refs
+    preact_ref, kappa_ref, active = refs
     c = lax.axis_index("chan")
     gathered = [ref[...] for ref in strip_refs]
     columns = sum(
@@ -345,10 +342,9 @@
             + low[1:, : p.hidden]
         )
         preact = dot(columns, p.layer(weight_refs, k)) + bias
-        squash = jax.nn.sigmoid(preact)
-        slope_ref[k] = squash * (1.0 + preact * (1.0 - squash))
+        preact_ref[k] = preact
         at = pl.multiple_of((c ^ p.mask(k)) * p.hidden, p.hidden)
-        active[:, pl.ds(at, p.hidden)] = (preact * squash).astype(jnp.bfloat16)
+        active[:, pl.ds(at, p.hidden)] = (preact * jax.nn.sigmoid(preact)).astype(jnp.bfloat16)
     part = p.rows // p.steps
     count = seen_refs[0].shape[0]
     for j, part_ref in enumerate(part_refs):
@@ -373,8 +369,15 @@
     kappa_ref[...] = sum(parts[:, k * p.lane : (k + 1) * p.lane] for k in range(3))
 
 
+def slope_kernel(preact_ref, slope_ref):
+    for k in range(preact_ref.shape[0]):
+        preact = preact_ref[k]
+        squash = jax.nn.sigmoid(preact)
+        slope_ref[k] = (squash * (1.0 + preact * (1.0 - squash))).T
+
+
 def choose_kernel(p, choices, *refs):
-    refs, out_ref, sems = refs[:-2], refs[-2], refs[-1]
+    refs, out_ref, sems = refs[:-3], refs[-2], refs[-1]
     size = refs[0].shape[0]
     role = (lax.axis_index("chan") // p.group) ^ lax.axis_index("tile")
     for place in range(p.chips):
@@ -405,56 +408,70 @@
         at = pl.multiple_of((c % p.group ^ k) * p.shard, p.shard)
         term = dot(ref[...], inv_cov_ref[pl.ds(at, p.shard), :])
         cotangent = term if cotangent is None else cotangent + term
-    cotangent = cotangent.astype(jnp.bfloat16)
-    total = jnp.zeros((p.rows, p.features), jnp.float32)
+    cotangent = cotangent.T.astype(jnp.bfloat16)
+    total = jnp.zeros((p.features, p.rows), jnp.float32)
     for k in range(p.chans):
         at = pl.multiple_of((c ^ p.mask(k)) * p.hidden, p.hidden)
-        grad_hidden = dot_nt(cotangent, w_radiance_ref[pl.ds(at, p.hidden), :])
+        grad_hidden = dot(w_radiance_ref[pl.ds(at, p.hidden), :], cotangent)
         grad_pre = (grad_hidden * slope_ref[k]).astype(jnp.bfloat16)
-        total = total + dot_nt(grad_pre, p.layer(weight_refs, k))
+        total = total + dot(p.layer(weight_refs, k), grad_pre)
     total = total.astype(jnp.bfloat16)
     for target_ref, out_ref in zip(target_refs, out_refs):
-        out_ref[...] = dot(one_hot(target_ref[...], 0, p.rows), total).astype(jnp.bfloat16)
-
-
-def add(refs, at=slice(None)):
-    total = refs[0][at, :].astype(jnp.float32)
+        out_ref[...] = dot_nt(one_hot(target_ref[...], 0, p.rows), total).astype(jnp.bfloat16)
+
+
+def add(refs):
+    total = refs[0][...].astype(jnp.float32)
     for ref in refs[1:]:
-        total = total + ref[at, :].astype(jnp.float32)
+        total = total + ref[...].astype(jnp.float32)
     return total
+
+
+def rows_and_cells(p, count):
+    target = lax.broadcasted_iota(jnp.int32, (count, 1), 0)
+    return target // p.per_row, target % p.per_row - 1
 
 
 def add_group_kernel(p, *refs):
     ins, outs = refs[: p.group], refs[p.group :]
-    for k, out_ref in enumerate(outs):
-        out_ref[...] = add(ins, slice(k * p.patch, (k + 1) * p.patch)).astype(jnp.bfloat16)
-
-
-def add_chips_kernel(p, *refs):
-    ins, outs = refs[: p.chips], refs[p.chips :]
     total = add(ins).astype(jnp.bfloat16)
-    shape = (p.room, p.patch)
-    target = lax.broadcasted_iota(jnp.int32, shape, 0)
-    source = lax.broadcasted_iota(jnp.int32, shape, 1)
-    row, along = target // p.per_row, target % p.per_row - 1
+    row, along = rows_and_cells(p, outs[0].shape[0])
     for k, out_ref in enumerate(outs):
         tile = (lax.axis_index("tile") + k) % p.tiles
         cell = (tile * p.own_cols + along + p.tiles * p.own_cols) % (p.tiles * p.own_cols)
-        pick = (source == row * (p.tiles * p.own_cols) + cell) & (row < 3)
-        out_ref[...] = dot(pick.astype(jnp.bfloat16), total).astype(jnp.bfloat16)
+        wanted = (cell // p.own_cols * p.rows_each + row) * p.own_cols + cell % p.own_cols
+        out_ref[...] = dot(one_hot(wanted, 0, total.shape[0]), total).astype(jnp.bfloat16)
+
+
+def add_tiles_kernel(p, *refs):
+    ins, outs = refs[: p.tiles], refs[p.tiles :]
+    total = add(ins).astype(jnp.bfloat16)
+    row, along = rows_and_cells(p, p.around)
+    c = lax.axis_index("chan")
+    for k, out_ref in enumerate(outs):
+        held = ((c // p.group) ^ k) * p.group - 1 + row - c % p.group * p.rows_each
+        wanted = jnp.where(
+            (held >= 0) & (held < p.rows_each), held * p.per_row + along + 1, -1
+        )
+        out_ref[...] = dot(one_hot(wanted, 0, total.shape[0]), total).astype(jnp.bfloat16)
+
+
+def add_chips_kernel(*refs):
+    refs[-1][...] = add(refs[:-1])
 
 
 def diffuse_kernel(p, edge, *refs):
-    ins, root_ref, out_ref = refs[: p.tiles], refs[-2], refs[-1]
+    ins, root_ref, out_ref = refs[: p.group], refs[-2], refs[-1]
     total = add(ins) * 0.0625
     length = p.along + 2 * edge
-    shape = (length, p.room)
+    shape = (length, p.around)
     cell = lax.broadcasted_iota(jnp.int32, shape, 0)
     source = lax.broadcasted_iota(jnp.int32, shape, 1)
     column = (cell - edge + 4) // 4
     spread = []
     for k in range(3):
-        pick = (source == column + k * p.per_row) & (column >= 0) & (column < p.per_row)
+        row = lax.axis_index("chan") % p.group + k
+        pick = (source == column + row * p.per_row) & (column >= 0) & (column < p.per_row)
         spread.append(
             jnp.dot(
                 pick.astype(jnp.float32),
@@ -566,7 +583,7 @@
     while bit < p.tiles:
         if 2 * bit < p.tiles:
             seen = grow(seen, lambda value: trade(value, bit))
-        strips = grow(strips, lambda value: trade(value, bit), [seen] if 2 * bit == p.tiles else ())
+        strips = grow(strips, lambda value: trade(value, bit), [seen] if bit == 1 else ())
         stages.append(strips)
         bit *= 2
     strips = join(
@@ -594,17 +611,24 @@
         functools.partial(place_kernel, p),
         [shape((p.rows, 1), jnp.int32)] * 2
         + [shape((3 * reach, 1), jnp.int32)]
-        + [shape((p.chips * p.patch, 1), jnp.int32)] * p.group,
+        + [shape((p.rows // p.group, 1), jnp.int32)] * p.group,
         [owners.reshape(1, p.rows)],
         flops=SLACK_FLOPS,
     )
-    *parts, slope, kappa = call(
+    *parts, preact, kappa = call(
         functools.partial(forward_kernel, p),
         [shape((p.rows // p.steps, p.shard), half)] * p.steps
         + [shape((p.chans, p.rows, p.hidden), single), shape((3 * reach, p.lane), single)],
         [place, source, cell, b_radiance, w_radiance] + strips + weights + seen,
         scratch=[pltpu.VMEM((p.rows, p.hidden * p.chans), half)],
         flops=2 * p.rows * p.hidden * p.chans * (p.features + p.shard),
+    )
+
+    slope = call(
+        slope_kernel,
+        shape((p.chans, p.hidden, p.rows), single),
+        [preact],
+        flops=40 * preact.size,
     )
 
     pool, held, choices = list(parts), {}, {}
@@ -631,8 +655,8 @@
     chosen = call(
         functools.partial(choose_kernel, p, choices),
         shape((p.rows, p.shard), half),
-        pool,
-        in_hbm=range(len(pool)),
+        pool + [slope],
+        in_hbm=range(len(pool) + 1),
         out_hbm=True,
         scratch=[pltpu.SemaphoreType.DMA((p.steps,))],
     )
@@ -640,23 +664,25 @@
 
     partial = call(
         functools.partial(backward_kernel, p),
-        [shape((p.chips * p.patch, p.features), half)] * p.group,
+        [shape((p.rows // p.group, p.features), half)] * p.group,
         [w_radiance, inv_cov, slope] + depart + weights + targets,
         flops=2 * p.rows * (p.hidden * p.chans * (p.features + p.shard) + inv_cov.size),
     )
     partial = [partial[0]] + [flip(partial[k], k) for k in range(1, p.group)]
     partial = call(
         functools.partial(add_group_kernel, p),
-        [shape((p.patch, p.features), half)] * p.chips,
+        [shape((p.rows_each * p.per_row, p.features), half)] * p.tiles,
         partial,
     )
+    partial = [partial[0]] + [shift(partial[k], k) for k in range(1, p.tiles)]
+    partial = call(
+        functools.partial(add_tiles_kernel, p),
+        [shape((p.around, p.features), half)] * p.chips,
+        partial,
+    )
     partial = [partial[0]] + [flip(partial[k], k * p.group) for k in range(1, p.chips)]
-    partial = call(
-        functools.partial(add_chips_kernel, p),
-        [shape((p.room, p.features), half)] * p.tiles,
-        partial,
-    )
-    partial = [partial[0]] + [shift(partial[k], k) for k in range(1, p.tiles)]
+    partial = call(add_chips_kernel, shape((p.around, p.features), single), partial)
+    partial = [partial] + [flip(partial, k) for k in range(1, p.group)]
 
     edge = 8
     kappa = kappa.reshape(3, reach, p.lane)

time: 73.2 us -> 72.3 us (0.988)
  waiting for transfers between devices: 28.4 us -> 27.3 us
  starting transfers between devices: 29.2 us -> 30.1 us
    ppermute x13 -> x14, starting transfers between devices: 13.9 us -> 11 us  [flip(): return lax.ppermute(value, 'chan', [(b, b ^ mask) for b in range(p.chans)])]
    ppermute x3, starting transfers between devices: 5.15 us -> 7.75 us  [shift(): lax.ppermute(value, 'tile', [(a, (a + by) % p.tiles) for a in range(p.til...]
    ppermute x3, starting transfers between devices: 4.75 us -> 5.82 us  [trade(): return lax.ppermute(value, 'tile', [(a, a ^ mask) for a in range(p.tiles)])]
    pallas_call x13 -> x15, Pallas kernels: 12.3 us -> 11.6 us  [call(): pl.pallas_call(kernel, out_shape=out_shape, in_specs=[far if k in in_hbm...]
    ppermute x13 -> x14, waiting for transfers between devices: 11.7 us -> 11.2 us  [flip(): return lax.ppermute(value, 'chan', [(b, b ^ mask) for b in range(p.chans)])]
  transfers between devices with their start and end apart: 26 -> 27, of which waited for: 16 -> 18; matrix products, arithmetic and copies ran while one was open for 0% -> 0% of each run, Pallas kernels for 5% -> 5%
where the time goes in v7:
time: 72.3 us; the launch traced here: 72.1 us
  starting transfers between devices  30.1 us (42%)
  waiting for transfers between devices  27.3 us (38%)
  Pallas kernels  11.6 us (16%)
  local copies, waits for them, and re-layouts  2.75 us (4%)
    pallas_call x15, Pallas kernels, call(): pl.pallas_call(kernel, out_shape=out_shape, in_specs=[far if k in in_hbm...  11.6 us
    ppermute x14, waiting for transfers between devices, flip(): return lax.ppermute(value, 'chan', [(b, b ^ mask) for b in range(p.chans)])  11.2 us
    ppermute x14, starting transfers between devices, flip(): return lax.ppermute(value, 'chan', [(b, b ^ mask) for b in range(p.chans)])  11 us
    ppermute x7, waiting for transfers between devices, send(): lax.ppermute(value, both, sorted(((number(a), number(b)) for a, b in pair...  9.41 us
    ppermute x3, starting transfers between devices, shift(): lax.ppermute(value, 'tile', [(a, (a + by) % p.tiles) for a in range(p.til...  7.75 us
    ppermute x3, starting transfers between devices, trade(): return lax.ppermute(value, 'tile', [(a, a ^ mask) for a in range(p.tiles)])  5.82 us
    ppermute x7, starting transfers between devices, send(): lax.ppermute(value, both, sorted(((number(a), number(b)) for a, b in pair...  5.53 us
    ppermute x3, waiting for transfers between devices, trade(): return lax.ppermute(value, 'tile', [(a, a ^ mask) for a in range(p.tiles)])  4.67 us
  transfers between devices with their start and end apart: 27, of which 18 were waited for; matrix products, arithmetic and copies ran while one was open for 0% of the time, Pallas kernels for 5%

profile of v7, /device:TPU:0, one launch (start us, length us, event | category | flops | bytes accessed | tf_op | source)
XLA Modules:
  0.0 72.1 jit_solution(8324372315746660706)
XLA Ops:
  0.0 3.0 %collective-permute-start.1 = (bf16[128,768]{1,0:T(8,128)(2,1)}, bf16[128,768]{1,0:T(8,128)(2,1)S(1)}, u32[]{:S(2)}, u32[]{:S(2)}) collective-permute-start(bf16[128,768]{1,0:T(8,128)(2,1)} %refs_0_.5), channel_id=1, source_target_pairs={{0,8},{8,0},{16,24},{24,16},{1,9},{9,1},{17,25},{25,17},{2,10},{10... | collective-permute-start | bytes 589832 | tf_op jit(solution)/shard_map/ppermute | solution.py:562
  3.0 1.5 %collective-permute-start.8 = (bf16[411,256]{1,0:T(8,128)(2,1)}, bf16[411,256]{1,0:T(8,128)(2,1)S(1)}, u32[]{:S(2)}, u32[]{:S(2)}) collective-permute-start(bf16[411,256]{1,0:T(8,128)(2,1)} %refs_0_.6), channel_id=1, source_target_pairs={{0,4},{1,5},{2,6},{3,7},{4,0},{5,1},{6,2},{7,3},{8,12},{9,13},{10,... | collective-permute-start | bytes 631304 | tf_op jit(solution)/shard_map/ppermute | solution.py:531
  4.5 1.5 %collective-permute-start.7 = (bf16[411,256]{1,0:T(8,128)(2,1)}, bf16[411,256]{1,0:T(8,128)(2,1)S(1)}, u32[]{:S(2)}, u32[]{:S(2)}) collective-permute-start(bf16[411,256]{1,0:T(8,128)(2,1)} %refs_0_.6), channel_id=1, source_target_pairs={{0,2},{1,3},{2,0},{3,1},{4,6},{5,7},{6,4},{7,5},{8,10},{9,11},{10,... | collective-permute-start | bytes 631304 | tf_op jit(solution)/shard_map/ppermute | solution.py:531
  6.0 0.5 collective-permute-start.9
  6.5 1.8 %shard_map.101.refs_0_ = bf16[16,512]{1,0:T(8,128)(2,1)} custom-call(f32[4,32,411]{2,1,0:T(8,128)} %refs_0_.4, f32[4,32]{1,0:T(4,128)} %refs_1_.2, s32[128]{0:T(128)} %refs_2_.1, f32[256]{0:T(256)} %refs_3_.2), custom_call_target="tpu_custom_call" | custom-call | bytes 212480 | tf_op jit(solution)/shard_map/pallas_call | solution.py:164
  8.3 0.1 collective-permute-start
  8.4 0.9 %copy-done.3 = bf16[128,768]{1,0:T(8,128)(2,1)S(1)} copy-done((bf16[128,768]{1,0:T(8,128)(2,1)S(1)}, bf16[128,768]{1,0:T(8,128)(2,1)}, u32[]{:S(2)}) %copy-start.3) | copy-done | bytes 196632
  9.4 0.5 shard_map.102.refs_2_.refs_9_
  9.9 2.5 %collective-permute-done.refs_1_ = bf16[16,512]{1,0:T(8,128)(2,1)S(1)} collective-permute-done((bf16[16,512]{1,0:T(8,128)(2,1)}, bf16[16,512]{1,0:T(8,128)(2,1)S(1)}, u32[]{:S(2)}, u32[]{:S(2)}) %collective-permute-start) | collective-permute-done | bytes 16416 | tf_op jit(solution)/shard_map/ppermute | solution.py:562
  12.3 0.7 copy-done.4
  13.1 2.7 %collective-permute-start.2 = (bf16[32,512]{1,0:T(8,128)(2,1)S(1)}, bf16[32,512]{1,0:T(8,128)(2,1)S(1)}, u32[]{:S(2)}, u32[]{:S(2)}) collective-permute-start(bf16[32,512]{1,0:T(8,128)(2,1)S(1)} %shard_map.103.refs_0_), channel_id=1, source_target_pairs={{0,16},{8,24},{16,0},{24,8},{1,17},{9,25},{17,1},{25,9},{2,18},{10... | collective-permute-start | bytes 98312 | tf_op jit(solution)/shard_map/ppermute | solution.py:562
  15.7 2.2 %collective-permute-done.2.refs_1_ = bf16[32,512]{1,0:T(8,128)(2,1)S(1)} collective-permute-done((bf16[32,512]{1,0:T(8,128)(2,1)S(1)}, bf16[32,512]{1,0:T(8,128)(2,1)S(1)}, u32[]{:S(2)}, u32[]{:S(2)}) %collective-permute-start.2) | collective-permute-done | bytes 32800 | tf_op jit(solution)/shard_map/ppermute | solution.py:562
  18.0 0.1 shard_map.104.refs_0_.refs_4_
  18.1 0.9 %copy-done.2 = bf16[411,256]{1,0:T(8,128)(2,1)S(1)} copy-done((bf16[411,256]{1,0:T(8,128)(2,1)S(1)}, bf16[411,256]{1,0:T(8,128)(2,1)}, u32[]{:S(2)}) %copy-start.2) | copy-done | bytes 210456
  19.0 0.1 shard_map.106.refs_7_.refs_5_
  19.1 0.1 collective-permute-start.10
  19.2 2.7 %collective-permute-start.11 = (bf16[256,768]{1,0:T(8,128)(2,1)S(1)}, bf16[256,768]{1,0:T(8,128)(2,1)S(1)}, u32[]{:S(2)}, u32[]{:S(2)}) collective-permute-start(bf16[256,768]{1,0:T(8,128)(2,1)S(1)} %shard_map.102.refs_2_.refs_9_), channel_id=1, source_target_pairs={{0,16},{1,17},{2,3},{3,2},{4,20},{5,21},{6,7},{7,6},{8,9},{9,8},{1... | collective-permute-start | bytes 1179656 | tf_op jit(solution)/shard_map/ppermute | solution.py:543
  21.8 0.5 collective-permute-start.5
  22.3 1.0 %collective-permute-start.4 = (bf16[64,512]{1,0:T(8,128)(2,1)S(1)}, bf16[64,512]{1,0:T(8,128)(2,1)S(1)}, u32[]{:S(2)}, u32[]{:S(2)}) collective-permute-start(bf16[64,512]{1,0:T(8,128)(2,1)S(1)} %shard_map.104.refs_0_.refs_4_), channel_id=1, source_target_pairs={{0,4},{1,5},{2,6},{3,7},{4,0},{5,1},{6,2},{7,3},{8,12},{9,13},{10,... | collective-permute-start | bytes 196616 | tf_op jit(solution)/shard_map/ppermute | solution.py:531
  23.3 2.0 %collective-permute-start.3 = (bf16[64,512]{1,0:T(8,128)(2,1)S(1)}, bf16[64,512]{1,0:T(8,128)(2,1)S(1)}, u32[]{:S(2)}, u32[]{:S(2)}) collective-permute-start(bf16[64,512]{1,0:T(8,128)(2,1)S(1)} %shard_map.104.refs_0_.refs_4_), channel_id=1, source_target_pairs={{0,2},{1,3},{2,0},{3,1},{4,6},{5,7},{6,4},{7,5},{8,10},{9,11},{10,... | collective-permute-start | bytes 196616 | tf_op jit(solution)/shard_map/ppermute | solution.py:531
  25.3 2.0 %collective-permute-done.5.refs_3_ = bf16[64,512]{1,0:T(8,128)(2,1)S(1)} collective-permute-done((bf16[64,512]{1,0:T(8,128)(2,1)S(1)}, bf16[64,512]{1,0:T(8,128)(2,1)S(1)}, u32[]{:S(2)}, u32[]{:S(2)}) %collective-permute-start.5) | collective-permute-done | bytes 65568 | tf_op jit(solution)/shard_map/ppermute | solution.py:531
  27.3 0.2 collective-permute-done.4.refs_2_
  27.6 0.7 %collective-permute-done.3.refs_1_ = bf16[64,512]{1,0:T(8,128)(2,1)S(1)} collective-permute-done((bf16[64,512]{1,0:T(8,128)(2,1)S(1)}, bf16[64,512]{1,0:T(8,128)(2,1)S(1)}, u32[]{:S(2)}, u32[]{:S(2)}) %collective-permute-start.3) | collective-permute-done | bytes 65568 | tf_op jit(solution)/shard_map/ppermute | solution.py:531
  28.3 0.3 shard_map.105.refs_5_
  28.7 0.1 collective-permute-start.6
  28.8 0.0 copy-start.5
  28.8 0.4 shard_map.100
  29.2 1.1 %collective-permute-done.6.refs_6_ = bf16[256,512]{1,0:T(8,128)(2,1)S(1)} collective-permute-done((bf16[256,512]{1,0:T(8,128)(2,1)S(1)}, bf16[256,512]{1,0:T(8,128)(2,1)S(1)}, u32[]{:S(2)}, u32[]{:S(2)}) %collective-permute-start.6) | collective-permute-done | bytes 262176 | tf_op jit(solution)/shard_map/ppermute | solution.py:531
  30.3 1.3 %collective-permute-done.11.refs_10_ = bf16[256,768]{1,0:T(8,128)(2,1)S(1)} collective-permute-done((bf16[256,768]{1,0:T(8,128)(2,1)S(1)}, bf16[256,768]{1,0:T(8,128)(2,1)S(1)}, u32[]{:S(2)}, u32[]{:S(2)}) %collective-permute-start.11) | collective-permute-done | bytes 393248 | tf_op jit(solution)/shard_map/ppermute | solution.py:543
  31.6 2.2 %shard_map.107 = (bf16[128,768]{1,0:T(8,128)(2,1)S(1)}, bf16[128,768]{1,0:T(8,128)(2,1)S(1)}, f32[8,256,256]{2,1,0:T(8,128)S(1)}, f32[24,128]{1,0:T(8,128)S(1)}) custom-call(s32[256,1]{1,0:T(8,128)S(1)} %get-tuple-element.24.refs_0_, s32[256,1]{1,0:T(8,128)S(1)} %get-tuple-element.25.refs_1_, s32[24,1]{1,0:T(8,128)S(1)} %get-tuple-element.26.refs_2_, ...), custom_call_target="tpu_custom_call" | custom-call | flops 1236271104 | bytes 6165600 | tf_op jit(solution)/shard_map/pallas_call | solution.py:164
  33.8 0.4 collective-permute-start.12
  34.2 1.5 %collective-permute-start.13 = (bf16[128,768]{1,0:T(8,128)(2,1)S(1)}, bf16[128,768]{1,0:T(8,128)(2,1)S(1)}, u32[]{:S(2)}, u32[]{:S(2)}) collective-permute-start(bf16[128,768]{1,0:T(8,128)(2,1)S(1)} %get-tuple-element.29.refs_1_), channel_id=1, source_target_pairs={{0,4},{1,5},{2,3},{3,2},{4,0},{5,1},{6,7},{7,6},{8,9},{9,8},{10,14... | collective-permute-start | bytes 589832 | tf_op jit(solution)/shard_map/ppermute | solution.py:543
  35.7 0.5 collective-permute-start.14
  36.2 0.2 collective-permute-start.15
  36.4 5.3 %collective-permute-done.12.refs_2_ = bf16[128,768]{1,0:T(8,128)(2,1)S(1)} collective-permute-done((bf16[128,768]{1,0:T(8,128)(2,1)S(1)}, bf16[128,768]{1,0:T(8,128)(2,1)S(1)}, u32[]{:S(2)}, u32[]{:S(2)}) %collective-permute-start.12) | collective-permute-done | bytes 196640 | tf_op jit(solution)/shard_map/ppermute | solution.py:543
  41.7 0.2 collective-permute-done.13.refs_3_
  41.9 0.3 collective-permute-start.17
  42.2 0.6 shard_map.108.refs_8_.refs_2_
  42.8 2.6 %collective-permute-done.14.refs_4_ = bf16[128,768]{1,0:T(8,128)(2,1)S(1)} collective-permute-done((bf16[128,768]{1,0:T(8,128)(2,1)S(1)}, bf16[128,768]{1,0:T(8,128)(2,1)S(1)}, u32[]{:S(2)}, u32[]{:S(2)}) %collective-permute-start.14) | collective-permute-done | bytes 196640 | tf_op jit(solution)/shard_map/ppermute | solution.py:543
  45.4 0.6 shard_map.109.refs_3_
  46.0 0.1 collective-permute-start.18
  46.1 1.7 %collective-permute-done.18.refs_4_ = bf16[256,768]{1,0:T(8,128)(2,1)S(1)} collective-permute-done((bf16[256,768]{1,0:T(8,128)(2,1)S(1)}, bf16[256,768]{1,0:T(8,128)(2,1)S(1)}, u32[]{:S(2)}, u32[]{:S(2)}) %collective-permute-start.18) | collective-permute-done | bytes 393248 | tf_op jit(solution)/shard_map/ppermute | solution.py:531
  47.8 3.2 %shard_map.110 = (bf16[128,411]{1,0:T(8,128)(2,1)S(1)}, bf16[128,411]{1,0:T(8,128)(2,1)S(1)}) custom-call(bf16[2048,768]{1,0:T(8,128)(2,1)S(1)} %copy-done, bf16[1536,768]{1,0:T(8,128)(2,1)S(1)} %copy-done.1, f32[8,256,256]{2,1,0:T(8,128)S(1)} %shard_map.108.refs_8_.refs_2_, bf16[256,768]{1,0:T(8,128)(2,1)S(1)} %shard_map.109.refs_3_, ...), custom_call_target="tpu_custom_call" | custom-call | flops 1840250880 | bytes 10093568 | tf_op jit(solution)/shard_map/pallas_call | solution.py:164
  51.0 0.2 collective-permute-start.19
  51.2 1.2 %collective-permute-done.19.refs_1_ = bf16[128,411]{1,0:T(8,128)(2,1)S(1)} collective-permute-done((bf16[128,411]{1,0:T(8,128)(2,1)S(1)}, bf16[128,411]{1,0:T(8,128)(2,1)S(1)}, u32[]{:S(2)}, u32[]{:S(2)}) %collective-permute-start.19) | collective-permute-done | bytes 105248 | tf_op jit(solution)/shard_map/ppermute | solution.py:531
  52.4 0.3 shard_map.111
  52.6 2.5 %collective-permute-start.20 = (bf16[40,411]{1,0:T(8,128)(2,1)S(1)}, bf16[40,411]{1,0:T(8,128)(2,1)S(1)}, u32[]{:S(2)}, u32[]{:S(2)}) collective-permute-start(bf16[40,411]{1,0:T(8,128)(2,1)S(1)} %get-tuple-element.35), channel_id=1, source_target_pairs={{0,8},{8,16},{16,24},{24,0},{1,9},{9,17},{17,25},{25,1},{2,10},{10... | collective-permute-start | bytes 98648 | tf_op jit(solution)/shard_map/ppermute | solution.py:534
  55.1 3.4 %collective-permute-start.21 = (bf16[40,411]{1,0:T(8,128)(2,1)S(1)}, bf16[40,411]{1,0:T(8,128)(2,1)S(1)}, u32[]{:S(2)}, u32[]{:S(2)}) collective-permute-start(bf16[40,411]{1,0:T(8,128)(2,1)S(1)} %get-tuple-element.36), channel_id=1, source_target_pairs={{0,16},{8,24},{16,0},{24,8},{1,17},{9,25},{17,1},{25,9},{2,18},{10... | collective-permute-start | bytes 98648 | tf_op jit(solution)/shard_map/ppermute | solution.py:534
  58.5 1.8 %collective-permute-start.22 = (bf16[40,411]{1,0:T(8,128)(2,1)S(1)}, bf16[40,411]{1,0:T(8,128)(2,1)S(1)}, u32[]{:S(2)}, u32[]{:S(2)}) collective-permute-start(bf16[40,411]{1,0:T(8,128)(2,1)S(1)} %get-tuple-element.37), channel_id=1, source_target_pairs={{0,24},{8,0},{16,8},{24,16},{1,25},{9,1},{17,9},{25,17},{2,26},{10... | collective-permute-start | bytes 98648 | tf_op jit(solution)/shard_map/ppermute | solution.py:534
  60.4 0.1 slice_bitcast_fusion.2
  60.5 0.9 %collective-permute-done.21.refs_2_ = bf16[40,411]{1,0:T(8,128)(2,1)S(1)} collective-permute-done((bf16[40,411]{1,0:T(8,128)(2,1)S(1)}, bf16[40,411]{1,0:T(8,128)(2,1)S(1)}, u32[]{:S(2)}, u32[]{:S(2)}) %collective-permute-start.21) | collective-permute-done | bytes 32912 | tf_op jit(solution)/shard_map/ppermute | solution.py:534
  61.4 1.2 %collective-permute-done.22.refs_3_ = bf16[40,411]{1,0:T(8,128)(2,1)S(1)} collective-permute-done((bf16[40,411]{1,0:T(8,128)(2,1)S(1)}, bf16[40,411]{1,0:T(8,128)(2,1)S(1)}, u32[]{:S(2)}, u32[]{:S(2)}) %collective-permute-start.22) | collective-permute-done | bytes 32912 | tf_op jit(solution)/shard_map/ppermute | solution.py:534
  62.5 0.2 shard_map.112
  62.8 0.9 %collective-permute-start.23 = (bf16[40,411]{1,0:T(8,128)(2,1)S(1)}, bf16[40,411]{1,0:T(8,128)(2,1)S(1)}, u32[]{:S(2)}, u32[]{:S(2)}) collective-permute-start(bf16[40,411]{1,0:T(8,128)(2,1)S(1)} %get-tuple-element.39), channel_id=1, source_target_pairs={{0,2},{1,3},{2,0},{3,1},{4,6},{5,7},{6,4},{7,5},{8,10},{9,11},{10,... | collective-permute-start | bytes 98648 | tf_op jit(solution)/shard_map/ppermute | solution.py:531
  63.7 0.8 %collective-permute-start.24 = (bf16[40,411]{1,0:T(8,128)(2,1)S(1)}, bf16[40,411]{1,0:T(8,128)(2,1)S(1)}, u32[]{:S(2)}, u32[]{:S(2)}) collective-permute-start(bf16[40,411]{1,0:T(8,128)(2,1)S(1)} %get-tuple-element.40), channel_id=1, source_target_pairs={{0,4},{1,5},{2,6},{3,7},{4,0},{5,1},{6,2},{7,3},{8,12},{9,13},{10,... | collective-permute-start | bytes 98648 | tf_op jit(solution)/shard_map/ppermute | solution.py:531
  64.5 1.8 %collective-permute-start.25 = (bf16[40,411]{1,0:T(8,128)(2,1)S(1)}, bf16[40,411]{1,0:T(8,128)(2,1)S(1)}, u32[]{:S(2)}, u32[]{:S(2)}) collective-permute-start(bf16[40,411]{1,0:T(8,128)(2,1)S(1)} %get-tuple-element.41), channel_id=1, source_target_pairs={{0,6},{1,7},{2,4},{3,5},{4,2},{5,3},{6,0},{7,1},{8,14},{9,15},{10,... | collective-permute-start | bytes 98648 | tf_op jit(solution)/shard_map/ppermute | solution.py:531
  66.3 0.7 collective-permute-done.23.refs_1_
  67.0 1.1 %collective-permute-done.24.refs_2_ = bf16[40,411]{1,0:T(8,128)(2,1)S(1)} collective-permute-done((bf16[40,411]{1,0:T(8,128)(2,1)S(1)}, bf16[40,411]{1,0:T(8,128)(2,1)S(1)}, u32[]{:S(2)}, u32[]{:S(2)}) %collective-permute-start.24) | collective-permute-done | bytes 32912 | tf_op jit(solution)/shard_map/ppermute | solution.py:531
  68.1 1.3 %collective-permute-done.25.refs_3_ = bf16[40,411]{1,0:T(8,128)(2,1)S(1)} collective-permute-done((bf16[40,411]{1,0:T(8,128)(2,1)S(1)}, bf16[40,411]{1,0:T(8,128)(2,1)S(1)}, u32[]{:S(2)}, u32[]{:S(2)}) %collective-permute-start.25) | collective-permute-done | bytes 32912 | tf_op jit(solution)/shard_map/ppermute | solution.py:531
  69.4 0.1 collective-permute-start.26
  69.5 0.1 maximum_sqrt_fusion
  69.6 0.1 copy.19
  69.7 1.1 %collective-permute-done.26.refs_1_ = f32[40,411]{1,0:T(8,128)S(1)} collective-permute-done((f32[40,411]{1,0:T(8,128)S(1)}, f32[40,411]{1,0:T(8,128)S(1)}, u32[]{:S(2)}, u32[]{:S(2)}) %collective-permute-start.26) | collective-permute-done | bytes 65792 | tf_op jit(solution)/shard_map/ppermute | solution.py:531
  70.8 1.3 %shard_map.114 = f32[4,32,411]{2,1,0:T(8,128)} custom-call(f32[40,411]{1,0:T(8,128)S(1)} %shard_map.113.refs_0_, f32[40,411]{1,0:T(8,128)S(1)} %collective-permute-done.26.refs_1_, f32[48,8]{1,0:T(8,128)S(1)} %bitcast.9), custom_call_target="tpu_custom_call" | custom-call | flops 5260800 | bytes 133056 | tf_op jit(solution)/shard_map/pallas_call | solution.py:164
  (23 shorter events, 0.1 us)
Async XLA Ops:
  0.0 28.8 %copy-start.6 = (s32[256,1]{0,1:T(1,128)S(1)}, s32[256,1]{0,1:T(1,128)}, u32[]{:S(2)}) copy-start(s32[256,1]{0,1:T(1,128)} %param.12) | copy-start | bytes 3076
  0.0 8.4 %collective-permute-start.1 = (bf16[128,768]{1,0:T(8,128)(2,1)}, bf16[128,768]{1,0:T(8,128)(2,1)S(1)}, u32[]{:S(2)}, u32[]{:S(2)}) collective-permute-start(bf16[128,768]{1,0:T(8,128)(2,1)} %refs_0_.5), channel_id=1, source_target_pairs={{0,8},{8,0},{16,24},{24,16},{1,9},{9,1},{17,25},{25,17},{2,10},{10... | collective-permute-start | bytes 589832 | tf_op jit(solution)/shard_map/ppermute | solution.py:562
  3.0 15.0 %collective-permute-start.8 = (bf16[411,256]{1,0:T(8,128)(2,1)}, bf16[411,256]{1,0:T(8,128)(2,1)S(1)}, u32[]{:S(2)}, u32[]{:S(2)}) collective-permute-start(bf16[411,256]{1,0:T(8,128)(2,1)} %refs_0_.6), channel_id=1, source_target_pairs={{0,4},{1,5},{2,6},{3,7},{4,0},{5,1},{6,2},{7,3},{8,12},{9,13},{10,... | collective-permute-start | bytes 631304 | tf_op jit(solution)/shard_map/ppermute | solution.py:531
  4.5 13.5 %collective-permute-start.7 = (bf16[411,256]{1,0:T(8,128)(2,1)}, bf16[411,256]{1,0:T(8,128)(2,1)S(1)}, u32[]{:S(2)}, u32[]{:S(2)}) collective-permute-start(bf16[411,256]{1,0:T(8,128)(2,1)} %refs_0_.6), channel_id=1, source_target_pairs={{0,2},{1,3},{2,0},{3,1},{4,6},{5,7},{6,4},{7,5},{8,10},{9,11},{10,... | collective-permute-start | bytes 631304 | tf_op jit(solution)/shard_map/ppermute | solution.py:531
  6.0 12.0 %collective-permute-start.9 = (bf16[411,256]{1,0:T(8,128)(2,1)}, bf16[411,256]{1,0:T(8,128)(2,1)S(1)}, u32[]{:S(2)}, u32[]{:S(2)}) collective-permute-start(bf16[411,256]{1,0:T(8,128)(2,1)} %refs_0_.6), channel_id=1, source_target_pairs={{0,6},{1,7},{2,4},{3,5},{4,2},{5,3},{6,0},{7,1},{8,14},{9,15},{10,... | collective-permute-start | bytes 631304 | tf_op jit(solution)/shard_map/ppermute | solution.py:531
  8.3 4.0 %collective-permute-start = (bf16[16,512]{1,0:T(8,128)(2,1)}, bf16[16,512]{1,0:T(8,128)(2,1)S(1)}, u32[]{:S(2)}, u32[]{:S(2)}) collective-permute-start(bf16[16,512]{1,0:T(8,128)(2,1)} %shard_map.101.refs_0_), channel_id=1, source_target_pairs={{0,8},{8,0},{16,24},{24,16},{1,9},{9,1},{17,25},{25,17},{2,10},{10... | collective-permute-start | bytes 49160 | tf_op jit(solution)/shard_map/ppermute | solution.py:562
  8.4 0.9 %copy-start.3 = (bf16[128,768]{1,0:T(8,128)(2,1)S(1)}, bf16[128,768]{1,0:T(8,128)(2,1)}, u32[]{:S(2)}) copy-start(bf16[128,768]{1,0:T(8,128)(2,1)} %refs_0_.5) | copy-start | bytes 589828
  12.3 0.7 copy-start.4
  13.1 4.9 %collective-permute-start.2 = (bf16[32,512]{1,0:T(8,128)(2,1)S(1)}, bf16[32,512]{1,0:T(8,128)(2,1)S(1)}, u32[]{:S(2)}, u32[]{:S(2)}) collective-permute-start(bf16[32,512]{1,0:T(8,128)(2,1)S(1)} %shard_map.103.refs_0_), channel_id=1, source_target_pairs={{0,16},{8,24},{16,0},{24,8},{1,17},{9,25},{17,1},{25,9},{2,18},{10... | collective-permute-start | bytes 98312 | tf_op jit(solution)/shard_map/ppermute | solution.py:562
  18.1 0.9 %copy-start.2 = (bf16[411,256]{1,0:T(8,128)(2,1)S(1)}, bf16[411,256]{1,0:T(8,128)(2,1)}, u32[]{:S(2)}) copy-start(bf16[411,256]{1,0:T(8,128)(2,1)} %refs_0_.6) | copy-start | bytes 631300
  19.1 12.5 %collective-permute-start.10 = (bf16[1664,256]{1,0:T(8,128)(2,1)S(1)}, bf16[1664,256]{1,0:T(8,128)(2,1)S(1)}, u32[]{:S(2)}, u32[]{:S(2)}) collective-permute-start(bf16[1664,256]{1,0:T(8,128)(2,1)S(1)} %shard_map.106.refs_7_.refs_5_), channel_id=1, source_target_pairs={{0,1},{1,0},{2,3},{3,2},{4,5},{5,4},{6,7},{7,6},{8,9},{9,8},{10,11... | collective-permute-start | bytes 2555912 | tf_op jit(solution)/shard_map/ppermute | solution.py:531
  19.2 12.4 %collective-permute-start.11 = (bf16[256,768]{1,0:T(8,128)(2,1)S(1)}, bf16[256,768]{1,0:T(8,128)(2,1)S(1)}, u32[]{:S(2)}, u32[]{:S(2)}) collective-permute-start(bf16[256,768]{1,0:T(8,128)(2,1)S(1)} %shard_map.102.refs_2_.refs_9_), channel_id=1, source_target_pairs={{0,16},{1,17},{2,3},{3,2},{4,20},{5,21},{6,7},{7,6},{8,9},{9,8},{1... | collective-permute-start | bytes 1179656 | tf_op jit(solution)/shard_map/ppermute | solution.py:543
  21.8 5.5 %collective-permute-start.5 = (bf16[64,512]{1,0:T(8,128)(2,1)S(1)}, bf16[64,512]{1,0:T(8,128)(2,1)S(1)}, u32[]{:S(2)}, u32[]{:S(2)}) collective-permute-start(bf16[64,512]{1,0:T(8,128)(2,1)S(1)} %shard_map.104.refs_0_.refs_4_), channel_id=1, source_target_pairs={{0,6},{1,7},{2,4},{3,5},{4,2},{5,3},{6,0},{7,1},{8,14},{9,15},{10,... | collective-permute-start | bytes 196616 | tf_op jit(solution)/shard_map/ppermute | solution.py:531
  22.3 5.2 %collective-permute-start.4 = (bf16[64,512]{1,0:T(8,128)(2,1)S(1)}, bf16[64,512]{1,0:T(8,128)(2,1)S(1)}, u32[]{:S(2)}, u32[]{:S(2)}) collective-permute-start(bf16[64,512]{1,0:T(8,128)(2,1)S(1)} %shard_map.104.refs_0_.refs_4_), channel_id=1, source_target_pairs={{0,4},{1,5},{2,6},{3,7},{4,0},{5,1},{6,2},{7,3},{8,12},{9,13},{10,... | collective-permute-start | bytes 196616 | tf_op jit(solution)/shard_map/ppermute | solution.py:531
  23.3 5.0 %collective-permute-start.3 = (bf16[64,512]{1,0:T(8,128)(2,1)S(1)}, bf16[64,512]{1,0:T(8,128)(2,1)S(1)}, u32[]{:S(2)}, u32[]{:S(2)}) collective-permute-start(bf16[64,512]{1,0:T(8,128)(2,1)S(1)} %shard_map.104.refs_0_.refs_4_), channel_id=1, source_target_pairs={{0,2},{1,3},{2,0},{3,1},{4,6},{5,7},{6,4},{7,5},{8,10},{9,11},{10,... | collective-permute-start | bytes 196616 | tf_op jit(solution)/shard_map/ppermute | solution.py:531
  28.7 1.6 %collective-permute-start.6 = (bf16[256,512]{1,0:T(8,128)(2,1)S(1)}, bf16[256,512]{1,0:T(8,128)(2,1)S(1)}, u32[]{:S(2)}, u32[]{:S(2)}) collective-permute-start(bf16[256,512]{1,0:T(8,128)(2,1)S(1)} %shard_map.105.refs_5_), channel_id=1, source_target_pairs={{0,1},{1,0},{2,3},{3,2},{4,5},{5,4},{6,7},{7,6},{8,9},{9,8},{10,11... | collective-permute-start | bytes 786440 | tf_op jit(solution)/shard_map/ppermute | solution.py:531
  28.8 2.8 %copy-start = (bf16[2048,768]{1,0:T(8,128)(2,1)S(1)}, bf16[2048,768]{1,0:T(8,128)(2,1)}, u32[]{:S(2)}) copy-start(bf16[2048,768]{1,0:T(8,128)(2,1)} %refs_0_.7) | copy-start | bytes 9437188
  28.8 2.8 %copy-start.5 = (f32[768]{0:T(1024)S(1)}, f32[768]{0:T(1024)}, u32[]{:S(2)}) copy-start(f32[768]{0:T(1024)} %refs_3_.3) | copy-start | bytes 9220
  33.8 7.9 %collective-permute-start.12 = (bf16[128,768]{1,0:T(8,128)(2,1)S(1)}, bf16[128,768]{1,0:T(8,128)(2,1)S(1)}, u32[]{:S(2)}, u32[]{:S(2)}) collective-permute-start(bf16[128,768]{1,0:T(8,128)(2,1)S(1)} %get-tuple-element.28.refs_0_), channel_id=1, source_target_pairs={{0,2},{1,3},{2,0},{3,1},{4,5},{5,4},{6,7},{7,6},{8,10},{9,11},{10,... | collective-permute-start | bytes 589832 | tf_op jit(solution)/shard_map/ppermute | solution.py:543
  34.2 7.7 %collective-permute-start.13 = (bf16[128,768]{1,0:T(8,128)(2,1)S(1)}, bf16[128,768]{1,0:T(8,128)(2,1)S(1)}, u32[]{:S(2)}, u32[]{:S(2)}) collective-permute-start(bf16[128,768]{1,0:T(8,128)(2,1)S(1)} %get-tuple-element.29.refs_1_), channel_id=1, source_target_pairs={{0,4},{1,5},{2,3},{3,2},{4,0},{5,1},{6,7},{7,6},{8,9},{9,8},{10,14... | collective-permute-start | bytes 589832 | tf_op jit(solution)/shard_map/ppermute | solution.py:543
  35.7 9.7 %collective-permute-start.14 = (bf16[128,768]{1,0:T(8,128)(2,1)S(1)}, bf16[128,768]{1,0:T(8,128)(2,1)S(1)}, u32[]{:S(2)}, u32[]{:S(2)}) collective-permute-start(bf16[128,768]{1,0:T(8,128)(2,1)S(1)} %get-tuple-element.28.refs_0_), channel_id=1, source_target_pairs={{0,4},{1,5},{2,3},{3,2},{4,0},{5,1},{6,7},{7,6},{8,9},{9,8},{10,14... | collective-permute-start | bytes 589832 | tf_op jit(solution)/shard_map/ppermute | solution.py:543
  36.2 9.2 %collective-permute-start.15 = (bf16[128,768]{1,0:T(8,128)(2,1)S(1)}, bf16[128,768]{1,0:T(8,128)(2,1)S(1)}, u32[]{:S(2)}, u32[]{:S(2)}) collective-permute-start(bf16[128,768]{1,0:T(8,128)(2,1)S(1)} %get-tuple-element.29.refs_1_), channel_id=1, source_target_pairs={{0,2},{1,3},{2,0},{3,1},{4,5},{5,4},{6,7},{7,6},{8,10},{9,11},{10,... | collective-permute-start | bytes 589832 | tf_op jit(solution)/shard_map/ppermute | solution.py:543
  41.7 3.7 %collective-permute-start.16 = (bf16[128,768]{1,0:T(8,128)(2,1)S(1)}, bf16[128,768]{1,0:T(8,128)(2,1)S(1)}, u32[]{:S(2)}, u32[]{:S(2)}) collective-permute-start(bf16[128,768]{1,0:T(8,128)(2,1)S(1)} %collective-permute-done.12.refs_2_), channel_id=1, source_target_pairs={{0,1},{1,0},{2,6},{3,7},{4,5},{5,4},{6,2},{7,3},{8,12},{9,13},{10,... | collective-permute-start | bytes 589832 | tf_op jit(solution)/shard_map/ppermute | solution.py:543
  41.9 3.5 %collective-permute-start.17 = (bf16[128,768]{1,0:T(8,128)(2,1)S(1)}, bf16[128,768]{1,0:T(8,128)(2,1)S(1)}, u32[]{:S(2)}, u32[]{:S(2)}) collective-permute-start(bf16[128,768]{1,0:T(8,128)(2,1)S(1)} %collective-permute-done.13.refs_3_), channel_id=1, source_target_pairs={{0,1},{1,0},{2,3},{3,2},{4,6},{5,7},{6,4},{7,5},{8,9},{9,8},{10,11... | collective-permute-start | bytes 589832 | tf_op jit(solution)/shard_map/ppermute | solution.py:543
  42.8 5.0 %copy-start.1 = (bf16[1536,768]{1,0:T(8,128)(2,1)S(1)}, bf16[1536,768]{1,0:T(8,128)(2,1)}, u32[]{:S(2)}) copy-start(bf16[1536,768]{1,0:T(8,128)(2,1)} %refs_1_.3) | copy-start | bytes 7077892
  46.0 1.8 %collective-permute-start.18 = (bf16[256,768]{1,0:T(8,128)(2,1)S(1)}, bf16[256,768]{1,0:T(8,128)(2,1)S(1)}, u32[]{:S(2)}, u32[]{:S(2)}) collective-permute-start(bf16[256,768]{1,0:T(8,128)(2,1)S(1)} %shard_map.109.refs_3_), channel_id=1, source_target_pairs={{0,1},{1,0},{2,3},{3,2},{4,5},{5,4},{6,7},{7,6},{8,9},{9,8},{10,11... | collective-permute-start | bytes 1179656 | tf_op jit(solution)/shard_map/ppermute | solution.py:531
  51.0 1.4 %collective-permute-start.19 = (bf16[128,411]{1,0:T(8,128)(2,1)S(1)}, bf16[128,411]{1,0:T(8,128)(2,1)S(1)}, u32[]{:S(2)}, u32[]{:S(2)}) collective-permute-start(bf16[128,411]{1,0:T(8,128)(2,1)S(1)} %get-tuple-element.33), channel_id=1, source_target_pairs={{0,1},{1,0},{2,3},{3,2},{4,5},{5,4},{6,7},{7,6},{8,9},{9,8},{10,11... | collective-permute-start | bytes 315656 | tf_op jit(solution)/shard_map/ppermute | solution.py:531
  52.6 7.8 %collective-permute-start.20 = (bf16[40,411]{1,0:T(8,128)(2,1)S(1)}, bf16[40,411]{1,0:T(8,128)(2,1)S(1)}, u32[]{:S(2)}, u32[]{:S(2)}) collective-permute-start(bf16[40,411]{1,0:T(8,128)(2,1)S(1)} %get-tuple-element.35), channel_id=1, source_target_pairs={{0,8},{8,16},{16,24},{24,0},{1,9},{9,17},{17,25},{25,1},{2,10},{10... | collective-permute-start | bytes 98648 | tf_op jit(solution)/shard_map/ppermute | solution.py:534
  55.1 6.3 %collective-permute-start.21 = (bf16[40,411]{1,0:T(8,128)(2,1)S(1)}, bf16[40,411]{1,0:T(8,128)(2,1)S(1)}, u32[]{:S(2)}, u32[]{:S(2)}) collective-permute-start(bf16[40,411]{1,0:T(8,128)(2,1)S(1)} %get-tuple-element.36), channel_id=1, source_target_pairs={{0,16},{8,24},{16,0},{24,8},{1,17},{9,25},{17,1},{25,9},{2,18},{10... | collective-permute-start | bytes 98648 | tf_op jit(solution)/shard_map/ppermute | solution.py:534
  58.5 4.0 %collective-permute-start.22 = (bf16[40,411]{1,0:T(8,128)(2,1)S(1)}, bf16[40,411]{1,0:T(8,128)(2,1)S(1)}, u32[]{:S(2)}, u32[]{:S(2)}) collective-permute-start(bf16[40,411]{1,0:T(8,128)(2,1)S(1)} %get-tuple-element.37), channel_id=1, source_target_pairs={{0,24},{8,0},{16,8},{24,16},{1,25},{9,1},{17,9},{25,17},{2,26},{10... | collective-permute-start | bytes 98648 | tf_op jit(solution)/shard_map/ppermute | solution.py:534
  62.8 4.2 %collective-permute-start.23 = (bf16[40,411]{1,0:T(8,128)(2,1)S(1)}, bf16[40,411]{1,0:T(8,128)(2,1)S(1)}, u32[]{:S(2)}, u32[]{:S(2)}) collective-permute-start(bf16[40,411]{1,0:T(8,128)(2,1)S(1)} %get-tuple-element.39), channel_id=1, source_target_pairs={{0,2},{1,3},{2,0},{3,1},{4,6},{5,7},{6,4},{7,5},{8,10},{9,11},{10,... | collective-permute-start | bytes 98648 | tf_op jit(solution)/shard_map/ppermute | solution.py:531
  63.7 4.4 %collective-permute-start.24 = (bf16[40,411]{1,0:T(8,128)(2,1)S(1)}, bf16[40,411]{1,0:T(8,128)(2,1)S(1)}, u32[]{:S(2)}, u32[]{:S(2)}) collective-permute-start(bf16[40,411]{1,0:T(8,128)(2,1)S(1)} %get-tuple-element.40), channel_id=1, source_target_pairs={{0,4},{1,5},{2,6},{3,7},{4,0},{5,1},{6,2},{7,3},{8,12},{9,13},{10,... | collective-permute-start | bytes 98648 | tf_op jit(solution)/shard_map/ppermute | solution.py:531
  64.5 4.9 %collective-permute-start.25 = (bf16[40,411]{1,0:T(8,128)(2,1)S(1)}, bf16[40,411]{1,0:T(8,128)(2,1)S(1)}, u32[]{:S(2)}, u32[]{:S(2)}) collective-permute-start(bf16[40,411]{1,0:T(8,128)(2,1)S(1)} %get-tuple-element.41), channel_id=1, source_target_pairs={{0,6},{1,7},{2,4},{3,5},{4,2},{5,3},{6,0},{7,1},{8,14},{9,15},{10,... | collective-permute-start | bytes 98648 | tf_op jit(solution)/shard_map/ppermute | solution.py:531
  69.4 1.3 %collective-permute-start.26 = (f32[40,411]{1,0:T(8,128)S(1)}, f32[40,411]{1,0:T(8,128)S(1)}, u32[]{:S(2)}, u32[]{:S(2)}) collective-permute-start(f32[40,411]{1,0:T(8,128)S(1)} %shard_map.113.refs_0_), channel_id=1, source_target_pairs={{0,1},{1,0},{2,3},{3,2},{4,5},{5,4},{6,7},{7,6},{8,9},{9,8},{10,11... | collective-permute-start | bytes 197288 | tf_op jit(solution)/shard_map/ppermute | solution.py:531

commit v8 on v7

--- a/solution.py
+++ b/solution.py
@@ -322,7 +322,7 @@
     refs = list(refs)
     take = lambda n: [refs.pop(0) for _ in range(n)]
     place_ref, source_ref, cell_ref, bias_ref, w_radiance_ref = take(5)
-    strip_refs, weight_refs, seen_refs = take(p.group), take(p.group), take(2)
+    strip_refs, weight_refs, seen_refs = take(p.group), take(p.group), take(p.tiles)
     part_refs = take(p.steps)
     preact_ref, kappa_ref, active = refs
     c = lax.axis_index("chan")
@@ -376,24 +376,22 @@
         slope_ref[k] = (squash * (1.0 + preact * (1.0 - squash))).T
 
 
-def choose_kernel(p, choices, *refs):
-    refs, out_ref, sems = refs[:-3], refs[-2], refs[-1]
-    size = refs[0].shape[0]
+def choose_kernel(p, early, count, *refs):
+    refs, out_ref, sems = refs[: 2 * count], refs[-2], refs[-1]
+    size = out_ref.shape[0] // count
     role = (lax.axis_index("chan") // p.group) ^ lax.axis_index("tile")
-    for place in range(p.chips):
-
-        @pl.when(role == place)
-        def _():
-            copies = [
-                pltpu.make_async_copy(
-                    refs[choices[place, j]], out_ref.at[pl.ds(j * size, size)], sems.at[j]
-                )
-                for j in range(p.steps)
-            ]
-            for copy in copies:
-                copy.start()
-            for copy in copies:
-                copy.wait()
+    for j in range(count):
+        held = (role & ~early[j]) == 0
+        for ref, wanted in ((refs[2 * j], held), (refs[2 * j + 1], ~held)):
+
+            @pl.when(wanted)
+            def _():
+                pltpu.make_async_copy(ref, out_ref.at[pl.ds(j * size, size)], sems.at[j]).start()
+
+    for j in range(count):
+        pltpu.make_async_copy(
+            refs[2 * j], out_ref.at[pl.ds(j * size, size)], sems.at[j]
+        ).wait()
 
 
 def backward_kernel(p, *refs):
@@ -437,7 +435,7 @@
     total = add(ins).astype(jnp.bfloat16)
     row, along = rows_and_cells(p, outs[0].shape[0])
     for k, out_ref in enumerate(outs):
-        tile = (lax.axis_index("tile") + k) % p.tiles
+        tile = lax.axis_index("tile") ^ k
         cell = (tile * p.own_cols + along + p.tiles * p.own_cols) % (p.tiles * p.own_cols)
         wanted = (cell // p.own_cols * p.rows_each + row) * p.own_cols + cell % p.own_cols
         out_ref[...] = dot(one_hot(wanted, 0, total.shape[0]), total).astype(jnp.bfloat16)
@@ -530,8 +528,8 @@
     def flip(value, mask):
         return lax.ppermute(value, "chan", [(b, b ^ mask) for b in range(p.chans)])
 
-    def shift(value, by):
-        return lax.ppermute(value, "tile", [(a, (a + by) % p.tiles) for a in range(p.tiles)])
+    def trade(value, mask):
+        return lax.ppermute(value, "tile", [(a, a ^ mask) for a in range(p.tiles)])
 
     def send(value, wanted):
         pairs = dict(wanted)
@@ -554,12 +552,6 @@
             scratch=[pltpu.SemaphoreType.DMA((len(values),))],
             flops=0,
         )
-
-    def grow(value, over, after=()):
-        return join([value, over(value)], (2 * value.shape[0],) + value.shape[1:], after)
-
-    def trade(value, mask):
-        return lax.ppermute(value, "tile", [(a, a ^ mask) for a in range(p.tiles)])
 
     strips = call(
         functools.partial(prepare_kernel, p),
@@ -578,33 +570,39 @@
         ],
         vmem=WHOLE_VMEM_BYTES,
     )
-    seen, stages = observed, []
-    bit = 1
+    _, layer, held = lax.optimization_barrier((strips, w_hidden, observed))
+    held, bit = [held], 1
+    while 2 * bit < p.tiles:
+        held += [trade(value, bit) for value in held]
+        bit *= 2
+    wanted = {(b // p.group ^ bit, b): (b // p.group, b) for b in range(p.chans)}
+    far = [send(value, wanted) for value in held]
+    seen = [observed] + held[1:] + far
+
+    near = [w_hidden] + [flip(layer, chip * p.group) for chip in range(1, p.chips - 1)]
+    bit, before = 1, held[1:] + far[:1]
     while bit < p.tiles:
-        if 2 * bit < p.tiles:
-            seen = grow(seen, lambda value: trade(value, bit))
-        strips = grow(strips, lambda value: trade(value, bit), [seen] if bit == 1 else ())
-        stages.append(strips)
-        bit *= 2
-    strips = join(
-        [strips] + [flip(strips, k * p.group) for k in range(1, p.chips)], (p.strips, p.width)
-    )
-    strips = [strips] + [flip(strips, k) for k in range(1, p.group)]
-
-    near = [w_hidden] + [flip(w_hidden, chip * p.group) for chip in range(1, p.chips)]
+        strips = join(
+            [strips, trade(strips, bit)], (2 * strips.shape[0], p.width), before
+        )
+        if bit == 1:
+            _, layer = lax.optimization_barrier((strips, layer))
+            near.append(flip(layer, (p.chips - 1) * p.group))
+        bit, before = 2 * bit, ()
+
     near = call(
         functools.partial(stack_kernel, p),
         shape((p.chips * p.deep, p.hidden), half),
-        near + [stages[-1]],
+        near + [strips],
         in_hbm=[len(near)],
     )
     weights = [near] + [flip(near, k) for k in range(1, p.group)]
-
-    far_half = p.tiles // 2
-    seen = [
-        seen,
-        send(seen, {(b // p.group ^ far_half, b): (b // p.group, b) for b in range(p.chans)}),
-    ]
+    strips = join(
+        [strips] + [flip(strips, k * p.group) for k in range(1, p.chips)],
+        (p.strips, p.width),
+        far[1:],
+    )
+    strips = [strips] + [flip(strips, k) for k in range(1, p.group)]
 
     reach = p.across + 4
     place, source, cell, *targets = call(
@@ -631,35 +629,31 @@
         flops=40 * preact.size,
     )
 
-    pool, held, choices = list(parts), {}, {}
-    for j in range(p.steps):
-        held[0, j] = choices[0, j] = j
+    def choose(pairs, early, after=()):
+        values = [value for pair in pairs for value in pair]
+        return call(
+            functools.partial(choose_kernel, p, early, len(pairs)),
+            shape((len(pairs) * values[0].shape[0], p.shard), half),
+            [*values, *after],
+            in_hbm=range(len(values) + len(after)),
+            out_hbm=True,
+            scratch=[pltpu.SemaphoreType.DMA((len(pairs),))],
+        )
+
+    held = [(part, None, 0) for part in parts]
     for step in range(p.steps):
-        for since in range(-1, step):
-            for j in range(p.steps):
-                order = [1 << (j + k) % p.steps for k in range(p.steps)]
-                roles = [0] if since < 0 else [
-                    order[since] + rest
-                    for rest in range(p.chips)
-                    if rest & ~sum(order[:since]) == 0
-                ]
-                wanted = {
-                    (a, b): (a, b ^ order[step] * p.group)
-                    for a, b in everyone
-                    if (b // p.group ^ a) in roles
-                }
-                source = pool[choices[roles[0], j]]
-                for role in roles:
-                    choices[role + order[step], j] = len(pool)
-                pool.append(send(source, wanted))
-    chosen = call(
-        functools.partial(choose_kernel, p, choices),
-        shape((p.rows, p.shard), half),
-        pool + [slope],
-        in_hbm=range(len(pool) + 1),
-        out_hbm=True,
-        scratch=[pltpu.SemaphoreType.DMA((p.steps,))],
-    )
+        for j, (part, arrived, early) in enumerate(held):
+            bit = 1 << (j + step) % p.steps
+            if arrived is not None:
+                reached = early | 1 << (j + step - 1) % p.steps
+                part, early = choose([(part, arrived)], [early]), reached
+            wanted = {
+                (a, b): (a, b ^ bit * p.group)
+                for a, b in everyone
+                if (b // p.group ^ a) & ~early == 0
+            }
+            held[j] = part, send(part, wanted), early
+    chosen = choose([pair[:2] for pair in held], [pair[2] for pair in held], [slope])
     depart = [chosen] + [flip(chosen, k) for k in range(1, p.group)]
 
     partial = call(
@@ -674,7 +668,7 @@
         [shape((p.rows_each * p.per_row, p.features), half)] * p.tiles,
         partial,
     )
-    partial = [partial[0]] + [shift(partial[k], k) for k in range(1, p.tiles)]
+    partial = [partial[0]] + [trade(partial[k], k) for k in range(1, p.tiles)]
     partial = call(
         functools.partial(add_tiles_kernel, p),
         [shape((p.around, p.features), half)] * p.chips,

time: 72.3 us -> 79.9 us (1.11)
  waiting for transfers between devices: 27.3 us -> 37.2 us
  starting transfers between devices: 30.1 us -> 28.2 us
    ppermute x3 -> x0, starting transfers between devices: 7.75 us -> none  [shift(): lax.ppermute(value, 'tile', [(a, (a + by) % p.tiles) for a in range(p.til...]
    ppermute x3 -> x6, waiting for transfers between devices: 4.67 us -> 11.9 us  [trade(): return lax.ppermute(value, 'tile', [(a, a ^ mask) for a in range(p.tiles)])]
    ppermute x3 -> x6, starting transfers between devices: 5.82 us -> 10.5 us  [trade(): return lax.ppermute(value, 'tile', [(a, a ^ mask) for a in range(p.tiles)])]
    ppermute x7 -> x6, waiting for transfers between devices: 9.41 us -> 12.1 us  [send(): lax.ppermute(value, both, sorted(((number(a), number(b)) for a, b in pair...]
    ppermute x3 -> x0, waiting for transfers between devices: 2.08 us -> none  [shift(): lax.ppermute(value, 'tile', [(a, (a + by) % p.tiles) for a in range(p.til...]
    ppermute x14, waiting for transfers between devices: 11.2 us -> 13.2 us  [flip(): return lax.ppermute(value, 'chan', [(b, b ^ mask) for b in range(p.chans)])]
    ppermute x7 -> x6, starting transfers between devices: 5.53 us -> 7.45 us  [send(): lax.ppermute(value, both, sorted(((number(a), number(b)) for a, b in pair...]
    ppermute x14, starting transfers between devices: 11 us -> 10.2 us  [flip(): return lax.ppermute(value, 'chan', [(b, b ^ mask) for b in range(p.chans)])]
  transfers between devices with their start and end apart: 27 -> 26, of which waited for: 18 -> 18; matrix products, arithmetic and copies ran while one was open for 0% -> 0% of each run, Pallas kernels for 5% -> 3%
where the time goes in v8:
time: 79.9 us; the launch traced here: 79.6 us
  waiting for transfers between devices  37.2 us (47%)
  starting transfers between devices  28.2 us (35%)
  Pallas kernels  11.7 us (15%)
  local copies, waits for them, and re-layouts  2.21 us (3%)
    ppermute x14, waiting for transfers between devices, flip(): return lax.ppermute(value, 'chan', [(b, b ^ mask) for b in range(p.chans)])  13.2 us
    ppermute x6, waiting for transfers between devices, send(): lax.ppermute(value, both, sorted(((number(a), number(b)) for a, b in pair...  12.1 us
    ppermute x6, waiting for transfers between devices, trade(): return lax.ppermute(value, 'tile', [(a, a ^ mask) for a in range(p.tiles)])  11.9 us
    pallas_call x16, Pallas kernels, call(): pl.pallas_call(kernel, out_shape=out_shape, in_specs=[far if k in in_hbm...  11.7 us
    ppermute x6, starting transfers between devices, trade(): return lax.ppermute(value, 'tile', [(a, a ^ mask) for a in range(p.tiles)])  10.5 us
    ppermute x14, starting transfers between devices, flip(): return lax.ppermute(value, 'chan', [(b, b ^ mask) for b in range(p.chans)])  10.2 us
    ppermute x6, starting transfers between devices, send(): lax.ppermute(value, both, sorted(((number(a), number(b)) for a, b in pair...  7.45 us
    unnamed x14, local copies, waits for them, and re-layouts  2.05 us
  transfers between devices with their start and end apart: 26, of which 18 were waited for; matrix products, arithmetic and copies ran while one was open for 0% of the time, Pallas kernels for 3%

profile of v8, /device:TPU:0, one launch (start us, length us, event | category | flops | bytes accessed | tf_op | source)
XLA Modules:
  0.0 79.6 jit_solution(7783511693310862129)
XLA Ops:
  0.0 1.8 %shard_map.101.refs_0_ = bf16[16,512]{1,0:T(8,128)(2,1)} custom-call(f32[4,32,411]{2,1,0:T(8,128)} %refs_0_.3, f32[4,32]{1,0:T(4,128)} %refs_1_.2, s32[128]{0:T(128)} %refs_2_.1, f32[256]{0:T(256)} %refs_3_.2), custom_call_target="tpu_custom_call" | custom-call | bytes 212480 | tf_op jit(solution)/shard_map/pallas_call | solution.py:164
  1.8 4.1 %collective-permute-start.2 = (bf16[128,768]{1,0:T(8,128)(2,1)}, bf16[128,768]{1,0:T(8,128)(2,1)S(1)}, u32[]{:S(2)}, u32[]{:S(2)}) collective-permute-start(bf16[128,768]{1,0:T(8,128)(2,1)} %refs_9_.1), channel_id=1, source_target_pairs={{0,16},{1,17},{2,3},{3,2},{4,20},{5,21},{6,7},{7,6},{8,9},{9,8},{1... | collective-permute-start | bytes 589832 | tf_op jit(solution)/shard_map/ppermute | solution.py:541
  5.9 2.0 %collective-permute-start = (bf16[16,512]{1,0:T(8,128)(2,1)}, bf16[16,512]{1,0:T(8,128)(2,1)S(1)}, u32[]{:S(2)}, u32[]{:S(2)}) collective-permute-start(bf16[16,512]{1,0:T(8,128)(2,1)} %shard_map.101.refs_0_), channel_id=1, source_target_pairs={{0,8},{8,0},{16,24},{24,16},{1,9},{9,1},{17,25},{25,17},{2,10},{10... | collective-permute-start | bytes 49160 | tf_op jit(solution)/shard_map/ppermute | solution.py:532
  7.9 1.5 %collective-permute-start.10 = (bf16[411,256]{1,0:T(8,128)(2,1)}, bf16[411,256]{1,0:T(8,128)(2,1)S(1)}, u32[]{:S(2)}, u32[]{:S(2)}) collective-permute-start(bf16[411,256]{1,0:T(8,128)(2,1)} %refs_0_.4), channel_id=1, source_target_pairs={{0,4},{1,5},{2,6},{3,7},{4,0},{5,1},{6,2},{7,3},{8,12},{9,13},{10,... | collective-permute-start | bytes 631304 | tf_op jit(solution)/shard_map/ppermute | solution.py:529
  9.4 1.1 %collective-permute-start.9 = (bf16[411,256]{1,0:T(8,128)(2,1)}, bf16[411,256]{1,0:T(8,128)(2,1)S(1)}, u32[]{:S(2)}, u32[]{:S(2)}) collective-permute-start(bf16[411,256]{1,0:T(8,128)(2,1)} %refs_0_.4), channel_id=1, source_target_pairs={{0,2},{1,3},{2,0},{3,1},{4,6},{5,7},{6,4},{7,5},{8,10},{9,11},{10,... | collective-permute-start | bytes 631304 | tf_op jit(solution)/shard_map/ppermute | solution.py:529
  10.5 5.1 %collective-permute-done.refs_1_ = bf16[16,512]{1,0:T(8,128)(2,1)S(1)} collective-permute-done((bf16[16,512]{1,0:T(8,128)(2,1)}, bf16[16,512]{1,0:T(8,128)(2,1)S(1)}, u32[]{:S(2)}, u32[]{:S(2)}) %collective-permute-start) | collective-permute-done | bytes 16416 | tf_op jit(solution)/shard_map/ppermute | solution.py:532
  15.6 0.7 copy-done.4
  16.3 0.1 collective-permute-start.11
  16.4 4.1 %collective-permute-start.3 = (bf16[32,512]{1,0:T(8,128)(2,1)S(1)}, bf16[32,512]{1,0:T(8,128)(2,1)S(1)}, u32[]{:S(2)}, u32[]{:S(2)}) collective-permute-start(bf16[32,512]{1,0:T(8,128)(2,1)S(1)} %shard_map.102.refs_0_), channel_id=1, source_target_pairs={{0,16},{8,24},{16,0},{24,8},{1,17},{9,25},{17,1},{25,9},{2,18},{10... | collective-permute-start | bytes 98312 | tf_op jit(solution)/shard_map/ppermute | solution.py:532
  20.5 1.9 %collective-permute-done.3.refs_1_ = bf16[32,512]{1,0:T(8,128)(2,1)S(1)} collective-permute-done((bf16[32,512]{1,0:T(8,128)(2,1)S(1)}, bf16[32,512]{1,0:T(8,128)(2,1)S(1)}, u32[]{:S(2)}, u32[]{:S(2)}) %collective-permute-start.3) | collective-permute-done | bytes 32800 | tf_op jit(solution)/shard_map/ppermute | solution.py:532
  22.4 0.1 shard_map.103.refs_0_.refs_4_
  22.5 2.2 %collective-permute-done.11.refs_3_ = bf16[411,256]{1,0:T(8,128)(2,1)S(1)} collective-permute-done((bf16[411,256]{1,0:T(8,128)(2,1)}, bf16[411,256]{1,0:T(8,128)(2,1)S(1)}, u32[]{:S(2)}, u32[]{:S(2)}) %collective-permute-start.11) | collective-permute-done | bytes 210464 | tf_op jit(solution)/shard_map/ppermute | solution.py:529
  24.7 0.9 %copy-done.2 = bf16[411,256]{1,0:T(8,128)(2,1)S(1)} copy-done((bf16[411,256]{1,0:T(8,128)(2,1)S(1)}, bf16[411,256]{1,0:T(8,128)(2,1)}, u32[]{:S(2)}) %copy-start.2) | copy-done | bytes 210456
  25.6 0.1 shard_map.105.refs_7_.refs_5_
  25.7 0.1 collective-permute-start.12
  25.8 0.8 collective-permute-start.7
  26.6 1.6 %collective-permute-start.5 = (bf16[64,512]{1,0:T(8,128)(2,1)S(1)}, bf16[64,512]{1,0:T(8,128)(2,1)S(1)}, u32[]{:S(2)}, u32[]{:S(2)}) collective-permute-start(bf16[64,512]{1,0:T(8,128)(2,1)S(1)} %shard_map.103.refs_0_.refs_4_), channel_id=1, source_target_pairs={{0,4},{1,5},{2,6},{3,7},{4,0},{5,1},{6,2},{7,3},{8,12},{9,13},{10,... | collective-permute-start | bytes 196616 | tf_op jit(solution)/shard_map/ppermute | solution.py:529
  28.1 1.9 %collective-permute-start.4 = (bf16[64,512]{1,0:T(8,128)(2,1)S(1)}, bf16[64,512]{1,0:T(8,128)(2,1)S(1)}, u32[]{:S(2)}, u32[]{:S(2)}) collective-permute-start(bf16[64,512]{1,0:T(8,128)(2,1)S(1)} %shard_map.103.refs_0_.refs_4_), channel_id=1, source_target_pairs={{0,2},{1,3},{2,0},{3,1},{4,6},{5,7},{6,4},{7,5},{8,10},{9,11},{10,... | collective-permute-start | bytes 196616 | tf_op jit(solution)/shard_map/ppermute | solution.py:529
  30.1 2.3 %collective-permute-done.6.refs_3_ = bf16[64,512]{1,0:T(8,128)(2,1)S(1)} collective-permute-done((bf16[64,512]{1,0:T(8,128)(2,1)S(1)}, bf16[64,512]{1,0:T(8,128)(2,1)S(1)}, u32[]{:S(2)}, u32[]{:S(2)}) %collective-permute-start.6) | collective-permute-done | bytes 65568 | tf_op jit(solution)/shard_map/ppermute | solution.py:529
  32.4 0.3 collective-permute-done.4.refs_1_
  32.7 1.3 %collective-permute-done.7.refs_4_.refs_12_ = bf16[128,768]{1,0:T(8,128)(2,1)S(1)} collective-permute-done((bf16[128,768]{1,0:T(8,128)(2,1)S(1)}, bf16[128,768]{1,0:T(8,128)(2,1)S(1)}, u32[]{:S(2)}, u32[]{:S(2)}) %collective-permute-start.7) | collective-permute-done | bytes 196640 | tf_op jit(solution)/shard_map/ppermute | solution.py:541
  34.0 0.3 shard_map.104.refs_5_
  34.4 0.1 collective-permute-start.8
  34.5 0.0 copy-start.3
  34.5 0.0 copy-start.5
  34.5 0.4 shard_map.100
  34.9 1.0 %collective-permute-done.8.refs_6_ = bf16[256,512]{1,0:T(8,128)(2,1)S(1)} collective-permute-done((bf16[256,512]{1,0:T(8,128)(2,1)S(1)}, bf16[256,512]{1,0:T(8,128)(2,1)S(1)}, u32[]{:S(2)}, u32[]{:S(2)}) %collective-permute-start.8) | collective-permute-done | bytes 262176 | tf_op jit(solution)/shard_map/ppermute | solution.py:529
  36.0 0.4 copy-done
  36.3 2.3 %shard_map.106 = (bf16[128,768]{1,0:T(8,128)(2,1)S(1)}, bf16[128,768]{1,0:T(8,128)(2,1)S(1)}, f32[8,256,256]{2,1,0:T(8,128)S(1)}, f32[24,128]{1,0:T(8,128)S(1)}) custom-call(s32[256,1]{1,0:T(8,128)S(1)} %get-tuple-element.27.refs_0_, s32[256,1]{1,0:T(8,128)S(1)} %get-tuple-element.28.refs_1_, s32[24,1]{1,0:T(8,128)S(1)} %get-tuple-element.29.refs_2_, ...), custom_call_target="tpu_custom_call" | custom-call | flops 1236271104 | bytes 6165600 | tf_op jit(solution)/shard_map/pallas_call | solution.py:164
  38.7 0.4 collective-permute-start.13
  39.1 1.7 %collective-permute-start.15 = (bf16[128,768]{1,0:T(8,128)(2,1)S(1)}, bf16[128,768]{1,0:T(8,128)(2,1)S(1)}, u32[]{:S(2)}, u32[]{:S(2)}) collective-permute-start(bf16[128,768]{1,0:T(8,128)(2,1)S(1)} %get-tuple-element.35.refs_0_), channel_id=1, source_target_pairs={{0,4},{1,5},{2,3},{3,2},{4,0},{5,1},{6,7},{7,6},{8,9},{9,8},{10,14... | collective-permute-start | bytes 589832 | tf_op jit(solution)/shard_map/ppermute | solution.py:541
  40.8 5.2 %collective-permute-done.13.refs_1_ = bf16[128,768]{1,0:T(8,128)(2,1)S(1)} collective-permute-done((bf16[128,768]{1,0:T(8,128)(2,1)S(1)}, bf16[128,768]{1,0:T(8,128)(2,1)S(1)}, u32[]{:S(2)}, u32[]{:S(2)}) %collective-permute-start.13) | collective-permute-done | bytes 196640 | tf_op jit(solution)/shard_map/ppermute | solution.py:541
  46.0 0.2 shard_map.108.refs_0_
  46.3 0.1 collective-permute-start.14
  46.4 0.3 shard_map.109.refs_2_
  46.6 0.4 collective-permute-start.16
  47.0 0.6 shard_map.107.refs_4_.refs_2_
  47.7 5.2 %collective-permute-done.14.refs_1_ = bf16[128,768]{1,0:T(8,128)(2,1)S(1)} collective-permute-done((bf16[128,768]{1,0:T(8,128)(2,1)S(1)}, bf16[128,768]{1,0:T(8,128)(2,1)S(1)}, u32[]{:S(2)}, u32[]{:S(2)}) %collective-permute-start.14) | collective-permute-done | bytes 196640 | tf_op jit(solution)/shard_map/ppermute | solution.py:541
  52.9 0.4 collective-permute-done.16.refs_3_
  53.2 0.5 shard_map.110.refs_3_
  53.8 0.1 collective-permute-start.17
  53.8 1.7 %collective-permute-done.17.refs_4_ = bf16[256,768]{1,0:T(8,128)(2,1)S(1)} collective-permute-done((bf16[256,768]{1,0:T(8,128)(2,1)S(1)}, bf16[256,768]{1,0:T(8,128)(2,1)S(1)}, u32[]{:S(2)}, u32[]{:S(2)}) %collective-permute-start.17) | collective-permute-done | bytes 393248 | tf_op jit(solution)/shard_map/ppermute | solution.py:529
  55.6 3.2 %shard_map.111 = (bf16[128,411]{1,0:T(8,128)(2,1)S(1)}, bf16[128,411]{1,0:T(8,128)(2,1)S(1)}) custom-call(bf16[2048,768]{1,0:T(8,128)(2,1)S(1)} %copy-done, bf16[1536,768]{1,0:T(8,128)(2,1)S(1)} %copy-done.1, f32[8,256,256]{2,1,0:T(8,128)S(1)} %shard_map.107.refs_4_.refs_2_, bf16[256,768]{1,0:T(8,128)(2,1)S(1)} %shard_map.110.refs_3_, ...), custom_call_target="tpu_custom_call" | custom-call | flops 1840250880 | bytes 10093568 | tf_op jit(solution)/shard_map/pallas_call | solution.py:164
  58.7 0.2 collective-permute-start.18
  58.9 1.2 %collective-permute-done.18.refs_1_ = bf16[128,411]{1,0:T(8,128)(2,1)S(1)} collective-permute-done((bf16[128,411]{1,0:T(8,128)(2,1)S(1)}, bf16[128,411]{1,0:T(8,128)(2,1)S(1)}, u32[]{:S(2)}, u32[]{:S(2)}) %collective-permute-start.18) | collective-permute-done | bytes 105248 | tf_op jit(solution)/shard_map/ppermute | solution.py:529
  60.1 0.3 shard_map.112
  60.4 1.7 %collective-permute-start.19 = (bf16[40,411]{1,0:T(8,128)(2,1)S(1)}, bf16[40,411]{1,0:T(8,128)(2,1)S(1)}, u32[]{:S(2)}, u32[]{:S(2)}) collective-permute-start(bf16[40,411]{1,0:T(8,128)(2,1)S(1)} %get-tuple-element.41), channel_id=1, source_target_pairs={{0,8},{8,0},{16,24},{24,16},{1,9},{9,1},{17,25},{25,17},{2,10},{10... | collective-permute-start | bytes 98648 | tf_op jit(solution)/shard_map/ppermute | solution.py:532
  62.1 2.0 %collective-permute-start.20 = (bf16[40,411]{1,0:T(8,128)(2,1)S(1)}, bf16[40,411]{1,0:T(8,128)(2,1)S(1)}, u32[]{:S(2)}, u32[]{:S(2)}) collective-permute-start(bf16[40,411]{1,0:T(8,128)(2,1)S(1)} %get-tuple-element.42), channel_id=1, source_target_pairs={{0,16},{8,24},{16,0},{24,8},{1,17},{9,25},{17,1},{25,9},{2,18},{10... | collective-permute-start | bytes 98648 | tf_op jit(solution)/shard_map/ppermute | solution.py:532
  64.1 0.8 collective-permute-start.21
  64.9 0.1 slice_bitcast_fusion.2
  64.9 2.6 %collective-permute-done.20.refs_2_ = bf16[40,411]{1,0:T(8,128)(2,1)S(1)} collective-permute-done((bf16[40,411]{1,0:T(8,128)(2,1)S(1)}, bf16[40,411]{1,0:T(8,128)(2,1)S(1)}, u32[]{:S(2)}, u32[]{:S(2)}) %collective-permute-start.20) | collective-permute-done | bytes 32912 | tf_op jit(solution)/shard_map/ppermute | solution.py:532
  67.6 2.3 %collective-permute-done.21.refs_3_ = bf16[40,411]{1,0:T(8,128)(2,1)S(1)} collective-permute-done((bf16[40,411]{1,0:T(8,128)(2,1)S(1)}, bf16[40,411]{1,0:T(8,128)(2,1)S(1)}, u32[]{:S(2)}, u32[]{:S(2)}) %collective-permute-start.21) | collective-permute-done | bytes 32912 | tf_op jit(solution)/shard_map/ppermute | solution.py:532
  69.9 0.2 shard_map.113
  70.1 1.6 %collective-permute-start.22 = (bf16[40,411]{1,0:T(8,128)(2,1)S(1)}, bf16[40,411]{1,0:T(8,128)(2,1)S(1)}, u32[]{:S(2)}, u32[]{:S(2)}) collective-permute-start(bf16[40,411]{1,0:T(8,128)(2,1)S(1)} %get-tuple-element.45), channel_id=1, source_target_pairs={{0,2},{1,3},{2,0},{3,1},{4,6},{5,7},{6,4},{7,5},{8,10},{9,11},{10,... | collective-permute-start | bytes 98648 | tf_op jit(solution)/shard_map/ppermute | solution.py:529
  71.7 0.3 collective-permute-start.23
  72.0 1.6 %collective-permute-start.24 = (bf16[40,411]{1,0:T(8,128)(2,1)S(1)}, bf16[40,411]{1,0:T(8,128)(2,1)S(1)}, u32[]{:S(2)}, u32[]{:S(2)}) collective-permute-start(bf16[40,411]{1,0:T(8,128)(2,1)S(1)} %get-tuple-element.47), channel_id=1, source_target_pairs={{0,6},{1,7},{2,4},{3,5},{4,2},{5,3},{6,0},{7,1},{8,14},{9,15},{10,... | collective-permute-start | bytes 98648 | tf_op jit(solution)/shard_map/ppermute | solution.py:529
  73.6 0.9 %collective-permute-done.22.refs_1_ = bf16[40,411]{1,0:T(8,128)(2,1)S(1)} collective-permute-done((bf16[40,411]{1,0:T(8,128)(2,1)S(1)}, bf16[40,411]{1,0:T(8,128)(2,1)S(1)}, u32[]{:S(2)}, u32[]{:S(2)}) %collective-permute-start.22) | collective-permute-done | bytes 32912 | tf_op jit(solution)/shard_map/ppermute | solution.py:529
  74.6 1.1 %collective-permute-done.23.refs_2_ = bf16[40,411]{1,0:T(8,128)(2,1)S(1)} collective-permute-done((bf16[40,411]{1,0:T(8,128)(2,1)S(1)}, bf16[40,411]{1,0:T(8,128)(2,1)S(1)}, u32[]{:S(2)}, u32[]{:S(2)}) %collective-permute-start.23) | collective-permute-done | bytes 32912 | tf_op jit(solution)/shard_map/ppermute | solution.py:529
  75.7 1.2 %collective-permute-done.24.refs_3_ = bf16[40,411]{1,0:T(8,128)(2,1)S(1)} collective-permute-done((bf16[40,411]{1,0:T(8,128)(2,1)S(1)}, bf16[40,411]{1,0:T(8,128)(2,1)S(1)}, u32[]{:S(2)}, u32[]{:S(2)}) %collective-permute-start.24) | collective-permute-done | bytes 32912 | tf_op jit(solution)/shard_map/ppermute | solution.py:529
  77.0 0.1 collective-permute-start.25
  77.0 0.1 maximum_sqrt_fusion
  77.1 0.1 copy.19
  77.2 1.1 %collective-permute-done.25.refs_1_ = f32[40,411]{1,0:T(8,128)S(1)} collective-permute-done((f32[40,411]{1,0:T(8,128)S(1)}, f32[40,411]{1,0:T(8,128)S(1)}, u32[]{:S(2)}, u32[]{:S(2)}) %collective-permute-start.25) | collective-permute-done | bytes 65792 | tf_op jit(solution)/shard_map/ppermute | solution.py:529
  78.3 1.3 %shard_map.115 = f32[4,32,411]{2,1,0:T(8,128)} custom-call(f32[40,411]{1,0:T(8,128)S(1)} %shard_map.114.refs_0_, f32[40,411]{1,0:T(8,128)S(1)} %collective-permute-done.25.refs_1_, f32[48,8]{1,0:T(8,128)S(1)} %bitcast.9), custom_call_target="tpu_custom_call" | custom-call | flops 5260800 | bytes 133056 | tf_op jit(solution)/shard_map/pallas_call | solution.py:164
  (22 shorter events, 0.1 us)
Async XLA Ops:
  0.0 34.4 %copy-start.6 = (s32[256,1]{0,1:T(1,128)S(1)}, s32[256,1]{0,1:T(1,128)}, u32[]{:S(2)}) copy-start(s32[256,1]{0,1:T(1,128)} %param.12) | copy-start | bytes 3076
  1.8 13.8 %collective-permute-start.2 = (bf16[128,768]{1,0:T(8,128)(2,1)}, bf16[128,768]{1,0:T(8,128)(2,1)S(1)}, u32[]{:S(2)}, u32[]{:S(2)}) collective-permute-start(bf16[128,768]{1,0:T(8,128)(2,1)} %refs_9_.1), channel_id=1, source_target_pairs={{0,16},{1,17},{2,3},{3,2},{4,20},{5,21},{6,7},{7,6},{8,9},{9,8},{1... | collective-permute-start | bytes 589832 | tf_op jit(solution)/shard_map/ppermute | solution.py:541
  5.9 9.7 %collective-permute-start.1 = (bf16[128,768]{1,0:T(8,128)(2,1)}, bf16[128,768]{1,0:T(8,128)(2,1)S(1)}, u32[]{:S(2)}, u32[]{:S(2)}) collective-permute-start(bf16[128,768]{1,0:T(8,128)(2,1)} %refs_9_.1), channel_id=1, source_target_pairs={{0,8},{8,0},{16,24},{24,16},{1,9},{9,1},{17,25},{25,17},{2,10},{10... | collective-permute-start | bytes 589832 | tf_op jit(solution)/shard_map/ppermute | solution.py:532
  5.9 9.7 %collective-permute-start = (bf16[16,512]{1,0:T(8,128)(2,1)}, bf16[16,512]{1,0:T(8,128)(2,1)S(1)}, u32[]{:S(2)}, u32[]{:S(2)}) collective-permute-start(bf16[16,512]{1,0:T(8,128)(2,1)} %shard_map.101.refs_0_), channel_id=1, source_target_pairs={{0,8},{8,0},{16,24},{24,16},{1,9},{9,1},{17,25},{25,17},{2,10},{10... | collective-permute-start | bytes 49160 | tf_op jit(solution)/shard_map/ppermute | solution.py:532
  7.9 14.5 %collective-permute-start.10 = (bf16[411,256]{1,0:T(8,128)(2,1)}, bf16[411,256]{1,0:T(8,128)(2,1)S(1)}, u32[]{:S(2)}, u32[]{:S(2)}) collective-permute-start(bf16[411,256]{1,0:T(8,128)(2,1)} %refs_0_.4), channel_id=1, source_target_pairs={{0,4},{1,5},{2,6},{3,7},{4,0},{5,1},{6,2},{7,3},{8,12},{9,13},{10,... | collective-permute-start | bytes 631304 | tf_op jit(solution)/shard_map/ppermute | solution.py:529
  9.4 13.0 %collective-permute-start.9 = (bf16[411,256]{1,0:T(8,128)(2,1)}, bf16[411,256]{1,0:T(8,128)(2,1)S(1)}, u32[]{:S(2)}, u32[]{:S(2)}) collective-permute-start(bf16[411,256]{1,0:T(8,128)(2,1)} %refs_0_.4), channel_id=1, source_target_pairs={{0,2},{1,3},{2,0},{3,1},{4,6},{5,7},{6,4},{7,5},{8,10},{9,11},{10,... | collective-permute-start | bytes 631304 | tf_op jit(solution)/shard_map/ppermute | solution.py:529
  15.6 0.7 copy-start.4
  16.3 8.3 %collective-permute-start.11 = (bf16[411,256]{1,0:T(8,128)(2,1)}, bf16[411,256]{1,0:T(8,128)(2,1)S(1)}, u32[]{:S(2)}, u32[]{:S(2)}) collective-permute-start(bf16[411,256]{1,0:T(8,128)(2,1)} %refs_0_.4), channel_id=1, source_target_pairs={{0,6},{1,7},{2,4},{3,5},{4,2},{5,3},{6,0},{7,1},{8,14},{9,15},{10,... | collective-permute-start | bytes 631304 | tf_op jit(solution)/shard_map/ppermute | solution.py:529
  16.4 5.9 %collective-permute-start.3 = (bf16[32,512]{1,0:T(8,128)(2,1)S(1)}, bf16[32,512]{1,0:T(8,128)(2,1)S(1)}, u32[]{:S(2)}, u32[]{:S(2)}) collective-permute-start(bf16[32,512]{1,0:T(8,128)(2,1)S(1)} %shard_map.102.refs_0_), channel_id=1, source_target_pairs={{0,16},{8,24},{16,0},{24,8},{1,17},{9,25},{17,1},{25,9},{2,18},{10... | collective-permute-start | bytes 98312 | tf_op jit(solution)/shard_map/ppermute | solution.py:532
  24.7 0.9 %copy-start.2 = (bf16[411,256]{1,0:T(8,128)(2,1)S(1)}, bf16[411,256]{1,0:T(8,128)(2,1)}, u32[]{:S(2)}) copy-start(bf16[411,256]{1,0:T(8,128)(2,1)} %refs_0_.4) | copy-start | bytes 631300
  25.7 10.3 %collective-permute-start.12 = (bf16[1664,256]{1,0:T(8,128)(2,1)S(1)}, bf16[1664,256]{1,0:T(8,128)(2,1)S(1)}, u32[]{:S(2)}, u32[]{:S(2)}) collective-permute-start(bf16[1664,256]{1,0:T(8,128)(2,1)S(1)} %shard_map.105.refs_7_.refs_5_), channel_id=1, source_target_pairs={{0,1},{1,0},{2,3},{3,2},{4,5},{5,4},{6,7},{7,6},{8,9},{9,8},{10,11... | collective-permute-start | bytes 2555912 | tf_op jit(solution)/shard_map/ppermute | solution.py:529
  25.8 8.2 %collective-permute-start.7 = (bf16[128,768]{1,0:T(8,128)(2,1)S(1)}, bf16[128,768]{1,0:T(8,128)(2,1)S(1)}, u32[]{:S(2)}, u32[]{:S(2)}) collective-permute-start(bf16[128,768]{1,0:T(8,128)(2,1)S(1)} %collective-permute-done.1.refs_2_.refs_10_), channel_id=1, source_target_pairs={{0,16},{1,17},{2,3},{3,2},{4,20},{5,21},{6,7},{7,6},{8,9},{9,8},{1... | collective-permute-start | bytes 589832 | tf_op jit(solution)/shard_map/ppermute | solution.py:541
  26.6 5.8 %collective-permute-start.6 = (bf16[64,512]{1,0:T(8,128)(2,1)S(1)}, bf16[64,512]{1,0:T(8,128)(2,1)S(1)}, u32[]{:S(2)}, u32[]{:S(2)}) collective-permute-start(bf16[64,512]{1,0:T(8,128)(2,1)S(1)} %shard_map.103.refs_0_.refs_4_), channel_id=1, source_target_pairs={{0,6},{1,7},{2,4},{3,5},{4,2},{5,3},{6,0},{7,1},{8,14},{9,15},{10,... | collective-permute-start | bytes 196616 | tf_op jit(solution)/shard_map/ppermute | solution.py:529
  26.6 5.8 %collective-permute-start.5 = (bf16[64,512]{1,0:T(8,128)(2,1)S(1)}, bf16[64,512]{1,0:T(8,128)(2,1)S(1)}, u32[]{:S(2)}, u32[]{:S(2)}) collective-permute-start(bf16[64,512]{1,0:T(8,128)(2,1)S(1)} %shard_map.103.refs_0_.refs_4_), channel_id=1, source_target_pairs={{0,4},{1,5},{2,6},{3,7},{4,0},{5,1},{6,2},{7,3},{8,12},{9,13},{10,... | collective-permute-start | bytes 196616 | tf_op jit(solution)/shard_map/ppermute | solution.py:529
  28.1 4.6 %collective-permute-start.4 = (bf16[64,512]{1,0:T(8,128)(2,1)S(1)}, bf16[64,512]{1,0:T(8,128)(2,1)S(1)}, u32[]{:S(2)}, u32[]{:S(2)}) collective-permute-start(bf16[64,512]{1,0:T(8,128)(2,1)S(1)} %shard_map.103.refs_0_.refs_4_), channel_id=1, source_target_pairs={{0,2},{1,3},{2,0},{3,1},{4,6},{5,7},{6,4},{7,5},{8,10},{9,11},{10,... | collective-permute-start | bytes 196616 | tf_op jit(solution)/shard_map/ppermute | solution.py:529
  34.4 1.6 %collective-permute-start.8 = (bf16[256,512]{1,0:T(8,128)(2,1)S(1)}, bf16[256,512]{1,0:T(8,128)(2,1)S(1)}, u32[]{:S(2)}, u32[]{:S(2)}) collective-permute-start(bf16[256,512]{1,0:T(8,128)(2,1)S(1)} %shard_map.104.refs_5_), channel_id=1, source_target_pairs={{0,1},{1,0},{2,3},{3,2},{4,5},{5,4},{6,7},{7,6},{8,9},{9,8},{10,11... | collective-permute-start | bytes 786440 | tf_op jit(solution)/shard_map/ppermute | solution.py:529
  34.4 1.9 %copy-start = (bf16[2048,768]{1,0:T(8,128)(2,1)S(1)}, bf16[2048,768]{1,0:T(8,128)(2,1)}, u32[]{:S(2)}) copy-start(bf16[2048,768]{1,0:T(8,128)(2,1)} %refs_0_.5) | copy-start | bytes 9437188
  34.5 1.9 %copy-start.3 = (bf16[128,768]{1,0:T(8,128)(2,1)S(1)}, bf16[128,768]{1,0:T(8,128)(2,1)}, u32[]{:S(2)}) copy-start(bf16[128,768]{1,0:T(8,128)(2,1)} %refs_9_.1) | copy-start | bytes 589828
  34.5 1.9 %copy-start.5 = (f32[768]{0:T(1024)S(1)}, f32[768]{0:T(1024)}, u32[]{:S(2)}) copy-start(f32[768]{0:T(1024)} %refs_3_.3) | copy-start | bytes 9220
  38.7 7.4 %collective-permute-start.13 = (bf16[128,768]{1,0:T(8,128)(2,1)S(1)}, bf16[128,768]{1,0:T(8,128)(2,1)S(1)}, u32[]{:S(2)}, u32[]{:S(2)}) collective-permute-start(bf16[128,768]{1,0:T(8,128)(2,1)S(1)} %get-tuple-element.34.refs_0_), channel_id=1, source_target_pairs={{0,2},{1,3},{2,0},{3,1},{4,5},{5,4},{6,7},{7,6},{8,10},{9,11},{10,... | collective-permute-start | bytes 589832 | tf_op jit(solution)/shard_map/ppermute | solution.py:541
  39.1 7.3 %collective-permute-start.15 = (bf16[128,768]{1,0:T(8,128)(2,1)S(1)}, bf16[128,768]{1,0:T(8,128)(2,1)S(1)}, u32[]{:S(2)}, u32[]{:S(2)}) collective-permute-start(bf16[128,768]{1,0:T(8,128)(2,1)S(1)} %get-tuple-element.35.refs_0_), channel_id=1, source_target_pairs={{0,4},{1,5},{2,3},{3,2},{4,0},{5,1},{6,7},{7,6},{8,9},{9,8},{10,14... | collective-permute-start | bytes 589832 | tf_op jit(solution)/shard_map/ppermute | solution.py:541
  46.3 6.6 %collective-permute-start.14 = (bf16[128,768]{1,0:T(8,128)(2,1)S(1)}, bf16[128,768]{1,0:T(8,128)(2,1)S(1)}, u32[]{:S(2)}, u32[]{:S(2)}) collective-permute-start(bf16[128,768]{1,0:T(8,128)(2,1)S(1)} %shard_map.108.refs_0_), channel_id=1, source_target_pairs={{0,4},{1,5},{2,6},{3,7},{4,0},{5,1},{6,2},{7,3},{8,12},{9,13},{10,... | collective-permute-start | bytes 589832 | tf_op jit(solution)/shard_map/ppermute | solution.py:541
  46.6 6.6 %collective-permute-start.16 = (bf16[128,768]{1,0:T(8,128)(2,1)S(1)}, bf16[128,768]{1,0:T(8,128)(2,1)S(1)}, u32[]{:S(2)}, u32[]{:S(2)}) collective-permute-start(bf16[128,768]{1,0:T(8,128)(2,1)S(1)} %shard_map.109.refs_2_), channel_id=1, source_target_pairs={{0,2},{1,3},{2,0},{3,1},{4,6},{5,7},{6,4},{7,5},{8,10},{9,11},{10,... | collective-permute-start | bytes 589832 | tf_op jit(solution)/shard_map/ppermute | solution.py:541
  47.6 7.9 %copy-start.1 = (bf16[1536,768]{1,0:T(8,128)(2,1)S(1)}, bf16[1536,768]{1,0:T(8,128)(2,1)}, u32[]{:S(2)}) copy-start(bf16[1536,768]{1,0:T(8,128)(2,1)} %refs_1_.3) | copy-start | bytes 7077892
  53.8 1.8 %collective-permute-start.17 = (bf16[256,768]{1,0:T(8,128)(2,1)S(1)}, bf16[256,768]{1,0:T(8,128)(2,1)S(1)}, u32[]{:S(2)}, u32[]{:S(2)}) collective-permute-start(bf16[256,768]{1,0:T(8,128)(2,1)S(1)} %shard_map.110.refs_3_), channel_id=1, source_target_pairs={{0,1},{1,0},{2,3},{3,2},{4,5},{5,4},{6,7},{7,6},{8,9},{9,8},{10,11... | collective-permute-start | bytes 1179656 | tf_op jit(solution)/shard_map/ppermute | solution.py:529
  58.7 1.4 %collective-permute-start.18 = (bf16[128,411]{1,0:T(8,128)(2,1)S(1)}, bf16[128,411]{1,0:T(8,128)(2,1)S(1)}, u32[]{:S(2)}, u32[]{:S(2)}) collective-permute-start(bf16[128,411]{1,0:T(8,128)(2,1)S(1)} %get-tuple-element.39), channel_id=1, source_target_pairs={{0,1},{1,0},{2,3},{3,2},{4,5},{5,4},{6,7},{7,6},{8,9},{9,8},{10,11... | collective-permute-start | bytes 315656 | tf_op jit(solution)/shard_map/ppermute | solution.py:529
  60.4 4.5 %collective-permute-start.19 = (bf16[40,411]{1,0:T(8,128)(2,1)S(1)}, bf16[40,411]{1,0:T(8,128)(2,1)S(1)}, u32[]{:S(2)}, u32[]{:S(2)}) collective-permute-start(bf16[40,411]{1,0:T(8,128)(2,1)S(1)} %get-tuple-element.41), channel_id=1, source_target_pairs={{0,8},{8,0},{16,24},{24,16},{1,9},{9,1},{17,25},{25,17},{2,10},{10... | collective-permute-start | bytes 98648 | tf_op jit(solution)/shard_map/ppermute | solution.py:532
  62.1 5.5 %collective-permute-start.20 = (bf16[40,411]{1,0:T(8,128)(2,1)S(1)}, bf16[40,411]{1,0:T(8,128)(2,1)S(1)}, u32[]{:S(2)}, u32[]{:S(2)}) collective-permute-start(bf16[40,411]{1,0:T(8,128)(2,1)S(1)} %get-tuple-element.42), channel_id=1, source_target_pairs={{0,16},{8,24},{16,0},{24,8},{1,17},{9,25},{17,1},{25,9},{2,18},{10... | collective-permute-start | bytes 98648 | tf_op jit(solution)/shard_map/ppermute | solution.py:532
  64.1 5.8 %collective-permute-start.21 = (bf16[40,411]{1,0:T(8,128)(2,1)S(1)}, bf16[40,411]{1,0:T(8,128)(2,1)S(1)}, u32[]{:S(2)}, u32[]{:S(2)}) collective-permute-start(bf16[40,411]{1,0:T(8,128)(2,1)S(1)} %get-tuple-element.43), channel_id=1, source_target_pairs={{0,24},{8,16},{16,8},{24,0},{1,25},{9,17},{17,9},{25,1},{2,26},{10... | collective-permute-start | bytes 98648 | tf_op jit(solution)/shard_map/ppermute | solution.py:532
  70.1 4.5 %collective-permute-start.22 = (bf16[40,411]{1,0:T(8,128)(2,1)S(1)}, bf16[40,411]{1,0:T(8,128)(2,1)S(1)}, u32[]{:S(2)}, u32[]{:S(2)}) collective-permute-start(bf16[40,411]{1,0:T(8,128)(2,1)S(1)} %get-tuple-element.45), channel_id=1, source_target_pairs={{0,2},{1,3},{2,0},{3,1},{4,6},{5,7},{6,4},{7,5},{8,10},{9,11},{10,... | collective-permute-start | bytes 98648 | tf_op jit(solution)/shard_map/ppermute | solution.py:529
  71.7 4.0 %collective-permute-start.23 = (bf16[40,411]{1,0:T(8,128)(2,1)S(1)}, bf16[40,411]{1,0:T(8,128)(2,1)S(1)}, u32[]{:S(2)}, u32[]{:S(2)}) collective-permute-start(bf16[40,411]{1,0:T(8,128)(2,1)S(1)} %get-tuple-element.46), channel_id=1, source_target_pairs={{0,4},{1,5},{2,6},{3,7},{4,0},{5,1},{6,2},{7,3},{8,12},{9,13},{10,... | collective-permute-start | bytes 98648 | tf_op jit(solution)/shard_map/ppermute | solution.py:529
  72.0 4.9 %collective-permute-start.24 = (bf16[40,411]{1,0:T(8,128)(2,1)S(1)}, bf16[40,411]{1,0:T(8,128)(2,1)S(1)}, u32[]{:S(2)}, u32[]{:S(2)}) collective-permute-start(bf16[40,411]{1,0:T(8,128)(2,1)S(1)} %get-tuple-element.47), channel_id=1, source_target_pairs={{0,6},{1,7},{2,4},{3,5},{4,2},{5,3},{6,0},{7,1},{8,14},{9,15},{10,... | collective-permute-start | bytes 98648 | tf_op jit(solution)/shard_map/ppermute | solution.py:529
  77.0 1.3 %collective-permute-start.25 = (f32[40,411]{1,0:T(8,128)S(1)}, f32[40,411]{1,0:T(8,128)S(1)}, u32[]{:S(2)}, u32[]{:S(2)}) collective-permute-start(f32[40,411]{1,0:T(8,128)S(1)} %shard_map.114.refs_0_), channel_id=1, source_target_pairs={{0,1},{1,0},{2,3},{3,2},{4,5},{5,4},{6,7},{7,6},{8,9},{9,8},{10,11... | collective-permute-start | bytes 197288 | tf_op jit(solution)/shard_map/ppermute | solution.py:529

commit v9 on v7

--- a/solution.py
+++ b/solution.py
@@ -322,7 +322,7 @@
     refs = list(refs)
     take = lambda n: [refs.pop(0) for _ in range(n)]
     place_ref, source_ref, cell_ref, bias_ref, w_radiance_ref = take(5)
-    strip_refs, weight_refs, seen_refs = take(p.group), take(p.group), take(2)
+    strip_refs, weight_refs, seen_refs = take(p.group), take(p.group), take(p.tiles)
     part_refs = take(p.steps)
     preact_ref, kappa_ref, active = refs
     c = lax.axis_index("chan")
@@ -437,7 +437,7 @@
     total = add(ins).astype(jnp.bfloat16)
     row, along = rows_and_cells(p, outs[0].shape[0])
     for k, out_ref in enumerate(outs):
-        tile = (lax.axis_index("tile") + k) % p.tiles
+        tile = lax.axis_index("tile") ^ k
         cell = (tile * p.own_cols + along + p.tiles * p.own_cols) % (p.tiles * p.own_cols)
         wanted = (cell // p.own_cols * p.rows_each + row) * p.own_cols + cell % p.own_cols
         out_ref[...] = dot(one_hot(wanted, 0, total.shape[0]), total).astype(jnp.bfloat16)
@@ -530,8 +530,8 @@
     def flip(value, mask):
         return lax.ppermute(value, "chan", [(b, b ^ mask) for b in range(p.chans)])
 
-    def shift(value, by):
-        return lax.ppermute(value, "tile", [(a, (a + by) % p.tiles) for a in range(p.tiles)])
+    def trade(value, mask):
+        return lax.ppermute(value, "tile", [(a, a ^ mask) for a in range(p.tiles)])
 
     def send(value, wanted):
         pairs = dict(wanted)
@@ -554,12 +554,6 @@
             scratch=[pltpu.SemaphoreType.DMA((len(values),))],
             flops=0,
         )
-
-    def grow(value, over, after=()):
-        return join([value, over(value)], (2 * value.shape[0],) + value.shape[1:], after)
-
-    def trade(value, mask):
-        return lax.ppermute(value, "tile", [(a, a ^ mask) for a in range(p.tiles)])
 
     strips = call(
         functools.partial(prepare_kernel, p),
@@ -578,33 +572,28 @@
         ],
         vmem=WHOLE_VMEM_BYTES,
     )
-    seen, stages = observed, []
-    bit = 1
-    while bit < p.tiles:
-        if 2 * bit < p.tiles:
-            seen = grow(seen, lambda value: trade(value, bit))
-        strips = grow(strips, lambda value: trade(value, bit), [seen] if bit == 1 else ())
-        stages.append(strips)
-        bit *= 2
-    strips = join(
-        [strips] + [flip(strips, k * p.group) for k in range(1, p.chips)], (p.strips, p.width)
-    )
-    strips = [strips] + [flip(strips, k) for k in range(1, p.group)]
-
     near = [w_hidden] + [flip(w_hidden, chip * p.group) for chip in range(1, p.chips)]
+    strips = [strips] + [trade(strips, k) for k in range(1, p.tiles)]
+    strips = join(strips, (p.tiles * p.block, p.width), near[1:])
     near = call(
         functools.partial(stack_kernel, p),
         shape((p.chips * p.deep, p.hidden), half),
-        near + [stages[-1]],
+        near + [strips],
         in_hbm=[len(near)],
     )
     weights = [near] + [flip(near, k) for k in range(1, p.group)]
 
-    far_half = p.tiles // 2
-    seen = [
-        seen,
-        send(seen, {(b // p.group ^ far_half, b): (b // p.group, b) for b in range(p.chans)}),
+    _, leaving = lax.optimization_barrier((strips, observed))
+    seen = [observed] + [
+        send(leaving, {(b // p.group ^ k, b): (b // p.group, b) for b in range(p.chans)})
+        for k in range(1, p.tiles)
     ]
+    strips = join(
+        [strips] + [flip(strips, k * p.group) for k in range(1, p.chips)],
+        (p.strips, p.width),
+        weights[1:] + seen[1:],
+    )
+    strips = [strips] + [flip(strips, k) for k in range(1, p.group)]
 
     reach = p.across + 4
     place, source, cell, *targets = call(
@@ -674,7 +663,7 @@
         [shape((p.rows_each * p.per_row, p.features), half)] * p.tiles,
         partial,
     )
-    partial = [partial[0]] + [shift(partial[k], k) for k in range(1, p.tiles)]
+    partial = [partial[0]] + [trade(partial[k], k) for k in range(1, p.tiles)]
     partial = call(
         functools.partial(add_tiles_kernel, p),
         [shape((p.around, p.features), half)] * p.chips,

time: 72.3 us -> 82.2 us (1.14)
  waiting for transfers between devices: 27.3 us -> 37.9 us
    ppermute x3 -> x0, starting transfers between devices: 7.75 us -> none  [shift(): lax.ppermute(value, 'tile', [(a, (a + by) % p.tiles) for a in range(p.til...]
    ppermute x3 -> x6, waiting for transfers between devices: 4.67 us -> 9.54 us  [trade(): return lax.ppermute(value, 'tile', [(a, a ^ mask) for a in range(p.tiles)])]
    ppermute x3 -> x6, starting transfers between devices: 5.82 us -> 10.5 us  [trade(): return lax.ppermute(value, 'tile', [(a, a ^ mask) for a in range(p.tiles)])]
    ppermute x14, waiting for transfers between devices: 11.2 us -> 15.3 us  [flip(): return lax.ppermute(value, 'chan', [(b, b ^ mask) for b in range(p.chans)])]
    ppermute x7 -> x9, waiting for transfers between devices: 9.41 us -> 13.1 us  [send(): lax.ppermute(value, both, sorted(((number(a), number(b)) for a, b in pair...]
    ppermute x14, starting transfers between devices: 11 us -> 13.3 us  [flip(): return lax.ppermute(value, 'chan', [(b, b ^ mask) for b in range(p.chans)])]
    ppermute x3 -> x0, waiting for transfers between devices: 2.08 us -> none  [shift(): lax.ppermute(value, 'tile', [(a, (a + by) % p.tiles) for a in range(p.til...]
    ppermute x7 -> x9, starting transfers between devices: 5.53 us -> 6.62 us  [send(): lax.ppermute(value, both, sorted(((number(a), number(b)) for a, b in pair...]
  transfers between devices with their start and end apart: 27 -> 29, of which waited for: 18 -> 18; matrix products, arithmetic and copies ran while one was open for 0% -> 0% of each run, Pallas kernels for 5% -> 3%
where the time goes in v9:
time: 82.2 us; the launch traced here: 82 us
  waiting for transfers between devices  37.9 us (46%)
  starting transfers between devices  30.4 us (37%)
  Pallas kernels  11.2 us (14%)
  local copies, waits for them, and re-layouts  2.2 us (3%)
    ppermute x14, waiting for transfers between devices, flip(): return lax.ppermute(value, 'chan', [(b, b ^ mask) for b in range(p.chans)])  15.3 us
    ppermute x14, starting transfers between devices, flip(): return lax.ppermute(value, 'chan', [(b, b ^ mask) for b in range(p.chans)])  13.3 us
    ppermute x9, waiting for transfers between devices, send(): lax.ppermute(value, both, sorted(((number(a), number(b)) for a, b in pair...  13.1 us
    pallas_call x13, Pallas kernels, call(): pl.pallas_call(kernel, out_shape=out_shape, in_specs=[far if k in in_hbm...  11.2 us
    ppermute x6, starting transfers between devices, trade(): return lax.ppermute(value, 'tile', [(a, a ^ mask) for a in range(p.tiles)])  10.5 us
    ppermute x6, waiting for transfers between devices, trade(): return lax.ppermute(value, 'tile', [(a, a ^ mask) for a in range(p.tiles)])  9.54 us
    ppermute x9, starting transfers between devices, send(): lax.ppermute(value, both, sorted(((number(a), number(b)) for a, b in pair...  6.62 us
    unnamed x14, local copies, waits for them, and re-layouts  2.04 us
  transfers between devices with their start and end apart: 29, of which 18 were waited for; matrix products, arithmetic and copies ran while one was open for 0% of the time, Pallas kernels for 3%

profile of v9, /device:TPU:0, one launch (start us, length us, event | category | flops | bytes accessed | tf_op | source)
XLA Modules:
  0.0 82.0 jit_solution(16710888091034205908)
XLA Ops:
  0.0 3.0 %collective-permute-start.4 = (bf16[411,256]{1,0:T(8,128)(2,1)}, bf16[411,256]{1,0:T(8,128)(2,1)S(1)}, u32[]{:S(2)}, u32[]{:S(2)}) collective-permute-start(bf16[411,256]{1,0:T(8,128)(2,1)} %refs_0_.4), channel_id=1, source_target_pairs={{0,4},{1,5},{2,6},{3,7},{4,0},{5,1},{6,2},{7,3},{8,12},{9,13},{10,... | collective-permute-start | bytes 631304 | tf_op jit(solution)/shard_map/ppermute | solution.py:531
  3.0 1.5 %collective-permute-start.3 = (bf16[411,256]{1,0:T(8,128)(2,1)}, bf16[411,256]{1,0:T(8,128)(2,1)S(1)}, u32[]{:S(2)}, u32[]{:S(2)}) collective-permute-start(bf16[411,256]{1,0:T(8,128)(2,1)} %refs_0_.4), channel_id=1, source_target_pairs={{0,2},{1,3},{2,0},{3,1},{4,6},{5,7},{6,4},{7,5},{8,10},{9,11},{10,... | collective-permute-start | bytes 631304 | tf_op jit(solution)/shard_map/ppermute | solution.py:531
  4.5 0.0 collective-permute-start.5
  4.5 1.8 %shard_map.101.refs_0_ = bf16[16,512]{1,0:T(8,128)(2,1)} custom-call(f32[4,32,411]{2,1,0:T(8,128)} %refs_0_.3, f32[4,32]{1,0:T(4,128)} %refs_1_.2, s32[128]{0:T(128)} %refs_2_.1, f32[256]{0:T(256)} %refs_3_.2), custom_call_target="tpu_custom_call" | custom-call | bytes 212480 | tf_op jit(solution)/shard_map/pallas_call | solution.py:164
  6.3 4.1 %collective-permute-start.2 = (bf16[16,512]{1,0:T(8,128)(2,1)}, bf16[16,512]{1,0:T(8,128)(2,1)S(1)}, u32[]{:S(2)}, u32[]{:S(2)}) collective-permute-start(bf16[16,512]{1,0:T(8,128)(2,1)} %shard_map.101.refs_0_), channel_id=1, source_target_pairs={{0,24},{8,16},{16,8},{24,0},{1,25},{9,17},{17,9},{25,1},{2,26},{10... | collective-permute-start | bytes 49160 | tf_op jit(solution)/shard_map/ppermute | solution.py:534
  10.4 1.9 %collective-permute-done.2.refs_3_ = bf16[16,512]{1,0:T(8,128)(2,1)S(1)} collective-permute-done((bf16[16,512]{1,0:T(8,128)(2,1)}, bf16[16,512]{1,0:T(8,128)(2,1)S(1)}, u32[]{:S(2)}, u32[]{:S(2)}) %collective-permute-start.2) | collective-permute-done | bytes 16416 | tf_op jit(solution)/shard_map/ppermute | solution.py:534
  12.3 2.9 %collective-permute-done.1.refs_2_ = bf16[16,512]{1,0:T(8,128)(2,1)S(1)} collective-permute-done((bf16[16,512]{1,0:T(8,128)(2,1)}, bf16[16,512]{1,0:T(8,128)(2,1)S(1)}, u32[]{:S(2)}, u32[]{:S(2)}) %collective-permute-start.1) | collective-permute-done | bytes 16416 | tf_op jit(solution)/shard_map/ppermute | solution.py:534
  15.2 1.0 %collective-permute-done.refs_1_ = bf16[16,512]{1,0:T(8,128)(2,1)S(1)} collective-permute-done((bf16[16,512]{1,0:T(8,128)(2,1)}, bf16[16,512]{1,0:T(8,128)(2,1)S(1)}, u32[]{:S(2)}, u32[]{:S(2)}) %collective-permute-start) | collective-permute-done | bytes 16416 | tf_op jit(solution)/shard_map/ppermute | solution.py:534
  16.3 0.0 copy-start.4
  16.3 0.7 copy-done.4
  17.0 0.1 shard_map.102.refs_4_.refs_0_
  17.1 0.0 copy-start.2
  17.1 0.9 %copy-done.2 = bf16[411,256]{1,0:T(8,128)(2,1)S(1)} copy-done((bf16[411,256]{1,0:T(8,128)(2,1)S(1)}, bf16[411,256]{1,0:T(8,128)(2,1)}, u32[]{:S(2)}) %copy-start.2) | copy-done | bytes 210456
  18.0 0.1 shard_map.103.refs_7_.refs_5_
  18.1 0.1 collective-permute-start.9
  18.2 2.7 %collective-permute-start.8 = (bf16[64,512]{1,0:T(8,128)(2,1)S(1)}, bf16[64,512]{1,0:T(8,128)(2,1)S(1)}, u32[]{:S(2)}, u32[]{:S(2)}) collective-permute-start(bf16[64,512]{1,0:T(8,128)(2,1)S(1)} %shard_map.102.refs_4_.refs_0_), channel_id=1, source_target_pairs={{0,6},{1,7},{2,4},{3,5},{4,2},{5,3},{6,0},{7,1},{8,14},{9,15},{10,... | collective-permute-start | bytes 196616 | tf_op jit(solution)/shard_map/ppermute | solution.py:531
  20.9 3.6 %collective-permute-start.12 = (bf16[128,768]{1,0:T(8,128)(2,1)S(1)}, bf16[128,768]{1,0:T(8,128)(2,1)S(1)}, u32[]{:S(2)}, u32[]{:S(2)}) collective-permute-start(bf16[128,768]{1,0:T(8,128)(2,1)S(1)} %copy-done.3), channel_id=1, source_target_pairs={{0,24},{1,25},{2,3},{3,2},{4,5},{5,4},{6,30},{7,31},{8,9},{9,8},{1... | collective-permute-start | bytes 589832 | tf_op jit(solution)/shard_map/ppermute | solution.py:543
  24.5 0.8 collective-permute-start.7
  25.3 3.5 %collective-permute-done.7.refs_2_ = bf16[64,512]{1,0:T(8,128)(2,1)S(1)} collective-permute-done((bf16[64,512]{1,0:T(8,128)(2,1)S(1)}, bf16[64,512]{1,0:T(8,128)(2,1)S(1)}, u32[]{:S(2)}, u32[]{:S(2)}) %collective-permute-start.7) | collective-permute-done | bytes 65568 | tf_op jit(solution)/shard_map/ppermute | solution.py:531
  28.9 1.2 %collective-permute-start.6 = (bf16[64,512]{1,0:T(8,128)(2,1)S(1)}, bf16[64,512]{1,0:T(8,128)(2,1)S(1)}, u32[]{:S(2)}, u32[]{:S(2)}) collective-permute-start(bf16[64,512]{1,0:T(8,128)(2,1)S(1)} %shard_map.102.refs_4_.refs_0_), channel_id=1, source_target_pairs={{0,2},{1,3},{2,0},{3,1},{4,6},{5,7},{6,4},{7,5},{8,10},{9,11},{10,... | collective-permute-start | bytes 196616 | tf_op jit(solution)/shard_map/ppermute | solution.py:531
  30.1 3.1 %collective-permute-done.6.refs_1_ = bf16[64,512]{1,0:T(8,128)(2,1)S(1)} collective-permute-done((bf16[64,512]{1,0:T(8,128)(2,1)S(1)}, bf16[64,512]{1,0:T(8,128)(2,1)S(1)}, u32[]{:S(2)}, u32[]{:S(2)}) %collective-permute-start.6) | collective-permute-done | bytes 65568 | tf_op jit(solution)/shard_map/ppermute | solution.py:531
  33.1 0.9 %collective-permute-done.11.refs_6_.refs_11_ = bf16[128,768]{1,0:T(8,128)(2,1)S(1)} collective-permute-done((bf16[128,768]{1,0:T(8,128)(2,1)S(1)}, bf16[128,768]{1,0:T(8,128)(2,1)S(1)}, u32[]{:S(2)}, u32[]{:S(2)}) %collective-permute-start.11) | collective-permute-done | bytes 196640 | tf_op jit(solution)/shard_map/ppermute | solution.py:543
  34.1 4.1 %collective-permute-done.10.refs_5_.refs_10_ = bf16[128,768]{1,0:T(8,128)(2,1)S(1)} collective-permute-done((bf16[128,768]{1,0:T(8,128)(2,1)S(1)}, bf16[128,768]{1,0:T(8,128)(2,1)S(1)}, u32[]{:S(2)}, u32[]{:S(2)}) %collective-permute-start.10) | collective-permute-done | bytes 196640 | tf_op jit(solution)/shard_map/ppermute | solution.py:543
  38.2 0.4 shard_map.104.refs_5_
  38.6 0.1 collective-permute-start.13
  38.6 0.0 copy-start
  38.7 0.0 copy-start.5
  38.7 0.4 shard_map.100
  39.1 1.1 %collective-permute-done.13.refs_6_ = bf16[256,512]{1,0:T(8,128)(2,1)S(1)} collective-permute-done((bf16[256,512]{1,0:T(8,128)(2,1)S(1)}, bf16[256,512]{1,0:T(8,128)(2,1)S(1)}, u32[]{:S(2)}, u32[]{:S(2)}) %collective-permute-start.13) | collective-permute-done | bytes 262176 | tf_op jit(solution)/shard_map/ppermute | solution.py:531
  40.2 0.4 copy-done
  40.5 2.3 %shard_map.105 = (bf16[128,768]{1,0:T(8,128)(2,1)S(1)}, bf16[128,768]{1,0:T(8,128)(2,1)S(1)}, f32[8,256,256]{2,1,0:T(8,128)S(1)}, f32[24,128]{1,0:T(8,128)S(1)}) custom-call(s32[256,1]{1,0:T(8,128)S(1)} %get-tuple-element.25.refs_0_, s32[256,1]{1,0:T(8,128)S(1)} %get-tuple-element.26.refs_1_, s32[24,1]{1,0:T(8,128)S(1)} %get-tuple-element.27.refs_2_, ...), custom_call_target="tpu_custom_call" | custom-call | flops 1236271104 | bytes 6165600 | tf_op jit(solution)/shard_map/pallas_call | solution.py:164
  42.9 0.1 collective-permute-start.14
  42.9 0.1 collective-permute-start.15
  43.0 2.0 %collective-permute-start.16 = (bf16[128,768]{1,0:T(8,128)(2,1)S(1)}, bf16[128,768]{1,0:T(8,128)(2,1)S(1)}, u32[]{:S(2)}, u32[]{:S(2)}) collective-permute-start(bf16[128,768]{1,0:T(8,128)(2,1)S(1)} %get-tuple-element.30.refs_0_), channel_id=1, source_target_pairs={{0,4},{1,5},{2,3},{3,2},{4,0},{5,1},{6,7},{7,6},{8,9},{9,8},{10,14... | collective-permute-start | bytes 589832 | tf_op jit(solution)/shard_map/ppermute | solution.py:543
  45.0 0.4 collective-permute-start.17
  45.4 5.2 %collective-permute-done.14.refs_2_ = bf16[128,768]{1,0:T(8,128)(2,1)S(1)} collective-permute-done((bf16[128,768]{1,0:T(8,128)(2,1)S(1)}, bf16[128,768]{1,0:T(8,128)(2,1)S(1)}, u32[]{:S(2)}, u32[]{:S(2)}) %collective-permute-start.14) | collective-permute-done | bytes 196640 | tf_op jit(solution)/shard_map/ppermute | solution.py:543
  50.6 0.1 collective-permute-done.15.refs_3_
  50.7 0.4 collective-permute-start.19
  51.1 0.6 shard_map.106.refs_8_.refs_2_
  51.7 0.0 copy-start.1
  51.8 2.8 %collective-permute-done.16.refs_4_ = bf16[128,768]{1,0:T(8,128)(2,1)S(1)} collective-permute-done((bf16[128,768]{1,0:T(8,128)(2,1)S(1)}, bf16[128,768]{1,0:T(8,128)(2,1)S(1)}, u32[]{:S(2)}, u32[]{:S(2)}) %collective-permute-start.16) | collective-permute-done | bytes 196640 | tf_op jit(solution)/shard_map/ppermute | solution.py:543
  54.5 0.6 shard_map.107.refs_3_
  55.1 0.1 collective-permute-start.20
  55.2 1.7 %collective-permute-done.20.refs_4_ = bf16[256,768]{1,0:T(8,128)(2,1)S(1)} collective-permute-done((bf16[256,768]{1,0:T(8,128)(2,1)S(1)}, bf16[256,768]{1,0:T(8,128)(2,1)S(1)}, u32[]{:S(2)}, u32[]{:S(2)}) %collective-permute-start.20) | collective-permute-done | bytes 393248 | tf_op jit(solution)/shard_map/ppermute | solution.py:531
  56.9 3.2 %shard_map.108 = (bf16[128,411]{1,0:T(8,128)(2,1)S(1)}, bf16[128,411]{1,0:T(8,128)(2,1)S(1)}) custom-call(bf16[2048,768]{1,0:T(8,128)(2,1)S(1)} %copy-done, bf16[1536,768]{1,0:T(8,128)(2,1)S(1)} %copy-done.1, f32[8,256,256]{2,1,0:T(8,128)S(1)} %shard_map.106.refs_8_.refs_2_, bf16[256,768]{1,0:T(8,128)(2,1)S(1)} %shard_map.107.refs_3_, ...), custom_call_target="tpu_custom_call" | custom-call | flops 1840250880 | bytes 10093568 | tf_op jit(solution)/shard_map/pallas_call | solution.py:164
  60.1 0.2 collective-permute-start.21
  60.3 1.2 %collective-permute-done.21.refs_1_ = bf16[128,411]{1,0:T(8,128)(2,1)S(1)} collective-permute-done((bf16[128,411]{1,0:T(8,128)(2,1)S(1)}, bf16[128,411]{1,0:T(8,128)(2,1)S(1)}, u32[]{:S(2)}, u32[]{:S(2)}) %collective-permute-start.21) | collective-permute-done | bytes 105248 | tf_op jit(solution)/shard_map/ppermute | solution.py:531
  61.5 0.3 shard_map.109
  61.8 4.0 %collective-permute-start.22 = (bf16[40,411]{1,0:T(8,128)(2,1)S(1)}, bf16[40,411]{1,0:T(8,128)(2,1)S(1)}, u32[]{:S(2)}, u32[]{:S(2)}) collective-permute-start(bf16[40,411]{1,0:T(8,128)(2,1)S(1)} %get-tuple-element.37), channel_id=1, source_target_pairs={{0,8},{8,0},{16,24},{24,16},{1,9},{9,1},{17,25},{25,17},{2,10},{10... | collective-permute-start | bytes 98648 | tf_op jit(solution)/shard_map/ppermute | solution.py:534
  65.7 2.4 %collective-permute-start.24 = (bf16[40,411]{1,0:T(8,128)(2,1)S(1)}, bf16[40,411]{1,0:T(8,128)(2,1)S(1)}, u32[]{:S(2)}, u32[]{:S(2)}) collective-permute-start(bf16[40,411]{1,0:T(8,128)(2,1)S(1)} %get-tuple-element.39), channel_id=1, source_target_pairs={{0,24},{8,16},{16,8},{24,0},{1,25},{9,17},{17,9},{25,1},{2,26},{10... | collective-permute-start | bytes 98648 | tf_op jit(solution)/shard_map/ppermute | solution.py:534
  68.2 0.1 slice_bitcast_fusion.2
  68.2 3.7 %collective-permute-done.23.refs_2_ = bf16[40,411]{1,0:T(8,128)(2,1)S(1)} collective-permute-done((bf16[40,411]{1,0:T(8,128)(2,1)S(1)}, bf16[40,411]{1,0:T(8,128)(2,1)S(1)}, u32[]{:S(2)}, u32[]{:S(2)}) %collective-permute-start.23) | collective-permute-done | bytes 32912 | tf_op jit(solution)/shard_map/ppermute | solution.py:534
  71.9 0.2 shard_map.110
  72.1 0.1 collective-permute-start.25
  72.2 2.2 %collective-permute-start.26 = (bf16[40,411]{1,0:T(8,128)(2,1)S(1)}, bf16[40,411]{1,0:T(8,128)(2,1)S(1)}, u32[]{:S(2)}, u32[]{:S(2)}) collective-permute-start(bf16[40,411]{1,0:T(8,128)(2,1)S(1)} %get-tuple-element.42), channel_id=1, source_target_pairs={{0,4},{1,5},{2,6},{3,7},{4,0},{5,1},{6,2},{7,3},{8,12},{9,13},{10,... | collective-permute-start | bytes 98648 | tf_op jit(solution)/shard_map/ppermute | solution.py:531
  74.4 1.3 %collective-permute-start.27 = (bf16[40,411]{1,0:T(8,128)(2,1)S(1)}, bf16[40,411]{1,0:T(8,128)(2,1)S(1)}, u32[]{:S(2)}, u32[]{:S(2)}) collective-permute-start(bf16[40,411]{1,0:T(8,128)(2,1)S(1)} %get-tuple-element.43), channel_id=1, source_target_pairs={{0,6},{1,7},{2,4},{3,5},{4,2},{5,3},{6,0},{7,1},{8,14},{9,15},{10,... | collective-permute-start | bytes 98648 | tf_op jit(solution)/shard_map/ppermute | solution.py:531
  75.7 0.5 collective-permute-done.25.refs_1_
  76.2 0.6 collective-permute-done.26.refs_2_
  76.8 2.5 %collective-permute-done.27.refs_3_ = bf16[40,411]{1,0:T(8,128)(2,1)S(1)} collective-permute-done((bf16[40,411]{1,0:T(8,128)(2,1)S(1)}, bf16[40,411]{1,0:T(8,128)(2,1)S(1)}, u32[]{:S(2)}, u32[]{:S(2)}) %collective-permute-start.27) | collective-permute-done | bytes 32912 | tf_op jit(solution)/shard_map/ppermute | solution.py:531
  79.3 0.1 collective-permute-start.28
  79.4 0.1 maximum_sqrt_fusion
  79.5 0.1 copy.19
  79.6 1.1 %collective-permute-done.28.refs_1_ = f32[40,411]{1,0:T(8,128)S(1)} collective-permute-done((f32[40,411]{1,0:T(8,128)S(1)}, f32[40,411]{1,0:T(8,128)S(1)}, u32[]{:S(2)}, u32[]{:S(2)}) %collective-permute-start.28) | collective-permute-done | bytes 65792 | tf_op jit(solution)/shard_map/ppermute | solution.py:531
  80.7 1.3 %shard_map.112 = f32[4,32,411]{2,1,0:T(8,128)} custom-call(f32[40,411]{1,0:T(8,128)S(1)} %shard_map.111.refs_0_, f32[40,411]{1,0:T(8,128)S(1)} %collective-permute-done.28.refs_1_, f32[48,8]{1,0:T(8,128)S(1)} %bitcast.9), custom_call_target="tpu_custom_call" | custom-call | flops 5260800 | bytes 133056 | tf_op jit(solution)/shard_map/pallas_call | solution.py:164
  (25 shorter events, 0.1 us)
Async XLA Ops:
  0.0 20.9 %copy-start.3 = (bf16[128,768]{1,0:T(8,128)(2,1)S(1)}, bf16[128,768]{1,0:T(8,128)(2,1)}, u32[]{:S(2)}) copy-start(bf16[128,768]{1,0:T(8,128)(2,1)} %refs_9_.1) | copy-start | bytes 589828
  0.0 38.6 %copy-start.6 = (s32[256,1]{0,1:T(1,128)S(1)}, s32[256,1]{0,1:T(1,128)}, u32[]{:S(2)}) copy-start(s32[256,1]{0,1:T(1,128)} %param.12) | copy-start | bytes 3076
  0.0 16.3 %collective-permute-start.4 = (bf16[411,256]{1,0:T(8,128)(2,1)}, bf16[411,256]{1,0:T(8,128)(2,1)S(1)}, u32[]{:S(2)}, u32[]{:S(2)}) collective-permute-start(bf16[411,256]{1,0:T(8,128)(2,1)} %refs_0_.4), channel_id=1, source_target_pairs={{0,4},{1,5},{2,6},{3,7},{4,0},{5,1},{6,2},{7,3},{8,12},{9,13},{10,... | collective-permute-start | bytes 631304 | tf_op jit(solution)/shard_map/ppermute | solution.py:531
  3.0 13.3 %collective-permute-start.3 = (bf16[411,256]{1,0:T(8,128)(2,1)}, bf16[411,256]{1,0:T(8,128)(2,1)S(1)}, u32[]{:S(2)}, u32[]{:S(2)}) collective-permute-start(bf16[411,256]{1,0:T(8,128)(2,1)} %refs_0_.4), channel_id=1, source_target_pairs={{0,2},{1,3},{2,0},{3,1},{4,6},{5,7},{6,4},{7,5},{8,10},{9,11},{10,... | collective-permute-start | bytes 631304 | tf_op jit(solution)/shard_map/ppermute | solution.py:531
  4.5 11.8 %collective-permute-start.5 = (bf16[411,256]{1,0:T(8,128)(2,1)}, bf16[411,256]{1,0:T(8,128)(2,1)S(1)}, u32[]{:S(2)}, u32[]{:S(2)}) collective-permute-start(bf16[411,256]{1,0:T(8,128)(2,1)} %refs_0_.4), channel_id=1, source_target_pairs={{0,6},{1,7},{2,4},{3,5},{4,2},{5,3},{6,0},{7,1},{8,14},{9,15},{10,... | collective-permute-start | bytes 631304 | tf_op jit(solution)/shard_map/ppermute | solution.py:531
  6.3 6.0 %collective-permute-start.2 = (bf16[16,512]{1,0:T(8,128)(2,1)}, bf16[16,512]{1,0:T(8,128)(2,1)S(1)}, u32[]{:S(2)}, u32[]{:S(2)}) collective-permute-start(bf16[16,512]{1,0:T(8,128)(2,1)} %shard_map.101.refs_0_), channel_id=1, source_target_pairs={{0,24},{8,16},{16,8},{24,0},{1,25},{9,17},{17,9},{25,1},{2,26},{10... | collective-permute-start | bytes 49160 | tf_op jit(solution)/shard_map/ppermute | solution.py:534
  10.4 4.8 %collective-permute-start.1 = (bf16[16,512]{1,0:T(8,128)(2,1)}, bf16[16,512]{1,0:T(8,128)(2,1)S(1)}, u32[]{:S(2)}, u32[]{:S(2)}) collective-permute-start(bf16[16,512]{1,0:T(8,128)(2,1)} %shard_map.101.refs_0_), channel_id=1, source_target_pairs={{0,16},{8,24},{16,0},{24,8},{1,17},{9,25},{17,1},{25,9},{2,18},{10... | collective-permute-start | bytes 49160 | tf_op jit(solution)/shard_map/ppermute | solution.py:534
  12.3 3.9 %collective-permute-start = (bf16[16,512]{1,0:T(8,128)(2,1)}, bf16[16,512]{1,0:T(8,128)(2,1)S(1)}, u32[]{:S(2)}, u32[]{:S(2)}) collective-permute-start(bf16[16,512]{1,0:T(8,128)(2,1)} %shard_map.101.refs_0_), channel_id=1, source_target_pairs={{0,8},{8,0},{16,24},{24,16},{1,9},{9,1},{17,25},{25,17},{2,10},{10... | collective-permute-start | bytes 49160 | tf_op jit(solution)/shard_map/ppermute | solution.py:534
  16.3 0.7 copy-start.4
  17.1 0.9 %copy-start.2 = (bf16[411,256]{1,0:T(8,128)(2,1)S(1)}, bf16[411,256]{1,0:T(8,128)(2,1)}, u32[]{:S(2)}) copy-start(bf16[411,256]{1,0:T(8,128)(2,1)} %refs_0_.4) | copy-start | bytes 631300
  18.1 20.1 %collective-permute-start.9 = (bf16[1664,256]{1,0:T(8,128)(2,1)S(1)}, bf16[1664,256]{1,0:T(8,128)(2,1)S(1)}, u32[]{:S(2)}, u32[]{:S(2)}) collective-permute-start(bf16[1664,256]{1,0:T(8,128)(2,1)S(1)} %shard_map.103.refs_7_.refs_5_), channel_id=1, source_target_pairs={{0,1},{1,0},{2,3},{3,2},{4,5},{5,4},{6,7},{7,6},{8,9},{9,8},{10,11... | collective-permute-start | bytes 2555912 | tf_op jit(solution)/shard_map/ppermute | solution.py:531
  18.2 6.3 %collective-permute-start.8 = (bf16[64,512]{1,0:T(8,128)(2,1)S(1)}, bf16[64,512]{1,0:T(8,128)(2,1)S(1)}, u32[]{:S(2)}, u32[]{:S(2)}) collective-permute-start(bf16[64,512]{1,0:T(8,128)(2,1)S(1)} %shard_map.102.refs_4_.refs_0_), channel_id=1, source_target_pairs={{0,6},{1,7},{2,4},{3,5},{4,2},{5,3},{6,0},{7,1},{8,14},{9,15},{10,... | collective-permute-start | bytes 196616 | tf_op jit(solution)/shard_map/ppermute | solution.py:531
  20.9 12.2 %collective-permute-start.12 = (bf16[128,768]{1,0:T(8,128)(2,1)S(1)}, bf16[128,768]{1,0:T(8,128)(2,1)S(1)}, u32[]{:S(2)}, u32[]{:S(2)}) collective-permute-start(bf16[128,768]{1,0:T(8,128)(2,1)S(1)} %copy-done.3), channel_id=1, source_target_pairs={{0,24},{1,25},{2,3},{3,2},{4,5},{5,4},{6,30},{7,31},{8,9},{9,8},{1... | collective-permute-start | bytes 589832 | tf_op jit(solution)/shard_map/ppermute | solution.py:543
  24.5 9.5 %collective-permute-start.11 = (bf16[128,768]{1,0:T(8,128)(2,1)S(1)}, bf16[128,768]{1,0:T(8,128)(2,1)S(1)}, u32[]{:S(2)}, u32[]{:S(2)}) collective-permute-start(bf16[128,768]{1,0:T(8,128)(2,1)S(1)} %copy-done.3), channel_id=1, source_target_pairs={{0,16},{1,17},{2,3},{3,2},{4,20},{5,21},{6,7},{7,6},{8,9},{9,8},{1... | collective-permute-start | bytes 589832 | tf_op jit(solution)/shard_map/ppermute | solution.py:543
  24.5 13.7 %collective-permute-start.10 = (bf16[128,768]{1,0:T(8,128)(2,1)S(1)}, bf16[128,768]{1,0:T(8,128)(2,1)S(1)}, u32[]{:S(2)}, u32[]{:S(2)}) collective-permute-start(bf16[128,768]{1,0:T(8,128)(2,1)S(1)} %copy-done.3), channel_id=1, source_target_pairs={{0,8},{1,9},{2,10},{3,11},{4,5},{5,4},{6,7},{7,6},{8,0},{9,1},{10,... | collective-permute-start | bytes 589832 | tf_op jit(solution)/shard_map/ppermute | solution.py:543
  24.5 4.3 %collective-permute-start.7 = (bf16[64,512]{1,0:T(8,128)(2,1)S(1)}, bf16[64,512]{1,0:T(8,128)(2,1)S(1)}, u32[]{:S(2)}, u32[]{:S(2)}) collective-permute-start(bf16[64,512]{1,0:T(8,128)(2,1)S(1)} %shard_map.102.refs_4_.refs_0_), channel_id=1, source_target_pairs={{0,4},{1,5},{2,6},{3,7},{4,0},{5,1},{6,2},{7,3},{8,12},{9,13},{10,... | collective-permute-start | bytes 196616 | tf_op jit(solution)/shard_map/ppermute | solution.py:531
  28.9 4.3 %collective-permute-start.6 = (bf16[64,512]{1,0:T(8,128)(2,1)S(1)}, bf16[64,512]{1,0:T(8,128)(2,1)S(1)}, u32[]{:S(2)}, u32[]{:S(2)}) collective-permute-start(bf16[64,512]{1,0:T(8,128)(2,1)S(1)} %shard_map.102.refs_4_.refs_0_), channel_id=1, source_target_pairs={{0,2},{1,3},{2,0},{3,1},{4,6},{5,7},{6,4},{7,5},{8,10},{9,11},{10,... | collective-permute-start | bytes 196616 | tf_op jit(solution)/shard_map/ppermute | solution.py:531
  38.6 1.6 %collective-permute-start.13 = (bf16[256,512]{1,0:T(8,128)(2,1)S(1)}, bf16[256,512]{1,0:T(8,128)(2,1)S(1)}, u32[]{:S(2)}, u32[]{:S(2)}) collective-permute-start(bf16[256,512]{1,0:T(8,128)(2,1)S(1)} %shard_map.104.refs_5_), channel_id=1, source_target_pairs={{0,1},{1,0},{2,3},{3,2},{4,5},{5,4},{6,7},{7,6},{8,9},{9,8},{10,11... | collective-permute-start | bytes 786440 | tf_op jit(solution)/shard_map/ppermute | solution.py:531
  38.6 1.9 %copy-start = (bf16[2048,768]{1,0:T(8,128)(2,1)S(1)}, bf16[2048,768]{1,0:T(8,128)(2,1)}, u32[]{:S(2)}) copy-start(bf16[2048,768]{1,0:T(8,128)(2,1)} %refs_0_.5) | copy-start | bytes 9437188
  38.7 1.9 %copy-start.5 = (f32[768]{0:T(1024)S(1)}, f32[768]{0:T(1024)}, u32[]{:S(2)}) copy-start(f32[768]{0:T(1024)} %refs_3_.3) | copy-start | bytes 9220
  42.9 7.7 %collective-permute-start.14 = (bf16[128,768]{1,0:T(8,128)(2,1)S(1)}, bf16[128,768]{1,0:T(8,128)(2,1)S(1)}, u32[]{:S(2)}, u32[]{:S(2)}) collective-permute-start(bf16[128,768]{1,0:T(8,128)(2,1)S(1)} %get-tuple-element.30.refs_0_), channel_id=1, source_target_pairs={{0,2},{1,3},{2,0},{3,1},{4,5},{5,4},{6,7},{7,6},{8,10},{9,11},{10,... | collective-permute-start | bytes 589832 | tf_op jit(solution)/shard_map/ppermute | solution.py:543
  42.9 7.8 %collective-permute-start.15 = (bf16[128,768]{1,0:T(8,128)(2,1)S(1)}, bf16[128,768]{1,0:T(8,128)(2,1)S(1)}, u32[]{:S(2)}, u32[]{:S(2)}) collective-permute-start(bf16[128,768]{1,0:T(8,128)(2,1)S(1)} %get-tuple-element.31.refs_1_), channel_id=1, source_target_pairs={{0,4},{1,5},{2,3},{3,2},{4,0},{5,1},{6,7},{7,6},{8,9},{9,8},{10,14... | collective-permute-start | bytes 589832 | tf_op jit(solution)/shard_map/ppermute | solution.py:543
  43.0 11.5 %collective-permute-start.16 = (bf16[128,768]{1,0:T(8,128)(2,1)S(1)}, bf16[128,768]{1,0:T(8,128)(2,1)S(1)}, u32[]{:S(2)}, u32[]{:S(2)}) collective-permute-start(bf16[128,768]{1,0:T(8,128)(2,1)S(1)} %get-tuple-element.30.refs_0_), channel_id=1, source_target_pairs={{0,4},{1,5},{2,3},{3,2},{4,0},{5,1},{6,7},{7,6},{8,9},{9,8},{10,14... | collective-permute-start | bytes 589832 | tf_op jit(solution)/shard_map/ppermute | solution.py:543
  45.0 9.5 %collective-permute-start.17 = (bf16[128,768]{1,0:T(8,128)(2,1)S(1)}, bf16[128,768]{1,0:T(8,128)(2,1)S(1)}, u32[]{:S(2)}, u32[]{:S(2)}) collective-permute-start(bf16[128,768]{1,0:T(8,128)(2,1)S(1)} %get-tuple-element.31.refs_1_), channel_id=1, source_target_pairs={{0,2},{1,3},{2,0},{3,1},{4,5},{5,4},{6,7},{7,6},{8,10},{9,11},{10,... | collective-permute-start | bytes 589832 | tf_op jit(solution)/shard_map/ppermute | solution.py:543
  50.6 3.9 %collective-permute-start.18 = (bf16[128,768]{1,0:T(8,128)(2,1)S(1)}, bf16[128,768]{1,0:T(8,128)(2,1)S(1)}, u32[]{:S(2)}, u32[]{:S(2)}) collective-permute-start(bf16[128,768]{1,0:T(8,128)(2,1)S(1)} %collective-permute-done.14.refs_2_), channel_id=1, source_target_pairs={{0,1},{1,0},{2,6},{3,7},{4,5},{5,4},{6,2},{7,3},{8,12},{9,13},{10,... | collective-permute-start | bytes 589832 | tf_op jit(solution)/shard_map/ppermute | solution.py:543
  50.7 3.9 %collective-permute-start.19 = (bf16[128,768]{1,0:T(8,128)(2,1)S(1)}, bf16[128,768]{1,0:T(8,128)(2,1)S(1)}, u32[]{:S(2)}, u32[]{:S(2)}) collective-permute-start(bf16[128,768]{1,0:T(8,128)(2,1)S(1)} %collective-permute-done.15.refs_3_), channel_id=1, source_target_pairs={{0,1},{1,0},{2,3},{3,2},{4,6},{5,7},{6,4},{7,5},{8,9},{9,8},{10,11... | collective-permute-start | bytes 589832 | tf_op jit(solution)/shard_map/ppermute | solution.py:543
  51.7 5.2 %copy-start.1 = (bf16[1536,768]{1,0:T(8,128)(2,1)S(1)}, bf16[1536,768]{1,0:T(8,128)(2,1)}, u32[]{:S(2)}) copy-start(bf16[1536,768]{1,0:T(8,128)(2,1)} %refs_1_.3) | copy-start | bytes 7077892
  55.1 1.8 %collective-permute-start.20 = (bf16[256,768]{1,0:T(8,128)(2,1)S(1)}, bf16[256,768]{1,0:T(8,128)(2,1)S(1)}, u32[]{:S(2)}, u32[]{:S(2)}) collective-permute-start(bf16[256,768]{1,0:T(8,128)(2,1)S(1)} %shard_map.107.refs_3_), channel_id=1, source_target_pairs={{0,1},{1,0},{2,3},{3,2},{4,5},{5,4},{6,7},{7,6},{8,9},{9,8},{10,11... | collective-permute-start | bytes 1179656 | tf_op jit(solution)/shard_map/ppermute | solution.py:531
  60.1 1.4 %collective-permute-start.21 = (bf16[128,411]{1,0:T(8,128)(2,1)S(1)}, bf16[128,411]{1,0:T(8,128)(2,1)S(1)}, u32[]{:S(2)}, u32[]{:S(2)}) collective-permute-start(bf16[128,411]{1,0:T(8,128)(2,1)S(1)} %get-tuple-element.35), channel_id=1, source_target_pairs={{0,1},{1,0},{2,3},{3,2},{4,5},{5,4},{6,7},{7,6},{8,9},{9,8},{10,11... | collective-permute-start | bytes 315656 | tf_op jit(solution)/shard_map/ppermute | solution.py:531
  61.8 6.5 %collective-permute-start.22 = (bf16[40,411]{1,0:T(8,128)(2,1)S(1)}, bf16[40,411]{1,0:T(8,128)(2,1)S(1)}, u32[]{:S(2)}, u32[]{:S(2)}) collective-permute-start(bf16[40,411]{1,0:T(8,128)(2,1)S(1)} %get-tuple-element.37), channel_id=1, source_target_pairs={{0,8},{8,0},{16,24},{24,16},{1,9},{9,1},{17,25},{25,17},{2,10},{10... | collective-permute-start | bytes 98648 | tf_op jit(solution)/shard_map/ppermute | solution.py:534
  65.7 6.2 %collective-permute-start.23 = (bf16[40,411]{1,0:T(8,128)(2,1)S(1)}, bf16[40,411]{1,0:T(8,128)(2,1)S(1)}, u32[]{:S(2)}, u32[]{:S(2)}) collective-permute-start(bf16[40,411]{1,0:T(8,128)(2,1)S(1)} %get-tuple-element.38), channel_id=1, source_target_pairs={{0,16},{8,24},{16,0},{24,8},{1,17},{9,25},{17,1},{25,9},{2,18},{10... | collective-permute-start | bytes 98648 | tf_op jit(solution)/shard_map/ppermute | solution.py:534
  65.7 6.2 %collective-permute-start.24 = (bf16[40,411]{1,0:T(8,128)(2,1)S(1)}, bf16[40,411]{1,0:T(8,128)(2,1)S(1)}, u32[]{:S(2)}, u32[]{:S(2)}) collective-permute-start(bf16[40,411]{1,0:T(8,128)(2,1)S(1)} %get-tuple-element.39), channel_id=1, source_target_pairs={{0,24},{8,16},{16,8},{24,0},{1,25},{9,17},{17,9},{25,1},{2,26},{10... | collective-permute-start | bytes 98648 | tf_op jit(solution)/shard_map/ppermute | solution.py:534
  72.1 4.1 %collective-permute-start.25 = (bf16[40,411]{1,0:T(8,128)(2,1)S(1)}, bf16[40,411]{1,0:T(8,128)(2,1)S(1)}, u32[]{:S(2)}, u32[]{:S(2)}) collective-permute-start(bf16[40,411]{1,0:T(8,128)(2,1)S(1)} %get-tuple-element.41), channel_id=1, source_target_pairs={{0,2},{1,3},{2,0},{3,1},{4,6},{5,7},{6,4},{7,5},{8,10},{9,11},{10,... | collective-permute-start | bytes 98648 | tf_op jit(solution)/shard_map/ppermute | solution.py:531
  72.2 4.6 %collective-permute-start.26 = (bf16[40,411]{1,0:T(8,128)(2,1)S(1)}, bf16[40,411]{1,0:T(8,128)(2,1)S(1)}, u32[]{:S(2)}, u32[]{:S(2)}) collective-permute-start(bf16[40,411]{1,0:T(8,128)(2,1)S(1)} %get-tuple-element.42), channel_id=1, source_target_pairs={{0,4},{1,5},{2,6},{3,7},{4,0},{5,1},{6,2},{7,3},{8,12},{9,13},{10,... | collective-permute-start | bytes 98648 | tf_op jit(solution)/shard_map/ppermute | solution.py:531
  74.4 4.9 %collective-permute-start.27 = (bf16[40,411]{1,0:T(8,128)(2,1)S(1)}, bf16[40,411]{1,0:T(8,128)(2,1)S(1)}, u32[]{:S(2)}, u32[]{:S(2)}) collective-permute-start(bf16[40,411]{1,0:T(8,128)(2,1)S(1)} %get-tuple-element.43), channel_id=1, source_target_pairs={{0,6},{1,7},{2,4},{3,5},{4,2},{5,3},{6,0},{7,1},{8,14},{9,15},{10,... | collective-permute-start | bytes 98648 | tf_op jit(solution)/shard_map/ppermute | solution.py:531
  79.3 1.3 %collective-permute-start.28 = (f32[40,411]{1,0:T(8,128)S(1)}, f32[40,411]{1,0:T(8,128)S(1)}, u32[]{:S(2)}, u32[]{:S(2)}) collective-permute-start(f32[40,411]{1,0:T(8,128)S(1)} %shard_map.111.refs_0_), channel_id=1, source_target_pairs={{0,1},{1,0},{2,3},{3,2},{4,5},{5,4},{6,7},{7,6},{8,9},{9,8},{10,11... | collective-permute-start | bytes 197288 | tf_op jit(solution)/shard_map/ppermute | solution.py:531

commit v10 on v9

--- a/solution.py
+++ b/solution.py
@@ -573,25 +573,33 @@
         vmem=WHOLE_VMEM_BYTES,
     )
     near = [w_hidden] + [flip(w_hidden, chip * p.group) for chip in range(1, p.chips)]
-    strips = [strips] + [trade(strips, k) for k in range(1, p.tiles)]
-    strips = join(strips, (p.tiles * p.block, p.width), near[1:])
-    near = call(
-        functools.partial(stack_kernel, p),
-        shape((p.chips * p.deep, p.hidden), half),
-        near + [strips],
-        in_hbm=[len(near)],
-    )
-    weights = [near] + [flip(near, k) for k in range(1, p.group)]
-
-    _, leaving = lax.optimization_barrier((strips, observed))
-    seen = [observed] + [
-        send(leaving, {(b // p.group ^ k, b): (b // p.group, b) for b in range(p.chans)})
-        for k in range(1, p.tiles)
-    ]
+    held, bit = [observed], 1
+    while 2 * bit < p.tiles:
+        held += [trade(value, bit) for value in held]
+        bit *= 2
+
+    bit = 1
+    while bit < p.tiles:
+        before = held[1:] if bit == 1 else weights[1:]
+        strips = join([strips, trade(strips, bit)], (2 * strips.shape[0], p.width), before)
+        if bit == 1:
+            near = call(
+                functools.partial(stack_kernel, p),
+                shape((p.chips * p.deep, p.hidden), half),
+                near + [strips],
+                in_hbm=[len(near)],
+            )
+            weights = [near] + [flip(near, k) for k in range(1, p.group)]
+        bit *= 2
+
+    _, *leaving = lax.optimization_barrier((strips, *held))
+    wanted = {(b // p.group ^ p.tiles // 2, b): (b // p.group, b) for b in range(p.chans)}
+    far = [send(value, wanted) for value in leaving]
+    seen = held + far
     strips = join(
         [strips] + [flip(strips, k * p.group) for k in range(1, p.chips)],
         (p.strips, p.width),
-        weights[1:] + seen[1:],
+        far,
     )
     strips = [strips] + [flip(strips, k) for k in range(1, p.group)]
 

time: 82.2 us -> 78.4 us (0.954)
  waiting for transfers between devices: 37.9 us -> 32.8 us
  starting transfers between devices: 30.4 us -> 31.5 us
    ppermute x14, waiting for transfers between devices: 15.3 us -> 10.8 us  [flip(): return lax.ppermute(value, 'chan', [(b, b ^ mask) for b in range(p.chans)])]
    ppermute x6, starting transfers between devices: 10.5 us -> 13.5 us  [trade(): return lax.ppermute(value, 'tile', [(a, a ^ mask) for a in range(p.tiles)])]
    ppermute x9 -> x8, waiting for transfers between devices: 13.1 us -> 10.3 us  [send(): lax.ppermute(value, both, sorted(((number(a), number(b)) for a, b in pair...]
    ppermute x6, waiting for transfers between devices: 9.54 us -> 11.7 us  [trade(): return lax.ppermute(value, 'tile', [(a, a ^ mask) for a in range(p.tiles)])]
    ppermute x14, starting transfers between devices: 13.3 us -> 12 us  [flip(): return lax.ppermute(value, 'chan', [(b, b ^ mask) for b in range(p.chans)])]
    ppermute x9 -> x8, starting transfers between devices: 6.62 us -> 6 us  [send(): lax.ppermute(value, both, sorted(((number(a), number(b)) for a, b in pair...]
    pallas_call x13 -> x14, Pallas kernels: 11.2 us -> 11.2 us  [call(): pl.pallas_call(kernel, out_shape=out_shape, in_specs=[far if k in in_hbm...]
  transfers between devices with their start and end apart: 29 -> 28, of which waited for: 18 -> 18; matrix products, arithmetic and copies ran while one was open for 0% -> 0% of each run, Pallas kernels for 3% -> 4%
where the time goes in v10:
time: 78.4 us; the launch traced here: 78.1 us
  waiting for transfers between devices  32.8 us (42%)
  starting transfers between devices  31.5 us (40%)
  Pallas kernels  11.2 us (14%)
  local copies, waits for them, and re-layouts  2.21 us (3%)
    ppermute x6, starting transfers between devices, trade(): return lax.ppermute(value, 'tile', [(a, a ^ mask) for a in range(p.tiles)])  13.5 us
    ppermute x14, starting transfers between devices, flip(): return lax.ppermute(value, 'chan', [(b, b ^ mask) for b in range(p.chans)])  12 us
    ppermute x6, waiting for transfers between devices, trade(): return lax.ppermute(value, 'tile', [(a, a ^ mask) for a in range(p.tiles)])  11.7 us
    pallas_call x14, Pallas kernels, call(): pl.pallas_call(kernel, out_shape=out_shape, in_specs=[far if k in in_hbm...  11.2 us
    ppermute x14, waiting for transfers between devices, flip(): return lax.ppermute(value, 'chan', [(b, b ^ mask) for b in range(p.chans)])  10.8 us
    ppermute x8, waiting for transfers between devices, send(): lax.ppermute(value, both, sorted(((number(a), number(b)) for a, b in pair...  10.3 us
    ppermute x8, starting transfers between devices, send(): lax.ppermute(value, both, sorted(((number(a), number(b)) for a, b in pair...  6 us
    unnamed x14, local copies, waits for them, and re-layouts  2.06 us
  transfers between devices with their start and end apart: 28, of which 18 were waited for; matrix products, arithmetic and copies ran while one was open for 0% of the time, Pallas kernels for 4%

profile of v10, /device:TPU:0, one launch (start us, length us, event | category | flops | bytes accessed | tf_op | source)
XLA Modules:
  0.0 78.1 jit_solution(12865700637294092616)
XLA Ops:
  0.0 3.0 %collective-permute-start.4 = (bf16[411,256]{1,0:T(8,128)(2,1)}, bf16[411,256]{1,0:T(8,128)(2,1)S(1)}, u32[]{:S(2)}, u32[]{:S(2)}) collective-permute-start(bf16[411,256]{1,0:T(8,128)(2,1)} %refs_0_.4), channel_id=1, source_target_pairs={{0,4},{1,5},{2,6},{3,7},{4,0},{5,1},{6,2},{7,3},{8,12},{9,13},{10,... | collective-permute-start | bytes 631304 | tf_op jit(solution)/shard_map/ppermute | solution.py:531
  3.0 1.5 %collective-permute-start.3 = (bf16[411,256]{1,0:T(8,128)(2,1)}, bf16[411,256]{1,0:T(8,128)(2,1)S(1)}, u32[]{:S(2)}, u32[]{:S(2)}) collective-permute-start(bf16[411,256]{1,0:T(8,128)(2,1)} %refs_0_.4), channel_id=1, source_target_pairs={{0,2},{1,3},{2,0},{3,1},{4,6},{5,7},{6,4},{7,5},{8,10},{9,11},{10,... | collective-permute-start | bytes 631304 | tf_op jit(solution)/shard_map/ppermute | solution.py:531
  4.5 0.0 collective-permute-start.5
  4.5 2.0 %collective-permute-start.1 = (bf16[128,768]{1,0:T(8,128)(2,1)}, bf16[128,768]{1,0:T(8,128)(2,1)S(1)}, u32[]{:S(2)}, u32[]{:S(2)}) collective-permute-start(bf16[128,768]{1,0:T(8,128)(2,1)} %refs_9_.1), channel_id=1, source_target_pairs={{0,8},{8,0},{16,24},{24,16},{1,9},{9,1},{17,25},{25,17},{2,10},{10... | collective-permute-start | bytes 589832 | tf_op jit(solution)/shard_map/ppermute | solution.py:534
  6.5 1.8 %shard_map.101.refs_0_ = bf16[16,512]{1,0:T(8,128)(2,1)} custom-call(f32[4,32,411]{2,1,0:T(8,128)} %refs_0_.3, f32[4,32]{1,0:T(4,128)} %refs_1_.2, s32[128]{0:T(128)} %refs_2_.1, f32[256]{0:T(256)} %refs_3_.2), custom_call_target="tpu_custom_call" | custom-call | bytes 212480 | tf_op jit(solution)/shard_map/pallas_call | solution.py:164
  8.3 0.0 copy-start.3
  8.3 0.1 collective-permute-start
  8.4 3.9 %collective-permute-done.refs_1_ = bf16[16,512]{1,0:T(8,128)(2,1)S(1)} collective-permute-done((bf16[16,512]{1,0:T(8,128)(2,1)}, bf16[16,512]{1,0:T(8,128)(2,1)S(1)}, u32[]{:S(2)}, u32[]{:S(2)}) %collective-permute-start) | collective-permute-done | bytes 16416 | tf_op jit(solution)/shard_map/ppermute | solution.py:534
  12.3 0.7 copy-done.4
  13.1 1.1 %collective-permute-done.5.refs_3_ = bf16[411,256]{1,0:T(8,128)(2,1)S(1)} collective-permute-done((bf16[411,256]{1,0:T(8,128)(2,1)}, bf16[411,256]{1,0:T(8,128)(2,1)S(1)}, u32[]{:S(2)}, u32[]{:S(2)}) %collective-permute-start.5) | collective-permute-done | bytes 210464 | tf_op jit(solution)/shard_map/ppermute | solution.py:531
  14.2 0.9 %copy-done.2 = bf16[411,256]{1,0:T(8,128)(2,1)S(1)} copy-done((bf16[411,256]{1,0:T(8,128)(2,1)S(1)}, bf16[411,256]{1,0:T(8,128)(2,1)}, u32[]{:S(2)}) %copy-start.2) | copy-done | bytes 210456
  15.2 0.1 shard_map.103.refs_7_.refs_5_
  15.2 0.1 collective-permute-start.6
  15.3 2.8 %collective-permute-start.2 = (bf16[32,512]{1,0:T(8,128)(2,1)S(1)}, bf16[32,512]{1,0:T(8,128)(2,1)S(1)}, u32[]{:S(2)}, u32[]{:S(2)}) collective-permute-start(bf16[32,512]{1,0:T(8,128)(2,1)S(1)} %shard_map.102.refs_4_.refs_0_), channel_id=1, source_target_pairs={{0,16},{8,24},{16,0},{24,8},{1,17},{9,25},{17,1},{25,9},{2,18},{10... | collective-permute-start | bytes 98312 | tf_op jit(solution)/shard_map/ppermute | solution.py:534
  18.1 2.1 %collective-permute-done.2.refs_1_ = bf16[32,512]{1,0:T(8,128)(2,1)S(1)} collective-permute-done((bf16[32,512]{1,0:T(8,128)(2,1)S(1)}, bf16[32,512]{1,0:T(8,128)(2,1)S(1)}, u32[]{:S(2)}, u32[]{:S(2)}) %collective-permute-start.2) | collective-permute-done | bytes 32800 | tf_op jit(solution)/shard_map/ppermute | solution.py:534
  20.2 0.1 shard_map.104.refs_0_
  20.3 2.8 %collective-permute-start.10 = (bf16[128,768]{1,0:T(8,128)(2,1)S(1)}, bf16[128,768]{1,0:T(8,128)(2,1)S(1)}, u32[]{:S(2)}, u32[]{:S(2)}) collective-permute-start(bf16[128,768]{1,0:T(8,128)(2,1)S(1)} %copy-done.3), channel_id=1, source_target_pairs={{0,16},{1,17},{2,3},{3,2},{4,20},{5,21},{6,7},{7,6},{8,9},{9,8},{1... | collective-permute-start | bytes 589832 | tf_op jit(solution)/shard_map/ppermute | solution.py:543
  23.1 0.2 collective-permute-start.11
  23.3 0.2 collective-permute-start.9
  23.5 1.5 %collective-permute-start.8 = (bf16[64,512]{1,0:T(8,128)(2,1)S(1)}, bf16[64,512]{1,0:T(8,128)(2,1)S(1)}, u32[]{:S(2)}, u32[]{:S(2)}) collective-permute-start(bf16[64,512]{1,0:T(8,128)(2,1)S(1)} %shard_map.104.refs_0_), channel_id=1, source_target_pairs={{0,4},{1,5},{2,6},{3,7},{4,0},{5,1},{6,2},{7,3},{8,12},{9,13},{10,... | collective-permute-start | bytes 196616 | tf_op jit(solution)/shard_map/ppermute | solution.py:531
  25.0 1.8 %collective-permute-start.7 = (bf16[64,512]{1,0:T(8,128)(2,1)S(1)}, bf16[64,512]{1,0:T(8,128)(2,1)S(1)}, u32[]{:S(2)}, u32[]{:S(2)}) collective-permute-start(bf16[64,512]{1,0:T(8,128)(2,1)S(1)} %shard_map.104.refs_0_), channel_id=1, source_target_pairs={{0,2},{1,3},{2,0},{3,1},{4,6},{5,7},{6,4},{7,5},{8,10},{9,11},{10,... | collective-permute-start | bytes 196616 | tf_op jit(solution)/shard_map/ppermute | solution.py:531
  26.8 1.8 %collective-permute-done.9.refs_3_ = bf16[64,512]{1,0:T(8,128)(2,1)S(1)} collective-permute-done((bf16[64,512]{1,0:T(8,128)(2,1)S(1)}, bf16[64,512]{1,0:T(8,128)(2,1)S(1)}, u32[]{:S(2)}, u32[]{:S(2)}) %collective-permute-start.9) | collective-permute-done | bytes 65568 | tf_op jit(solution)/shard_map/ppermute | solution.py:531
  28.5 0.8 %collective-permute-done.7.refs_1_ = bf16[64,512]{1,0:T(8,128)(2,1)S(1)} collective-permute-done((bf16[64,512]{1,0:T(8,128)(2,1)S(1)}, bf16[64,512]{1,0:T(8,128)(2,1)S(1)}, u32[]{:S(2)}, u32[]{:S(2)}) %collective-permute-start.7) | collective-permute-done | bytes 65568 | tf_op jit(solution)/shard_map/ppermute | solution.py:531
  29.4 2.3 %collective-permute-done.11.refs_5_.refs_12_ = bf16[128,768]{1,0:T(8,128)(2,1)S(1)} collective-permute-done((bf16[128,768]{1,0:T(8,128)(2,1)S(1)}, bf16[128,768]{1,0:T(8,128)(2,1)S(1)}, u32[]{:S(2)}, u32[]{:S(2)}) %collective-permute-start.11) | collective-permute-done | bytes 196640 | tf_op jit(solution)/shard_map/ppermute | solution.py:543
  31.7 0.3 shard_map.105.refs_5_
  32.1 0.1 collective-permute-start.12
  32.2 0.0 copy-start
  32.2 0.4 shard_map.100
  32.6 1.1 %collective-permute-done.12.refs_6_ = bf16[256,512]{1,0:T(8,128)(2,1)S(1)} collective-permute-done((bf16[256,512]{1,0:T(8,128)(2,1)S(1)}, bf16[256,512]{1,0:T(8,128)(2,1)S(1)}, u32[]{:S(2)}, u32[]{:S(2)}) %collective-permute-start.12) | collective-permute-done | bytes 262176 | tf_op jit(solution)/shard_map/ppermute | solution.py:531
  33.7 0.4 copy-done
  34.1 2.3 %shard_map.106 = (bf16[128,768]{1,0:T(8,128)(2,1)S(1)}, bf16[128,768]{1,0:T(8,128)(2,1)S(1)}, f32[8,256,256]{2,1,0:T(8,128)S(1)}, f32[24,128]{1,0:T(8,128)S(1)}) custom-call(s32[256,1]{1,0:T(8,128)S(1)} %get-tuple-element.26.refs_0_, s32[256,1]{1,0:T(8,128)S(1)} %get-tuple-element.27.refs_1_, s32[24,1]{1,0:T(8,128)S(1)} %get-tuple-element.28.refs_2_, ...), custom_call_target="tpu_custom_call" | custom-call | flops 1236271104 | bytes 6165600 | tf_op jit(solution)/shard_map/pallas_call | solution.py:164
  36.4 0.1 collective-permute-start.13
  36.4 2.0 %collective-permute-start.14 = (bf16[128,768]{1,0:T(8,128)(2,1)S(1)}, bf16[128,768]{1,0:T(8,128)(2,1)S(1)}, u32[]{:S(2)}, u32[]{:S(2)}) collective-permute-start(bf16[128,768]{1,0:T(8,128)(2,1)S(1)} %get-tuple-element.33.refs_1_), channel_id=1, source_target_pairs={{0,4},{1,5},{2,3},{3,2},{4,0},{5,1},{6,7},{7,6},{8,9},{9,8},{10,14... | collective-permute-start | bytes 589832 | tf_op jit(solution)/shard_map/ppermute | solution.py:543
  38.5 0.1 collective-permute-start.15
  38.5 0.4 collective-permute-start.16
  39.0 5.2 %collective-permute-done.13.refs_2_ = bf16[128,768]{1,0:T(8,128)(2,1)S(1)} collective-permute-done((bf16[128,768]{1,0:T(8,128)(2,1)S(1)}, bf16[128,768]{1,0:T(8,128)(2,1)S(1)}, u32[]{:S(2)}, u32[]{:S(2)}) %collective-permute-start.13) | collective-permute-done | bytes 196640 | tf_op jit(solution)/shard_map/ppermute | solution.py:543
  44.1 0.1 collective-permute-done.14.refs_3_
  44.2 0.4 collective-permute-start.18
  44.6 0.6 shard_map.107.refs_8_.refs_2_
  45.3 0.0 copy-start.1
  45.3 2.8 %collective-permute-done.15.refs_4_ = bf16[128,768]{1,0:T(8,128)(2,1)S(1)} collective-permute-done((bf16[128,768]{1,0:T(8,128)(2,1)S(1)}, bf16[128,768]{1,0:T(8,128)(2,1)S(1)}, u32[]{:S(2)}, u32[]{:S(2)}) %collective-permute-start.15) | collective-permute-done | bytes 196640 | tf_op jit(solution)/shard_map/ppermute | solution.py:543
  48.0 0.6 shard_map.108.refs_3_
  48.6 0.1 collective-permute-start.19
  48.7 1.7 %collective-permute-done.19.refs_4_ = bf16[256,768]{1,0:T(8,128)(2,1)S(1)} collective-permute-done((bf16[256,768]{1,0:T(8,128)(2,1)S(1)}, bf16[256,768]{1,0:T(8,128)(2,1)S(1)}, u32[]{:S(2)}, u32[]{:S(2)}) %collective-permute-start.19) | collective-permute-done | bytes 393248 | tf_op jit(solution)/shard_map/ppermute | solution.py:531
  50.4 3.2 %shard_map.109 = (bf16[128,411]{1,0:T(8,128)(2,1)S(1)}, bf16[128,411]{1,0:T(8,128)(2,1)S(1)}) custom-call(bf16[2048,768]{1,0:T(8,128)(2,1)S(1)} %copy-done, bf16[1536,768]{1,0:T(8,128)(2,1)S(1)} %copy-done.1, f32[8,256,256]{2,1,0:T(8,128)S(1)} %shard_map.107.refs_8_.refs_2_, bf16[256,768]{1,0:T(8,128)(2,1)S(1)} %shard_map.108.refs_3_, ...), custom_call_target="tpu_custom_call" | custom-call | flops 1840250880 | bytes 10093568 | tf_op jit(solution)/shard_map/pallas_call | solution.py:164
  53.6 0.2 collective-permute-start.20
  53.8 1.2 %collective-permute-done.20.refs_1_ = bf16[128,411]{1,0:T(8,128)(2,1)S(1)} collective-permute-done((bf16[128,411]{1,0:T(8,128)(2,1)S(1)}, bf16[128,411]{1,0:T(8,128)(2,1)S(1)}, u32[]{:S(2)}, u32[]{:S(2)}) %collective-permute-start.20) | collective-permute-done | bytes 105248 | tf_op jit(solution)/shard_map/ppermute | solution.py:531
  55.0 0.3 shard_map.110
  55.3 4.8 %collective-permute-start.21 = (bf16[40,411]{1,0:T(8,128)(2,1)S(1)}, bf16[40,411]{1,0:T(8,128)(2,1)S(1)}, u32[]{:S(2)}, u32[]{:S(2)}) collective-permute-start(bf16[40,411]{1,0:T(8,128)(2,1)S(1)} %get-tuple-element.39), channel_id=1, source_target_pairs={{0,8},{8,0},{16,24},{24,16},{1,9},{9,1},{17,25},{25,17},{2,10},{10... | collective-permute-start | bytes 98648 | tf_op jit(solution)/shard_map/ppermute | solution.py:534
  60.0 3.8 %collective-permute-start.22 = (bf16[40,411]{1,0:T(8,128)(2,1)S(1)}, bf16[40,411]{1,0:T(8,128)(2,1)S(1)}, u32[]{:S(2)}, u32[]{:S(2)}) collective-permute-start(bf16[40,411]{1,0:T(8,128)(2,1)S(1)} %get-tuple-element.40), channel_id=1, source_target_pairs={{0,16},{8,24},{16,0},{24,8},{1,17},{9,25},{17,1},{25,9},{2,18},{10... | collective-permute-start | bytes 98648 | tf_op jit(solution)/shard_map/ppermute | solution.py:534
  63.9 0.1 slice_bitcast_fusion.2
  63.9 2.7 %collective-permute-done.22.refs_2_ = bf16[40,411]{1,0:T(8,128)(2,1)S(1)} collective-permute-done((bf16[40,411]{1,0:T(8,128)(2,1)S(1)}, bf16[40,411]{1,0:T(8,128)(2,1)S(1)}, u32[]{:S(2)}, u32[]{:S(2)}) %collective-permute-start.22) | collective-permute-done | bytes 32912 | tf_op jit(solution)/shard_map/ppermute | solution.py:534
  66.7 3.0 %collective-permute-done.23.refs_3_ = bf16[40,411]{1,0:T(8,128)(2,1)S(1)} collective-permute-done((bf16[40,411]{1,0:T(8,128)(2,1)S(1)}, bf16[40,411]{1,0:T(8,128)(2,1)S(1)}, u32[]{:S(2)}, u32[]{:S(2)}) %collective-permute-start.23) | collective-permute-done | bytes 32912 | tf_op jit(solution)/shard_map/ppermute | solution.py:534
  69.7 0.2 shard_map.111
  69.9 0.5 collective-permute-start.24
  70.4 3.0 %collective-permute-start.26 = (bf16[40,411]{1,0:T(8,128)(2,1)S(1)}, bf16[40,411]{1,0:T(8,128)(2,1)S(1)}, u32[]{:S(2)}, u32[]{:S(2)}) collective-permute-start(bf16[40,411]{1,0:T(8,128)(2,1)S(1)} %get-tuple-element.45), channel_id=1, source_target_pairs={{0,6},{1,7},{2,4},{3,5},{4,2},{5,3},{6,0},{7,1},{8,14},{9,15},{10,... | collective-permute-start | bytes 98648 | tf_op jit(solution)/shard_map/ppermute | solution.py:531
  73.4 0.5 collective-permute-done.24.refs_1_
  73.9 0.4 collective-permute-done.25.refs_2_
  74.4 1.0 %collective-permute-done.26.refs_3_ = bf16[40,411]{1,0:T(8,128)(2,1)S(1)} collective-permute-done((bf16[40,411]{1,0:T(8,128)(2,1)S(1)}, bf16[40,411]{1,0:T(8,128)(2,1)S(1)}, u32[]{:S(2)}, u32[]{:S(2)}) %collective-permute-start.26) | collective-permute-done | bytes 32912 | tf_op jit(solution)/shard_map/ppermute | solution.py:531
  75.4 0.1 collective-permute-start.27
  75.5 0.1 maximum_sqrt_fusion
  75.6 0.1 copy.19
  75.7 1.1 %collective-permute-done.27.refs_1_ = f32[40,411]{1,0:T(8,128)S(1)} collective-permute-done((f32[40,411]{1,0:T(8,128)S(1)}, f32[40,411]{1,0:T(8,128)S(1)}, u32[]{:S(2)}, u32[]{:S(2)}) %collective-permute-start.27) | collective-permute-done | bytes 65792 | tf_op jit(solution)/shard_map/ppermute | solution.py:531
  76.8 1.3 %shard_map.113 = f32[4,32,411]{2,1,0:T(8,128)} custom-call(f32[40,411]{1,0:T(8,128)S(1)} %shard_map.112.refs_0_, f32[40,411]{1,0:T(8,128)S(1)} %collective-permute-done.27.refs_1_, f32[48,8]{1,0:T(8,128)S(1)} %bitcast.9), custom_call_target="tpu_custom_call" | custom-call | flops 5260800 | bytes 133056 | tf_op jit(solution)/shard_map/pallas_call | solution.py:164
  (24 shorter events, 0.1 us)
Async XLA Ops:
  0.0 32.2 %copy-start.6 = (s32[256,1]{0,1:T(1,128)S(1)}, s32[256,1]{0,1:T(1,128)}, u32[]{:S(2)}) copy-start(s32[256,1]{0,1:T(1,128)} %param.12) | copy-start | bytes 3076
  0.0 13.1 %collective-permute-start.4 = (bf16[411,256]{1,0:T(8,128)(2,1)}, bf16[411,256]{1,0:T(8,128)(2,1)S(1)}, u32[]{:S(2)}, u32[]{:S(2)}) collective-permute-start(bf16[411,256]{1,0:T(8,128)(2,1)} %refs_0_.4), channel_id=1, source_target_pairs={{0,4},{1,5},{2,6},{3,7},{4,0},{5,1},{6,2},{7,3},{8,12},{9,13},{10,... | collective-permute-start | bytes 631304 | tf_op jit(solution)/shard_map/ppermute | solution.py:531
  3.0 10.1 %collective-permute-start.3 = (bf16[411,256]{1,0:T(8,128)(2,1)}, bf16[411,256]{1,0:T(8,128)(2,1)S(1)}, u32[]{:S(2)}, u32[]{:S(2)}) collective-permute-start(bf16[411,256]{1,0:T(8,128)(2,1)} %refs_0_.4), channel_id=1, source_target_pairs={{0,2},{1,3},{2,0},{3,1},{4,6},{5,7},{6,4},{7,5},{8,10},{9,11},{10,... | collective-permute-start | bytes 631304 | tf_op jit(solution)/shard_map/ppermute | solution.py:531
  4.5 9.8 %collective-permute-start.5 = (bf16[411,256]{1,0:T(8,128)(2,1)}, bf16[411,256]{1,0:T(8,128)(2,1)S(1)}, u32[]{:S(2)}, u32[]{:S(2)}) collective-permute-start(bf16[411,256]{1,0:T(8,128)(2,1)} %refs_0_.4), channel_id=1, source_target_pairs={{0,6},{1,7},{2,4},{3,5},{4,2},{5,3},{6,0},{7,1},{8,14},{9,15},{10,... | collective-permute-start | bytes 631304 | tf_op jit(solution)/shard_map/ppermute | solution.py:531
  4.5 7.8 %collective-permute-start.1 = (bf16[128,768]{1,0:T(8,128)(2,1)}, bf16[128,768]{1,0:T(8,128)(2,1)S(1)}, u32[]{:S(2)}, u32[]{:S(2)}) collective-permute-start(bf16[128,768]{1,0:T(8,128)(2,1)} %refs_9_.1), channel_id=1, source_target_pairs={{0,8},{8,0},{16,24},{24,16},{1,9},{9,1},{17,25},{25,17},{2,10},{10... | collective-permute-start | bytes 589832 | tf_op jit(solution)/shard_map/ppermute | solution.py:534
  8.3 12.0 %copy-start.3 = (bf16[128,768]{1,0:T(8,128)(2,1)S(1)}, bf16[128,768]{1,0:T(8,128)(2,1)}, u32[]{:S(2)}) copy-start(bf16[128,768]{1,0:T(8,128)(2,1)} %refs_9_.1) | copy-start | bytes 589828
  8.3 4.0 %collective-permute-start = (bf16[16,512]{1,0:T(8,128)(2,1)}, bf16[16,512]{1,0:T(8,128)(2,1)S(1)}, u32[]{:S(2)}, u32[]{:S(2)}) collective-permute-start(bf16[16,512]{1,0:T(8,128)(2,1)} %shard_map.101.refs_0_), channel_id=1, source_target_pairs={{0,8},{8,0},{16,24},{24,16},{1,9},{9,1},{17,25},{25,17},{2,10},{10... | collective-permute-start | bytes 49160 | tf_op jit(solution)/shard_map/ppermute | solution.py:534
  12.3 0.7 copy-start.4
  14.2 0.9 %copy-start.2 = (bf16[411,256]{1,0:T(8,128)(2,1)S(1)}, bf16[411,256]{1,0:T(8,128)(2,1)}, u32[]{:S(2)}) copy-start(bf16[411,256]{1,0:T(8,128)(2,1)} %refs_0_.4) | copy-start | bytes 631300
  15.2 5.0 %collective-permute-start.6 = (bf16[1664,256]{1,0:T(8,128)(2,1)S(1)}, bf16[1664,256]{1,0:T(8,128)(2,1)S(1)}, u32[]{:S(2)}, u32[]{:S(2)}) collective-permute-start(bf16[1664,256]{1,0:T(8,128)(2,1)S(1)} %shard_map.103.refs_7_.refs_5_), channel_id=1, source_target_pairs={{0,1},{1,0},{2,3},{3,2},{4,5},{5,4},{6,7},{7,6},{8,9},{9,8},{10,11... | collective-permute-start | bytes 2555912 | tf_op jit(solution)/shard_map/ppermute | solution.py:531
  15.3 4.9 %collective-permute-start.2 = (bf16[32,512]{1,0:T(8,128)(2,1)S(1)}, bf16[32,512]{1,0:T(8,128)(2,1)S(1)}, u32[]{:S(2)}, u32[]{:S(2)}) collective-permute-start(bf16[32,512]{1,0:T(8,128)(2,1)S(1)} %shard_map.102.refs_4_.refs_0_), channel_id=1, source_target_pairs={{0,16},{8,24},{16,0},{24,8},{1,17},{9,25},{17,1},{25,9},{2,18},{10... | collective-permute-start | bytes 98312 | tf_op jit(solution)/shard_map/ppermute | solution.py:534
  20.3 9.1 %collective-permute-start.10 = (bf16[128,768]{1,0:T(8,128)(2,1)S(1)}, bf16[128,768]{1,0:T(8,128)(2,1)S(1)}, u32[]{:S(2)}, u32[]{:S(2)}) collective-permute-start(bf16[128,768]{1,0:T(8,128)(2,1)S(1)} %copy-done.3), channel_id=1, source_target_pairs={{0,16},{1,17},{2,3},{3,2},{4,20},{5,21},{6,7},{7,6},{8,9},{9,8},{1... | collective-permute-start | bytes 589832 | tf_op jit(solution)/shard_map/ppermute | solution.py:543
  23.1 8.6 %collective-permute-start.11 = (bf16[128,768]{1,0:T(8,128)(2,1)S(1)}, bf16[128,768]{1,0:T(8,128)(2,1)S(1)}, u32[]{:S(2)}, u32[]{:S(2)}) collective-permute-start(bf16[128,768]{1,0:T(8,128)(2,1)S(1)} %collective-permute-done.1.refs_2_.refs_10_), channel_id=1, source_target_pairs={{0,16},{1,17},{2,3},{3,2},{4,20},{5,21},{6,7},{7,6},{8,9},{9,8},{1... | collective-permute-start | bytes 589832 | tf_op jit(solution)/shard_map/ppermute | solution.py:543
  23.3 5.2 %collective-permute-start.9 = (bf16[64,512]{1,0:T(8,128)(2,1)S(1)}, bf16[64,512]{1,0:T(8,128)(2,1)S(1)}, u32[]{:S(2)}, u32[]{:S(2)}) collective-permute-start(bf16[64,512]{1,0:T(8,128)(2,1)S(1)} %shard_map.104.refs_0_), channel_id=1, source_target_pairs={{0,6},{1,7},{2,4},{3,5},{4,2},{5,3},{6,0},{7,1},{8,14},{9,15},{10,... | collective-permute-start | bytes 196616 | tf_op jit(solution)/shard_map/ppermute | solution.py:531
  23.5 5.1 %collective-permute-start.8 = (bf16[64,512]{1,0:T(8,128)(2,1)S(1)}, bf16[64,512]{1,0:T(8,128)(2,1)S(1)}, u32[]{:S(2)}, u32[]{:S(2)}) collective-permute-start(bf16[64,512]{1,0:T(8,128)(2,1)S(1)} %shard_map.104.refs_0_), channel_id=1, source_target_pairs={{0,4},{1,5},{2,6},{3,7},{4,0},{5,1},{6,2},{7,3},{8,12},{9,13},{10,... | collective-permute-start | bytes 196616 | tf_op jit(solution)/shard_map/ppermute | solution.py:531
  25.0 4.4 %collective-permute-start.7 = (bf16[64,512]{1,0:T(8,128)(2,1)S(1)}, bf16[64,512]{1,0:T(8,128)(2,1)S(1)}, u32[]{:S(2)}, u32[]{:S(2)}) collective-permute-start(bf16[64,512]{1,0:T(8,128)(2,1)S(1)} %shard_map.104.refs_0_), channel_id=1, source_target_pairs={{0,2},{1,3},{2,0},{3,1},{4,6},{5,7},{6,4},{7,5},{8,10},{9,11},{10,... | collective-permute-start | bytes 196616 | tf_op jit(solution)/shard_map/ppermute | solution.py:531
  32.1 1.6 %collective-permute-start.12 = (bf16[256,512]{1,0:T(8,128)(2,1)S(1)}, bf16[256,512]{1,0:T(8,128)(2,1)S(1)}, u32[]{:S(2)}, u32[]{:S(2)}) collective-permute-start(bf16[256,512]{1,0:T(8,128)(2,1)S(1)} %shard_map.105.refs_5_), channel_id=1, source_target_pairs={{0,1},{1,0},{2,3},{3,2},{4,5},{5,4},{6,7},{7,6},{8,9},{9,8},{10,11... | collective-permute-start | bytes 786440 | tf_op jit(solution)/shard_map/ppermute | solution.py:531
  32.2 1.9 %copy-start = (bf16[2048,768]{1,0:T(8,128)(2,1)S(1)}, bf16[2048,768]{1,0:T(8,128)(2,1)}, u32[]{:S(2)}) copy-start(bf16[2048,768]{1,0:T(8,128)(2,1)} %refs_0_.5) | copy-start | bytes 9437188
  32.2 1.9 %copy-start.5 = (f32[768]{0:T(1024)S(1)}, f32[768]{0:T(1024)}, u32[]{:S(2)}) copy-start(f32[768]{0:T(1024)} %refs_3_.3) | copy-start | bytes 9220
  36.4 7.7 %collective-permute-start.13 = (bf16[128,768]{1,0:T(8,128)(2,1)S(1)}, bf16[128,768]{1,0:T(8,128)(2,1)S(1)}, u32[]{:S(2)}, u32[]{:S(2)}) collective-permute-start(bf16[128,768]{1,0:T(8,128)(2,1)S(1)} %get-tuple-element.32.refs_0_), channel_id=1, source_target_pairs={{0,2},{1,3},{2,0},{3,1},{4,5},{5,4},{6,7},{7,6},{8,10},{9,11},{10,... | collective-permute-start | bytes 589832 | tf_op jit(solution)/shard_map/ppermute | solution.py:543
  36.4 7.8 %collective-permute-start.14 = (bf16[128,768]{1,0:T(8,128)(2,1)S(1)}, bf16[128,768]{1,0:T(8,128)(2,1)S(1)}, u32[]{:S(2)}, u32[]{:S(2)}) collective-permute-start(bf16[128,768]{1,0:T(8,128)(2,1)S(1)} %get-tuple-element.33.refs_1_), channel_id=1, source_target_pairs={{0,4},{1,5},{2,3},{3,2},{4,0},{5,1},{6,7},{7,6},{8,9},{9,8},{10,14... | collective-permute-start | bytes 589832 | tf_op jit(solution)/shard_map/ppermute | solution.py:543
  38.5 9.6 %collective-permute-start.15 = (bf16[128,768]{1,0:T(8,128)(2,1)S(1)}, bf16[128,768]{1,0:T(8,128)(2,1)S(1)}, u32[]{:S(2)}, u32[]{:S(2)}) collective-permute-start(bf16[128,768]{1,0:T(8,128)(2,1)S(1)} %get-tuple-element.32.refs_0_), channel_id=1, source_target_pairs={{0,4},{1,5},{2,3},{3,2},{4,0},{5,1},{6,7},{7,6},{8,9},{9,8},{10,14... | collective-permute-start | bytes 589832 | tf_op jit(solution)/shard_map/ppermute | solution.py:543
  38.5 9.5 %collective-permute-start.16 = (bf16[128,768]{1,0:T(8,128)(2,1)S(1)}, bf16[128,768]{1,0:T(8,128)(2,1)S(1)}, u32[]{:S(2)}, u32[]{:S(2)}) collective-permute-start(bf16[128,768]{1,0:T(8,128)(2,1)S(1)} %get-tuple-element.33.refs_1_), channel_id=1, source_target_pairs={{0,2},{1,3},{2,0},{3,1},{4,5},{5,4},{6,7},{7,6},{8,10},{9,11},{10,... | collective-permute-start | bytes 589832 | tf_op jit(solution)/shard_map/ppermute | solution.py:543
  44.1 3.9 %collective-permute-start.17 = (bf16[128,768]{1,0:T(8,128)(2,1)S(1)}, bf16[128,768]{1,0:T(8,128)(2,1)S(1)}, u32[]{:S(2)}, u32[]{:S(2)}) collective-permute-start(bf16[128,768]{1,0:T(8,128)(2,1)S(1)} %collective-permute-done.13.refs_2_), channel_id=1, source_target_pairs={{0,1},{1,0},{2,6},{3,7},{4,5},{5,4},{6,2},{7,3},{8,12},{9,13},{10,... | collective-permute-start | bytes 589832 | tf_op jit(solution)/shard_map/ppermute | solution.py:543
  44.2 3.8 %collective-permute-start.18 = (bf16[128,768]{1,0:T(8,128)(2,1)S(1)}, bf16[128,768]{1,0:T(8,128)(2,1)S(1)}, u32[]{:S(2)}, u32[]{:S(2)}) collective-permute-start(bf16[128,768]{1,0:T(8,128)(2,1)S(1)} %collective-permute-done.14.refs_3_), channel_id=1, source_target_pairs={{0,1},{1,0},{2,3},{3,2},{4,6},{5,7},{6,4},{7,5},{8,9},{9,8},{10,11... | collective-permute-start | bytes 589832 | tf_op jit(solution)/shard_map/ppermute | solution.py:543
  45.3 5.1 %copy-start.1 = (bf16[1536,768]{1,0:T(8,128)(2,1)S(1)}, bf16[1536,768]{1,0:T(8,128)(2,1)}, u32[]{:S(2)}) copy-start(bf16[1536,768]{1,0:T(8,128)(2,1)} %refs_1_.3) | copy-start | bytes 7077892
  48.6 1.8 %collective-permute-start.19 = (bf16[256,768]{1,0:T(8,128)(2,1)S(1)}, bf16[256,768]{1,0:T(8,128)(2,1)S(1)}, u32[]{:S(2)}, u32[]{:S(2)}) collective-permute-start(bf16[256,768]{1,0:T(8,128)(2,1)S(1)} %shard_map.108.refs_3_), channel_id=1, source_target_pairs={{0,1},{1,0},{2,3},{3,2},{4,5},{5,4},{6,7},{7,6},{8,9},{9,8},{10,11... | collective-permute-start | bytes 1179656 | tf_op jit(solution)/shard_map/ppermute | solution.py:531
  53.6 1.4 %collective-permute-start.20 = (bf16[128,411]{1,0:T(8,128)(2,1)S(1)}, bf16[128,411]{1,0:T(8,128)(2,1)S(1)}, u32[]{:S(2)}, u32[]{:S(2)}) collective-permute-start(bf16[128,411]{1,0:T(8,128)(2,1)S(1)} %get-tuple-element.37), channel_id=1, source_target_pairs={{0,1},{1,0},{2,3},{3,2},{4,5},{5,4},{6,7},{7,6},{8,9},{9,8},{10,11... | collective-permute-start | bytes 315656 | tf_op jit(solution)/shard_map/ppermute | solution.py:531
  55.3 8.7 %collective-permute-start.21 = (bf16[40,411]{1,0:T(8,128)(2,1)S(1)}, bf16[40,411]{1,0:T(8,128)(2,1)S(1)}, u32[]{:S(2)}, u32[]{:S(2)}) collective-permute-start(bf16[40,411]{1,0:T(8,128)(2,1)S(1)} %get-tuple-element.39), channel_id=1, source_target_pairs={{0,8},{8,0},{16,24},{24,16},{1,9},{9,1},{17,25},{25,17},{2,10},{10... | collective-permute-start | bytes 98648 | tf_op jit(solution)/shard_map/ppermute | solution.py:534
  60.0 6.6 %collective-permute-start.22 = (bf16[40,411]{1,0:T(8,128)(2,1)S(1)}, bf16[40,411]{1,0:T(8,128)(2,1)S(1)}, u32[]{:S(2)}, u32[]{:S(2)}) collective-permute-start(bf16[40,411]{1,0:T(8,128)(2,1)S(1)} %get-tuple-element.40), channel_id=1, source_target_pairs={{0,16},{8,24},{16,0},{24,8},{1,17},{9,25},{17,1},{25,9},{2,18},{10... | collective-permute-start | bytes 98648 | tf_op jit(solution)/shard_map/ppermute | solution.py:534
  63.9 5.8 %collective-permute-start.23 = (bf16[40,411]{1,0:T(8,128)(2,1)S(1)}, bf16[40,411]{1,0:T(8,128)(2,1)S(1)}, u32[]{:S(2)}, u32[]{:S(2)}) collective-permute-start(bf16[40,411]{1,0:T(8,128)(2,1)S(1)} %get-tuple-element.41), channel_id=1, source_target_pairs={{0,24},{8,16},{16,8},{24,0},{1,25},{9,17},{17,9},{25,1},{2,26},{10... | collective-permute-start | bytes 98648 | tf_op jit(solution)/shard_map/ppermute | solution.py:534
  69.9 4.1 %collective-permute-start.24 = (bf16[40,411]{1,0:T(8,128)(2,1)S(1)}, bf16[40,411]{1,0:T(8,128)(2,1)S(1)}, u32[]{:S(2)}, u32[]{:S(2)}) collective-permute-start(bf16[40,411]{1,0:T(8,128)(2,1)S(1)} %get-tuple-element.43), channel_id=1, source_target_pairs={{0,2},{1,3},{2,0},{3,1},{4,6},{5,7},{6,4},{7,5},{8,10},{9,11},{10,... | collective-permute-start | bytes 98648 | tf_op jit(solution)/shard_map/ppermute | solution.py:531
  70.4 4.0 %collective-permute-start.25 = (bf16[40,411]{1,0:T(8,128)(2,1)S(1)}, bf16[40,411]{1,0:T(8,128)(2,1)S(1)}, u32[]{:S(2)}, u32[]{:S(2)}) collective-permute-start(bf16[40,411]{1,0:T(8,128)(2,1)S(1)} %get-tuple-element.44), channel_id=1, source_target_pairs={{0,4},{1,5},{2,6},{3,7},{4,0},{5,1},{6,2},{7,3},{8,12},{9,13},{10,... | collective-permute-start | bytes 98648 | tf_op jit(solution)/shard_map/ppermute | solution.py:531
  70.4 5.0 %collective-permute-start.26 = (bf16[40,411]{1,0:T(8,128)(2,1)S(1)}, bf16[40,411]{1,0:T(8,128)(2,1)S(1)}, u32[]{:S(2)}, u32[]{:S(2)}) collective-permute-start(bf16[40,411]{1,0:T(8,128)(2,1)S(1)} %get-tuple-element.45), channel_id=1, source_target_pairs={{0,6},{1,7},{2,4},{3,5},{4,2},{5,3},{6,0},{7,1},{8,14},{9,15},{10,... | collective-permute-start | bytes 98648 | tf_op jit(solution)/shard_map/ppermute | solution.py:531
  75.4 1.3 %collective-permute-start.27 = (f32[40,411]{1,0:T(8,128)S(1)}, f32[40,411]{1,0:T(8,128)S(1)}, u32[]{:S(2)}, u32[]{:S(2)}) collective-permute-start(f32[40,411]{1,0:T(8,128)S(1)} %shard_map.112.refs_0_), channel_id=1, source_target_pairs={{0,1},{1,0},{2,3},{3,2},{4,5},{5,4},{6,7},{7,6},{8,9},{9,8},{10,11... | collective-permute-start | bytes 197288 | tf_op jit(solution)/shard_map/ppermute | solution.py:531

commit v11 on v7

--- a/solution.py
+++ b/solution.py
@@ -10,6 +10,7 @@
 VMEM_BYTES = 24 * 1024 * 1024
 WHOLE_VMEM_BYTES = 63 * 1024 * 1024
 SLACK_FLOPS = 2 * 10**9
+FORWARD_FLOPS = 10**8
 NT_DIMS = (((1,), (1,)), ((), ()))
 
 
@@ -322,9 +323,8 @@
     refs = list(refs)
     take = lambda n: [refs.pop(0) for _ in range(n)]
     place_ref, source_ref, cell_ref, bias_ref, w_radiance_ref = take(5)
-    strip_refs, weight_refs, seen_refs = take(p.group), take(p.group), take(2)
-    part_refs = take(p.steps)
-    preact_ref, kappa_ref, active = refs
+    strip_refs, weight_refs = take(p.group), take(p.group)
+    radiance_ref, in_use_ref, preact_ref, kappa_ref, active = refs
     c = lax.axis_index("chan")
     gathered = [ref[...] for ref in strip_refs]
     columns = sum(
@@ -345,28 +345,33 @@
         preact_ref[k] = preact
         at = pl.multiple_of((c ^ p.mask(k)) * p.hidden, p.hidden)
         active[:, pl.ds(at, p.hidden)] = (preact * jax.nn.sigmoid(preact)).astype(jnp.bfloat16)
-    part = p.rows // p.steps
-    count = seen_refs[0].shape[0]
+    in_use = jnp.zeros((p.rows, 1), jnp.float32)
+    for k in range(p.tiles):
+        slot = lax.broadcasted_iota(jnp.int32, (p.rows, p.slots), 1) + k * p.slots
+        low = k * p.block + p.own_cols + 1
+        flags = strip_refs[0][low : low + 1, p.flag_at : p.flag_at + p.slots]
+        flags = jnp.where(place_ref[...] == slot, flags.astype(jnp.float32), 0.0)
+        in_use = in_use + jnp.sum(flags, axis=1, keepdims=True)
+    in_use_ref[...] = in_use
+    radiance_ref[...] = dot(active[...], w_radiance_ref[...]) + bias_ref[...].reshape(1, p.shard)
+    parts = sum(
+        dot(one_hot(cell_ref[...], k * p.strips, p.strips), strips)
+        for k, strips in enumerate(gathered)
+    )
+    kappa_ref[...] = sum(parts[:, k * p.lane : (k + 1) * p.lane] for k in range(3))
+
+
+def depart_kernel(p, radiance_ref, in_use_ref, place_ref, *refs):
+    seen_refs, part_refs = refs[: -p.steps], refs[-p.steps :]
+    part, count = p.rows // p.steps, seen_refs[0].shape[0]
     for j, part_ref in enumerate(part_refs):
         at = slice(j * part, (j + 1) * part)
-        in_use = jnp.zeros((part, 1), jnp.float32)
-        for k in range(p.tiles):
-            slot = lax.broadcasted_iota(jnp.int32, (part, p.slots), 1) + k * p.slots
-            low = k * p.block + p.own_cols + 1
-            flags = strip_refs[0][low : low + 1, p.flag_at : p.flag_at + p.slots]
-            flags = jnp.where(place_ref[at, :] == slot, flags.astype(jnp.float32), 0.0)
-            in_use = in_use + jnp.sum(flags, axis=1, keepdims=True)
         observed = sum(
             dot(one_hot(place_ref[at, :], k * count, count), ref[...])
             for k, ref in enumerate(seen_refs)
         )
-        radiance = dot(active[at, :], w_radiance_ref[...]) + bias_ref[...].reshape(1, p.shard)
-        part_ref[...] = ((radiance - observed) * in_use).astype(jnp.bfloat16)
-    parts = sum(
-        dot(one_hot(cell_ref[...], k * p.strips, p.strips), strips)
-        for k, strips in enumerate(gathered)
-    )
-    kappa_ref[...] = sum(parts[:, k * p.lane : (k + 1) * p.lane] for k in range(3))
+        departure = (radiance_ref[at, :] - observed) * in_use_ref[at, :]
+        part_ref[...] = departure.astype(jnp.bfloat16)
 
 
 def slope_kernel(preact_ref, slope_ref):
@@ -396,18 +401,22 @@
                 copy.wait()
 
 
+def near_kernel(p, depart_ref, inv_cov_ref, out_ref):
+    at = pl.multiple_of(lax.axis_index("chan") % p.group * p.shard, p.shard)
+    out_ref[...] = dot(depart_ref[...], inv_cov_ref[pl.ds(at, p.shard), :])
+
+
 def backward_kernel(p, *refs):
     refs = list(refs)
     take = lambda n: [refs.pop(0) for _ in range(n)]
-    w_radiance_ref, inv_cov_ref, slope_ref = take(3)
-    depart_refs, weight_refs, target_refs = take(p.group), take(p.group), take(p.group)
+    w_radiance_ref, inv_cov_ref, slope_ref, near_ref = take(4)
+    depart_refs, weight_refs, target_refs = take(p.group - 1), take(p.group), take(p.group)
     out_refs = refs
     c = lax.axis_index("chan")
-    cotangent = None
+    cotangent = near_ref[...]
     for k, ref in enumerate(depart_refs):
-        at = pl.multiple_of((c % p.group ^ k) * p.shard, p.shard)
-        term = dot(ref[...], inv_cov_ref[pl.ds(at, p.shard), :])
-        cotangent = term if cotangent is None else cotangent + term
+        at = pl.multiple_of((c % p.group ^ (k + 1)) * p.shard, p.shard)
+        cotangent = cotangent + dot(ref[...], inv_cov_ref[pl.ds(at, p.shard), :])
     cotangent = cotangent.T.astype(jnp.bfloat16)
     total = jnp.zeros((p.features, p.rows), jnp.float32)
     for k in range(p.chans):
@@ -437,7 +446,7 @@
     total = add(ins).astype(jnp.bfloat16)
     row, along = rows_and_cells(p, outs[0].shape[0])
     for k, out_ref in enumerate(outs):
-        tile = (lax.axis_index("tile") + k) % p.tiles
+        tile = lax.axis_index("tile") ^ k
         cell = (tile * p.own_cols + along + p.tiles * p.own_cols) % (p.tiles * p.own_cols)
         wanted = (cell // p.own_cols * p.rows_each + row) * p.own_cols + cell % p.own_cols
         out_ref[...] = dot(one_hot(wanted, 0, total.shape[0]), total).astype(jnp.bfloat16)
@@ -530,8 +539,8 @@
     def flip(value, mask):
         return lax.ppermute(value, "chan", [(b, b ^ mask) for b in range(p.chans)])
 
-    def shift(value, by):
-        return lax.ppermute(value, "tile", [(a, (a + by) % p.tiles) for a in range(p.tiles)])
+    def trade(value, mask):
+        return lax.ppermute(value, "tile", [(a, a ^ mask) for a in range(p.tiles)])
 
     def send(value, wanted):
         pairs = dict(wanted)
@@ -557,9 +566,6 @@
 
     def grow(value, over, after=()):
         return join([value, over(value)], (2 * value.shape[0],) + value.shape[1:], after)
-
-    def trade(value, mask):
-        return lax.ppermute(value, "tile", [(a, a ^ mask) for a in range(p.tiles)])
 
     strips = call(
         functools.partial(prepare_kernel, p),
@@ -615,13 +621,22 @@
         [owners.reshape(1, p.rows)],
         flops=SLACK_FLOPS,
     )
-    *parts, preact, kappa = call(
+    radiance, in_use, preact, kappa = call(
         functools.partial(forward_kernel, p),
-        [shape((p.rows // p.steps, p.shard), half)] * p.steps
-        + [shape((p.chans, p.rows, p.hidden), single), shape((3 * reach, p.lane), single)],
-        [place, source, cell, b_radiance, w_radiance] + strips + weights + seen,
+        [
+            shape((p.rows, p.shard), single),
+            shape((p.rows, 1), single),
+            shape((p.chans, p.rows, p.hidden), single),
+            shape((3 * reach, p.lane), single),
+        ],
+        [place, source, cell, b_radiance, w_radiance] + strips + weights,
         scratch=[pltpu.VMEM((p.rows, p.hidden * p.chans), half)],
-        flops=2 * p.rows * p.hidden * p.chans * (p.features + p.shard),
+        flops=FORWARD_FLOPS,
+    )
+    parts = call(
+        functools.partial(depart_kernel, p),
+        [shape((p.rows // p.steps, p.shard), half)] * p.steps,
+        [radiance, in_use, place] + seen,
     )
 
     slope = call(
@@ -660,12 +675,18 @@
         out_hbm=True,
         scratch=[pltpu.SemaphoreType.DMA((p.steps,))],
     )
-    depart = [chosen] + [flip(chosen, k) for k in range(1, p.group)]
-
+    depart = [flip(chosen, k) for k in range(1, p.group)]
+
+    partial = call(
+        functools.partial(near_kernel, p),
+        shape((p.rows, p.shard), single),
+        [chosen, inv_cov],
+        flops=2 * p.rows * p.shard * p.shard,
+    )
     partial = call(
         functools.partial(backward_kernel, p),
         [shape((p.rows // p.group, p.features), half)] * p.group,
-        [w_radiance, inv_cov, slope] + depart + weights + targets,
+        [w_radiance, inv_cov, slope, partial] + depart + weights + targets,
         flops=2 * p.rows * (p.hidden * p.chans * (p.features + p.shard) + inv_cov.size),
     )
     partial = [partial[0]] + [flip(partial[k], k) for k in range(1, p.group)]
@@ -674,7 +695,7 @@
         [shape((p.rows_each * p.per_row, p.features), half)] * p.tiles,
         partial,
     )
-    partial = [partial[0]] + [shift(partial[k], k) for k in range(1, p.tiles)]
+    partial = [partial[0]] + [trade(partial[k], k) for k in range(1, p.tiles)]
     partial = call(
         functools.partial(add_tiles_kernel, p),
         [shape((p.around, p.features), half)] * p.chips,

time: 72.3 us -> 72.2 us (level)
  starting transfers between devices: 30.1 us -> 27.8 us
  waiting for transfers between devices: 27.3 us -> 28.4 us
  Pallas kernels: 11.6 us -> 12.4 us
    ppermute x3 -> x0, starting transfers between devices: 7.75 us -> none  [shift(): lax.ppermute(value, 'tile', [(a, (a + by) % p.tiles) for a in range(p.til...]
    ppermute x3 -> x6, starting transfers between devices: 5.82 us -> 10.8 us  [trade(): return lax.ppermute(value, 'tile', [(a, a ^ mask) for a in range(p.tiles)])]
    ppermute x3 -> x6, waiting for transfers between devices: 4.67 us -> 9.52 us  [trade(): return lax.ppermute(value, 'tile', [(a, a ^ mask) for a in range(p.tiles)])]
    ppermute x3 -> x0, waiting for transfers between devices: 2.08 us -> none  [shift(): lax.ppermute(value, 'tile', [(a, (a + by) % p.tiles) for a in range(p.til...]
    ppermute x14, waiting for transfers between devices: 11.2 us -> 10.3 us  [flip(): return lax.ppermute(value, 'chan', [(b, b ^ mask) for b in range(p.chans)])]
    ppermute x7, waiting for transfers between devices: 9.41 us -> 8.58 us  [send(): lax.ppermute(value, both, sorted(((number(a), number(b)) for a, b in pair...]
    pallas_call x15 -> x17, Pallas kernels: 11.6 us -> 12.4 us  [call(): pl.pallas_call(kernel, out_shape=out_shape, in_specs=[far if k in in_hbm...]
  transfers between devices with their start and end apart: 27 -> 27, of which waited for: 18 -> 17; matrix products, arithmetic and copies ran while one was open for 0% -> 0% of each run, Pallas kernels for 5% -> 9%
where the time goes in v11:
time: 72.2 us; the launch traced here: 72 us
  waiting for transfers between devices  28.4 us (39%)
  starting transfers between devices  27.8 us (39%)
  Pallas kernels  12.4 us (17%)
  local copies, waits for them, and re-layouts  3.13 us (4%)
    pallas_call x17, Pallas kernels, call(): pl.pallas_call(kernel, out_shape=out_shape, in_specs=[far if k in in_hbm...  12.4 us
    ppermute x14, starting transfers between devices, flip(): return lax.ppermute(value, 'chan', [(b, b ^ mask) for b in range(p.chans)])  11 us
    ppermute x6, starting transfers between devices, trade(): return lax.ppermute(value, 'tile', [(a, a ^ mask) for a in range(p.tiles)])  10.8 us
    ppermute x14, waiting for transfers between devices, flip(): return lax.ppermute(value, 'chan', [(b, b ^ mask) for b in range(p.chans)])  10.3 us
    ppermute x6, waiting for transfers between devices, trade(): return lax.ppermute(value, 'tile', [(a, a ^ mask) for a in range(p.tiles)])  9.52 us
    ppermute x7, waiting for transfers between devices, send(): lax.ppermute(value, both, sorted(((number(a), number(b)) for a, b in pair...  8.58 us
    ppermute x7, starting transfers between devices, send(): lax.ppermute(value, both, sorted(((number(a), number(b)) for a, b in pair...  6 us
    unnamed x14, local copies, waits for them, and re-layouts  2.97 us
  transfers between devices with their start and end apart: 27, of which 17 were waited for; matrix products, arithmetic and copies ran while one was open for 0% of the time, Pallas kernels for 9%

profile of v11, /device:TPU:0, one launch (start us, length us, event | category | flops | bytes accessed | tf_op | source)
XLA Modules:
  0.0 72.0 jit_solution(13077003693188473004)
XLA Ops:
  0.0 3.0 %collective-permute-start.1 = (bf16[128,768]{1,0:T(8,128)(2,1)}, bf16[128,768]{1,0:T(8,128)(2,1)S(1)}, u32[]{:S(2)}, u32[]{:S(2)}) collective-permute-start(bf16[128,768]{1,0:T(8,128)(2,1)} %refs_0_.5), channel_id=1, source_target_pairs={{0,8},{8,0},{16,24},{24,16},{1,9},{9,1},{17,25},{25,17},{2,10},{10... | collective-permute-start | bytes 589832 | tf_op jit(solution)/shard_map/ppermute | solution.py:543
  3.0 1.5 %collective-permute-start.8 = (bf16[411,256]{1,0:T(8,128)(2,1)}, bf16[411,256]{1,0:T(8,128)(2,1)S(1)}, u32[]{:S(2)}, u32[]{:S(2)}) collective-permute-start(bf16[411,256]{1,0:T(8,128)(2,1)} %refs_0_.6), channel_id=1, source_target_pairs={{0,4},{1,5},{2,6},{3,7},{4,0},{5,1},{6,2},{7,3},{8,12},{9,13},{10,... | collective-permute-start | bytes 631304 | tf_op jit(solution)/shard_map/ppermute | solution.py:540
  4.5 1.5 %collective-permute-start.7 = (bf16[411,256]{1,0:T(8,128)(2,1)}, bf16[411,256]{1,0:T(8,128)(2,1)S(1)}, u32[]{:S(2)}, u32[]{:S(2)}) collective-permute-start(bf16[411,256]{1,0:T(8,128)(2,1)} %refs_0_.6), channel_id=1, source_target_pairs={{0,2},{1,3},{2,0},{3,1},{4,6},{5,7},{6,4},{7,5},{8,10},{9,11},{10,... | collective-permute-start | bytes 631304 | tf_op jit(solution)/shard_map/ppermute | solution.py:540
  6.0 0.5 collective-permute-start.9
  6.5 1.8 %shard_map.101.refs_0_ = bf16[16,512]{1,0:T(8,128)(2,1)} custom-call(f32[4,32,411]{2,1,0:T(8,128)} %refs_0_.4, f32[4,32]{1,0:T(4,128)} %refs_1_.2, s32[128]{0:T(128)} %refs_2_.1, f32[256]{0:T(256)} %refs_3_.2), custom_call_target="tpu_custom_call" | custom-call | bytes 212480 | tf_op jit(solution)/shard_map/pallas_call | solution.py:165
  8.3 0.1 collective-permute-start
  8.4 0.9 %copy-done.3 = bf16[128,768]{1,0:T(8,128)(2,1)S(1)} copy-done((bf16[128,768]{1,0:T(8,128)(2,1)S(1)}, bf16[128,768]{1,0:T(8,128)(2,1)}, u32[]{:S(2)}) %copy-start.3) | copy-done | bytes 196632
  9.4 0.5 shard_map.102.refs_2_.refs_0_
  9.9 2.5 %collective-permute-done.refs_1_ = bf16[16,512]{1,0:T(8,128)(2,1)S(1)} collective-permute-done((bf16[16,512]{1,0:T(8,128)(2,1)}, bf16[16,512]{1,0:T(8,128)(2,1)S(1)}, u32[]{:S(2)}, u32[]{:S(2)}) %collective-permute-start) | collective-permute-done | bytes 16416 | tf_op jit(solution)/shard_map/ppermute | solution.py:543
  12.3 0.7 copy-done.4
  13.1 2.7 %collective-permute-start.2 = (bf16[32,512]{1,0:T(8,128)(2,1)S(1)}, bf16[32,512]{1,0:T(8,128)(2,1)S(1)}, u32[]{:S(2)}, u32[]{:S(2)}) collective-permute-start(bf16[32,512]{1,0:T(8,128)(2,1)S(1)} %shard_map.103.refs_0_), channel_id=1, source_target_pairs={{0,16},{8,24},{16,0},{24,8},{1,17},{9,25},{17,1},{25,9},{2,18},{10... | collective-permute-start | bytes 98312 | tf_op jit(solution)/shard_map/ppermute | solution.py:543
  15.7 2.2 %collective-permute-done.2.refs_1_ = bf16[32,512]{1,0:T(8,128)(2,1)S(1)} collective-permute-done((bf16[32,512]{1,0:T(8,128)(2,1)S(1)}, bf16[32,512]{1,0:T(8,128)(2,1)S(1)}, u32[]{:S(2)}, u32[]{:S(2)}) %collective-permute-start.2) | collective-permute-done | bytes 32800 | tf_op jit(solution)/shard_map/ppermute | solution.py:543
  18.0 0.1 shard_map.104.refs_0_.refs_4_
  18.1 0.0 copy-start.2
  18.1 0.9 %copy-done.2 = bf16[411,256]{1,0:T(8,128)(2,1)S(1)} copy-done((bf16[411,256]{1,0:T(8,128)(2,1)S(1)}, bf16[411,256]{1,0:T(8,128)(2,1)}, u32[]{:S(2)}) %copy-start.2) | copy-done | bytes 210456
  19.0 0.1 shard_map.106.refs_7_.refs_5_
  19.1 0.1 collective-permute-start.10
  19.2 2.7 %collective-permute-start.11 = (bf16[256,768]{1,0:T(8,128)(2,1)S(1)}, bf16[256,768]{1,0:T(8,128)(2,1)S(1)}, u32[]{:S(2)}, u32[]{:S(2)}) collective-permute-start(bf16[256,768]{1,0:T(8,128)(2,1)S(1)} %shard_map.102.refs_2_.refs_0_), channel_id=1, source_target_pairs={{0,16},{1,17},{2,3},{3,2},{4,20},{5,21},{6,7},{7,6},{8,9},{9,8},{1... | collective-permute-start | bytes 1179656 | tf_op jit(solution)/shard_map/ppermute | solution.py:552
  21.8 0.5 collective-permute-start.5
  22.3 1.0 %collective-permute-start.4 = (bf16[64,512]{1,0:T(8,128)(2,1)S(1)}, bf16[64,512]{1,0:T(8,128)(2,1)S(1)}, u32[]{:S(2)}, u32[]{:S(2)}) collective-permute-start(bf16[64,512]{1,0:T(8,128)(2,1)S(1)} %shard_map.104.refs_0_.refs_4_), channel_id=1, source_target_pairs={{0,4},{1,5},{2,6},{3,7},{4,0},{5,1},{6,2},{7,3},{8,12},{9,13},{10,... | collective-permute-start | bytes 196616 | tf_op jit(solution)/shard_map/ppermute | solution.py:540
  23.3 2.0 %collective-permute-start.3 = (bf16[64,512]{1,0:T(8,128)(2,1)S(1)}, bf16[64,512]{1,0:T(8,128)(2,1)S(1)}, u32[]{:S(2)}, u32[]{:S(2)}) collective-permute-start(bf16[64,512]{1,0:T(8,128)(2,1)S(1)} %shard_map.104.refs_0_.refs_4_), channel_id=1, source_target_pairs={{0,2},{1,3},{2,0},{3,1},{4,6},{5,7},{6,4},{7,5},{8,10},{9,11},{10,... | collective-permute-start | bytes 196616 | tf_op jit(solution)/shard_map/ppermute | solution.py:540
  25.3 2.0 %collective-permute-done.5.refs_3_ = bf16[64,512]{1,0:T(8,128)(2,1)S(1)} collective-permute-done((bf16[64,512]{1,0:T(8,128)(2,1)S(1)}, bf16[64,512]{1,0:T(8,128)(2,1)S(1)}, u32[]{:S(2)}, u32[]{:S(2)}) %collective-permute-start.5) | collective-permute-done | bytes 65568 | tf_op jit(solution)/shard_map/ppermute | solution.py:540
  27.3 0.2 collective-permute-done.4.refs_2_
  27.6 0.7 %collective-permute-done.3.refs_1_ = bf16[64,512]{1,0:T(8,128)(2,1)S(1)} collective-permute-done((bf16[64,512]{1,0:T(8,128)(2,1)S(1)}, bf16[64,512]{1,0:T(8,128)(2,1)S(1)}, u32[]{:S(2)}, u32[]{:S(2)}) %collective-permute-start.3) | collective-permute-done | bytes 65568 | tf_op jit(solution)/shard_map/ppermute | solution.py:540
  28.3 0.3 shard_map.105.refs_5_
  28.7 0.1 collective-permute-start.6
  28.8 0.4 shard_map.100
  29.2 1.1 %collective-permute-done.6.refs_6_ = bf16[256,512]{1,0:T(8,128)(2,1)S(1)} collective-permute-done((bf16[256,512]{1,0:T(8,128)(2,1)S(1)}, bf16[256,512]{1,0:T(8,128)(2,1)S(1)}, u32[]{:S(2)}, u32[]{:S(2)}) %collective-permute-start.6) | collective-permute-done | bytes 262176 | tf_op jit(solution)/shard_map/ppermute | solution.py:540
  30.3 0.4 copy-done
  30.7 2.3 %shard_map.107 = (f32[256,768]{1,0:T(8,128)S(1)}, f32[256,1]{1,0:T(8,128)S(1)}, f32[8,256,256]{2,1,0:T(8,128)S(1)}, f32[24,128]{1,0:T(8,128)S(1)}) custom-call(s32[256,1]{1,0:T(8,128)S(1)} %get-tuple-element.26.refs_0_.place_ref, s32[256,1]{1,0:T(8,128)S(1)} %get-tuple-element.27.refs_1_, s32[24,1]{1,0:T(8,128)S(1)} %get-tuple-element.28.refs_2_, ...), custom_call_target="tpu_custom_call" | custom-call | flops 100000000 | bytes 5379168 | tf_op jit(solution)/shard_map/pallas_call | solution.py:165
  33.0 0.4 shard_map.109
  33.4 1.3 %collective-permute-start.12 = (bf16[128,768]{1,0:T(8,128)(2,1)S(1)}, bf16[128,768]{1,0:T(8,128)(2,1)S(1)}, u32[]{:S(2)}, u32[]{:S(2)}) collective-permute-start(bf16[128,768]{1,0:T(8,128)(2,1)S(1)} %get-tuple-element.32.refs_0_), channel_id=1, source_target_pairs={{0,2},{1,3},{2,0},{3,1},{4,5},{5,4},{6,7},{7,6},{8,10},{9,11},{10,... | collective-permute-start | bytes 589832 | tf_op jit(solution)/shard_map/ppermute | solution.py:552
  34.7 0.0 collective-permute-start.13
  34.8 2.0 %collective-permute-start.14 = (bf16[128,768]{1,0:T(8,128)(2,1)S(1)}, bf16[128,768]{1,0:T(8,128)(2,1)S(1)}, u32[]{:S(2)}, u32[]{:S(2)}) collective-permute-start(bf16[128,768]{1,0:T(8,128)(2,1)S(1)} %get-tuple-element.32.refs_0_), channel_id=1, source_target_pairs={{0,4},{1,5},{2,3},{3,2},{4,0},{5,1},{6,7},{7,6},{8,9},{9,8},{10,14... | collective-permute-start | bytes 589832 | tf_op jit(solution)/shard_map/ppermute | solution.py:552
  36.8 4.4 %collective-permute-done.12.refs_2_ = bf16[128,768]{1,0:T(8,128)(2,1)S(1)} collective-permute-done((bf16[128,768]{1,0:T(8,128)(2,1)S(1)}, bf16[128,768]{1,0:T(8,128)(2,1)S(1)}, u32[]{:S(2)}, u32[]{:S(2)}) %collective-permute-start.12) | collective-permute-done | bytes 196640 | tf_op jit(solution)/shard_map/ppermute | solution.py:552
  41.2 1.3 %collective-permute-done.13.refs_3_ = bf16[128,768]{1,0:T(8,128)(2,1)S(1)} collective-permute-done((bf16[128,768]{1,0:T(8,128)(2,1)S(1)}, bf16[128,768]{1,0:T(8,128)(2,1)S(1)}, u32[]{:S(2)}, u32[]{:S(2)}) %collective-permute-start.13) | collective-permute-done | bytes 196640 | tf_op jit(solution)/shard_map/ppermute | solution.py:552
  42.5 0.6 shard_map.108.refs_8_.refs_2_
  43.1 2.9 %collective-permute-done.14.refs_4_ = bf16[128,768]{1,0:T(8,128)(2,1)S(1)} collective-permute-done((bf16[128,768]{1,0:T(8,128)(2,1)S(1)}, bf16[128,768]{1,0:T(8,128)(2,1)S(1)}, u32[]{:S(2)}, u32[]{:S(2)}) %collective-permute-start.14) | collective-permute-done | bytes 196640 | tf_op jit(solution)/shard_map/ppermute | solution.py:552
  46.0 0.6 shard_map.110.depart_ref
  46.5 0.1 collective-permute-start.18
  46.6 0.5 shard_map.111.refs_3_
  47.1 1.2 %collective-permute-done.18.refs_4_ = bf16[256,768]{1,0:T(8,128)(2,1)S(1)} collective-permute-done((bf16[256,768]{1,0:T(8,128)(2,1)S(1)}, bf16[256,768]{1,0:T(8,128)(2,1)S(1)}, u32[]{:S(2)}, u32[]{:S(2)}) %collective-permute-start.18) | collective-permute-done | bytes 393248 | tf_op jit(solution)/shard_map/ppermute | solution.py:540
  48.3 2.9 %shard_map.112 = (bf16[128,411]{1,0:T(8,128)(2,1)S(1)}, bf16[128,411]{1,0:T(8,128)(2,1)S(1)}) custom-call(bf16[2048,768]{1,0:T(8,128)(2,1)S(1)} %copy-done, bf16[1536,768]{1,0:T(8,128)(2,1)S(1)} %copy-done.1, f32[8,256,256]{2,1,0:T(8,128)S(1)} %shard_map.108.refs_8_.refs_2_, f32[256,768]{1,0:T(8,128)S(1)} %shard_map.111.refs_3_, ...), custom_call_target="tpu_custom_call" | custom-call | flops 1840250880 | bytes 10486784 | tf_op jit(solution)/shard_map/pallas_call | solution.py:165
  51.2 0.2 collective-permute-start.19
  51.4 1.2 %collective-permute-done.19.refs_1_ = bf16[128,411]{1,0:T(8,128)(2,1)S(1)} collective-permute-done((bf16[128,411]{1,0:T(8,128)(2,1)S(1)}, bf16[128,411]{1,0:T(8,128)(2,1)S(1)}, u32[]{:S(2)}, u32[]{:S(2)}) %collective-permute-start.19) | collective-permute-done | bytes 105248 | tf_op jit(solution)/shard_map/ppermute | solution.py:540
  52.7 0.3 shard_map.113
  52.9 2.5 %collective-permute-start.20 = (bf16[40,411]{1,0:T(8,128)(2,1)S(1)}, bf16[40,411]{1,0:T(8,128)(2,1)S(1)}, u32[]{:S(2)}, u32[]{:S(2)}) collective-permute-start(bf16[40,411]{1,0:T(8,128)(2,1)S(1)} %get-tuple-element.39), channel_id=1, source_target_pairs={{0,8},{8,0},{16,24},{24,16},{1,9},{9,1},{17,25},{25,17},{2,10},{10... | collective-permute-start | bytes 98648 | tf_op jit(solution)/shard_map/ppermute | solution.py:543
  55.4 1.6 %collective-permute-start.21 = (bf16[40,411]{1,0:T(8,128)(2,1)S(1)}, bf16[40,411]{1,0:T(8,128)(2,1)S(1)}, u32[]{:S(2)}, u32[]{:S(2)}) collective-permute-start(bf16[40,411]{1,0:T(8,128)(2,1)S(1)} %get-tuple-element.40), channel_id=1, source_target_pairs={{0,16},{8,24},{16,0},{24,8},{1,17},{9,25},{17,1},{25,9},{2,18},{10... | collective-permute-start | bytes 98648 | tf_op jit(solution)/shard_map/ppermute | solution.py:543
  57.0 0.9 %collective-permute-start.22 = (bf16[40,411]{1,0:T(8,128)(2,1)S(1)}, bf16[40,411]{1,0:T(8,128)(2,1)S(1)}, u32[]{:S(2)}, u32[]{:S(2)}) collective-permute-start(bf16[40,411]{1,0:T(8,128)(2,1)S(1)} %get-tuple-element.41), channel_id=1, source_target_pairs={{0,24},{8,16},{16,8},{24,0},{1,25},{9,17},{17,9},{25,1},{2,26},{10... | collective-permute-start | bytes 98648 | tf_op jit(solution)/shard_map/ppermute | solution.py:543
  57.9 0.1 slice_bitcast_fusion.2
  57.9 2.9 %collective-permute-done.21.refs_2_ = bf16[40,411]{1,0:T(8,128)(2,1)S(1)} collective-permute-done((bf16[40,411]{1,0:T(8,128)(2,1)S(1)}, bf16[40,411]{1,0:T(8,128)(2,1)S(1)}, u32[]{:S(2)}, u32[]{:S(2)}) %collective-permute-start.21) | collective-permute-done | bytes 32912 | tf_op jit(solution)/shard_map/ppermute | solution.py:543
  60.9 1.9 %collective-permute-done.22.refs_3_ = bf16[40,411]{1,0:T(8,128)(2,1)S(1)} collective-permute-done((bf16[40,411]{1,0:T(8,128)(2,1)S(1)}, bf16[40,411]{1,0:T(8,128)(2,1)S(1)}, u32[]{:S(2)}, u32[]{:S(2)}) %collective-permute-start.22) | collective-permute-done | bytes 32912 | tf_op jit(solution)/shard_map/ppermute | solution.py:543
  62.8 0.2 shard_map.114
  63.0 0.5 collective-permute-start.23
  63.5 0.9 %collective-permute-start.24 = (bf16[40,411]{1,0:T(8,128)(2,1)S(1)}, bf16[40,411]{1,0:T(8,128)(2,1)S(1)}, u32[]{:S(2)}, u32[]{:S(2)}) collective-permute-start(bf16[40,411]{1,0:T(8,128)(2,1)S(1)} %get-tuple-element.44), channel_id=1, source_target_pairs={{0,4},{1,5},{2,6},{3,7},{4,0},{5,1},{6,2},{7,3},{8,12},{9,13},{10,... | collective-permute-start | bytes 98648 | tf_op jit(solution)/shard_map/ppermute | solution.py:540
  64.4 2.2 %collective-permute-start.25 = (bf16[40,411]{1,0:T(8,128)(2,1)S(1)}, bf16[40,411]{1,0:T(8,128)(2,1)S(1)}, u32[]{:S(2)}, u32[]{:S(2)}) collective-permute-start(bf16[40,411]{1,0:T(8,128)(2,1)S(1)} %get-tuple-element.45), channel_id=1, source_target_pairs={{0,6},{1,7},{2,4},{3,5},{4,2},{5,3},{6,0},{7,1},{8,14},{9,15},{10,... | collective-permute-start | bytes 98648 | tf_op jit(solution)/shard_map/ppermute | solution.py:540
  66.6 0.5 collective-permute-done.23.refs_1_
  67.1 0.4 collective-permute-done.24.refs_2_
  67.5 1.8 %collective-permute-done.25.refs_3_ = bf16[40,411]{1,0:T(8,128)(2,1)S(1)} collective-permute-done((bf16[40,411]{1,0:T(8,128)(2,1)S(1)}, bf16[40,411]{1,0:T(8,128)(2,1)S(1)}, u32[]{:S(2)}, u32[]{:S(2)}) %collective-permute-start.25) | collective-permute-done | bytes 32912 | tf_op jit(solution)/shard_map/ppermute | solution.py:540
  69.3 0.1 collective-permute-start.26
  69.4 0.1 maximum_sqrt_fusion
  69.5 0.1 copy.19
  69.6 1.1 %collective-permute-done.26.refs_1_ = f32[40,411]{1,0:T(8,128)S(1)} collective-permute-done((f32[40,411]{1,0:T(8,128)S(1)}, f32[40,411]{1,0:T(8,128)S(1)}, u32[]{:S(2)}, u32[]{:S(2)}) %collective-permute-start.26) | collective-permute-done | bytes 65792 | tf_op jit(solution)/shard_map/ppermute | solution.py:540
  70.7 1.3 %shard_map.116 = f32[4,32,411]{2,1,0:T(8,128)} custom-call(f32[40,411]{1,0:T(8,128)S(1)} %shard_map.115.refs_0_, f32[40,411]{1,0:T(8,128)S(1)} %collective-permute-done.26.refs_1_, f32[48,8]{1,0:T(8,128)S(1)} %bitcast.9), custom_call_target="tpu_custom_call" | custom-call | flops 5260800 | bytes 133056 | tf_op jit(solution)/shard_map/pallas_call | solution.py:165
  (25 shorter events, 0.1 us)
Async XLA Ops:
  0.0 28.8 %copy-start.6 = (s32[256,1]{0,1:T(1,128)S(1)}, s32[256,1]{0,1:T(1,128)}, u32[]{:S(2)}) copy-start(s32[256,1]{0,1:T(1,128)} %param.12) | copy-start | bytes 3076
  0.0 8.4 %collective-permute-start.1 = (bf16[128,768]{1,0:T(8,128)(2,1)}, bf16[128,768]{1,0:T(8,128)(2,1)S(1)}, u32[]{:S(2)}, u32[]{:S(2)}) collective-permute-start(bf16[128,768]{1,0:T(8,128)(2,1)} %refs_0_.5), channel_id=1, source_target_pairs={{0,8},{8,0},{16,24},{24,16},{1,9},{9,1},{17,25},{25,17},{2,10},{10... | collective-permute-start | bytes 589832 | tf_op jit(solution)/shard_map/ppermute | solution.py:543
  3.0 15.0 %collective-permute-start.8 = (bf16[411,256]{1,0:T(8,128)(2,1)}, bf16[411,256]{1,0:T(8,128)(2,1)S(1)}, u32[]{:S(2)}, u32[]{:S(2)}) collective-permute-start(bf16[411,256]{1,0:T(8,128)(2,1)} %refs_0_.6), channel_id=1, source_target_pairs={{0,4},{1,5},{2,6},{3,7},{4,0},{5,1},{6,2},{7,3},{8,12},{9,13},{10,... | collective-permute-start | bytes 631304 | tf_op jit(solution)/shard_map/ppermute | solution.py:540
  4.5 13.5 %collective-permute-start.7 = (bf16[411,256]{1,0:T(8,128)(2,1)}, bf16[411,256]{1,0:T(8,128)(2,1)S(1)}, u32[]{:S(2)}, u32[]{:S(2)}) collective-permute-start(bf16[411,256]{1,0:T(8,128)(2,1)} %refs_0_.6), channel_id=1, source_target_pairs={{0,2},{1,3},{2,0},{3,1},{4,6},{5,7},{6,4},{7,5},{8,10},{9,11},{10,... | collective-permute-start | bytes 631304 | tf_op jit(solution)/shard_map/ppermute | solution.py:540
  6.0 12.0 %collective-permute-start.9 = (bf16[411,256]{1,0:T(8,128)(2,1)}, bf16[411,256]{1,0:T(8,128)(2,1)S(1)}, u32[]{:S(2)}, u32[]{:S(2)}) collective-permute-start(bf16[411,256]{1,0:T(8,128)(2,1)} %refs_0_.6), channel_id=1, source_target_pairs={{0,6},{1,7},{2,4},{3,5},{4,2},{5,3},{6,0},{7,1},{8,14},{9,15},{10,... | collective-permute-start | bytes 631304 | tf_op jit(solution)/shard_map/ppermute | solution.py:540
  8.3 4.0 %collective-permute-start = (bf16[16,512]{1,0:T(8,128)(2,1)}, bf16[16,512]{1,0:T(8,128)(2,1)S(1)}, u32[]{:S(2)}, u32[]{:S(2)}) collective-permute-start(bf16[16,512]{1,0:T(8,128)(2,1)} %shard_map.101.refs_0_), channel_id=1, source_target_pairs={{0,8},{8,0},{16,24},{24,16},{1,9},{9,1},{17,25},{25,17},{2,10},{10... | collective-permute-start | bytes 49160 | tf_op jit(solution)/shard_map/ppermute | solution.py:543
  8.4 0.9 %copy-start.3 = (bf16[128,768]{1,0:T(8,128)(2,1)S(1)}, bf16[128,768]{1,0:T(8,128)(2,1)}, u32[]{:S(2)}) copy-start(bf16[128,768]{1,0:T(8,128)(2,1)} %refs_0_.5) | copy-start | bytes 589828
  12.3 0.7 copy-start.4
  13.1 4.9 %collective-permute-start.2 = (bf16[32,512]{1,0:T(8,128)(2,1)S(1)}, bf16[32,512]{1,0:T(8,128)(2,1)S(1)}, u32[]{:S(2)}, u32[]{:S(2)}) collective-permute-start(bf16[32,512]{1,0:T(8,128)(2,1)S(1)} %shard_map.103.refs_0_), channel_id=1, source_target_pairs={{0,16},{8,24},{16,0},{24,8},{1,17},{9,25},{17,1},{25,9},{2,18},{10... | collective-permute-start | bytes 98312 | tf_op jit(solution)/shard_map/ppermute | solution.py:543
  18.1 0.9 %copy-start.2 = (bf16[411,256]{1,0:T(8,128)(2,1)S(1)}, bf16[411,256]{1,0:T(8,128)(2,1)}, u32[]{:S(2)}) copy-start(bf16[411,256]{1,0:T(8,128)(2,1)} %refs_0_.6) | copy-start | bytes 631300
  19.1 11.2 %collective-permute-start.10 = (bf16[1664,256]{1,0:T(8,128)(2,1)S(1)}, bf16[1664,256]{1,0:T(8,128)(2,1)S(1)}, u32[]{:S(2)}, u32[]{:S(2)}) collective-permute-start(bf16[1664,256]{1,0:T(8,128)(2,1)S(1)} %shard_map.106.refs_7_.refs_5_), channel_id=1, source_target_pairs={{0,1},{1,0},{2,3},{3,2},{4,5},{5,4},{6,7},{7,6},{8,9},{9,8},{10,11... | collective-permute-start | bytes 2555912 | tf_op jit(solution)/shard_map/ppermute | solution.py:540
  19.2 13.8 %collective-permute-start.11 = (bf16[256,768]{1,0:T(8,128)(2,1)S(1)}, bf16[256,768]{1,0:T(8,128)(2,1)S(1)}, u32[]{:S(2)}, u32[]{:S(2)}) collective-permute-start(bf16[256,768]{1,0:T(8,128)(2,1)S(1)} %shard_map.102.refs_2_.refs_0_), channel_id=1, source_target_pairs={{0,16},{1,17},{2,3},{3,2},{4,20},{5,21},{6,7},{7,6},{8,9},{9,8},{1... | collective-permute-start | bytes 1179656 | tf_op jit(solution)/shard_map/ppermute | solution.py:552
  21.8 5.5 %collective-permute-start.5 = (bf16[64,512]{1,0:T(8,128)(2,1)S(1)}, bf16[64,512]{1,0:T(8,128)(2,1)S(1)}, u32[]{:S(2)}, u32[]{:S(2)}) collective-permute-start(bf16[64,512]{1,0:T(8,128)(2,1)S(1)} %shard_map.104.refs_0_.refs_4_), channel_id=1, source_target_pairs={{0,6},{1,7},{2,4},{3,5},{4,2},{5,3},{6,0},{7,1},{8,14},{9,15},{10,... | collective-permute-start | bytes 196616 | tf_op jit(solution)/shard_map/ppermute | solution.py:540
  22.3 5.2 %collective-permute-start.4 = (bf16[64,512]{1,0:T(8,128)(2,1)S(1)}, bf16[64,512]{1,0:T(8,128)(2,1)S(1)}, u32[]{:S(2)}, u32[]{:S(2)}) collective-permute-start(bf16[64,512]{1,0:T(8,128)(2,1)S(1)} %shard_map.104.refs_0_.refs_4_), channel_id=1, source_target_pairs={{0,4},{1,5},{2,6},{3,7},{4,0},{5,1},{6,2},{7,3},{8,12},{9,13},{10,... | collective-permute-start | bytes 196616 | tf_op jit(solution)/shard_map/ppermute | solution.py:540
  23.3 5.0 %collective-permute-start.3 = (bf16[64,512]{1,0:T(8,128)(2,1)S(1)}, bf16[64,512]{1,0:T(8,128)(2,1)S(1)}, u32[]{:S(2)}, u32[]{:S(2)}) collective-permute-start(bf16[64,512]{1,0:T(8,128)(2,1)S(1)} %shard_map.104.refs_0_.refs_4_), channel_id=1, source_target_pairs={{0,2},{1,3},{2,0},{3,1},{4,6},{5,7},{6,4},{7,5},{8,10},{9,11},{10,... | collective-permute-start | bytes 196616 | tf_op jit(solution)/shard_map/ppermute | solution.py:540
  28.7 1.6 %collective-permute-start.6 = (bf16[256,512]{1,0:T(8,128)(2,1)S(1)}, bf16[256,512]{1,0:T(8,128)(2,1)S(1)}, u32[]{:S(2)}, u32[]{:S(2)}) collective-permute-start(bf16[256,512]{1,0:T(8,128)(2,1)S(1)} %shard_map.105.refs_5_), channel_id=1, source_target_pairs={{0,1},{1,0},{2,3},{3,2},{4,5},{5,4},{6,7},{7,6},{8,9},{9,8},{10,11... | collective-permute-start | bytes 786440 | tf_op jit(solution)/shard_map/ppermute | solution.py:540
  28.8 1.9 %copy-start = (bf16[2048,768]{1,0:T(8,128)(2,1)S(1)}, bf16[2048,768]{1,0:T(8,128)(2,1)}, u32[]{:S(2)}) copy-start(bf16[2048,768]{1,0:T(8,128)(2,1)} %refs_0_.7) | copy-start | bytes 9437188
  28.8 1.9 %copy-start.5 = (f32[768]{0:T(1024)S(1)}, f32[768]{0:T(1024)}, u32[]{:S(2)}) copy-start(f32[768]{0:T(1024)} %refs_3_.3) | copy-start | bytes 9220
  33.4 7.8 %collective-permute-start.12 = (bf16[128,768]{1,0:T(8,128)(2,1)S(1)}, bf16[128,768]{1,0:T(8,128)(2,1)S(1)}, u32[]{:S(2)}, u32[]{:S(2)}) collective-permute-start(bf16[128,768]{1,0:T(8,128)(2,1)S(1)} %get-tuple-element.32.refs_0_), channel_id=1, source_target_pairs={{0,2},{1,3},{2,0},{3,1},{4,5},{5,4},{6,7},{7,6},{8,10},{9,11},{10,... | collective-permute-start | bytes 589832 | tf_op jit(solution)/shard_map/ppermute | solution.py:552
  34.7 7.7 %collective-permute-start.13 = (bf16[128,768]{1,0:T(8,128)(2,1)S(1)}, bf16[128,768]{1,0:T(8,128)(2,1)S(1)}, u32[]{:S(2)}, u32[]{:S(2)}) collective-permute-start(bf16[128,768]{1,0:T(8,128)(2,1)S(1)} %get-tuple-element.33.refs_1_), channel_id=1, source_target_pairs={{0,4},{1,5},{2,3},{3,2},{4,0},{5,1},{6,7},{7,6},{8,9},{9,8},{10,14... | collective-permute-start | bytes 589832 | tf_op jit(solution)/shard_map/ppermute | solution.py:552
  34.8 11.2 %collective-permute-start.14 = (bf16[128,768]{1,0:T(8,128)(2,1)S(1)}, bf16[128,768]{1,0:T(8,128)(2,1)S(1)}, u32[]{:S(2)}, u32[]{:S(2)}) collective-permute-start(bf16[128,768]{1,0:T(8,128)(2,1)S(1)} %get-tuple-element.32.refs_0_), channel_id=1, source_target_pairs={{0,4},{1,5},{2,3},{3,2},{4,0},{5,1},{6,7},{7,6},{8,9},{9,8},{10,14... | collective-permute-start | bytes 589832 | tf_op jit(solution)/shard_map/ppermute | solution.py:552
  36.8 9.2 %collective-permute-start.15 = (bf16[128,768]{1,0:T(8,128)(2,1)S(1)}, bf16[128,768]{1,0:T(8,128)(2,1)S(1)}, u32[]{:S(2)}, u32[]{:S(2)}) collective-permute-start(bf16[128,768]{1,0:T(8,128)(2,1)S(1)} %get-tuple-element.33.refs_1_), channel_id=1, source_target_pairs={{0,2},{1,3},{2,0},{3,1},{4,5},{5,4},{6,7},{7,6},{8,10},{9,11},{10,... | collective-permute-start | bytes 589832 | tf_op jit(solution)/shard_map/ppermute | solution.py:552
  41.2 4.8 %collective-permute-start.16 = (bf16[128,768]{1,0:T(8,128)(2,1)S(1)}, bf16[128,768]{1,0:T(8,128)(2,1)S(1)}, u32[]{:S(2)}, u32[]{:S(2)}) collective-permute-start(bf16[128,768]{1,0:T(8,128)(2,1)S(1)} %collective-permute-done.12.refs_2_), channel_id=1, source_target_pairs={{0,1},{1,0},{2,6},{3,7},{4,5},{5,4},{6,2},{7,3},{8,12},{9,13},{10,... | collective-permute-start | bytes 589832 | tf_op jit(solution)/shard_map/ppermute | solution.py:552
  42.5 3.5 %collective-permute-start.17 = (bf16[128,768]{1,0:T(8,128)(2,1)S(1)}, bf16[128,768]{1,0:T(8,128)(2,1)S(1)}, u32[]{:S(2)}, u32[]{:S(2)}) collective-permute-start(bf16[128,768]{1,0:T(8,128)(2,1)S(1)} %collective-permute-done.13.refs_3_), channel_id=1, source_target_pairs={{0,1},{1,0},{2,3},{3,2},{4,6},{5,7},{6,4},{7,5},{8,9},{9,8},{10,11... | collective-permute-start | bytes 589832 | tf_op jit(solution)/shard_map/ppermute | solution.py:552
  43.1 3.5 %copy-start.1 = (bf16[1536,768]{1,0:T(8,128)(2,1)S(1)}, bf16[1536,768]{1,0:T(8,128)(2,1)}, u32[]{:S(2)}) copy-start(bf16[1536,768]{1,0:T(8,128)(2,1)} %refs_1_.3) | copy-start | bytes 7077892
  46.5 1.8 %collective-permute-start.18 = (bf16[256,768]{1,0:T(8,128)(2,1)S(1)}, bf16[256,768]{1,0:T(8,128)(2,1)S(1)}, u32[]{:S(2)}, u32[]{:S(2)}) collective-permute-start(bf16[256,768]{1,0:T(8,128)(2,1)S(1)} %shard_map.110.depart_ref), channel_id=1, source_target_pairs={{0,1},{1,0},{2,3},{3,2},{4,5},{5,4},{6,7},{7,6},{8,9},{9,8},{10,11... | collective-permute-start | bytes 1179656 | tf_op jit(solution)/shard_map/ppermute | solution.py:540
  51.2 1.4 %collective-permute-start.19 = (bf16[128,411]{1,0:T(8,128)(2,1)S(1)}, bf16[128,411]{1,0:T(8,128)(2,1)S(1)}, u32[]{:S(2)}, u32[]{:S(2)}) collective-permute-start(bf16[128,411]{1,0:T(8,128)(2,1)S(1)} %get-tuple-element.37), channel_id=1, source_target_pairs={{0,1},{1,0},{2,3},{3,2},{4,5},{5,4},{6,7},{7,6},{8,9},{9,8},{10,11... | collective-permute-start | bytes 315656 | tf_op jit(solution)/shard_map/ppermute | solution.py:540
  52.9 5.0 %collective-permute-start.20 = (bf16[40,411]{1,0:T(8,128)(2,1)S(1)}, bf16[40,411]{1,0:T(8,128)(2,1)S(1)}, u32[]{:S(2)}, u32[]{:S(2)}) collective-permute-start(bf16[40,411]{1,0:T(8,128)(2,1)S(1)} %get-tuple-element.39), channel_id=1, source_target_pairs={{0,8},{8,0},{16,24},{24,16},{1,9},{9,1},{17,25},{25,17},{2,10},{10... | collective-permute-start | bytes 98648 | tf_op jit(solution)/shard_map/ppermute | solution.py:543
  55.4 5.4 %collective-permute-start.21 = (bf16[40,411]{1,0:T(8,128)(2,1)S(1)}, bf16[40,411]{1,0:T(8,128)(2,1)S(1)}, u32[]{:S(2)}, u32[]{:S(2)}) collective-permute-start(bf16[40,411]{1,0:T(8,128)(2,1)S(1)} %get-tuple-element.40), channel_id=1, source_target_pairs={{0,16},{8,24},{16,0},{24,8},{1,17},{9,25},{17,1},{25,9},{2,18},{10... | collective-permute-start | bytes 98648 | tf_op jit(solution)/shard_map/ppermute | solution.py:543
  57.0 5.8 %collective-permute-start.22 = (bf16[40,411]{1,0:T(8,128)(2,1)S(1)}, bf16[40,411]{1,0:T(8,128)(2,1)S(1)}, u32[]{:S(2)}, u32[]{:S(2)}) collective-permute-start(bf16[40,411]{1,0:T(8,128)(2,1)S(1)} %get-tuple-element.41), channel_id=1, source_target_pairs={{0,24},{8,16},{16,8},{24,0},{1,25},{9,17},{17,9},{25,1},{2,26},{10... | collective-permute-start | bytes 98648 | tf_op jit(solution)/shard_map/ppermute | solution.py:543
  63.0 4.1 %collective-permute-start.23 = (bf16[40,411]{1,0:T(8,128)(2,1)S(1)}, bf16[40,411]{1,0:T(8,128)(2,1)S(1)}, u32[]{:S(2)}, u32[]{:S(2)}) collective-permute-start(bf16[40,411]{1,0:T(8,128)(2,1)S(1)} %get-tuple-element.43), channel_id=1, source_target_pairs={{0,2},{1,3},{2,0},{3,1},{4,6},{5,7},{6,4},{7,5},{8,10},{9,11},{10,... | collective-permute-start | bytes 98648 | tf_op jit(solution)/shard_map/ppermute | solution.py:540
  63.5 4.0 %collective-permute-start.24 = (bf16[40,411]{1,0:T(8,128)(2,1)S(1)}, bf16[40,411]{1,0:T(8,128)(2,1)S(1)}, u32[]{:S(2)}, u32[]{:S(2)}) collective-permute-start(bf16[40,411]{1,0:T(8,128)(2,1)S(1)} %get-tuple-element.44), channel_id=1, source_target_pairs={{0,4},{1,5},{2,6},{3,7},{4,0},{5,1},{6,2},{7,3},{8,12},{9,13},{10,... | collective-permute-start | bytes 98648 | tf_op jit(solution)/shard_map/ppermute | solution.py:540
  64.4 4.9 %collective-permute-start.25 = (bf16[40,411]{1,0:T(8,128)(2,1)S(1)}, bf16[40,411]{1,0:T(8,128)(2,1)S(1)}, u32[]{:S(2)}, u32[]{:S(2)}) collective-permute-start(bf16[40,411]{1,0:T(8,128)(2,1)S(1)} %get-tuple-element.45), channel_id=1, source_target_pairs={{0,6},{1,7},{2,4},{3,5},{4,2},{5,3},{6,0},{7,1},{8,14},{9,15},{10,... | collective-permute-start | bytes 98648 | tf_op jit(solution)/shard_map/ppermute | solution.py:540
  69.3 1.3 %collective-permute-start.26 = (f32[40,411]{1,0:T(8,128)S(1)}, f32[40,411]{1,0:T(8,128)S(1)}, u32[]{:S(2)}, u32[]{:S(2)}) collective-permute-start(f32[40,411]{1,0:T(8,128)S(1)} %shard_map.115.refs_0_), channel_id=1, source_target_pairs={{0,1},{1,0},{2,3},{3,2},{4,5},{5,4},{6,7},{7,6},{8,9},{9,8},{10,11... | collective-permute-start | bytes 197288 | tf_op jit(solution)/shard_map/ppermute | solution.py:540

commit v12 on v11

--- a/solution.py
+++ b/solution.py
@@ -8,7 +8,6 @@
 from jax.sharding import PartitionSpec as P
 
 VMEM_BYTES = 24 * 1024 * 1024
-WHOLE_VMEM_BYTES = 63 * 1024 * 1024
 SLACK_FLOPS = 2 * 10**9
 FORWARD_FLOPS = 10**8
 NT_DIMS = (((1,), (1,)), ((), ()))
@@ -200,7 +199,7 @@
         self.block = up_to(self.own_cols + 2 + self.across, 16)
         self.per_row = self.own_cols + 2
         self.rows_each = chans // self.group
-        self.around = (self.group + 2) * self.per_row
+        self.room = up_to(self.per_row, 16)
         self.deep = up_to(self.features, 16)
         self.strips = self.chips * tiles * self.block
 
@@ -215,18 +214,8 @@
         return k % self.chips * self.group + k // self.chips
 
 
-def prepare_kernel(p, *refs):
-    ins, out_ref = refs[:4], refs[4]
-    fields_ref, diffusivity_ref, usable_ref, bias_ref, flat, packed, sems = refs[5:]
-    copies = [
-        pltpu.make_async_copy(source, target, sems.at[k])
-        for k, (source, target) in enumerate(zip(ins, refs[5:9]))
-    ]
-    for copy in copies:
-        copy.start()
+def prepare_kernel(p, fields_ref, diffusivity_ref, usable_ref, bias_ref, after_ref, out_ref, flat):
     flat[...] = jnp.zeros(flat.shape, jnp.float32)
-    for copy in copies:
-        copy.wait()
     shape = (p.own_cols, p.along)
     row = lax.broadcasted_iota(jnp.int32, shape, 0)
     member = row == lax.broadcasted_iota(jnp.int32, shape, 1) // 4
@@ -246,14 +235,37 @@
     flat[at + 1 : at + 2, p.flag_at : p.flag_at + p.slots] = flags
     for k, part in enumerate(split_three(diffusivity_ref[...])):
         flat[at + 2 : at + 2 + p.across, k * p.lane : k * p.lane + p.along] = part
-    packed[...] = flat[...].astype(jnp.bfloat16)
-    copy = pltpu.make_async_copy(packed, out_ref, sems.at[4])
-    copy.start()
-    copy.wait()
-
-
-def place_kernel(p, owners_ref, place_ref, source_ref, cell_ref, *target_refs):
+    out_ref[...] = flat[...].astype(jnp.bfloat16)
+
+
+def strip_of(p, tile, chan):
+    other = chan ^ lax.axis_index("chan")
+    return p.order(other) * p.tiles + (tile ^ lax.axis_index("tile"))
+
+
+def index_kernel(p, cell_ref, *target_refs):
     t, c = lax.axis_index("tile"), lax.axis_index("chan")
+    row = lax.broadcasted_iota(jnp.int32, cell_ref.shape, 0)
+    reach = p.across + 4
+    tile = (t + row // reach - 1 + p.tiles) % p.tiles
+    cell = c * p.across - 2 + row % reach
+    inside = (cell >= 0) & (cell < p.chans * p.across)
+    cell = jnp.where(inside, cell, 0)
+    wanted = strip_of(p, tile, cell // p.across) * p.block + p.own_cols + 2 + cell % p.across
+    cell_ref[...] = jnp.where(inside, wanted, -1)
+
+    each = p.tiles * p.own_cols
+    target = lax.broadcasted_iota(jnp.int32, target_refs[0].shape, 0)
+    chip, inner = target // each, target % each
+    for k, target_ref in enumerate(target_refs):
+        row = (chip ^ (c // p.group)) * p.group + (c % p.group ^ k)
+        target_ref[...] = (
+            inner // p.own_cols * p.tile_cols + row * p.own_cols + inner % p.own_cols
+        )
+
+
+def place_kernel(p, owners_ref, place_ref, source_ref):
+    t = lax.axis_index("tile")
     across = owners_ref[...]
     shape = (p.rows, p.rows)
     row = lax.broadcasted_iota(jnp.int32, shape, 0)
@@ -265,29 +277,9 @@
     rank = jnp.sum(jnp.where(same, 1, 0), axis=1, keepdims=True)
     tile = first // p.tile_cols
     place_ref[...] = (owner ^ t) * p.slots + tile * p.capacity + rank
-
-    def strip(tile, chan):
-        other = chan ^ c
-        return p.order(other) * p.tiles + (tile ^ t)
-
     source_ref[...] = (
-        strip(tile, first % p.tile_cols // p.own_cols) * p.block + first % p.own_cols
-    )
-
-    row = lax.broadcasted_iota(jnp.int32, cell_ref.shape, 0)
-    reach = p.across + 4
-    tile = (t + row // reach - 1 + p.tiles) % p.tiles
-    cell = c * p.across - 2 + row % reach
-    inside = (cell >= 0) & (cell < p.chans * p.across)
-    cell = jnp.where(inside, cell, 0)
-    wanted = strip(tile, cell // p.across) * p.block + p.own_cols + 2 + cell % p.across
-    cell_ref[...] = jnp.where(inside, wanted, -1)
-
-    each = p.rows_each * p.own_cols
-    target = lax.broadcasted_iota(jnp.int32, target_refs[0].shape, 0)
-    for k, target_ref in enumerate(target_refs):
-        first = (c % p.group ^ k) * each
-        target_ref[...] = target // each * p.tile_cols + first + target % each
+        strip_of(p, tile, first % p.tile_cols // p.own_cols) * p.block + first % p.own_cols
+    )
 
 
 def join_kernel(count, *refs):
@@ -436,55 +428,43 @@
     return total
 
 
-def rows_and_cells(p, count):
-    target = lax.broadcasted_iota(jnp.int32, (count, 1), 0)
-    return target // p.per_row, target % p.per_row - 1
-
-
 def add_group_kernel(p, *refs):
     ins, outs = refs[: p.group], refs[p.group :]
     total = add(ins).astype(jnp.bfloat16)
-    row, along = rows_and_cells(p, outs[0].shape[0])
+    each = p.tiles * p.own_cols
+    for k, out_ref in enumerate(outs):
+        out_ref[...] = total[k * each : (k + 1) * each]
+
+
+def add_chips_kernel(p, *refs):
+    ins, outs = refs[: p.chips], refs[p.chips :]
+    total = add(ins).astype(jnp.bfloat16)
+    along = lax.broadcasted_iota(jnp.int32, (p.room, 1), 0) - 1
+    count = p.tiles * p.own_cols
     for k, out_ref in enumerate(outs):
         tile = lax.axis_index("tile") ^ k
-        cell = (tile * p.own_cols + along + p.tiles * p.own_cols) % (p.tiles * p.own_cols)
-        wanted = (cell // p.own_cols * p.rows_each + row) * p.own_cols + cell % p.own_cols
-        out_ref[...] = dot(one_hot(wanted, 0, total.shape[0]), total).astype(jnp.bfloat16)
-
-
-def add_tiles_kernel(p, *refs):
-    ins, outs = refs[: p.tiles], refs[p.tiles :]
-    total = add(ins).astype(jnp.bfloat16)
-    row, along = rows_and_cells(p, p.around)
-    c = lax.axis_index("chan")
-    for k, out_ref in enumerate(outs):
-        held = ((c // p.group) ^ k) * p.group - 1 + row - c % p.group * p.rows_each
-        wanted = jnp.where(
-            (held >= 0) & (held < p.rows_each), held * p.per_row + along + 1, -1
-        )
-        out_ref[...] = dot(one_hot(wanted, 0, total.shape[0]), total).astype(jnp.bfloat16)
-
-
-def add_chips_kernel(*refs):
+        wanted = (tile * p.own_cols + along + count) % count
+        out_ref[...] = dot(one_hot(wanted, 0, count), total).astype(jnp.bfloat16)
+
+
+def add_tiles_kernel(*refs):
     refs[-1][...] = add(refs[:-1])
 
 
 def diffuse_kernel(p, edge, *refs):
-    ins, root_ref, out_ref = refs[: p.group], refs[-2], refs[-1]
-    total = add(ins) * 0.0625
+    ins, root_ref, out_ref = refs[:3], refs[-2], refs[-1]
     length = p.along + 2 * edge
-    shape = (length, p.around)
+    shape = (length, p.room)
     cell = lax.broadcasted_iota(jnp.int32, shape, 0)
     source = lax.broadcasted_iota(jnp.int32, shape, 1)
     column = (cell - edge + 4) // 4
     spread = []
     for k in range(3):
-        row = lax.axis_index("chan") % p.group + k
-        pick = (source == column + row * p.per_row) & (column >= 0) & (column < p.per_row)
+        pick = (source == column) & (column >= 0) & (column < p.per_row)
         spread.append(
             jnp.dot(
                 pick.astype(jnp.float32),
-                total,
+                ins[k][...] * 0.0625,
                 precision=lax.Precision.HIGHEST,
                 preferred_element_type=jnp.float32,
             )
@@ -567,22 +547,20 @@
     def grow(value, over, after=()):
         return join([value, over(value)], (2 * value.shape[0],) + value.shape[1:], after)
 
+    reach = p.across + 4
+    cell, *targets = call(
+        functools.partial(index_kernel, p),
+        [shape((3 * reach, 1), jnp.int32)] + [shape((p.rows // p.group, 1), jnp.int32)] * p.group,
+        [],
+        flops=SLACK_FLOPS,
+    )
+
     strips = call(
         functools.partial(prepare_kernel, p),
         shape((p.block, p.width), half),
-        [fields, diffusivity, usable, b_hidden],
-        in_hbm=range(4),
-        out_hbm=True,
-        scratch=[
-            pltpu.VMEM(fields.shape, single),
-            pltpu.VMEM(diffusivity.shape, single),
-            pltpu.VMEM(usable.shape, jnp.int32),
-            pltpu.VMEM(b_hidden.shape, single),
-            pltpu.VMEM((p.block, p.width), single),
-            pltpu.VMEM((p.block, p.width), half),
-            pltpu.SemaphoreType.DMA((5,)),
-        ],
-        vmem=WHOLE_VMEM_BYTES,
+        [fields, diffusivity, usable, b_hidden, cell],
+        in_hbm=[4],
+        scratch=[pltpu.VMEM((p.block, p.width), single)],
     )
     seen, stages = observed, []
     bit = 1
@@ -612,12 +590,9 @@
         send(seen, {(b // p.group ^ far_half, b): (b // p.group, b) for b in range(p.chans)}),
     ]
 
-    reach = p.across + 4
-    place, source, cell, *targets = call(
+    place, source = call(
         functools.partial(place_kernel, p),
-        [shape((p.rows, 1), jnp.int32)] * 2
-        + [shape((3 * reach, 1), jnp.int32)]
-        + [shape((p.rows // p.group, 1), jnp.int32)] * p.group,
+        [shape((p.rows, 1), jnp.int32)] * 2,
         [owners.reshape(1, p.rows)],
         flops=SLACK_FLOPS,
     )
@@ -692,18 +667,20 @@
     partial = [partial[0]] + [flip(partial[k], k) for k in range(1, p.group)]
     partial = call(
         functools.partial(add_group_kernel, p),
-        [shape((p.rows_each * p.per_row, p.features), half)] * p.tiles,
+        [shape((p.tiles * p.own_cols, p.features), half)] * p.chips,
         partial,
     )
+    partial = [partial[0]] + [flip(partial[k], k * p.group) for k in range(1, p.chips)]
+    partial = call(
+        functools.partial(add_chips_kernel, p),
+        [shape((p.room, p.features), half)] * p.tiles,
+        partial,
+    )
     partial = [partial[0]] + [trade(partial[k], k) for k in range(1, p.tiles)]
-    partial = call(
-        functools.partial(add_tiles_kernel, p),
-        [shape((p.around, p.features), half)] * p.chips,
-        partial,
-    )
-    partial = [partial[0]] + [flip(partial[k], k * p.group) for k in range(1, p.chips)]
-    partial = call(add_chips_kernel, shape((p.around, p.features), single), partial)
-    partial = [partial] + [flip(partial, k) for k in range(1, p.group)]
+    partial = call(add_tiles_kernel, shape((p.room, p.features), single), partial)
+    before = lax.ppermute(partial, "chan", [(b, (b + 1) % p.chans) for b in range(p.chans)])
+    after = lax.ppermute(partial, "chan", [((b + 1) % p.chans, b) for b in range(p.chans)])
+    partial = [before, partial, after]
 
     edge = 8
     kappa = kappa.reshape(3, reach, p.lane)

time: 72.2 us -> 73.2 us (1.014)
  waiting for transfers between devices: 28.4 us -> 32.8 us
  local copies, waits for them, and re-layouts: 3.13 us -> 0.58 us
  Pallas kernels: 12.4 us -> 10.5 us
  starting transfers between devices: 27.8 us -> 28.8 us
    ppermute x0 -> x2, waiting for transfers between devices: none -> 3.99 us  [the longest x1 3.06 us: body_by_column(): lax.ppermute(partial, 'chan', [(b, (b + 1) % p.chans) for b in range(p.ch...]
    unnamed x14 -> x20, local copies, waits for them, and re-layouts: 2.97 us -> 0.42 us
    pallas_call x17 -> x18, Pallas kernels: 12.4 us -> 10.5 us  [call(): pl.pallas_call(kernel, out_shape=out_shape, in_specs=[far if k in in_hbm...]
    ppermute x14 -> x13, starting transfers between devices: 11 us -> 12.8 us  [flip(): return lax.ppermute(value, 'chan', [(b, b ^ mask) for b in range(p.chans)])]
    ppermute x6, starting transfers between devices: 10.8 us -> 9.29 us  [trade(): return lax.ppermute(value, 'tile', [(a, a ^ mask) for a in range(p.tiles)])]
    ppermute x14 -> x13, waiting for transfers between devices: 10.3 us -> 11.3 us  [flip(): return lax.ppermute(value, 'chan', [(b, b ^ mask) for b in range(p.chans)])]
  transfers between devices with their start and end apart: 27 -> 28, of which waited for: 17 -> 18; matrix products, arithmetic and copies ran while one was open for 0% -> 0% of each run, Pallas kernels for 9% -> 7%
where the time goes in v12:
time: 73.2 us; the launch traced here: 73.1 us
  waiting for transfers between devices  32.8 us (45%)
  starting transfers between devices  28.8 us (39%)
  Pallas kernels  10.5 us (14%)
    ppermute x13, starting transfers between devices, flip(): return lax.ppermute(value, 'chan', [(b, b ^ mask) for b in range(p.chans)])  12.8 us
    ppermute x13, waiting for transfers between devices, flip(): return lax.ppermute(value, 'chan', [(b, b ^ mask) for b in range(p.chans)])  11.3 us
    pallas_call x18, Pallas kernels, call(): pl.pallas_call(kernel, out_shape=out_shape, in_specs=[far if k in in_hbm...  10.5 us
    ppermute x6, starting transfers between devices, trade(): return lax.ppermute(value, 'tile', [(a, a ^ mask) for a in range(p.tiles)])  9.29 us
    ppermute x6, waiting for transfers between devices, trade(): return lax.ppermute(value, 'tile', [(a, a ^ mask) for a in range(p.tiles)])  8.9 us
    ppermute x7, waiting for transfers between devices, send(): lax.ppermute(value, both, sorted(((number(a), number(b)) for a, b in pair...  8.57 us
    ppermute x7, starting transfers between devices, send(): lax.ppermute(value, both, sorted(((number(a), number(b)) for a, b in pair...  6.16 us
    ppermute x1, waiting for transfers between devices, body_by_column(): lax.ppermute(partial, 'chan', [(b, (b + 1) % p.chans) for b in range(p.ch...  3.06 us
  transfers between devices with their start and end apart: 28, of which 18 were waited for; matrix products, arithmetic and copies ran while one was open for 0% of the time, Pallas kernels for 7%

profile of v12, /device:TPU:0, one launch (start us, length us, event | category | flops | bytes accessed | tf_op | source)
XLA Modules:
  0.0 73.1 jit_solution(9445346940757327928)
XLA Ops:
  0.0 3.0 %collective-permute-start.8 = (bf16[411,256]{1,0:T(8,128)(2,1)}, bf16[411,256]{1,0:T(8,128)(2,1)S(1)}, u32[]{:S(2)}, u32[]{:S(2)}) collective-permute-start(bf16[411,256]{1,0:T(8,128)(2,1)} %refs_0_.4), channel_id=1, source_target_pairs={{0,4},{1,5},{2,6},{3,7},{4,0},{5,1},{6,2},{7,3},{8,12},{9,13},{10,... | collective-permute-start | bytes 631304 | tf_op jit(solution)/shard_map/ppermute | solution.py:520
  3.1 1.5 %collective-permute-start.7 = (bf16[411,256]{1,0:T(8,128)(2,1)}, bf16[411,256]{1,0:T(8,128)(2,1)S(1)}, u32[]{:S(2)}, u32[]{:S(2)}) collective-permute-start(bf16[411,256]{1,0:T(8,128)(2,1)} %refs_0_.4), channel_id=1, source_target_pairs={{0,2},{1,3},{2,0},{3,1},{4,6},{5,7},{6,4},{7,5},{8,10},{9,11},{10,... | collective-permute-start | bytes 631304 | tf_op jit(solution)/shard_map/ppermute | solution.py:520
  4.6 0.0 collective-permute-start.9
  4.6 2.0 %collective-permute-start.1 = (bf16[128,768]{1,0:T(8,128)(2,1)}, bf16[128,768]{1,0:T(8,128)(2,1)S(1)}, u32[]{:S(2)}, u32[]{:S(2)}) collective-permute-start(bf16[128,768]{1,0:T(8,128)(2,1)} %refs_0_.3), channel_id=1, source_target_pairs={{0,8},{8,0},{16,24},{24,16},{1,9},{9,1},{17,25},{25,17},{2,10},{10... | collective-permute-start | bytes 589832 | tf_op jit(solution)/shard_map/ppermute | solution.py:523
  6.6 0.1 shard_map.101
  6.7 0.0 copy-start.9
  6.7 0.2 shard_map.102.refs_0_
  6.9 0.0 collective-permute-start
  7.0 4.1 %collective-permute-done.1.refs_1_ = bf16[128,768]{1,0:T(8,128)(2,1)S(1)} collective-permute-done((bf16[128,768]{1,0:T(8,128)(2,1)}, bf16[128,768]{1,0:T(8,128)(2,1)S(1)}, u32[]{:S(2)}, u32[]{:S(2)}) %collective-permute-start.1) | collective-permute-done | bytes 196640 | tf_op jit(solution)/shard_map/ppermute | solution.py:523
  11.1 0.5 shard_map.103.refs_2_.refs_0_
  11.6 0.1 shard_map.104.refs_0_
  11.7 2.8 %collective-permute-start.2 = (bf16[32,512]{1,0:T(8,128)(2,1)S(1)}, bf16[32,512]{1,0:T(8,128)(2,1)S(1)}, u32[]{:S(2)}, u32[]{:S(2)}) collective-permute-start(bf16[32,512]{1,0:T(8,128)(2,1)S(1)} %shard_map.104.refs_0_), channel_id=1, source_target_pairs={{0,16},{8,24},{16,0},{24,8},{1,17},{9,25},{17,1},{25,9},{2,18},{10... | collective-permute-start | bytes 98312 | tf_op jit(solution)/shard_map/ppermute | solution.py:523
  14.5 2.1 %collective-permute-done.2.refs_1_ = bf16[32,512]{1,0:T(8,128)(2,1)S(1)} collective-permute-done((bf16[32,512]{1,0:T(8,128)(2,1)S(1)}, bf16[32,512]{1,0:T(8,128)(2,1)S(1)}, u32[]{:S(2)}, u32[]{:S(2)}) %collective-permute-start.2) | collective-permute-done | bytes 32800 | tf_op jit(solution)/shard_map/ppermute | solution.py:523
  16.6 0.1 shard_map.105.refs_0_.refs_4_
  16.7 0.1 shard_map.107.refs_7_.refs_5_
  16.8 0.1 collective-permute-start.10
  16.8 2.8 %collective-permute-start.11 = (bf16[256,768]{1,0:T(8,128)(2,1)S(1)}, bf16[256,768]{1,0:T(8,128)(2,1)S(1)}, u32[]{:S(2)}, u32[]{:S(2)}) collective-permute-start(bf16[256,768]{1,0:T(8,128)(2,1)S(1)} %shard_map.103.refs_2_.refs_0_), channel_id=1, source_target_pairs={{0,16},{1,17},{2,3},{3,2},{4,20},{5,21},{6,7},{7,6},{8,9},{9,8},{1... | collective-permute-start | bytes 1179656 | tf_op jit(solution)/shard_map/ppermute | solution.py:532
  19.7 0.3 collective-permute-start.5
  19.9 1.3 %collective-permute-start.4 = (bf16[64,512]{1,0:T(8,128)(2,1)S(1)}, bf16[64,512]{1,0:T(8,128)(2,1)S(1)}, u32[]{:S(2)}, u32[]{:S(2)}) collective-permute-start(bf16[64,512]{1,0:T(8,128)(2,1)S(1)} %shard_map.105.refs_0_.refs_4_), channel_id=1, source_target_pairs={{0,4},{1,5},{2,6},{3,7},{4,0},{5,1},{6,2},{7,3},{8,12},{9,13},{10,... | collective-permute-start | bytes 196616 | tf_op jit(solution)/shard_map/ppermute | solution.py:520
  21.2 2.0 %collective-permute-start.3 = (bf16[64,512]{1,0:T(8,128)(2,1)S(1)}, bf16[64,512]{1,0:T(8,128)(2,1)S(1)}, u32[]{:S(2)}, u32[]{:S(2)}) collective-permute-start(bf16[64,512]{1,0:T(8,128)(2,1)S(1)} %shard_map.105.refs_0_.refs_4_), channel_id=1, source_target_pairs={{0,2},{1,3},{2,0},{3,1},{4,6},{5,7},{6,4},{7,5},{8,10},{9,11},{10,... | collective-permute-start | bytes 196616 | tf_op jit(solution)/shard_map/ppermute | solution.py:520
  23.1 2.0 %collective-permute-done.5.refs_3_ = bf16[64,512]{1,0:T(8,128)(2,1)S(1)} collective-permute-done((bf16[64,512]{1,0:T(8,128)(2,1)S(1)}, bf16[64,512]{1,0:T(8,128)(2,1)S(1)}, u32[]{:S(2)}, u32[]{:S(2)}) %collective-permute-start.5) | collective-permute-done | bytes 65568 | tf_op jit(solution)/shard_map/ppermute | solution.py:520
  25.2 0.3 collective-permute-done.4.refs_2_
  25.4 0.8 %collective-permute-done.3.refs_1_ = bf16[64,512]{1,0:T(8,128)(2,1)S(1)} collective-permute-done((bf16[64,512]{1,0:T(8,128)(2,1)S(1)}, bf16[64,512]{1,0:T(8,128)(2,1)S(1)}, u32[]{:S(2)}, u32[]{:S(2)}) %collective-permute-start.3) | collective-permute-done | bytes 65568 | tf_op jit(solution)/shard_map/ppermute | solution.py:520
  26.2 0.3 shard_map.106.refs_5_
  26.5 0.1 collective-permute-start.6
  26.6 0.0 copy-start
  26.6 0.0 copy-start.5
  26.7 0.4 shard_map.100
  27.0 1.1 %collective-permute-done.6.refs_6_ = bf16[256,512]{1,0:T(8,128)(2,1)S(1)} collective-permute-done((bf16[256,512]{1,0:T(8,128)(2,1)S(1)}, bf16[256,512]{1,0:T(8,128)(2,1)S(1)}, u32[]{:S(2)}, u32[]{:S(2)}) %collective-permute-start.6) | collective-permute-done | bytes 262176 | tf_op jit(solution)/shard_map/ppermute | solution.py:520
  28.1 0.4 copy-done
  28.5 2.3 %shard_map.108 = (f32[256,768]{1,0:T(8,128)S(1)}, f32[256,1]{1,0:T(8,128)S(1)}, f32[8,256,256]{2,1,0:T(8,128)S(1)}, f32[24,128]{1,0:T(8,128)S(1)}) custom-call(s32[256,1]{1,0:T(8,128)S(1)} %get-tuple-element.26.refs_0_.place_ref, s32[256,1]{1,0:T(8,128)S(1)} %get-tuple-element.27.refs_1_, s32[24,1]{1,0:T(8,128)S(1)} %get-tuple-element.28.after_ref.refs_2_, ...), custom_call_target="tpu_custom_call" | custom-call | flops 100000000 | bytes 5379168 | tf_op jit(solution)/shard_map/pallas_call | solution.py:164
  30.9 0.4 shard_map.110
  31.3 1.3 %collective-permute-start.12 = (bf16[128,768]{1,0:T(8,128)(2,1)S(1)}, bf16[128,768]{1,0:T(8,128)(2,1)S(1)}, u32[]{:S(2)}, u32[]{:S(2)}) collective-permute-start(bf16[128,768]{1,0:T(8,128)(2,1)S(1)} %get-tuple-element.32.refs_0_), channel_id=1, source_target_pairs={{0,2},{1,3},{2,0},{3,1},{4,5},{5,4},{6,7},{7,6},{8,10},{9,11},{10,... | collective-permute-start | bytes 589832 | tf_op jit(solution)/shard_map/ppermute | solution.py:532
  32.6 0.0 collective-permute-start.13
  32.6 2.0 %collective-permute-start.14 = (bf16[128,768]{1,0:T(8,128)(2,1)S(1)}, bf16[128,768]{1,0:T(8,128)(2,1)S(1)}, u32[]{:S(2)}, u32[]{:S(2)}) collective-permute-start(bf16[128,768]{1,0:T(8,128)(2,1)S(1)} %get-tuple-element.32.refs_0_), channel_id=1, source_target_pairs={{0,4},{1,5},{2,3},{3,2},{4,0},{5,1},{6,7},{7,6},{8,9},{9,8},{10,14... | collective-permute-start | bytes 589832 | tf_op jit(solution)/shard_map/ppermute | solution.py:532
  34.6 4.4 %collective-permute-done.12.refs_2_ = bf16[128,768]{1,0:T(8,128)(2,1)S(1)} collective-permute-done((bf16[128,768]{1,0:T(8,128)(2,1)S(1)}, bf16[128,768]{1,0:T(8,128)(2,1)S(1)}, u32[]{:S(2)}, u32[]{:S(2)}) %collective-permute-start.12) | collective-permute-done | bytes 196640 | tf_op jit(solution)/shard_map/ppermute | solution.py:532
  39.1 1.3 %collective-permute-done.13.refs_3_ = bf16[128,768]{1,0:T(8,128)(2,1)S(1)} collective-permute-done((bf16[128,768]{1,0:T(8,128)(2,1)S(1)}, bf16[128,768]{1,0:T(8,128)(2,1)S(1)}, u32[]{:S(2)}, u32[]{:S(2)}) %collective-permute-start.13) | collective-permute-done | bytes 196640 | tf_op jit(solution)/shard_map/ppermute | solution.py:532
  40.3 0.6 shard_map.109.refs_8_.refs_2_
  41.0 2.8 %collective-permute-done.14.refs_4_ = bf16[128,768]{1,0:T(8,128)(2,1)S(1)} collective-permute-done((bf16[128,768]{1,0:T(8,128)(2,1)S(1)}, bf16[128,768]{1,0:T(8,128)(2,1)S(1)}, u32[]{:S(2)}, u32[]{:S(2)}) %collective-permute-start.14) | collective-permute-done | bytes 196640 | tf_op jit(solution)/shard_map/ppermute | solution.py:532
  43.8 0.6 shard_map.111.depart_ref
  44.4 0.1 collective-permute-start.18
  44.5 0.5 shard_map.112.refs_3_
  45.0 1.2 %collective-permute-done.18.refs_4_ = bf16[256,768]{1,0:T(8,128)(2,1)S(1)} collective-permute-done((bf16[256,768]{1,0:T(8,128)(2,1)S(1)}, bf16[256,768]{1,0:T(8,128)(2,1)S(1)}, u32[]{:S(2)}, u32[]{:S(2)}) %collective-permute-start.18) | collective-permute-done | bytes 393248 | tf_op jit(solution)/shard_map/ppermute | solution.py:520
  46.2 2.9 %shard_map.113 = (bf16[128,411]{1,0:T(8,128)(2,1)S(1)}, bf16[128,411]{1,0:T(8,128)(2,1)S(1)}) custom-call(bf16[2048,768]{1,0:T(8,128)(2,1)S(1)} %copy-done, bf16[1536,768]{1,0:T(8,128)(2,1)S(1)} %copy-done.1, f32[8,256,256]{2,1,0:T(8,128)S(1)} %shard_map.109.refs_8_.refs_2_, f32[256,768]{1,0:T(8,128)S(1)} %shard_map.112.refs_3_, ...), custom_call_target="tpu_custom_call" | custom-call | flops 1840250880 | bytes 10486784 | tf_op jit(solution)/shard_map/pallas_call | solution.py:164
  49.1 0.2 collective-permute-start.19
  49.3 1.2 %collective-permute-done.19.refs_1_ = bf16[128,411]{1,0:T(8,128)(2,1)S(1)} collective-permute-done((bf16[128,411]{1,0:T(8,128)(2,1)S(1)}, bf16[128,411]{1,0:T(8,128)(2,1)S(1)}, u32[]{:S(2)}, u32[]{:S(2)}) %collective-permute-start.19) | collective-permute-done | bytes 105248 | tf_op jit(solution)/shard_map/ppermute | solution.py:520
  50.6 2.6 %collective-permute-start.20 = (bf16[32,411]{1,0:T(8,128)(2,1)S(1)}, bf16[32,411]{1,0:T(8,128)(2,1)S(1)}, u32[]{:S(2)}, u32[]{:S(2)}) collective-permute-start(bf16[32,411]{1,0:T(8,128)(2,1)S(1)} %get-tuple-element.39), channel_id=1, source_target_pairs={{0,2},{1,3},{2,0},{3,1},{4,6},{5,7},{6,4},{7,5},{8,10},{9,11},{10,... | collective-permute-start | bytes 78920 | tf_op jit(solution)/shard_map/ppermute | solution.py:520
  53.1 1.7 %collective-permute-start.21 = (bf16[32,411]{1,0:T(8,128)(2,1)S(1)}, bf16[32,411]{1,0:T(8,128)(2,1)S(1)}, u32[]{:S(2)}, u32[]{:S(2)}) collective-permute-start(bf16[32,411]{1,0:T(8,128)(2,1)S(1)} %get-tuple-element.40), channel_id=1, source_target_pairs={{0,4},{1,5},{2,6},{3,7},{4,0},{5,1},{6,2},{7,3},{8,12},{9,13},{10,... | collective-permute-start | bytes 78920 | tf_op jit(solution)/shard_map/ppermute | solution.py:520
  54.9 0.1 slice_bitcast_fusion.2
  54.9 0.1 collective-permute-done.20.refs_1_
  55.0 2.0 %collective-permute-done.21.refs_2_ = bf16[32,411]{1,0:T(8,128)(2,1)S(1)} collective-permute-done((bf16[32,411]{1,0:T(8,128)(2,1)S(1)}, bf16[32,411]{1,0:T(8,128)(2,1)S(1)}, u32[]{:S(2)}, u32[]{:S(2)}) %collective-permute-start.21) | collective-permute-done | bytes 26336 | tf_op jit(solution)/shard_map/ppermute | solution.py:520
  57.1 2.6 %collective-permute-done.22.refs_3_ = bf16[32,411]{1,0:T(8,128)(2,1)S(1)} collective-permute-done((bf16[32,411]{1,0:T(8,128)(2,1)S(1)}, bf16[32,411]{1,0:T(8,128)(2,1)S(1)}, u32[]{:S(2)}, u32[]{:S(2)}) %collective-permute-start.22) | collective-permute-done | bytes 26336 | tf_op jit(solution)/shard_map/ppermute | solution.py:520
  59.7 0.2 shard_map.115
  59.8 1.6 %collective-permute-start.23 = (bf16[16,411]{1,0:T(8,128)(2,1)S(1)}, bf16[16,411]{1,0:T(8,128)(2,1)S(1)}, u32[]{:S(2)}, u32[]{:S(2)}) collective-permute-start(bf16[16,411]{1,0:T(8,128)(2,1)S(1)} %get-tuple-element.43), channel_id=1, source_target_pairs={{0,8},{8,0},{16,24},{24,16},{1,9},{9,1},{17,25},{25,17},{2,10},{10... | collective-permute-start | bytes 39464 | tf_op jit(solution)/shard_map/ppermute | solution.py:523
  61.5 2.8 %collective-permute-start.25 = (bf16[16,411]{1,0:T(8,128)(2,1)S(1)}, bf16[16,411]{1,0:T(8,128)(2,1)S(1)}, u32[]{:S(2)}, u32[]{:S(2)}) collective-permute-start(bf16[16,411]{1,0:T(8,128)(2,1)S(1)} %get-tuple-element.45), channel_id=1, source_target_pairs={{0,24},{8,16},{16,8},{24,0},{1,25},{9,17},{17,9},{25,1},{2,26},{10... | collective-permute-start | bytes 39464 | tf_op jit(solution)/shard_map/ppermute | solution.py:523
  64.3 1.9 %collective-permute-done.24.refs_2_ = bf16[16,411]{1,0:T(8,128)(2,1)S(1)} collective-permute-done((bf16[16,411]{1,0:T(8,128)(2,1)S(1)}, bf16[16,411]{1,0:T(8,128)(2,1)S(1)}, u32[]{:S(2)}, u32[]{:S(2)}) %collective-permute-start.24) | collective-permute-done | bytes 13184 | tf_op jit(solution)/shard_map/ppermute | solution.py:523
  66.2 0.8 %collective-permute-done.25.refs_3_ = bf16[16,411]{1,0:T(8,128)(2,1)S(1)} collective-permute-done((bf16[16,411]{1,0:T(8,128)(2,1)S(1)}, bf16[16,411]{1,0:T(8,128)(2,1)S(1)}, u32[]{:S(2)}, u32[]{:S(2)}) %collective-permute-start.25) | collective-permute-done | bytes 13184 | tf_op jit(solution)/shard_map/ppermute | solution.py:523
  67.0 0.1 collective-permute-start.27
  67.1 0.5 collective-permute-start.26
  67.6 0.1 maximum_sqrt_fusion
  67.7 0.1 copy.19
  67.7 0.9 %collective-permute-done.27.refs_2_ = f32[16,411]{1,0:T(8,128)S(1)} collective-permute-done((f32[16,411]{1,0:T(8,128)S(1)}, f32[16,411]{1,0:T(8,128)S(1)}, u32[]{:S(2)}, u32[]{:S(2)}) %collective-permute-start.27) | collective-permute-done | bytes 26336 | tf_op jit(solution)/shard_map/ppermute | solution.py:682
  68.7 3.1 %collective-permute-done.26.refs_0_ = f32[16,411]{1,0:T(8,128)S(1)} collective-permute-done((f32[16,411]{1,0:T(8,128)S(1)}, f32[16,411]{1,0:T(8,128)S(1)}, u32[]{:S(2)}, u32[]{:S(2)}) %collective-permute-start.26) | collective-permute-done | bytes 26336 | tf_op jit(solution)/shard_map/ppermute | solution.py:681
  71.7 1.3 %shard_map.117 = f32[4,32,411]{2,1,0:T(8,128)} custom-call(f32[16,411]{1,0:T(8,128)S(1)} %collective-permute-done.26.refs_0_, f32[16,411]{1,0:T(8,128)S(1)} %shard_map.116.refs_1_, f32[16,411]{1,0:T(8,128)S(1)} %collective-permute-done.27.refs_2_, f32[48,8]{1,0:T(8,128)S(1)} %bitcast.9), custom_call_target="tpu_custom_call" | custom-call | flops 5260800 | bytes 80448 | tf_op jit(solution)/shard_map/pallas_call | solution.py:164
  (34 shorter events, 0.1 us)
Async XLA Ops:
  0.0 16.7 %copy-start.3 = (bf16[411,256]{1,0:T(8,128)(2,1)S(1)}, bf16[411,256]{1,0:T(8,128)(2,1)}, u32[]{:S(2)}) copy-start(bf16[411,256]{1,0:T(8,128)(2,1)} %refs_0_.4) | copy-start | bytes 631300
  0.0 11.1 %copy-start.4 = (bf16[128,768]{1,0:T(8,128)(2,1)S(1)}, bf16[128,768]{1,0:T(8,128)(2,1)}, u32[]{:S(2)}) copy-start(bf16[128,768]{1,0:T(8,128)(2,1)} %refs_0_.3) | copy-start | bytes 589828
  0.0 6.7 %copy-start.7 = (f32[256]{0:T(256)S(1)}, f32[256]{0:T(256)}, u32[]{:S(2)}) copy-start(f32[256]{0:T(256)} %bias_ref.1) | copy-start | bytes 3076
  0.0 6.7 %copy-start.8 = (s32[128]{0:T(128)S(1)}, s32[128]{0:T(128)}, u32[]{:S(2)}) copy-start(s32[128]{0:T(128)} %usable_ref.1) | copy-start | bytes 1540
  0.0 6.7 %copy-start.6 = (f32[4,32]{1,0:T(4,128)S(1)}, f32[4,32]{1,0:T(4,128)}, u32[]{:S(2)}) copy-start(f32[4,32]{1,0:T(4,128)} %diffusivity_ref.1) | copy-start | bytes 1540
  0.0 6.7 %copy-start.2 = (f32[4,32,411]{2,1,0:T(8,128)S(1)}, f32[4,32,411]{2,1,0:T(8,128)}, u32[]{:S(2)}) copy-start(f32[4,32,411]{2,1,0:T(8,128)} %fields_ref.1) | copy-start | bytes 631300
  0.0 16.6 %collective-permute-start.8 = (bf16[411,256]{1,0:T(8,128)(2,1)}, bf16[411,256]{1,0:T(8,128)(2,1)S(1)}, u32[]{:S(2)}, u32[]{:S(2)}) collective-permute-start(bf16[411,256]{1,0:T(8,128)(2,1)} %refs_0_.4), channel_id=1, source_target_pairs={{0,4},{1,5},{2,6},{3,7},{4,0},{5,1},{6,2},{7,3},{8,12},{9,13},{10,... | collective-permute-start | bytes 631304 | tf_op jit(solution)/shard_map/ppermute | solution.py:520
  3.1 13.6 %collective-permute-start.7 = (bf16[411,256]{1,0:T(8,128)(2,1)}, bf16[411,256]{1,0:T(8,128)(2,1)S(1)}, u32[]{:S(2)}, u32[]{:S(2)}) collective-permute-start(bf16[411,256]{1,0:T(8,128)(2,1)} %refs_0_.4), channel_id=1, source_target_pairs={{0,2},{1,3},{2,0},{3,1},{4,6},{5,7},{6,4},{7,5},{8,10},{9,11},{10,... | collective-permute-start | bytes 631304 | tf_op jit(solution)/shard_map/ppermute | solution.py:520
  4.6 12.1 %collective-permute-start.9 = (bf16[411,256]{1,0:T(8,128)(2,1)}, bf16[411,256]{1,0:T(8,128)(2,1)S(1)}, u32[]{:S(2)}, u32[]{:S(2)}) collective-permute-start(bf16[411,256]{1,0:T(8,128)(2,1)} %refs_0_.4), channel_id=1, source_target_pairs={{0,6},{1,7},{2,4},{3,5},{4,2},{5,3},{6,0},{7,1},{8,14},{9,15},{10,... | collective-permute-start | bytes 631304 | tf_op jit(solution)/shard_map/ppermute | solution.py:520
  4.6 6.5 %collective-permute-start.1 = (bf16[128,768]{1,0:T(8,128)(2,1)}, bf16[128,768]{1,0:T(8,128)(2,1)S(1)}, u32[]{:S(2)}, u32[]{:S(2)}) collective-permute-start(bf16[128,768]{1,0:T(8,128)(2,1)} %refs_0_.3), channel_id=1, source_target_pairs={{0,8},{8,0},{16,24},{24,16},{1,9},{9,1},{17,25},{25,17},{2,10},{10... | collective-permute-start | bytes 589832 | tf_op jit(solution)/shard_map/ppermute | solution.py:523
  6.7 19.9 %copy-start.9 = (s32[256,1]{0,1:T(1,128)S(1)}, s32[256,1]{0,1:T(1,128)}, u32[]{:S(2)}) copy-start(s32[256,1]{0,1:T(1,128)} %param.12) | copy-start | bytes 3076
  6.9 4.7 %collective-permute-start = (bf16[16,512]{1,0:T(8,128)(2,1)S(1)}, bf16[16,512]{1,0:T(8,128)(2,1)S(1)}, u32[]{:S(2)}, u32[]{:S(2)}) collective-permute-start(bf16[16,512]{1,0:T(8,128)(2,1)S(1)} %shard_map.102.refs_0_), channel_id=1, source_target_pairs={{0,8},{8,0},{16,24},{24,16},{1,9},{9,1},{17,25},{25,17},{2,10},{10... | collective-permute-start | bytes 49160 | tf_op jit(solution)/shard_map/ppermute | solution.py:523
  11.7 4.9 %collective-permute-start.2 = (bf16[32,512]{1,0:T(8,128)(2,1)S(1)}, bf16[32,512]{1,0:T(8,128)(2,1)S(1)}, u32[]{:S(2)}, u32[]{:S(2)}) collective-permute-start(bf16[32,512]{1,0:T(8,128)(2,1)S(1)} %shard_map.104.refs_0_), channel_id=1, source_target_pairs={{0,16},{8,24},{16,0},{24,8},{1,17},{9,25},{17,1},{25,9},{2,18},{10... | collective-permute-start | bytes 98312 | tf_op jit(solution)/shard_map/ppermute | solution.py:523
  16.8 11.4 %collective-permute-start.10 = (bf16[1664,256]{1,0:T(8,128)(2,1)S(1)}, bf16[1664,256]{1,0:T(8,128)(2,1)S(1)}, u32[]{:S(2)}, u32[]{:S(2)}) collective-permute-start(bf16[1664,256]{1,0:T(8,128)(2,1)S(1)} %shard_map.107.refs_7_.refs_5_), channel_id=1, source_target_pairs={{0,1},{1,0},{2,3},{3,2},{4,5},{5,4},{6,7},{7,6},{8,9},{9,8},{10,11... | collective-permute-start | bytes 2555912 | tf_op jit(solution)/shard_map/ppermute | solution.py:520
  16.8 14.0 %collective-permute-start.11 = (bf16[256,768]{1,0:T(8,128)(2,1)S(1)}, bf16[256,768]{1,0:T(8,128)(2,1)S(1)}, u32[]{:S(2)}, u32[]{:S(2)}) collective-permute-start(bf16[256,768]{1,0:T(8,128)(2,1)S(1)} %shard_map.103.refs_2_.refs_0_), channel_id=1, source_target_pairs={{0,16},{1,17},{2,3},{3,2},{4,20},{5,21},{6,7},{7,6},{8,9},{9,8},{1... | collective-permute-start | bytes 1179656 | tf_op jit(solution)/shard_map/ppermute | solution.py:532
  19.7 5.5 %collective-permute-start.5 = (bf16[64,512]{1,0:T(8,128)(2,1)S(1)}, bf16[64,512]{1,0:T(8,128)(2,1)S(1)}, u32[]{:S(2)}, u32[]{:S(2)}) collective-permute-start(bf16[64,512]{1,0:T(8,128)(2,1)S(1)} %shard_map.105.refs_0_.refs_4_), channel_id=1, source_target_pairs={{0,6},{1,7},{2,4},{3,5},{4,2},{5,3},{6,0},{7,1},{8,14},{9,15},{10,... | collective-permute-start | bytes 196616 | tf_op jit(solution)/shard_map/ppermute | solution.py:520
  19.9 5.5 %collective-permute-start.4 = (bf16[64,512]{1,0:T(8,128)(2,1)S(1)}, bf16[64,512]{1,0:T(8,128)(2,1)S(1)}, u32[]{:S(2)}, u32[]{:S(2)}) collective-permute-start(bf16[64,512]{1,0:T(8,128)(2,1)S(1)} %shard_map.105.refs_0_.refs_4_), channel_id=1, source_target_pairs={{0,4},{1,5},{2,6},{3,7},{4,0},{5,1},{6,2},{7,3},{8,12},{9,13},{10,... | collective-permute-start | bytes 196616 | tf_op jit(solution)/shard_map/ppermute | solution.py:520
  21.2 5.0 %collective-permute-start.3 = (bf16[64,512]{1,0:T(8,128)(2,1)S(1)}, bf16[64,512]{1,0:T(8,128)(2,1)S(1)}, u32[]{:S(2)}, u32[]{:S(2)}) collective-permute-start(bf16[64,512]{1,0:T(8,128)(2,1)S(1)} %shard_map.105.refs_0_.refs_4_), channel_id=1, source_target_pairs={{0,2},{1,3},{2,0},{3,1},{4,6},{5,7},{6,4},{7,5},{8,10},{9,11},{10,... | collective-permute-start | bytes 196616 | tf_op jit(solution)/shard_map/ppermute | solution.py:520
  26.5 1.6 %collective-permute-start.6 = (bf16[256,512]{1,0:T(8,128)(2,1)S(1)}, bf16[256,512]{1,0:T(8,128)(2,1)S(1)}, u32[]{:S(2)}, u32[]{:S(2)}) collective-permute-start(bf16[256,512]{1,0:T(8,128)(2,1)S(1)} %shard_map.106.refs_5_), channel_id=1, source_target_pairs={{0,1},{1,0},{2,3},{3,2},{4,5},{5,4},{6,7},{7,6},{8,9},{9,8},{10,11... | collective-permute-start | bytes 786440 | tf_op jit(solution)/shard_map/ppermute | solution.py:520
  26.6 1.9 %copy-start = (bf16[2048,768]{1,0:T(8,128)(2,1)S(1)}, bf16[2048,768]{1,0:T(8,128)(2,1)}, u32[]{:S(2)}) copy-start(bf16[2048,768]{1,0:T(8,128)(2,1)} %refs_0_.5) | copy-start | bytes 9437188
  26.6 1.9 %copy-start.5 = (f32[768]{0:T(1024)S(1)}, f32[768]{0:T(1024)}, u32[]{:S(2)}) copy-start(f32[768]{0:T(1024)} %refs_3_.1) | copy-start | bytes 9220
  31.3 7.8 %collective-permute-start.12 = (bf16[128,768]{1,0:T(8,128)(2,1)S(1)}, bf16[128,768]{1,0:T(8,128)(2,1)S(1)}, u32[]{:S(2)}, u32[]{:S(2)}) collective-permute-start(bf16[128,768]{1,0:T(8,128)(2,1)S(1)} %get-tuple-element.32.refs_0_), channel_id=1, source_target_pairs={{0,2},{1,3},{2,0},{3,1},{4,5},{5,4},{6,7},{7,6},{8,10},{9,11},{10,... | collective-permute-start | bytes 589832 | tf_op jit(solution)/shard_map/ppermute | solution.py:532
  32.6 7.7 %collective-permute-start.13 = (bf16[128,768]{1,0:T(8,128)(2,1)S(1)}, bf16[128,768]{1,0:T(8,128)(2,1)S(1)}, u32[]{:S(2)}, u32[]{:S(2)}) collective-permute-start(bf16[128,768]{1,0:T(8,128)(2,1)S(1)} %get-tuple-element.33.refs_1_), channel_id=1, source_target_pairs={{0,4},{1,5},{2,3},{3,2},{4,0},{5,1},{6,7},{7,6},{8,9},{9,8},{10,14... | collective-permute-start | bytes 589832 | tf_op jit(solution)/shard_map/ppermute | solution.py:532
  32.6 11.2 %collective-permute-start.14 = (bf16[128,768]{1,0:T(8,128)(2,1)S(1)}, bf16[128,768]{1,0:T(8,128)(2,1)S(1)}, u32[]{:S(2)}, u32[]{:S(2)}) collective-permute-start(bf16[128,768]{1,0:T(8,128)(2,1)S(1)} %get-tuple-element.32.refs_0_), channel_id=1, source_target_pairs={{0,4},{1,5},{2,3},{3,2},{4,0},{5,1},{6,7},{7,6},{8,9},{9,8},{10,14... | collective-permute-start | bytes 589832 | tf_op jit(solution)/shard_map/ppermute | solution.py:532
  34.6 9.2 %collective-permute-start.15 = (bf16[128,768]{1,0:T(8,128)(2,1)S(1)}, bf16[128,768]{1,0:T(8,128)(2,1)S(1)}, u32[]{:S(2)}, u32[]{:S(2)}) collective-permute-start(bf16[128,768]{1,0:T(8,128)(2,1)S(1)} %get-tuple-element.33.refs_1_), channel_id=1, source_target_pairs={{0,2},{1,3},{2,0},{3,1},{4,5},{5,4},{6,7},{7,6},{8,10},{9,11},{10,... | collective-permute-start | bytes 589832 | tf_op jit(solution)/shard_map/ppermute | solution.py:532
  39.1 4.8 %collective-permute-start.16 = (bf16[128,768]{1,0:T(8,128)(2,1)S(1)}, bf16[128,768]{1,0:T(8,128)(2,1)S(1)}, u32[]{:S(2)}, u32[]{:S(2)}) collective-permute-start(bf16[128,768]{1,0:T(8,128)(2,1)S(1)} %collective-permute-done.12.refs_2_), channel_id=1, source_target_pairs={{0,1},{1,0},{2,6},{3,7},{4,5},{5,4},{6,2},{7,3},{8,12},{9,13},{10,... | collective-permute-start | bytes 589832 | tf_op jit(solution)/shard_map/ppermute | solution.py:532
  40.3 3.5 %collective-permute-start.17 = (bf16[128,768]{1,0:T(8,128)(2,1)S(1)}, bf16[128,768]{1,0:T(8,128)(2,1)S(1)}, u32[]{:S(2)}, u32[]{:S(2)}) collective-permute-start(bf16[128,768]{1,0:T(8,128)(2,1)S(1)} %collective-permute-done.13.refs_3_), channel_id=1, source_target_pairs={{0,1},{1,0},{2,3},{3,2},{4,6},{5,7},{6,4},{7,5},{8,9},{9,8},{10,11... | collective-permute-start | bytes 589832 | tf_op jit(solution)/shard_map/ppermute | solution.py:532
  41.0 3.5 %copy-start.1 = (bf16[1536,768]{1,0:T(8,128)(2,1)S(1)}, bf16[1536,768]{1,0:T(8,128)(2,1)}, u32[]{:S(2)}) copy-start(bf16[1536,768]{1,0:T(8,128)(2,1)} %refs_1_.1) | copy-start | bytes 7077892
  44.4 1.8 %collective-permute-start.18 = (bf16[256,768]{1,0:T(8,128)(2,1)S(1)}, bf16[256,768]{1,0:T(8,128)(2,1)S(1)}, u32[]{:S(2)}, u32[]{:S(2)}) collective-permute-start(bf16[256,768]{1,0:T(8,128)(2,1)S(1)} %shard_map.111.depart_ref), channel_id=1, source_target_pairs={{0,1},{1,0},{2,3},{3,2},{4,5},{5,4},{6,7},{7,6},{8,9},{9,8},{10,11... | collective-permute-start | bytes 1179656 | tf_op jit(solution)/shard_map/ppermute | solution.py:520
  49.1 1.4 %collective-permute-start.19 = (bf16[128,411]{1,0:T(8,128)(2,1)S(1)}, bf16[128,411]{1,0:T(8,128)(2,1)S(1)}, u32[]{:S(2)}, u32[]{:S(2)}) collective-permute-start(bf16[128,411]{1,0:T(8,128)(2,1)S(1)} %get-tuple-element.37), channel_id=1, source_target_pairs={{0,1},{1,0},{2,3},{3,2},{4,5},{5,4},{6,7},{7,6},{8,9},{9,8},{10,11... | collective-permute-start | bytes 315656 | tf_op jit(solution)/shard_map/ppermute | solution.py:520
  50.6 4.5 %collective-permute-start.20 = (bf16[32,411]{1,0:T(8,128)(2,1)S(1)}, bf16[32,411]{1,0:T(8,128)(2,1)S(1)}, u32[]{:S(2)}, u32[]{:S(2)}) collective-permute-start(bf16[32,411]{1,0:T(8,128)(2,1)S(1)} %get-tuple-element.39), channel_id=1, source_target_pairs={{0,2},{1,3},{2,0},{3,1},{4,6},{5,7},{6,4},{7,5},{8,10},{9,11},{10,... | collective-permute-start | bytes 78920 | tf_op jit(solution)/shard_map/ppermute | solution.py:520
  53.1 3.9 %collective-permute-start.21 = (bf16[32,411]{1,0:T(8,128)(2,1)S(1)}, bf16[32,411]{1,0:T(8,128)(2,1)S(1)}, u32[]{:S(2)}, u32[]{:S(2)}) collective-permute-start(bf16[32,411]{1,0:T(8,128)(2,1)S(1)} %get-tuple-element.40), channel_id=1, source_target_pairs={{0,4},{1,5},{2,6},{3,7},{4,0},{5,1},{6,2},{7,3},{8,12},{9,13},{10,... | collective-permute-start | bytes 78920 | tf_op jit(solution)/shard_map/ppermute | solution.py:520
  54.9 4.8 %collective-permute-start.22 = (bf16[32,411]{1,0:T(8,128)(2,1)S(1)}, bf16[32,411]{1,0:T(8,128)(2,1)S(1)}, u32[]{:S(2)}, u32[]{:S(2)}) collective-permute-start(bf16[32,411]{1,0:T(8,128)(2,1)S(1)} %get-tuple-element.41), channel_id=1, source_target_pairs={{0,6},{1,7},{2,4},{3,5},{4,2},{5,3},{6,0},{7,1},{8,14},{9,15},{10,... | collective-permute-start | bytes 78920 | tf_op jit(solution)/shard_map/ppermute | solution.py:520
  59.8 4.5 %collective-permute-start.23 = (bf16[16,411]{1,0:T(8,128)(2,1)S(1)}, bf16[16,411]{1,0:T(8,128)(2,1)S(1)}, u32[]{:S(2)}, u32[]{:S(2)}) collective-permute-start(bf16[16,411]{1,0:T(8,128)(2,1)S(1)} %get-tuple-element.43), channel_id=1, source_target_pairs={{0,8},{8,0},{16,24},{24,16},{1,9},{9,1},{17,25},{25,17},{2,10},{10... | collective-permute-start | bytes 39464 | tf_op jit(solution)/shard_map/ppermute | solution.py:523
  61.5 4.7 %collective-permute-start.24 = (bf16[16,411]{1,0:T(8,128)(2,1)S(1)}, bf16[16,411]{1,0:T(8,128)(2,1)S(1)}, u32[]{:S(2)}, u32[]{:S(2)}) collective-permute-start(bf16[16,411]{1,0:T(8,128)(2,1)S(1)} %get-tuple-element.44), channel_id=1, source_target_pairs={{0,16},{8,24},{16,0},{24,8},{1,17},{9,25},{17,1},{25,9},{2,18},{10... | collective-permute-start | bytes 39464 | tf_op jit(solution)/shard_map/ppermute | solution.py:523
  61.5 5.5 %collective-permute-start.25 = (bf16[16,411]{1,0:T(8,128)(2,1)S(1)}, bf16[16,411]{1,0:T(8,128)(2,1)S(1)}, u32[]{:S(2)}, u32[]{:S(2)}) collective-permute-start(bf16[16,411]{1,0:T(8,128)(2,1)S(1)} %get-tuple-element.45), channel_id=1, source_target_pairs={{0,24},{8,16},{16,8},{24,0},{1,25},{9,17},{17,9},{25,1},{2,26},{10... | collective-permute-start | bytes 39464 | tf_op jit(solution)/shard_map/ppermute | solution.py:523
  67.0 1.7 %collective-permute-start.27 = (f32[16,411]{1,0:T(8,128)S(1)}, f32[16,411]{1,0:T(8,128)S(1)}, u32[]{:S(2)}, u32[]{:S(2)}) collective-permute-start(f32[16,411]{1,0:T(8,128)S(1)} %shard_map.116.refs_1_), channel_id=1, source_target_pairs={{1,0},{2,1},{3,2},{4,3},{5,4},{6,5},{7,6},{0,7},{9,8},{10,9},{11,1... | collective-permute-start | bytes 78920 | tf_op jit(solution)/shard_map/ppermute | solution.py:682
  67.1 4.7 %collective-permute-start.26 = (f32[16,411]{1,0:T(8,128)S(1)}, f32[16,411]{1,0:T(8,128)S(1)}, u32[]{:S(2)}, u32[]{:S(2)}) collective-permute-start(f32[16,411]{1,0:T(8,128)S(1)} %shard_map.116.refs_1_), channel_id=1, source_target_pairs={{0,1},{1,2},{2,3},{3,4},{4,5},{5,6},{6,7},{7,0},{8,9},{9,10},{10,1... | collective-permute-start | bytes 78920 | tf_op jit(solution)/shard_map/ppermute | solution.py:681

commit v13 on v12

--- a/solution.py
+++ b/solution.py
@@ -198,8 +198,8 @@
         )
         self.block = up_to(self.own_cols + 2 + self.across, 16)
         self.per_row = self.own_cols + 2
-        self.rows_each = chans // self.group
-        self.room = up_to(self.per_row, 16)
+        self.patch = 3 * tiles * self.own_cols
+        self.room = up_to(3 * self.per_row, 16)
         self.deep = up_to(self.features, 16)
         self.strips = self.chips * tiles * self.block
 
@@ -254,14 +254,14 @@
     wanted = strip_of(p, tile, cell // p.across) * p.block + p.own_cols + 2 + cell % p.across
     cell_ref[...] = jnp.where(inside, wanted, -1)
 
-    each = p.tiles * p.own_cols
     target = lax.broadcasted_iota(jnp.int32, target_refs[0].shape, 0)
-    chip, inner = target // each, target % each
+    chip, inner = target // p.patch, target % p.patch
+    beside, inner = inner // (p.patch // 3) - 1, inner % (p.patch // 3)
+    tile, along = inner // p.own_cols, inner % p.own_cols
     for k, target_ref in enumerate(target_refs):
-        row = (chip ^ (c // p.group)) * p.group + (c % p.group ^ k)
-        target_ref[...] = (
-            inner // p.own_cols * p.tile_cols + row * p.own_cols + inner % p.own_cols
-        )
+        row = (chip ^ (c // p.group)) * p.group + (c % p.group ^ k) + beside
+        wanted = tile * p.tile_cols + row * p.own_cols + along
+        target_ref[...] = jnp.where((row >= 0) & (row < p.chans), wanted, -1)
 
 
 def place_kernel(p, owners_ref, place_ref, source_ref):
@@ -421,38 +421,34 @@
         out_ref[...] = dot_nt(one_hot(target_ref[...], 0, p.rows), total).astype(jnp.bfloat16)
 
 
-def add(refs):
-    total = refs[0][...].astype(jnp.float32)
+def add(refs, at=slice(None)):
+    total = refs[0][at, :].astype(jnp.float32)
     for ref in refs[1:]:
-        total = total + ref[...].astype(jnp.float32)
+        total = total + ref[at, :].astype(jnp.float32)
     return total
 
 
 def add_group_kernel(p, *refs):
     ins, outs = refs[: p.group], refs[p.group :]
-    total = add(ins).astype(jnp.bfloat16)
-    each = p.tiles * p.own_cols
     for k, out_ref in enumerate(outs):
-        out_ref[...] = total[k * each : (k + 1) * each]
+        out_ref[...] = add(ins, slice(k * p.patch, (k + 1) * p.patch)).astype(jnp.bfloat16)
 
 
 def add_chips_kernel(p, *refs):
     ins, outs = refs[: p.chips], refs[p.chips :]
     total = add(ins).astype(jnp.bfloat16)
-    along = lax.broadcasted_iota(jnp.int32, (p.room, 1), 0) - 1
+    target = lax.broadcasted_iota(jnp.int32, (p.room, 1), 0)
+    row, along = target // p.per_row, target % p.per_row - 1
     count = p.tiles * p.own_cols
     for k, out_ref in enumerate(outs):
-        tile = lax.axis_index("tile") ^ k
-        wanted = (tile * p.own_cols + along + count) % count
-        out_ref[...] = dot(one_hot(wanted, 0, count), total).astype(jnp.bfloat16)
-
-
-def add_tiles_kernel(*refs):
-    refs[-1][...] = add(refs[:-1])
+        cell = ((lax.axis_index("tile") ^ k) * p.own_cols + along + count) % count
+        wanted = jnp.where(row < 3, row * count + cell, -1)
+        out_ref[...] = dot(one_hot(wanted, 0, p.patch), total).astype(jnp.bfloat16)
 
 
 def diffuse_kernel(p, edge, *refs):
-    ins, root_ref, out_ref = refs[:3], refs[-2], refs[-1]
+    ins, root_ref, out_ref = refs[: p.tiles], refs[-2], refs[-1]
+    total = add(ins) * 0.0625
     length = p.along + 2 * edge
     shape = (length, p.room)
     cell = lax.broadcasted_iota(jnp.int32, shape, 0)
@@ -460,11 +456,11 @@
     column = (cell - edge + 4) // 4
     spread = []
     for k in range(3):
-        pick = (source == column) & (column >= 0) & (column < p.per_row)
+        pick = (source == column + k * p.per_row) & (column >= 0) & (column < p.per_row)
         spread.append(
             jnp.dot(
                 pick.astype(jnp.float32),
-                ins[k][...] * 0.0625,
+                total,
                 precision=lax.Precision.HIGHEST,
                 preferred_element_type=jnp.float32,
             )
@@ -550,7 +546,7 @@
     reach = p.across + 4
     cell, *targets = call(
         functools.partial(index_kernel, p),
-        [shape((3 * reach, 1), jnp.int32)] + [shape((p.rows // p.group, 1), jnp.int32)] * p.group,
+        [shape((3 * reach, 1), jnp.int32)] + [shape((p.chips * p.patch, 1), jnp.int32)] * p.group,
         [],
         flops=SLACK_FLOPS,
     )
@@ -562,12 +558,13 @@
         in_hbm=[4],
         scratch=[pltpu.VMEM((p.block, p.width), single)],
     )
-    seen, stages = observed, []
+    seen, stages, before = observed, [], ()
     bit = 1
     while bit < p.tiles:
+        strips = grow(strips, lambda value: trade(value, bit), before)
         if 2 * bit < p.tiles:
-            seen = grow(seen, lambda value: trade(value, bit))
-        strips = grow(strips, lambda value: trade(value, bit), [seen] if bit == 1 else ())
+            seen = grow(seen, lambda value: trade(value, bit), [strips])
+            before = [seen]
         stages.append(strips)
         bit *= 2
     strips = join(
@@ -660,14 +657,14 @@
     )
     partial = call(
         functools.partial(backward_kernel, p),
-        [shape((p.rows // p.group, p.features), half)] * p.group,
+        [shape((p.chips * p.patch, p.features), half)] * p.group,
         [w_radiance, inv_cov, slope, partial] + depart + weights + targets,
         flops=2 * p.rows * (p.hidden * p.chans * (p.features + p.shard) + inv_cov.size),
     )
     partial = [partial[0]] + [flip(partial[k], k) for k in range(1, p.group)]
     partial = call(
         functools.partial(add_group_kernel, p),
-        [shape((p.tiles * p.own_cols, p.features), half)] * p.chips,
+        [shape((p.patch, p.features), half)] * p.chips,
         partial,
     )
     partial = [partial[0]] + [flip(partial[k], k * p.group) for k in range(1, p.chips)]
@@ -677,11 +674,6 @@
         partial,
     )
     partial = [partial[0]] + [trade(partial[k], k) for k in range(1, p.tiles)]
-    partial = call(add_tiles_kernel, shape((p.room, p.features), single), partial)
-    before = lax.ppermute(partial, "chan", [(b, (b + 1) % p.chans) for b in range(p.chans)])
-    after = lax.ppermute(partial, "chan", [((b + 1) % p.chans, b) for b in range(p.chans)])
-    partial = [before, partial, after]
-
     edge = 8
     kappa = kappa.reshape(3, reach, p.lane)
     root = jnp.sqrt(

time: 73.2 us -> 70.6 us (0.964)
  waiting for transfers between devices: 32.8 us -> 29.9 us
    ppermute x2 -> x0, waiting for transfers between devices: 3.99 us -> none  [the longest x1 3.06 us: body_by_column(): lax.ppermute(partial, 'chan', [(b, (b + 1) % p.chans) for b in range(p.ch...]
    ppermute x13, waiting for transfers between devices: 11.3 us -> 12.4 us  [flip(): return lax.ppermute(value, 'chan', [(b, b ^ mask) for b in range(p.chans)])]
    pallas_call x18 -> x17, Pallas kernels: 10.5 us -> 11.2 us  [call(): pl.pallas_call(kernel, out_shape=out_shape, in_specs=[far if k in in_hbm...]
  transfers between devices with their start and end apart: 28 -> 26, of which waited for: 18 -> 16; matrix products, arithmetic and copies ran while one was open for 0% -> 0% of each run, Pallas kernels for 7% -> 8%
where the time goes in v13:
time: 70.6 us; the launch traced here: 70.5 us
  waiting for transfers between devices  29.9 us (42%)
  starting transfers between devices  28.4 us (40%)
  Pallas kernels  11.2 us (16%)
    ppermute x13, starting transfers between devices, flip(): return lax.ppermute(value, 'chan', [(b, b ^ mask) for b in range(p.chans)])  12.8 us
    ppermute x13, waiting for transfers between devices, flip(): return lax.ppermute(value, 'chan', [(b, b ^ mask) for b in range(p.chans)])  12.4 us
    pallas_call x17, Pallas kernels, call(): pl.pallas_call(kernel, out_shape=out_shape, in_specs=[far if k in in_hbm...  11.2 us
    ppermute x6, starting transfers between devices, trade(): return lax.ppermute(value, 'tile', [(a, a ^ mask) for a in range(p.tiles)])  9.48 us
    ppermute x6, waiting for transfers between devices, trade(): return lax.ppermute(value, 'tile', [(a, a ^ mask) for a in range(p.tiles)])  8.98 us
    ppermute x7, waiting for transfers between devices, send(): lax.ppermute(value, both, sorted(((number(a), number(b)) for a, b in pair...  8.56 us
    ppermute x7, starting transfers between devices, send(): lax.ppermute(value, both, sorted(((number(a), number(b)) for a, b in pair...  6.16 us
  transfers between devices with their start and end apart: 26, of which 16 were waited for; matrix products, arithmetic and copies ran while one was open for 0% of the time, Pallas kernels for 8%

profile of v13, /device:TPU:0, one launch (start us, length us, event | category | flops | bytes accessed | tf_op | source)
XLA Modules:
  0.0 70.5 jit_solution(1020567922899689794)
XLA Ops:
  0.0 3.0 %collective-permute-start.8 = (bf16[411,256]{1,0:T(8,128)(2,1)}, bf16[411,256]{1,0:T(8,128)(2,1)S(1)}, u32[]{:S(2)}, u32[]{:S(2)}) collective-permute-start(bf16[411,256]{1,0:T(8,128)(2,1)} %refs_0_.4), channel_id=1, source_target_pairs={{0,4},{1,5},{2,6},{3,7},{4,0},{5,1},{6,2},{7,3},{8,12},{9,13},{10,... | collective-permute-start | bytes 631304 | tf_op jit(solution)/shard_map/ppermute | solution.py:516
  3.1 1.5 %collective-permute-start.7 = (bf16[411,256]{1,0:T(8,128)(2,1)}, bf16[411,256]{1,0:T(8,128)(2,1)S(1)}, u32[]{:S(2)}, u32[]{:S(2)}) collective-permute-start(bf16[411,256]{1,0:T(8,128)(2,1)} %refs_0_.4), channel_id=1, source_target_pairs={{0,2},{1,3},{2,0},{3,1},{4,6},{5,7},{6,4},{7,5},{8,10},{9,11},{10,... | collective-permute-start | bytes 631304 | tf_op jit(solution)/shard_map/ppermute | solution.py:516
  4.6 0.0 collective-permute-start.9
  4.6 2.0 %collective-permute-start.2 = (bf16[128,768]{1,0:T(8,128)(2,1)}, bf16[128,768]{1,0:T(8,128)(2,1)S(1)}, u32[]{:S(2)}, u32[]{:S(2)}) collective-permute-start(bf16[128,768]{1,0:T(8,128)(2,1)} %refs_0_.3), channel_id=1, source_target_pairs={{0,8},{8,0},{16,24},{24,16},{1,9},{9,1},{17,25},{25,17},{2,10},{10... | collective-permute-start | bytes 589832 | tf_op jit(solution)/shard_map/ppermute | solution.py:519
  6.6 0.5 shard_map.101
  7.2 0.0 copy-start.9
  7.2 0.2 shard_map.102.refs_0_
  7.4 0.0 collective-permute-start
  7.4 3.8 %collective-permute-done.refs_1_ = bf16[16,512]{1,0:T(8,128)(2,1)S(1)} collective-permute-done((bf16[16,512]{1,0:T(8,128)(2,1)S(1)}, bf16[16,512]{1,0:T(8,128)(2,1)S(1)}, u32[]{:S(2)}, u32[]{:S(2)}) %collective-permute-start) | collective-permute-done | bytes 16416 | tf_op jit(solution)/shard_map/ppermute | solution.py:519
  11.3 2.8 %collective-permute-start.1 = (bf16[32,512]{1,0:T(8,128)(2,1)S(1)}, bf16[32,512]{1,0:T(8,128)(2,1)S(1)}, u32[]{:S(2)}, u32[]{:S(2)}) collective-permute-start(bf16[32,512]{1,0:T(8,128)(2,1)S(1)} %shard_map.103.refs_2_.refs_0_), channel_id=1, source_target_pairs={{0,16},{8,24},{16,0},{24,8},{1,17},{9,25},{17,1},{25,9},{2,18},{10... | collective-permute-start | bytes 98312 | tf_op jit(solution)/shard_map/ppermute | solution.py:519
  14.1 0.0 collective-permute-done.2.refs_1_
  14.1 0.5 shard_map.104.refs_2_.refs_0_
  14.6 1.5 %collective-permute-done.1.refs_1_ = bf16[32,512]{1,0:T(8,128)(2,1)S(1)} collective-permute-done((bf16[32,512]{1,0:T(8,128)(2,1)S(1)}, bf16[32,512]{1,0:T(8,128)(2,1)S(1)}, u32[]{:S(2)}, u32[]{:S(2)}) %collective-permute-start.1) | collective-permute-done | bytes 32800 | tf_op jit(solution)/shard_map/ppermute | solution.py:519
  16.2 0.1 shard_map.105.refs_0_.refs_4_
  16.3 0.0 collective-permute-done.8.refs_2_
  16.3 0.1 shard_map.107.refs_7_.refs_5_
  16.4 0.1 collective-permute-start.10
  16.5 2.8 %collective-permute-start.11 = (bf16[256,768]{1,0:T(8,128)(2,1)S(1)}, bf16[256,768]{1,0:T(8,128)(2,1)S(1)}, u32[]{:S(2)}, u32[]{:S(2)}) collective-permute-start(bf16[256,768]{1,0:T(8,128)(2,1)S(1)} %shard_map.104.refs_2_.refs_0_), channel_id=1, source_target_pairs={{0,16},{1,17},{2,3},{3,2},{4,20},{5,21},{6,7},{7,6},{8,9},{9,8},{1... | collective-permute-start | bytes 1179656 | tf_op jit(solution)/shard_map/ppermute | solution.py:528
  19.3 0.3 collective-permute-start.5
  19.5 1.3 %collective-permute-start.4 = (bf16[64,512]{1,0:T(8,128)(2,1)S(1)}, bf16[64,512]{1,0:T(8,128)(2,1)S(1)}, u32[]{:S(2)}, u32[]{:S(2)}) collective-permute-start(bf16[64,512]{1,0:T(8,128)(2,1)S(1)} %shard_map.105.refs_0_.refs_4_), channel_id=1, source_target_pairs={{0,4},{1,5},{2,6},{3,7},{4,0},{5,1},{6,2},{7,3},{8,12},{9,13},{10,... | collective-permute-start | bytes 196616 | tf_op jit(solution)/shard_map/ppermute | solution.py:516
  20.8 2.0 %collective-permute-start.3 = (bf16[64,512]{1,0:T(8,128)(2,1)S(1)}, bf16[64,512]{1,0:T(8,128)(2,1)S(1)}, u32[]{:S(2)}, u32[]{:S(2)}) collective-permute-start(bf16[64,512]{1,0:T(8,128)(2,1)S(1)} %shard_map.105.refs_0_.refs_4_), channel_id=1, source_target_pairs={{0,2},{1,3},{2,0},{3,1},{4,6},{5,7},{6,4},{7,5},{8,10},{9,11},{10,... | collective-permute-start | bytes 196616 | tf_op jit(solution)/shard_map/ppermute | solution.py:516
  22.8 2.0 %collective-permute-done.5.refs_3_ = bf16[64,512]{1,0:T(8,128)(2,1)S(1)} collective-permute-done((bf16[64,512]{1,0:T(8,128)(2,1)S(1)}, bf16[64,512]{1,0:T(8,128)(2,1)S(1)}, u32[]{:S(2)}, u32[]{:S(2)}) %collective-permute-start.5) | collective-permute-done | bytes 65568 | tf_op jit(solution)/shard_map/ppermute | solution.py:516
  24.8 0.3 collective-permute-done.4.refs_2_
  25.0 0.8 %collective-permute-done.3.refs_1_ = bf16[64,512]{1,0:T(8,128)(2,1)S(1)} collective-permute-done((bf16[64,512]{1,0:T(8,128)(2,1)S(1)}, bf16[64,512]{1,0:T(8,128)(2,1)S(1)}, u32[]{:S(2)}, u32[]{:S(2)}) %collective-permute-start.3) | collective-permute-done | bytes 65568 | tf_op jit(solution)/shard_map/ppermute | solution.py:516
  25.8 0.3 shard_map.106.refs_5_
  26.2 0.1 collective-permute-start.6
  26.2 0.0 copy-start
  26.3 0.0 copy-start.5
  26.3 0.4 shard_map.100
  26.7 1.1 %collective-permute-done.6.refs_6_ = bf16[256,512]{1,0:T(8,128)(2,1)S(1)} collective-permute-done((bf16[256,512]{1,0:T(8,128)(2,1)S(1)}, bf16[256,512]{1,0:T(8,128)(2,1)S(1)}, u32[]{:S(2)}, u32[]{:S(2)}) %collective-permute-start.6) | collective-permute-done | bytes 262176 | tf_op jit(solution)/shard_map/ppermute | solution.py:516
  27.8 0.4 copy-done
  28.1 2.3 %shard_map.108 = (f32[256,768]{1,0:T(8,128)S(1)}, f32[256,1]{1,0:T(8,128)S(1)}, f32[8,256,256]{2,1,0:T(8,128)S(1)}, f32[24,128]{1,0:T(8,128)S(1)}) custom-call(s32[256,1]{1,0:T(8,128)S(1)} %get-tuple-element.26.refs_0_.place_ref, s32[256,1]{1,0:T(8,128)S(1)} %get-tuple-element.27.refs_1_, s32[24,1]{1,0:T(8,128)S(1)} %get-tuple-element.28.after_ref.refs_2_, ...), custom_call_target="tpu_custom_call" | custom-call | flops 100000000 | bytes 5379168 | tf_op jit(solution)/shard_map/pallas_call | solution.py:164
  30.5 0.4 shard_map.110
  30.9 1.3 %collective-permute-start.12 = (bf16[128,768]{1,0:T(8,128)(2,1)S(1)}, bf16[128,768]{1,0:T(8,128)(2,1)S(1)}, u32[]{:S(2)}, u32[]{:S(2)}) collective-permute-start(bf16[128,768]{1,0:T(8,128)(2,1)S(1)} %get-tuple-element.32.refs_0_), channel_id=1, source_target_pairs={{0,2},{1,3},{2,0},{3,1},{4,5},{5,4},{6,7},{7,6},{8,10},{9,11},{10,... | collective-permute-start | bytes 589832 | tf_op jit(solution)/shard_map/ppermute | solution.py:528
  32.2 0.0 collective-permute-start.13
  32.3 2.0 %collective-permute-start.14 = (bf16[128,768]{1,0:T(8,128)(2,1)S(1)}, bf16[128,768]{1,0:T(8,128)(2,1)S(1)}, u32[]{:S(2)}, u32[]{:S(2)}) collective-permute-start(bf16[128,768]{1,0:T(8,128)(2,1)S(1)} %get-tuple-element.32.refs_0_), channel_id=1, source_target_pairs={{0,4},{1,5},{2,3},{3,2},{4,0},{5,1},{6,7},{7,6},{8,9},{9,8},{10,14... | collective-permute-start | bytes 589832 | tf_op jit(solution)/shard_map/ppermute | solution.py:528
  34.2 4.4 %collective-permute-done.12.refs_2_ = bf16[128,768]{1,0:T(8,128)(2,1)S(1)} collective-permute-done((bf16[128,768]{1,0:T(8,128)(2,1)S(1)}, bf16[128,768]{1,0:T(8,128)(2,1)S(1)}, u32[]{:S(2)}, u32[]{:S(2)}) %collective-permute-start.12) | collective-permute-done | bytes 196640 | tf_op jit(solution)/shard_map/ppermute | solution.py:528
  38.7 1.3 %collective-permute-done.13.refs_3_ = bf16[128,768]{1,0:T(8,128)(2,1)S(1)} collective-permute-done((bf16[128,768]{1,0:T(8,128)(2,1)S(1)}, bf16[128,768]{1,0:T(8,128)(2,1)S(1)}, u32[]{:S(2)}, u32[]{:S(2)}) %collective-permute-start.13) | collective-permute-done | bytes 196640 | tf_op jit(solution)/shard_map/ppermute | solution.py:528
  40.0 0.6 shard_map.109.refs_8_.refs_2_
  40.6 0.0 copy-start.1
  40.6 2.8 %collective-permute-done.14.refs_4_ = bf16[128,768]{1,0:T(8,128)(2,1)S(1)} collective-permute-done((bf16[128,768]{1,0:T(8,128)(2,1)S(1)}, bf16[128,768]{1,0:T(8,128)(2,1)S(1)}, u32[]{:S(2)}, u32[]{:S(2)}) %collective-permute-start.14) | collective-permute-done | bytes 196640 | tf_op jit(solution)/shard_map/ppermute | solution.py:528
  43.4 0.6 shard_map.111.depart_ref
  44.0 0.1 collective-permute-start.18
  44.1 0.5 shard_map.112.refs_3_
  44.6 1.2 %collective-permute-done.18.refs_4_ = bf16[256,768]{1,0:T(8,128)(2,1)S(1)} collective-permute-done((bf16[256,768]{1,0:T(8,128)(2,1)S(1)}, bf16[256,768]{1,0:T(8,128)(2,1)S(1)}, u32[]{:S(2)}, u32[]{:S(2)}) %collective-permute-start.18) | collective-permute-done | bytes 393248 | tf_op jit(solution)/shard_map/ppermute | solution.py:516
  45.8 3.0 %shard_map.113 = (bf16[384,411]{1,0:T(8,128)(2,1)S(1)}, bf16[384,411]{1,0:T(8,128)(2,1)S(1)}) custom-call(bf16[2048,768]{1,0:T(8,128)(2,1)S(1)} %copy-done, bf16[1536,768]{1,0:T(8,128)(2,1)S(1)} %copy-done.1, f32[8,256,256]{2,1,0:T(8,128)S(1)} %shard_map.109.refs_8_.refs_2_, f32[256,768]{1,0:T(8,128)S(1)} %shard_map.112.refs_3_, ...), custom_call_target="tpu_custom_call" | custom-call | flops 1840250880 | bytes 10488832 | tf_op jit(solution)/shard_map/pallas_call | solution.py:164
  48.8 0.2 collective-permute-start.19
  49.0 0.1 slice_bitcast_fusion.2
  49.0 1.5 %collective-permute-done.19.refs_1_ = bf16[384,411]{1,0:T(8,128)(2,1)S(1)} collective-permute-done((bf16[384,411]{1,0:T(8,128)(2,1)S(1)}, bf16[384,411]{1,0:T(8,128)(2,1)S(1)}, u32[]{:S(2)}, u32[]{:S(2)}) %collective-permute-start.19) | collective-permute-done | bytes 315680 | tf_op jit(solution)/shard_map/ppermute | solution.py:516
  50.6 0.1 shard_map.114
  50.6 2.6 %collective-permute-start.20 = (bf16[96,411]{1,0:T(8,128)(2,1)S(1)}, bf16[96,411]{1,0:T(8,128)(2,1)S(1)}, u32[]{:S(2)}, u32[]{:S(2)}) collective-permute-start(bf16[96,411]{1,0:T(8,128)(2,1)S(1)} %get-tuple-element.39), channel_id=1, source_target_pairs={{0,2},{1,3},{2,0},{3,1},{4,6},{5,7},{6,4},{7,5},{8,10},{9,11},{10,... | collective-permute-start | bytes 236744 | tf_op jit(solution)/shard_map/ppermute | solution.py:516
  53.2 1.7 %collective-permute-start.21 = (bf16[96,411]{1,0:T(8,128)(2,1)S(1)}, bf16[96,411]{1,0:T(8,128)(2,1)S(1)}, u32[]{:S(2)}, u32[]{:S(2)}) collective-permute-start(bf16[96,411]{1,0:T(8,128)(2,1)S(1)} %get-tuple-element.40), channel_id=1, source_target_pairs={{0,4},{1,5},{2,6},{3,7},{4,0},{5,1},{6,2},{7,3},{8,12},{9,13},{10,... | collective-permute-start | bytes 236744 | tf_op jit(solution)/shard_map/ppermute | solution.py:516
  55.0 1.4 %collective-permute-done.20.refs_1_ = bf16[96,411]{1,0:T(8,128)(2,1)S(1)} collective-permute-done((bf16[96,411]{1,0:T(8,128)(2,1)S(1)}, bf16[96,411]{1,0:T(8,128)(2,1)S(1)}, u32[]{:S(2)}, u32[]{:S(2)}) %collective-permute-start.20) | collective-permute-done | bytes 78944 | tf_op jit(solution)/shard_map/ppermute | solution.py:516
  56.3 2.8 %collective-permute-done.21.refs_2_ = bf16[96,411]{1,0:T(8,128)(2,1)S(1)} collective-permute-done((bf16[96,411]{1,0:T(8,128)(2,1)S(1)}, bf16[96,411]{1,0:T(8,128)(2,1)S(1)}, u32[]{:S(2)}, u32[]{:S(2)}) %collective-permute-start.21) | collective-permute-done | bytes 78944 | tf_op jit(solution)/shard_map/ppermute | solution.py:516
  59.1 1.3 %collective-permute-done.22.refs_3_ = bf16[96,411]{1,0:T(8,128)(2,1)S(1)} collective-permute-done((bf16[96,411]{1,0:T(8,128)(2,1)S(1)}, bf16[96,411]{1,0:T(8,128)(2,1)S(1)}, u32[]{:S(2)}, u32[]{:S(2)}) %collective-permute-start.22) | collective-permute-done | bytes 78944 | tf_op jit(solution)/shard_map/ppermute | solution.py:516
  60.5 0.2 shard_map.115
  60.7 2.2 %collective-permute-start.23 = (bf16[32,411]{1,0:T(8,128)(2,1)S(1)}, bf16[32,411]{1,0:T(8,128)(2,1)S(1)}, u32[]{:S(2)}, u32[]{:S(2)}) collective-permute-start(bf16[32,411]{1,0:T(8,128)(2,1)S(1)} %get-tuple-element.43), channel_id=1, source_target_pairs={{0,8},{8,0},{16,24},{24,16},{1,9},{9,1},{17,25},{25,17},{2,10},{10... | collective-permute-start | bytes 78920 | tf_op jit(solution)/shard_map/ppermute | solution.py:519
  62.9 0.5 collective-permute-start.24
  63.4 2.0 %collective-permute-start.25 = (bf16[32,411]{1,0:T(8,128)(2,1)S(1)}, bf16[32,411]{1,0:T(8,128)(2,1)S(1)}, u32[]{:S(2)}, u32[]{:S(2)}) collective-permute-start(bf16[32,411]{1,0:T(8,128)(2,1)S(1)} %get-tuple-element.45), channel_id=1, source_target_pairs={{0,24},{8,16},{16,8},{24,0},{1,25},{9,17},{17,9},{25,1},{2,26},{10... | collective-permute-start | bytes 78920 | tf_op jit(solution)/shard_map/ppermute | solution.py:519
  65.4 0.1 maximum_sqrt_fusion
  65.4 0.1 copy.19
  65.5 2.2 %collective-permute-done.24.refs_2_ = bf16[32,411]{1,0:T(8,128)(2,1)S(1)} collective-permute-done((bf16[32,411]{1,0:T(8,128)(2,1)S(1)}, bf16[32,411]{1,0:T(8,128)(2,1)S(1)}, u32[]{:S(2)}, u32[]{:S(2)}) %collective-permute-start.24) | collective-permute-done | bytes 26336 | tf_op jit(solution)/shard_map/ppermute | solution.py:519
  67.7 1.4 %collective-permute-done.25.refs_3_ = bf16[32,411]{1,0:T(8,128)(2,1)S(1)} collective-permute-done((bf16[32,411]{1,0:T(8,128)(2,1)S(1)}, bf16[32,411]{1,0:T(8,128)(2,1)S(1)}, u32[]{:S(2)}, u32[]{:S(2)}) %collective-permute-start.25) | collective-permute-done | bytes 26336 | tf_op jit(solution)/shard_map/ppermute | solution.py:519
  69.1 1.4 %shard_map.116 = f32[4,32,411]{2,1,0:T(8,128)} custom-call(bf16[32,411]{1,0:T(8,128)(2,1)S(1)} %get-tuple-element.42.refs_0_, bf16[32,411]{1,0:T(8,128)(2,1)S(1)} %collective-permute-done.23.refs_1_, bf16[32,411]{1,0:T(8,128)(2,1)S(1)} %collective-permute-done.24.refs_2_, bf16[32,411]{1,0:T(8,128)(2,1)S(1)} %collective-permute-done.25.refs_3_, ...), custom_call_target="tpu_custom_call" | custom-call | flops 5260800 | bytes 106752 | tf_op jit(solution)/shard_map/pallas_call | solution.py:164
  (29 shorter events, 0.1 us)
Async XLA Ops:
  0.0 16.3 %copy-start.3 = (bf16[411,256]{1,0:T(8,128)(2,1)S(1)}, bf16[411,256]{1,0:T(8,128)(2,1)}, u32[]{:S(2)}) copy-start(bf16[411,256]{1,0:T(8,128)(2,1)} %refs_0_.4) | copy-start | bytes 631300
  0.0 14.1 %copy-start.4 = (bf16[128,768]{1,0:T(8,128)(2,1)S(1)}, bf16[128,768]{1,0:T(8,128)(2,1)}, u32[]{:S(2)}) copy-start(bf16[128,768]{1,0:T(8,128)(2,1)} %refs_0_.3) | copy-start | bytes 589828
  0.0 7.2 %copy-start.7 = (f32[256]{0:T(256)S(1)}, f32[256]{0:T(256)}, u32[]{:S(2)}) copy-start(f32[256]{0:T(256)} %bias_ref.1) | copy-start | bytes 3076
  0.0 7.2 %copy-start.8 = (s32[128]{0:T(128)S(1)}, s32[128]{0:T(128)}, u32[]{:S(2)}) copy-start(s32[128]{0:T(128)} %usable_ref.1) | copy-start | bytes 1540
  0.0 7.2 %copy-start.6 = (f32[4,32]{1,0:T(4,128)S(1)}, f32[4,32]{1,0:T(4,128)}, u32[]{:S(2)}) copy-start(f32[4,32]{1,0:T(4,128)} %diffusivity_ref.1) | copy-start | bytes 1540
  0.0 7.2 %copy-start.2 = (f32[4,32,411]{2,1,0:T(8,128)S(1)}, f32[4,32,411]{2,1,0:T(8,128)}, u32[]{:S(2)}) copy-start(f32[4,32,411]{2,1,0:T(8,128)} %fields_ref.1) | copy-start | bytes 631300
  0.0 16.2 %collective-permute-start.8 = (bf16[411,256]{1,0:T(8,128)(2,1)}, bf16[411,256]{1,0:T(8,128)(2,1)S(1)}, u32[]{:S(2)}, u32[]{:S(2)}) collective-permute-start(bf16[411,256]{1,0:T(8,128)(2,1)} %refs_0_.4), channel_id=1, source_target_pairs={{0,4},{1,5},{2,6},{3,7},{4,0},{5,1},{6,2},{7,3},{8,12},{9,13},{10,... | collective-permute-start | bytes 631304 | tf_op jit(solution)/shard_map/ppermute | solution.py:516
  3.1 13.2 %collective-permute-start.7 = (bf16[411,256]{1,0:T(8,128)(2,1)}, bf16[411,256]{1,0:T(8,128)(2,1)S(1)}, u32[]{:S(2)}, u32[]{:S(2)}) collective-permute-start(bf16[411,256]{1,0:T(8,128)(2,1)} %refs_0_.4), channel_id=1, source_target_pairs={{0,2},{1,3},{2,0},{3,1},{4,6},{5,7},{6,4},{7,5},{8,10},{9,11},{10,... | collective-permute-start | bytes 631304 | tf_op jit(solution)/shard_map/ppermute | solution.py:516
  4.6 11.7 %collective-permute-start.9 = (bf16[411,256]{1,0:T(8,128)(2,1)}, bf16[411,256]{1,0:T(8,128)(2,1)S(1)}, u32[]{:S(2)}, u32[]{:S(2)}) collective-permute-start(bf16[411,256]{1,0:T(8,128)(2,1)} %refs_0_.4), channel_id=1, source_target_pairs={{0,6},{1,7},{2,4},{3,5},{4,2},{5,3},{6,0},{7,1},{8,14},{9,15},{10,... | collective-permute-start | bytes 631304 | tf_op jit(solution)/shard_map/ppermute | solution.py:516
  4.6 9.5 %collective-permute-start.2 = (bf16[128,768]{1,0:T(8,128)(2,1)}, bf16[128,768]{1,0:T(8,128)(2,1)S(1)}, u32[]{:S(2)}, u32[]{:S(2)}) collective-permute-start(bf16[128,768]{1,0:T(8,128)(2,1)} %refs_0_.3), channel_id=1, source_target_pairs={{0,8},{8,0},{16,24},{24,16},{1,9},{9,1},{17,25},{25,17},{2,10},{10... | collective-permute-start | bytes 589832 | tf_op jit(solution)/shard_map/ppermute | solution.py:519
  7.2 19.1 %copy-start.9 = (s32[256,1]{0,1:T(1,128)S(1)}, s32[256,1]{0,1:T(1,128)}, u32[]{:S(2)}) copy-start(s32[256,1]{0,1:T(1,128)} %param.12) | copy-start | bytes 3076
  7.4 3.9 %collective-permute-start = (bf16[16,512]{1,0:T(8,128)(2,1)S(1)}, bf16[16,512]{1,0:T(8,128)(2,1)S(1)}, u32[]{:S(2)}, u32[]{:S(2)}) collective-permute-start(bf16[16,512]{1,0:T(8,128)(2,1)S(1)} %shard_map.102.refs_0_), channel_id=1, source_target_pairs={{0,8},{8,0},{16,24},{24,16},{1,9},{9,1},{17,25},{25,17},{2,10},{10... | collective-permute-start | bytes 49160 | tf_op jit(solution)/shard_map/ppermute | solution.py:519
  11.3 4.9 %collective-permute-start.1 = (bf16[32,512]{1,0:T(8,128)(2,1)S(1)}, bf16[32,512]{1,0:T(8,128)(2,1)S(1)}, u32[]{:S(2)}, u32[]{:S(2)}) collective-permute-start(bf16[32,512]{1,0:T(8,128)(2,1)S(1)} %shard_map.103.refs_2_.refs_0_), channel_id=1, source_target_pairs={{0,16},{8,24},{16,0},{24,8},{1,17},{9,25},{17,1},{25,9},{2,18},{10... | collective-permute-start | bytes 98312 | tf_op jit(solution)/shard_map/ppermute | solution.py:519
  16.4 11.4 %collective-permute-start.10 = (bf16[1664,256]{1,0:T(8,128)(2,1)S(1)}, bf16[1664,256]{1,0:T(8,128)(2,1)S(1)}, u32[]{:S(2)}, u32[]{:S(2)}) collective-permute-start(bf16[1664,256]{1,0:T(8,128)(2,1)S(1)} %shard_map.107.refs_7_.refs_5_), channel_id=1, source_target_pairs={{0,1},{1,0},{2,3},{3,2},{4,5},{5,4},{6,7},{7,6},{8,9},{9,8},{10,11... | collective-permute-start | bytes 2555912 | tf_op jit(solution)/shard_map/ppermute | solution.py:516
  16.5 14.0 %collective-permute-start.11 = (bf16[256,768]{1,0:T(8,128)(2,1)S(1)}, bf16[256,768]{1,0:T(8,128)(2,1)S(1)}, u32[]{:S(2)}, u32[]{:S(2)}) collective-permute-start(bf16[256,768]{1,0:T(8,128)(2,1)S(1)} %shard_map.104.refs_2_.refs_0_), channel_id=1, source_target_pairs={{0,16},{1,17},{2,3},{3,2},{4,20},{5,21},{6,7},{7,6},{8,9},{9,8},{1... | collective-permute-start | bytes 1179656 | tf_op jit(solution)/shard_map/ppermute | solution.py:528
  19.3 5.5 %collective-permute-start.5 = (bf16[64,512]{1,0:T(8,128)(2,1)S(1)}, bf16[64,512]{1,0:T(8,128)(2,1)S(1)}, u32[]{:S(2)}, u32[]{:S(2)}) collective-permute-start(bf16[64,512]{1,0:T(8,128)(2,1)S(1)} %shard_map.105.refs_0_.refs_4_), channel_id=1, source_target_pairs={{0,6},{1,7},{2,4},{3,5},{4,2},{5,3},{6,0},{7,1},{8,14},{9,15},{10,... | collective-permute-start | bytes 196616 | tf_op jit(solution)/shard_map/ppermute | solution.py:516
  19.5 5.5 %collective-permute-start.4 = (bf16[64,512]{1,0:T(8,128)(2,1)S(1)}, bf16[64,512]{1,0:T(8,128)(2,1)S(1)}, u32[]{:S(2)}, u32[]{:S(2)}) collective-permute-start(bf16[64,512]{1,0:T(8,128)(2,1)S(1)} %shard_map.105.refs_0_.refs_4_), channel_id=1, source_target_pairs={{0,4},{1,5},{2,6},{3,7},{4,0},{5,1},{6,2},{7,3},{8,12},{9,13},{10,... | collective-permute-start | bytes 196616 | tf_op jit(solution)/shard_map/ppermute | solution.py:516
  20.8 5.0 %collective-permute-start.3 = (bf16[64,512]{1,0:T(8,128)(2,1)S(1)}, bf16[64,512]{1,0:T(8,128)(2,1)S(1)}, u32[]{:S(2)}, u32[]{:S(2)}) collective-permute-start(bf16[64,512]{1,0:T(8,128)(2,1)S(1)} %shard_map.105.refs_0_.refs_4_), channel_id=1, source_target_pairs={{0,2},{1,3},{2,0},{3,1},{4,6},{5,7},{6,4},{7,5},{8,10},{9,11},{10,... | collective-permute-start | bytes 196616 | tf_op jit(solution)/shard_map/ppermute | solution.py:516
  26.2 1.6 %collective-permute-start.6 = (bf16[256,512]{1,0:T(8,128)(2,1)S(1)}, bf16[256,512]{1,0:T(8,128)(2,1)S(1)}, u32[]{:S(2)}, u32[]{:S(2)}) collective-permute-start(bf16[256,512]{1,0:T(8,128)(2,1)S(1)} %shard_map.106.refs_5_), channel_id=1, source_target_pairs={{0,1},{1,0},{2,3},{3,2},{4,5},{5,4},{6,7},{7,6},{8,9},{9,8},{10,11... | collective-permute-start | bytes 786440 | tf_op jit(solution)/shard_map/ppermute | solution.py:516
  26.2 1.9 %copy-start = (bf16[2048,768]{1,0:T(8,128)(2,1)S(1)}, bf16[2048,768]{1,0:T(8,128)(2,1)}, u32[]{:S(2)}) copy-start(bf16[2048,768]{1,0:T(8,128)(2,1)} %refs_0_.5) | copy-start | bytes 9437188
  26.3 1.9 %copy-start.5 = (f32[768]{0:T(1024)S(1)}, f32[768]{0:T(1024)}, u32[]{:S(2)}) copy-start(f32[768]{0:T(1024)} %refs_3_.1) | copy-start | bytes 9220
  30.9 7.8 %collective-permute-start.12 = (bf16[128,768]{1,0:T(8,128)(2,1)S(1)}, bf16[128,768]{1,0:T(8,128)(2,1)S(1)}, u32[]{:S(2)}, u32[]{:S(2)}) collective-permute-start(bf16[128,768]{1,0:T(8,128)(2,1)S(1)} %get-tuple-element.32.refs_0_), channel_id=1, source_target_pairs={{0,2},{1,3},{2,0},{3,1},{4,5},{5,4},{6,7},{7,6},{8,10},{9,11},{10,... | collective-permute-start | bytes 589832 | tf_op jit(solution)/shard_map/ppermute | solution.py:528
  32.2 7.7 %collective-permute-start.13 = (bf16[128,768]{1,0:T(8,128)(2,1)S(1)}, bf16[128,768]{1,0:T(8,128)(2,1)S(1)}, u32[]{:S(2)}, u32[]{:S(2)}) collective-permute-start(bf16[128,768]{1,0:T(8,128)(2,1)S(1)} %get-tuple-element.33.refs_1_), channel_id=1, source_target_pairs={{0,4},{1,5},{2,3},{3,2},{4,0},{5,1},{6,7},{7,6},{8,9},{9,8},{10,14... | collective-permute-start | bytes 589832 | tf_op jit(solution)/shard_map/ppermute | solution.py:528
  32.3 11.2 %collective-permute-start.14 = (bf16[128,768]{1,0:T(8,128)(2,1)S(1)}, bf16[128,768]{1,0:T(8,128)(2,1)S(1)}, u32[]{:S(2)}, u32[]{:S(2)}) collective-permute-start(bf16[128,768]{1,0:T(8,128)(2,1)S(1)} %get-tuple-element.32.refs_0_), channel_id=1, source_target_pairs={{0,4},{1,5},{2,3},{3,2},{4,0},{5,1},{6,7},{7,6},{8,9},{9,8},{10,14... | collective-permute-start | bytes 589832 | tf_op jit(solution)/shard_map/ppermute | solution.py:528
  34.2 9.2 %collective-permute-start.15 = (bf16[128,768]{1,0:T(8,128)(2,1)S(1)}, bf16[128,768]{1,0:T(8,128)(2,1)S(1)}, u32[]{:S(2)}, u32[]{:S(2)}) collective-permute-start(bf16[128,768]{1,0:T(8,128)(2,1)S(1)} %get-tuple-element.33.refs_1_), channel_id=1, source_target_pairs={{0,2},{1,3},{2,0},{3,1},{4,5},{5,4},{6,7},{7,6},{8,10},{9,11},{10,... | collective-permute-start | bytes 589832 | tf_op jit(solution)/shard_map/ppermute | solution.py:528
  38.7 4.8 %collective-permute-start.16 = (bf16[128,768]{1,0:T(8,128)(2,1)S(1)}, bf16[128,768]{1,0:T(8,128)(2,1)S(1)}, u32[]{:S(2)}, u32[]{:S(2)}) collective-permute-start(bf16[128,768]{1,0:T(8,128)(2,1)S(1)} %collective-permute-done.12.refs_2_), channel_id=1, source_target_pairs={{0,1},{1,0},{2,6},{3,7},{4,5},{5,4},{6,2},{7,3},{8,12},{9,13},{10,... | collective-permute-start | bytes 589832 | tf_op jit(solution)/shard_map/ppermute | solution.py:528
  40.0 3.5 %collective-permute-start.17 = (bf16[128,768]{1,0:T(8,128)(2,1)S(1)}, bf16[128,768]{1,0:T(8,128)(2,1)S(1)}, u32[]{:S(2)}, u32[]{:S(2)}) collective-permute-start(bf16[128,768]{1,0:T(8,128)(2,1)S(1)} %collective-permute-done.13.refs_3_), channel_id=1, source_target_pairs={{0,1},{1,0},{2,3},{3,2},{4,6},{5,7},{6,4},{7,5},{8,9},{9,8},{10,11... | collective-permute-start | bytes 589832 | tf_op jit(solution)/shard_map/ppermute | solution.py:528
  40.6 3.5 %copy-start.1 = (bf16[1536,768]{1,0:T(8,128)(2,1)S(1)}, bf16[1536,768]{1,0:T(8,128)(2,1)}, u32[]{:S(2)}) copy-start(bf16[1536,768]{1,0:T(8,128)(2,1)} %refs_1_.1) | copy-start | bytes 7077892
  44.0 1.8 %collective-permute-start.18 = (bf16[256,768]{1,0:T(8,128)(2,1)S(1)}, bf16[256,768]{1,0:T(8,128)(2,1)S(1)}, u32[]{:S(2)}, u32[]{:S(2)}) collective-permute-start(bf16[256,768]{1,0:T(8,128)(2,1)S(1)} %shard_map.111.depart_ref), channel_id=1, source_target_pairs={{0,1},{1,0},{2,3},{3,2},{4,5},{5,4},{6,7},{7,6},{8,9},{9,8},{10,11... | collective-permute-start | bytes 1179656 | tf_op jit(solution)/shard_map/ppermute | solution.py:516
  48.8 1.8 %collective-permute-start.19 = (bf16[384,411]{1,0:T(8,128)(2,1)S(1)}, bf16[384,411]{1,0:T(8,128)(2,1)S(1)}, u32[]{:S(2)}, u32[]{:S(2)}) collective-permute-start(bf16[384,411]{1,0:T(8,128)(2,1)S(1)} %get-tuple-element.37), channel_id=1, source_target_pairs={{0,1},{1,0},{2,3},{3,2},{4,5},{5,4},{6,7},{7,6},{8,9},{9,8},{10,11... | collective-permute-start | bytes 946952 | tf_op jit(solution)/shard_map/ppermute | solution.py:516
  50.6 5.7 %collective-permute-start.20 = (bf16[96,411]{1,0:T(8,128)(2,1)S(1)}, bf16[96,411]{1,0:T(8,128)(2,1)S(1)}, u32[]{:S(2)}, u32[]{:S(2)}) collective-permute-start(bf16[96,411]{1,0:T(8,128)(2,1)S(1)} %get-tuple-element.39), channel_id=1, source_target_pairs={{0,2},{1,3},{2,0},{3,1},{4,6},{5,7},{6,4},{7,5},{8,10},{9,11},{10,... | collective-permute-start | bytes 236744 | tf_op jit(solution)/shard_map/ppermute | solution.py:516
  53.2 5.9 %collective-permute-start.21 = (bf16[96,411]{1,0:T(8,128)(2,1)S(1)}, bf16[96,411]{1,0:T(8,128)(2,1)S(1)}, u32[]{:S(2)}, u32[]{:S(2)}) collective-permute-start(bf16[96,411]{1,0:T(8,128)(2,1)S(1)} %get-tuple-element.40), channel_id=1, source_target_pairs={{0,4},{1,5},{2,6},{3,7},{4,0},{5,1},{6,2},{7,3},{8,12},{9,13},{10,... | collective-permute-start | bytes 236744 | tf_op jit(solution)/shard_map/ppermute | solution.py:516
  55.0 5.5 %collective-permute-start.22 = (bf16[96,411]{1,0:T(8,128)(2,1)S(1)}, bf16[96,411]{1,0:T(8,128)(2,1)S(1)}, u32[]{:S(2)}, u32[]{:S(2)}) collective-permute-start(bf16[96,411]{1,0:T(8,128)(2,1)S(1)} %get-tuple-element.41), channel_id=1, source_target_pairs={{0,6},{1,7},{2,4},{3,5},{4,2},{5,3},{6,0},{7,1},{8,14},{9,15},{10,... | collective-permute-start | bytes 236744 | tf_op jit(solution)/shard_map/ppermute | solution.py:516
  60.7 4.8 %collective-permute-start.23 = (bf16[32,411]{1,0:T(8,128)(2,1)S(1)}, bf16[32,411]{1,0:T(8,128)(2,1)S(1)}, u32[]{:S(2)}, u32[]{:S(2)}) collective-permute-start(bf16[32,411]{1,0:T(8,128)(2,1)S(1)} %get-tuple-element.43), channel_id=1, source_target_pairs={{0,8},{8,0},{16,24},{24,16},{1,9},{9,1},{17,25},{25,17},{2,10},{10... | collective-permute-start | bytes 78920 | tf_op jit(solution)/shard_map/ppermute | solution.py:519
  62.9 4.8 %collective-permute-start.24 = (bf16[32,411]{1,0:T(8,128)(2,1)S(1)}, bf16[32,411]{1,0:T(8,128)(2,1)S(1)}, u32[]{:S(2)}, u32[]{:S(2)}) collective-permute-start(bf16[32,411]{1,0:T(8,128)(2,1)S(1)} %get-tuple-element.44), channel_id=1, source_target_pairs={{0,16},{8,24},{16,0},{24,8},{1,17},{9,25},{17,1},{25,9},{2,18},{10... | collective-permute-start | bytes 78920 | tf_op jit(solution)/shard_map/ppermute | solution.py:519
  63.4 5.7 %collective-permute-start.25 = (bf16[32,411]{1,0:T(8,128)(2,1)S(1)}, bf16[32,411]{1,0:T(8,128)(2,1)S(1)}, u32[]{:S(2)}, u32[]{:S(2)}) collective-permute-start(bf16[32,411]{1,0:T(8,128)(2,1)S(1)} %get-tuple-element.45), channel_id=1, source_target_pairs={{0,24},{8,16},{16,8},{24,0},{1,25},{9,17},{17,9},{25,1},{2,26},{10... | collective-permute-start | bytes 78920 | tf_op jit(solution)/shard_map/ppermute | solution.py:519

commit v14 on v13

--- a/solution.py
+++ b/solution.py
@@ -548,7 +548,7 @@
         functools.partial(index_kernel, p),
         [shape((3 * reach, 1), jnp.int32)] + [shape((p.chips * p.patch, 1), jnp.int32)] * p.group,
         [],
-        flops=SLACK_FLOPS,
+        flops=10**9,
     )
 
     strips = call(
@@ -561,10 +561,11 @@
     seen, stages, before = observed, [], ()
     bit = 1
     while bit < p.tiles:
+        if 2 * bit < p.tiles:
+            seen = grow(seen, lambda value: trade(value, bit))
+            before = [seen]
         strips = grow(strips, lambda value: trade(value, bit), before)
-        if 2 * bit < p.tiles:
-            seen = grow(seen, lambda value: trade(value, bit), [strips])
-            before = [seen]
+        before = ()
         stages.append(strips)
         bit *= 2
     strips = join(

time: 70.6 us -> 69 us (0.977)
  waiting for transfers between devices: 29.9 us -> 28.8 us
    ppermute x6, waiting for transfers between devices: 8.98 us -> 7.81 us  [trade(): return lax.ppermute(value, 'tile', [(a, a ^ mask) for a in range(p.tiles)])]
    ppermute x13, starting transfers between devices: 12.8 us -> 11.7 us  [flip(): return lax.ppermute(value, 'chan', [(b, b ^ mask) for b in range(p.chans)])]
    ppermute x6, starting transfers between devices: 9.48 us -> 10.3 us  [trade(): return lax.ppermute(value, 'tile', [(a, a ^ mask) for a in range(p.tiles)])]
  transfers between devices with their start and end apart: 26 -> 26, of which waited for: 16 -> 17; matrix products, arithmetic and copies ran while one was open for 0% -> 0% of each run, Pallas kernels for 8% -> 8%
where the time goes in v14:
time: 69 us; the launch traced here: 68.9 us
  waiting for transfers between devices  28.8 us (42%)
  starting transfers between devices  28 us (41%)
  Pallas kernels  11.2 us (16%)
    ppermute x13, waiting for transfers between devices, flip(): return lax.ppermute(value, 'chan', [(b, b ^ mask) for b in range(p.chans)])  12.4 us
    ppermute x13, starting transfers between devices, flip(): return lax.ppermute(value, 'chan', [(b, b ^ mask) for b in range(p.chans)])  11.7 us
    pallas_call x17, Pallas kernels, call(): pl.pallas_call(kernel, out_shape=out_shape, in_specs=[far if k in in_hbm...  11.2 us
    ppermute x6, starting transfers between devices, trade(): return lax.ppermute(value, 'tile', [(a, a ^ mask) for a in range(p.tiles)])  10.3 us
    ppermute x7, waiting for transfers between devices, send(): lax.ppermute(value, both, sorted(((number(a), number(b)) for a, b in pair...  8.55 us
    ppermute x6, waiting for transfers between devices, trade(): return lax.ppermute(value, 'tile', [(a, a ^ mask) for a in range(p.tiles)])  7.81 us
    ppermute x7, starting transfers between devices, send(): lax.ppermute(value, both, sorted(((number(a), number(b)) for a, b in pair...  5.98 us
  transfers between devices with their start and end apart: 26, of which 17 were waited for; matrix products, arithmetic and copies ran while one was open for 0% of the time, Pallas kernels for 8%

profile of v14, /device:TPU:0, one launch (start us, length us, event | category | flops | bytes accessed | tf_op | source)
XLA Modules:
  0.0 68.9 jit_solution(15476807932545358799)
XLA Ops:
  0.0 3.1 %collective-permute-start.1 = (bf16[128,768]{1,0:T(8,128)(2,1)}, bf16[128,768]{1,0:T(8,128)(2,1)S(1)}, u32[]{:S(2)}, u32[]{:S(2)}) collective-permute-start(bf16[128,768]{1,0:T(8,128)(2,1)} %refs_0_.3), channel_id=1, source_target_pairs={{0,8},{8,0},{16,24},{24,16},{1,9},{9,1},{17,25},{25,17},{2,10},{10... | collective-permute-start | bytes 589832 | tf_op jit(solution)/shard_map/ppermute | solution.py:519
  3.1 1.5 %collective-permute-start.8 = (bf16[411,256]{1,0:T(8,128)(2,1)}, bf16[411,256]{1,0:T(8,128)(2,1)S(1)}, u32[]{:S(2)}, u32[]{:S(2)}) collective-permute-start(bf16[411,256]{1,0:T(8,128)(2,1)} %refs_0_.4), channel_id=1, source_target_pairs={{0,4},{1,5},{2,6},{3,7},{4,0},{5,1},{6,2},{7,3},{8,12},{9,13},{10,... | collective-permute-start | bytes 631304 | tf_op jit(solution)/shard_map/ppermute | solution.py:516
  4.6 1.5 %collective-permute-start.7 = (bf16[411,256]{1,0:T(8,128)(2,1)}, bf16[411,256]{1,0:T(8,128)(2,1)S(1)}, u32[]{:S(2)}, u32[]{:S(2)}) collective-permute-start(bf16[411,256]{1,0:T(8,128)(2,1)} %refs_0_.4), channel_id=1, source_target_pairs={{0,2},{1,3},{2,0},{3,1},{4,6},{5,7},{6,4},{7,5},{8,10},{9,11},{10,... | collective-permute-start | bytes 631304 | tf_op jit(solution)/shard_map/ppermute | solution.py:516
  6.1 0.5 collective-permute-start.9
  6.6 0.5 shard_map.101
  7.2 0.0 copy-start.9
  7.2 0.2 shard_map.102.refs_0_
  7.4 0.1 collective-permute-start
  7.5 0.8 %collective-permute-done.1.refs_1_ = bf16[128,768]{1,0:T(8,128)(2,1)S(1)} collective-permute-done((bf16[128,768]{1,0:T(8,128)(2,1)}, bf16[128,768]{1,0:T(8,128)(2,1)S(1)}, u32[]{:S(2)}, u32[]{:S(2)}) %collective-permute-start.1) | collective-permute-done | bytes 196640 | tf_op jit(solution)/shard_map/ppermute | solution.py:519
  8.2 0.5 shard_map.103.refs_2_.refs_0_
  8.8 2.4 %collective-permute-done.refs_1_ = bf16[16,512]{1,0:T(8,128)(2,1)S(1)} collective-permute-done((bf16[16,512]{1,0:T(8,128)(2,1)S(1)}, bf16[16,512]{1,0:T(8,128)(2,1)S(1)}, u32[]{:S(2)}, u32[]{:S(2)}) %collective-permute-start) | collective-permute-done | bytes 16416 | tf_op jit(solution)/shard_map/ppermute | solution.py:519
  11.2 2.7 %collective-permute-start.2 = (bf16[32,512]{1,0:T(8,128)(2,1)S(1)}, bf16[32,512]{1,0:T(8,128)(2,1)S(1)}, u32[]{:S(2)}, u32[]{:S(2)}) collective-permute-start(bf16[32,512]{1,0:T(8,128)(2,1)S(1)} %shard_map.104.refs_0_), channel_id=1, source_target_pairs={{0,16},{8,24},{16,0},{24,8},{1,17},{9,25},{17,1},{25,9},{2,18},{10... | collective-permute-start | bytes 98312 | tf_op jit(solution)/shard_map/ppermute | solution.py:519
  13.9 2.2 %collective-permute-done.2.refs_1_ = bf16[32,512]{1,0:T(8,128)(2,1)S(1)} collective-permute-done((bf16[32,512]{1,0:T(8,128)(2,1)S(1)}, bf16[32,512]{1,0:T(8,128)(2,1)S(1)}, u32[]{:S(2)}, u32[]{:S(2)}) %collective-permute-start.2) | collective-permute-done | bytes 32800 | tf_op jit(solution)/shard_map/ppermute | solution.py:519
  16.1 0.1 shard_map.105.refs_0_.refs_4_
  16.1 0.0 collective-permute-done.8.refs_2_
  16.2 0.1 shard_map.107.refs_7_.refs_5_
  16.2 0.1 collective-permute-start.10
  16.3 2.7 %collective-permute-start.11 = (bf16[256,768]{1,0:T(8,128)(2,1)S(1)}, bf16[256,768]{1,0:T(8,128)(2,1)S(1)}, u32[]{:S(2)}, u32[]{:S(2)}) collective-permute-start(bf16[256,768]{1,0:T(8,128)(2,1)S(1)} %shard_map.103.refs_2_.refs_0_), channel_id=1, source_target_pairs={{0,16},{1,17},{2,3},{3,2},{4,20},{5,21},{6,7},{7,6},{8,9},{9,8},{1... | collective-permute-start | bytes 1179656 | tf_op jit(solution)/shard_map/ppermute | solution.py:528
  19.0 0.5 collective-permute-start.5
  19.5 1.1 %collective-permute-start.4 = (bf16[64,512]{1,0:T(8,128)(2,1)S(1)}, bf16[64,512]{1,0:T(8,128)(2,1)S(1)}, u32[]{:S(2)}, u32[]{:S(2)}) collective-permute-start(bf16[64,512]{1,0:T(8,128)(2,1)S(1)} %shard_map.105.refs_0_.refs_4_), channel_id=1, source_target_pairs={{0,4},{1,5},{2,6},{3,7},{4,0},{5,1},{6,2},{7,3},{8,12},{9,13},{10,... | collective-permute-start | bytes 196616 | tf_op jit(solution)/shard_map/ppermute | solution.py:516
  20.6 1.9 %collective-permute-start.3 = (bf16[64,512]{1,0:T(8,128)(2,1)S(1)}, bf16[64,512]{1,0:T(8,128)(2,1)S(1)}, u32[]{:S(2)}, u32[]{:S(2)}) collective-permute-start(bf16[64,512]{1,0:T(8,128)(2,1)S(1)} %shard_map.105.refs_0_.refs_4_), channel_id=1, source_target_pairs={{0,2},{1,3},{2,0},{3,1},{4,6},{5,7},{6,4},{7,5},{8,10},{9,11},{10,... | collective-permute-start | bytes 196616 | tf_op jit(solution)/shard_map/ppermute | solution.py:516
  22.5 2.0 %collective-permute-done.5.refs_3_ = bf16[64,512]{1,0:T(8,128)(2,1)S(1)} collective-permute-done((bf16[64,512]{1,0:T(8,128)(2,1)S(1)}, bf16[64,512]{1,0:T(8,128)(2,1)S(1)}, u32[]{:S(2)}, u32[]{:S(2)}) %collective-permute-start.5) | collective-permute-done | bytes 65568 | tf_op jit(solution)/shard_map/ppermute | solution.py:516
  24.5 0.3 collective-permute-done.4.refs_2_
  24.8 0.8 %collective-permute-done.3.refs_1_ = bf16[64,512]{1,0:T(8,128)(2,1)S(1)} collective-permute-done((bf16[64,512]{1,0:T(8,128)(2,1)S(1)}, bf16[64,512]{1,0:T(8,128)(2,1)S(1)}, u32[]{:S(2)}, u32[]{:S(2)}) %collective-permute-start.3) | collective-permute-done | bytes 65568 | tf_op jit(solution)/shard_map/ppermute | solution.py:516
  25.6 0.3 shard_map.106.refs_5_
  25.9 0.1 collective-permute-start.6
  26.0 0.0 copy-start
  26.1 0.0 copy-start.5
  26.1 0.4 shard_map.100
  26.4 1.1 %collective-permute-done.6.refs_6_ = bf16[256,512]{1,0:T(8,128)(2,1)S(1)} collective-permute-done((bf16[256,512]{1,0:T(8,128)(2,1)S(1)}, bf16[256,512]{1,0:T(8,128)(2,1)S(1)}, u32[]{:S(2)}, u32[]{:S(2)}) %collective-permute-start.6) | collective-permute-done | bytes 262176 | tf_op jit(solution)/shard_map/ppermute | solution.py:516
  27.6 0.4 copy-done
  27.9 2.3 %shard_map.108 = (f32[256,768]{1,0:T(8,128)S(1)}, f32[256,1]{1,0:T(8,128)S(1)}, f32[8,256,256]{2,1,0:T(8,128)S(1)}, f32[24,128]{1,0:T(8,128)S(1)}) custom-call(s32[256,1]{1,0:T(8,128)S(1)} %get-tuple-element.26.refs_0_.place_ref, s32[256,1]{1,0:T(8,128)S(1)} %get-tuple-element.27.refs_1_, s32[24,1]{1,0:T(8,128)S(1)} %get-tuple-element.28.after_ref.refs_2_, ...), custom_call_target="tpu_custom_call" | custom-call | flops 100000000 | bytes 5379168 | tf_op jit(solution)/shard_map/pallas_call | solution.py:164
  30.3 0.4 shard_map.110
  30.7 1.3 %collective-permute-start.12 = (bf16[128,768]{1,0:T(8,128)(2,1)S(1)}, bf16[128,768]{1,0:T(8,128)(2,1)S(1)}, u32[]{:S(2)}, u32[]{:S(2)}) collective-permute-start(bf16[128,768]{1,0:T(8,128)(2,1)S(1)} %get-tuple-element.32.refs_0_), channel_id=1, source_target_pairs={{0,2},{1,3},{2,0},{3,1},{4,5},{5,4},{6,7},{7,6},{8,10},{9,11},{10,... | collective-permute-start | bytes 589832 | tf_op jit(solution)/shard_map/ppermute | solution.py:528
  32.0 0.1 collective-permute-start.13
  32.0 1.9 %collective-permute-start.14 = (bf16[128,768]{1,0:T(8,128)(2,1)S(1)}, bf16[128,768]{1,0:T(8,128)(2,1)S(1)}, u32[]{:S(2)}, u32[]{:S(2)}) collective-permute-start(bf16[128,768]{1,0:T(8,128)(2,1)S(1)} %get-tuple-element.32.refs_0_), channel_id=1, source_target_pairs={{0,4},{1,5},{2,3},{3,2},{4,0},{5,1},{6,7},{7,6},{8,9},{9,8},{10,14... | collective-permute-start | bytes 589832 | tf_op jit(solution)/shard_map/ppermute | solution.py:528
  34.0 4.5 %collective-permute-done.12.refs_2_ = bf16[128,768]{1,0:T(8,128)(2,1)S(1)} collective-permute-done((bf16[128,768]{1,0:T(8,128)(2,1)S(1)}, bf16[128,768]{1,0:T(8,128)(2,1)S(1)}, u32[]{:S(2)}, u32[]{:S(2)}) %collective-permute-start.12) | collective-permute-done | bytes 196640 | tf_op jit(solution)/shard_map/ppermute | solution.py:528
  38.5 1.2 %collective-permute-done.13.refs_3_ = bf16[128,768]{1,0:T(8,128)(2,1)S(1)} collective-permute-done((bf16[128,768]{1,0:T(8,128)(2,1)S(1)}, bf16[128,768]{1,0:T(8,128)(2,1)S(1)}, u32[]{:S(2)}, u32[]{:S(2)}) %collective-permute-start.13) | collective-permute-done | bytes 196640 | tf_op jit(solution)/shard_map/ppermute | solution.py:528
  39.7 0.6 shard_map.109.refs_8_.refs_2_
  40.3 0.0 copy-start.1
  40.3 2.8 %collective-permute-done.14.refs_4_ = bf16[128,768]{1,0:T(8,128)(2,1)S(1)} collective-permute-done((bf16[128,768]{1,0:T(8,128)(2,1)S(1)}, bf16[128,768]{1,0:T(8,128)(2,1)S(1)}, u32[]{:S(2)}, u32[]{:S(2)}) %collective-permute-start.14) | collective-permute-done | bytes 196640 | tf_op jit(solution)/shard_map/ppermute | solution.py:528
  43.2 0.6 shard_map.111.depart_ref
  43.8 0.1 collective-permute-start.18
  43.8 0.5 shard_map.112.refs_3_
  44.3 1.2 %collective-permute-done.18.refs_4_ = bf16[256,768]{1,0:T(8,128)(2,1)S(1)} collective-permute-done((bf16[256,768]{1,0:T(8,128)(2,1)S(1)}, bf16[256,768]{1,0:T(8,128)(2,1)S(1)}, u32[]{:S(2)}, u32[]{:S(2)}) %collective-permute-start.18) | collective-permute-done | bytes 393248 | tf_op jit(solution)/shard_map/ppermute | solution.py:516
  45.5 3.0 %shard_map.113 = (bf16[384,411]{1,0:T(8,128)(2,1)S(1)}, bf16[384,411]{1,0:T(8,128)(2,1)S(1)}) custom-call(bf16[2048,768]{1,0:T(8,128)(2,1)S(1)} %copy-done, bf16[1536,768]{1,0:T(8,128)(2,1)S(1)} %copy-done.1, f32[8,256,256]{2,1,0:T(8,128)S(1)} %shard_map.109.refs_8_.refs_2_, f32[256,768]{1,0:T(8,128)S(1)} %shard_map.112.refs_3_, ...), custom_call_target="tpu_custom_call" | custom-call | flops 1840250880 | bytes 10488832 | tf_op jit(solution)/shard_map/pallas_call | solution.py:164
  48.5 0.2 collective-permute-start.19
  48.7 0.1 slice_bitcast_fusion.2
  48.8 1.5 %collective-permute-done.19.refs_1_ = bf16[384,411]{1,0:T(8,128)(2,1)S(1)} collective-permute-done((bf16[384,411]{1,0:T(8,128)(2,1)S(1)}, bf16[384,411]{1,0:T(8,128)(2,1)S(1)}, u32[]{:S(2)}, u32[]{:S(2)}) %collective-permute-start.19) | collective-permute-done | bytes 315680 | tf_op jit(solution)/shard_map/ppermute | solution.py:516
  50.3 0.1 shard_map.114
  50.4 2.6 %collective-permute-start.20 = (bf16[96,411]{1,0:T(8,128)(2,1)S(1)}, bf16[96,411]{1,0:T(8,128)(2,1)S(1)}, u32[]{:S(2)}, u32[]{:S(2)}) collective-permute-start(bf16[96,411]{1,0:T(8,128)(2,1)S(1)} %get-tuple-element.39), channel_id=1, source_target_pairs={{0,2},{1,3},{2,0},{3,1},{4,6},{5,7},{6,4},{7,5},{8,10},{9,11},{10,... | collective-permute-start | bytes 236744 | tf_op jit(solution)/shard_map/ppermute | solution.py:516
  53.0 1.7 %collective-permute-start.21 = (bf16[96,411]{1,0:T(8,128)(2,1)S(1)}, bf16[96,411]{1,0:T(8,128)(2,1)S(1)}, u32[]{:S(2)}, u32[]{:S(2)}) collective-permute-start(bf16[96,411]{1,0:T(8,128)(2,1)S(1)} %get-tuple-element.40), channel_id=1, source_target_pairs={{0,4},{1,5},{2,6},{3,7},{4,0},{5,1},{6,2},{7,3},{8,12},{9,13},{10,... | collective-permute-start | bytes 236744 | tf_op jit(solution)/shard_map/ppermute | solution.py:516
  54.7 1.4 %collective-permute-done.20.refs_1_ = bf16[96,411]{1,0:T(8,128)(2,1)S(1)} collective-permute-done((bf16[96,411]{1,0:T(8,128)(2,1)S(1)}, bf16[96,411]{1,0:T(8,128)(2,1)S(1)}, u32[]{:S(2)}, u32[]{:S(2)}) %collective-permute-start.20) | collective-permute-done | bytes 78944 | tf_op jit(solution)/shard_map/ppermute | solution.py:516
  56.1 2.8 %collective-permute-done.21.refs_2_ = bf16[96,411]{1,0:T(8,128)(2,1)S(1)} collective-permute-done((bf16[96,411]{1,0:T(8,128)(2,1)S(1)}, bf16[96,411]{1,0:T(8,128)(2,1)S(1)}, u32[]{:S(2)}, u32[]{:S(2)}) %collective-permute-start.21) | collective-permute-done | bytes 78944 | tf_op jit(solution)/shard_map/ppermute | solution.py:516
  58.9 1.3 %collective-permute-done.22.refs_3_ = bf16[96,411]{1,0:T(8,128)(2,1)S(1)} collective-permute-done((bf16[96,411]{1,0:T(8,128)(2,1)S(1)}, bf16[96,411]{1,0:T(8,128)(2,1)S(1)}, u32[]{:S(2)}, u32[]{:S(2)}) %collective-permute-start.22) | collective-permute-done | bytes 78944 | tf_op jit(solution)/shard_map/ppermute | solution.py:516
  60.2 0.2 shard_map.115
  60.4 0.8 %collective-permute-start.23 = (bf16[32,411]{1,0:T(8,128)(2,1)S(1)}, bf16[32,411]{1,0:T(8,128)(2,1)S(1)}, u32[]{:S(2)}, u32[]{:S(2)}) collective-permute-start(bf16[32,411]{1,0:T(8,128)(2,1)S(1)} %get-tuple-element.43), channel_id=1, source_target_pairs={{0,8},{8,0},{16,24},{24,16},{1,9},{9,1},{17,25},{25,17},{2,10},{10... | collective-permute-start | bytes 78920 | tf_op jit(solution)/shard_map/ppermute | solution.py:519
  61.3 0.5 collective-permute-start.24
  61.8 3.1 %collective-permute-start.25 = (bf16[32,411]{1,0:T(8,128)(2,1)S(1)}, bf16[32,411]{1,0:T(8,128)(2,1)S(1)}, u32[]{:S(2)}, u32[]{:S(2)}) collective-permute-start(bf16[32,411]{1,0:T(8,128)(2,1)S(1)} %get-tuple-element.45), channel_id=1, source_target_pairs={{0,24},{8,16},{16,8},{24,0},{1,25},{9,17},{17,9},{25,1},{2,26},{10... | collective-permute-start | bytes 78920 | tf_op jit(solution)/shard_map/ppermute | solution.py:519
  64.9 0.1 maximum_sqrt_fusion
  65.0 0.1 copy.19
  65.1 1.0 %collective-permute-done.24.refs_2_ = bf16[32,411]{1,0:T(8,128)(2,1)S(1)} collective-permute-done((bf16[32,411]{1,0:T(8,128)(2,1)S(1)}, bf16[32,411]{1,0:T(8,128)(2,1)S(1)}, u32[]{:S(2)}, u32[]{:S(2)}) %collective-permute-start.24) | collective-permute-done | bytes 26336 | tf_op jit(solution)/shard_map/ppermute | solution.py:519
  66.1 1.4 %collective-permute-done.25.refs_3_ = bf16[32,411]{1,0:T(8,128)(2,1)S(1)} collective-permute-done((bf16[32,411]{1,0:T(8,128)(2,1)S(1)}, bf16[32,411]{1,0:T(8,128)(2,1)S(1)}, u32[]{:S(2)}, u32[]{:S(2)}) %collective-permute-start.25) | collective-permute-done | bytes 26336 | tf_op jit(solution)/shard_map/ppermute | solution.py:519
  67.5 1.4 %shard_map.116 = f32[4,32,411]{2,1,0:T(8,128)} custom-call(bf16[32,411]{1,0:T(8,128)(2,1)S(1)} %get-tuple-element.42.refs_0_, bf16[32,411]{1,0:T(8,128)(2,1)S(1)} %collective-permute-done.23.refs_1_, bf16[32,411]{1,0:T(8,128)(2,1)S(1)} %collective-permute-done.24.refs_2_, bf16[32,411]{1,0:T(8,128)(2,1)S(1)} %collective-permute-done.25.refs_3_, ...), custom_call_target="tpu_custom_call" | custom-call | flops 5260800 | bytes 106752 | tf_op jit(solution)/shard_map/pallas_call | solution.py:164
  (29 shorter events, 0.1 us)
Async XLA Ops:
  0.0 8.2 %copy-start.4 = (bf16[128,768]{1,0:T(8,128)(2,1)S(1)}, bf16[128,768]{1,0:T(8,128)(2,1)}, u32[]{:S(2)}) copy-start(bf16[128,768]{1,0:T(8,128)(2,1)} %refs_0_.3) | copy-start | bytes 589828
  0.0 16.2 %copy-start.3 = (bf16[411,256]{1,0:T(8,128)(2,1)S(1)}, bf16[411,256]{1,0:T(8,128)(2,1)}, u32[]{:S(2)}) copy-start(bf16[411,256]{1,0:T(8,128)(2,1)} %refs_0_.4) | copy-start | bytes 631300
  0.0 7.2 %copy-start.7 = (f32[256]{0:T(256)S(1)}, f32[256]{0:T(256)}, u32[]{:S(2)}) copy-start(f32[256]{0:T(256)} %bias_ref.1) | copy-start | bytes 3076
  0.0 7.2 %copy-start.8 = (s32[128]{0:T(128)S(1)}, s32[128]{0:T(128)}, u32[]{:S(2)}) copy-start(s32[128]{0:T(128)} %usable_ref.1) | copy-start | bytes 1540
  0.0 7.2 %copy-start.6 = (f32[4,32]{1,0:T(4,128)S(1)}, f32[4,32]{1,0:T(4,128)}, u32[]{:S(2)}) copy-start(f32[4,32]{1,0:T(4,128)} %diffusivity_ref.1) | copy-start | bytes 1540
  0.0 7.2 %copy-start.2 = (f32[4,32,411]{2,1,0:T(8,128)S(1)}, f32[4,32,411]{2,1,0:T(8,128)}, u32[]{:S(2)}) copy-start(f32[4,32,411]{2,1,0:T(8,128)} %fields_ref.1) | copy-start | bytes 631300
  0.0 8.2 %collective-permute-start.1 = (bf16[128,768]{1,0:T(8,128)(2,1)}, bf16[128,768]{1,0:T(8,128)(2,1)S(1)}, u32[]{:S(2)}, u32[]{:S(2)}) collective-permute-start(bf16[128,768]{1,0:T(8,128)(2,1)} %refs_0_.3), channel_id=1, source_target_pairs={{0,8},{8,0},{16,24},{24,16},{1,9},{9,1},{17,25},{25,17},{2,10},{10... | collective-permute-start | bytes 589832 | tf_op jit(solution)/shard_map/ppermute | solution.py:519
  3.1 13.0 %collective-permute-start.8 = (bf16[411,256]{1,0:T(8,128)(2,1)}, bf16[411,256]{1,0:T(8,128)(2,1)S(1)}, u32[]{:S(2)}, u32[]{:S(2)}) collective-permute-start(bf16[411,256]{1,0:T(8,128)(2,1)} %refs_0_.4), channel_id=1, source_target_pairs={{0,4},{1,5},{2,6},{3,7},{4,0},{5,1},{6,2},{7,3},{8,12},{9,13},{10,... | collective-permute-start | bytes 631304 | tf_op jit(solution)/shard_map/ppermute | solution.py:516
  4.6 11.5 %collective-permute-start.7 = (bf16[411,256]{1,0:T(8,128)(2,1)}, bf16[411,256]{1,0:T(8,128)(2,1)S(1)}, u32[]{:S(2)}, u32[]{:S(2)}) collective-permute-start(bf16[411,256]{1,0:T(8,128)(2,1)} %refs_0_.4), channel_id=1, source_target_pairs={{0,2},{1,3},{2,0},{3,1},{4,6},{5,7},{6,4},{7,5},{8,10},{9,11},{10,... | collective-permute-start | bytes 631304 | tf_op jit(solution)/shard_map/ppermute | solution.py:516
  6.1 10.0 %collective-permute-start.9 = (bf16[411,256]{1,0:T(8,128)(2,1)}, bf16[411,256]{1,0:T(8,128)(2,1)S(1)}, u32[]{:S(2)}, u32[]{:S(2)}) collective-permute-start(bf16[411,256]{1,0:T(8,128)(2,1)} %refs_0_.4), channel_id=1, source_target_pairs={{0,6},{1,7},{2,4},{3,5},{4,2},{5,3},{6,0},{7,1},{8,14},{9,15},{10,... | collective-permute-start | bytes 631304 | tf_op jit(solution)/shard_map/ppermute | solution.py:516
  7.2 18.9 %copy-start.9 = (s32[256,1]{0,1:T(1,128)S(1)}, s32[256,1]{0,1:T(1,128)}, u32[]{:S(2)}) copy-start(s32[256,1]{0,1:T(1,128)} %param.12) | copy-start | bytes 3076
  7.4 3.7 %collective-permute-start = (bf16[16,512]{1,0:T(8,128)(2,1)S(1)}, bf16[16,512]{1,0:T(8,128)(2,1)S(1)}, u32[]{:S(2)}, u32[]{:S(2)}) collective-permute-start(bf16[16,512]{1,0:T(8,128)(2,1)S(1)} %shard_map.102.refs_0_), channel_id=1, source_target_pairs={{0,8},{8,0},{16,24},{24,16},{1,9},{9,1},{17,25},{25,17},{2,10},{10... | collective-permute-start | bytes 49160 | tf_op jit(solution)/shard_map/ppermute | solution.py:519
  11.2 4.9 %collective-permute-start.2 = (bf16[32,512]{1,0:T(8,128)(2,1)S(1)}, bf16[32,512]{1,0:T(8,128)(2,1)S(1)}, u32[]{:S(2)}, u32[]{:S(2)}) collective-permute-start(bf16[32,512]{1,0:T(8,128)(2,1)S(1)} %shard_map.104.refs_0_), channel_id=1, source_target_pairs={{0,16},{8,24},{16,0},{24,8},{1,17},{9,25},{17,1},{25,9},{2,18},{10... | collective-permute-start | bytes 98312 | tf_op jit(solution)/shard_map/ppermute | solution.py:519
  16.2 11.3 %collective-permute-start.10 = (bf16[1664,256]{1,0:T(8,128)(2,1)S(1)}, bf16[1664,256]{1,0:T(8,128)(2,1)S(1)}, u32[]{:S(2)}, u32[]{:S(2)}) collective-permute-start(bf16[1664,256]{1,0:T(8,128)(2,1)S(1)} %shard_map.107.refs_7_.refs_5_), channel_id=1, source_target_pairs={{0,1},{1,0},{2,3},{3,2},{4,5},{5,4},{6,7},{7,6},{8,9},{9,8},{10,11... | collective-permute-start | bytes 2555912 | tf_op jit(solution)/shard_map/ppermute | solution.py:516
  16.3 13.9 %collective-permute-start.11 = (bf16[256,768]{1,0:T(8,128)(2,1)S(1)}, bf16[256,768]{1,0:T(8,128)(2,1)S(1)}, u32[]{:S(2)}, u32[]{:S(2)}) collective-permute-start(bf16[256,768]{1,0:T(8,128)(2,1)S(1)} %shard_map.103.refs_2_.refs_0_), channel_id=1, source_target_pairs={{0,16},{1,17},{2,3},{3,2},{4,20},{5,21},{6,7},{7,6},{8,9},{9,8},{1... | collective-permute-start | bytes 1179656 | tf_op jit(solution)/shard_map/ppermute | solution.py:528
  19.0 5.4 %collective-permute-start.5 = (bf16[64,512]{1,0:T(8,128)(2,1)S(1)}, bf16[64,512]{1,0:T(8,128)(2,1)S(1)}, u32[]{:S(2)}, u32[]{:S(2)}) collective-permute-start(bf16[64,512]{1,0:T(8,128)(2,1)S(1)} %shard_map.105.refs_0_.refs_4_), channel_id=1, source_target_pairs={{0,6},{1,7},{2,4},{3,5},{4,2},{5,3},{6,0},{7,1},{8,14},{9,15},{10,... | collective-permute-start | bytes 196616 | tf_op jit(solution)/shard_map/ppermute | solution.py:516
  19.5 5.3 %collective-permute-start.4 = (bf16[64,512]{1,0:T(8,128)(2,1)S(1)}, bf16[64,512]{1,0:T(8,128)(2,1)S(1)}, u32[]{:S(2)}, u32[]{:S(2)}) collective-permute-start(bf16[64,512]{1,0:T(8,128)(2,1)S(1)} %shard_map.105.refs_0_.refs_4_), channel_id=1, source_target_pairs={{0,4},{1,5},{2,6},{3,7},{4,0},{5,1},{6,2},{7,3},{8,12},{9,13},{10,... | collective-permute-start | bytes 196616 | tf_op jit(solution)/shard_map/ppermute | solution.py:516
  20.6 5.0 %collective-permute-start.3 = (bf16[64,512]{1,0:T(8,128)(2,1)S(1)}, bf16[64,512]{1,0:T(8,128)(2,1)S(1)}, u32[]{:S(2)}, u32[]{:S(2)}) collective-permute-start(bf16[64,512]{1,0:T(8,128)(2,1)S(1)} %shard_map.105.refs_0_.refs_4_), channel_id=1, source_target_pairs={{0,2},{1,3},{2,0},{3,1},{4,6},{5,7},{6,4},{7,5},{8,10},{9,11},{10,... | collective-permute-start | bytes 196616 | tf_op jit(solution)/shard_map/ppermute | solution.py:516
  25.9 1.6 %collective-permute-start.6 = (bf16[256,512]{1,0:T(8,128)(2,1)S(1)}, bf16[256,512]{1,0:T(8,128)(2,1)S(1)}, u32[]{:S(2)}, u32[]{:S(2)}) collective-permute-start(bf16[256,512]{1,0:T(8,128)(2,1)S(1)} %shard_map.106.refs_5_), channel_id=1, source_target_pairs={{0,1},{1,0},{2,3},{3,2},{4,5},{5,4},{6,7},{7,6},{8,9},{9,8},{10,11... | collective-permute-start | bytes 786440 | tf_op jit(solution)/shard_map/ppermute | solution.py:516
  26.0 1.9 %copy-start = (bf16[2048,768]{1,0:T(8,128)(2,1)S(1)}, bf16[2048,768]{1,0:T(8,128)(2,1)}, u32[]{:S(2)}) copy-start(bf16[2048,768]{1,0:T(8,128)(2,1)} %refs_0_.5) | copy-start | bytes 9437188
  26.1 1.9 %copy-start.5 = (f32[768]{0:T(1024)S(1)}, f32[768]{0:T(1024)}, u32[]{:S(2)}) copy-start(f32[768]{0:T(1024)} %refs_3_.1) | copy-start | bytes 9220
  30.7 7.8 %collective-permute-start.12 = (bf16[128,768]{1,0:T(8,128)(2,1)S(1)}, bf16[128,768]{1,0:T(8,128)(2,1)S(1)}, u32[]{:S(2)}, u32[]{:S(2)}) collective-permute-start(bf16[128,768]{1,0:T(8,128)(2,1)S(1)} %get-tuple-element.32.refs_0_), channel_id=1, source_target_pairs={{0,2},{1,3},{2,0},{3,1},{4,5},{5,4},{6,7},{7,6},{8,10},{9,11},{10,... | collective-permute-start | bytes 589832 | tf_op jit(solution)/shard_map/ppermute | solution.py:528
  32.0 7.7 %collective-permute-start.13 = (bf16[128,768]{1,0:T(8,128)(2,1)S(1)}, bf16[128,768]{1,0:T(8,128)(2,1)S(1)}, u32[]{:S(2)}, u32[]{:S(2)}) collective-permute-start(bf16[128,768]{1,0:T(8,128)(2,1)S(1)} %get-tuple-element.33.refs_1_), channel_id=1, source_target_pairs={{0,4},{1,5},{2,3},{3,2},{4,0},{5,1},{6,7},{7,6},{8,9},{9,8},{10,14... | collective-permute-start | bytes 589832 | tf_op jit(solution)/shard_map/ppermute | solution.py:528
  32.0 11.1 %collective-permute-start.14 = (bf16[128,768]{1,0:T(8,128)(2,1)S(1)}, bf16[128,768]{1,0:T(8,128)(2,1)S(1)}, u32[]{:S(2)}, u32[]{:S(2)}) collective-permute-start(bf16[128,768]{1,0:T(8,128)(2,1)S(1)} %get-tuple-element.32.refs_0_), channel_id=1, source_target_pairs={{0,4},{1,5},{2,3},{3,2},{4,0},{5,1},{6,7},{7,6},{8,9},{9,8},{10,14... | collective-permute-start | bytes 589832 | tf_op jit(solution)/shard_map/ppermute | solution.py:528
  34.0 9.2 %collective-permute-start.15 = (bf16[128,768]{1,0:T(8,128)(2,1)S(1)}, bf16[128,768]{1,0:T(8,128)(2,1)S(1)}, u32[]{:S(2)}, u32[]{:S(2)}) collective-permute-start(bf16[128,768]{1,0:T(8,128)(2,1)S(1)} %get-tuple-element.33.refs_1_), channel_id=1, source_target_pairs={{0,2},{1,3},{2,0},{3,1},{4,5},{5,4},{6,7},{7,6},{8,10},{9,11},{10,... | collective-permute-start | bytes 589832 | tf_op jit(solution)/shard_map/ppermute | solution.py:528
  38.5 4.7 %collective-permute-start.16 = (bf16[128,768]{1,0:T(8,128)(2,1)S(1)}, bf16[128,768]{1,0:T(8,128)(2,1)S(1)}, u32[]{:S(2)}, u32[]{:S(2)}) collective-permute-start(bf16[128,768]{1,0:T(8,128)(2,1)S(1)} %collective-permute-done.12.refs_2_), channel_id=1, source_target_pairs={{0,1},{1,0},{2,6},{3,7},{4,5},{5,4},{6,2},{7,3},{8,12},{9,13},{10,... | collective-permute-start | bytes 589832 | tf_op jit(solution)/shard_map/ppermute | solution.py:528
  39.7 3.5 %collective-permute-start.17 = (bf16[128,768]{1,0:T(8,128)(2,1)S(1)}, bf16[128,768]{1,0:T(8,128)(2,1)S(1)}, u32[]{:S(2)}, u32[]{:S(2)}) collective-permute-start(bf16[128,768]{1,0:T(8,128)(2,1)S(1)} %collective-permute-done.13.refs_3_), channel_id=1, source_target_pairs={{0,1},{1,0},{2,3},{3,2},{4,6},{5,7},{6,4},{7,5},{8,9},{9,8},{10,11... | collective-permute-start | bytes 589832 | tf_op jit(solution)/shard_map/ppermute | solution.py:528
  40.3 3.5 %copy-start.1 = (bf16[1536,768]{1,0:T(8,128)(2,1)S(1)}, bf16[1536,768]{1,0:T(8,128)(2,1)}, u32[]{:S(2)}) copy-start(bf16[1536,768]{1,0:T(8,128)(2,1)} %refs_1_.1) | copy-start | bytes 7077892
  43.8 1.8 %collective-permute-start.18 = (bf16[256,768]{1,0:T(8,128)(2,1)S(1)}, bf16[256,768]{1,0:T(8,128)(2,1)S(1)}, u32[]{:S(2)}, u32[]{:S(2)}) collective-permute-start(bf16[256,768]{1,0:T(8,128)(2,1)S(1)} %shard_map.111.depart_ref), channel_id=1, source_target_pairs={{0,1},{1,0},{2,3},{3,2},{4,5},{5,4},{6,7},{7,6},{8,9},{9,8},{10,11... | collective-permute-start | bytes 1179656 | tf_op jit(solution)/shard_map/ppermute | solution.py:516
  48.5 1.8 %collective-permute-start.19 = (bf16[384,411]{1,0:T(8,128)(2,1)S(1)}, bf16[384,411]{1,0:T(8,128)(2,1)S(1)}, u32[]{:S(2)}, u32[]{:S(2)}) collective-permute-start(bf16[384,411]{1,0:T(8,128)(2,1)S(1)} %get-tuple-element.37), channel_id=1, source_target_pairs={{0,1},{1,0},{2,3},{3,2},{4,5},{5,4},{6,7},{7,6},{8,9},{9,8},{10,11... | collective-permute-start | bytes 946952 | tf_op jit(solution)/shard_map/ppermute | solution.py:516
  50.4 5.7 %collective-permute-start.20 = (bf16[96,411]{1,0:T(8,128)(2,1)S(1)}, bf16[96,411]{1,0:T(8,128)(2,1)S(1)}, u32[]{:S(2)}, u32[]{:S(2)}) collective-permute-start(bf16[96,411]{1,0:T(8,128)(2,1)S(1)} %get-tuple-element.39), channel_id=1, source_target_pairs={{0,2},{1,3},{2,0},{3,1},{4,6},{5,7},{6,4},{7,5},{8,10},{9,11},{10,... | collective-permute-start | bytes 236744 | tf_op jit(solution)/shard_map/ppermute | solution.py:516
  53.0 5.9 %collective-permute-start.21 = (bf16[96,411]{1,0:T(8,128)(2,1)S(1)}, bf16[96,411]{1,0:T(8,128)(2,1)S(1)}, u32[]{:S(2)}, u32[]{:S(2)}) collective-permute-start(bf16[96,411]{1,0:T(8,128)(2,1)S(1)} %get-tuple-element.40), channel_id=1, source_target_pairs={{0,4},{1,5},{2,6},{3,7},{4,0},{5,1},{6,2},{7,3},{8,12},{9,13},{10,... | collective-permute-start | bytes 236744 | tf_op jit(solution)/shard_map/ppermute | solution.py:516
  54.7 5.5 %collective-permute-start.22 = (bf16[96,411]{1,0:T(8,128)(2,1)S(1)}, bf16[96,411]{1,0:T(8,128)(2,1)S(1)}, u32[]{:S(2)}, u32[]{:S(2)}) collective-permute-start(bf16[96,411]{1,0:T(8,128)(2,1)S(1)} %get-tuple-element.41), channel_id=1, source_target_pairs={{0,6},{1,7},{2,4},{3,5},{4,2},{5,3},{6,0},{7,1},{8,14},{9,15},{10,... | collective-permute-start | bytes 236744 | tf_op jit(solution)/shard_map/ppermute | solution.py:516
  60.4 4.6 %collective-permute-start.23 = (bf16[32,411]{1,0:T(8,128)(2,1)S(1)}, bf16[32,411]{1,0:T(8,128)(2,1)S(1)}, u32[]{:S(2)}, u32[]{:S(2)}) collective-permute-start(bf16[32,411]{1,0:T(8,128)(2,1)S(1)} %get-tuple-element.43), channel_id=1, source_target_pairs={{0,8},{8,0},{16,24},{24,16},{1,9},{9,1},{17,25},{25,17},{2,10},{10... | collective-permute-start | bytes 78920 | tf_op jit(solution)/shard_map/ppermute | solution.py:519
  61.3 4.8 %collective-permute-start.24 = (bf16[32,411]{1,0:T(8,128)(2,1)S(1)}, bf16[32,411]{1,0:T(8,128)(2,1)S(1)}, u32[]{:S(2)}, u32[]{:S(2)}) collective-permute-start(bf16[32,411]{1,0:T(8,128)(2,1)S(1)} %get-tuple-element.44), channel_id=1, source_target_pairs={{0,16},{8,24},{16,0},{24,8},{1,17},{9,25},{17,1},{25,9},{2,18},{10... | collective-permute-start | bytes 78920 | tf_op jit(solution)/shard_map/ppermute | solution.py:519
  61.8 5.7 %collective-permute-start.25 = (bf16[32,411]{1,0:T(8,128)(2,1)S(1)}, bf16[32,411]{1,0:T(8,128)(2,1)S(1)}, u32[]{:S(2)}, u32[]{:S(2)}) collective-permute-start(bf16[32,411]{1,0:T(8,128)(2,1)S(1)} %get-tuple-element.45), channel_id=1, source_target_pairs={{0,24},{8,16},{16,8},{24,0},{1,25},{9,17},{17,9},{25,1},{2,26},{10... | collective-permute-start | bytes 78920 | tf_op jit(solution)/shard_map/ppermute | solution.py:519

commit v15 on v14

--- a/solution.py
+++ b/solution.py
@@ -668,13 +668,13 @@
         [shape((p.patch, p.features), half)] * p.chips,
         partial,
     )
-    partial = [partial[0]] + [flip(partial[k], k * p.group) for k in range(1, p.chips)]
+    partial = [flip(partial[k], k * p.group) for k in range(p.chips - 1, 0, -1)] + [partial[0]]
     partial = call(
         functools.partial(add_chips_kernel, p),
         [shape((p.room, p.features), half)] * p.tiles,
         partial,
     )
-    partial = [partial[0]] + [trade(partial[k], k) for k in range(1, p.tiles)]
+    partial = [trade(partial[k], k) for k in range(p.tiles - 1, 0, -1)] + [partial[0]]
     edge = 8
     kappa = kappa.reshape(3, reach, p.lane)
     root = jnp.sqrt(

time: 69 us -> 68.2 us (0.988)
  waiting for transfers between devices: 28.8 us -> 27.9 us
    ppermute x13, waiting for transfers between devices: 12.4 us -> 11.5 us  [flip(): return lax.ppermute(value, 'chan', [(b, b ^ mask) for b in range(p.chans)])]
where the time goes in v15:
time: 68.2 us; the launch traced here: 68.1 us
  starting transfers between devices  28.1 us (41%)
  waiting for transfers between devices  27.9 us (41%)
  Pallas kernels  11.2 us (16%)
    ppermute x13, starting transfers between devices, flip(): return lax.ppermute(value, 'chan', [(b, b ^ mask) for b in range(p.chans)])  11.8 us
    ppermute x13, waiting for transfers between devices, flip(): return lax.ppermute(value, 'chan', [(b, b ^ mask) for b in range(p.chans)])  11.5 us
    pallas_call x17, Pallas kernels, call(): pl.pallas_call(kernel, out_shape=out_shape, in_specs=[far if k in in_hbm...  11.2 us
    ppermute x6, starting transfers between devices, trade(): return lax.ppermute(value, 'tile', [(a, a ^ mask) for a in range(p.tiles)])  10.3 us
    ppermute x7, waiting for transfers between devices, send(): lax.ppermute(value, both, sorted(((number(a), number(b)) for a, b in pair...  8.55 us
    ppermute x6, waiting for transfers between devices, trade(): return lax.ppermute(value, 'tile', [(a, a ^ mask) for a in range(p.tiles)])  7.85 us
    ppermute x7, starting transfers between devices, send(): lax.ppermute(value, both, sorted(((number(a), number(b)) for a, b in pair...  5.98 us
  transfers between devices with their start and end apart: 26, of which 17 were waited for; matrix products, arithmetic and copies ran while one was open for 0% of the time, Pallas kernels for 8%

profile of v15, /device:TPU:0, one launch (start us, length us, event | category | flops | bytes accessed | tf_op | source)
XLA Modules:
  0.0 68.1 jit_solution(7775229287447555165)
XLA Ops:
  0.0 3.1 %collective-permute-start.1 = (bf16[128,768]{1,0:T(8,128)(2,1)}, bf16[128,768]{1,0:T(8,128)(2,1)S(1)}, u32[]{:S(2)}, u32[]{:S(2)}) collective-permute-start(bf16[128,768]{1,0:T(8,128)(2,1)} %refs_0_.3), channel_id=1, source_target_pairs={{0,8},{8,0},{16,24},{24,16},{1,9},{9,1},{17,25},{25,17},{2,10},{10... | collective-permute-start | bytes 589832 | tf_op jit(solution)/shard_map/ppermute | solution.py:519
  3.1 1.5 %collective-permute-start.8 = (bf16[411,256]{1,0:T(8,128)(2,1)}, bf16[411,256]{1,0:T(8,128)(2,1)S(1)}, u32[]{:S(2)}, u32[]{:S(2)}) collective-permute-start(bf16[411,256]{1,0:T(8,128)(2,1)} %refs_0_.4), channel_id=1, source_target_pairs={{0,4},{1,5},{2,6},{3,7},{4,0},{5,1},{6,2},{7,3},{8,12},{9,13},{10,... | collective-permute-start | bytes 631304 | tf_op jit(solution)/shard_map/ppermute | solution.py:516
  4.6 1.5 %collective-permute-start.7 = (bf16[411,256]{1,0:T(8,128)(2,1)}, bf16[411,256]{1,0:T(8,128)(2,1)S(1)}, u32[]{:S(2)}, u32[]{:S(2)}) collective-permute-start(bf16[411,256]{1,0:T(8,128)(2,1)} %refs_0_.4), channel_id=1, source_target_pairs={{0,2},{1,3},{2,0},{3,1},{4,6},{5,7},{6,4},{7,5},{8,10},{9,11},{10,... | collective-permute-start | bytes 631304 | tf_op jit(solution)/shard_map/ppermute | solution.py:516
  6.1 0.5 collective-permute-start.9
  6.6 0.5 shard_map.101
  7.2 0.0 copy-start.9
  7.2 0.2 shard_map.102.refs_0_
  7.4 0.1 collective-permute-start
  7.5 0.8 %collective-permute-done.1.refs_1_ = bf16[128,768]{1,0:T(8,128)(2,1)S(1)} collective-permute-done((bf16[128,768]{1,0:T(8,128)(2,1)}, bf16[128,768]{1,0:T(8,128)(2,1)S(1)}, u32[]{:S(2)}, u32[]{:S(2)}) %collective-permute-start.1) | collective-permute-done | bytes 196640 | tf_op jit(solution)/shard_map/ppermute | solution.py:519
  8.2 0.5 shard_map.103.refs_2_.refs_0_
  8.8 2.4 %collective-permute-done.refs_1_ = bf16[16,512]{1,0:T(8,128)(2,1)S(1)} collective-permute-done((bf16[16,512]{1,0:T(8,128)(2,1)S(1)}, bf16[16,512]{1,0:T(8,128)(2,1)S(1)}, u32[]{:S(2)}, u32[]{:S(2)}) %collective-permute-start) | collective-permute-done | bytes 16416 | tf_op jit(solution)/shard_map/ppermute | solution.py:519
  11.2 2.7 %collective-permute-start.2 = (bf16[32,512]{1,0:T(8,128)(2,1)S(1)}, bf16[32,512]{1,0:T(8,128)(2,1)S(1)}, u32[]{:S(2)}, u32[]{:S(2)}) collective-permute-start(bf16[32,512]{1,0:T(8,128)(2,1)S(1)} %shard_map.104.refs_0_), channel_id=1, source_target_pairs={{0,16},{8,24},{16,0},{24,8},{1,17},{9,25},{17,1},{25,9},{2,18},{10... | collective-permute-start | bytes 98312 | tf_op jit(solution)/shard_map/ppermute | solution.py:519
  13.9 2.2 %collective-permute-done.2.refs_1_ = bf16[32,512]{1,0:T(8,128)(2,1)S(1)} collective-permute-done((bf16[32,512]{1,0:T(8,128)(2,1)S(1)}, bf16[32,512]{1,0:T(8,128)(2,1)S(1)}, u32[]{:S(2)}, u32[]{:S(2)}) %collective-permute-start.2) | collective-permute-done | bytes 32800 | tf_op jit(solution)/shard_map/ppermute | solution.py:519
  16.1 0.1 shard_map.105.refs_0_.refs_4_
  16.2 0.1 shard_map.107.refs_7_.refs_5_
  16.2 0.1 collective-permute-start.10
  16.3 2.7 %collective-permute-start.11 = (bf16[256,768]{1,0:T(8,128)(2,1)S(1)}, bf16[256,768]{1,0:T(8,128)(2,1)S(1)}, u32[]{:S(2)}, u32[]{:S(2)}) collective-permute-start(bf16[256,768]{1,0:T(8,128)(2,1)S(1)} %shard_map.103.refs_2_.refs_0_), channel_id=1, source_target_pairs={{0,16},{1,17},{2,3},{3,2},{4,20},{5,21},{6,7},{7,6},{8,9},{9,8},{1... | collective-permute-start | bytes 1179656 | tf_op jit(solution)/shard_map/ppermute | solution.py:528
  19.0 0.5 collective-permute-start.5
  19.5 1.1 %collective-permute-start.4 = (bf16[64,512]{1,0:T(8,128)(2,1)S(1)}, bf16[64,512]{1,0:T(8,128)(2,1)S(1)}, u32[]{:S(2)}, u32[]{:S(2)}) collective-permute-start(bf16[64,512]{1,0:T(8,128)(2,1)S(1)} %shard_map.105.refs_0_.refs_4_), channel_id=1, source_target_pairs={{0,4},{1,5},{2,6},{3,7},{4,0},{5,1},{6,2},{7,3},{8,12},{9,13},{10,... | collective-permute-start | bytes 196616 | tf_op jit(solution)/shard_map/ppermute | solution.py:516
  20.6 1.9 %collective-permute-start.3 = (bf16[64,512]{1,0:T(8,128)(2,1)S(1)}, bf16[64,512]{1,0:T(8,128)(2,1)S(1)}, u32[]{:S(2)}, u32[]{:S(2)}) collective-permute-start(bf16[64,512]{1,0:T(8,128)(2,1)S(1)} %shard_map.105.refs_0_.refs_4_), channel_id=1, source_target_pairs={{0,2},{1,3},{2,0},{3,1},{4,6},{5,7},{6,4},{7,5},{8,10},{9,11},{10,... | collective-permute-start | bytes 196616 | tf_op jit(solution)/shard_map/ppermute | solution.py:516
  22.5 2.0 %collective-permute-done.5.refs_3_ = bf16[64,512]{1,0:T(8,128)(2,1)S(1)} collective-permute-done((bf16[64,512]{1,0:T(8,128)(2,1)S(1)}, bf16[64,512]{1,0:T(8,128)(2,1)S(1)}, u32[]{:S(2)}, u32[]{:S(2)}) %collective-permute-start.5) | collective-permute-done | bytes 65568 | tf_op jit(solution)/shard_map/ppermute | solution.py:516
  24.5 0.3 collective-permute-done.4.refs_2_
  24.8 0.8 %collective-permute-done.3.refs_1_ = bf16[64,512]{1,0:T(8,128)(2,1)S(1)} collective-permute-done((bf16[64,512]{1,0:T(8,128)(2,1)S(1)}, bf16[64,512]{1,0:T(8,128)(2,1)S(1)}, u32[]{:S(2)}, u32[]{:S(2)}) %collective-permute-start.3) | collective-permute-done | bytes 65568 | tf_op jit(solution)/shard_map/ppermute | solution.py:516
  25.6 0.3 shard_map.106.refs_5_
  25.9 0.1 collective-permute-start.6
  26.0 0.0 copy-start
  26.1 0.0 copy-start.5
  26.1 0.4 shard_map.100
  26.4 1.1 %collective-permute-done.6.refs_6_ = bf16[256,512]{1,0:T(8,128)(2,1)S(1)} collective-permute-done((bf16[256,512]{1,0:T(8,128)(2,1)S(1)}, bf16[256,512]{1,0:T(8,128)(2,1)S(1)}, u32[]{:S(2)}, u32[]{:S(2)}) %collective-permute-start.6) | collective-permute-done | bytes 262176 | tf_op jit(solution)/shard_map/ppermute | solution.py:516
  27.6 0.4 copy-done
  27.9 2.3 %shard_map.108 = (f32[256,768]{1,0:T(8,128)S(1)}, f32[256,1]{1,0:T(8,128)S(1)}, f32[8,256,256]{2,1,0:T(8,128)S(1)}, f32[24,128]{1,0:T(8,128)S(1)}) custom-call(s32[256,1]{1,0:T(8,128)S(1)} %get-tuple-element.26.refs_0_.place_ref, s32[256,1]{1,0:T(8,128)S(1)} %get-tuple-element.27.refs_1_, s32[24,1]{1,0:T(8,128)S(1)} %get-tuple-element.28.after_ref.refs_2_, ...), custom_call_target="tpu_custom_call" | custom-call | flops 100000000 | bytes 5379168 | tf_op jit(solution)/shard_map/pallas_call | solution.py:164
  30.3 0.4 shard_map.110
  30.7 1.3 %collective-permute-start.12 = (bf16[128,768]{1,0:T(8,128)(2,1)S(1)}, bf16[128,768]{1,0:T(8,128)(2,1)S(1)}, u32[]{:S(2)}, u32[]{:S(2)}) collective-permute-start(bf16[128,768]{1,0:T(8,128)(2,1)S(1)} %get-tuple-element.32.refs_0_), channel_id=1, source_target_pairs={{0,2},{1,3},{2,0},{3,1},{4,5},{5,4},{6,7},{7,6},{8,10},{9,11},{10,... | collective-permute-start | bytes 589832 | tf_op jit(solution)/shard_map/ppermute | solution.py:528
  32.0 0.1 collective-permute-start.13
  32.0 1.9 %collective-permute-start.14 = (bf16[128,768]{1,0:T(8,128)(2,1)S(1)}, bf16[128,768]{1,0:T(8,128)(2,1)S(1)}, u32[]{:S(2)}, u32[]{:S(2)}) collective-permute-start(bf16[128,768]{1,0:T(8,128)(2,1)S(1)} %get-tuple-element.32.refs_0_), channel_id=1, source_target_pairs={{0,4},{1,5},{2,3},{3,2},{4,0},{5,1},{6,7},{7,6},{8,9},{9,8},{10,14... | collective-permute-start | bytes 589832 | tf_op jit(solution)/shard_map/ppermute | solution.py:528
  34.0 4.5 %collective-permute-done.12.refs_2_ = bf16[128,768]{1,0:T(8,128)(2,1)S(1)} collective-permute-done((bf16[128,768]{1,0:T(8,128)(2,1)S(1)}, bf16[128,768]{1,0:T(8,128)(2,1)S(1)}, u32[]{:S(2)}, u32[]{:S(2)}) %collective-permute-start.12) | collective-permute-done | bytes 196640 | tf_op jit(solution)/shard_map/ppermute | solution.py:528
  38.5 1.2 %collective-permute-done.13.refs_3_ = bf16[128,768]{1,0:T(8,128)(2,1)S(1)} collective-permute-done((bf16[128,768]{1,0:T(8,128)(2,1)S(1)}, bf16[128,768]{1,0:T(8,128)(2,1)S(1)}, u32[]{:S(2)}, u32[]{:S(2)}) %collective-permute-start.13) | collective-permute-done | bytes 196640 | tf_op jit(solution)/shard_map/ppermute | solution.py:528
  39.7 0.6 shard_map.109.refs_8_.refs_2_
  40.3 0.0 copy-start.1
  40.3 2.8 %collective-permute-done.14.refs_4_ = bf16[128,768]{1,0:T(8,128)(2,1)S(1)} collective-permute-done((bf16[128,768]{1,0:T(8,128)(2,1)S(1)}, bf16[128,768]{1,0:T(8,128)(2,1)S(1)}, u32[]{:S(2)}, u32[]{:S(2)}) %collective-permute-start.14) | collective-permute-done | bytes 196640 | tf_op jit(solution)/shard_map/ppermute | solution.py:528
  43.2 0.6 shard_map.111.depart_ref
  43.8 0.1 collective-permute-start.18
  43.8 0.5 shard_map.112.refs_3_
  44.3 1.2 %collective-permute-done.18.refs_4_ = bf16[256,768]{1,0:T(8,128)(2,1)S(1)} collective-permute-done((bf16[256,768]{1,0:T(8,128)(2,1)S(1)}, bf16[256,768]{1,0:T(8,128)(2,1)S(1)}, u32[]{:S(2)}, u32[]{:S(2)}) %collective-permute-start.18) | collective-permute-done | bytes 393248 | tf_op jit(solution)/shard_map/ppermute | solution.py:516
  45.5 3.0 %shard_map.113 = (bf16[384,411]{1,0:T(8,128)(2,1)S(1)}, bf16[384,411]{1,0:T(8,128)(2,1)S(1)}) custom-call(bf16[2048,768]{1,0:T(8,128)(2,1)S(1)} %copy-done, bf16[1536,768]{1,0:T(8,128)(2,1)S(1)} %copy-done.1, f32[8,256,256]{2,1,0:T(8,128)S(1)} %shard_map.109.refs_8_.refs_2_, f32[256,768]{1,0:T(8,128)S(1)} %shard_map.112.refs_3_, ...), custom_call_target="tpu_custom_call" | custom-call | flops 1840250880 | bytes 10488832 | tf_op jit(solution)/shard_map/pallas_call | solution.py:164
  48.5 0.2 collective-permute-start.19
  48.7 0.1 slice_bitcast_fusion.2
  48.8 1.5 %collective-permute-done.19.refs_1_ = bf16[384,411]{1,0:T(8,128)(2,1)S(1)} collective-permute-done((bf16[384,411]{1,0:T(8,128)(2,1)S(1)}, bf16[384,411]{1,0:T(8,128)(2,1)S(1)}, u32[]{:S(2)}, u32[]{:S(2)}) %collective-permute-start.19) | collective-permute-done | bytes 315680 | tf_op jit(solution)/shard_map/ppermute | solution.py:516
  50.3 0.1 shard_map.114
  50.4 3.7 %collective-permute-start.20 = (bf16[96,411]{1,0:T(8,128)(2,1)S(1)}, bf16[96,411]{1,0:T(8,128)(2,1)S(1)}, u32[]{:S(2)}, u32[]{:S(2)}) collective-permute-start(bf16[96,411]{1,0:T(8,128)(2,1)S(1)} %get-tuple-element.38), channel_id=1, source_target_pairs={{0,6},{1,7},{2,4},{3,5},{4,2},{5,3},{6,0},{7,1},{8,14},{9,15},{10,... | collective-permute-start | bytes 236744 | tf_op jit(solution)/shard_map/ppermute | solution.py:516
  54.1 0.3 collective-permute-start.21
  54.4 0.3 collective-permute-start.22
  54.8 2.6 %collective-permute-done.20.refs_0_ = bf16[96,411]{1,0:T(8,128)(2,1)S(1)} collective-permute-done((bf16[96,411]{1,0:T(8,128)(2,1)S(1)}, bf16[96,411]{1,0:T(8,128)(2,1)S(1)}, u32[]{:S(2)}, u32[]{:S(2)}) %collective-permute-start.20) | collective-permute-done | bytes 78944 | tf_op jit(solution)/shard_map/ppermute | solution.py:516
  57.3 2.0 %collective-permute-done.21.refs_1_ = bf16[96,411]{1,0:T(8,128)(2,1)S(1)} collective-permute-done((bf16[96,411]{1,0:T(8,128)(2,1)S(1)}, bf16[96,411]{1,0:T(8,128)(2,1)S(1)}, u32[]{:S(2)}, u32[]{:S(2)}) %collective-permute-start.21) | collective-permute-done | bytes 78944 | tf_op jit(solution)/shard_map/ppermute | solution.py:516
  59.3 0.2 shard_map.115
  59.6 1.6 %collective-permute-start.23 = (bf16[32,411]{1,0:T(8,128)(2,1)S(1)}, bf16[32,411]{1,0:T(8,128)(2,1)S(1)}, u32[]{:S(2)}, u32[]{:S(2)}) collective-permute-start(bf16[32,411]{1,0:T(8,128)(2,1)S(1)} %get-tuple-element.42), channel_id=1, source_target_pairs={{0,24},{8,16},{16,8},{24,0},{1,25},{9,17},{17,9},{25,1},{2,26},{10... | collective-permute-start | bytes 78920 | tf_op jit(solution)/shard_map/ppermute | solution.py:519
  61.2 1.6 %collective-permute-start.24 = (bf16[32,411]{1,0:T(8,128)(2,1)S(1)}, bf16[32,411]{1,0:T(8,128)(2,1)S(1)}, u32[]{:S(2)}, u32[]{:S(2)}) collective-permute-start(bf16[32,411]{1,0:T(8,128)(2,1)S(1)} %get-tuple-element.43), channel_id=1, source_target_pairs={{0,16},{8,24},{16,0},{24,8},{1,17},{9,25},{17,1},{25,9},{2,18},{10... | collective-permute-start | bytes 78920 | tf_op jit(solution)/shard_map/ppermute | solution.py:519
  62.8 1.2 %collective-permute-start.25 = (bf16[32,411]{1,0:T(8,128)(2,1)S(1)}, bf16[32,411]{1,0:T(8,128)(2,1)S(1)}, u32[]{:S(2)}, u32[]{:S(2)}) collective-permute-start(bf16[32,411]{1,0:T(8,128)(2,1)S(1)} %get-tuple-element.44), channel_id=1, source_target_pairs={{0,8},{8,0},{16,24},{24,16},{1,9},{9,1},{17,25},{25,17},{2,10},{10... | collective-permute-start | bytes 78920 | tf_op jit(solution)/shard_map/ppermute | solution.py:519
  64.0 0.1 maximum_sqrt_fusion
  64.1 0.1 copy.19
  64.2 1.3 %collective-permute-done.23.refs_0_ = bf16[32,411]{1,0:T(8,128)(2,1)S(1)} collective-permute-done((bf16[32,411]{1,0:T(8,128)(2,1)S(1)}, bf16[32,411]{1,0:T(8,128)(2,1)S(1)}, u32[]{:S(2)}, u32[]{:S(2)}) %collective-permute-start.23) | collective-permute-done | bytes 26336 | tf_op jit(solution)/shard_map/ppermute | solution.py:519
  65.5 0.9 %collective-permute-done.24.refs_1_ = bf16[32,411]{1,0:T(8,128)(2,1)S(1)} collective-permute-done((bf16[32,411]{1,0:T(8,128)(2,1)S(1)}, bf16[32,411]{1,0:T(8,128)(2,1)S(1)}, u32[]{:S(2)}, u32[]{:S(2)}) %collective-permute-start.24) | collective-permute-done | bytes 26336 | tf_op jit(solution)/shard_map/ppermute | solution.py:519
  66.3 0.4 collective-permute-done.25.refs_2_
  66.7 1.4 %shard_map.116 = f32[4,32,411]{2,1,0:T(8,128)} custom-call(bf16[32,411]{1,0:T(8,128)(2,1)S(1)} %collective-permute-done.23.refs_0_, bf16[32,411]{1,0:T(8,128)(2,1)S(1)} %collective-permute-done.24.refs_1_, bf16[32,411]{1,0:T(8,128)(2,1)S(1)} %collective-permute-done.25.refs_2_, bf16[32,411]{1,0:T(8,128)(2,1)S(1)} %get-tuple-element.45.refs_3_, ...), custom_call_target="tpu_custom_call" | custom-call | flops 5260800 | bytes 106752 | tf_op jit(solution)/shard_map/pallas_call | solution.py:164
  (29 shorter events, 0.1 us)
Async XLA Ops:
  0.0 8.2 %copy-start.4 = (bf16[128,768]{1,0:T(8,128)(2,1)S(1)}, bf16[128,768]{1,0:T(8,128)(2,1)}, u32[]{:S(2)}) copy-start(bf16[128,768]{1,0:T(8,128)(2,1)} %refs_0_.3) | copy-start | bytes 589828
  0.0 16.2 %copy-start.3 = (bf16[411,256]{1,0:T(8,128)(2,1)S(1)}, bf16[411,256]{1,0:T(8,128)(2,1)}, u32[]{:S(2)}) copy-start(bf16[411,256]{1,0:T(8,128)(2,1)} %refs_0_.4) | copy-start | bytes 631300
  0.0 7.2 %copy-start.7 = (f32[256]{0:T(256)S(1)}, f32[256]{0:T(256)}, u32[]{:S(2)}) copy-start(f32[256]{0:T(256)} %bias_ref.1) | copy-start | bytes 3076
  0.0 7.2 %copy-start.8 = (s32[128]{0:T(128)S(1)}, s32[128]{0:T(128)}, u32[]{:S(2)}) copy-start(s32[128]{0:T(128)} %usable_ref.1) | copy-start | bytes 1540
  0.0 7.2 %copy-start.6 = (f32[4,32]{1,0:T(4,128)S(1)}, f32[4,32]{1,0:T(4,128)}, u32[]{:S(2)}) copy-start(f32[4,32]{1,0:T(4,128)} %diffusivity_ref.1) | copy-start | bytes 1540
  0.0 7.2 %copy-start.2 = (f32[4,32,411]{2,1,0:T(8,128)S(1)}, f32[4,32,411]{2,1,0:T(8,128)}, u32[]{:S(2)}) copy-start(f32[4,32,411]{2,1,0:T(8,128)} %fields_ref.1) | copy-start | bytes 631300
  0.0 8.2 %collective-permute-start.1 = (bf16[128,768]{1,0:T(8,128)(2,1)}, bf16[128,768]{1,0:T(8,128)(2,1)S(1)}, u32[]{:S(2)}, u32[]{:S(2)}) collective-permute-start(bf16[128,768]{1,0:T(8,128)(2,1)} %refs_0_.3), channel_id=1, source_target_pairs={{0,8},{8,0},{16,24},{24,16},{1,9},{9,1},{17,25},{25,17},{2,10},{10... | collective-permute-start | bytes 589832 | tf_op jit(solution)/shard_map/ppermute | solution.py:519
  3.1 13.0 %collective-permute-start.8 = (bf16[411,256]{1,0:T(8,128)(2,1)}, bf16[411,256]{1,0:T(8,128)(2,1)S(1)}, u32[]{:S(2)}, u32[]{:S(2)}) collective-permute-start(bf16[411,256]{1,0:T(8,128)(2,1)} %refs_0_.4), channel_id=1, source_target_pairs={{0,4},{1,5},{2,6},{3,7},{4,0},{5,1},{6,2},{7,3},{8,12},{9,13},{10,... | collective-permute-start | bytes 631304 | tf_op jit(solution)/shard_map/ppermute | solution.py:516
  4.6 11.5 %collective-permute-start.7 = (bf16[411,256]{1,0:T(8,128)(2,1)}, bf16[411,256]{1,0:T(8,128)(2,1)S(1)}, u32[]{:S(2)}, u32[]{:S(2)}) collective-permute-start(bf16[411,256]{1,0:T(8,128)(2,1)} %refs_0_.4), channel_id=1, source_target_pairs={{0,2},{1,3},{2,0},{3,1},{4,6},{5,7},{6,4},{7,5},{8,10},{9,11},{10,... | collective-permute-start | bytes 631304 | tf_op jit(solution)/shard_map/ppermute | solution.py:516
  6.1 10.0 %collective-permute-start.9 = (bf16[411,256]{1,0:T(8,128)(2,1)}, bf16[411,256]{1,0:T(8,128)(2,1)S(1)}, u32[]{:S(2)}, u32[]{:S(2)}) collective-permute-start(bf16[411,256]{1,0:T(8,128)(2,1)} %refs_0_.4), channel_id=1, source_target_pairs={{0,6},{1,7},{2,4},{3,5},{4,2},{5,3},{6,0},{7,1},{8,14},{9,15},{10,... | collective-permute-start | bytes 631304 | tf_op jit(solution)/shard_map/ppermute | solution.py:516
  7.2 18.9 %copy-start.9 = (s32[256,1]{0,1:T(1,128)S(1)}, s32[256,1]{0,1:T(1,128)}, u32[]{:S(2)}) copy-start(s32[256,1]{0,1:T(1,128)} %param.12) | copy-start | bytes 3076
  7.4 3.7 %collective-permute-start = (bf16[16,512]{1,0:T(8,128)(2,1)S(1)}, bf16[16,512]{1,0:T(8,128)(2,1)S(1)}, u32[]{:S(2)}, u32[]{:S(2)}) collective-permute-start(bf16[16,512]{1,0:T(8,128)(2,1)S(1)} %shard_map.102.refs_0_), channel_id=1, source_target_pairs={{0,8},{8,0},{16,24},{24,16},{1,9},{9,1},{17,25},{25,17},{2,10},{10... | collective-permute-start | bytes 49160 | tf_op jit(solution)/shard_map/ppermute | solution.py:519
  11.2 4.9 %collective-permute-start.2 = (bf16[32,512]{1,0:T(8,128)(2,1)S(1)}, bf16[32,512]{1,0:T(8,128)(2,1)S(1)}, u32[]{:S(2)}, u32[]{:S(2)}) collective-permute-start(bf16[32,512]{1,0:T(8,128)(2,1)S(1)} %shard_map.104.refs_0_), channel_id=1, source_target_pairs={{0,16},{8,24},{16,0},{24,8},{1,17},{9,25},{17,1},{25,9},{2,18},{10... | collective-permute-start | bytes 98312 | tf_op jit(solution)/shard_map/ppermute | solution.py:519
  16.2 11.3 %collective-permute-start.10 = (bf16[1664,256]{1,0:T(8,128)(2,1)S(1)}, bf16[1664,256]{1,0:T(8,128)(2,1)S(1)}, u32[]{:S(2)}, u32[]{:S(2)}) collective-permute-start(bf16[1664,256]{1,0:T(8,128)(2,1)S(1)} %shard_map.107.refs_7_.refs_5_), channel_id=1, source_target_pairs={{0,1},{1,0},{2,3},{3,2},{4,5},{5,4},{6,7},{7,6},{8,9},{9,8},{10,11... | collective-permute-start | bytes 2555912 | tf_op jit(solution)/shard_map/ppermute | solution.py:516
  16.3 13.9 %collective-permute-start.11 = (bf16[256,768]{1,0:T(8,128)(2,1)S(1)}, bf16[256,768]{1,0:T(8,128)(2,1)S(1)}, u32[]{:S(2)}, u32[]{:S(2)}) collective-permute-start(bf16[256,768]{1,0:T(8,128)(2,1)S(1)} %shard_map.103.refs_2_.refs_0_), channel_id=1, source_target_pairs={{0,16},{1,17},{2,3},{3,2},{4,20},{5,21},{6,7},{7,6},{8,9},{9,8},{1... | collective-permute-start | bytes 1179656 | tf_op jit(solution)/shard_map/ppermute | solution.py:528
  19.0 5.4 %collective-permute-start.5 = (bf16[64,512]{1,0:T(8,128)(2,1)S(1)}, bf16[64,512]{1,0:T(8,128)(2,1)S(1)}, u32[]{:S(2)}, u32[]{:S(2)}) collective-permute-start(bf16[64,512]{1,0:T(8,128)(2,1)S(1)} %shard_map.105.refs_0_.refs_4_), channel_id=1, source_target_pairs={{0,6},{1,7},{2,4},{3,5},{4,2},{5,3},{6,0},{7,1},{8,14},{9,15},{10,... | collective-permute-start | bytes 196616 | tf_op jit(solution)/shard_map/ppermute | solution.py:516
  19.5 5.3 %collective-permute-start.4 = (bf16[64,512]{1,0:T(8,128)(2,1)S(1)}, bf16[64,512]{1,0:T(8,128)(2,1)S(1)}, u32[]{:S(2)}, u32[]{:S(2)}) collective-permute-start(bf16[64,512]{1,0:T(8,128)(2,1)S(1)} %shard_map.105.refs_0_.refs_4_), channel_id=1, source_target_pairs={{0,4},{1,5},{2,6},{3,7},{4,0},{5,1},{6,2},{7,3},{8,12},{9,13},{10,... | collective-permute-start | bytes 196616 | tf_op jit(solution)/shard_map/ppermute | solution.py:516
  20.6 5.0 %collective-permute-start.3 = (bf16[64,512]{1,0:T(8,128)(2,1)S(1)}, bf16[64,512]{1,0:T(8,128)(2,1)S(1)}, u32[]{:S(2)}, u32[]{:S(2)}) collective-permute-start(bf16[64,512]{1,0:T(8,128)(2,1)S(1)} %shard_map.105.refs_0_.refs_4_), channel_id=1, source_target_pairs={{0,2},{1,3},{2,0},{3,1},{4,6},{5,7},{6,4},{7,5},{8,10},{9,11},{10,... | collective-permute-start | bytes 196616 | tf_op jit(solution)/shard_map/ppermute | solution.py:516
  25.9 1.6 %collective-permute-start.6 = (bf16[256,512]{1,0:T(8,128)(2,1)S(1)}, bf16[256,512]{1,0:T(8,128)(2,1)S(1)}, u32[]{:S(2)}, u32[]{:S(2)}) collective-permute-start(bf16[256,512]{1,0:T(8,128)(2,1)S(1)} %shard_map.106.refs_5_), channel_id=1, source_target_pairs={{0,1},{1,0},{2,3},{3,2},{4,5},{5,4},{6,7},{7,6},{8,9},{9,8},{10,11... | collective-permute-start | bytes 786440 | tf_op jit(solution)/shard_map/ppermute | solution.py:516
  26.0 1.9 %copy-start = (bf16[2048,768]{1,0:T(8,128)(2,1)S(1)}, bf16[2048,768]{1,0:T(8,128)(2,1)}, u32[]{:S(2)}) copy-start(bf16[2048,768]{1,0:T(8,128)(2,1)} %refs_0_.5) | copy-start | bytes 9437188
  26.1 1.9 %copy-start.5 = (f32[768]{0:T(1024)S(1)}, f32[768]{0:T(1024)}, u32[]{:S(2)}) copy-start(f32[768]{0:T(1024)} %refs_3_.1) | copy-start | bytes 9220
  30.7 7.8 %collective-permute-start.12 = (bf16[128,768]{1,0:T(8,128)(2,1)S(1)}, bf16[128,768]{1,0:T(8,128)(2,1)S(1)}, u32[]{:S(2)}, u32[]{:S(2)}) collective-permute-start(bf16[128,768]{1,0:T(8,128)(2,1)S(1)} %get-tuple-element.32.refs_0_), channel_id=1, source_target_pairs={{0,2},{1,3},{2,0},{3,1},{4,5},{5,4},{6,7},{7,6},{8,10},{9,11},{10,... | collective-permute-start | bytes 589832 | tf_op jit(solution)/shard_map/ppermute | solution.py:528
  32.0 7.7 %collective-permute-start.13 = (bf16[128,768]{1,0:T(8,128)(2,1)S(1)}, bf16[128,768]{1,0:T(8,128)(2,1)S(1)}, u32[]{:S(2)}, u32[]{:S(2)}) collective-permute-start(bf16[128,768]{1,0:T(8,128)(2,1)S(1)} %get-tuple-element.33.refs_1_), channel_id=1, source_target_pairs={{0,4},{1,5},{2,3},{3,2},{4,0},{5,1},{6,7},{7,6},{8,9},{9,8},{10,14... | collective-permute-start | bytes 589832 | tf_op jit(solution)/shard_map/ppermute | solution.py:528
  32.0 11.1 %collective-permute-start.14 = (bf16[128,768]{1,0:T(8,128)(2,1)S(1)}, bf16[128,768]{1,0:T(8,128)(2,1)S(1)}, u32[]{:S(2)}, u32[]{:S(2)}) collective-permute-start(bf16[128,768]{1,0:T(8,128)(2,1)S(1)} %get-tuple-element.32.refs_0_), channel_id=1, source_target_pairs={{0,4},{1,5},{2,3},{3,2},{4,0},{5,1},{6,7},{7,6},{8,9},{9,8},{10,14... | collective-permute-start | bytes 589832 | tf_op jit(solution)/shard_map/ppermute | solution.py:528
  34.0 9.2 %collective-permute-start.15 = (bf16[128,768]{1,0:T(8,128)(2,1)S(1)}, bf16[128,768]{1,0:T(8,128)(2,1)S(1)}, u32[]{:S(2)}, u32[]{:S(2)}) collective-permute-start(bf16[128,768]{1,0:T(8,128)(2,1)S(1)} %get-tuple-element.33.refs_1_), channel_id=1, source_target_pairs={{0,2},{1,3},{2,0},{3,1},{4,5},{5,4},{6,7},{7,6},{8,10},{9,11},{10,... | collective-permute-start | bytes 589832 | tf_op jit(solution)/shard_map/ppermute | solution.py:528
  38.5 4.7 %collective-permute-start.16 = (bf16[128,768]{1,0:T(8,128)(2,1)S(1)}, bf16[128,768]{1,0:T(8,128)(2,1)S(1)}, u32[]{:S(2)}, u32[]{:S(2)}) collective-permute-start(bf16[128,768]{1,0:T(8,128)(2,1)S(1)} %collective-permute-done.12.refs_2_), channel_id=1, source_target_pairs={{0,1},{1,0},{2,6},{3,7},{4,5},{5,4},{6,2},{7,3},{8,12},{9,13},{10,... | collective-permute-start | bytes 589832 | tf_op jit(solution)/shard_map/ppermute | solution.py:528
  39.7 3.5 %collective-permute-start.17 = (bf16[128,768]{1,0:T(8,128)(2,1)S(1)}, bf16[128,768]{1,0:T(8,128)(2,1)S(1)}, u32[]{:S(2)}, u32[]{:S(2)}) collective-permute-start(bf16[128,768]{1,0:T(8,128)(2,1)S(1)} %collective-permute-done.13.refs_3_), channel_id=1, source_target_pairs={{0,1},{1,0},{2,3},{3,2},{4,6},{5,7},{6,4},{7,5},{8,9},{9,8},{10,11... | collective-permute-start | bytes 589832 | tf_op jit(solution)/shard_map/ppermute | solution.py:528
  40.3 3.5 %copy-start.1 = (bf16[1536,768]{1,0:T(8,128)(2,1)S(1)}, bf16[1536,768]{1,0:T(8,128)(2,1)}, u32[]{:S(2)}) copy-start(bf16[1536,768]{1,0:T(8,128)(2,1)} %refs_1_.1) | copy-start | bytes 7077892
  43.8 1.8 %collective-permute-start.18 = (bf16[256,768]{1,0:T(8,128)(2,1)S(1)}, bf16[256,768]{1,0:T(8,128)(2,1)S(1)}, u32[]{:S(2)}, u32[]{:S(2)}) collective-permute-start(bf16[256,768]{1,0:T(8,128)(2,1)S(1)} %shard_map.111.depart_ref), channel_id=1, source_target_pairs={{0,1},{1,0},{2,3},{3,2},{4,5},{5,4},{6,7},{7,6},{8,9},{9,8},{10,11... | collective-permute-start | bytes 1179656 | tf_op jit(solution)/shard_map/ppermute | solution.py:516
  48.5 1.8 %collective-permute-start.19 = (bf16[384,411]{1,0:T(8,128)(2,1)S(1)}, bf16[384,411]{1,0:T(8,128)(2,1)S(1)}, u32[]{:S(2)}, u32[]{:S(2)}) collective-permute-start(bf16[384,411]{1,0:T(8,128)(2,1)S(1)} %get-tuple-element.37), channel_id=1, source_target_pairs={{0,1},{1,0},{2,3},{3,2},{4,5},{5,4},{6,7},{7,6},{8,9},{9,8},{10,11... | collective-permute-start | bytes 946952 | tf_op jit(solution)/shard_map/ppermute | solution.py:516
  50.4 6.9 %collective-permute-start.20 = (bf16[96,411]{1,0:T(8,128)(2,1)S(1)}, bf16[96,411]{1,0:T(8,128)(2,1)S(1)}, u32[]{:S(2)}, u32[]{:S(2)}) collective-permute-start(bf16[96,411]{1,0:T(8,128)(2,1)S(1)} %get-tuple-element.38), channel_id=1, source_target_pairs={{0,6},{1,7},{2,4},{3,5},{4,2},{5,3},{6,0},{7,1},{8,14},{9,15},{10,... | collective-permute-start | bytes 236744 | tf_op jit(solution)/shard_map/ppermute | solution.py:516
  54.1 5.2 %collective-permute-start.21 = (bf16[96,411]{1,0:T(8,128)(2,1)S(1)}, bf16[96,411]{1,0:T(8,128)(2,1)S(1)}, u32[]{:S(2)}, u32[]{:S(2)}) collective-permute-start(bf16[96,411]{1,0:T(8,128)(2,1)S(1)} %get-tuple-element.39), channel_id=1, source_target_pairs={{0,4},{1,5},{2,6},{3,7},{4,0},{5,1},{6,2},{7,3},{8,12},{9,13},{10,... | collective-permute-start | bytes 236744 | tf_op jit(solution)/shard_map/ppermute | solution.py:516
  54.4 4.9 %collective-permute-start.22 = (bf16[96,411]{1,0:T(8,128)(2,1)S(1)}, bf16[96,411]{1,0:T(8,128)(2,1)S(1)}, u32[]{:S(2)}, u32[]{:S(2)}) collective-permute-start(bf16[96,411]{1,0:T(8,128)(2,1)S(1)} %get-tuple-element.40), channel_id=1, source_target_pairs={{0,2},{1,3},{2,0},{3,1},{4,6},{5,7},{6,4},{7,5},{8,10},{9,11},{10,... | collective-permute-start | bytes 236744 | tf_op jit(solution)/shard_map/ppermute | solution.py:516
  59.6 5.9 %collective-permute-start.23 = (bf16[32,411]{1,0:T(8,128)(2,1)S(1)}, bf16[32,411]{1,0:T(8,128)(2,1)S(1)}, u32[]{:S(2)}, u32[]{:S(2)}) collective-permute-start(bf16[32,411]{1,0:T(8,128)(2,1)S(1)} %get-tuple-element.42), channel_id=1, source_target_pairs={{0,24},{8,16},{16,8},{24,0},{1,25},{9,17},{17,9},{25,1},{2,26},{10... | collective-permute-start | bytes 78920 | tf_op jit(solution)/shard_map/ppermute | solution.py:519
  61.2 5.1 %collective-permute-start.24 = (bf16[32,411]{1,0:T(8,128)(2,1)S(1)}, bf16[32,411]{1,0:T(8,128)(2,1)S(1)}, u32[]{:S(2)}, u32[]{:S(2)}) collective-permute-start(bf16[32,411]{1,0:T(8,128)(2,1)S(1)} %get-tuple-element.43), channel_id=1, source_target_pairs={{0,16},{8,24},{16,0},{24,8},{1,17},{9,25},{17,1},{25,9},{2,18},{10... | collective-permute-start | bytes 78920 | tf_op jit(solution)/shard_map/ppermute | solution.py:519
  62.8 3.9 %collective-permute-start.25 = (bf16[32,411]{1,0:T(8,128)(2,1)S(1)}, bf16[32,411]{1,0:T(8,128)(2,1)S(1)}, u32[]{:S(2)}, u32[]{:S(2)}) collective-permute-start(bf16[32,411]{1,0:T(8,128)(2,1)S(1)} %get-tuple-element.44), channel_id=1, source_target_pairs={{0,8},{8,0},{16,24},{24,16},{1,9},{9,1},{17,25},{25,17},{2,10},{10... | collective-permute-start | bytes 78920 | tf_op jit(solution)/shard_map/ppermute | solution.py:519

commit v16 on v15

--- a/solution.py
+++ b/solution.py
@@ -283,19 +283,10 @@
 
 
 def join_kernel(count, *refs):
-    ins, out_ref, sems = refs[:count], refs[-2], refs[-1]
+    ins, out_ref = refs[:count], refs[-1]
     size = out_ref.shape[0] // count
-    copies = [
-        pltpu.make_async_copy(
-            ref, out_ref.at[k] if ref.ndim < out_ref.ndim else out_ref.at[pl.ds(k * size, size)],
-            sems.at[k],
-        )
-        for k, ref in enumerate(ins)
-    ]
-    for copy in copies:
-        copy.start()
-    for copy in copies:
-        copy.wait()
+    for k, ref in enumerate(ins):
+        out_ref[k * size : (k + 1) * size, :] = ref[...]
 
 
 def stack_kernel(p, *refs):
@@ -374,23 +365,15 @@
 
 
 def choose_kernel(p, choices, *refs):
-    refs, out_ref, sems = refs[:-3], refs[-2], refs[-1]
+    refs, out_ref = refs[:-2], refs[-1]
     size = refs[0].shape[0]
     role = (lax.axis_index("chan") // p.group) ^ lax.axis_index("tile")
     for place in range(p.chips):
 
         @pl.when(role == place)
         def _():
-            copies = [
-                pltpu.make_async_copy(
-                    refs[choices[place, j]], out_ref.at[pl.ds(j * size, size)], sems.at[j]
-                )
-                for j in range(p.steps)
-            ]
-            for copy in copies:
-                copy.start()
-            for copy in copies:
-                copy.wait()
+            for j in range(p.steps):
+                out_ref[j * size : (j + 1) * size, :] = refs[choices[place, j]][...]
 
 
 def near_kernel(p, depart_ref, inv_cov_ref, out_ref):
@@ -402,7 +385,7 @@
     refs = list(refs)
     take = lambda n: [refs.pop(0) for _ in range(n)]
     w_radiance_ref, inv_cov_ref, slope_ref, near_ref = take(4)
-    depart_refs, weight_refs, target_refs = take(p.group - 1), take(p.group), take(p.group)
+    depart_refs, weight_refs, target_refs = take(p.group - 1), take(p.group), take(p.group - 1)
     out_refs = refs
     c = lax.axis_index("chan")
     cotangent = near_ref[...]
@@ -417,8 +400,14 @@
         grad_pre = (grad_hidden * slope_ref[k]).astype(jnp.bfloat16)
         total = total + dot(p.layer(weight_refs, k), grad_pre)
     total = total.astype(jnp.bfloat16)
-    for target_ref, out_ref in zip(target_refs, out_refs):
+    out_refs[0][...] = total
+    for target_ref, out_ref in zip(target_refs, out_refs[1:]):
         out_ref[...] = dot_nt(one_hot(target_ref[...], 0, p.rows), total).astype(jnp.bfloat16)
+
+
+def keep_kernel(total_ref, target_ref, out_ref):
+    pick = one_hot(target_ref[...], 0, total_ref.shape[1])
+    out_ref[...] = dot_nt(pick, total_ref[...]).astype(jnp.bfloat16)
 
 
 def add(refs, at=slice(None)):
@@ -534,10 +523,7 @@
             functools.partial(join_kernel, len(values)),
             shape(kernel_shape, half),
             [*values, *after],
-            in_hbm=range(len(values) + len(after)),
-            out_hbm=True,
-            scratch=[pltpu.SemaphoreType.DMA((len(values),))],
-            flops=0,
+            in_hbm=range(len(values), len(values) + len(after)),
         )
 
     def grow(value, over, after=()):
@@ -644,9 +630,7 @@
         functools.partial(choose_kernel, p, choices),
         shape((p.rows, p.shard), half),
         pool + [slope],
-        in_hbm=range(len(pool) + 1),
-        out_hbm=True,
-        scratch=[pltpu.SemaphoreType.DMA((p.steps,))],
+        in_hbm=[len(pool)],
     )
     depart = [flip(chosen, k) for k in range(1, p.group)]
 
@@ -658,11 +642,15 @@
     )
     partial = call(
         functools.partial(backward_kernel, p),
-        [shape((p.chips * p.patch, p.features), half)] * p.group,
-        [w_radiance, inv_cov, slope, partial] + depart + weights + targets,
+        [shape((p.features, p.rows), half)]
+        + [shape((p.chips * p.patch, p.features), half)] * (p.group - 1),
+        [w_radiance, inv_cov, slope, partial] + depart + weights + targets[1:],
         flops=2 * p.rows * (p.hidden * p.chans * (p.features + p.shard) + inv_cov.size),
     )
-    partial = [partial[0]] + [flip(partial[k], k) for k in range(1, p.group)]
+    kept = call(
+        keep_kernel, shape((p.chips * p.patch, p.features), half), [partial[0], targets[0]]
+    )
+    partial = [kept] + [flip(partial[k], k) for k in range(1, p.group)]
     partial = call(
         functools.partial(add_group_kernel, p),
         [shape((p.patch, p.features), half)] * p.chips,

time: 68.2 us -> 67.1 us (0.984)
  Pallas kernels: 11.2 us -> 9.91 us
    pallas_call x17 -> x18, Pallas kernels: 11.2 us -> 9.91 us  [call(): pl.pallas_call(kernel, out_shape=out_shape, in_specs=[far if k in in_hbm...]
  transfers between devices with their start and end apart: 26 -> 26, of which waited for: 17 -> 17; matrix products, arithmetic and copies ran while one was open for 0% -> 0% of each run, Pallas kernels for 8% -> 7%
where the time goes in v16:
time: 67.1 us; the launch traced here: 67 us
  waiting for transfers between devices  28.1 us (42%)
  starting transfers between devices  28 us (42%)
  Pallas kernels  9.91 us (15%)
    ppermute x13, starting transfers between devices, flip(): return lax.ppermute(value, 'chan', [(b, b ^ mask) for b in range(p.chans)])  11.8 us
    ppermute x13, waiting for transfers between devices, flip(): return lax.ppermute(value, 'chan', [(b, b ^ mask) for b in range(p.chans)])  11.1 us
    ppermute x6, starting transfers between devices, trade(): return lax.ppermute(value, 'tile', [(a, a ^ mask) for a in range(p.tiles)])  10.2 us
    pallas_call x18, Pallas kernels, call(): pl.pallas_call(kernel, out_shape=out_shape, in_specs=[far if k in in_hbm...  9.91 us
    ppermute x7, waiting for transfers between devices, send(): lax.ppermute(value, both, sorted(((number(a), number(b)) for a, b in pair...  8.57 us
    ppermute x6, waiting for transfers between devices, trade(): return lax.ppermute(value, 'tile', [(a, a ^ mask) for a in range(p.tiles)])  8.45 us
    ppermute x7, starting transfers between devices, send(): lax.ppermute(value, both, sorted(((number(a), number(b)) for a, b in pair...  5.99 us
  transfers between devices with their start and end apart: 26, of which 17 were waited for; matrix products, arithmetic and copies ran while one was open for 0% of the time, Pallas kernels for 7%

profile of v16, /device:TPU:0, one launch (start us, length us, event | category | flops | bytes accessed | tf_op | source)
XLA Modules:
  0.0 67.0 jit_solution(9184691040075166924)
XLA Ops:
  0.0 3.1 %collective-permute-start.1 = (bf16[128,768]{1,0:T(8,128)(2,1)}, bf16[128,768]{1,0:T(8,128)(2,1)S(1)}, u32[]{:S(2)}, u32[]{:S(2)}) collective-permute-start(bf16[128,768]{1,0:T(8,128)(2,1)} %refs_0_.3), channel_id=1, source_target_pairs={{0,8},{8,0},{16,24},{24,16},{1,9},{9,1},{17,25},{25,17},{2,10},{10... | collective-permute-start | bytes 589832 | tf_op jit(solution)/shard_map/ppermute | solution.py:508
  3.1 1.5 %collective-permute-start.8 = (bf16[411,256]{1,0:T(8,128)(2,1)}, bf16[411,256]{1,0:T(8,128)(2,1)S(1)}, u32[]{:S(2)}, u32[]{:S(2)}) collective-permute-start(bf16[411,256]{1,0:T(8,128)(2,1)} %refs_0_.4), channel_id=1, source_target_pairs={{0,4},{1,5},{2,6},{3,7},{4,0},{5,1},{6,2},{7,3},{8,12},{9,13},{10,... | collective-permute-start | bytes 631304 | tf_op jit(solution)/shard_map/ppermute | solution.py:505
  4.6 1.5 %collective-permute-start.7 = (bf16[411,256]{1,0:T(8,128)(2,1)}, bf16[411,256]{1,0:T(8,128)(2,1)S(1)}, u32[]{:S(2)}, u32[]{:S(2)}) collective-permute-start(bf16[411,256]{1,0:T(8,128)(2,1)} %refs_0_.4), channel_id=1, source_target_pairs={{0,2},{1,3},{2,0},{3,1},{4,6},{5,7},{6,4},{7,5},{8,10},{9,11},{10,... | collective-permute-start | bytes 631304 | tf_op jit(solution)/shard_map/ppermute | solution.py:505
  6.1 0.5 collective-permute-start.9
  6.6 0.5 shard_map.101
  7.2 0.0 copy-start.9
  7.2 0.2 shard_map.102.refs_0_
  7.4 0.1 collective-permute-start
  7.5 0.8 %collective-permute-done.1.refs_1_ = bf16[128,768]{1,0:T(8,128)(2,1)S(1)} collective-permute-done((bf16[128,768]{1,0:T(8,128)(2,1)}, bf16[128,768]{1,0:T(8,128)(2,1)S(1)}, u32[]{:S(2)}, u32[]{:S(2)}) %collective-permute-start.1) | collective-permute-done | bytes 196640 | tf_op jit(solution)/shard_map/ppermute | solution.py:508
  8.3 2.9 %collective-permute-done.refs_1_ = bf16[16,512]{1,0:T(8,128)(2,1)S(1)} collective-permute-done((bf16[16,512]{1,0:T(8,128)(2,1)S(1)}, bf16[16,512]{1,0:T(8,128)(2,1)S(1)}, u32[]{:S(2)}, u32[]{:S(2)}) %collective-permute-start) | collective-permute-done | bytes 16416 | tf_op jit(solution)/shard_map/ppermute | solution.py:508
  11.1 2.6 %collective-permute-start.2 = (bf16[32,512]{1,0:T(8,128)(2,1)S(1)}, bf16[32,512]{1,0:T(8,128)(2,1)S(1)}, u32[]{:S(2)}, u32[]{:S(2)}) collective-permute-start(bf16[32,512]{1,0:T(8,128)(2,1)S(1)} %shard_map.104.refs_0_), channel_id=1, source_target_pairs={{0,16},{8,24},{16,0},{24,8},{1,17},{9,25},{17,1},{25,9},{2,18},{10... | collective-permute-start | bytes 98312 | tf_op jit(solution)/shard_map/ppermute | solution.py:508
  13.7 2.2 %collective-permute-done.2.refs_1_ = bf16[32,512]{1,0:T(8,128)(2,1)S(1)} collective-permute-done((bf16[32,512]{1,0:T(8,128)(2,1)S(1)}, bf16[32,512]{1,0:T(8,128)(2,1)S(1)}, u32[]{:S(2)}, u32[]{:S(2)}) %collective-permute-start.2) | collective-permute-done | bytes 32800 | tf_op jit(solution)/shard_map/ppermute | solution.py:508
  16.0 0.0 collective-permute-done.8.refs_2_
  16.0 0.0 collective-permute-done.9.refs_3_
  16.0 0.1 shard_map.107.refs_7_.refs_5_
  16.1 0.1 collective-permute-start.10
  16.1 2.7 %collective-permute-start.11 = (bf16[256,768]{1,0:T(8,128)(2,1)S(1)}, bf16[256,768]{1,0:T(8,128)(2,1)S(1)}, u32[]{:S(2)}, u32[]{:S(2)}) collective-permute-start(bf16[256,768]{1,0:T(8,128)(2,1)S(1)} %shard_map.103.refs_2_.refs_0_), channel_id=1, source_target_pairs={{0,16},{1,17},{2,3},{3,2},{4,20},{5,21},{6,7},{7,6},{8,9},{9,8},{1... | collective-permute-start | bytes 1179656 | tf_op jit(solution)/shard_map/ppermute | solution.py:517
  18.8 0.5 collective-permute-start.5
  19.3 1.0 %collective-permute-start.4 = (bf16[64,512]{1,0:T(8,128)(2,1)S(1)}, bf16[64,512]{1,0:T(8,128)(2,1)S(1)}, u32[]{:S(2)}, u32[]{:S(2)}) collective-permute-start(bf16[64,512]{1,0:T(8,128)(2,1)S(1)} %shard_map.105.refs_0_.refs_4_), channel_id=1, source_target_pairs={{0,4},{1,5},{2,6},{3,7},{4,0},{5,1},{6,2},{7,3},{8,12},{9,13},{10,... | collective-permute-start | bytes 196616 | tf_op jit(solution)/shard_map/ppermute | solution.py:505
  20.3 2.0 %collective-permute-start.3 = (bf16[64,512]{1,0:T(8,128)(2,1)S(1)}, bf16[64,512]{1,0:T(8,128)(2,1)S(1)}, u32[]{:S(2)}, u32[]{:S(2)}) collective-permute-start(bf16[64,512]{1,0:T(8,128)(2,1)S(1)} %shard_map.105.refs_0_.refs_4_), channel_id=1, source_target_pairs={{0,2},{1,3},{2,0},{3,1},{4,6},{5,7},{6,4},{7,5},{8,10},{9,11},{10,... | collective-permute-start | bytes 196616 | tf_op jit(solution)/shard_map/ppermute | solution.py:505
  22.3 2.0 %collective-permute-done.5.refs_3_ = bf16[64,512]{1,0:T(8,128)(2,1)S(1)} collective-permute-done((bf16[64,512]{1,0:T(8,128)(2,1)S(1)}, bf16[64,512]{1,0:T(8,128)(2,1)S(1)}, u32[]{:S(2)}, u32[]{:S(2)}) %collective-permute-start.5) | collective-permute-done | bytes 65568 | tf_op jit(solution)/shard_map/ppermute | solution.py:505
  24.3 0.3 collective-permute-done.4.refs_2_
  24.6 0.8 %collective-permute-done.3.refs_1_ = bf16[64,512]{1,0:T(8,128)(2,1)S(1)} collective-permute-done((bf16[64,512]{1,0:T(8,128)(2,1)S(1)}, bf16[64,512]{1,0:T(8,128)(2,1)S(1)}, u32[]{:S(2)}, u32[]{:S(2)}) %collective-permute-start.3) | collective-permute-done | bytes 65568 | tf_op jit(solution)/shard_map/ppermute | solution.py:505
  25.3 0.1 collective-permute-start.6
  25.4 0.0 copy-start
  25.4 0.0 copy-start.5
  25.5 0.4 shard_map.100
  25.8 1.1 %collective-permute-done.6.refs_6_ = bf16[256,512]{1,0:T(8,128)(2,1)S(1)} collective-permute-done((bf16[256,512]{1,0:T(8,128)(2,1)S(1)}, bf16[256,512]{1,0:T(8,128)(2,1)S(1)}, u32[]{:S(2)}, u32[]{:S(2)}) %collective-permute-start.6) | collective-permute-done | bytes 262176 | tf_op jit(solution)/shard_map/ppermute | solution.py:505
  26.9 0.4 copy-done
  27.3 2.3 %shard_map.108 = (f32[256,768]{1,0:T(8,128)S(1)}, f32[256,1]{1,0:T(8,128)S(1)}, f32[8,256,256]{2,1,0:T(8,128)S(1)}, f32[24,128]{1,0:T(8,128)S(1)}) custom-call(s32[256,1]{1,0:T(8,128)S(1)} %get-tuple-element.26.refs_0_.place_ref, s32[256,1]{1,0:T(8,128)S(1)} %get-tuple-element.27.refs_1_, s32[24,1]{1,0:T(8,128)S(1)} %get-tuple-element.28.after_ref.refs_2_, ...), custom_call_target="tpu_custom_call" | custom-call | flops 100000000 | bytes 5379168 | tf_op jit(solution)/shard_map/pallas_call | solution.py:164
  29.7 0.4 shard_map.110
  30.1 1.3 %collective-permute-start.12 = (bf16[128,768]{1,0:T(8,128)(2,1)S(1)}, bf16[128,768]{1,0:T(8,128)(2,1)S(1)}, u32[]{:S(2)}, u32[]{:S(2)}) collective-permute-start(bf16[128,768]{1,0:T(8,128)(2,1)S(1)} %get-tuple-element.32.refs_0_), channel_id=1, source_target_pairs={{0,2},{1,3},{2,0},{3,1},{4,5},{5,4},{6,7},{7,6},{8,10},{9,11},{10,... | collective-permute-start | bytes 589832 | tf_op jit(solution)/shard_map/ppermute | solution.py:517
  31.4 0.0 collective-permute-start.13
  31.4 2.0 %collective-permute-start.14 = (bf16[128,768]{1,0:T(8,128)(2,1)S(1)}, bf16[128,768]{1,0:T(8,128)(2,1)S(1)}, u32[]{:S(2)}, u32[]{:S(2)}) collective-permute-start(bf16[128,768]{1,0:T(8,128)(2,1)S(1)} %get-tuple-element.32.refs_0_), channel_id=1, source_target_pairs={{0,4},{1,5},{2,3},{3,2},{4,0},{5,1},{6,7},{7,6},{8,9},{9,8},{10,14... | collective-permute-start | bytes 589832 | tf_op jit(solution)/shard_map/ppermute | solution.py:517
  33.4 4.4 %collective-permute-done.12.refs_2_ = bf16[128,768]{1,0:T(8,128)(2,1)S(1)} collective-permute-done((bf16[128,768]{1,0:T(8,128)(2,1)S(1)}, bf16[128,768]{1,0:T(8,128)(2,1)S(1)}, u32[]{:S(2)}, u32[]{:S(2)}) %collective-permute-start.12) | collective-permute-done | bytes 196640 | tf_op jit(solution)/shard_map/ppermute | solution.py:517
  37.9 1.3 %collective-permute-done.13.refs_3_ = bf16[128,768]{1,0:T(8,128)(2,1)S(1)} collective-permute-done((bf16[128,768]{1,0:T(8,128)(2,1)S(1)}, bf16[128,768]{1,0:T(8,128)(2,1)S(1)}, u32[]{:S(2)}, u32[]{:S(2)}) %collective-permute-start.13) | collective-permute-done | bytes 196640 | tf_op jit(solution)/shard_map/ppermute | solution.py:517
  39.1 0.6 shard_map.109.refs_8_.refs_2_
  39.8 0.0 copy-start.1
  39.8 2.8 %collective-permute-done.14.refs_4_ = bf16[128,768]{1,0:T(8,128)(2,1)S(1)} collective-permute-done((bf16[128,768]{1,0:T(8,128)(2,1)S(1)}, bf16[128,768]{1,0:T(8,128)(2,1)S(1)}, u32[]{:S(2)}, u32[]{:S(2)}) %collective-permute-start.14) | collective-permute-done | bytes 196640 | tf_op jit(solution)/shard_map/ppermute | solution.py:517
  42.6 0.1 shard_map.111.depart_ref
  42.7 0.1 collective-permute-start.18
  42.8 0.5 shard_map.112.refs_3_
  43.3 1.2 %collective-permute-done.18.refs_4_ = bf16[256,768]{1,0:T(8,128)(2,1)S(1)} collective-permute-done((bf16[256,768]{1,0:T(8,128)(2,1)S(1)}, bf16[256,768]{1,0:T(8,128)(2,1)S(1)}, u32[]{:S(2)}, u32[]{:S(2)}) %collective-permute-start.18) | collective-permute-done | bytes 393248 | tf_op jit(solution)/shard_map/ppermute | solution.py:505
  44.5 2.8 %shard_map.113 = (bf16[411,256]{1,0:T(8,128)(2,1)S(1)}, bf16[384,411]{1,0:T(8,128)(2,1)S(1)}) custom-call(bf16[2048,768]{1,0:T(8,128)(2,1)S(1)} %copy-done, bf16[1536,768]{1,0:T(8,128)(2,1)S(1)} %copy-done.1, f32[8,256,256]{2,1,0:T(8,128)S(1)} %shard_map.109.refs_8_.refs_2_, f32[256,768]{1,0:T(8,128)S(1)} %shard_map.112.refs_3_, ...), custom_call_target="tpu_custom_call" | custom-call | flops 1840250880 | bytes 10487296 | tf_op jit(solution)/shard_map/pallas_call | solution.py:164
  47.3 0.2 collective-permute-start.19
  47.5 0.1 slice_bitcast_fusion.2
  47.6 0.3 shard_map.114.refs_0_
  47.9 1.2 %collective-permute-done.19.refs_1_ = bf16[384,411]{1,0:T(8,128)(2,1)S(1)} collective-permute-done((bf16[384,411]{1,0:T(8,128)(2,1)S(1)}, bf16[384,411]{1,0:T(8,128)(2,1)S(1)}, u32[]{:S(2)}, u32[]{:S(2)}) %collective-permute-start.19) | collective-permute-done | bytes 315680 | tf_op jit(solution)/shard_map/ppermute | solution.py:505
  49.1 0.1 shard_map.115
  49.2 3.8 %collective-permute-start.20 = (bf16[96,411]{1,0:T(8,128)(2,1)S(1)}, bf16[96,411]{1,0:T(8,128)(2,1)S(1)}, u32[]{:S(2)}, u32[]{:S(2)}) collective-permute-start(bf16[96,411]{1,0:T(8,128)(2,1)S(1)} %get-tuple-element.38), channel_id=1, source_target_pairs={{0,6},{1,7},{2,4},{3,5},{4,2},{5,3},{6,0},{7,1},{8,14},{9,15},{10,... | collective-permute-start | bytes 236744 | tf_op jit(solution)/shard_map/ppermute | solution.py:505
  53.0 0.3 collective-permute-start.21
  53.3 0.4 collective-permute-start.22
  53.6 2.6 %collective-permute-done.20.refs_0_ = bf16[96,411]{1,0:T(8,128)(2,1)S(1)} collective-permute-done((bf16[96,411]{1,0:T(8,128)(2,1)S(1)}, bf16[96,411]{1,0:T(8,128)(2,1)S(1)}, u32[]{:S(2)}, u32[]{:S(2)}) %collective-permute-start.20) | collective-permute-done | bytes 78944 | tf_op jit(solution)/shard_map/ppermute | solution.py:505
  56.2 2.0 %collective-permute-done.21.refs_1_ = bf16[96,411]{1,0:T(8,128)(2,1)S(1)} collective-permute-done((bf16[96,411]{1,0:T(8,128)(2,1)S(1)}, bf16[96,411]{1,0:T(8,128)(2,1)S(1)}, u32[]{:S(2)}, u32[]{:S(2)}) %collective-permute-start.21) | collective-permute-done | bytes 78944 | tf_op jit(solution)/shard_map/ppermute | solution.py:505
  58.2 0.2 shard_map.116
  58.4 1.7 %collective-permute-start.23 = (bf16[32,411]{1,0:T(8,128)(2,1)S(1)}, bf16[32,411]{1,0:T(8,128)(2,1)S(1)}, u32[]{:S(2)}, u32[]{:S(2)}) collective-permute-start(bf16[32,411]{1,0:T(8,128)(2,1)S(1)} %get-tuple-element.42), channel_id=1, source_target_pairs={{0,24},{8,16},{16,8},{24,0},{1,25},{9,17},{17,9},{25,1},{2,26},{10... | collective-permute-start | bytes 78920 | tf_op jit(solution)/shard_map/ppermute | solution.py:508
  60.1 1.5 %collective-permute-start.24 = (bf16[32,411]{1,0:T(8,128)(2,1)S(1)}, bf16[32,411]{1,0:T(8,128)(2,1)S(1)}, u32[]{:S(2)}, u32[]{:S(2)}) collective-permute-start(bf16[32,411]{1,0:T(8,128)(2,1)S(1)} %get-tuple-element.43), channel_id=1, source_target_pairs={{0,16},{8,24},{16,0},{24,8},{1,17},{9,25},{17,1},{25,9},{2,18},{10... | collective-permute-start | bytes 78920 | tf_op jit(solution)/shard_map/ppermute | solution.py:508
  61.6 1.3 %collective-permute-start.25 = (bf16[32,411]{1,0:T(8,128)(2,1)S(1)}, bf16[32,411]{1,0:T(8,128)(2,1)S(1)}, u32[]{:S(2)}, u32[]{:S(2)}) collective-permute-start(bf16[32,411]{1,0:T(8,128)(2,1)S(1)} %get-tuple-element.44), channel_id=1, source_target_pairs={{0,8},{8,0},{16,24},{24,16},{1,9},{9,1},{17,25},{25,17},{2,10},{10... | collective-permute-start | bytes 78920 | tf_op jit(solution)/shard_map/ppermute | solution.py:508
  62.9 0.1 maximum_sqrt_fusion
  63.0 0.1 copy.19
  63.0 1.4 %collective-permute-done.23.refs_0_ = bf16[32,411]{1,0:T(8,128)(2,1)S(1)} collective-permute-done((bf16[32,411]{1,0:T(8,128)(2,1)S(1)}, bf16[32,411]{1,0:T(8,128)(2,1)S(1)}, u32[]{:S(2)}, u32[]{:S(2)}) %collective-permute-start.23) | collective-permute-done | bytes 26336 | tf_op jit(solution)/shard_map/ppermute | solution.py:508
  64.5 0.8 %collective-permute-done.24.refs_1_ = bf16[32,411]{1,0:T(8,128)(2,1)S(1)} collective-permute-done((bf16[32,411]{1,0:T(8,128)(2,1)S(1)}, bf16[32,411]{1,0:T(8,128)(2,1)S(1)}, u32[]{:S(2)}, u32[]{:S(2)}) %collective-permute-start.24) | collective-permute-done | bytes 26336 | tf_op jit(solution)/shard_map/ppermute | solution.py:508
  65.3 0.3 collective-permute-done.25.refs_2_
  65.6 1.4 %shard_map.117 = f32[4,32,411]{2,1,0:T(8,128)} custom-call(bf16[32,411]{1,0:T(8,128)(2,1)S(1)} %collective-permute-done.23.refs_0_, bf16[32,411]{1,0:T(8,128)(2,1)S(1)} %collective-permute-done.24.refs_1_, bf16[32,411]{1,0:T(8,128)(2,1)S(1)} %collective-permute-done.25.refs_2_, bf16[32,411]{1,0:T(8,128)(2,1)S(1)} %get-tuple-element.45.refs_3_, ...), custom_call_target="tpu_custom_call" | custom-call | flops 5260800 | bytes 106752 | tf_op jit(solution)/shard_map/pallas_call | solution.py:164
  (30 shorter events, 0.1 us)
Async XLA Ops:
  0.0 8.2 %copy-start.4 = (bf16[128,768]{1,0:T(8,128)(2,1)S(1)}, bf16[128,768]{1,0:T(8,128)(2,1)}, u32[]{:S(2)}) copy-start(bf16[128,768]{1,0:T(8,128)(2,1)} %refs_0_.3) | copy-start | bytes 589828
  0.0 16.0 %copy-start.3 = (bf16[411,256]{1,0:T(8,128)(2,1)S(1)}, bf16[411,256]{1,0:T(8,128)(2,1)}, u32[]{:S(2)}) copy-start(bf16[411,256]{1,0:T(8,128)(2,1)} %refs_0_.4) | copy-start | bytes 631300
  0.0 7.2 %copy-start.7 = (f32[256]{0:T(256)S(1)}, f32[256]{0:T(256)}, u32[]{:S(2)}) copy-start(f32[256]{0:T(256)} %bias_ref.1) | copy-start | bytes 3076
  0.0 7.2 %copy-start.8 = (s32[128]{0:T(128)S(1)}, s32[128]{0:T(128)}, u32[]{:S(2)}) copy-start(s32[128]{0:T(128)} %usable_ref.1) | copy-start | bytes 1540
  0.0 7.2 %copy-start.6 = (f32[4,32]{1,0:T(4,128)S(1)}, f32[4,32]{1,0:T(4,128)}, u32[]{:S(2)}) copy-start(f32[4,32]{1,0:T(4,128)} %diffusivity_ref.1) | copy-start | bytes 1540
  0.0 7.2 %copy-start.2 = (f32[4,32,411]{2,1,0:T(8,128)S(1)}, f32[4,32,411]{2,1,0:T(8,128)}, u32[]{:S(2)}) copy-start(f32[4,32,411]{2,1,0:T(8,128)} %fields_ref.1) | copy-start | bytes 631300
  0.0 8.2 %collective-permute-start.1 = (bf16[128,768]{1,0:T(8,128)(2,1)}, bf16[128,768]{1,0:T(8,128)(2,1)S(1)}, u32[]{:S(2)}, u32[]{:S(2)}) collective-permute-start(bf16[128,768]{1,0:T(8,128)(2,1)} %refs_0_.3), channel_id=1, source_target_pairs={{0,8},{8,0},{16,24},{24,16},{1,9},{9,1},{17,25},{25,17},{2,10},{10... | collective-permute-start | bytes 589832 | tf_op jit(solution)/shard_map/ppermute | solution.py:508
  3.1 12.8 %collective-permute-start.8 = (bf16[411,256]{1,0:T(8,128)(2,1)}, bf16[411,256]{1,0:T(8,128)(2,1)S(1)}, u32[]{:S(2)}, u32[]{:S(2)}) collective-permute-start(bf16[411,256]{1,0:T(8,128)(2,1)} %refs_0_.4), channel_id=1, source_target_pairs={{0,4},{1,5},{2,6},{3,7},{4,0},{5,1},{6,2},{7,3},{8,12},{9,13},{10,... | collective-permute-start | bytes 631304 | tf_op jit(solution)/shard_map/ppermute | solution.py:505
  4.6 11.3 %collective-permute-start.7 = (bf16[411,256]{1,0:T(8,128)(2,1)}, bf16[411,256]{1,0:T(8,128)(2,1)S(1)}, u32[]{:S(2)}, u32[]{:S(2)}) collective-permute-start(bf16[411,256]{1,0:T(8,128)(2,1)} %refs_0_.4), channel_id=1, source_target_pairs={{0,2},{1,3},{2,0},{3,1},{4,6},{5,7},{6,4},{7,5},{8,10},{9,11},{10,... | collective-permute-start | bytes 631304 | tf_op jit(solution)/shard_map/ppermute | solution.py:505
  6.1 9.8 %collective-permute-start.9 = (bf16[411,256]{1,0:T(8,128)(2,1)}, bf16[411,256]{1,0:T(8,128)(2,1)S(1)}, u32[]{:S(2)}, u32[]{:S(2)}) collective-permute-start(bf16[411,256]{1,0:T(8,128)(2,1)} %refs_0_.4), channel_id=1, source_target_pairs={{0,6},{1,7},{2,4},{3,5},{4,2},{5,3},{6,0},{7,1},{8,14},{9,15},{10,... | collective-permute-start | bytes 631304 | tf_op jit(solution)/shard_map/ppermute | solution.py:505
  7.2 18.3 %copy-start.9 = (s32[256,1]{0,1:T(1,128)S(1)}, s32[256,1]{0,1:T(1,128)}, u32[]{:S(2)}) copy-start(s32[256,1]{0,1:T(1,128)} %param.12) | copy-start | bytes 3076
  7.4 3.7 %collective-permute-start = (bf16[16,512]{1,0:T(8,128)(2,1)S(1)}, bf16[16,512]{1,0:T(8,128)(2,1)S(1)}, u32[]{:S(2)}, u32[]{:S(2)}) collective-permute-start(bf16[16,512]{1,0:T(8,128)(2,1)S(1)} %shard_map.102.refs_0_), channel_id=1, source_target_pairs={{0,8},{8,0},{16,24},{24,16},{1,9},{9,1},{17,25},{25,17},{2,10},{10... | collective-permute-start | bytes 49160 | tf_op jit(solution)/shard_map/ppermute | solution.py:508
  11.1 4.8 %collective-permute-start.2 = (bf16[32,512]{1,0:T(8,128)(2,1)S(1)}, bf16[32,512]{1,0:T(8,128)(2,1)S(1)}, u32[]{:S(2)}, u32[]{:S(2)}) collective-permute-start(bf16[32,512]{1,0:T(8,128)(2,1)S(1)} %shard_map.104.refs_0_), channel_id=1, source_target_pairs={{0,16},{8,24},{16,0},{24,8},{1,17},{9,25},{17,1},{25,9},{2,18},{10... | collective-permute-start | bytes 98312 | tf_op jit(solution)/shard_map/ppermute | solution.py:508
  16.1 10.9 %collective-permute-start.10 = (bf16[1664,256]{1,0:T(8,128)(2,1)S(1)}, bf16[1664,256]{1,0:T(8,128)(2,1)S(1)}, u32[]{:S(2)}, u32[]{:S(2)}) collective-permute-start(bf16[1664,256]{1,0:T(8,128)(2,1)S(1)} %shard_map.107.refs_7_.refs_5_), channel_id=1, source_target_pairs={{0,1},{1,0},{2,3},{3,2},{4,5},{5,4},{6,7},{7,6},{8,9},{9,8},{10,11... | collective-permute-start | bytes 2555912 | tf_op jit(solution)/shard_map/ppermute | solution.py:505
  16.1 13.5 %collective-permute-start.11 = (bf16[256,768]{1,0:T(8,128)(2,1)S(1)}, bf16[256,768]{1,0:T(8,128)(2,1)S(1)}, u32[]{:S(2)}, u32[]{:S(2)}) collective-permute-start(bf16[256,768]{1,0:T(8,128)(2,1)S(1)} %shard_map.103.refs_2_.refs_0_), channel_id=1, source_target_pairs={{0,16},{1,17},{2,3},{3,2},{4,20},{5,21},{6,7},{7,6},{8,9},{9,8},{1... | collective-permute-start | bytes 1179656 | tf_op jit(solution)/shard_map/ppermute | solution.py:517
  18.8 5.5 %collective-permute-start.5 = (bf16[64,512]{1,0:T(8,128)(2,1)S(1)}, bf16[64,512]{1,0:T(8,128)(2,1)S(1)}, u32[]{:S(2)}, u32[]{:S(2)}) collective-permute-start(bf16[64,512]{1,0:T(8,128)(2,1)S(1)} %shard_map.105.refs_0_.refs_4_), channel_id=1, source_target_pairs={{0,6},{1,7},{2,4},{3,5},{4,2},{5,3},{6,0},{7,1},{8,14},{9,15},{10,... | collective-permute-start | bytes 196616 | tf_op jit(solution)/shard_map/ppermute | solution.py:505
  19.3 5.2 %collective-permute-start.4 = (bf16[64,512]{1,0:T(8,128)(2,1)S(1)}, bf16[64,512]{1,0:T(8,128)(2,1)S(1)}, u32[]{:S(2)}, u32[]{:S(2)}) collective-permute-start(bf16[64,512]{1,0:T(8,128)(2,1)S(1)} %shard_map.105.refs_0_.refs_4_), channel_id=1, source_target_pairs={{0,4},{1,5},{2,6},{3,7},{4,0},{5,1},{6,2},{7,3},{8,12},{9,13},{10,... | collective-permute-start | bytes 196616 | tf_op jit(solution)/shard_map/ppermute | solution.py:505
  20.3 5.0 %collective-permute-start.3 = (bf16[64,512]{1,0:T(8,128)(2,1)S(1)}, bf16[64,512]{1,0:T(8,128)(2,1)S(1)}, u32[]{:S(2)}, u32[]{:S(2)}) collective-permute-start(bf16[64,512]{1,0:T(8,128)(2,1)S(1)} %shard_map.105.refs_0_.refs_4_), channel_id=1, source_target_pairs={{0,2},{1,3},{2,0},{3,1},{4,6},{5,7},{6,4},{7,5},{8,10},{9,11},{10,... | collective-permute-start | bytes 196616 | tf_op jit(solution)/shard_map/ppermute | solution.py:505
  25.3 1.6 %collective-permute-start.6 = (bf16[256,512]{1,0:T(8,128)(2,1)S(1)}, bf16[256,512]{1,0:T(8,128)(2,1)S(1)}, u32[]{:S(2)}, u32[]{:S(2)}) collective-permute-start(bf16[256,512]{1,0:T(8,128)(2,1)S(1)} %shard_map.106.refs_5_), channel_id=1, source_target_pairs={{0,1},{1,0},{2,3},{3,2},{4,5},{5,4},{6,7},{7,6},{8,9},{9,8},{10,11... | collective-permute-start | bytes 786440 | tf_op jit(solution)/shard_map/ppermute | solution.py:505
  25.4 1.9 %copy-start = (bf16[2048,768]{1,0:T(8,128)(2,1)S(1)}, bf16[2048,768]{1,0:T(8,128)(2,1)}, u32[]{:S(2)}) copy-start(bf16[2048,768]{1,0:T(8,128)(2,1)} %refs_0_.5) | copy-start | bytes 9437188
  25.4 1.9 %copy-start.5 = (f32[768]{0:T(1024)S(1)}, f32[768]{0:T(1024)}, u32[]{:S(2)}) copy-start(f32[768]{0:T(1024)} %refs_3_.1) | copy-start | bytes 9220
  30.1 7.8 %collective-permute-start.12 = (bf16[128,768]{1,0:T(8,128)(2,1)S(1)}, bf16[128,768]{1,0:T(8,128)(2,1)S(1)}, u32[]{:S(2)}, u32[]{:S(2)}) collective-permute-start(bf16[128,768]{1,0:T(8,128)(2,1)S(1)} %get-tuple-element.32.refs_0_), channel_id=1, source_target_pairs={{0,2},{1,3},{2,0},{3,1},{4,5},{5,4},{6,7},{7,6},{8,10},{9,11},{10,... | collective-permute-start | bytes 589832 | tf_op jit(solution)/shard_map/ppermute | solution.py:517
  31.4 7.7 %collective-permute-start.13 = (bf16[128,768]{1,0:T(8,128)(2,1)S(1)}, bf16[128,768]{1,0:T(8,128)(2,1)S(1)}, u32[]{:S(2)}, u32[]{:S(2)}) collective-permute-start(bf16[128,768]{1,0:T(8,128)(2,1)S(1)} %get-tuple-element.33.refs_1_), channel_id=1, source_target_pairs={{0,4},{1,5},{2,3},{3,2},{4,0},{5,1},{6,7},{7,6},{8,9},{9,8},{10,14... | collective-permute-start | bytes 589832 | tf_op jit(solution)/shard_map/ppermute | solution.py:517
  31.4 11.2 %collective-permute-start.14 = (bf16[128,768]{1,0:T(8,128)(2,1)S(1)}, bf16[128,768]{1,0:T(8,128)(2,1)S(1)}, u32[]{:S(2)}, u32[]{:S(2)}) collective-permute-start(bf16[128,768]{1,0:T(8,128)(2,1)S(1)} %get-tuple-element.32.refs_0_), channel_id=1, source_target_pairs={{0,4},{1,5},{2,3},{3,2},{4,0},{5,1},{6,7},{7,6},{8,9},{9,8},{10,14... | collective-permute-start | bytes 589832 | tf_op jit(solution)/shard_map/ppermute | solution.py:517
  33.4 9.2 %collective-permute-start.15 = (bf16[128,768]{1,0:T(8,128)(2,1)S(1)}, bf16[128,768]{1,0:T(8,128)(2,1)S(1)}, u32[]{:S(2)}, u32[]{:S(2)}) collective-permute-start(bf16[128,768]{1,0:T(8,128)(2,1)S(1)} %get-tuple-element.33.refs_1_), channel_id=1, source_target_pairs={{0,2},{1,3},{2,0},{3,1},{4,5},{5,4},{6,7},{7,6},{8,10},{9,11},{10,... | collective-permute-start | bytes 589832 | tf_op jit(solution)/shard_map/ppermute | solution.py:517
  37.9 4.8 %collective-permute-start.16 = (bf16[128,768]{1,0:T(8,128)(2,1)S(1)}, bf16[128,768]{1,0:T(8,128)(2,1)S(1)}, u32[]{:S(2)}, u32[]{:S(2)}) collective-permute-start(bf16[128,768]{1,0:T(8,128)(2,1)S(1)} %collective-permute-done.12.refs_2_), channel_id=1, source_target_pairs={{0,1},{1,0},{2,6},{3,7},{4,5},{5,4},{6,2},{7,3},{8,12},{9,13},{10,... | collective-permute-start | bytes 589832 | tf_op jit(solution)/shard_map/ppermute | solution.py:517
  39.1 3.5 %collective-permute-start.17 = (bf16[128,768]{1,0:T(8,128)(2,1)S(1)}, bf16[128,768]{1,0:T(8,128)(2,1)S(1)}, u32[]{:S(2)}, u32[]{:S(2)}) collective-permute-start(bf16[128,768]{1,0:T(8,128)(2,1)S(1)} %collective-permute-done.13.refs_3_), channel_id=1, source_target_pairs={{0,1},{1,0},{2,3},{3,2},{4,6},{5,7},{6,4},{7,5},{8,9},{9,8},{10,11... | collective-permute-start | bytes 589832 | tf_op jit(solution)/shard_map/ppermute | solution.py:517
  39.8 3.0 %copy-start.1 = (bf16[1536,768]{1,0:T(8,128)(2,1)S(1)}, bf16[1536,768]{1,0:T(8,128)(2,1)}, u32[]{:S(2)}) copy-start(bf16[1536,768]{1,0:T(8,128)(2,1)} %refs_1_.1) | copy-start | bytes 7077892
  42.7 1.8 %collective-permute-start.18 = (bf16[256,768]{1,0:T(8,128)(2,1)S(1)}, bf16[256,768]{1,0:T(8,128)(2,1)S(1)}, u32[]{:S(2)}, u32[]{:S(2)}) collective-permute-start(bf16[256,768]{1,0:T(8,128)(2,1)S(1)} %shard_map.111.depart_ref), channel_id=1, source_target_pairs={{0,1},{1,0},{2,3},{3,2},{4,5},{5,4},{6,7},{7,6},{8,9},{9,8},{10,11... | collective-permute-start | bytes 1179656 | tf_op jit(solution)/shard_map/ppermute | solution.py:505
  47.3 1.8 %collective-permute-start.19 = (bf16[384,411]{1,0:T(8,128)(2,1)S(1)}, bf16[384,411]{1,0:T(8,128)(2,1)S(1)}, u32[]{:S(2)}, u32[]{:S(2)}) collective-permute-start(bf16[384,411]{1,0:T(8,128)(2,1)S(1)} %get-tuple-element.37), channel_id=1, source_target_pairs={{0,1},{1,0},{2,3},{3,2},{4,5},{5,4},{6,7},{7,6},{8,9},{9,8},{10,11... | collective-permute-start | bytes 946952 | tf_op jit(solution)/shard_map/ppermute | solution.py:505
  49.2 7.0 %collective-permute-start.20 = (bf16[96,411]{1,0:T(8,128)(2,1)S(1)}, bf16[96,411]{1,0:T(8,128)(2,1)S(1)}, u32[]{:S(2)}, u32[]{:S(2)}) collective-permute-start(bf16[96,411]{1,0:T(8,128)(2,1)S(1)} %get-tuple-element.38), channel_id=1, source_target_pairs={{0,6},{1,7},{2,4},{3,5},{4,2},{5,3},{6,0},{7,1},{8,14},{9,15},{10,... | collective-permute-start | bytes 236744 | tf_op jit(solution)/shard_map/ppermute | solution.py:505
  53.0 5.2 %collective-permute-start.21 = (bf16[96,411]{1,0:T(8,128)(2,1)S(1)}, bf16[96,411]{1,0:T(8,128)(2,1)S(1)}, u32[]{:S(2)}, u32[]{:S(2)}) collective-permute-start(bf16[96,411]{1,0:T(8,128)(2,1)S(1)} %get-tuple-element.39), channel_id=1, source_target_pairs={{0,4},{1,5},{2,6},{3,7},{4,0},{5,1},{6,2},{7,3},{8,12},{9,13},{10,... | collective-permute-start | bytes 236744 | tf_op jit(solution)/shard_map/ppermute | solution.py:505
  53.3 4.9 %collective-permute-start.22 = (bf16[96,411]{1,0:T(8,128)(2,1)S(1)}, bf16[96,411]{1,0:T(8,128)(2,1)S(1)}, u32[]{:S(2)}, u32[]{:S(2)}) collective-permute-start(bf16[96,411]{1,0:T(8,128)(2,1)S(1)} %get-tuple-element.40), channel_id=1, source_target_pairs={{0,2},{1,3},{2,0},{3,1},{4,6},{5,7},{6,4},{7,5},{8,10},{9,11},{10,... | collective-permute-start | bytes 236744 | tf_op jit(solution)/shard_map/ppermute | solution.py:505
  58.4 6.0 %collective-permute-start.23 = (bf16[32,411]{1,0:T(8,128)(2,1)S(1)}, bf16[32,411]{1,0:T(8,128)(2,1)S(1)}, u32[]{:S(2)}, u32[]{:S(2)}) collective-permute-start(bf16[32,411]{1,0:T(8,128)(2,1)S(1)} %get-tuple-element.42), channel_id=1, source_target_pairs={{0,24},{8,16},{16,8},{24,0},{1,25},{9,17},{17,9},{25,1},{2,26},{10... | collective-permute-start | bytes 78920 | tf_op jit(solution)/shard_map/ppermute | solution.py:508
  60.1 5.2 %collective-permute-start.24 = (bf16[32,411]{1,0:T(8,128)(2,1)S(1)}, bf16[32,411]{1,0:T(8,128)(2,1)S(1)}, u32[]{:S(2)}, u32[]{:S(2)}) collective-permute-start(bf16[32,411]{1,0:T(8,128)(2,1)S(1)} %get-tuple-element.43), channel_id=1, source_target_pairs={{0,16},{8,24},{16,0},{24,8},{1,17},{9,25},{17,1},{25,9},{2,18},{10... | collective-permute-start | bytes 78920 | tf_op jit(solution)/shard_map/ppermute | solution.py:508
  61.6 4.0 %collective-permute-start.25 = (bf16[32,411]{1,0:T(8,128)(2,1)S(1)}, bf16[32,411]{1,0:T(8,128)(2,1)S(1)}, u32[]{:S(2)}, u32[]{:S(2)}) collective-permute-start(bf16[32,411]{1,0:T(8,128)(2,1)S(1)} %get-tuple-element.44), channel_id=1, source_target_pairs={{0,8},{8,0},{16,24},{24,16},{1,9},{9,1},{17,25},{25,17},{2,10},{10... | collective-permute-start | bytes 78920 | tf_op jit(solution)/shard_map/ppermute | solution.py:508

commit v17 on v16

--- a/solution.py
+++ b/solution.py
@@ -243,7 +243,7 @@
     return p.order(other) * p.tiles + (tile ^ lax.axis_index("tile"))
 
 
-def index_kernel(p, cell_ref, *target_refs):
+def index_kernel(p, cell_ref):
     t, c = lax.axis_index("tile"), lax.axis_index("chan")
     row = lax.broadcasted_iota(jnp.int32, cell_ref.shape, 0)
     reach = p.across + 4
@@ -254,17 +254,8 @@
     wanted = strip_of(p, tile, cell // p.across) * p.block + p.own_cols + 2 + cell % p.across
     cell_ref[...] = jnp.where(inside, wanted, -1)
 
-    target = lax.broadcasted_iota(jnp.int32, target_refs[0].shape, 0)
-    chip, inner = target // p.patch, target % p.patch
-    beside, inner = inner // (p.patch // 3) - 1, inner % (p.patch // 3)
-    tile, along = inner // p.own_cols, inner % p.own_cols
-    for k, target_ref in enumerate(target_refs):
-        row = (chip ^ (c // p.group)) * p.group + (c % p.group ^ k) + beside
-        wanted = tile * p.tile_cols + row * p.own_cols + along
-        target_ref[...] = jnp.where((row >= 0) & (row < p.chans), wanted, -1)
-
-
-def place_kernel(p, owners_ref, place_ref, source_ref):
+
+def place_kernel(p, owners_ref, place_ref, source_ref, *target_refs):
     t = lax.axis_index("tile")
     across = owners_ref[...]
     shape = (p.rows, p.rows)
@@ -280,6 +271,16 @@
     source_ref[...] = (
         strip_of(p, tile, first % p.tile_cols // p.own_cols) * p.block + first % p.own_cols
     )
+
+    c = lax.axis_index("chan")
+    target = lax.broadcasted_iota(jnp.int32, target_refs[0].shape, 0)
+    chip, inner = target // p.patch, target % p.patch
+    beside, inner = inner // (p.patch // 3) - 1, inner % (p.patch // 3)
+    tile, along = inner // p.own_cols, inner % p.own_cols
+    for k, target_ref in enumerate(target_refs):
+        row = (chip ^ (c // p.group)) * p.group + (c % p.group ^ k) + beside
+        wanted = tile * p.tile_cols + row * p.own_cols + along
+        target_ref[...] = jnp.where((row >= 0) & (row < p.chans), wanted, -1)
 
 
 def join_kernel(count, *refs):
@@ -530,9 +531,9 @@
         return join([value, over(value)], (2 * value.shape[0],) + value.shape[1:], after)
 
     reach = p.across + 4
-    cell, *targets = call(
+    cell = call(
         functools.partial(index_kernel, p),
-        [shape((3 * reach, 1), jnp.int32)] + [shape((p.chips * p.patch, 1), jnp.int32)] * p.group,
+        shape((3 * reach, 1), jnp.int32),
         [],
         flops=10**9,
     )
@@ -574,9 +575,10 @@
         send(seen, {(b // p.group ^ far_half, b): (b // p.group, b) for b in range(p.chans)}),
     ]
 
-    place, source = call(
+    place, source, *targets = call(
         functools.partial(place_kernel, p),
-        [shape((p.rows, 1), jnp.int32)] * 2,
+        [shape((p.rows, 1), jnp.int32)] * 2
+        + [shape((p.chips * p.patch, 1), jnp.int32)] * p.group,
         [owners.reshape(1, p.rows)],
         flops=SLACK_FLOPS,
     )

time: 67.1 us -> 66.9 us (level)
  transfers between devices with their start and end apart: 26 -> 26, of which waited for: 17 -> 18; matrix products, arithmetic and copies ran while one was open for 0% -> 0% of each run, Pallas kernels for 7% -> 7%
where the time goes in v17:
time: 66.9 us; the launch traced here: 66.7 us
  starting transfers between devices  28.1 us (42%)
  waiting for transfers between devices  27.9 us (42%)
  Pallas kernels  9.88 us (15%)
    ppermute x13, starting transfers between devices, flip(): return lax.ppermute(value, 'chan', [(b, b ^ mask) for b in range(p.chans)])  11.8 us
    ppermute x13, waiting for transfers between devices, flip(): return lax.ppermute(value, 'chan', [(b, b ^ mask) for b in range(p.chans)])  11 us
    ppermute x6, starting transfers between devices, trade(): return lax.ppermute(value, 'tile', [(a, a ^ mask) for a in range(p.tiles)])  10.3 us
    pallas_call x18, Pallas kernels, call(): pl.pallas_call(kernel, out_shape=out_shape, in_specs=[far if k in in_hbm...  9.88 us
    ppermute x7, waiting for transfers between devices, send(): lax.ppermute(value, both, sorted(((number(a), number(b)) for a, b in pair...  8.57 us
    ppermute x6, waiting for transfers between devices, trade(): return lax.ppermute(value, 'tile', [(a, a ^ mask) for a in range(p.tiles)])  8.29 us
    ppermute x7, starting transfers between devices, send(): lax.ppermute(value, both, sorted(((number(a), number(b)) for a, b in pair...  5.98 us
  transfers between devices with their start and end apart: 26, of which 18 were waited for; matrix products, arithmetic and copies ran while one was open for 0% of the time, Pallas kernels for 7%

profile of v17, /device:TPU:0, one launch (start us, length us, event | category | flops | bytes accessed | tf_op | source)
XLA Modules:
  0.0 66.7 jit_solution(227710626133289594)
XLA Ops:
  0.0 3.1 %collective-permute-start.1 = (bf16[128,768]{1,0:T(8,128)(2,1)}, bf16[128,768]{1,0:T(8,128)(2,1)S(1)}, u32[]{:S(2)}, u32[]{:S(2)}) collective-permute-start(bf16[128,768]{1,0:T(8,128)(2,1)} %refs_0_.3), channel_id=1, source_target_pairs={{0,8},{8,0},{16,24},{24,16},{1,9},{9,1},{17,25},{25,17},{2,10},{10... | collective-permute-start | bytes 589832 | tf_op jit(solution)/shard_map/ppermute | solution.py:509
  3.1 1.5 %collective-permute-start.8 = (bf16[411,256]{1,0:T(8,128)(2,1)}, bf16[411,256]{1,0:T(8,128)(2,1)S(1)}, u32[]{:S(2)}, u32[]{:S(2)}) collective-permute-start(bf16[411,256]{1,0:T(8,128)(2,1)} %refs_0_.4), channel_id=1, source_target_pairs={{0,4},{1,5},{2,6},{3,7},{4,0},{5,1},{6,2},{7,3},{8,12},{9,13},{10,... | collective-permute-start | bytes 631304 | tf_op jit(solution)/shard_map/ppermute | solution.py:506
  4.6 1.5 %collective-permute-start.7 = (bf16[411,256]{1,0:T(8,128)(2,1)}, bf16[411,256]{1,0:T(8,128)(2,1)S(1)}, u32[]{:S(2)}, u32[]{:S(2)}) collective-permute-start(bf16[411,256]{1,0:T(8,128)(2,1)} %refs_0_.4), channel_id=1, source_target_pairs={{0,2},{1,3},{2,0},{3,1},{4,6},{5,7},{6,4},{7,5},{8,10},{9,11},{10,... | collective-permute-start | bytes 631304 | tf_op jit(solution)/shard_map/ppermute | solution.py:506
  6.1 0.5 collective-permute-start.9
  6.7 0.0 copy-start.9
  6.7 0.2 shard_map.102.refs_0_
  6.9 0.1 collective-permute-start
  7.0 1.3 %collective-permute-done.1.refs_1_ = bf16[128,768]{1,0:T(8,128)(2,1)S(1)} collective-permute-done((bf16[128,768]{1,0:T(8,128)(2,1)}, bf16[128,768]{1,0:T(8,128)(2,1)S(1)}, u32[]{:S(2)}, u32[]{:S(2)}) %collective-permute-start.1) | collective-permute-done | bytes 196640 | tf_op jit(solution)/shard_map/ppermute | solution.py:509
  8.3 2.4 %collective-permute-done.refs_1_ = bf16[16,512]{1,0:T(8,128)(2,1)S(1)} collective-permute-done((bf16[16,512]{1,0:T(8,128)(2,1)S(1)}, bf16[16,512]{1,0:T(8,128)(2,1)S(1)}, u32[]{:S(2)}, u32[]{:S(2)}) %collective-permute-start) | collective-permute-done | bytes 16416 | tf_op jit(solution)/shard_map/ppermute | solution.py:509
  10.6 2.7 %collective-permute-start.2 = (bf16[32,512]{1,0:T(8,128)(2,1)S(1)}, bf16[32,512]{1,0:T(8,128)(2,1)S(1)}, u32[]{:S(2)}, u32[]{:S(2)}) collective-permute-start(bf16[32,512]{1,0:T(8,128)(2,1)S(1)} %shard_map.104.refs_0_), channel_id=1, source_target_pairs={{0,16},{8,24},{16,0},{24,8},{1,17},{9,25},{17,1},{25,9},{2,18},{10... | collective-permute-start | bytes 98312 | tf_op jit(solution)/shard_map/ppermute | solution.py:509
  13.3 2.1 %collective-permute-done.2.refs_1_ = bf16[32,512]{1,0:T(8,128)(2,1)S(1)} collective-permute-done((bf16[32,512]{1,0:T(8,128)(2,1)S(1)}, bf16[32,512]{1,0:T(8,128)(2,1)S(1)}, u32[]{:S(2)}, u32[]{:S(2)}) %collective-permute-start.2) | collective-permute-done | bytes 32800 | tf_op jit(solution)/shard_map/ppermute | solution.py:509
  15.5 0.3 collective-permute-done.9.refs_3_
  15.8 0.1 shard_map.107.refs_7_.refs_5_
  15.9 0.1 collective-permute-start.10
  15.9 2.7 %collective-permute-start.11 = (bf16[256,768]{1,0:T(8,128)(2,1)S(1)}, bf16[256,768]{1,0:T(8,128)(2,1)S(1)}, u32[]{:S(2)}, u32[]{:S(2)}) collective-permute-start(bf16[256,768]{1,0:T(8,128)(2,1)S(1)} %shard_map.103.refs_2_.refs_0_), channel_id=1, source_target_pairs={{0,16},{1,17},{2,3},{3,2},{4,20},{5,21},{6,7},{7,6},{8,9},{9,8},{1... | collective-permute-start | bytes 1179656 | tf_op jit(solution)/shard_map/ppermute | solution.py:518
  18.6 0.3 collective-permute-start.5
  18.9 1.2 %collective-permute-start.4 = (bf16[64,512]{1,0:T(8,128)(2,1)S(1)}, bf16[64,512]{1,0:T(8,128)(2,1)S(1)}, u32[]{:S(2)}, u32[]{:S(2)}) collective-permute-start(bf16[64,512]{1,0:T(8,128)(2,1)S(1)} %shard_map.105.refs_0_.refs_4_), channel_id=1, source_target_pairs={{0,4},{1,5},{2,6},{3,7},{4,0},{5,1},{6,2},{7,3},{8,12},{9,13},{10,... | collective-permute-start | bytes 196616 | tf_op jit(solution)/shard_map/ppermute | solution.py:506
  20.1 2.0 %collective-permute-start.3 = (bf16[64,512]{1,0:T(8,128)(2,1)S(1)}, bf16[64,512]{1,0:T(8,128)(2,1)S(1)}, u32[]{:S(2)}, u32[]{:S(2)}) collective-permute-start(bf16[64,512]{1,0:T(8,128)(2,1)S(1)} %shard_map.105.refs_0_.refs_4_), channel_id=1, source_target_pairs={{0,2},{1,3},{2,0},{3,1},{4,6},{5,7},{6,4},{7,5},{8,10},{9,11},{10,... | collective-permute-start | bytes 196616 | tf_op jit(solution)/shard_map/ppermute | solution.py:506
  22.1 2.0 %collective-permute-done.5.refs_3_ = bf16[64,512]{1,0:T(8,128)(2,1)S(1)} collective-permute-done((bf16[64,512]{1,0:T(8,128)(2,1)S(1)}, bf16[64,512]{1,0:T(8,128)(2,1)S(1)}, u32[]{:S(2)}, u32[]{:S(2)}) %collective-permute-start.5) | collective-permute-done | bytes 65568 | tf_op jit(solution)/shard_map/ppermute | solution.py:506
  24.1 0.3 collective-permute-done.4.refs_2_
  24.4 0.8 %collective-permute-done.3.refs_1_ = bf16[64,512]{1,0:T(8,128)(2,1)S(1)} collective-permute-done((bf16[64,512]{1,0:T(8,128)(2,1)S(1)}, bf16[64,512]{1,0:T(8,128)(2,1)S(1)}, u32[]{:S(2)}, u32[]{:S(2)}) %collective-permute-start.3) | collective-permute-done | bytes 65568 | tf_op jit(solution)/shard_map/ppermute | solution.py:506
  25.2 0.1 collective-permute-start.6
  25.2 0.0 copy-start
  25.3 0.0 copy-start.5
  25.3 0.8 %shard_map.100 = (s32[256,1]{1,0:T(8,128)S(1)}, s32[256,1]{1,0:T(8,128)S(1)}, s32[384,1]{1,0:T(8,128)S(1)}, s32[384,1]{1,0:T(8,128)S(1)}) custom-call(s32[1,256]{1,0:T(1,128)S(1)} %bitcast.12), custom_call_target="tpu_custom_call" | custom-call | flops 2000000000 | bytes 1024 | tf_op jit(solution)/shard_map/pallas_call | solution.py:164
  26.1 0.7 collective-permute-done.6.refs_6_
  26.8 0.0 collective-permute-done.10.refs_8_.refs_6_
  26.8 0.4 copy-done
  27.1 2.3 %shard_map.108 = (f32[256,768]{1,0:T(8,128)S(1)}, f32[256,1]{1,0:T(8,128)S(1)}, f32[8,256,256]{2,1,0:T(8,128)S(1)}, f32[24,128]{1,0:T(8,128)S(1)}) custom-call(s32[256,1]{1,0:T(8,128)S(1)} %get-tuple-element.25.refs_0_.place_ref, s32[256,1]{1,0:T(8,128)S(1)} %get-tuple-element.26.refs_1_, s32[24,1]{1,0:T(8,128)S(1)} %shard_map.101.after_ref.refs_2_, ...), custom_call_target="tpu_custom_call" | custom-call | flops 100000000 | bytes 5379168 | tf_op jit(solution)/shard_map/pallas_call | solution.py:164
  29.5 0.4 shard_map.110
  29.9 1.3 %collective-permute-start.12 = (bf16[128,768]{1,0:T(8,128)(2,1)S(1)}, bf16[128,768]{1,0:T(8,128)(2,1)S(1)}, u32[]{:S(2)}, u32[]{:S(2)}) collective-permute-start(bf16[128,768]{1,0:T(8,128)(2,1)S(1)} %get-tuple-element.30.refs_0_), channel_id=1, source_target_pairs={{0,2},{1,3},{2,0},{3,1},{4,5},{5,4},{6,7},{7,6},{8,10},{9,11},{10,... | collective-permute-start | bytes 589832 | tf_op jit(solution)/shard_map/ppermute | solution.py:518
  31.2 0.0 collective-permute-start.13
  31.2 2.0 %collective-permute-start.14 = (bf16[128,768]{1,0:T(8,128)(2,1)S(1)}, bf16[128,768]{1,0:T(8,128)(2,1)S(1)}, u32[]{:S(2)}, u32[]{:S(2)}) collective-permute-start(bf16[128,768]{1,0:T(8,128)(2,1)S(1)} %get-tuple-element.30.refs_0_), channel_id=1, source_target_pairs={{0,4},{1,5},{2,3},{3,2},{4,0},{5,1},{6,7},{7,6},{8,9},{9,8},{10,14... | collective-permute-start | bytes 589832 | tf_op jit(solution)/shard_map/ppermute | solution.py:518
  33.2 4.4 %collective-permute-done.12.refs_2_ = bf16[128,768]{1,0:T(8,128)(2,1)S(1)} collective-permute-done((bf16[128,768]{1,0:T(8,128)(2,1)S(1)}, bf16[128,768]{1,0:T(8,128)(2,1)S(1)}, u32[]{:S(2)}, u32[]{:S(2)}) %collective-permute-start.12) | collective-permute-done | bytes 196640 | tf_op jit(solution)/shard_map/ppermute | solution.py:518
  37.7 0.0 collective-permute-start.16
  37.7 1.3 %collective-permute-done.13.refs_3_ = bf16[128,768]{1,0:T(8,128)(2,1)S(1)} collective-permute-done((bf16[128,768]{1,0:T(8,128)(2,1)S(1)}, bf16[128,768]{1,0:T(8,128)(2,1)S(1)}, u32[]{:S(2)}, u32[]{:S(2)}) %collective-permute-start.13) | collective-permute-done | bytes 196640 | tf_op jit(solution)/shard_map/ppermute | solution.py:518
  38.9 0.6 shard_map.109.refs_8_.refs_2_
  39.6 0.0 copy-start.1
  39.6 2.9 %collective-permute-done.14.refs_4_ = bf16[128,768]{1,0:T(8,128)(2,1)S(1)} collective-permute-done((bf16[128,768]{1,0:T(8,128)(2,1)S(1)}, bf16[128,768]{1,0:T(8,128)(2,1)S(1)}, u32[]{:S(2)}, u32[]{:S(2)}) %collective-permute-start.14) | collective-permute-done | bytes 196640 | tf_op jit(solution)/shard_map/ppermute | solution.py:518
  42.4 0.1 shard_map.111.depart_ref
  42.5 0.1 collective-permute-start.18
  42.6 0.5 shard_map.112.refs_3_
  43.1 1.2 %collective-permute-done.18.refs_4_ = bf16[256,768]{1,0:T(8,128)(2,1)S(1)} collective-permute-done((bf16[256,768]{1,0:T(8,128)(2,1)S(1)}, bf16[256,768]{1,0:T(8,128)(2,1)S(1)}, u32[]{:S(2)}, u32[]{:S(2)}) %collective-permute-start.18) | collective-permute-done | bytes 393248 | tf_op jit(solution)/shard_map/ppermute | solution.py:506
  44.3 2.8 %shard_map.113 = (bf16[411,256]{1,0:T(8,128)(2,1)S(1)}, bf16[384,411]{1,0:T(8,128)(2,1)S(1)}) custom-call(bf16[2048,768]{1,0:T(8,128)(2,1)S(1)} %copy-done, bf16[1536,768]{1,0:T(8,128)(2,1)S(1)} %copy-done.1, f32[8,256,256]{2,1,0:T(8,128)S(1)} %shard_map.109.refs_8_.refs_2_, f32[256,768]{1,0:T(8,128)S(1)} %shard_map.112.refs_3_, ...), custom_call_target="tpu_custom_call" | custom-call | flops 1840250880 | bytes 10487296 | tf_op jit(solution)/shard_map/pallas_call | solution.py:164
  47.1 0.2 collective-permute-start.19
  47.3 0.1 slice_bitcast_fusion.2
  47.4 0.3 shard_map.114.refs_0_
  47.7 1.2 %collective-permute-done.19.refs_1_ = bf16[384,411]{1,0:T(8,128)(2,1)S(1)} collective-permute-done((bf16[384,411]{1,0:T(8,128)(2,1)S(1)}, bf16[384,411]{1,0:T(8,128)(2,1)S(1)}, u32[]{:S(2)}, u32[]{:S(2)}) %collective-permute-start.19) | collective-permute-done | bytes 315680 | tf_op jit(solution)/shard_map/ppermute | solution.py:506
  48.9 0.1 shard_map.115
  49.0 3.8 %collective-permute-start.20 = (bf16[96,411]{1,0:T(8,128)(2,1)S(1)}, bf16[96,411]{1,0:T(8,128)(2,1)S(1)}, u32[]{:S(2)}, u32[]{:S(2)}) collective-permute-start(bf16[96,411]{1,0:T(8,128)(2,1)S(1)} %get-tuple-element.36), channel_id=1, source_target_pairs={{0,6},{1,7},{2,4},{3,5},{4,2},{5,3},{6,0},{7,1},{8,14},{9,15},{10,... | collective-permute-start | bytes 236744 | tf_op jit(solution)/shard_map/ppermute | solution.py:506
  52.8 0.3 collective-permute-start.21
  53.1 0.4 collective-permute-start.22
  53.4 2.6 %collective-permute-done.20.refs_0_ = bf16[96,411]{1,0:T(8,128)(2,1)S(1)} collective-permute-done((bf16[96,411]{1,0:T(8,128)(2,1)S(1)}, bf16[96,411]{1,0:T(8,128)(2,1)S(1)}, u32[]{:S(2)}, u32[]{:S(2)}) %collective-permute-start.20) | collective-permute-done | bytes 78944 | tf_op jit(solution)/shard_map/ppermute | solution.py:506
  56.0 2.0 %collective-permute-done.21.refs_1_ = bf16[96,411]{1,0:T(8,128)(2,1)S(1)} collective-permute-done((bf16[96,411]{1,0:T(8,128)(2,1)S(1)}, bf16[96,411]{1,0:T(8,128)(2,1)S(1)}, u32[]{:S(2)}, u32[]{:S(2)}) %collective-permute-start.21) | collective-permute-done | bytes 78944 | tf_op jit(solution)/shard_map/ppermute | solution.py:506
  58.0 0.2 shard_map.116
  58.2 1.7 %collective-permute-start.23 = (bf16[32,411]{1,0:T(8,128)(2,1)S(1)}, bf16[32,411]{1,0:T(8,128)(2,1)S(1)}, u32[]{:S(2)}, u32[]{:S(2)}) collective-permute-start(bf16[32,411]{1,0:T(8,128)(2,1)S(1)} %get-tuple-element.40), channel_id=1, source_target_pairs={{0,24},{8,16},{16,8},{24,0},{1,25},{9,17},{17,9},{25,1},{2,26},{10... | collective-permute-start | bytes 78920 | tf_op jit(solution)/shard_map/ppermute | solution.py:509
  59.9 1.5 %collective-permute-start.24 = (bf16[32,411]{1,0:T(8,128)(2,1)S(1)}, bf16[32,411]{1,0:T(8,128)(2,1)S(1)}, u32[]{:S(2)}, u32[]{:S(2)}) collective-permute-start(bf16[32,411]{1,0:T(8,128)(2,1)S(1)} %get-tuple-element.41), channel_id=1, source_target_pairs={{0,16},{8,24},{16,0},{24,8},{1,17},{9,25},{17,1},{25,9},{2,18},{10... | collective-permute-start | bytes 78920 | tf_op jit(solution)/shard_map/ppermute | solution.py:509
  61.4 1.2 %collective-permute-start.25 = (bf16[32,411]{1,0:T(8,128)(2,1)S(1)}, bf16[32,411]{1,0:T(8,128)(2,1)S(1)}, u32[]{:S(2)}, u32[]{:S(2)}) collective-permute-start(bf16[32,411]{1,0:T(8,128)(2,1)S(1)} %get-tuple-element.42), channel_id=1, source_target_pairs={{0,8},{8,0},{16,24},{24,16},{1,9},{9,1},{17,25},{25,17},{2,10},{10... | collective-permute-start | bytes 78920 | tf_op jit(solution)/shard_map/ppermute | solution.py:509
  62.7 0.1 maximum_sqrt_fusion
  62.8 0.1 copy.19
  62.8 1.3 %collective-permute-done.23.refs_0_ = bf16[32,411]{1,0:T(8,128)(2,1)S(1)} collective-permute-done((bf16[32,411]{1,0:T(8,128)(2,1)S(1)}, bf16[32,411]{1,0:T(8,128)(2,1)S(1)}, u32[]{:S(2)}, u32[]{:S(2)}) %collective-permute-start.23) | collective-permute-done | bytes 26336 | tf_op jit(solution)/shard_map/ppermute | solution.py:509
  64.1 0.9 %collective-permute-done.24.refs_1_ = bf16[32,411]{1,0:T(8,128)(2,1)S(1)} collective-permute-done((bf16[32,411]{1,0:T(8,128)(2,1)S(1)}, bf16[32,411]{1,0:T(8,128)(2,1)S(1)}, u32[]{:S(2)}, u32[]{:S(2)}) %collective-permute-start.24) | collective-permute-done | bytes 26336 | tf_op jit(solution)/shard_map/ppermute | solution.py:509
  65.0 0.4 collective-permute-done.25.refs_2_
  65.4 1.4 %shard_map.117 = f32[4,32,411]{2,1,0:T(8,128)} custom-call(bf16[32,411]{1,0:T(8,128)(2,1)S(1)} %collective-permute-done.23.refs_0_, bf16[32,411]{1,0:T(8,128)(2,1)S(1)} %collective-permute-done.24.refs_1_, bf16[32,411]{1,0:T(8,128)(2,1)S(1)} %collective-permute-done.25.refs_2_, bf16[32,411]{1,0:T(8,128)(2,1)S(1)} %get-tuple-element.43.refs_3_, ...), custom_call_target="tpu_custom_call" | custom-call | flops 5260800 | bytes 106752 | tf_op jit(solution)/shard_map/pallas_call | solution.py:164
  (30 shorter events, 0.2 us)
Async XLA Ops:
  0.0 8.2 %copy-start.4 = (bf16[128,768]{1,0:T(8,128)(2,1)S(1)}, bf16[128,768]{1,0:T(8,128)(2,1)}, u32[]{:S(2)}) copy-start(bf16[128,768]{1,0:T(8,128)(2,1)} %refs_0_.3) | copy-start | bytes 589828
  0.0 15.8 %copy-start.3 = (bf16[411,256]{1,0:T(8,128)(2,1)S(1)}, bf16[411,256]{1,0:T(8,128)(2,1)}, u32[]{:S(2)}) copy-start(bf16[411,256]{1,0:T(8,128)(2,1)} %refs_0_.4) | copy-start | bytes 631300
  0.0 6.7 %copy-start.7 = (f32[256]{0:T(256)S(1)}, f32[256]{0:T(256)}, u32[]{:S(2)}) copy-start(f32[256]{0:T(256)} %bias_ref.1) | copy-start | bytes 3076
  0.0 6.7 %copy-start.8 = (s32[128]{0:T(128)S(1)}, s32[128]{0:T(128)}, u32[]{:S(2)}) copy-start(s32[128]{0:T(128)} %usable_ref.1) | copy-start | bytes 1540
  0.0 6.7 %copy-start.6 = (f32[4,32]{1,0:T(4,128)S(1)}, f32[4,32]{1,0:T(4,128)}, u32[]{:S(2)}) copy-start(f32[4,32]{1,0:T(4,128)} %diffusivity_ref.1) | copy-start | bytes 1540
  0.0 6.7 %copy-start.2 = (f32[4,32,411]{2,1,0:T(8,128)S(1)}, f32[4,32,411]{2,1,0:T(8,128)}, u32[]{:S(2)}) copy-start(f32[4,32,411]{2,1,0:T(8,128)} %fields_ref.1) | copy-start | bytes 631300
  0.0 8.2 %collective-permute-start.1 = (bf16[128,768]{1,0:T(8,128)(2,1)}, bf16[128,768]{1,0:T(8,128)(2,1)S(1)}, u32[]{:S(2)}, u32[]{:S(2)}) collective-permute-start(bf16[128,768]{1,0:T(8,128)(2,1)} %refs_0_.3), channel_id=1, source_target_pairs={{0,8},{8,0},{16,24},{24,16},{1,9},{9,1},{17,25},{25,17},{2,10},{10... | collective-permute-start | bytes 589832 | tf_op jit(solution)/shard_map/ppermute | solution.py:509
  3.1 12.3 %collective-permute-start.8 = (bf16[411,256]{1,0:T(8,128)(2,1)}, bf16[411,256]{1,0:T(8,128)(2,1)S(1)}, u32[]{:S(2)}, u32[]{:S(2)}) collective-permute-start(bf16[411,256]{1,0:T(8,128)(2,1)} %refs_0_.4), channel_id=1, source_target_pairs={{0,4},{1,5},{2,6},{3,7},{4,0},{5,1},{6,2},{7,3},{8,12},{9,13},{10,... | collective-permute-start | bytes 631304 | tf_op jit(solution)/shard_map/ppermute | solution.py:506
  4.6 10.8 %collective-permute-start.7 = (bf16[411,256]{1,0:T(8,128)(2,1)}, bf16[411,256]{1,0:T(8,128)(2,1)S(1)}, u32[]{:S(2)}, u32[]{:S(2)}) collective-permute-start(bf16[411,256]{1,0:T(8,128)(2,1)} %refs_0_.4), channel_id=1, source_target_pairs={{0,2},{1,3},{2,0},{3,1},{4,6},{5,7},{6,4},{7,5},{8,10},{9,11},{10,... | collective-permute-start | bytes 631304 | tf_op jit(solution)/shard_map/ppermute | solution.py:506
  6.1 9.7 %collective-permute-start.9 = (bf16[411,256]{1,0:T(8,128)(2,1)}, bf16[411,256]{1,0:T(8,128)(2,1)S(1)}, u32[]{:S(2)}, u32[]{:S(2)}) collective-permute-start(bf16[411,256]{1,0:T(8,128)(2,1)} %refs_0_.4), channel_id=1, source_target_pairs={{0,6},{1,7},{2,4},{3,5},{4,2},{5,3},{6,0},{7,1},{8,14},{9,15},{10,... | collective-permute-start | bytes 631304 | tf_op jit(solution)/shard_map/ppermute | solution.py:506
  6.7 18.5 %copy-start.9 = (s32[256,1]{0,1:T(1,128)S(1)}, s32[256,1]{0,1:T(1,128)}, u32[]{:S(2)}) copy-start(s32[256,1]{0,1:T(1,128)} %param.12) | copy-start | bytes 3076
  6.9 3.7 %collective-permute-start = (bf16[16,512]{1,0:T(8,128)(2,1)S(1)}, bf16[16,512]{1,0:T(8,128)(2,1)S(1)}, u32[]{:S(2)}, u32[]{:S(2)}) collective-permute-start(bf16[16,512]{1,0:T(8,128)(2,1)S(1)} %shard_map.102.refs_0_), channel_id=1, source_target_pairs={{0,8},{8,0},{16,24},{24,16},{1,9},{9,1},{17,25},{25,17},{2,10},{10... | collective-permute-start | bytes 49160 | tf_op jit(solution)/shard_map/ppermute | solution.py:509
  10.6 4.8 %collective-permute-start.2 = (bf16[32,512]{1,0:T(8,128)(2,1)S(1)}, bf16[32,512]{1,0:T(8,128)(2,1)S(1)}, u32[]{:S(2)}, u32[]{:S(2)}) collective-permute-start(bf16[32,512]{1,0:T(8,128)(2,1)S(1)} %shard_map.104.refs_0_), channel_id=1, source_target_pairs={{0,16},{8,24},{16,0},{24,8},{1,17},{9,25},{17,1},{25,9},{2,18},{10... | collective-permute-start | bytes 98312 | tf_op jit(solution)/shard_map/ppermute | solution.py:509
  15.9 10.9 %collective-permute-start.10 = (bf16[1664,256]{1,0:T(8,128)(2,1)S(1)}, bf16[1664,256]{1,0:T(8,128)(2,1)S(1)}, u32[]{:S(2)}, u32[]{:S(2)}) collective-permute-start(bf16[1664,256]{1,0:T(8,128)(2,1)S(1)} %shard_map.107.refs_7_.refs_5_), channel_id=1, source_target_pairs={{0,1},{1,0},{2,3},{3,2},{4,5},{5,4},{6,7},{7,6},{8,9},{9,8},{10,11... | collective-permute-start | bytes 2555912 | tf_op jit(solution)/shard_map/ppermute | solution.py:506
  15.9 13.5 %collective-permute-start.11 = (bf16[256,768]{1,0:T(8,128)(2,1)S(1)}, bf16[256,768]{1,0:T(8,128)(2,1)S(1)}, u32[]{:S(2)}, u32[]{:S(2)}) collective-permute-start(bf16[256,768]{1,0:T(8,128)(2,1)S(1)} %shard_map.103.refs_2_.refs_0_), channel_id=1, source_target_pairs={{0,16},{1,17},{2,3},{3,2},{4,20},{5,21},{6,7},{7,6},{8,9},{9,8},{1... | collective-permute-start | bytes 1179656 | tf_op jit(solution)/shard_map/ppermute | solution.py:518
  18.6 5.5 %collective-permute-start.5 = (bf16[64,512]{1,0:T(8,128)(2,1)S(1)}, bf16[64,512]{1,0:T(8,128)(2,1)S(1)}, u32[]{:S(2)}, u32[]{:S(2)}) collective-permute-start(bf16[64,512]{1,0:T(8,128)(2,1)S(1)} %shard_map.105.refs_0_.refs_4_), channel_id=1, source_target_pairs={{0,6},{1,7},{2,4},{3,5},{4,2},{5,3},{6,0},{7,1},{8,14},{9,15},{10,... | collective-permute-start | bytes 196616 | tf_op jit(solution)/shard_map/ppermute | solution.py:506
  18.9 5.5 %collective-permute-start.4 = (bf16[64,512]{1,0:T(8,128)(2,1)S(1)}, bf16[64,512]{1,0:T(8,128)(2,1)S(1)}, u32[]{:S(2)}, u32[]{:S(2)}) collective-permute-start(bf16[64,512]{1,0:T(8,128)(2,1)S(1)} %shard_map.105.refs_0_.refs_4_), channel_id=1, source_target_pairs={{0,4},{1,5},{2,6},{3,7},{4,0},{5,1},{6,2},{7,3},{8,12},{9,13},{10,... | collective-permute-start | bytes 196616 | tf_op jit(solution)/shard_map/ppermute | solution.py:506
  20.1 5.0 %collective-permute-start.3 = (bf16[64,512]{1,0:T(8,128)(2,1)S(1)}, bf16[64,512]{1,0:T(8,128)(2,1)S(1)}, u32[]{:S(2)}, u32[]{:S(2)}) collective-permute-start(bf16[64,512]{1,0:T(8,128)(2,1)S(1)} %shard_map.105.refs_0_.refs_4_), channel_id=1, source_target_pairs={{0,2},{1,3},{2,0},{3,1},{4,6},{5,7},{6,4},{7,5},{8,10},{9,11},{10,... | collective-permute-start | bytes 196616 | tf_op jit(solution)/shard_map/ppermute | solution.py:506
  25.2 1.6 %collective-permute-start.6 = (bf16[256,512]{1,0:T(8,128)(2,1)S(1)}, bf16[256,512]{1,0:T(8,128)(2,1)S(1)}, u32[]{:S(2)}, u32[]{:S(2)}) collective-permute-start(bf16[256,512]{1,0:T(8,128)(2,1)S(1)} %shard_map.106.refs_5_), channel_id=1, source_target_pairs={{0,1},{1,0},{2,3},{3,2},{4,5},{5,4},{6,7},{7,6},{8,9},{9,8},{10,11... | collective-permute-start | bytes 786440 | tf_op jit(solution)/shard_map/ppermute | solution.py:506
  25.2 1.9 %copy-start = (bf16[2048,768]{1,0:T(8,128)(2,1)S(1)}, bf16[2048,768]{1,0:T(8,128)(2,1)}, u32[]{:S(2)}) copy-start(bf16[2048,768]{1,0:T(8,128)(2,1)} %refs_0_.5) | copy-start | bytes 9437188
  25.3 1.9 %copy-start.5 = (f32[768]{0:T(1024)S(1)}, f32[768]{0:T(1024)}, u32[]{:S(2)}) copy-start(f32[768]{0:T(1024)} %refs_3_.1) | copy-start | bytes 9220
  29.9 7.8 %collective-permute-start.12 = (bf16[128,768]{1,0:T(8,128)(2,1)S(1)}, bf16[128,768]{1,0:T(8,128)(2,1)S(1)}, u32[]{:S(2)}, u32[]{:S(2)}) collective-permute-start(bf16[128,768]{1,0:T(8,128)(2,1)S(1)} %get-tuple-element.30.refs_0_), channel_id=1, source_target_pairs={{0,2},{1,3},{2,0},{3,1},{4,5},{5,4},{6,7},{7,6},{8,10},{9,11},{10,... | collective-permute-start | bytes 589832 | tf_op jit(solution)/shard_map/ppermute | solution.py:518
  31.2 7.7 %collective-permute-start.13 = (bf16[128,768]{1,0:T(8,128)(2,1)S(1)}, bf16[128,768]{1,0:T(8,128)(2,1)S(1)}, u32[]{:S(2)}, u32[]{:S(2)}) collective-permute-start(bf16[128,768]{1,0:T(8,128)(2,1)S(1)} %get-tuple-element.31.refs_1_), channel_id=1, source_target_pairs={{0,4},{1,5},{2,3},{3,2},{4,0},{5,1},{6,7},{7,6},{8,9},{9,8},{10,14... | collective-permute-start | bytes 589832 | tf_op jit(solution)/shard_map/ppermute | solution.py:518
  31.2 11.2 %collective-permute-start.14 = (bf16[128,768]{1,0:T(8,128)(2,1)S(1)}, bf16[128,768]{1,0:T(8,128)(2,1)S(1)}, u32[]{:S(2)}, u32[]{:S(2)}) collective-permute-start(bf16[128,768]{1,0:T(8,128)(2,1)S(1)} %get-tuple-element.30.refs_0_), channel_id=1, source_target_pairs={{0,4},{1,5},{2,3},{3,2},{4,0},{5,1},{6,7},{7,6},{8,9},{9,8},{10,14... | collective-permute-start | bytes 589832 | tf_op jit(solution)/shard_map/ppermute | solution.py:518
  33.2 9.2 %collective-permute-start.15 = (bf16[128,768]{1,0:T(8,128)(2,1)S(1)}, bf16[128,768]{1,0:T(8,128)(2,1)S(1)}, u32[]{:S(2)}, u32[]{:S(2)}) collective-permute-start(bf16[128,768]{1,0:T(8,128)(2,1)S(1)} %get-tuple-element.31.refs_1_), channel_id=1, source_target_pairs={{0,2},{1,3},{2,0},{3,1},{4,5},{5,4},{6,7},{7,6},{8,10},{9,11},{10,... | collective-permute-start | bytes 589832 | tf_op jit(solution)/shard_map/ppermute | solution.py:518
  37.7 4.8 %collective-permute-start.16 = (bf16[128,768]{1,0:T(8,128)(2,1)S(1)}, bf16[128,768]{1,0:T(8,128)(2,1)S(1)}, u32[]{:S(2)}, u32[]{:S(2)}) collective-permute-start(bf16[128,768]{1,0:T(8,128)(2,1)S(1)} %collective-permute-done.12.refs_2_), channel_id=1, source_target_pairs={{0,1},{1,0},{2,6},{3,7},{4,5},{5,4},{6,2},{7,3},{8,12},{9,13},{10,... | collective-permute-start | bytes 589832 | tf_op jit(solution)/shard_map/ppermute | solution.py:518
  38.9 3.5 %collective-permute-start.17 = (bf16[128,768]{1,0:T(8,128)(2,1)S(1)}, bf16[128,768]{1,0:T(8,128)(2,1)S(1)}, u32[]{:S(2)}, u32[]{:S(2)}) collective-permute-start(bf16[128,768]{1,0:T(8,128)(2,1)S(1)} %collective-permute-done.13.refs_3_), channel_id=1, source_target_pairs={{0,1},{1,0},{2,3},{3,2},{4,6},{5,7},{6,4},{7,5},{8,9},{9,8},{10,11... | collective-permute-start | bytes 589832 | tf_op jit(solution)/shard_map/ppermute | solution.py:518
  39.6 3.0 %copy-start.1 = (bf16[1536,768]{1,0:T(8,128)(2,1)S(1)}, bf16[1536,768]{1,0:T(8,128)(2,1)}, u32[]{:S(2)}) copy-start(bf16[1536,768]{1,0:T(8,128)(2,1)} %refs_1_.1) | copy-start | bytes 7077892
  42.5 1.8 %collective-permute-start.18 = (bf16[256,768]{1,0:T(8,128)(2,1)S(1)}, bf16[256,768]{1,0:T(8,128)(2,1)S(1)}, u32[]{:S(2)}, u32[]{:S(2)}) collective-permute-start(bf16[256,768]{1,0:T(8,128)(2,1)S(1)} %shard_map.111.depart_ref), channel_id=1, source_target_pairs={{0,1},{1,0},{2,3},{3,2},{4,5},{5,4},{6,7},{7,6},{8,9},{9,8},{10,11... | collective-permute-start | bytes 1179656 | tf_op jit(solution)/shard_map/ppermute | solution.py:506
  47.1 1.8 %collective-permute-start.19 = (bf16[384,411]{1,0:T(8,128)(2,1)S(1)}, bf16[384,411]{1,0:T(8,128)(2,1)S(1)}, u32[]{:S(2)}, u32[]{:S(2)}) collective-permute-start(bf16[384,411]{1,0:T(8,128)(2,1)S(1)} %get-tuple-element.35), channel_id=1, source_target_pairs={{0,1},{1,0},{2,3},{3,2},{4,5},{5,4},{6,7},{7,6},{8,9},{9,8},{10,11... | collective-permute-start | bytes 946952 | tf_op jit(solution)/shard_map/ppermute | solution.py:506
  49.0 7.0 %collective-permute-start.20 = (bf16[96,411]{1,0:T(8,128)(2,1)S(1)}, bf16[96,411]{1,0:T(8,128)(2,1)S(1)}, u32[]{:S(2)}, u32[]{:S(2)}) collective-permute-start(bf16[96,411]{1,0:T(8,128)(2,1)S(1)} %get-tuple-element.36), channel_id=1, source_target_pairs={{0,6},{1,7},{2,4},{3,5},{4,2},{5,3},{6,0},{7,1},{8,14},{9,15},{10,... | collective-permute-start | bytes 236744 | tf_op jit(solution)/shard_map/ppermute | solution.py:506
  52.8 5.2 %collective-permute-start.21 = (bf16[96,411]{1,0:T(8,128)(2,1)S(1)}, bf16[96,411]{1,0:T(8,128)(2,1)S(1)}, u32[]{:S(2)}, u32[]{:S(2)}) collective-permute-start(bf16[96,411]{1,0:T(8,128)(2,1)S(1)} %get-tuple-element.37), channel_id=1, source_target_pairs={{0,4},{1,5},{2,6},{3,7},{4,0},{5,1},{6,2},{7,3},{8,12},{9,13},{10,... | collective-permute-start | bytes 236744 | tf_op jit(solution)/shard_map/ppermute | solution.py:506
  53.1 4.9 %collective-permute-start.22 = (bf16[96,411]{1,0:T(8,128)(2,1)S(1)}, bf16[96,411]{1,0:T(8,128)(2,1)S(1)}, u32[]{:S(2)}, u32[]{:S(2)}) collective-permute-start(bf16[96,411]{1,0:T(8,128)(2,1)S(1)} %get-tuple-element.38), channel_id=1, source_target_pairs={{0,2},{1,3},{2,0},{3,1},{4,6},{5,7},{6,4},{7,5},{8,10},{9,11},{10,... | collective-permute-start | bytes 236744 | tf_op jit(solution)/shard_map/ppermute | solution.py:506
  58.2 5.9 %collective-permute-start.23 = (bf16[32,411]{1,0:T(8,128)(2,1)S(1)}, bf16[32,411]{1,0:T(8,128)(2,1)S(1)}, u32[]{:S(2)}, u32[]{:S(2)}) collective-permute-start(bf16[32,411]{1,0:T(8,128)(2,1)S(1)} %get-tuple-element.40), channel_id=1, source_target_pairs={{0,24},{8,16},{16,8},{24,0},{1,25},{9,17},{17,9},{25,1},{2,26},{10... | collective-permute-start | bytes 78920 | tf_op jit(solution)/shard_map/ppermute | solution.py:509
  59.9 5.1 %collective-permute-start.24 = (bf16[32,411]{1,0:T(8,128)(2,1)S(1)}, bf16[32,411]{1,0:T(8,128)(2,1)S(1)}, u32[]{:S(2)}, u32[]{:S(2)}) collective-permute-start(bf16[32,411]{1,0:T(8,128)(2,1)S(1)} %get-tuple-element.41), channel_id=1, source_target_pairs={{0,16},{8,24},{16,0},{24,8},{1,17},{9,25},{17,1},{25,9},{2,18},{10... | collective-permute-start | bytes 78920 | tf_op jit(solution)/shard_map/ppermute | solution.py:509
  61.4 3.9 %collective-permute-start.25 = (bf16[32,411]{1,0:T(8,128)(2,1)S(1)}, bf16[32,411]{1,0:T(8,128)(2,1)S(1)}, u32[]{:S(2)}, u32[]{:S(2)}) collective-permute-start(bf16[32,411]{1,0:T(8,128)(2,1)S(1)} %get-tuple-element.42), channel_id=1, source_target_pairs={{0,8},{8,0},{16,24},{24,16},{1,9},{9,1},{17,25},{25,17},{2,10},{10... | collective-permute-start | bytes 78920 | tf_op jit(solution)/shard_map/ppermute | solution.py:509

commit v18 on v17

--- a/solution.py
+++ b/solution.py
@@ -445,16 +445,10 @@
     source = lax.broadcasted_iota(jnp.int32, shape, 1)
     column = (cell - edge + 4) // 4
     spread = []
+    terms = [term.astype(jnp.bfloat16) for term in split_three(total)]
     for k in range(3):
         pick = (source == column + k * p.per_row) & (column >= 0) & (column < p.per_row)
-        spread.append(
-            jnp.dot(
-                pick.astype(jnp.float32),
-                total,
-                precision=lax.Precision.HIGHEST,
-                preferred_element_type=jnp.float32,
-            )
-        )
+        spread.append(sum(dot(pick.astype(jnp.bfloat16), term) for term in terms))
     root = root_ref[...]
     state = [spread[(row + 2) // 4] for row in range(p.across + 4)]
     east_of = functools.partial(pltpu.roll, shift=length - 1, axis=0)
@@ -560,7 +554,8 @@
     )
     strips = [strips] + [flip(strips, k) for k in range(1, p.group)]
 
-    near = [w_hidden] + [flip(w_hidden, chip * p.group) for chip in range(1, p.chips)]
+    near = [flip(w_hidden, chip * p.group) for chip in range(p.chips - 1, 0, -1)]
+    near = [w_hidden] + near[::-1]
     near = call(
         functools.partial(stack_kernel, p),
         shape((p.chips * p.deep, p.hidden), half),

time: 66.9 us -> 66.8 us (level)
  no operation moved by 1% of the time
where the time goes in v18:
time: 66.8 us; the launch traced here: 66.7 us
  starting transfers between devices  28.1 us (42%)
  waiting for transfers between devices  27.9 us (42%)
  Pallas kernels  9.8 us (15%)
    ppermute x13, starting transfers between devices, flip(): return lax.ppermute(value, 'chan', [(b, b ^ mask) for b in range(p.chans)])  11.8 us
    ppermute x13, waiting for transfers between devices, flip(): return lax.ppermute(value, 'chan', [(b, b ^ mask) for b in range(p.chans)])  11 us
    ppermute x6, starting transfers between devices, trade(): return lax.ppermute(value, 'tile', [(a, a ^ mask) for a in range(p.tiles)])  10.3 us
    pallas_call x18, Pallas kernels, call(): pl.pallas_call(kernel, out_shape=out_shape, in_specs=[far if k in in_hbm...  9.8 us
    ppermute x7, waiting for transfers between devices, send(): lax.ppermute(value, both, sorted(((number(a), number(b)) for a, b in pair...  8.57 us
    ppermute x6, waiting for transfers between devices, trade(): return lax.ppermute(value, 'tile', [(a, a ^ mask) for a in range(p.tiles)])  8.29 us
    ppermute x7, starting transfers between devices, send(): lax.ppermute(value, both, sorted(((number(a), number(b)) for a, b in pair...  5.98 us
  transfers between devices with their start and end apart: 26, of which 18 were waited for; matrix products, arithmetic and copies ran while one was open for 0% of the time, Pallas kernels for 7%

profile of v18, /device:TPU:0, one launch (start us, length us, event | category | flops | bytes accessed | tf_op | source)
XLA Modules:
  0.0 66.7 jit_solution(5915386288165078)
XLA Ops:
  0.0 3.1 %collective-permute-start.1 = (bf16[128,768]{1,0:T(8,128)(2,1)}, bf16[128,768]{1,0:T(8,128)(2,1)S(1)}, u32[]{:S(2)}, u32[]{:S(2)}) collective-permute-start(bf16[128,768]{1,0:T(8,128)(2,1)} %refs_0_.3), channel_id=1, source_target_pairs={{0,8},{8,0},{16,24},{24,16},{1,9},{9,1},{17,25},{25,17},{2,10},{10... | collective-permute-start | bytes 589832 | tf_op jit(solution)/shard_map/ppermute | solution.py:503
  3.1 1.5 %collective-permute-start.8 = (bf16[411,256]{1,0:T(8,128)(2,1)}, bf16[411,256]{1,0:T(8,128)(2,1)S(1)}, u32[]{:S(2)}, u32[]{:S(2)}) collective-permute-start(bf16[411,256]{1,0:T(8,128)(2,1)} %refs_0_.4), channel_id=1, source_target_pairs={{0,4},{1,5},{2,6},{3,7},{4,0},{5,1},{6,2},{7,3},{8,12},{9,13},{10,... | collective-permute-start | bytes 631304 | tf_op jit(solution)/shard_map/ppermute | solution.py:500
  4.6 1.5 %collective-permute-start.7 = (bf16[411,256]{1,0:T(8,128)(2,1)}, bf16[411,256]{1,0:T(8,128)(2,1)S(1)}, u32[]{:S(2)}, u32[]{:S(2)}) collective-permute-start(bf16[411,256]{1,0:T(8,128)(2,1)} %refs_0_.4), channel_id=1, source_target_pairs={{0,2},{1,3},{2,0},{3,1},{4,6},{5,7},{6,4},{7,5},{8,10},{9,11},{10,... | collective-permute-start | bytes 631304 | tf_op jit(solution)/shard_map/ppermute | solution.py:500
  6.1 0.5 collective-permute-start.9
  6.7 0.0 copy-start.9
  6.7 0.2 shard_map.102.refs_0_
  6.9 0.1 collective-permute-start
  7.0 1.3 %collective-permute-done.1.refs_1_ = bf16[128,768]{1,0:T(8,128)(2,1)S(1)} collective-permute-done((bf16[128,768]{1,0:T(8,128)(2,1)}, bf16[128,768]{1,0:T(8,128)(2,1)S(1)}, u32[]{:S(2)}, u32[]{:S(2)}) %collective-permute-start.1) | collective-permute-done | bytes 196640 | tf_op jit(solution)/shard_map/ppermute | solution.py:503
  8.3 2.4 %collective-permute-done.refs_1_ = bf16[16,512]{1,0:T(8,128)(2,1)S(1)} collective-permute-done((bf16[16,512]{1,0:T(8,128)(2,1)S(1)}, bf16[16,512]{1,0:T(8,128)(2,1)S(1)}, u32[]{:S(2)}, u32[]{:S(2)}) %collective-permute-start) | collective-permute-done | bytes 16416 | tf_op jit(solution)/shard_map/ppermute | solution.py:503
  10.6 2.7 %collective-permute-start.2 = (bf16[32,512]{1,0:T(8,128)(2,1)S(1)}, bf16[32,512]{1,0:T(8,128)(2,1)S(1)}, u32[]{:S(2)}, u32[]{:S(2)}) collective-permute-start(bf16[32,512]{1,0:T(8,128)(2,1)S(1)} %shard_map.104.refs_0_), channel_id=1, source_target_pairs={{0,16},{8,24},{16,0},{24,8},{1,17},{9,25},{17,1},{25,9},{2,18},{10... | collective-permute-start | bytes 98312 | tf_op jit(solution)/shard_map/ppermute | solution.py:503
  13.3 2.1 %collective-permute-done.2.refs_1_ = bf16[32,512]{1,0:T(8,128)(2,1)S(1)} collective-permute-done((bf16[32,512]{1,0:T(8,128)(2,1)S(1)}, bf16[32,512]{1,0:T(8,128)(2,1)S(1)}, u32[]{:S(2)}, u32[]{:S(2)}) %collective-permute-start.2) | collective-permute-done | bytes 32800 | tf_op jit(solution)/shard_map/ppermute | solution.py:503
  15.5 0.0 collective-permute-done.8.refs_2_
  15.5 0.0 collective-permute-done.7.refs_1_
  15.5 0.3 collective-permute-done.9.refs_3_
  15.8 0.1 shard_map.107.refs_7_.refs_5_
  15.9 0.1 collective-permute-start.10
  15.9 2.7 %collective-permute-start.11 = (bf16[256,768]{1,0:T(8,128)(2,1)S(1)}, bf16[256,768]{1,0:T(8,128)(2,1)S(1)}, u32[]{:S(2)}, u32[]{:S(2)}) collective-permute-start(bf16[256,768]{1,0:T(8,128)(2,1)S(1)} %shard_map.103.refs_2_.refs_0_), channel_id=1, source_target_pairs={{0,16},{1,17},{2,3},{3,2},{4,20},{5,21},{6,7},{7,6},{8,9},{9,8},{1... | collective-permute-start | bytes 1179656 | tf_op jit(solution)/shard_map/ppermute | solution.py:512
  18.6 0.3 collective-permute-start.5
  18.9 1.2 %collective-permute-start.4 = (bf16[64,512]{1,0:T(8,128)(2,1)S(1)}, bf16[64,512]{1,0:T(8,128)(2,1)S(1)}, u32[]{:S(2)}, u32[]{:S(2)}) collective-permute-start(bf16[64,512]{1,0:T(8,128)(2,1)S(1)} %shard_map.105.refs_0_.refs_4_), channel_id=1, source_target_pairs={{0,4},{1,5},{2,6},{3,7},{4,0},{5,1},{6,2},{7,3},{8,12},{9,13},{10,... | collective-permute-start | bytes 196616 | tf_op jit(solution)/shard_map/ppermute | solution.py:500
  20.1 2.0 %collective-permute-start.3 = (bf16[64,512]{1,0:T(8,128)(2,1)S(1)}, bf16[64,512]{1,0:T(8,128)(2,1)S(1)}, u32[]{:S(2)}, u32[]{:S(2)}) collective-permute-start(bf16[64,512]{1,0:T(8,128)(2,1)S(1)} %shard_map.105.refs_0_.refs_4_), channel_id=1, source_target_pairs={{0,2},{1,3},{2,0},{3,1},{4,6},{5,7},{6,4},{7,5},{8,10},{9,11},{10,... | collective-permute-start | bytes 196616 | tf_op jit(solution)/shard_map/ppermute | solution.py:500
  22.1 2.0 %collective-permute-done.5.refs_3_ = bf16[64,512]{1,0:T(8,128)(2,1)S(1)} collective-permute-done((bf16[64,512]{1,0:T(8,128)(2,1)S(1)}, bf16[64,512]{1,0:T(8,128)(2,1)S(1)}, u32[]{:S(2)}, u32[]{:S(2)}) %collective-permute-start.5) | collective-permute-done | bytes 65568 | tf_op jit(solution)/shard_map/ppermute | solution.py:500
  24.1 0.3 collective-permute-done.4.refs_2_
  24.4 0.8 %collective-permute-done.3.refs_1_ = bf16[64,512]{1,0:T(8,128)(2,1)S(1)} collective-permute-done((bf16[64,512]{1,0:T(8,128)(2,1)S(1)}, bf16[64,512]{1,0:T(8,128)(2,1)S(1)}, u32[]{:S(2)}, u32[]{:S(2)}) %collective-permute-start.3) | collective-permute-done | bytes 65568 | tf_op jit(solution)/shard_map/ppermute | solution.py:500
  25.2 0.1 collective-permute-start.6
  25.2 0.0 copy-start
  25.3 0.0 copy-start.5
  25.3 0.8 %shard_map.100 = (s32[256,1]{1,0:T(8,128)S(1)}, s32[256,1]{1,0:T(8,128)S(1)}, s32[384,1]{1,0:T(8,128)S(1)}, s32[384,1]{1,0:T(8,128)S(1)}) custom-call(s32[1,256]{1,0:T(1,128)S(1)} %bitcast.12), custom_call_target="tpu_custom_call" | custom-call | flops 2000000000 | bytes 1024 | tf_op jit(solution)/shard_map/pallas_call | solution.py:164
  26.1 0.7 collective-permute-done.6.refs_6_
  26.8 0.4 copy-done
  27.1 2.3 %shard_map.108 = (f32[256,768]{1,0:T(8,128)S(1)}, f32[256,1]{1,0:T(8,128)S(1)}, f32[8,256,256]{2,1,0:T(8,128)S(1)}, f32[24,128]{1,0:T(8,128)S(1)}) custom-call(s32[256,1]{1,0:T(8,128)S(1)} %get-tuple-element.25.refs_0_.place_ref, s32[256,1]{1,0:T(8,128)S(1)} %get-tuple-element.26.refs_1_, s32[24,1]{1,0:T(8,128)S(1)} %shard_map.101.after_ref.refs_2_, ...), custom_call_target="tpu_custom_call" | custom-call | flops 100000000 | bytes 5379168 | tf_op jit(solution)/shard_map/pallas_call | solution.py:164
  29.5 0.4 shard_map.110
  29.9 1.3 %collective-permute-start.12 = (bf16[128,768]{1,0:T(8,128)(2,1)S(1)}, bf16[128,768]{1,0:T(8,128)(2,1)S(1)}, u32[]{:S(2)}, u32[]{:S(2)}) collective-permute-start(bf16[128,768]{1,0:T(8,128)(2,1)S(1)} %get-tuple-element.30.refs_0_), channel_id=1, source_target_pairs={{0,2},{1,3},{2,0},{3,1},{4,5},{5,4},{6,7},{7,6},{8,10},{9,11},{10,... | collective-permute-start | bytes 589832 | tf_op jit(solution)/shard_map/ppermute | solution.py:512
  31.2 0.0 collective-permute-start.13
  31.2 2.0 %collective-permute-start.14 = (bf16[128,768]{1,0:T(8,128)(2,1)S(1)}, bf16[128,768]{1,0:T(8,128)(2,1)S(1)}, u32[]{:S(2)}, u32[]{:S(2)}) collective-permute-start(bf16[128,768]{1,0:T(8,128)(2,1)S(1)} %get-tuple-element.30.refs_0_), channel_id=1, source_target_pairs={{0,4},{1,5},{2,3},{3,2},{4,0},{5,1},{6,7},{7,6},{8,9},{9,8},{10,14... | collective-permute-start | bytes 589832 | tf_op jit(solution)/shard_map/ppermute | solution.py:512
  33.2 4.4 %collective-permute-done.12.refs_2_ = bf16[128,768]{1,0:T(8,128)(2,1)S(1)} collective-permute-done((bf16[128,768]{1,0:T(8,128)(2,1)S(1)}, bf16[128,768]{1,0:T(8,128)(2,1)S(1)}, u32[]{:S(2)}, u32[]{:S(2)}) %collective-permute-start.12) | collective-permute-done | bytes 196640 | tf_op jit(solution)/shard_map/ppermute | solution.py:512
  37.7 1.3 %collective-permute-done.13.refs_3_ = bf16[128,768]{1,0:T(8,128)(2,1)S(1)} collective-permute-done((bf16[128,768]{1,0:T(8,128)(2,1)S(1)}, bf16[128,768]{1,0:T(8,128)(2,1)S(1)}, u32[]{:S(2)}, u32[]{:S(2)}) %collective-permute-start.13) | collective-permute-done | bytes 196640 | tf_op jit(solution)/shard_map/ppermute | solution.py:512
  38.9 0.6 shard_map.109.refs_8_.refs_2_
  39.6 0.0 copy-start.1
  39.6 2.9 %collective-permute-done.14.refs_4_ = bf16[128,768]{1,0:T(8,128)(2,1)S(1)} collective-permute-done((bf16[128,768]{1,0:T(8,128)(2,1)S(1)}, bf16[128,768]{1,0:T(8,128)(2,1)S(1)}, u32[]{:S(2)}, u32[]{:S(2)}) %collective-permute-start.14) | collective-permute-done | bytes 196640 | tf_op jit(solution)/shard_map/ppermute | solution.py:512
  42.4 0.1 shard_map.111.depart_ref
  42.5 0.1 collective-permute-start.18
  42.6 0.5 shard_map.112.refs_3_
  43.1 1.2 %collective-permute-done.18.refs_4_ = bf16[256,768]{1,0:T(8,128)(2,1)S(1)} collective-permute-done((bf16[256,768]{1,0:T(8,128)(2,1)S(1)}, bf16[256,768]{1,0:T(8,128)(2,1)S(1)}, u32[]{:S(2)}, u32[]{:S(2)}) %collective-permute-start.18) | collective-permute-done | bytes 393248 | tf_op jit(solution)/shard_map/ppermute | solution.py:500
  44.3 2.8 %shard_map.113 = (bf16[411,256]{1,0:T(8,128)(2,1)S(1)}, bf16[384,411]{1,0:T(8,128)(2,1)S(1)}) custom-call(bf16[2048,768]{1,0:T(8,128)(2,1)S(1)} %copy-done, bf16[1536,768]{1,0:T(8,128)(2,1)S(1)} %copy-done.1, f32[8,256,256]{2,1,0:T(8,128)S(1)} %shard_map.109.refs_8_.refs_2_, f32[256,768]{1,0:T(8,128)S(1)} %shard_map.112.refs_3_, ...), custom_call_target="tpu_custom_call" | custom-call | flops 1840250880 | bytes 10487296 | tf_op jit(solution)/shard_map/pallas_call | solution.py:164
  47.1 0.2 collective-permute-start.19
  47.3 0.1 slice_bitcast_fusion.2
  47.4 0.3 shard_map.114.refs_0_
  47.7 1.2 %collective-permute-done.19.refs_1_ = bf16[384,411]{1,0:T(8,128)(2,1)S(1)} collective-permute-done((bf16[384,411]{1,0:T(8,128)(2,1)S(1)}, bf16[384,411]{1,0:T(8,128)(2,1)S(1)}, u32[]{:S(2)}, u32[]{:S(2)}) %collective-permute-start.19) | collective-permute-done | bytes 315680 | tf_op jit(solution)/shard_map/ppermute | solution.py:500
  48.9 0.1 shard_map.115
  49.0 3.8 %collective-permute-start.20 = (bf16[96,411]{1,0:T(8,128)(2,1)S(1)}, bf16[96,411]{1,0:T(8,128)(2,1)S(1)}, u32[]{:S(2)}, u32[]{:S(2)}) collective-permute-start(bf16[96,411]{1,0:T(8,128)(2,1)S(1)} %get-tuple-element.36), channel_id=1, source_target_pairs={{0,6},{1,7},{2,4},{3,5},{4,2},{5,3},{6,0},{7,1},{8,14},{9,15},{10,... | collective-permute-start | bytes 236744 | tf_op jit(solution)/shard_map/ppermute | solution.py:500
  52.8 0.3 collective-permute-start.21
  53.1 0.4 collective-permute-start.22
  53.4 2.6 %collective-permute-done.20.refs_0_ = bf16[96,411]{1,0:T(8,128)(2,1)S(1)} collective-permute-done((bf16[96,411]{1,0:T(8,128)(2,1)S(1)}, bf16[96,411]{1,0:T(8,128)(2,1)S(1)}, u32[]{:S(2)}, u32[]{:S(2)}) %collective-permute-start.20) | collective-permute-done | bytes 78944 | tf_op jit(solution)/shard_map/ppermute | solution.py:500
  56.0 2.0 %collective-permute-done.21.refs_1_ = bf16[96,411]{1,0:T(8,128)(2,1)S(1)} collective-permute-done((bf16[96,411]{1,0:T(8,128)(2,1)S(1)}, bf16[96,411]{1,0:T(8,128)(2,1)S(1)}, u32[]{:S(2)}, u32[]{:S(2)}) %collective-permute-start.21) | collective-permute-done | bytes 78944 | tf_op jit(solution)/shard_map/ppermute | solution.py:500
  58.0 0.2 shard_map.116
  58.2 1.7 %collective-permute-start.23 = (bf16[32,411]{1,0:T(8,128)(2,1)S(1)}, bf16[32,411]{1,0:T(8,128)(2,1)S(1)}, u32[]{:S(2)}, u32[]{:S(2)}) collective-permute-start(bf16[32,411]{1,0:T(8,128)(2,1)S(1)} %get-tuple-element.40), channel_id=1, source_target_pairs={{0,24},{8,16},{16,8},{24,0},{1,25},{9,17},{17,9},{25,1},{2,26},{10... | collective-permute-start | bytes 78920 | tf_op jit(solution)/shard_map/ppermute | solution.py:503
  59.9 1.5 %collective-permute-start.24 = (bf16[32,411]{1,0:T(8,128)(2,1)S(1)}, bf16[32,411]{1,0:T(8,128)(2,1)S(1)}, u32[]{:S(2)}, u32[]{:S(2)}) collective-permute-start(bf16[32,411]{1,0:T(8,128)(2,1)S(1)} %get-tuple-element.41), channel_id=1, source_target_pairs={{0,16},{8,24},{16,0},{24,8},{1,17},{9,25},{17,1},{25,9},{2,18},{10... | collective-permute-start | bytes 78920 | tf_op jit(solution)/shard_map/ppermute | solution.py:503
  61.4 1.2 %collective-permute-start.25 = (bf16[32,411]{1,0:T(8,128)(2,1)S(1)}, bf16[32,411]{1,0:T(8,128)(2,1)S(1)}, u32[]{:S(2)}, u32[]{:S(2)}) collective-permute-start(bf16[32,411]{1,0:T(8,128)(2,1)S(1)} %get-tuple-element.42), channel_id=1, source_target_pairs={{0,8},{8,0},{16,24},{24,16},{1,9},{9,1},{17,25},{25,17},{2,10},{10... | collective-permute-start | bytes 78920 | tf_op jit(solution)/shard_map/ppermute | solution.py:503
  62.7 0.1 maximum_sqrt_fusion
  62.8 0.1 copy.19
  62.8 1.3 %collective-permute-done.23.refs_0_ = bf16[32,411]{1,0:T(8,128)(2,1)S(1)} collective-permute-done((bf16[32,411]{1,0:T(8,128)(2,1)S(1)}, bf16[32,411]{1,0:T(8,128)(2,1)S(1)}, u32[]{:S(2)}, u32[]{:S(2)}) %collective-permute-start.23) | collective-permute-done | bytes 26336 | tf_op jit(solution)/shard_map/ppermute | solution.py:503
  64.1 0.9 %collective-permute-done.24.refs_1_ = bf16[32,411]{1,0:T(8,128)(2,1)S(1)} collective-permute-done((bf16[32,411]{1,0:T(8,128)(2,1)S(1)}, bf16[32,411]{1,0:T(8,128)(2,1)S(1)}, u32[]{:S(2)}, u32[]{:S(2)}) %collective-permute-start.24) | collective-permute-done | bytes 26336 | tf_op jit(solution)/shard_map/ppermute | solution.py:503
  65.0 0.4 collective-permute-done.25.refs_2_
  65.4 1.3 %shard_map.117 = f32[4,32,411]{2,1,0:T(8,128)} custom-call(bf16[32,411]{1,0:T(8,128)(2,1)S(1)} %collective-permute-done.23.refs_0_, bf16[32,411]{1,0:T(8,128)(2,1)S(1)} %collective-permute-done.24.refs_1_, bf16[32,411]{1,0:T(8,128)(2,1)S(1)} %collective-permute-done.25.refs_2_, bf16[32,411]{1,0:T(8,128)(2,1)S(1)} %get-tuple-element.43.refs_3_, ...), custom_call_target="tpu_custom_call" | custom-call | flops 5260800 | bytes 106752 | tf_op jit(solution)/shard_map/pallas_call | solution.py:164
  (30 shorter events, 0.2 us)
Async XLA Ops:
  0.0 8.2 %copy-start.4 = (bf16[128,768]{1,0:T(8,128)(2,1)S(1)}, bf16[128,768]{1,0:T(8,128)(2,1)}, u32[]{:S(2)}) copy-start(bf16[128,768]{1,0:T(8,128)(2,1)} %refs_0_.3) | copy-start | bytes 589828
  0.0 15.8 %copy-start.3 = (bf16[411,256]{1,0:T(8,128)(2,1)S(1)}, bf16[411,256]{1,0:T(8,128)(2,1)}, u32[]{:S(2)}) copy-start(bf16[411,256]{1,0:T(8,128)(2,1)} %refs_0_.4) | copy-start | bytes 631300
  0.0 6.7 %copy-start.7 = (f32[256]{0:T(256)S(1)}, f32[256]{0:T(256)}, u32[]{:S(2)}) copy-start(f32[256]{0:T(256)} %bias_ref.1) | copy-start | bytes 3076
  0.0 6.7 %copy-start.8 = (s32[128]{0:T(128)S(1)}, s32[128]{0:T(128)}, u32[]{:S(2)}) copy-start(s32[128]{0:T(128)} %usable_ref.1) | copy-start | bytes 1540
  0.0 6.7 %copy-start.6 = (f32[4,32]{1,0:T(4,128)S(1)}, f32[4,32]{1,0:T(4,128)}, u32[]{:S(2)}) copy-start(f32[4,32]{1,0:T(4,128)} %diffusivity_ref.1) | copy-start | bytes 1540
  0.0 6.7 %copy-start.2 = (f32[4,32,411]{2,1,0:T(8,128)S(1)}, f32[4,32,411]{2,1,0:T(8,128)}, u32[]{:S(2)}) copy-start(f32[4,32,411]{2,1,0:T(8,128)} %fields_ref.1) | copy-start | bytes 631300
  0.0 8.2 %collective-permute-start.1 = (bf16[128,768]{1,0:T(8,128)(2,1)}, bf16[128,768]{1,0:T(8,128)(2,1)S(1)}, u32[]{:S(2)}, u32[]{:S(2)}) collective-permute-start(bf16[128,768]{1,0:T(8,128)(2,1)} %refs_0_.3), channel_id=1, source_target_pairs={{0,8},{8,0},{16,24},{24,16},{1,9},{9,1},{17,25},{25,17},{2,10},{10... | collective-permute-start | bytes 589832 | tf_op jit(solution)/shard_map/ppermute | solution.py:503
  3.1 12.3 %collective-permute-start.8 = (bf16[411,256]{1,0:T(8,128)(2,1)}, bf16[411,256]{1,0:T(8,128)(2,1)S(1)}, u32[]{:S(2)}, u32[]{:S(2)}) collective-permute-start(bf16[411,256]{1,0:T(8,128)(2,1)} %refs_0_.4), channel_id=1, source_target_pairs={{0,4},{1,5},{2,6},{3,7},{4,0},{5,1},{6,2},{7,3},{8,12},{9,13},{10,... | collective-permute-start | bytes 631304 | tf_op jit(solution)/shard_map/ppermute | solution.py:500
  4.6 10.8 %collective-permute-start.7 = (bf16[411,256]{1,0:T(8,128)(2,1)}, bf16[411,256]{1,0:T(8,128)(2,1)S(1)}, u32[]{:S(2)}, u32[]{:S(2)}) collective-permute-start(bf16[411,256]{1,0:T(8,128)(2,1)} %refs_0_.4), channel_id=1, source_target_pairs={{0,2},{1,3},{2,0},{3,1},{4,6},{5,7},{6,4},{7,5},{8,10},{9,11},{10,... | collective-permute-start | bytes 631304 | tf_op jit(solution)/shard_map/ppermute | solution.py:500
  6.1 9.7 %collective-permute-start.9 = (bf16[411,256]{1,0:T(8,128)(2,1)}, bf16[411,256]{1,0:T(8,128)(2,1)S(1)}, u32[]{:S(2)}, u32[]{:S(2)}) collective-permute-start(bf16[411,256]{1,0:T(8,128)(2,1)} %refs_0_.4), channel_id=1, source_target_pairs={{0,6},{1,7},{2,4},{3,5},{4,2},{5,3},{6,0},{7,1},{8,14},{9,15},{10,... | collective-permute-start | bytes 631304 | tf_op jit(solution)/shard_map/ppermute | solution.py:500
  6.7 18.5 %copy-start.9 = (s32[256,1]{0,1:T(1,128)S(1)}, s32[256,1]{0,1:T(1,128)}, u32[]{:S(2)}) copy-start(s32[256,1]{0,1:T(1,128)} %param.12) | copy-start | bytes 3076
  6.9 3.7 %collective-permute-start = (bf16[16,512]{1,0:T(8,128)(2,1)S(1)}, bf16[16,512]{1,0:T(8,128)(2,1)S(1)}, u32[]{:S(2)}, u32[]{:S(2)}) collective-permute-start(bf16[16,512]{1,0:T(8,128)(2,1)S(1)} %shard_map.102.refs_0_), channel_id=1, source_target_pairs={{0,8},{8,0},{16,24},{24,16},{1,9},{9,1},{17,25},{25,17},{2,10},{10... | collective-permute-start | bytes 49160 | tf_op jit(solution)/shard_map/ppermute | solution.py:503
  10.6 4.8 %collective-permute-start.2 = (bf16[32,512]{1,0:T(8,128)(2,1)S(1)}, bf16[32,512]{1,0:T(8,128)(2,1)S(1)}, u32[]{:S(2)}, u32[]{:S(2)}) collective-permute-start(bf16[32,512]{1,0:T(8,128)(2,1)S(1)} %shard_map.104.refs_0_), channel_id=1, source_target_pairs={{0,16},{8,24},{16,0},{24,8},{1,17},{9,25},{17,1},{25,9},{2,18},{10... | collective-permute-start | bytes 98312 | tf_op jit(solution)/shard_map/ppermute | solution.py:503
  15.9 10.9 %collective-permute-start.10 = (bf16[1664,256]{1,0:T(8,128)(2,1)S(1)}, bf16[1664,256]{1,0:T(8,128)(2,1)S(1)}, u32[]{:S(2)}, u32[]{:S(2)}) collective-permute-start(bf16[1664,256]{1,0:T(8,128)(2,1)S(1)} %shard_map.107.refs_7_.refs_5_), channel_id=1, source_target_pairs={{0,1},{1,0},{2,3},{3,2},{4,5},{5,4},{6,7},{7,6},{8,9},{9,8},{10,11... | collective-permute-start | bytes 2555912 | tf_op jit(solution)/shard_map/ppermute | solution.py:500
  15.9 13.5 %collective-permute-start.11 = (bf16[256,768]{1,0:T(8,128)(2,1)S(1)}, bf16[256,768]{1,0:T(8,128)(2,1)S(1)}, u32[]{:S(2)}, u32[]{:S(2)}) collective-permute-start(bf16[256,768]{1,0:T(8,128)(2,1)S(1)} %shard_map.103.refs_2_.refs_0_), channel_id=1, source_target_pairs={{0,16},{1,17},{2,3},{3,2},{4,20},{5,21},{6,7},{7,6},{8,9},{9,8},{1... | collective-permute-start | bytes 1179656 | tf_op jit(solution)/shard_map/ppermute | solution.py:512
  18.6 5.5 %collective-permute-start.5 = (bf16[64,512]{1,0:T(8,128)(2,1)S(1)}, bf16[64,512]{1,0:T(8,128)(2,1)S(1)}, u32[]{:S(2)}, u32[]{:S(2)}) collective-permute-start(bf16[64,512]{1,0:T(8,128)(2,1)S(1)} %shard_map.105.refs_0_.refs_4_), channel_id=1, source_target_pairs={{0,6},{1,7},{2,4},{3,5},{4,2},{5,3},{6,0},{7,1},{8,14},{9,15},{10,... | collective-permute-start | bytes 196616 | tf_op jit(solution)/shard_map/ppermute | solution.py:500
  18.9 5.5 %collective-permute-start.4 = (bf16[64,512]{1,0:T(8,128)(2,1)S(1)}, bf16[64,512]{1,0:T(8,128)(2,1)S(1)}, u32[]{:S(2)}, u32[]{:S(2)}) collective-permute-start(bf16[64,512]{1,0:T(8,128)(2,1)S(1)} %shard_map.105.refs_0_.refs_4_), channel_id=1, source_target_pairs={{0,4},{1,5},{2,6},{3,7},{4,0},{5,1},{6,2},{7,3},{8,12},{9,13},{10,... | collective-permute-start | bytes 196616 | tf_op jit(solution)/shard_map/ppermute | solution.py:500
  20.1 5.0 %collective-permute-start.3 = (bf16[64,512]{1,0:T(8,128)(2,1)S(1)}, bf16[64,512]{1,0:T(8,128)(2,1)S(1)}, u32[]{:S(2)}, u32[]{:S(2)}) collective-permute-start(bf16[64,512]{1,0:T(8,128)(2,1)S(1)} %shard_map.105.refs_0_.refs_4_), channel_id=1, source_target_pairs={{0,2},{1,3},{2,0},{3,1},{4,6},{5,7},{6,4},{7,5},{8,10},{9,11},{10,... | collective-permute-start | bytes 196616 | tf_op jit(solution)/shard_map/ppermute | solution.py:500
  25.2 1.6 %collective-permute-start.6 = (bf16[256,512]{1,0:T(8,128)(2,1)S(1)}, bf16[256,512]{1,0:T(8,128)(2,1)S(1)}, u32[]{:S(2)}, u32[]{:S(2)}) collective-permute-start(bf16[256,512]{1,0:T(8,128)(2,1)S(1)} %shard_map.106.refs_5_), channel_id=1, source_target_pairs={{0,1},{1,0},{2,3},{3,2},{4,5},{5,4},{6,7},{7,6},{8,9},{9,8},{10,11... | collective-permute-start | bytes 786440 | tf_op jit(solution)/shard_map/ppermute | solution.py:500
  25.2 1.9 %copy-start = (bf16[2048,768]{1,0:T(8,128)(2,1)S(1)}, bf16[2048,768]{1,0:T(8,128)(2,1)}, u32[]{:S(2)}) copy-start(bf16[2048,768]{1,0:T(8,128)(2,1)} %refs_0_.5) | copy-start | bytes 9437188
  25.3 1.9 %copy-start.5 = (f32[768]{0:T(1024)S(1)}, f32[768]{0:T(1024)}, u32[]{:S(2)}) copy-start(f32[768]{0:T(1024)} %refs_3_.1) | copy-start | bytes 9220
  29.9 7.8 %collective-permute-start.12 = (bf16[128,768]{1,0:T(8,128)(2,1)S(1)}, bf16[128,768]{1,0:T(8,128)(2,1)S(1)}, u32[]{:S(2)}, u32[]{:S(2)}) collective-permute-start(bf16[128,768]{1,0:T(8,128)(2,1)S(1)} %get-tuple-element.30.refs_0_), channel_id=1, source_target_pairs={{0,2},{1,3},{2,0},{3,1},{4,5},{5,4},{6,7},{7,6},{8,10},{9,11},{10,... | collective-permute-start | bytes 589832 | tf_op jit(solution)/shard_map/ppermute | solution.py:512
  31.2 7.7 %collective-permute-start.13 = (bf16[128,768]{1,0:T(8,128)(2,1)S(1)}, bf16[128,768]{1,0:T(8,128)(2,1)S(1)}, u32[]{:S(2)}, u32[]{:S(2)}) collective-permute-start(bf16[128,768]{1,0:T(8,128)(2,1)S(1)} %get-tuple-element.31.refs_1_), channel_id=1, source_target_pairs={{0,4},{1,5},{2,3},{3,2},{4,0},{5,1},{6,7},{7,6},{8,9},{9,8},{10,14... | collective-permute-start | bytes 589832 | tf_op jit(solution)/shard_map/ppermute | solution.py:512
  31.2 11.2 %collective-permute-start.14 = (bf16[128,768]{1,0:T(8,128)(2,1)S(1)}, bf16[128,768]{1,0:T(8,128)(2,1)S(1)}, u32[]{:S(2)}, u32[]{:S(2)}) collective-permute-start(bf16[128,768]{1,0:T(8,128)(2,1)S(1)} %get-tuple-element.30.refs_0_), channel_id=1, source_target_pairs={{0,4},{1,5},{2,3},{3,2},{4,0},{5,1},{6,7},{7,6},{8,9},{9,8},{10,14... | collective-permute-start | bytes 589832 | tf_op jit(solution)/shard_map/ppermute | solution.py:512
  33.2 9.2 %collective-permute-start.15 = (bf16[128,768]{1,0:T(8,128)(2,1)S(1)}, bf16[128,768]{1,0:T(8,128)(2,1)S(1)}, u32[]{:S(2)}, u32[]{:S(2)}) collective-permute-start(bf16[128,768]{1,0:T(8,128)(2,1)S(1)} %get-tuple-element.31.refs_1_), channel_id=1, source_target_pairs={{0,2},{1,3},{2,0},{3,1},{4,5},{5,4},{6,7},{7,6},{8,10},{9,11},{10,... | collective-permute-start | bytes 589832 | tf_op jit(solution)/shard_map/ppermute | solution.py:512
  37.7 4.8 %collective-permute-start.16 = (bf16[128,768]{1,0:T(8,128)(2,1)S(1)}, bf16[128,768]{1,0:T(8,128)(2,1)S(1)}, u32[]{:S(2)}, u32[]{:S(2)}) collective-permute-start(bf16[128,768]{1,0:T(8,128)(2,1)S(1)} %collective-permute-done.12.refs_2_), channel_id=1, source_target_pairs={{0,1},{1,0},{2,6},{3,7},{4,5},{5,4},{6,2},{7,3},{8,12},{9,13},{10,... | collective-permute-start | bytes 589832 | tf_op jit(solution)/shard_map/ppermute | solution.py:512
  38.9 3.5 %collective-permute-start.17 = (bf16[128,768]{1,0:T(8,128)(2,1)S(1)}, bf16[128,768]{1,0:T(8,128)(2,1)S(1)}, u32[]{:S(2)}, u32[]{:S(2)}) collective-permute-start(bf16[128,768]{1,0:T(8,128)(2,1)S(1)} %collective-permute-done.13.refs_3_), channel_id=1, source_target_pairs={{0,1},{1,0},{2,3},{3,2},{4,6},{5,7},{6,4},{7,5},{8,9},{9,8},{10,11... | collective-permute-start | bytes 589832 | tf_op jit(solution)/shard_map/ppermute | solution.py:512
  39.6 3.0 %copy-start.1 = (bf16[1536,768]{1,0:T(8,128)(2,1)S(1)}, bf16[1536,768]{1,0:T(8,128)(2,1)}, u32[]{:S(2)}) copy-start(bf16[1536,768]{1,0:T(8,128)(2,1)} %refs_1_.1) | copy-start | bytes 7077892
  42.5 1.8 %collective-permute-start.18 = (bf16[256,768]{1,0:T(8,128)(2,1)S(1)}, bf16[256,768]{1,0:T(8,128)(2,1)S(1)}, u32[]{:S(2)}, u32[]{:S(2)}) collective-permute-start(bf16[256,768]{1,0:T(8,128)(2,1)S(1)} %shard_map.111.depart_ref), channel_id=1, source_target_pairs={{0,1},{1,0},{2,3},{3,2},{4,5},{5,4},{6,7},{7,6},{8,9},{9,8},{10,11... | collective-permute-start | bytes 1179656 | tf_op jit(solution)/shard_map/ppermute | solution.py:500
  47.1 1.8 %collective-permute-start.19 = (bf16[384,411]{1,0:T(8,128)(2,1)S(1)}, bf16[384,411]{1,0:T(8,128)(2,1)S(1)}, u32[]{:S(2)}, u32[]{:S(2)}) collective-permute-start(bf16[384,411]{1,0:T(8,128)(2,1)S(1)} %get-tuple-element.35), channel_id=1, source_target_pairs={{0,1},{1,0},{2,3},{3,2},{4,5},{5,4},{6,7},{7,6},{8,9},{9,8},{10,11... | collective-permute-start | bytes 946952 | tf_op jit(solution)/shard_map/ppermute | solution.py:500
  49.0 7.0 %collective-permute-start.20 = (bf16[96,411]{1,0:T(8,128)(2,1)S(1)}, bf16[96,411]{1,0:T(8,128)(2,1)S(1)}, u32[]{:S(2)}, u32[]{:S(2)}) collective-permute-start(bf16[96,411]{1,0:T(8,128)(2,1)S(1)} %get-tuple-element.36), channel_id=1, source_target_pairs={{0,6},{1,7},{2,4},{3,5},{4,2},{5,3},{6,0},{7,1},{8,14},{9,15},{10,... | collective-permute-start | bytes 236744 | tf_op jit(solution)/shard_map/ppermute | solution.py:500
  52.8 5.2 %collective-permute-start.21 = (bf16[96,411]{1,0:T(8,128)(2,1)S(1)}, bf16[96,411]{1,0:T(8,128)(2,1)S(1)}, u32[]{:S(2)}, u32[]{:S(2)}) collective-permute-start(bf16[96,411]{1,0:T(8,128)(2,1)S(1)} %get-tuple-element.37), channel_id=1, source_target_pairs={{0,4},{1,5},{2,6},{3,7},{4,0},{5,1},{6,2},{7,3},{8,12},{9,13},{10,... | collective-permute-start | bytes 236744 | tf_op jit(solution)/shard_map/ppermute | solution.py:500
  53.1 4.9 %collective-permute-start.22 = (bf16[96,411]{1,0:T(8,128)(2,1)S(1)}, bf16[96,411]{1,0:T(8,128)(2,1)S(1)}, u32[]{:S(2)}, u32[]{:S(2)}) collective-permute-start(bf16[96,411]{1,0:T(8,128)(2,1)S(1)} %get-tuple-element.38), channel_id=1, source_target_pairs={{0,2},{1,3},{2,0},{3,1},{4,6},{5,7},{6,4},{7,5},{8,10},{9,11},{10,... | collective-permute-start | bytes 236744 | tf_op jit(solution)/shard_map/ppermute | solution.py:500
  58.2 5.9 %collective-permute-start.23 = (bf16[32,411]{1,0:T(8,128)(2,1)S(1)}, bf16[32,411]{1,0:T(8,128)(2,1)S(1)}, u32[]{:S(2)}, u32[]{:S(2)}) collective-permute-start(bf16[32,411]{1,0:T(8,128)(2,1)S(1)} %get-tuple-element.40), channel_id=1, source_target_pairs={{0,24},{8,16},{16,8},{24,0},{1,25},{9,17},{17,9},{25,1},{2,26},{10... | collective-permute-start | bytes 78920 | tf_op jit(solution)/shard_map/ppermute | solution.py:503
  59.9 5.1 %collective-permute-start.24 = (bf16[32,411]{1,0:T(8,128)(2,1)S(1)}, bf16[32,411]{1,0:T(8,128)(2,1)S(1)}, u32[]{:S(2)}, u32[]{:S(2)}) collective-permute-start(bf16[32,411]{1,0:T(8,128)(2,1)S(1)} %get-tuple-element.41), channel_id=1, source_target_pairs={{0,16},{8,24},{16,0},{24,8},{1,17},{9,25},{17,1},{25,9},{2,18},{10... | collective-permute-start | bytes 78920 | tf_op jit(solution)/shard_map/ppermute | solution.py:503
  61.4 3.9 %collective-permute-start.25 = (bf16[32,411]{1,0:T(8,128)(2,1)S(1)}, bf16[32,411]{1,0:T(8,128)(2,1)S(1)}, u32[]{:S(2)}, u32[]{:S(2)}) collective-permute-start(bf16[32,411]{1,0:T(8,128)(2,1)S(1)} %get-tuple-element.42), channel_id=1, source_target_pairs={{0,8},{8,0},{16,24},{24,16},{1,9},{9,1},{17,25},{25,17},{2,10},{10... | collective-permute-start | bytes 78920 | tf_op jit(solution)/shard_map/ppermute | solution.py:503

commit v19 on v18

--- a/solution.py
+++ b/solution.py
@@ -507,7 +507,7 @@
         pairs.update({target: source for source, target in wanted.items()})
         for a, b in everyone:
             if (a, b) not in pairs:
-                pairs[a, b] = (a, b ^ 1)
+                pairs[a, b] = (a, b)
         number = lambda place: place[0] * p.chans + place[1]
         return lax.ppermute(
             value, both, sorted((number(a), number(b)) for a, b in pairs.items())

time: 66.8 us -> 76.7 us (1.15)
  starting transfers between devices: 28.1 us -> 41.9 us
  waiting for transfers between devices: 27.9 us -> 23.7 us
    ppermute x7, starting transfers between devices: 5.98 us -> 16.7 us  [send(): lax.ppermute(value, both, sorted(((number(a), number(b)) for a, b in pair...]
    ppermute x7, waiting for transfers between devices: 8.57 us -> 4.43 us  [send(): lax.ppermute(value, both, sorted(((number(a), number(b)) for a, b in pair...]
    ppermute x13, starting transfers between devices: 11.8 us -> 14.9 us  [flip(): return lax.ppermute(value, 'chan', [(b, b ^ mask) for b in range(p.chans)])]
  transfers between devices with their start and end apart: 26 -> 26, of which waited for: 18 -> 18; matrix products, arithmetic and copies ran while one was open for 0% -> 0% of each run, Pallas kernels for 7% -> 6%
where the time goes in v19:
time: 76.7 us; the launch traced here: 76.4 us
  starting transfers between devices  41.9 us (55%)
  waiting for transfers between devices  23.7 us (31%)
  Pallas kernels  9.78 us (13%)
    ppermute x7, starting transfers between devices, send(): lax.ppermute(value, both, sorted(((number(a), number(b)) for a, b in pair...  16.7 us
    ppermute x13, starting transfers between devices, flip(): return lax.ppermute(value, 'chan', [(b, b ^ mask) for b in range(p.chans)])  14.9 us
    ppermute x13, waiting for transfers between devices, flip(): return lax.ppermute(value, 'chan', [(b, b ^ mask) for b in range(p.chans)])  11 us
    ppermute x6, starting transfers between devices, trade(): return lax.ppermute(value, 'tile', [(a, a ^ mask) for a in range(p.tiles)])  10.3 us
    pallas_call x18, Pallas kernels, call(): pl.pallas_call(kernel, out_shape=out_shape, in_specs=[far if k in in_hbm...  9.78 us
    ppermute x6, waiting for transfers between devices, trade(): return lax.ppermute(value, 'tile', [(a, a ^ mask) for a in range(p.tiles)])  8.28 us
    ppermute x7, waiting for transfers between devices, send(): lax.ppermute(value, both, sorted(((number(a), number(b)) for a, b in pair...  4.43 us
  transfers between devices with their start and end apart: 26, of which 18 were waited for; matrix products, arithmetic and copies ran while one was open for 0% of the time, Pallas kernels for 6%

profile of v19, /device:TPU:0, one launch (start us, length us, event | category | flops | bytes accessed | tf_op | source)
XLA Modules:
  0.0 76.4 jit_solution(7525866610306613226)
XLA Ops:
  0.0 3.1 %collective-permute-start.1 = (bf16[128,768]{1,0:T(8,128)(2,1)}, bf16[128,768]{1,0:T(8,128)(2,1)S(1)}, u32[]{:S(2)}, u32[]{:S(2)}) collective-permute-start(bf16[128,768]{1,0:T(8,128)(2,1)} %refs_0_.3), channel_id=1, source_target_pairs={{0,8},{8,0},{16,24},{24,16},{1,9},{9,1},{17,25},{25,17},{2,10},{10... | collective-permute-start | bytes 589832 | tf_op jit(solution)/shard_map/ppermute | solution.py:503
  3.1 1.5 %collective-permute-start.8 = (bf16[411,256]{1,0:T(8,128)(2,1)}, bf16[411,256]{1,0:T(8,128)(2,1)S(1)}, u32[]{:S(2)}, u32[]{:S(2)}) collective-permute-start(bf16[411,256]{1,0:T(8,128)(2,1)} %refs_0_.4), channel_id=1, source_target_pairs={{0,4},{1,5},{2,6},{3,7},{4,0},{5,1},{6,2},{7,3},{8,12},{9,13},{10,... | collective-permute-start | bytes 631304 | tf_op jit(solution)/shard_map/ppermute | solution.py:500
  4.6 1.5 %collective-permute-start.7 = (bf16[411,256]{1,0:T(8,128)(2,1)}, bf16[411,256]{1,0:T(8,128)(2,1)S(1)}, u32[]{:S(2)}, u32[]{:S(2)}) collective-permute-start(bf16[411,256]{1,0:T(8,128)(2,1)} %refs_0_.4), channel_id=1, source_target_pairs={{0,2},{1,3},{2,0},{3,1},{4,6},{5,7},{6,4},{7,5},{8,10},{9,11},{10,... | collective-permute-start | bytes 631304 | tf_op jit(solution)/shard_map/ppermute | solution.py:500
  6.1 0.5 collective-permute-start.9
  6.7 0.0 copy-start.9
  6.7 0.2 shard_map.102.refs_0_
  6.9 0.1 collective-permute-start
  7.0 1.3 %collective-permute-done.1.refs_1_ = bf16[128,768]{1,0:T(8,128)(2,1)S(1)} collective-permute-done((bf16[128,768]{1,0:T(8,128)(2,1)}, bf16[128,768]{1,0:T(8,128)(2,1)S(1)}, u32[]{:S(2)}, u32[]{:S(2)}) %collective-permute-start.1) | collective-permute-done | bytes 196640 | tf_op jit(solution)/shard_map/ppermute | solution.py:503
  8.3 2.4 %collective-permute-done.refs_1_ = bf16[16,512]{1,0:T(8,128)(2,1)S(1)} collective-permute-done((bf16[16,512]{1,0:T(8,128)(2,1)S(1)}, bf16[16,512]{1,0:T(8,128)(2,1)S(1)}, u32[]{:S(2)}, u32[]{:S(2)}) %collective-permute-start) | collective-permute-done | bytes 16416 | tf_op jit(solution)/shard_map/ppermute | solution.py:503
  10.6 2.7 %collective-permute-start.2 = (bf16[32,512]{1,0:T(8,128)(2,1)S(1)}, bf16[32,512]{1,0:T(8,128)(2,1)S(1)}, u32[]{:S(2)}, u32[]{:S(2)}) collective-permute-start(bf16[32,512]{1,0:T(8,128)(2,1)S(1)} %shard_map.104.refs_0_), channel_id=1, source_target_pairs={{0,16},{8,24},{16,0},{24,8},{1,17},{9,25},{17,1},{25,9},{2,18},{10... | collective-permute-start | bytes 98312 | tf_op jit(solution)/shard_map/ppermute | solution.py:503
  13.3 2.1 %collective-permute-done.2.refs_1_ = bf16[32,512]{1,0:T(8,128)(2,1)S(1)} collective-permute-done((bf16[32,512]{1,0:T(8,128)(2,1)S(1)}, bf16[32,512]{1,0:T(8,128)(2,1)S(1)}, u32[]{:S(2)}, u32[]{:S(2)}) %collective-permute-start.2) | collective-permute-done | bytes 32800 | tf_op jit(solution)/shard_map/ppermute | solution.py:503
  15.5 0.3 collective-permute-done.9.refs_3_
  15.8 0.1 shard_map.107.refs_7_.refs_5_
  15.9 0.1 collective-permute-start.10
  15.9 4.5 %collective-permute-start.11 = (bf16[256,768]{1,0:T(8,128)(2,1)S(1)}, bf16[256,768]{1,0:T(8,128)(2,1)S(1)}, u32[]{:S(2)}, u32[]{:S(2)}) collective-permute-start(bf16[256,768]{1,0:T(8,128)(2,1)S(1)} %shard_map.103.refs_2_.refs_0_), channel_id=1, source_target_pairs={{0,16},{1,17},{2,2},{3,3},{4,20},{5,21},{6,6},{7,7},{8,8},{9,9},{1... | collective-permute-start | bytes 1179656 | tf_op jit(solution)/shard_map/ppermute | solution.py:512
  20.5 0.1 collective-permute-start.5
  20.5 1.6 %collective-permute-start.4 = (bf16[64,512]{1,0:T(8,128)(2,1)S(1)}, bf16[64,512]{1,0:T(8,128)(2,1)S(1)}, u32[]{:S(2)}, u32[]{:S(2)}) collective-permute-start(bf16[64,512]{1,0:T(8,128)(2,1)S(1)} %shard_map.105.refs_0_.refs_4_), channel_id=1, source_target_pairs={{0,4},{1,5},{2,6},{3,7},{4,0},{5,1},{6,2},{7,3},{8,12},{9,13},{10,... | collective-permute-start | bytes 196616 | tf_op jit(solution)/shard_map/ppermute | solution.py:500
  22.1 1.9 %collective-permute-start.3 = (bf16[64,512]{1,0:T(8,128)(2,1)S(1)}, bf16[64,512]{1,0:T(8,128)(2,1)S(1)}, u32[]{:S(2)}, u32[]{:S(2)}) collective-permute-start(bf16[64,512]{1,0:T(8,128)(2,1)S(1)} %shard_map.105.refs_0_.refs_4_), channel_id=1, source_target_pairs={{0,2},{1,3},{2,0},{3,1},{4,6},{5,7},{6,4},{7,5},{8,10},{9,11},{10,... | collective-permute-start | bytes 196616 | tf_op jit(solution)/shard_map/ppermute | solution.py:500
  24.0 2.0 %collective-permute-done.5.refs_3_ = bf16[64,512]{1,0:T(8,128)(2,1)S(1)} collective-permute-done((bf16[64,512]{1,0:T(8,128)(2,1)S(1)}, bf16[64,512]{1,0:T(8,128)(2,1)S(1)}, u32[]{:S(2)}, u32[]{:S(2)}) %collective-permute-start.5) | collective-permute-done | bytes 65568 | tf_op jit(solution)/shard_map/ppermute | solution.py:500
  26.0 0.3 collective-permute-done.4.refs_2_
  26.3 0.8 %collective-permute-done.3.refs_1_ = bf16[64,512]{1,0:T(8,128)(2,1)S(1)} collective-permute-done((bf16[64,512]{1,0:T(8,128)(2,1)S(1)}, bf16[64,512]{1,0:T(8,128)(2,1)S(1)}, u32[]{:S(2)}, u32[]{:S(2)}) %collective-permute-start.3) | collective-permute-done | bytes 65568 | tf_op jit(solution)/shard_map/ppermute | solution.py:500
  27.1 0.1 collective-permute-start.6
  27.2 0.0 copy-start
  27.2 0.0 copy-start.5
  27.2 0.8 %shard_map.100 = (s32[256,1]{1,0:T(8,128)S(1)}, s32[256,1]{1,0:T(8,128)S(1)}, s32[384,1]{1,0:T(8,128)S(1)}, s32[384,1]{1,0:T(8,128)S(1)}) custom-call(s32[1,256]{1,0:T(1,128)S(1)} %bitcast.12), custom_call_target="tpu_custom_call" | custom-call | flops 2000000000 | bytes 1024 | tf_op jit(solution)/shard_map/pallas_call | solution.py:164
  28.1 0.7 collective-permute-done.6.refs_6_
  28.7 0.4 copy-done
  29.1 2.3 %shard_map.108 = (f32[256,768]{1,0:T(8,128)S(1)}, f32[256,1]{1,0:T(8,128)S(1)}, f32[8,256,256]{2,1,0:T(8,128)S(1)}, f32[24,128]{1,0:T(8,128)S(1)}) custom-call(s32[256,1]{1,0:T(8,128)S(1)} %get-tuple-element.25.refs_0_.place_ref, s32[256,1]{1,0:T(8,128)S(1)} %get-tuple-element.26.refs_1_, s32[24,1]{1,0:T(8,128)S(1)} %shard_map.101.after_ref.refs_2_, ...), custom_call_target="tpu_custom_call" | custom-call | flops 100000000 | bytes 5379168 | tf_op jit(solution)/shard_map/pallas_call | solution.py:164
  31.4 0.4 shard_map.110
  31.9 3.1 %collective-permute-start.12 = (bf16[128,768]{1,0:T(8,128)(2,1)S(1)}, bf16[128,768]{1,0:T(8,128)(2,1)S(1)}, u32[]{:S(2)}, u32[]{:S(2)}) collective-permute-start(bf16[128,768]{1,0:T(8,128)(2,1)S(1)} %get-tuple-element.30.refs_0_), channel_id=1, source_target_pairs={{0,2},{1,3},{2,0},{3,1},{4,4},{5,5},{6,6},{7,7},{8,10},{9,11},{10,... | collective-permute-start | bytes 589832 | tf_op jit(solution)/shard_map/ppermute | solution.py:512
  35.0 1.9 %collective-permute-start.13 = (bf16[128,768]{1,0:T(8,128)(2,1)S(1)}, bf16[128,768]{1,0:T(8,128)(2,1)S(1)}, u32[]{:S(2)}, u32[]{:S(2)}) collective-permute-start(bf16[128,768]{1,0:T(8,128)(2,1)S(1)} %get-tuple-element.31.refs_1_), channel_id=1, source_target_pairs={{0,4},{1,5},{2,2},{3,3},{4,0},{5,1},{6,6},{7,7},{8,8},{9,9},{10,14... | collective-permute-start | bytes 589832 | tf_op jit(solution)/shard_map/ppermute | solution.py:512
  36.9 3.9 %collective-permute-start.14 = (bf16[128,768]{1,0:T(8,128)(2,1)S(1)}, bf16[128,768]{1,0:T(8,128)(2,1)S(1)}, u32[]{:S(2)}, u32[]{:S(2)}) collective-permute-start(bf16[128,768]{1,0:T(8,128)(2,1)S(1)} %get-tuple-element.30.refs_0_), channel_id=1, source_target_pairs={{0,4},{1,5},{2,2},{3,3},{4,0},{5,1},{6,6},{7,7},{8,8},{9,9},{10,14... | collective-permute-start | bytes 589832 | tf_op jit(solution)/shard_map/ppermute | solution.py:512
  40.8 1.9 %collective-permute-start.15 = (bf16[128,768]{1,0:T(8,128)(2,1)S(1)}, bf16[128,768]{1,0:T(8,128)(2,1)S(1)}, u32[]{:S(2)}, u32[]{:S(2)}) collective-permute-start(bf16[128,768]{1,0:T(8,128)(2,1)S(1)} %get-tuple-element.31.refs_1_), channel_id=1, source_target_pairs={{0,2},{1,3},{2,0},{3,1},{4,4},{5,5},{6,6},{7,7},{8,10},{9,11},{10,... | collective-permute-start | bytes 589832 | tf_op jit(solution)/shard_map/ppermute | solution.py:512
  42.8 0.7 collective-permute-start.16
  43.4 1.2 %collective-permute-done.13.refs_3_ = bf16[128,768]{1,0:T(8,128)(2,1)S(1)} collective-permute-done((bf16[128,768]{1,0:T(8,128)(2,1)S(1)}, bf16[128,768]{1,0:T(8,128)(2,1)S(1)}, u32[]{:S(2)}, u32[]{:S(2)}) %collective-permute-start.13) | collective-permute-done | bytes 196640 | tf_op jit(solution)/shard_map/ppermute | solution.py:512
  44.6 0.7 collective-permute-start.17
  45.3 0.6 shard_map.109.refs_8_.refs_2_
  45.9 0.0 copy-start.1
  45.9 2.2 %collective-permute-done.14.refs_4_ = bf16[128,768]{1,0:T(8,128)(2,1)S(1)} collective-permute-done((bf16[128,768]{1,0:T(8,128)(2,1)S(1)}, bf16[128,768]{1,0:T(8,128)(2,1)S(1)}, u32[]{:S(2)}, u32[]{:S(2)}) %collective-permute-start.14) | collective-permute-done | bytes 196640 | tf_op jit(solution)/shard_map/ppermute | solution.py:512
  48.1 1.1 %collective-permute-done.15.refs_5_ = bf16[128,768]{1,0:T(8,128)(2,1)S(1)} collective-permute-done((bf16[128,768]{1,0:T(8,128)(2,1)S(1)}, bf16[128,768]{1,0:T(8,128)(2,1)S(1)}, u32[]{:S(2)}, u32[]{:S(2)}) %collective-permute-start.15) | collective-permute-done | bytes 196640 | tf_op jit(solution)/shard_map/ppermute | solution.py:512
  49.2 0.1 collective-permute-start.18
  49.3 0.5 shard_map.112.refs_3_
  49.8 1.2 %collective-permute-done.18.refs_4_ = bf16[256,768]{1,0:T(8,128)(2,1)S(1)} collective-permute-done((bf16[256,768]{1,0:T(8,128)(2,1)S(1)}, bf16[256,768]{1,0:T(8,128)(2,1)S(1)}, u32[]{:S(2)}, u32[]{:S(2)}) %collective-permute-start.18) | collective-permute-done | bytes 393248 | tf_op jit(solution)/shard_map/ppermute | solution.py:500
  51.0 2.8 %shard_map.113 = (bf16[411,256]{1,0:T(8,128)(2,1)S(1)}, bf16[384,411]{1,0:T(8,128)(2,1)S(1)}) custom-call(bf16[2048,768]{1,0:T(8,128)(2,1)S(1)} %copy-done, bf16[1536,768]{1,0:T(8,128)(2,1)S(1)} %copy-done.1, f32[8,256,256]{2,1,0:T(8,128)S(1)} %shard_map.109.refs_8_.refs_2_, f32[256,768]{1,0:T(8,128)S(1)} %shard_map.112.refs_3_, ...), custom_call_target="tpu_custom_call" | custom-call | flops 1840250880 | bytes 10487296 | tf_op jit(solution)/shard_map/pallas_call | solution.py:164
  53.8 0.2 collective-permute-start.19
  54.0 0.1 slice_bitcast_fusion.2
  54.1 0.3 shard_map.114.refs_0_
  54.4 1.2 %collective-permute-done.19.refs_1_ = bf16[384,411]{1,0:T(8,128)(2,1)S(1)} collective-permute-done((bf16[384,411]{1,0:T(8,128)(2,1)S(1)}, bf16[384,411]{1,0:T(8,128)(2,1)S(1)}, u32[]{:S(2)}, u32[]{:S(2)}) %collective-permute-start.19) | collective-permute-done | bytes 315680 | tf_op jit(solution)/shard_map/ppermute | solution.py:500
  55.6 0.1 shard_map.115
  55.7 6.8 %collective-permute-start.20 = (bf16[96,411]{1,0:T(8,128)(2,1)S(1)}, bf16[96,411]{1,0:T(8,128)(2,1)S(1)}, u32[]{:S(2)}, u32[]{:S(2)}) collective-permute-start(bf16[96,411]{1,0:T(8,128)(2,1)S(1)} %get-tuple-element.36), channel_id=1, source_target_pairs={{0,6},{1,7},{2,4},{3,5},{4,2},{5,3},{6,0},{7,1},{8,14},{9,15},{10,... | collective-permute-start | bytes 236744 | tf_op jit(solution)/shard_map/ppermute | solution.py:500
  62.5 0.6 collective-permute-start.22
  63.2 2.6 %collective-permute-done.20.refs_0_ = bf16[96,411]{1,0:T(8,128)(2,1)S(1)} collective-permute-done((bf16[96,411]{1,0:T(8,128)(2,1)S(1)}, bf16[96,411]{1,0:T(8,128)(2,1)S(1)}, u32[]{:S(2)}, u32[]{:S(2)}) %collective-permute-start.20) | collective-permute-done | bytes 78944 | tf_op jit(solution)/shard_map/ppermute | solution.py:500
  65.7 2.0 %collective-permute-done.21.refs_1_ = bf16[96,411]{1,0:T(8,128)(2,1)S(1)} collective-permute-done((bf16[96,411]{1,0:T(8,128)(2,1)S(1)}, bf16[96,411]{1,0:T(8,128)(2,1)S(1)}, u32[]{:S(2)}, u32[]{:S(2)}) %collective-permute-start.21) | collective-permute-done | bytes 78944 | tf_op jit(solution)/shard_map/ppermute | solution.py:500
  67.7 0.0 collective-permute-done.22.refs_2_
  67.8 0.2 shard_map.116
  68.0 1.6 %collective-permute-start.23 = (bf16[32,411]{1,0:T(8,128)(2,1)S(1)}, bf16[32,411]{1,0:T(8,128)(2,1)S(1)}, u32[]{:S(2)}, u32[]{:S(2)}) collective-permute-start(bf16[32,411]{1,0:T(8,128)(2,1)S(1)} %get-tuple-element.40), channel_id=1, source_target_pairs={{0,24},{8,16},{16,8},{24,0},{1,25},{9,17},{17,9},{25,1},{2,26},{10... | collective-permute-start | bytes 78920 | tf_op jit(solution)/shard_map/ppermute | solution.py:503
  69.6 1.6 %collective-permute-start.24 = (bf16[32,411]{1,0:T(8,128)(2,1)S(1)}, bf16[32,411]{1,0:T(8,128)(2,1)S(1)}, u32[]{:S(2)}, u32[]{:S(2)}) collective-permute-start(bf16[32,411]{1,0:T(8,128)(2,1)S(1)} %get-tuple-element.41), channel_id=1, source_target_pairs={{0,16},{8,24},{16,0},{24,8},{1,17},{9,25},{17,1},{25,9},{2,18},{10... | collective-permute-start | bytes 78920 | tf_op jit(solution)/shard_map/ppermute | solution.py:503
  71.2 1.2 %collective-permute-start.25 = (bf16[32,411]{1,0:T(8,128)(2,1)S(1)}, bf16[32,411]{1,0:T(8,128)(2,1)S(1)}, u32[]{:S(2)}, u32[]{:S(2)}) collective-permute-start(bf16[32,411]{1,0:T(8,128)(2,1)S(1)} %get-tuple-element.42), channel_id=1, source_target_pairs={{0,8},{8,0},{16,24},{24,16},{1,9},{9,1},{17,25},{25,17},{2,10},{10... | collective-permute-start | bytes 78920 | tf_op jit(solution)/shard_map/ppermute | solution.py:503
  72.5 0.1 maximum_sqrt_fusion
  72.5 0.1 copy.19
  72.6 1.2 %collective-permute-done.23.refs_0_ = bf16[32,411]{1,0:T(8,128)(2,1)S(1)} collective-permute-done((bf16[32,411]{1,0:T(8,128)(2,1)S(1)}, bf16[32,411]{1,0:T(8,128)(2,1)S(1)}, u32[]{:S(2)}, u32[]{:S(2)}) %collective-permute-start.23) | collective-permute-done | bytes 26336 | tf_op jit(solution)/shard_map/ppermute | solution.py:503
  73.8 0.8 collective-permute-done.24.refs_1_
  74.5 0.6 collective-permute-done.25.refs_2_
  75.1 1.3 %shard_map.117 = f32[4,32,411]{2,1,0:T(8,128)} custom-call(bf16[32,411]{1,0:T(8,128)(2,1)S(1)} %collective-permute-done.23.refs_0_, bf16[32,411]{1,0:T(8,128)(2,1)S(1)} %collective-permute-done.24.refs_1_, bf16[32,411]{1,0:T(8,128)(2,1)S(1)} %collective-permute-done.25.refs_2_, bf16[32,411]{1,0:T(8,128)(2,1)S(1)} %get-tuple-element.43.refs_3_, ...), custom_call_target="tpu_custom_call" | custom-call | flops 5260800 | bytes 106752 | tf_op jit(solution)/shard_map/pallas_call | solution.py:164
  (30 shorter events, 0.2 us)
Async XLA Ops:
  0.0 8.2 %copy-start.4 = (bf16[128,768]{1,0:T(8,128)(2,1)S(1)}, bf16[128,768]{1,0:T(8,128)(2,1)}, u32[]{:S(2)}) copy-start(bf16[128,768]{1,0:T(8,128)(2,1)} %refs_0_.3) | copy-start | bytes 589828
  0.0 15.8 %copy-start.3 = (bf16[411,256]{1,0:T(8,128)(2,1)S(1)}, bf16[411,256]{1,0:T(8,128)(2,1)}, u32[]{:S(2)}) copy-start(bf16[411,256]{1,0:T(8,128)(2,1)} %refs_0_.4) | copy-start | bytes 631300
  0.0 6.7 %copy-start.7 = (f32[256]{0:T(256)S(1)}, f32[256]{0:T(256)}, u32[]{:S(2)}) copy-start(f32[256]{0:T(256)} %bias_ref.1) | copy-start | bytes 3076
  0.0 6.7 %copy-start.8 = (s32[128]{0:T(128)S(1)}, s32[128]{0:T(128)}, u32[]{:S(2)}) copy-start(s32[128]{0:T(128)} %usable_ref.1) | copy-start | bytes 1540
  0.0 6.7 %copy-start.6 = (f32[4,32]{1,0:T(4,128)S(1)}, f32[4,32]{1,0:T(4,128)}, u32[]{:S(2)}) copy-start(f32[4,32]{1,0:T(4,128)} %diffusivity_ref.1) | copy-start | bytes 1540
  0.0 6.7 %copy-start.2 = (f32[4,32,411]{2,1,0:T(8,128)S(1)}, f32[4,32,411]{2,1,0:T(8,128)}, u32[]{:S(2)}) copy-start(f32[4,32,411]{2,1,0:T(8,128)} %fields_ref.1) | copy-start | bytes 631300
  0.0 8.2 %collective-permute-start.1 = (bf16[128,768]{1,0:T(8,128)(2,1)}, bf16[128,768]{1,0:T(8,128)(2,1)S(1)}, u32[]{:S(2)}, u32[]{:S(2)}) collective-permute-start(bf16[128,768]{1,0:T(8,128)(2,1)} %refs_0_.3), channel_id=1, source_target_pairs={{0,8},{8,0},{16,24},{24,16},{1,9},{9,1},{17,25},{25,17},{2,10},{10... | collective-permute-start | bytes 589832 | tf_op jit(solution)/shard_map/ppermute | solution.py:503
  3.1 12.3 %collective-permute-start.8 = (bf16[411,256]{1,0:T(8,128)(2,1)}, bf16[411,256]{1,0:T(8,128)(2,1)S(1)}, u32[]{:S(2)}, u32[]{:S(2)}) collective-permute-start(bf16[411,256]{1,0:T(8,128)(2,1)} %refs_0_.4), channel_id=1, source_target_pairs={{0,4},{1,5},{2,6},{3,7},{4,0},{5,1},{6,2},{7,3},{8,12},{9,13},{10,... | collective-permute-start | bytes 631304 | tf_op jit(solution)/shard_map/ppermute | solution.py:500
  4.6 10.8 %collective-permute-start.7 = (bf16[411,256]{1,0:T(8,128)(2,1)}, bf16[411,256]{1,0:T(8,128)(2,1)S(1)}, u32[]{:S(2)}, u32[]{:S(2)}) collective-permute-start(bf16[411,256]{1,0:T(8,128)(2,1)} %refs_0_.4), channel_id=1, source_target_pairs={{0,2},{1,3},{2,0},{3,1},{4,6},{5,7},{6,4},{7,5},{8,10},{9,11},{10,... | collective-permute-start | bytes 631304 | tf_op jit(solution)/shard_map/ppermute | solution.py:500
  6.1 9.7 %collective-permute-start.9 = (bf16[411,256]{1,0:T(8,128)(2,1)}, bf16[411,256]{1,0:T(8,128)(2,1)S(1)}, u32[]{:S(2)}, u32[]{:S(2)}) collective-permute-start(bf16[411,256]{1,0:T(8,128)(2,1)} %refs_0_.4), channel_id=1, source_target_pairs={{0,6},{1,7},{2,4},{3,5},{4,2},{5,3},{6,0},{7,1},{8,14},{9,15},{10,... | collective-permute-start | bytes 631304 | tf_op jit(solution)/shard_map/ppermute | solution.py:500
  6.7 20.5 %copy-start.9 = (s32[256,1]{0,1:T(1,128)S(1)}, s32[256,1]{0,1:T(1,128)}, u32[]{:S(2)}) copy-start(s32[256,1]{0,1:T(1,128)} %param.12) | copy-start | bytes 3076
  6.9 3.7 %collective-permute-start = (bf16[16,512]{1,0:T(8,128)(2,1)S(1)}, bf16[16,512]{1,0:T(8,128)(2,1)S(1)}, u32[]{:S(2)}, u32[]{:S(2)}) collective-permute-start(bf16[16,512]{1,0:T(8,128)(2,1)S(1)} %shard_map.102.refs_0_), channel_id=1, source_target_pairs={{0,8},{8,0},{16,24},{24,16},{1,9},{9,1},{17,25},{25,17},{2,10},{10... | collective-permute-start | bytes 49160 | tf_op jit(solution)/shard_map/ppermute | solution.py:503
  10.6 4.8 %collective-permute-start.2 = (bf16[32,512]{1,0:T(8,128)(2,1)S(1)}, bf16[32,512]{1,0:T(8,128)(2,1)S(1)}, u32[]{:S(2)}, u32[]{:S(2)}) collective-permute-start(bf16[32,512]{1,0:T(8,128)(2,1)S(1)} %shard_map.104.refs_0_), channel_id=1, source_target_pairs={{0,16},{8,24},{16,0},{24,8},{1,17},{9,25},{17,1},{25,9},{2,18},{10... | collective-permute-start | bytes 98312 | tf_op jit(solution)/shard_map/ppermute | solution.py:503
  15.9 12.8 %collective-permute-start.10 = (bf16[1664,256]{1,0:T(8,128)(2,1)S(1)}, bf16[1664,256]{1,0:T(8,128)(2,1)S(1)}, u32[]{:S(2)}, u32[]{:S(2)}) collective-permute-start(bf16[1664,256]{1,0:T(8,128)(2,1)S(1)} %shard_map.107.refs_7_.refs_5_), channel_id=1, source_target_pairs={{0,1},{1,0},{2,3},{3,2},{4,5},{5,4},{6,7},{7,6},{8,9},{9,8},{10,11... | collective-permute-start | bytes 2555912 | tf_op jit(solution)/shard_map/ppermute | solution.py:500
  15.9 15.5 %collective-permute-start.11 = (bf16[256,768]{1,0:T(8,128)(2,1)S(1)}, bf16[256,768]{1,0:T(8,128)(2,1)S(1)}, u32[]{:S(2)}, u32[]{:S(2)}) collective-permute-start(bf16[256,768]{1,0:T(8,128)(2,1)S(1)} %shard_map.103.refs_2_.refs_0_), channel_id=1, source_target_pairs={{0,16},{1,17},{2,2},{3,3},{4,20},{5,21},{6,6},{7,7},{8,8},{9,9},{1... | collective-permute-start | bytes 1179656 | tf_op jit(solution)/shard_map/ppermute | solution.py:512
  20.5 5.5 %collective-permute-start.5 = (bf16[64,512]{1,0:T(8,128)(2,1)S(1)}, bf16[64,512]{1,0:T(8,128)(2,1)S(1)}, u32[]{:S(2)}, u32[]{:S(2)}) collective-permute-start(bf16[64,512]{1,0:T(8,128)(2,1)S(1)} %shard_map.105.refs_0_.refs_4_), channel_id=1, source_target_pairs={{0,6},{1,7},{2,4},{3,5},{4,2},{5,3},{6,0},{7,1},{8,14},{9,15},{10,... | collective-permute-start | bytes 196616 | tf_op jit(solution)/shard_map/ppermute | solution.py:500
  20.5 5.7 %collective-permute-start.4 = (bf16[64,512]{1,0:T(8,128)(2,1)S(1)}, bf16[64,512]{1,0:T(8,128)(2,1)S(1)}, u32[]{:S(2)}, u32[]{:S(2)}) collective-permute-start(bf16[64,512]{1,0:T(8,128)(2,1)S(1)} %shard_map.105.refs_0_.refs_4_), channel_id=1, source_target_pairs={{0,4},{1,5},{2,6},{3,7},{4,0},{5,1},{6,2},{7,3},{8,12},{9,13},{10,... | collective-permute-start | bytes 196616 | tf_op jit(solution)/shard_map/ppermute | solution.py:500
  22.1 5.0 %collective-permute-start.3 = (bf16[64,512]{1,0:T(8,128)(2,1)S(1)}, bf16[64,512]{1,0:T(8,128)(2,1)S(1)}, u32[]{:S(2)}, u32[]{:S(2)}) collective-permute-start(bf16[64,512]{1,0:T(8,128)(2,1)S(1)} %shard_map.105.refs_0_.refs_4_), channel_id=1, source_target_pairs={{0,2},{1,3},{2,0},{3,1},{4,6},{5,7},{6,4},{7,5},{8,10},{9,11},{10,... | collective-permute-start | bytes 196616 | tf_op jit(solution)/shard_map/ppermute | solution.py:500
  27.1 1.6 %collective-permute-start.6 = (bf16[256,512]{1,0:T(8,128)(2,1)S(1)}, bf16[256,512]{1,0:T(8,128)(2,1)S(1)}, u32[]{:S(2)}, u32[]{:S(2)}) collective-permute-start(bf16[256,512]{1,0:T(8,128)(2,1)S(1)} %shard_map.106.refs_5_), channel_id=1, source_target_pairs={{0,1},{1,0},{2,3},{3,2},{4,5},{5,4},{6,7},{7,6},{8,9},{9,8},{10,11... | collective-permute-start | bytes 786440 | tf_op jit(solution)/shard_map/ppermute | solution.py:500
  27.2 1.9 %copy-start = (bf16[2048,768]{1,0:T(8,128)(2,1)S(1)}, bf16[2048,768]{1,0:T(8,128)(2,1)}, u32[]{:S(2)}) copy-start(bf16[2048,768]{1,0:T(8,128)(2,1)} %refs_0_.5) | copy-start | bytes 9437188
  27.2 1.9 %copy-start.5 = (f32[768]{0:T(1024)S(1)}, f32[768]{0:T(1024)}, u32[]{:S(2)}) copy-start(f32[768]{0:T(1024)} %refs_3_.1) | copy-start | bytes 9220
  31.9 10.9 %collective-permute-start.12 = (bf16[128,768]{1,0:T(8,128)(2,1)S(1)}, bf16[128,768]{1,0:T(8,128)(2,1)S(1)}, u32[]{:S(2)}, u32[]{:S(2)}) collective-permute-start(bf16[128,768]{1,0:T(8,128)(2,1)S(1)} %get-tuple-element.30.refs_0_), channel_id=1, source_target_pairs={{0,2},{1,3},{2,0},{3,1},{4,4},{5,5},{6,6},{7,7},{8,10},{9,11},{10,... | collective-permute-start | bytes 589832 | tf_op jit(solution)/shard_map/ppermute | solution.py:512
  35.0 9.6 %collective-permute-start.13 = (bf16[128,768]{1,0:T(8,128)(2,1)S(1)}, bf16[128,768]{1,0:T(8,128)(2,1)S(1)}, u32[]{:S(2)}, u32[]{:S(2)}) collective-permute-start(bf16[128,768]{1,0:T(8,128)(2,1)S(1)} %get-tuple-element.31.refs_1_), channel_id=1, source_target_pairs={{0,4},{1,5},{2,2},{3,3},{4,0},{5,1},{6,6},{7,7},{8,8},{9,9},{10,14... | collective-permute-start | bytes 589832 | tf_op jit(solution)/shard_map/ppermute | solution.py:512
  36.9 11.2 %collective-permute-start.14 = (bf16[128,768]{1,0:T(8,128)(2,1)S(1)}, bf16[128,768]{1,0:T(8,128)(2,1)S(1)}, u32[]{:S(2)}, u32[]{:S(2)}) collective-permute-start(bf16[128,768]{1,0:T(8,128)(2,1)S(1)} %get-tuple-element.30.refs_0_), channel_id=1, source_target_pairs={{0,4},{1,5},{2,2},{3,3},{4,0},{5,1},{6,6},{7,7},{8,8},{9,9},{10,14... | collective-permute-start | bytes 589832 | tf_op jit(solution)/shard_map/ppermute | solution.py:512
  40.8 8.3 %collective-permute-start.15 = (bf16[128,768]{1,0:T(8,128)(2,1)S(1)}, bf16[128,768]{1,0:T(8,128)(2,1)S(1)}, u32[]{:S(2)}, u32[]{:S(2)}) collective-permute-start(bf16[128,768]{1,0:T(8,128)(2,1)S(1)} %get-tuple-element.31.refs_1_), channel_id=1, source_target_pairs={{0,2},{1,3},{2,0},{3,1},{4,4},{5,5},{6,6},{7,7},{8,10},{9,11},{10,... | collective-permute-start | bytes 589832 | tf_op jit(solution)/shard_map/ppermute | solution.py:512
  42.8 6.4 %collective-permute-start.16 = (bf16[128,768]{1,0:T(8,128)(2,1)S(1)}, bf16[128,768]{1,0:T(8,128)(2,1)S(1)}, u32[]{:S(2)}, u32[]{:S(2)}) collective-permute-start(bf16[128,768]{1,0:T(8,128)(2,1)S(1)} %collective-permute-done.12.refs_2_), channel_id=1, source_target_pairs={{0,0},{1,1},{2,6},{3,7},{4,4},{5,5},{6,2},{7,3},{8,12},{9,13},{10,... | collective-permute-start | bytes 589832 | tf_op jit(solution)/shard_map/ppermute | solution.py:512
  44.6 4.6 %collective-permute-start.17 = (bf16[128,768]{1,0:T(8,128)(2,1)S(1)}, bf16[128,768]{1,0:T(8,128)(2,1)S(1)}, u32[]{:S(2)}, u32[]{:S(2)}) collective-permute-start(bf16[128,768]{1,0:T(8,128)(2,1)S(1)} %collective-permute-done.13.refs_3_), channel_id=1, source_target_pairs={{0,0},{1,1},{2,2},{3,3},{4,6},{5,7},{6,4},{7,5},{8,8},{9,9},{10,10... | collective-permute-start | bytes 589832 | tf_op jit(solution)/shard_map/ppermute | solution.py:512
  45.9 3.4 %copy-start.1 = (bf16[1536,768]{1,0:T(8,128)(2,1)S(1)}, bf16[1536,768]{1,0:T(8,128)(2,1)}, u32[]{:S(2)}) copy-start(bf16[1536,768]{1,0:T(8,128)(2,1)} %refs_1_.1) | copy-start | bytes 7077892
  49.2 1.8 %collective-permute-start.18 = (bf16[256,768]{1,0:T(8,128)(2,1)S(1)}, bf16[256,768]{1,0:T(8,128)(2,1)S(1)}, u32[]{:S(2)}, u32[]{:S(2)}) collective-permute-start(bf16[256,768]{1,0:T(8,128)(2,1)S(1)} %shard_map.111.depart_ref), channel_id=1, source_target_pairs={{0,1},{1,0},{2,3},{3,2},{4,5},{5,4},{6,7},{7,6},{8,9},{9,8},{10,11... | collective-permute-start | bytes 1179656 | tf_op jit(solution)/shard_map/ppermute | solution.py:500
  53.8 1.8 %collective-permute-start.19 = (bf16[384,411]{1,0:T(8,128)(2,1)S(1)}, bf16[384,411]{1,0:T(8,128)(2,1)S(1)}, u32[]{:S(2)}, u32[]{:S(2)}) collective-permute-start(bf16[384,411]{1,0:T(8,128)(2,1)S(1)} %get-tuple-element.35), channel_id=1, source_target_pairs={{0,1},{1,0},{2,3},{3,2},{4,5},{5,4},{6,7},{7,6},{8,9},{9,8},{10,11... | collective-permute-start | bytes 946952 | tf_op jit(solution)/shard_map/ppermute | solution.py:500
  55.7 10.0 %collective-permute-start.20 = (bf16[96,411]{1,0:T(8,128)(2,1)S(1)}, bf16[96,411]{1,0:T(8,128)(2,1)S(1)}, u32[]{:S(2)}, u32[]{:S(2)}) collective-permute-start(bf16[96,411]{1,0:T(8,128)(2,1)S(1)} %get-tuple-element.36), channel_id=1, source_target_pairs={{0,6},{1,7},{2,4},{3,5},{4,2},{5,3},{6,0},{7,1},{8,14},{9,15},{10,... | collective-permute-start | bytes 236744 | tf_op jit(solution)/shard_map/ppermute | solution.py:500
  62.5 5.2 %collective-permute-start.21 = (bf16[96,411]{1,0:T(8,128)(2,1)S(1)}, bf16[96,411]{1,0:T(8,128)(2,1)S(1)}, u32[]{:S(2)}, u32[]{:S(2)}) collective-permute-start(bf16[96,411]{1,0:T(8,128)(2,1)S(1)} %get-tuple-element.37), channel_id=1, source_target_pairs={{0,4},{1,5},{2,6},{3,7},{4,0},{5,1},{6,2},{7,3},{8,12},{9,13},{10,... | collective-permute-start | bytes 236744 | tf_op jit(solution)/shard_map/ppermute | solution.py:500
  62.5 5.2 %collective-permute-start.22 = (bf16[96,411]{1,0:T(8,128)(2,1)S(1)}, bf16[96,411]{1,0:T(8,128)(2,1)S(1)}, u32[]{:S(2)}, u32[]{:S(2)}) collective-permute-start(bf16[96,411]{1,0:T(8,128)(2,1)S(1)} %get-tuple-element.38), channel_id=1, source_target_pairs={{0,2},{1,3},{2,0},{3,1},{4,6},{5,7},{6,4},{7,5},{8,10},{9,11},{10,... | collective-permute-start | bytes 236744 | tf_op jit(solution)/shard_map/ppermute | solution.py:500
  68.0 5.8 %collective-permute-start.23 = (bf16[32,411]{1,0:T(8,128)(2,1)S(1)}, bf16[32,411]{1,0:T(8,128)(2,1)S(1)}, u32[]{:S(2)}, u32[]{:S(2)}) collective-permute-start(bf16[32,411]{1,0:T(8,128)(2,1)S(1)} %get-tuple-element.40), channel_id=1, source_target_pairs={{0,24},{8,16},{16,8},{24,0},{1,25},{9,17},{17,9},{25,1},{2,26},{10... | collective-permute-start | bytes 78920 | tf_op jit(solution)/shard_map/ppermute | solution.py:503
  69.6 4.9 %collective-permute-start.24 = (bf16[32,411]{1,0:T(8,128)(2,1)S(1)}, bf16[32,411]{1,0:T(8,128)(2,1)S(1)}, u32[]{:S(2)}, u32[]{:S(2)}) collective-permute-start(bf16[32,411]{1,0:T(8,128)(2,1)S(1)} %get-tuple-element.41), channel_id=1, source_target_pairs={{0,16},{8,24},{16,0},{24,8},{1,17},{9,25},{17,1},{25,9},{2,18},{10... | collective-permute-start | bytes 78920 | tf_op jit(solution)/shard_map/ppermute | solution.py:503
  71.2 3.9 %collective-permute-start.25 = (bf16[32,411]{1,0:T(8,128)(2,1)S(1)}, bf16[32,411]{1,0:T(8,128)(2,1)S(1)}, u32[]{:S(2)}, u32[]{:S(2)}) collective-permute-start(bf16[32,411]{1,0:T(8,128)(2,1)S(1)} %get-tuple-element.42), channel_id=1, source_target_pairs={{0,8},{8,0},{16,24},{24,16},{1,9},{9,1},{17,25},{25,17},{2,10},{10... | collective-permute-start | bytes 78920 | tf_op jit(solution)/shard_map/ppermute | solution.py:503

commit v20 on v18

--- a/solution.py
+++ b/solution.py
@@ -307,7 +307,7 @@
     refs = list(refs)
     take = lambda n: [refs.pop(0) for _ in range(n)]
     place_ref, source_ref, cell_ref, bias_ref, w_radiance_ref = take(5)
-    strip_refs, weight_refs = take(p.group), take(p.group)
+    strip_refs, weight_refs, (seen_ref,) = take(p.group), take(p.group), take(1)
     radiance_ref, in_use_ref, preact_ref, kappa_ref, active = refs
     c = lax.axis_index("chan")
     gathered = [ref[...] for ref in strip_refs]
@@ -337,7 +337,9 @@
         flags = jnp.where(place_ref[...] == slot, flags.astype(jnp.float32), 0.0)
         in_use = in_use + jnp.sum(flags, axis=1, keepdims=True)
     in_use_ref[...] = in_use
-    radiance_ref[...] = dot(active[...], w_radiance_ref[...]) + bias_ref[...].reshape(1, p.shard)
+    observed = dot(one_hot(place_ref[...], 0, seen_ref.shape[0]), seen_ref[...])
+    radiance = dot(active[...], w_radiance_ref[...]) + bias_ref[...].reshape(1, p.shard)
+    radiance_ref[...] = radiance - observed
     parts = sum(
         dot(one_hot(cell_ref[...], k * p.strips, p.strips), strips)
         for k, strips in enumerate(gathered)
@@ -351,7 +353,7 @@
     for j, part_ref in enumerate(part_refs):
         at = slice(j * part, (j + 1) * part)
         observed = sum(
-            dot(one_hot(place_ref[at, :], k * count, count), ref[...])
+            dot(one_hot(place_ref[at, :], (k + 1) * count, count), ref[...])
             for k, ref in enumerate(seen_refs)
         )
         departure = (radiance_ref[at, :] - observed) * in_use_ref[at, :]
@@ -585,14 +587,14 @@
             shape((p.chans, p.rows, p.hidden), single),
             shape((3 * reach, p.lane), single),
         ],
-        [place, source, cell, b_radiance, w_radiance] + strips + weights,
+        [place, source, cell, b_radiance, w_radiance] + strips + weights + seen[:1],
         scratch=[pltpu.VMEM((p.rows, p.hidden * p.chans), half)],
         flops=FORWARD_FLOPS,
     )
     parts = call(
         functools.partial(depart_kernel, p),
         [shape((p.rows // p.steps, p.shard), half)] * p.steps,
-        [radiance, in_use, place] + seen,
+        [radiance, in_use, place] + seen[1:],
     )
 
     slope = call(

time: 66.8 us -> 66.8 us (level)
  no operation moved by 1% of the time
where the time goes in v20:
time: 66.8 us; the launch traced here: 66.6 us
  starting transfers between devices  28.1 us (42%)
  waiting for transfers between devices  27.9 us (42%)
  Pallas kernels  9.75 us (15%)
    ppermute x13, starting transfers between devices, flip(): return lax.ppermute(value, 'chan', [(b, b ^ mask) for b in range(p.chans)])  11.8 us
    ppermute x13, waiting for transfers between devices, flip(): return lax.ppermute(value, 'chan', [(b, b ^ mask) for b in range(p.chans)])  11 us
    ppermute x6, starting transfers between devices, trade(): return lax.ppermute(value, 'tile', [(a, a ^ mask) for a in range(p.tiles)])  10.3 us
    pallas_call x18, Pallas kernels, call(): pl.pallas_call(kernel, out_shape=out_shape, in_specs=[far if k in in_hbm...  9.75 us
    ppermute x7, waiting for transfers between devices, send(): lax.ppermute(value, both, sorted(((number(a), number(b)) for a, b in pair...  8.56 us
    ppermute x6, waiting for transfers between devices, trade(): return lax.ppermute(value, 'tile', [(a, a ^ mask) for a in range(p.tiles)])  8.33 us
    ppermute x7, starting transfers between devices, send(): lax.ppermute(value, both, sorted(((number(a), number(b)) for a, b in pair...  5.99 us
  transfers between devices with their start and end apart: 26, of which 18 were waited for; matrix products, arithmetic and copies ran while one was open for 0% of the time, Pallas kernels for 7%

profile of v20, /device:TPU:0, one launch (start us, length us, event | category | flops | bytes accessed | tf_op | source)
XLA Modules:
  0.0 66.6 jit_solution(2772546015004472361)
XLA Ops:
  0.0 3.1 %collective-permute-start.1 = (bf16[128,768]{1,0:T(8,128)(2,1)}, bf16[128,768]{1,0:T(8,128)(2,1)S(1)}, u32[]{:S(2)}, u32[]{:S(2)}) collective-permute-start(bf16[128,768]{1,0:T(8,128)(2,1)} %refs_0_.3), channel_id=1, source_target_pairs={{0,8},{8,0},{16,24},{24,16},{1,9},{9,1},{17,25},{25,17},{2,10},{10... | collective-permute-start | bytes 589832 | tf_op jit(solution)/shard_map/ppermute | solution.py:505
  3.1 1.5 %collective-permute-start.8 = (bf16[411,256]{1,0:T(8,128)(2,1)}, bf16[411,256]{1,0:T(8,128)(2,1)S(1)}, u32[]{:S(2)}, u32[]{:S(2)}) collective-permute-start(bf16[411,256]{1,0:T(8,128)(2,1)} %refs_0_.4), channel_id=1, source_target_pairs={{0,4},{1,5},{2,6},{3,7},{4,0},{5,1},{6,2},{7,3},{8,12},{9,13},{10,... | collective-permute-start | bytes 631304 | tf_op jit(solution)/shard_map/ppermute | solution.py:502
  4.6 1.5 %collective-permute-start.7 = (bf16[411,256]{1,0:T(8,128)(2,1)}, bf16[411,256]{1,0:T(8,128)(2,1)S(1)}, u32[]{:S(2)}, u32[]{:S(2)}) collective-permute-start(bf16[411,256]{1,0:T(8,128)(2,1)} %refs_0_.4), channel_id=1, source_target_pairs={{0,2},{1,3},{2,0},{3,1},{4,6},{5,7},{6,4},{7,5},{8,10},{9,11},{10,... | collective-permute-start | bytes 631304 | tf_op jit(solution)/shard_map/ppermute | solution.py:502
  6.1 0.5 collective-permute-start.9
  6.7 0.0 copy-start.9
  6.7 0.2 shard_map.102.refs_0_
  6.9 0.1 collective-permute-start
  7.0 1.3 %collective-permute-done.1.refs_1_ = bf16[128,768]{1,0:T(8,128)(2,1)S(1)} collective-permute-done((bf16[128,768]{1,0:T(8,128)(2,1)}, bf16[128,768]{1,0:T(8,128)(2,1)S(1)}, u32[]{:S(2)}, u32[]{:S(2)}) %collective-permute-start.1) | collective-permute-done | bytes 196640 | tf_op jit(solution)/shard_map/ppermute | solution.py:505
  8.3 2.4 %collective-permute-done.refs_1_ = bf16[16,512]{1,0:T(8,128)(2,1)S(1)} collective-permute-done((bf16[16,512]{1,0:T(8,128)(2,1)S(1)}, bf16[16,512]{1,0:T(8,128)(2,1)S(1)}, u32[]{:S(2)}, u32[]{:S(2)}) %collective-permute-start) | collective-permute-done | bytes 16416 | tf_op jit(solution)/shard_map/ppermute | solution.py:505
  10.6 2.7 %collective-permute-start.2 = (bf16[32,512]{1,0:T(8,128)(2,1)S(1)}, bf16[32,512]{1,0:T(8,128)(2,1)S(1)}, u32[]{:S(2)}, u32[]{:S(2)}) collective-permute-start(bf16[32,512]{1,0:T(8,128)(2,1)S(1)} %shard_map.104.refs_0_), channel_id=1, source_target_pairs={{0,16},{8,24},{16,0},{24,8},{1,17},{9,25},{17,1},{25,9},{2,18},{10... | collective-permute-start | bytes 98312 | tf_op jit(solution)/shard_map/ppermute | solution.py:505
  13.3 2.1 %collective-permute-done.2.refs_1_ = bf16[32,512]{1,0:T(8,128)(2,1)S(1)} collective-permute-done((bf16[32,512]{1,0:T(8,128)(2,1)S(1)}, bf16[32,512]{1,0:T(8,128)(2,1)S(1)}, u32[]{:S(2)}, u32[]{:S(2)}) %collective-permute-start.2) | collective-permute-done | bytes 32800 | tf_op jit(solution)/shard_map/ppermute | solution.py:505
  15.5 0.3 collective-permute-done.9.refs_3_
  15.8 0.1 shard_map.107.refs_7_.refs_5_
  15.9 0.1 collective-permute-start.10
  16.0 2.7 %collective-permute-start.11 = (bf16[256,768]{1,0:T(8,128)(2,1)S(1)}, bf16[256,768]{1,0:T(8,128)(2,1)S(1)}, u32[]{:S(2)}, u32[]{:S(2)}) collective-permute-start(bf16[256,768]{1,0:T(8,128)(2,1)S(1)} %shard_map.103.refs_2_.refs_9_), channel_id=1, source_target_pairs={{0,16},{1,17},{2,3},{3,2},{4,20},{5,21},{6,7},{7,6},{8,9},{9,8},{1... | collective-permute-start | bytes 1179656 | tf_op jit(solution)/shard_map/ppermute | solution.py:514
  18.6 0.3 collective-permute-start.5
  18.9 1.2 %collective-permute-start.4 = (bf16[64,512]{1,0:T(8,128)(2,1)S(1)}, bf16[64,512]{1,0:T(8,128)(2,1)S(1)}, u32[]{:S(2)}, u32[]{:S(2)}) collective-permute-start(bf16[64,512]{1,0:T(8,128)(2,1)S(1)} %shard_map.105.refs_0_.refs_4_), channel_id=1, source_target_pairs={{0,4},{1,5},{2,6},{3,7},{4,0},{5,1},{6,2},{7,3},{8,12},{9,13},{10,... | collective-permute-start | bytes 196616 | tf_op jit(solution)/shard_map/ppermute | solution.py:502
  20.1 2.0 %collective-permute-start.3 = (bf16[64,512]{1,0:T(8,128)(2,1)S(1)}, bf16[64,512]{1,0:T(8,128)(2,1)S(1)}, u32[]{:S(2)}, u32[]{:S(2)}) collective-permute-start(bf16[64,512]{1,0:T(8,128)(2,1)S(1)} %shard_map.105.refs_0_.refs_4_), channel_id=1, source_target_pairs={{0,2},{1,3},{2,0},{3,1},{4,6},{5,7},{6,4},{7,5},{8,10},{9,11},{10,... | collective-permute-start | bytes 196616 | tf_op jit(solution)/shard_map/ppermute | solution.py:502
  22.1 2.0 %collective-permute-done.5.refs_3_ = bf16[64,512]{1,0:T(8,128)(2,1)S(1)} collective-permute-done((bf16[64,512]{1,0:T(8,128)(2,1)S(1)}, bf16[64,512]{1,0:T(8,128)(2,1)S(1)}, u32[]{:S(2)}, u32[]{:S(2)}) %collective-permute-start.5) | collective-permute-done | bytes 65568 | tf_op jit(solution)/shard_map/ppermute | solution.py:502
  24.1 0.3 collective-permute-done.4.refs_2_
  24.4 0.8 %collective-permute-done.3.refs_1_ = bf16[64,512]{1,0:T(8,128)(2,1)S(1)} collective-permute-done((bf16[64,512]{1,0:T(8,128)(2,1)S(1)}, bf16[64,512]{1,0:T(8,128)(2,1)S(1)}, u32[]{:S(2)}, u32[]{:S(2)}) %collective-permute-start.3) | collective-permute-done | bytes 65568 | tf_op jit(solution)/shard_map/ppermute | solution.py:502
  25.2 0.1 collective-permute-start.6
  25.2 0.0 copy-start
  25.3 0.0 copy-start.5
  25.3 0.8 %shard_map.100 = (s32[256,1]{1,0:T(8,128)S(1)}, s32[256,1]{1,0:T(8,128)S(1)}, s32[384,1]{1,0:T(8,128)S(1)}, s32[384,1]{1,0:T(8,128)S(1)}) custom-call(s32[1,256]{1,0:T(1,128)S(1)} %bitcast.12), custom_call_target="tpu_custom_call" | custom-call | flops 2000000000 | bytes 1024 | tf_op jit(solution)/shard_map/pallas_call | solution.py:164
  26.1 0.7 collective-permute-done.6.refs_6_
  26.8 0.4 copy-done
  27.1 2.4 %shard_map.108 = (f32[256,768]{1,0:T(8,128)S(1)}, f32[256,1]{1,0:T(8,128)S(1)}, f32[8,256,256]{2,1,0:T(8,128)S(1)}, f32[24,128]{1,0:T(8,128)S(1)}) custom-call(s32[256,1]{1,0:T(8,128)S(1)} %get-tuple-element.25.refs_0_.place_ref, s32[256,1]{1,0:T(8,128)S(1)} %get-tuple-element.26.refs_1_, s32[24,1]{1,0:T(8,128)S(1)} %shard_map.101.after_ref.refs_2_, ...), custom_call_target="tpu_custom_call" | custom-call | flops 100000000 | bytes 5772384 | tf_op jit(solution)/shard_map/pallas_call | solution.py:164
  29.5 0.0 collective-permute-done.11.refs_0_
  29.5 0.3 shard_map.110
  29.9 1.3 %collective-permute-start.12 = (bf16[128,768]{1,0:T(8,128)(2,1)S(1)}, bf16[128,768]{1,0:T(8,128)(2,1)S(1)}, u32[]{:S(2)}, u32[]{:S(2)}) collective-permute-start(bf16[128,768]{1,0:T(8,128)(2,1)S(1)} %get-tuple-element.30.refs_0_), channel_id=1, source_target_pairs={{0,2},{1,3},{2,0},{3,1},{4,5},{5,4},{6,7},{7,6},{8,10},{9,11},{10,... | collective-permute-start | bytes 589832 | tf_op jit(solution)/shard_map/ppermute | solution.py:514
  31.2 0.0 collective-permute-start.13
  31.2 2.0 %collective-permute-start.14 = (bf16[128,768]{1,0:T(8,128)(2,1)S(1)}, bf16[128,768]{1,0:T(8,128)(2,1)S(1)}, u32[]{:S(2)}, u32[]{:S(2)}) collective-permute-start(bf16[128,768]{1,0:T(8,128)(2,1)S(1)} %get-tuple-element.30.refs_0_), channel_id=1, source_target_pairs={{0,4},{1,5},{2,3},{3,2},{4,0},{5,1},{6,7},{7,6},{8,9},{9,8},{10,14... | collective-permute-start | bytes 589832 | tf_op jit(solution)/shard_map/ppermute | solution.py:514
  33.2 4.4 %collective-permute-done.12.refs_2_ = bf16[128,768]{1,0:T(8,128)(2,1)S(1)} collective-permute-done((bf16[128,768]{1,0:T(8,128)(2,1)S(1)}, bf16[128,768]{1,0:T(8,128)(2,1)S(1)}, u32[]{:S(2)}, u32[]{:S(2)}) %collective-permute-start.12) | collective-permute-done | bytes 196640 | tf_op jit(solution)/shard_map/ppermute | solution.py:514
  37.6 1.3 %collective-permute-done.13.refs_3_ = bf16[128,768]{1,0:T(8,128)(2,1)S(1)} collective-permute-done((bf16[128,768]{1,0:T(8,128)(2,1)S(1)}, bf16[128,768]{1,0:T(8,128)(2,1)S(1)}, u32[]{:S(2)}, u32[]{:S(2)}) %collective-permute-start.13) | collective-permute-done | bytes 196640 | tf_op jit(solution)/shard_map/ppermute | solution.py:514
  38.9 0.6 shard_map.109.refs_8_.refs_2_
  39.5 0.0 copy-start.1
  39.5 2.8 %collective-permute-done.14.refs_4_ = bf16[128,768]{1,0:T(8,128)(2,1)S(1)} collective-permute-done((bf16[128,768]{1,0:T(8,128)(2,1)S(1)}, bf16[128,768]{1,0:T(8,128)(2,1)S(1)}, u32[]{:S(2)}, u32[]{:S(2)}) %collective-permute-start.14) | collective-permute-done | bytes 196640 | tf_op jit(solution)/shard_map/ppermute | solution.py:514
  42.4 0.1 shard_map.111.depart_ref
  42.5 0.1 collective-permute-start.18
  42.5 0.5 shard_map.112.refs_3_
  43.0 1.2 %collective-permute-done.18.refs_4_ = bf16[256,768]{1,0:T(8,128)(2,1)S(1)} collective-permute-done((bf16[256,768]{1,0:T(8,128)(2,1)S(1)}, bf16[256,768]{1,0:T(8,128)(2,1)S(1)}, u32[]{:S(2)}, u32[]{:S(2)}) %collective-permute-start.18) | collective-permute-done | bytes 393248 | tf_op jit(solution)/shard_map/ppermute | solution.py:502
  44.2 2.8 %shard_map.113 = (bf16[411,256]{1,0:T(8,128)(2,1)S(1)}, bf16[384,411]{1,0:T(8,128)(2,1)S(1)}) custom-call(bf16[2048,768]{1,0:T(8,128)(2,1)S(1)} %copy-done, bf16[1536,768]{1,0:T(8,128)(2,1)S(1)} %copy-done.1, f32[8,256,256]{2,1,0:T(8,128)S(1)} %shard_map.109.refs_8_.refs_2_, f32[256,768]{1,0:T(8,128)S(1)} %shard_map.112.refs_3_, ...), custom_call_target="tpu_custom_call" | custom-call | flops 1840250880 | bytes 10487296 | tf_op jit(solution)/shard_map/pallas_call | solution.py:164
  47.1 0.2 collective-permute-start.19
  47.3 0.1 slice_bitcast_fusion.2
  47.3 0.3 shard_map.114.refs_0_
  47.6 1.2 %collective-permute-done.19.refs_1_ = bf16[384,411]{1,0:T(8,128)(2,1)S(1)} collective-permute-done((bf16[384,411]{1,0:T(8,128)(2,1)S(1)}, bf16[384,411]{1,0:T(8,128)(2,1)S(1)}, u32[]{:S(2)}, u32[]{:S(2)}) %collective-permute-start.19) | collective-permute-done | bytes 315680 | tf_op jit(solution)/shard_map/ppermute | solution.py:502
  48.9 0.1 shard_map.115
  48.9 3.8 %collective-permute-start.20 = (bf16[96,411]{1,0:T(8,128)(2,1)S(1)}, bf16[96,411]{1,0:T(8,128)(2,1)S(1)}, u32[]{:S(2)}, u32[]{:S(2)}) collective-permute-start(bf16[96,411]{1,0:T(8,128)(2,1)S(1)} %get-tuple-element.36), channel_id=1, source_target_pairs={{0,6},{1,7},{2,4},{3,5},{4,2},{5,3},{6,0},{7,1},{8,14},{9,15},{10,... | collective-permute-start | bytes 236744 | tf_op jit(solution)/shard_map/ppermute | solution.py:502
  52.7 0.3 collective-permute-start.21
  53.0 0.3 collective-permute-start.22
  53.4 2.6 %collective-permute-done.20.refs_0_ = bf16[96,411]{1,0:T(8,128)(2,1)S(1)} collective-permute-done((bf16[96,411]{1,0:T(8,128)(2,1)S(1)}, bf16[96,411]{1,0:T(8,128)(2,1)S(1)}, u32[]{:S(2)}, u32[]{:S(2)}) %collective-permute-start.20) | collective-permute-done | bytes 78944 | tf_op jit(solution)/shard_map/ppermute | solution.py:502
  55.9 2.0 %collective-permute-done.21.refs_1_ = bf16[96,411]{1,0:T(8,128)(2,1)S(1)} collective-permute-done((bf16[96,411]{1,0:T(8,128)(2,1)S(1)}, bf16[96,411]{1,0:T(8,128)(2,1)S(1)}, u32[]{:S(2)}, u32[]{:S(2)}) %collective-permute-start.21) | collective-permute-done | bytes 78944 | tf_op jit(solution)/shard_map/ppermute | solution.py:502
  57.9 0.0 collective-permute-done.22.refs_2_
  57.9 0.2 shard_map.116
  58.2 1.7 %collective-permute-start.23 = (bf16[32,411]{1,0:T(8,128)(2,1)S(1)}, bf16[32,411]{1,0:T(8,128)(2,1)S(1)}, u32[]{:S(2)}, u32[]{:S(2)}) collective-permute-start(bf16[32,411]{1,0:T(8,128)(2,1)S(1)} %get-tuple-element.40), channel_id=1, source_target_pairs={{0,24},{8,16},{16,8},{24,0},{1,25},{9,17},{17,9},{25,1},{2,26},{10... | collective-permute-start | bytes 78920 | tf_op jit(solution)/shard_map/ppermute | solution.py:505
  59.8 1.6 %collective-permute-start.24 = (bf16[32,411]{1,0:T(8,128)(2,1)S(1)}, bf16[32,411]{1,0:T(8,128)(2,1)S(1)}, u32[]{:S(2)}, u32[]{:S(2)}) collective-permute-start(bf16[32,411]{1,0:T(8,128)(2,1)S(1)} %get-tuple-element.41), channel_id=1, source_target_pairs={{0,16},{8,24},{16,0},{24,8},{1,17},{9,25},{17,1},{25,9},{2,18},{10... | collective-permute-start | bytes 78920 | tf_op jit(solution)/shard_map/ppermute | solution.py:505
  61.4 1.2 %collective-permute-start.25 = (bf16[32,411]{1,0:T(8,128)(2,1)S(1)}, bf16[32,411]{1,0:T(8,128)(2,1)S(1)}, u32[]{:S(2)}, u32[]{:S(2)}) collective-permute-start(bf16[32,411]{1,0:T(8,128)(2,1)S(1)} %get-tuple-element.42), channel_id=1, source_target_pairs={{0,8},{8,0},{16,24},{24,16},{1,9},{9,1},{17,25},{25,17},{2,10},{10... | collective-permute-start | bytes 78920 | tf_op jit(solution)/shard_map/ppermute | solution.py:505
  62.6 0.1 maximum_sqrt_fusion
  62.7 0.1 copy.19
  62.8 1.2 %collective-permute-done.23.refs_0_ = bf16[32,411]{1,0:T(8,128)(2,1)S(1)} collective-permute-done((bf16[32,411]{1,0:T(8,128)(2,1)S(1)}, bf16[32,411]{1,0:T(8,128)(2,1)S(1)}, u32[]{:S(2)}, u32[]{:S(2)}) %collective-permute-start.23) | collective-permute-done | bytes 26336 | tf_op jit(solution)/shard_map/ppermute | solution.py:505
  64.0 0.9 %collective-permute-done.24.refs_1_ = bf16[32,411]{1,0:T(8,128)(2,1)S(1)} collective-permute-done((bf16[32,411]{1,0:T(8,128)(2,1)S(1)}, bf16[32,411]{1,0:T(8,128)(2,1)S(1)}, u32[]{:S(2)}, u32[]{:S(2)}) %collective-permute-start.24) | collective-permute-done | bytes 26336 | tf_op jit(solution)/shard_map/ppermute | solution.py:505
  64.9 0.4 collective-permute-done.25.refs_2_
  65.3 1.3 %shard_map.117 = f32[4,32,411]{2,1,0:T(8,128)} custom-call(bf16[32,411]{1,0:T(8,128)(2,1)S(1)} %collective-permute-done.23.refs_0_, bf16[32,411]{1,0:T(8,128)(2,1)S(1)} %collective-permute-done.24.refs_1_, bf16[32,411]{1,0:T(8,128)(2,1)S(1)} %collective-permute-done.25.refs_2_, bf16[32,411]{1,0:T(8,128)(2,1)S(1)} %get-tuple-element.43.refs_3_, ...), custom_call_target="tpu_custom_call" | custom-call | flops 5260800 | bytes 106752 | tf_op jit(solution)/shard_map/pallas_call | solution.py:164
  (30 shorter events, 0.2 us)
Async XLA Ops:
  0.0 8.2 %copy-start.4 = (bf16[128,768]{1,0:T(8,128)(2,1)S(1)}, bf16[128,768]{1,0:T(8,128)(2,1)}, u32[]{:S(2)}) copy-start(bf16[128,768]{1,0:T(8,128)(2,1)} %refs_0_.3) | copy-start | bytes 589828
  0.0 15.8 %copy-start.3 = (bf16[411,256]{1,0:T(8,128)(2,1)S(1)}, bf16[411,256]{1,0:T(8,128)(2,1)}, u32[]{:S(2)}) copy-start(bf16[411,256]{1,0:T(8,128)(2,1)} %refs_0_.4) | copy-start | bytes 631300
  0.0 6.7 %copy-start.7 = (f32[256]{0:T(256)S(1)}, f32[256]{0:T(256)}, u32[]{:S(2)}) copy-start(f32[256]{0:T(256)} %bias_ref.1) | copy-start | bytes 3076
  0.0 6.7 %copy-start.8 = (s32[128]{0:T(128)S(1)}, s32[128]{0:T(128)}, u32[]{:S(2)}) copy-start(s32[128]{0:T(128)} %usable_ref.1) | copy-start | bytes 1540
  0.0 6.7 %copy-start.6 = (f32[4,32]{1,0:T(4,128)S(1)}, f32[4,32]{1,0:T(4,128)}, u32[]{:S(2)}) copy-start(f32[4,32]{1,0:T(4,128)} %diffusivity_ref.1) | copy-start | bytes 1540
  0.0 6.7 %copy-start.2 = (f32[4,32,411]{2,1,0:T(8,128)S(1)}, f32[4,32,411]{2,1,0:T(8,128)}, u32[]{:S(2)}) copy-start(f32[4,32,411]{2,1,0:T(8,128)} %fields_ref.1) | copy-start | bytes 631300
  0.0 8.2 %collective-permute-start.1 = (bf16[128,768]{1,0:T(8,128)(2,1)}, bf16[128,768]{1,0:T(8,128)(2,1)S(1)}, u32[]{:S(2)}, u32[]{:S(2)}) collective-permute-start(bf16[128,768]{1,0:T(8,128)(2,1)} %refs_0_.3), channel_id=1, source_target_pairs={{0,8},{8,0},{16,24},{24,16},{1,9},{9,1},{17,25},{25,17},{2,10},{10... | collective-permute-start | bytes 589832 | tf_op jit(solution)/shard_map/ppermute | solution.py:505
  3.1 12.3 %collective-permute-start.8 = (bf16[411,256]{1,0:T(8,128)(2,1)}, bf16[411,256]{1,0:T(8,128)(2,1)S(1)}, u32[]{:S(2)}, u32[]{:S(2)}) collective-permute-start(bf16[411,256]{1,0:T(8,128)(2,1)} %refs_0_.4), channel_id=1, source_target_pairs={{0,4},{1,5},{2,6},{3,7},{4,0},{5,1},{6,2},{7,3},{8,12},{9,13},{10,... | collective-permute-start | bytes 631304 | tf_op jit(solution)/shard_map/ppermute | solution.py:502
  4.6 10.8 %collective-permute-start.7 = (bf16[411,256]{1,0:T(8,128)(2,1)}, bf16[411,256]{1,0:T(8,128)(2,1)S(1)}, u32[]{:S(2)}, u32[]{:S(2)}) collective-permute-start(bf16[411,256]{1,0:T(8,128)(2,1)} %refs_0_.4), channel_id=1, source_target_pairs={{0,2},{1,3},{2,0},{3,1},{4,6},{5,7},{6,4},{7,5},{8,10},{9,11},{10,... | collective-permute-start | bytes 631304 | tf_op jit(solution)/shard_map/ppermute | solution.py:502
  6.1 9.7 %collective-permute-start.9 = (bf16[411,256]{1,0:T(8,128)(2,1)}, bf16[411,256]{1,0:T(8,128)(2,1)S(1)}, u32[]{:S(2)}, u32[]{:S(2)}) collective-permute-start(bf16[411,256]{1,0:T(8,128)(2,1)} %refs_0_.4), channel_id=1, source_target_pairs={{0,6},{1,7},{2,4},{3,5},{4,2},{5,3},{6,0},{7,1},{8,14},{9,15},{10,... | collective-permute-start | bytes 631304 | tf_op jit(solution)/shard_map/ppermute | solution.py:502
  6.7 18.5 %copy-start.9 = (s32[256,1]{0,1:T(1,128)S(1)}, s32[256,1]{0,1:T(1,128)}, u32[]{:S(2)}) copy-start(s32[256,1]{0,1:T(1,128)} %param.12) | copy-start | bytes 3076
  6.9 3.7 %collective-permute-start = (bf16[16,512]{1,0:T(8,128)(2,1)S(1)}, bf16[16,512]{1,0:T(8,128)(2,1)S(1)}, u32[]{:S(2)}, u32[]{:S(2)}) collective-permute-start(bf16[16,512]{1,0:T(8,128)(2,1)S(1)} %shard_map.102.refs_0_), channel_id=1, source_target_pairs={{0,8},{8,0},{16,24},{24,16},{1,9},{9,1},{17,25},{25,17},{2,10},{10... | collective-permute-start | bytes 49160 | tf_op jit(solution)/shard_map/ppermute | solution.py:505
  10.6 4.8 %collective-permute-start.2 = (bf16[32,512]{1,0:T(8,128)(2,1)S(1)}, bf16[32,512]{1,0:T(8,128)(2,1)S(1)}, u32[]{:S(2)}, u32[]{:S(2)}) collective-permute-start(bf16[32,512]{1,0:T(8,128)(2,1)S(1)} %shard_map.104.refs_0_), channel_id=1, source_target_pairs={{0,16},{8,24},{16,0},{24,8},{1,17},{9,25},{17,1},{25,9},{2,18},{10... | collective-permute-start | bytes 98312 | tf_op jit(solution)/shard_map/ppermute | solution.py:505
  15.9 10.9 %collective-permute-start.10 = (bf16[1664,256]{1,0:T(8,128)(2,1)S(1)}, bf16[1664,256]{1,0:T(8,128)(2,1)S(1)}, u32[]{:S(2)}, u32[]{:S(2)}) collective-permute-start(bf16[1664,256]{1,0:T(8,128)(2,1)S(1)} %shard_map.107.refs_7_.refs_5_), channel_id=1, source_target_pairs={{0,1},{1,0},{2,3},{3,2},{4,5},{5,4},{6,7},{7,6},{8,9},{9,8},{10,11... | collective-permute-start | bytes 2555912 | tf_op jit(solution)/shard_map/ppermute | solution.py:502
  16.0 13.6 %collective-permute-start.11 = (bf16[256,768]{1,0:T(8,128)(2,1)S(1)}, bf16[256,768]{1,0:T(8,128)(2,1)S(1)}, u32[]{:S(2)}, u32[]{:S(2)}) collective-permute-start(bf16[256,768]{1,0:T(8,128)(2,1)S(1)} %shard_map.103.refs_2_.refs_9_), channel_id=1, source_target_pairs={{0,16},{1,17},{2,3},{3,2},{4,20},{5,21},{6,7},{7,6},{8,9},{9,8},{1... | collective-permute-start | bytes 1179656 | tf_op jit(solution)/shard_map/ppermute | solution.py:514
  18.6 5.5 %collective-permute-start.5 = (bf16[64,512]{1,0:T(8,128)(2,1)S(1)}, bf16[64,512]{1,0:T(8,128)(2,1)S(1)}, u32[]{:S(2)}, u32[]{:S(2)}) collective-permute-start(bf16[64,512]{1,0:T(8,128)(2,1)S(1)} %shard_map.105.refs_0_.refs_4_), channel_id=1, source_target_pairs={{0,6},{1,7},{2,4},{3,5},{4,2},{5,3},{6,0},{7,1},{8,14},{9,15},{10,... | collective-permute-start | bytes 196616 | tf_op jit(solution)/shard_map/ppermute | solution.py:502
  18.9 5.5 %collective-permute-start.4 = (bf16[64,512]{1,0:T(8,128)(2,1)S(1)}, bf16[64,512]{1,0:T(8,128)(2,1)S(1)}, u32[]{:S(2)}, u32[]{:S(2)}) collective-permute-start(bf16[64,512]{1,0:T(8,128)(2,1)S(1)} %shard_map.105.refs_0_.refs_4_), channel_id=1, source_target_pairs={{0,4},{1,5},{2,6},{3,7},{4,0},{5,1},{6,2},{7,3},{8,12},{9,13},{10,... | collective-permute-start | bytes 196616 | tf_op jit(solution)/shard_map/ppermute | solution.py:502
  20.1 5.0 %collective-permute-start.3 = (bf16[64,512]{1,0:T(8,128)(2,1)S(1)}, bf16[64,512]{1,0:T(8,128)(2,1)S(1)}, u32[]{:S(2)}, u32[]{:S(2)}) collective-permute-start(bf16[64,512]{1,0:T(8,128)(2,1)S(1)} %shard_map.105.refs_0_.refs_4_), channel_id=1, source_target_pairs={{0,2},{1,3},{2,0},{3,1},{4,6},{5,7},{6,4},{7,5},{8,10},{9,11},{10,... | collective-permute-start | bytes 196616 | tf_op jit(solution)/shard_map/ppermute | solution.py:502
  25.2 1.6 %collective-permute-start.6 = (bf16[256,512]{1,0:T(8,128)(2,1)S(1)}, bf16[256,512]{1,0:T(8,128)(2,1)S(1)}, u32[]{:S(2)}, u32[]{:S(2)}) collective-permute-start(bf16[256,512]{1,0:T(8,128)(2,1)S(1)} %shard_map.106.refs_5_), channel_id=1, source_target_pairs={{0,1},{1,0},{2,3},{3,2},{4,5},{5,4},{6,7},{7,6},{8,9},{9,8},{10,11... | collective-permute-start | bytes 786440 | tf_op jit(solution)/shard_map/ppermute | solution.py:502
  25.2 1.9 %copy-start = (bf16[2048,768]{1,0:T(8,128)(2,1)S(1)}, bf16[2048,768]{1,0:T(8,128)(2,1)}, u32[]{:S(2)}) copy-start(bf16[2048,768]{1,0:T(8,128)(2,1)} %refs_0_.5) | copy-start | bytes 9437188
  25.3 1.9 %copy-start.5 = (f32[768]{0:T(1024)S(1)}, f32[768]{0:T(1024)}, u32[]{:S(2)}) copy-start(f32[768]{0:T(1024)} %refs_3_.1) | copy-start | bytes 9220
  29.9 7.8 %collective-permute-start.12 = (bf16[128,768]{1,0:T(8,128)(2,1)S(1)}, bf16[128,768]{1,0:T(8,128)(2,1)S(1)}, u32[]{:S(2)}, u32[]{:S(2)}) collective-permute-start(bf16[128,768]{1,0:T(8,128)(2,1)S(1)} %get-tuple-element.30.refs_0_), channel_id=1, source_target_pairs={{0,2},{1,3},{2,0},{3,1},{4,5},{5,4},{6,7},{7,6},{8,10},{9,11},{10,... | collective-permute-start | bytes 589832 | tf_op jit(solution)/shard_map/ppermute | solution.py:514
  31.2 7.7 %collective-permute-start.13 = (bf16[128,768]{1,0:T(8,128)(2,1)S(1)}, bf16[128,768]{1,0:T(8,128)(2,1)S(1)}, u32[]{:S(2)}, u32[]{:S(2)}) collective-permute-start(bf16[128,768]{1,0:T(8,128)(2,1)S(1)} %get-tuple-element.31.refs_1_), channel_id=1, source_target_pairs={{0,4},{1,5},{2,3},{3,2},{4,0},{5,1},{6,7},{7,6},{8,9},{9,8},{10,14... | collective-permute-start | bytes 589832 | tf_op jit(solution)/shard_map/ppermute | solution.py:514
  31.2 11.2 %collective-permute-start.14 = (bf16[128,768]{1,0:T(8,128)(2,1)S(1)}, bf16[128,768]{1,0:T(8,128)(2,1)S(1)}, u32[]{:S(2)}, u32[]{:S(2)}) collective-permute-start(bf16[128,768]{1,0:T(8,128)(2,1)S(1)} %get-tuple-element.30.refs_0_), channel_id=1, source_target_pairs={{0,4},{1,5},{2,3},{3,2},{4,0},{5,1},{6,7},{7,6},{8,9},{9,8},{10,14... | collective-permute-start | bytes 589832 | tf_op jit(solution)/shard_map/ppermute | solution.py:514
  33.2 9.2 %collective-permute-start.15 = (bf16[128,768]{1,0:T(8,128)(2,1)S(1)}, bf16[128,768]{1,0:T(8,128)(2,1)S(1)}, u32[]{:S(2)}, u32[]{:S(2)}) collective-permute-start(bf16[128,768]{1,0:T(8,128)(2,1)S(1)} %get-tuple-element.31.refs_1_), channel_id=1, source_target_pairs={{0,2},{1,3},{2,0},{3,1},{4,5},{5,4},{6,7},{7,6},{8,10},{9,11},{10,... | collective-permute-start | bytes 589832 | tf_op jit(solution)/shard_map/ppermute | solution.py:514
  37.6 4.8 %collective-permute-start.16 = (bf16[128,768]{1,0:T(8,128)(2,1)S(1)}, bf16[128,768]{1,0:T(8,128)(2,1)S(1)}, u32[]{:S(2)}, u32[]{:S(2)}) collective-permute-start(bf16[128,768]{1,0:T(8,128)(2,1)S(1)} %collective-permute-done.12.refs_2_), channel_id=1, source_target_pairs={{0,1},{1,0},{2,6},{3,7},{4,5},{5,4},{6,2},{7,3},{8,12},{9,13},{10,... | collective-permute-start | bytes 589832 | tf_op jit(solution)/shard_map/ppermute | solution.py:514
  38.9 3.5 %collective-permute-start.17 = (bf16[128,768]{1,0:T(8,128)(2,1)S(1)}, bf16[128,768]{1,0:T(8,128)(2,1)S(1)}, u32[]{:S(2)}, u32[]{:S(2)}) collective-permute-start(bf16[128,768]{1,0:T(8,128)(2,1)S(1)} %collective-permute-done.13.refs_3_), channel_id=1, source_target_pairs={{0,1},{1,0},{2,3},{3,2},{4,6},{5,7},{6,4},{7,5},{8,9},{9,8},{10,11... | collective-permute-start | bytes 589832 | tf_op jit(solution)/shard_map/ppermute | solution.py:514
  39.5 3.0 %copy-start.1 = (bf16[1536,768]{1,0:T(8,128)(2,1)S(1)}, bf16[1536,768]{1,0:T(8,128)(2,1)}, u32[]{:S(2)}) copy-start(bf16[1536,768]{1,0:T(8,128)(2,1)} %refs_1_.1) | copy-start | bytes 7077892
  42.5 1.8 %collective-permute-start.18 = (bf16[256,768]{1,0:T(8,128)(2,1)S(1)}, bf16[256,768]{1,0:T(8,128)(2,1)S(1)}, u32[]{:S(2)}, u32[]{:S(2)}) collective-permute-start(bf16[256,768]{1,0:T(8,128)(2,1)S(1)} %shard_map.111.depart_ref), channel_id=1, source_target_pairs={{0,1},{1,0},{2,3},{3,2},{4,5},{5,4},{6,7},{7,6},{8,9},{9,8},{10,11... | collective-permute-start | bytes 1179656 | tf_op jit(solution)/shard_map/ppermute | solution.py:502
  47.1 1.8 %collective-permute-start.19 = (bf16[384,411]{1,0:T(8,128)(2,1)S(1)}, bf16[384,411]{1,0:T(8,128)(2,1)S(1)}, u32[]{:S(2)}, u32[]{:S(2)}) collective-permute-start(bf16[384,411]{1,0:T(8,128)(2,1)S(1)} %get-tuple-element.35), channel_id=1, source_target_pairs={{0,1},{1,0},{2,3},{3,2},{4,5},{5,4},{6,7},{7,6},{8,9},{9,8},{10,11... | collective-permute-start | bytes 946952 | tf_op jit(solution)/shard_map/ppermute | solution.py:502
  48.9 7.0 %collective-permute-start.20 = (bf16[96,411]{1,0:T(8,128)(2,1)S(1)}, bf16[96,411]{1,0:T(8,128)(2,1)S(1)}, u32[]{:S(2)}, u32[]{:S(2)}) collective-permute-start(bf16[96,411]{1,0:T(8,128)(2,1)S(1)} %get-tuple-element.36), channel_id=1, source_target_pairs={{0,6},{1,7},{2,4},{3,5},{4,2},{5,3},{6,0},{7,1},{8,14},{9,15},{10,... | collective-permute-start | bytes 236744 | tf_op jit(solution)/shard_map/ppermute | solution.py:502
  52.7 5.2 %collective-permute-start.21 = (bf16[96,411]{1,0:T(8,128)(2,1)S(1)}, bf16[96,411]{1,0:T(8,128)(2,1)S(1)}, u32[]{:S(2)}, u32[]{:S(2)}) collective-permute-start(bf16[96,411]{1,0:T(8,128)(2,1)S(1)} %get-tuple-element.37), channel_id=1, source_target_pairs={{0,4},{1,5},{2,6},{3,7},{4,0},{5,1},{6,2},{7,3},{8,12},{9,13},{10,... | collective-permute-start | bytes 236744 | tf_op jit(solution)/shard_map/ppermute | solution.py:502
  53.0 4.9 %collective-permute-start.22 = (bf16[96,411]{1,0:T(8,128)(2,1)S(1)}, bf16[96,411]{1,0:T(8,128)(2,1)S(1)}, u32[]{:S(2)}, u32[]{:S(2)}) collective-permute-start(bf16[96,411]{1,0:T(8,128)(2,1)S(1)} %get-tuple-element.38), channel_id=1, source_target_pairs={{0,2},{1,3},{2,0},{3,1},{4,6},{5,7},{6,4},{7,5},{8,10},{9,11},{10,... | collective-permute-start | bytes 236744 | tf_op jit(solution)/shard_map/ppermute | solution.py:502
  58.2 5.9 %collective-permute-start.23 = (bf16[32,411]{1,0:T(8,128)(2,1)S(1)}, bf16[32,411]{1,0:T(8,128)(2,1)S(1)}, u32[]{:S(2)}, u32[]{:S(2)}) collective-permute-start(bf16[32,411]{1,0:T(8,128)(2,1)S(1)} %get-tuple-element.40), channel_id=1, source_target_pairs={{0,24},{8,16},{16,8},{24,0},{1,25},{9,17},{17,9},{25,1},{2,26},{10... | collective-permute-start | bytes 78920 | tf_op jit(solution)/shard_map/ppermute | solution.py:505
  59.8 5.1 %collective-permute-start.24 = (bf16[32,411]{1,0:T(8,128)(2,1)S(1)}, bf16[32,411]{1,0:T(8,128)(2,1)S(1)}, u32[]{:S(2)}, u32[]{:S(2)}) collective-permute-start(bf16[32,411]{1,0:T(8,128)(2,1)S(1)} %get-tuple-element.41), channel_id=1, source_target_pairs={{0,16},{8,24},{16,0},{24,8},{1,17},{9,25},{17,1},{25,9},{2,18},{10... | collective-permute-start | bytes 78920 | tf_op jit(solution)/shard_map/ppermute | solution.py:505
  61.4 3.9 %collective-permute-start.25 = (bf16[32,411]{1,0:T(8,128)(2,1)S(1)}, bf16[32,411]{1,0:T(8,128)(2,1)S(1)}, u32[]{:S(2)}, u32[]{:S(2)}) collective-permute-start(bf16[32,411]{1,0:T(8,128)(2,1)S(1)} %get-tuple-element.42), channel_id=1, source_target_pairs={{0,8},{8,0},{16,24},{24,16},{1,9},{9,1},{17,25},{25,17},{2,10},{10... | collective-permute-start | bytes 78920 | tf_op jit(solution)/shard_map/ppermute | solution.py:505

commit v21 on v18

--- a/solution.py
+++ b/solution.py
@@ -659,7 +659,7 @@
         [shape((p.room, p.features), half)] * p.tiles,
         partial,
     )
-    partial = [trade(partial[k], k) for k in range(p.tiles - 1, 0, -1)] + [partial[0]]
+    partial = [trade(partial[k], k) for k in sorted(range(1, p.tiles), key=lambda k: -(k & -k))] + [partial[0]]
     edge = 8
     kappa = kappa.reshape(3, reach, p.lane)
     root = jnp.sqrt(

time: 66.8 us -> 67.6 us (1.012)
  waiting for transfers between devices: 27.9 us -> 28.7 us
    ppermute x6, waiting for transfers between devices: 8.29 us -> 9.11 us  [trade(): return lax.ppermute(value, 'tile', [(a, a ^ mask) for a in range(p.tiles)])]
where the time goes in v21:
time: 67.6 us; the launch traced here: 67.5 us
  waiting for transfers between devices  28.7 us (42%)
  starting transfers between devices  28.1 us (42%)
  Pallas kernels  9.8 us (14%)
    ppermute x13, starting transfers between devices, flip(): return lax.ppermute(value, 'chan', [(b, b ^ mask) for b in range(p.chans)])  11.8 us
    ppermute x13, waiting for transfers between devices, flip(): return lax.ppermute(value, 'chan', [(b, b ^ mask) for b in range(p.chans)])  11 us
    ppermute x6, starting transfers between devices, trade(): return lax.ppermute(value, 'tile', [(a, a ^ mask) for a in range(p.tiles)])  10.3 us
    pallas_call x18, Pallas kernels, call(): pl.pallas_call(kernel, out_shape=out_shape, in_specs=[far if k in in_hbm...  9.8 us
    ppermute x6, waiting for transfers between devices, trade(): return lax.ppermute(value, 'tile', [(a, a ^ mask) for a in range(p.tiles)])  9.11 us
    ppermute x7, waiting for transfers between devices, send(): lax.ppermute(value, both, sorted(((number(a), number(b)) for a, b in pair...  8.57 us
    ppermute x7, starting transfers between devices, send(): lax.ppermute(value, both, sorted(((number(a), number(b)) for a, b in pair...  5.98 us
  transfers between devices with their start and end apart: 26, of which 18 were waited for; matrix products, arithmetic and copies ran while one was open for 0% of the time, Pallas kernels for 7%

profile of v21, /device:TPU:0, one launch (start us, length us, event | category | flops | bytes accessed | tf_op | source)
XLA Modules:
  0.0 67.5 jit_solution(11448263482501413521)
XLA Ops:
  0.0 3.1 %collective-permute-start.1 = (bf16[128,768]{1,0:T(8,128)(2,1)}, bf16[128,768]{1,0:T(8,128)(2,1)S(1)}, u32[]{:S(2)}, u32[]{:S(2)}) collective-permute-start(bf16[128,768]{1,0:T(8,128)(2,1)} %refs_0_.3), channel_id=1, source_target_pairs={{0,8},{8,0},{16,24},{24,16},{1,9},{9,1},{17,25},{25,17},{2,10},{10... | collective-permute-start | bytes 589832 | tf_op jit(solution)/shard_map/ppermute | solution.py:503
  3.1 1.5 %collective-permute-start.8 = (bf16[411,256]{1,0:T(8,128)(2,1)}, bf16[411,256]{1,0:T(8,128)(2,1)S(1)}, u32[]{:S(2)}, u32[]{:S(2)}) collective-permute-start(bf16[411,256]{1,0:T(8,128)(2,1)} %refs_0_.4), channel_id=1, source_target_pairs={{0,4},{1,5},{2,6},{3,7},{4,0},{5,1},{6,2},{7,3},{8,12},{9,13},{10,... | collective-permute-start | bytes 631304 | tf_op jit(solution)/shard_map/ppermute | solution.py:500
  4.6 1.5 %collective-permute-start.7 = (bf16[411,256]{1,0:T(8,128)(2,1)}, bf16[411,256]{1,0:T(8,128)(2,1)S(1)}, u32[]{:S(2)}, u32[]{:S(2)}) collective-permute-start(bf16[411,256]{1,0:T(8,128)(2,1)} %refs_0_.4), channel_id=1, source_target_pairs={{0,2},{1,3},{2,0},{3,1},{4,6},{5,7},{6,4},{7,5},{8,10},{9,11},{10,... | collective-permute-start | bytes 631304 | tf_op jit(solution)/shard_map/ppermute | solution.py:500
  6.1 0.5 collective-permute-start.9
  6.7 0.0 copy-start.9
  6.7 0.2 shard_map.102.refs_0_
  6.9 0.1 collective-permute-start
  7.0 1.3 %collective-permute-done.1.refs_1_ = bf16[128,768]{1,0:T(8,128)(2,1)S(1)} collective-permute-done((bf16[128,768]{1,0:T(8,128)(2,1)}, bf16[128,768]{1,0:T(8,128)(2,1)S(1)}, u32[]{:S(2)}, u32[]{:S(2)}) %collective-permute-start.1) | collective-permute-done | bytes 196640 | tf_op jit(solution)/shard_map/ppermute | solution.py:503
  8.3 2.4 %collective-permute-done.refs_1_ = bf16[16,512]{1,0:T(8,128)(2,1)S(1)} collective-permute-done((bf16[16,512]{1,0:T(8,128)(2,1)S(1)}, bf16[16,512]{1,0:T(8,128)(2,1)S(1)}, u32[]{:S(2)}, u32[]{:S(2)}) %collective-permute-start) | collective-permute-done | bytes 16416 | tf_op jit(solution)/shard_map/ppermute | solution.py:503
  10.6 2.7 %collective-permute-start.2 = (bf16[32,512]{1,0:T(8,128)(2,1)S(1)}, bf16[32,512]{1,0:T(8,128)(2,1)S(1)}, u32[]{:S(2)}, u32[]{:S(2)}) collective-permute-start(bf16[32,512]{1,0:T(8,128)(2,1)S(1)} %shard_map.104.refs_0_), channel_id=1, source_target_pairs={{0,16},{8,24},{16,0},{24,8},{1,17},{9,25},{17,1},{25,9},{2,18},{10... | collective-permute-start | bytes 98312 | tf_op jit(solution)/shard_map/ppermute | solution.py:503
  13.3 2.1 %collective-permute-done.2.refs_1_ = bf16[32,512]{1,0:T(8,128)(2,1)S(1)} collective-permute-done((bf16[32,512]{1,0:T(8,128)(2,1)S(1)}, bf16[32,512]{1,0:T(8,128)(2,1)S(1)}, u32[]{:S(2)}, u32[]{:S(2)}) %collective-permute-start.2) | collective-permute-done | bytes 32800 | tf_op jit(solution)/shard_map/ppermute | solution.py:503
  15.5 0.0 collective-permute-done.7.refs_1_
  15.5 0.3 collective-permute-done.9.refs_3_
  15.8 0.1 shard_map.107.refs_7_.refs_5_
  15.9 0.1 collective-permute-start.10
  15.9 2.7 %collective-permute-start.11 = (bf16[256,768]{1,0:T(8,128)(2,1)S(1)}, bf16[256,768]{1,0:T(8,128)(2,1)S(1)}, u32[]{:S(2)}, u32[]{:S(2)}) collective-permute-start(bf16[256,768]{1,0:T(8,128)(2,1)S(1)} %shard_map.103.refs_2_.refs_0_), channel_id=1, source_target_pairs={{0,16},{1,17},{2,3},{3,2},{4,20},{5,21},{6,7},{7,6},{8,9},{9,8},{1... | collective-permute-start | bytes 1179656 | tf_op jit(solution)/shard_map/ppermute | solution.py:512
  18.6 0.3 collective-permute-start.5
  18.9 1.2 %collective-permute-start.4 = (bf16[64,512]{1,0:T(8,128)(2,1)S(1)}, bf16[64,512]{1,0:T(8,128)(2,1)S(1)}, u32[]{:S(2)}, u32[]{:S(2)}) collective-permute-start(bf16[64,512]{1,0:T(8,128)(2,1)S(1)} %shard_map.105.refs_0_.refs_4_), channel_id=1, source_target_pairs={{0,4},{1,5},{2,6},{3,7},{4,0},{5,1},{6,2},{7,3},{8,12},{9,13},{10,... | collective-permute-start | bytes 196616 | tf_op jit(solution)/shard_map/ppermute | solution.py:500
  20.1 2.0 %collective-permute-start.3 = (bf16[64,512]{1,0:T(8,128)(2,1)S(1)}, bf16[64,512]{1,0:T(8,128)(2,1)S(1)}, u32[]{:S(2)}, u32[]{:S(2)}) collective-permute-start(bf16[64,512]{1,0:T(8,128)(2,1)S(1)} %shard_map.105.refs_0_.refs_4_), channel_id=1, source_target_pairs={{0,2},{1,3},{2,0},{3,1},{4,6},{5,7},{6,4},{7,5},{8,10},{9,11},{10,... | collective-permute-start | bytes 196616 | tf_op jit(solution)/shard_map/ppermute | solution.py:500
  22.1 2.0 %collective-permute-done.5.refs_3_ = bf16[64,512]{1,0:T(8,128)(2,1)S(1)} collective-permute-done((bf16[64,512]{1,0:T(8,128)(2,1)S(1)}, bf16[64,512]{1,0:T(8,128)(2,1)S(1)}, u32[]{:S(2)}, u32[]{:S(2)}) %collective-permute-start.5) | collective-permute-done | bytes 65568 | tf_op jit(solution)/shard_map/ppermute | solution.py:500
  24.1 0.3 collective-permute-done.4.refs_2_
  24.4 0.8 %collective-permute-done.3.refs_1_ = bf16[64,512]{1,0:T(8,128)(2,1)S(1)} collective-permute-done((bf16[64,512]{1,0:T(8,128)(2,1)S(1)}, bf16[64,512]{1,0:T(8,128)(2,1)S(1)}, u32[]{:S(2)}, u32[]{:S(2)}) %collective-permute-start.3) | collective-permute-done | bytes 65568 | tf_op jit(solution)/shard_map/ppermute | solution.py:500
  25.2 0.1 collective-permute-start.6
  25.2 0.0 copy-start
  25.3 0.0 copy-start.5
  25.3 0.8 %shard_map.100 = (s32[256,1]{1,0:T(8,128)S(1)}, s32[256,1]{1,0:T(8,128)S(1)}, s32[384,1]{1,0:T(8,128)S(1)}, s32[384,1]{1,0:T(8,128)S(1)}) custom-call(s32[1,256]{1,0:T(1,128)S(1)} %bitcast.12), custom_call_target="tpu_custom_call" | custom-call | flops 2000000000 | bytes 1024 | tf_op jit(solution)/shard_map/pallas_call | solution.py:164
  26.1 0.7 collective-permute-done.6.refs_6_
  26.8 0.0 collective-permute-done.10.refs_8_.refs_6_
  26.8 0.4 copy-done
  27.1 2.3 %shard_map.108 = (f32[256,768]{1,0:T(8,128)S(1)}, f32[256,1]{1,0:T(8,128)S(1)}, f32[8,256,256]{2,1,0:T(8,128)S(1)}, f32[24,128]{1,0:T(8,128)S(1)}) custom-call(s32[256,1]{1,0:T(8,128)S(1)} %get-tuple-element.25.refs_0_.place_ref, s32[256,1]{1,0:T(8,128)S(1)} %get-tuple-element.26.refs_1_, s32[24,1]{1,0:T(8,128)S(1)} %shard_map.101.after_ref.refs_2_, ...), custom_call_target="tpu_custom_call" | custom-call | flops 100000000 | bytes 5379168 | tf_op jit(solution)/shard_map/pallas_call | solution.py:164
  29.5 0.4 shard_map.110
  29.9 1.3 %collective-permute-start.12 = (bf16[128,768]{1,0:T(8,128)(2,1)S(1)}, bf16[128,768]{1,0:T(8,128)(2,1)S(1)}, u32[]{:S(2)}, u32[]{:S(2)}) collective-permute-start(bf16[128,768]{1,0:T(8,128)(2,1)S(1)} %get-tuple-element.30.refs_0_), channel_id=1, source_target_pairs={{0,2},{1,3},{2,0},{3,1},{4,5},{5,4},{6,7},{7,6},{8,10},{9,11},{10,... | collective-permute-start | bytes 589832 | tf_op jit(solution)/shard_map/ppermute | solution.py:512
  31.2 0.0 collective-permute-start.13
  31.2 2.0 %collective-permute-start.14 = (bf16[128,768]{1,0:T(8,128)(2,1)S(1)}, bf16[128,768]{1,0:T(8,128)(2,1)S(1)}, u32[]{:S(2)}, u32[]{:S(2)}) collective-permute-start(bf16[128,768]{1,0:T(8,128)(2,1)S(1)} %get-tuple-element.30.refs_0_), channel_id=1, source_target_pairs={{0,4},{1,5},{2,3},{3,2},{4,0},{5,1},{6,7},{7,6},{8,9},{9,8},{10,14... | collective-permute-start | bytes 589832 | tf_op jit(solution)/shard_map/ppermute | solution.py:512
  33.2 4.4 %collective-permute-done.12.refs_2_ = bf16[128,768]{1,0:T(8,128)(2,1)S(1)} collective-permute-done((bf16[128,768]{1,0:T(8,128)(2,1)S(1)}, bf16[128,768]{1,0:T(8,128)(2,1)S(1)}, u32[]{:S(2)}, u32[]{:S(2)}) %collective-permute-start.12) | collective-permute-done | bytes 196640 | tf_op jit(solution)/shard_map/ppermute | solution.py:512
  37.7 1.3 %collective-permute-done.13.refs_3_ = bf16[128,768]{1,0:T(8,128)(2,1)S(1)} collective-permute-done((bf16[128,768]{1,0:T(8,128)(2,1)S(1)}, bf16[128,768]{1,0:T(8,128)(2,1)S(1)}, u32[]{:S(2)}, u32[]{:S(2)}) %collective-permute-start.13) | collective-permute-done | bytes 196640 | tf_op jit(solution)/shard_map/ppermute | solution.py:512
  38.9 0.6 shard_map.109.refs_8_.refs_2_
  39.6 0.0 copy-start.1
  39.6 2.9 %collective-permute-done.14.refs_4_ = bf16[128,768]{1,0:T(8,128)(2,1)S(1)} collective-permute-done((bf16[128,768]{1,0:T(8,128)(2,1)S(1)}, bf16[128,768]{1,0:T(8,128)(2,1)S(1)}, u32[]{:S(2)}, u32[]{:S(2)}) %collective-permute-start.14) | collective-permute-done | bytes 196640 | tf_op jit(solution)/shard_map/ppermute | solution.py:512
  42.4 0.1 shard_map.111.depart_ref
  42.5 0.1 collective-permute-start.18
  42.6 0.5 shard_map.112.refs_3_
  43.1 1.2 %collective-permute-done.18.refs_4_ = bf16[256,768]{1,0:T(8,128)(2,1)S(1)} collective-permute-done((bf16[256,768]{1,0:T(8,128)(2,1)S(1)}, bf16[256,768]{1,0:T(8,128)(2,1)S(1)}, u32[]{:S(2)}, u32[]{:S(2)}) %collective-permute-start.18) | collective-permute-done | bytes 393248 | tf_op jit(solution)/shard_map/ppermute | solution.py:500
  44.3 2.8 %shard_map.113 = (bf16[411,256]{1,0:T(8,128)(2,1)S(1)}, bf16[384,411]{1,0:T(8,128)(2,1)S(1)}) custom-call(bf16[2048,768]{1,0:T(8,128)(2,1)S(1)} %copy-done, bf16[1536,768]{1,0:T(8,128)(2,1)S(1)} %copy-done.1, f32[8,256,256]{2,1,0:T(8,128)S(1)} %shard_map.109.refs_8_.refs_2_, f32[256,768]{1,0:T(8,128)S(1)} %shard_map.112.refs_3_, ...), custom_call_target="tpu_custom_call" | custom-call | flops 1840250880 | bytes 10487296 | tf_op jit(solution)/shard_map/pallas_call | solution.py:164
  47.1 0.2 collective-permute-start.19
  47.3 0.1 slice_bitcast_fusion.2
  47.4 0.3 shard_map.114.refs_0_
  47.7 1.2 %collective-permute-done.19.refs_1_ = bf16[384,411]{1,0:T(8,128)(2,1)S(1)} collective-permute-done((bf16[384,411]{1,0:T(8,128)(2,1)S(1)}, bf16[384,411]{1,0:T(8,128)(2,1)S(1)}, u32[]{:S(2)}, u32[]{:S(2)}) %collective-permute-start.19) | collective-permute-done | bytes 315680 | tf_op jit(solution)/shard_map/ppermute | solution.py:500
  48.9 0.1 shard_map.115
  49.0 3.8 %collective-permute-start.20 = (bf16[96,411]{1,0:T(8,128)(2,1)S(1)}, bf16[96,411]{1,0:T(8,128)(2,1)S(1)}, u32[]{:S(2)}, u32[]{:S(2)}) collective-permute-start(bf16[96,411]{1,0:T(8,128)(2,1)S(1)} %get-tuple-element.36), channel_id=1, source_target_pairs={{0,6},{1,7},{2,4},{3,5},{4,2},{5,3},{6,0},{7,1},{8,14},{9,15},{10,... | collective-permute-start | bytes 236744 | tf_op jit(solution)/shard_map/ppermute | solution.py:500
  52.8 0.3 collective-permute-start.21
  53.1 0.4 collective-permute-start.22
  53.4 2.6 %collective-permute-done.20.refs_0_ = bf16[96,411]{1,0:T(8,128)(2,1)S(1)} collective-permute-done((bf16[96,411]{1,0:T(8,128)(2,1)S(1)}, bf16[96,411]{1,0:T(8,128)(2,1)S(1)}, u32[]{:S(2)}, u32[]{:S(2)}) %collective-permute-start.20) | collective-permute-done | bytes 78944 | tf_op jit(solution)/shard_map/ppermute | solution.py:500
  56.0 2.0 %collective-permute-done.21.refs_1_ = bf16[96,411]{1,0:T(8,128)(2,1)S(1)} collective-permute-done((bf16[96,411]{1,0:T(8,128)(2,1)S(1)}, bf16[96,411]{1,0:T(8,128)(2,1)S(1)}, u32[]{:S(2)}, u32[]{:S(2)}) %collective-permute-start.21) | collective-permute-done | bytes 78944 | tf_op jit(solution)/shard_map/ppermute | solution.py:500
  58.0 0.2 shard_map.116
  58.2 1.6 %collective-permute-start.23 = (bf16[32,411]{1,0:T(8,128)(2,1)S(1)}, bf16[32,411]{1,0:T(8,128)(2,1)S(1)}, u32[]{:S(2)}, u32[]{:S(2)}) collective-permute-start(bf16[32,411]{1,0:T(8,128)(2,1)S(1)} %get-tuple-element.40), channel_id=1, source_target_pairs={{0,16},{8,24},{16,0},{24,8},{1,17},{9,25},{17,1},{25,9},{2,18},{10... | collective-permute-start | bytes 78920 | tf_op jit(solution)/shard_map/ppermute | solution.py:503
  59.9 0.6 collective-permute-start.24
  60.5 2.2 %collective-permute-start.25 = (bf16[32,411]{1,0:T(8,128)(2,1)S(1)}, bf16[32,411]{1,0:T(8,128)(2,1)S(1)}, u32[]{:S(2)}, u32[]{:S(2)}) collective-permute-start(bf16[32,411]{1,0:T(8,128)(2,1)S(1)} %get-tuple-element.42), channel_id=1, source_target_pairs={{0,24},{8,16},{16,8},{24,0},{1,25},{9,17},{17,9},{25,1},{2,26},{10... | collective-permute-start | bytes 78920 | tf_op jit(solution)/shard_map/ppermute | solution.py:503
  62.7 0.1 maximum_sqrt_fusion
  62.8 0.1 copy.19
  62.8 0.5 collective-permute-done.23.refs_0_
  63.3 0.5 collective-permute-done.24.refs_1_
  63.8 2.4 %collective-permute-done.25.refs_2_ = bf16[32,411]{1,0:T(8,128)(2,1)S(1)} collective-permute-done((bf16[32,411]{1,0:T(8,128)(2,1)S(1)}, bf16[32,411]{1,0:T(8,128)(2,1)S(1)}, u32[]{:S(2)}, u32[]{:S(2)}) %collective-permute-start.25) | collective-permute-done | bytes 26336 | tf_op jit(solution)/shard_map/ppermute | solution.py:503
  66.2 1.3 %shard_map.117 = f32[4,32,411]{2,1,0:T(8,128)} custom-call(bf16[32,411]{1,0:T(8,128)(2,1)S(1)} %collective-permute-done.23.refs_0_, bf16[32,411]{1,0:T(8,128)(2,1)S(1)} %collective-permute-done.24.refs_1_, bf16[32,411]{1,0:T(8,128)(2,1)S(1)} %collective-permute-done.25.refs_2_, bf16[32,411]{1,0:T(8,128)(2,1)S(1)} %get-tuple-element.43.refs_3_, ...), custom_call_target="tpu_custom_call" | custom-call | flops 5260800 | bytes 106752 | tf_op jit(solution)/shard_map/pallas_call | solution.py:164
  (30 shorter events, 0.2 us)
Async XLA Ops:
  0.0 8.2 %copy-start.4 = (bf16[128,768]{1,0:T(8,128)(2,1)S(1)}, bf16[128,768]{1,0:T(8,128)(2,1)}, u32[]{:S(2)}) copy-start(bf16[128,768]{1,0:T(8,128)(2,1)} %refs_0_.3) | copy-start | bytes 589828
  0.0 15.8 %copy-start.3 = (bf16[411,256]{1,0:T(8,128)(2,1)S(1)}, bf16[411,256]{1,0:T(8,128)(2,1)}, u32[]{:S(2)}) copy-start(bf16[411,256]{1,0:T(8,128)(2,1)} %refs_0_.4) | copy-start | bytes 631300
  0.0 6.7 %copy-start.7 = (f32[256]{0:T(256)S(1)}, f32[256]{0:T(256)}, u32[]{:S(2)}) copy-start(f32[256]{0:T(256)} %bias_ref.1) | copy-start | bytes 3076
  0.0 6.7 %copy-start.8 = (s32[128]{0:T(128)S(1)}, s32[128]{0:T(128)}, u32[]{:S(2)}) copy-start(s32[128]{0:T(128)} %usable_ref.1) | copy-start | bytes 1540
  0.0 6.7 %copy-start.6 = (f32[4,32]{1,0:T(4,128)S(1)}, f32[4,32]{1,0:T(4,128)}, u32[]{:S(2)}) copy-start(f32[4,32]{1,0:T(4,128)} %diffusivity_ref.1) | copy-start | bytes 1540
  0.0 6.7 %copy-start.2 = (f32[4,32,411]{2,1,0:T(8,128)S(1)}, f32[4,32,411]{2,1,0:T(8,128)}, u32[]{:S(2)}) copy-start(f32[4,32,411]{2,1,0:T(8,128)} %fields_ref.1) | copy-start | bytes 631300
  0.0 8.2 %collective-permute-start.1 = (bf16[128,768]{1,0:T(8,128)(2,1)}, bf16[128,768]{1,0:T(8,128)(2,1)S(1)}, u32[]{:S(2)}, u32[]{:S(2)}) collective-permute-start(bf16[128,768]{1,0:T(8,128)(2,1)} %refs_0_.3), channel_id=1, source_target_pairs={{0,8},{8,0},{16,24},{24,16},{1,9},{9,1},{17,25},{25,17},{2,10},{10... | collective-permute-start | bytes 589832 | tf_op jit(solution)/shard_map/ppermute | solution.py:503
  3.1 12.3 %collective-permute-start.8 = (bf16[411,256]{1,0:T(8,128)(2,1)}, bf16[411,256]{1,0:T(8,128)(2,1)S(1)}, u32[]{:S(2)}, u32[]{:S(2)}) collective-permute-start(bf16[411,256]{1,0:T(8,128)(2,1)} %refs_0_.4), channel_id=1, source_target_pairs={{0,4},{1,5},{2,6},{3,7},{4,0},{5,1},{6,2},{7,3},{8,12},{9,13},{10,... | collective-permute-start | bytes 631304 | tf_op jit(solution)/shard_map/ppermute | solution.py:500
  4.6 10.8 %collective-permute-start.7 = (bf16[411,256]{1,0:T(8,128)(2,1)}, bf16[411,256]{1,0:T(8,128)(2,1)S(1)}, u32[]{:S(2)}, u32[]{:S(2)}) collective-permute-start(bf16[411,256]{1,0:T(8,128)(2,1)} %refs_0_.4), channel_id=1, source_target_pairs={{0,2},{1,3},{2,0},{3,1},{4,6},{5,7},{6,4},{7,5},{8,10},{9,11},{10,... | collective-permute-start | bytes 631304 | tf_op jit(solution)/shard_map/ppermute | solution.py:500
  6.1 9.7 %collective-permute-start.9 = (bf16[411,256]{1,0:T(8,128)(2,1)}, bf16[411,256]{1,0:T(8,128)(2,1)S(1)}, u32[]{:S(2)}, u32[]{:S(2)}) collective-permute-start(bf16[411,256]{1,0:T(8,128)(2,1)} %refs_0_.4), channel_id=1, source_target_pairs={{0,6},{1,7},{2,4},{3,5},{4,2},{5,3},{6,0},{7,1},{8,14},{9,15},{10,... | collective-permute-start | bytes 631304 | tf_op jit(solution)/shard_map/ppermute | solution.py:500
  6.7 18.5 %copy-start.9 = (s32[256,1]{0,1:T(1,128)S(1)}, s32[256,1]{0,1:T(1,128)}, u32[]{:S(2)}) copy-start(s32[256,1]{0,1:T(1,128)} %param.12) | copy-start | bytes 3076
  6.9 3.7 %collective-permute-start = (bf16[16,512]{1,0:T(8,128)(2,1)S(1)}, bf16[16,512]{1,0:T(8,128)(2,1)S(1)}, u32[]{:S(2)}, u32[]{:S(2)}) collective-permute-start(bf16[16,512]{1,0:T(8,128)(2,1)S(1)} %shard_map.102.refs_0_), channel_id=1, source_target_pairs={{0,8},{8,0},{16,24},{24,16},{1,9},{9,1},{17,25},{25,17},{2,10},{10... | collective-permute-start | bytes 49160 | tf_op jit(solution)/shard_map/ppermute | solution.py:503
  10.6 4.8 %collective-permute-start.2 = (bf16[32,512]{1,0:T(8,128)(2,1)S(1)}, bf16[32,512]{1,0:T(8,128)(2,1)S(1)}, u32[]{:S(2)}, u32[]{:S(2)}) collective-permute-start(bf16[32,512]{1,0:T(8,128)(2,1)S(1)} %shard_map.104.refs_0_), channel_id=1, source_target_pairs={{0,16},{8,24},{16,0},{24,8},{1,17},{9,25},{17,1},{25,9},{2,18},{10... | collective-permute-start | bytes 98312 | tf_op jit(solution)/shard_map/ppermute | solution.py:503
  15.9 10.9 %collective-permute-start.10 = (bf16[1664,256]{1,0:T(8,128)(2,1)S(1)}, bf16[1664,256]{1,0:T(8,128)(2,1)S(1)}, u32[]{:S(2)}, u32[]{:S(2)}) collective-permute-start(bf16[1664,256]{1,0:T(8,128)(2,1)S(1)} %shard_map.107.refs_7_.refs_5_), channel_id=1, source_target_pairs={{0,1},{1,0},{2,3},{3,2},{4,5},{5,4},{6,7},{7,6},{8,9},{9,8},{10,11... | collective-permute-start | bytes 2555912 | tf_op jit(solution)/shard_map/ppermute | solution.py:500
  15.9 13.5 %collective-permute-start.11 = (bf16[256,768]{1,0:T(8,128)(2,1)S(1)}, bf16[256,768]{1,0:T(8,128)(2,1)S(1)}, u32[]{:S(2)}, u32[]{:S(2)}) collective-permute-start(bf16[256,768]{1,0:T(8,128)(2,1)S(1)} %shard_map.103.refs_2_.refs_0_), channel_id=1, source_target_pairs={{0,16},{1,17},{2,3},{3,2},{4,20},{5,21},{6,7},{7,6},{8,9},{9,8},{1... | collective-permute-start | bytes 1179656 | tf_op jit(solution)/shard_map/ppermute | solution.py:512
  18.6 5.5 %collective-permute-start.5 = (bf16[64,512]{1,0:T(8,128)(2,1)S(1)}, bf16[64,512]{1,0:T(8,128)(2,1)S(1)}, u32[]{:S(2)}, u32[]{:S(2)}) collective-permute-start(bf16[64,512]{1,0:T(8,128)(2,1)S(1)} %shard_map.105.refs_0_.refs_4_), channel_id=1, source_target_pairs={{0,6},{1,7},{2,4},{3,5},{4,2},{5,3},{6,0},{7,1},{8,14},{9,15},{10,... | collective-permute-start | bytes 196616 | tf_op jit(solution)/shard_map/ppermute | solution.py:500
  18.9 5.5 %collective-permute-start.4 = (bf16[64,512]{1,0:T(8,128)(2,1)S(1)}, bf16[64,512]{1,0:T(8,128)(2,1)S(1)}, u32[]{:S(2)}, u32[]{:S(2)}) collective-permute-start(bf16[64,512]{1,0:T(8,128)(2,1)S(1)} %shard_map.105.refs_0_.refs_4_), channel_id=1, source_target_pairs={{0,4},{1,5},{2,6},{3,7},{4,0},{5,1},{6,2},{7,3},{8,12},{9,13},{10,... | collective-permute-start | bytes 196616 | tf_op jit(solution)/shard_map/ppermute | solution.py:500
  20.1 5.0 %collective-permute-start.3 = (bf16[64,512]{1,0:T(8,128)(2,1)S(1)}, bf16[64,512]{1,0:T(8,128)(2,1)S(1)}, u32[]{:S(2)}, u32[]{:S(2)}) collective-permute-start(bf16[64,512]{1,0:T(8,128)(2,1)S(1)} %shard_map.105.refs_0_.refs_4_), channel_id=1, source_target_pairs={{0,2},{1,3},{2,0},{3,1},{4,6},{5,7},{6,4},{7,5},{8,10},{9,11},{10,... | collective-permute-start | bytes 196616 | tf_op jit(solution)/shard_map/ppermute | solution.py:500
  25.2 1.6 %collective-permute-start.6 = (bf16[256,512]{1,0:T(8,128)(2,1)S(1)}, bf16[256,512]{1,0:T(8,128)(2,1)S(1)}, u32[]{:S(2)}, u32[]{:S(2)}) collective-permute-start(bf16[256,512]{1,0:T(8,128)(2,1)S(1)} %shard_map.106.refs_5_), channel_id=1, source_target_pairs={{0,1},{1,0},{2,3},{3,2},{4,5},{5,4},{6,7},{7,6},{8,9},{9,8},{10,11... | collective-permute-start | bytes 786440 | tf_op jit(solution)/shard_map/ppermute | solution.py:500
  25.2 1.9 %copy-start = (bf16[2048,768]{1,0:T(8,128)(2,1)S(1)}, bf16[2048,768]{1,0:T(8,128)(2,1)}, u32[]{:S(2)}) copy-start(bf16[2048,768]{1,0:T(8,128)(2,1)} %refs_0_.5) | copy-start | bytes 9437188
  25.3 1.9 %copy-start.5 = (f32[768]{0:T(1024)S(1)}, f32[768]{0:T(1024)}, u32[]{:S(2)}) copy-start(f32[768]{0:T(1024)} %refs_3_.1) | copy-start | bytes 9220
  29.9 7.8 %collective-permute-start.12 = (bf16[128,768]{1,0:T(8,128)(2,1)S(1)}, bf16[128,768]{1,0:T(8,128)(2,1)S(1)}, u32[]{:S(2)}, u32[]{:S(2)}) collective-permute-start(bf16[128,768]{1,0:T(8,128)(2,1)S(1)} %get-tuple-element.30.refs_0_), channel_id=1, source_target_pairs={{0,2},{1,3},{2,0},{3,1},{4,5},{5,4},{6,7},{7,6},{8,10},{9,11},{10,... | collective-permute-start | bytes 589832 | tf_op jit(solution)/shard_map/ppermute | solution.py:512
  31.2 7.7 %collective-permute-start.13 = (bf16[128,768]{1,0:T(8,128)(2,1)S(1)}, bf16[128,768]{1,0:T(8,128)(2,1)S(1)}, u32[]{:S(2)}, u32[]{:S(2)}) collective-permute-start(bf16[128,768]{1,0:T(8,128)(2,1)S(1)} %get-tuple-element.31.refs_1_), channel_id=1, source_target_pairs={{0,4},{1,5},{2,3},{3,2},{4,0},{5,1},{6,7},{7,6},{8,9},{9,8},{10,14... | collective-permute-start | bytes 589832 | tf_op jit(solution)/shard_map/ppermute | solution.py:512
  31.2 11.2 %collective-permute-start.14 = (bf16[128,768]{1,0:T(8,128)(2,1)S(1)}, bf16[128,768]{1,0:T(8,128)(2,1)S(1)}, u32[]{:S(2)}, u32[]{:S(2)}) collective-permute-start(bf16[128,768]{1,0:T(8,128)(2,1)S(1)} %get-tuple-element.30.refs_0_), channel_id=1, source_target_pairs={{0,4},{1,5},{2,3},{3,2},{4,0},{5,1},{6,7},{7,6},{8,9},{9,8},{10,14... | collective-permute-start | bytes 589832 | tf_op jit(solution)/shard_map/ppermute | solution.py:512
  33.2 9.2 %collective-permute-start.15 = (bf16[128,768]{1,0:T(8,128)(2,1)S(1)}, bf16[128,768]{1,0:T(8,128)(2,1)S(1)}, u32[]{:S(2)}, u32[]{:S(2)}) collective-permute-start(bf16[128,768]{1,0:T(8,128)(2,1)S(1)} %get-tuple-element.31.refs_1_), channel_id=1, source_target_pairs={{0,2},{1,3},{2,0},{3,1},{4,5},{5,4},{6,7},{7,6},{8,10},{9,11},{10,... | collective-permute-start | bytes 589832 | tf_op jit(solution)/shard_map/ppermute | solution.py:512
  37.7 4.8 %collective-permute-start.16 = (bf16[128,768]{1,0:T(8,128)(2,1)S(1)}, bf16[128,768]{1,0:T(8,128)(2,1)S(1)}, u32[]{:S(2)}, u32[]{:S(2)}) collective-permute-start(bf16[128,768]{1,0:T(8,128)(2,1)S(1)} %collective-permute-done.12.refs_2_), channel_id=1, source_target_pairs={{0,1},{1,0},{2,6},{3,7},{4,5},{5,4},{6,2},{7,3},{8,12},{9,13},{10,... | collective-permute-start | bytes 589832 | tf_op jit(solution)/shard_map/ppermute | solution.py:512
  38.9 3.5 %collective-permute-start.17 = (bf16[128,768]{1,0:T(8,128)(2,1)S(1)}, bf16[128,768]{1,0:T(8,128)(2,1)S(1)}, u32[]{:S(2)}, u32[]{:S(2)}) collective-permute-start(bf16[128,768]{1,0:T(8,128)(2,1)S(1)} %collective-permute-done.13.refs_3_), channel_id=1, source_target_pairs={{0,1},{1,0},{2,3},{3,2},{4,6},{5,7},{6,4},{7,5},{8,9},{9,8},{10,11... | collective-permute-start | bytes 589832 | tf_op jit(solution)/shard_map/ppermute | solution.py:512
  39.6 3.0 %copy-start.1 = (bf16[1536,768]{1,0:T(8,128)(2,1)S(1)}, bf16[1536,768]{1,0:T(8,128)(2,1)}, u32[]{:S(2)}) copy-start(bf16[1536,768]{1,0:T(8,128)(2,1)} %refs_1_.1) | copy-start | bytes 7077892
  42.5 1.8 %collective-permute-start.18 = (bf16[256,768]{1,0:T(8,128)(2,1)S(1)}, bf16[256,768]{1,0:T(8,128)(2,1)S(1)}, u32[]{:S(2)}, u32[]{:S(2)}) collective-permute-start(bf16[256,768]{1,0:T(8,128)(2,1)S(1)} %shard_map.111.depart_ref), channel_id=1, source_target_pairs={{0,1},{1,0},{2,3},{3,2},{4,5},{5,4},{6,7},{7,6},{8,9},{9,8},{10,11... | collective-permute-start | bytes 1179656 | tf_op jit(solution)/shard_map/ppermute | solution.py:500
  47.1 1.8 %collective-permute-start.19 = (bf16[384,411]{1,0:T(8,128)(2,1)S(1)}, bf16[384,411]{1,0:T(8,128)(2,1)S(1)}, u32[]{:S(2)}, u32[]{:S(2)}) collective-permute-start(bf16[384,411]{1,0:T(8,128)(2,1)S(1)} %get-tuple-element.35), channel_id=1, source_target_pairs={{0,1},{1,0},{2,3},{3,2},{4,5},{5,4},{6,7},{7,6},{8,9},{9,8},{10,11... | collective-permute-start | bytes 946952 | tf_op jit(solution)/shard_map/ppermute | solution.py:500
  49.0 7.0 %collective-permute-start.20 = (bf16[96,411]{1,0:T(8,128)(2,1)S(1)}, bf16[96,411]{1,0:T(8,128)(2,1)S(1)}, u32[]{:S(2)}, u32[]{:S(2)}) collective-permute-start(bf16[96,411]{1,0:T(8,128)(2,1)S(1)} %get-tuple-element.36), channel_id=1, source_target_pairs={{0,6},{1,7},{2,4},{3,5},{4,2},{5,3},{6,0},{7,1},{8,14},{9,15},{10,... | collective-permute-start | bytes 236744 | tf_op jit(solution)/shard_map/ppermute | solution.py:500
  52.8 5.2 %collective-permute-start.21 = (bf16[96,411]{1,0:T(8,128)(2,1)S(1)}, bf16[96,411]{1,0:T(8,128)(2,1)S(1)}, u32[]{:S(2)}, u32[]{:S(2)}) collective-permute-start(bf16[96,411]{1,0:T(8,128)(2,1)S(1)} %get-tuple-element.37), channel_id=1, source_target_pairs={{0,4},{1,5},{2,6},{3,7},{4,0},{5,1},{6,2},{7,3},{8,12},{9,13},{10,... | collective-permute-start | bytes 236744 | tf_op jit(solution)/shard_map/ppermute | solution.py:500
  53.1 4.9 %collective-permute-start.22 = (bf16[96,411]{1,0:T(8,128)(2,1)S(1)}, bf16[96,411]{1,0:T(8,128)(2,1)S(1)}, u32[]{:S(2)}, u32[]{:S(2)}) collective-permute-start(bf16[96,411]{1,0:T(8,128)(2,1)S(1)} %get-tuple-element.38), channel_id=1, source_target_pairs={{0,2},{1,3},{2,0},{3,1},{4,6},{5,7},{6,4},{7,5},{8,10},{9,11},{10,... | collective-permute-start | bytes 236744 | tf_op jit(solution)/shard_map/ppermute | solution.py:500
  58.2 5.1 %collective-permute-start.23 = (bf16[32,411]{1,0:T(8,128)(2,1)S(1)}, bf16[32,411]{1,0:T(8,128)(2,1)S(1)}, u32[]{:S(2)}, u32[]{:S(2)}) collective-permute-start(bf16[32,411]{1,0:T(8,128)(2,1)S(1)} %get-tuple-element.40), channel_id=1, source_target_pairs={{0,16},{8,24},{16,0},{24,8},{1,17},{9,25},{17,1},{25,9},{2,18},{10... | collective-permute-start | bytes 78920 | tf_op jit(solution)/shard_map/ppermute | solution.py:503
  59.9 3.9 %collective-permute-start.24 = (bf16[32,411]{1,0:T(8,128)(2,1)S(1)}, bf16[32,411]{1,0:T(8,128)(2,1)S(1)}, u32[]{:S(2)}, u32[]{:S(2)}) collective-permute-start(bf16[32,411]{1,0:T(8,128)(2,1)S(1)} %get-tuple-element.41), channel_id=1, source_target_pairs={{0,8},{8,0},{16,24},{24,16},{1,9},{9,1},{17,25},{25,17},{2,10},{10... | collective-permute-start | bytes 78920 | tf_op jit(solution)/shard_map/ppermute | solution.py:503
  60.5 5.7 %collective-permute-start.25 = (bf16[32,411]{1,0:T(8,128)(2,1)S(1)}, bf16[32,411]{1,0:T(8,128)(2,1)S(1)}, u32[]{:S(2)}, u32[]{:S(2)}) collective-permute-start(bf16[32,411]{1,0:T(8,128)(2,1)S(1)} %get-tuple-element.42), channel_id=1, source_target_pairs={{0,24},{8,16},{16,8},{24,0},{1,25},{9,17},{17,9},{25,1},{2,26},{10... | collective-permute-start | bytes 78920 | tf_op jit(solution)/shard_map/ppermute | solution.py:503
